TPU v7x, 32 devices: a whole 2x2x4 slice. The times are simulated.
32 devices in a mesh: groups: 2 (over x), ex: 4 (over y, core), layer: 4 (over z).
Axes of the slice: x: 2, y: 2, z: 4, core: 2. Of those that a mesh axis runs over, the one named last changes fastest.
Arguments:
- queries: bfloat16 [512, 4, 4096], P(None, 'layer', 'ex'), may hold values from -6 to 6
- hessian: bfloat16 [4, 4096, 4096], P('layer', 'ex'), as said below
- store: bfloat16 [10240, 4, 4096], P(('groups', 'ex'), 'layer'), parts along dimension 0, may hold values from -0.09375 to 0.09375
Outputs:
- scores: float32 [10240, 512], P(('groups', 'ex', 'layer')), parts along dimension 0
There are 2 independent parts, one for each index of `groups`. A program takes and returns all parts, laid end to end along the dimension named above; an argument that names none is the same for every part. Nothing has to cross between parts.
Inputs may be any that keep to these rules, and one draw needn't show every extreme that they name: `hessian`: each layer's block is symmetric with a positive diagonal and full-rank off-diagonal part.
All inputs are finite; a program needn't handle non-finite values.
Results may differ from a plain program's by a relative error of at most 0.0029.
Values may be sent and summed in bfloat16 or wider, within the bound.
No kernel may reach another device: no remote copies, remote signals or barrier semaphores. Data moves between devices by JAX's collectives and lax.ppermute only.
A program may use at most 128 MiB of HBM per device.

v0:
```python
import jax
import jax.numpy as jnp
from jax import lax
from jax.sharding import PartitionSpec as P


def shards(queries, hessian, store):
    query_cols = queries[:, 0, :]
    hess_rows = hessian[0]
    store_rows = store[:, 0, :]
    share = lax.psum_scatter(
        lax.dot_general(
            hess_rows, query_cols, (((0,), (1,)), ((), ())), preferred_element_type=jnp.float32
        ),
        "ex",
        scatter_dimension=0,
        tiled=True,
    ).astype(jnp.bfloat16)
    total = jnp.dot(
        store_rows,
        lax.all_gather(share, "ex", axis=0, tiled=True),
        preferred_element_type=jnp.float32,
    )
    return lax.psum_scatter(total, "layer", scatter_dimension=0, tiled=True)


def solution(mesh):
    in_specs = (P(None, "layer", "ex"), P("layer", "ex", None), P(("groups", "ex"), "layer", None))
    out_specs = P(("groups", "ex", "layer"), None)
    return jax.shard_map(shards, mesh=mesh, in_specs=in_specs, out_specs=out_specs, check_vma=False)
```

profile of v0, /device:TPU:0, one launch (start us, length us, event | category | flops | bytes accessed | tf_op | source)
XLA Modules:
  0.0 203.8 jit_solution(15386517277108928332)
XLA Ops:
  6.5 0.0 copy-start
  6.5 0.0 reduce-scatter.5.cloned.1.call-start
  6.5 1.2 copy-done
  7.8 10.4 %fusion.2 = f32[4096,512]{1,0:T(8,128)} fusion(bf16[1,1024,4096]{2,1,0:T(8,128)(2,1)} %param.4, bf16[512,1,1024]{2,0,1:T(8,128)(2,1)S(1)} %copy-done), kind=kOutput, calls=%fused_computation.2 | convolution fusion | flops 4294967296 | bytes 17825792 | tf_op jit(solution)/shard_map/dot_general | solution.py:12
  18.1 0.0 reduce-scatter.5.cloned.1.call-update
  18.2 0.0 all-gather.2.cloned.1.call-start
  18.2 74.5 %reduce-scatter.5.cloned.1.call-done = f32[1024,512]{1,0:T(8,128)} async-done(((f32[4096,512]{1,0:T(8,128)}), f32[1024,512]{1,0:T(8,128)}) %reduce-scatter.5.cloned.1.call-update) | async-done | bytes 2097168 | tf_op jit(solution)/shard_map/reduce_scatter | solution.py:11
  92.8 2.7 %convert_element_type.3 = bf16[1024,512]{1,0:T(8,128)(2,1)} convert(f32[1024,512]{1,0:T(8,128)} %reduce-scatter.5.cloned.1.call-done) | non-fusion elementwise | flops 524288 | bytes 3145728 | tf_op jit(solution)/shard_map/convert_element_type | solution.py:18
  95.5 0.0 all-gather.2.cloned.1.call-update
  95.5 0.0 reduce-scatter.7.cloned.1.call-start
  95.5 34.6 %all-gather.2.cloned.1.call-done = bf16[4096,512]{1,0:T(8,128)(2,1)} async-done(((bf16[1024,512]{1,0:T(8,128)(2,1)}), bf16[4096,512]{1,0:T(8,128)(2,1)}) %all-gather.2.cloned.1.call-update) | async-done | bytes 4194320 | tf_op jit(solution)/shard_map/all_gather | solution.py:21
  130.1 11.6 %fusion.4 = f32[1280,512]{0,1:T(8,128)} fusion(bf16[4096,512]{1,0:T(8,128)(2,1)} %all-gather.2.cloned.1.call-done, bf16[1280,1,4096]{2,0,1:T(8,128)(2,1)} %param.5), kind=kOutput, calls=%fused_computation.4 | convolution fusion | flops 5368709120 | bytes 17301504 | tf_op jit(solution)/shard_map/dot_general | solution.py:19
  141.7 3.2 %copy.6 = f32[1280,512]{1,0:T(8,128)} copy(f32[1280,512]{0,1:T(8,128)} %fusion.4) | data formatting | bytes 5242880
  144.9 0.0 reduce-scatter.7.cloned.1.call-update
  145.0 52.3 %reduce-scatter.7.cloned.1.call-done = f32[320,512]{1,0:T(8,128)} async-done(((f32[1280,512]{1,0:T(8,128)}), f32[320,512]{1,0:T(8,128)}) %reduce-scatter.7.cloned.1.call-update) | async-done | bytes 655376 | tf_op jit(solution)/shard_map/reduce_scatter | solution.py:24
Async XLA Ops:
  6.5 1.2 copy-start
  6.5 86.2 %reduce-scatter.5.cloned.1.call-start = ((), (), s32[]{:S(2)}) async-start(), calls=%async_computation.2 | async-start | bytes 10485760 | tf_op jit(solution)/shard_map/reduce_scatter | solution.py:11
  18.2 111.9 %all-gather.2.cloned.1.call-start = ((), (), s32[]{:S(2)}) async-start(), calls=%async_computation.3 | async-start | bytes 5242880 | tf_op jit(solution)/shard_map/all_gather | solution.py:21
  95.5 101.7 %reduce-scatter.7.cloned.1.call-start = ((), (), s32[]{:S(2)}) async-start(), calls=%async_computation.4 | async-start | bytes 3276800 | tf_op jit(solution)/shard_map/reduce_scatter | solution.py:24
Sparse Core Ops, SparseCore 0:
  18.3 74.4 reduce-scatter.4
  95.6 34.4 all-gather.1
  145.1 52.0 reduce-scatter.6
where the time goes:
time: 204 us
  waiting for transfers between devices  161 us (79%)
  matrix products  22 us (11%)
  between operations  13.1 us (6%)
  local copies, waits for them, and re-layouts  4.44 us (2%)
  other arithmetic  2.7 us (1%)
    reduce_scatter x1, waiting for transfers between devices, shards(): lax.psum_scatter(lax.dot_general(hess_rows, query_cols, (((0,), (1,)), ((...  74.5 us
    reduce_scatter x1, waiting for transfers between devices, shards(): return lax.psum_scatter(total, 'layer', scatter_dimension=0, tiled=True)  52.3 us
    all_gather x1, waiting for transfers between devices, shards(): lax.all_gather(share, 'ex', axis=0, tiled=True)  34.6 us
    dot_general x1, matrix products, shards(): jnp.dot(store_rows, lax.all_gather(share, 'ex', axis=0, tiled=True), pref...  11.6 us
    dot_general x1, matrix products, shards(): lax.dot_general(hess_rows, query_cols, (((0,), (1,)), ((), ())), preferre...  10.4 us
    unnamed x3, local copies, waits for them, and re-layouts  4.44 us
  transfers between devices with their start and end apart: 3, of which 3 were waited for; matrix products, arithmetic and copies ran while one was open for 0% of the time, Pallas kernels for 0%

commit v1 on v0

v1 whole, which is shorter than its diff:
```python
import functools

import jax
import jax.numpy as jnp
from jax import lax
from jax.experimental import pallas as pl
from jax.experimental.pallas import tpu as pltpu
from jax.sharding import PartitionSpec as P

F32, BF16 = jnp.float32, jnp.bfloat16
CORES = 2
CHUNKS = 2
MIB = 1 << 20
VMEM = pl.BlockSpec(memory_space=pltpu.VMEM)
SMEM = pl.BlockSpec(memory_space=pltpu.SMEM)
ANY = pl.BlockSpec(memory_space=pl.ANY)


def load_kernel(hess_hbm, store_hbm, hess_ref, store_ref, sems):
    copies = [
        pltpu.make_async_copy(hess_hbm, hess_ref, sems.at[0]),
        pltpu.make_async_copy(store_hbm, store_ref, sems.at[1]),
    ]
    for copy in copies:
        copy.start()
    for copy in copies:
        copy.wait()


def load(hess, store):
    return pl.pallas_call(
        load_kernel,
        out_shape=(pltpu.VMEM(hess.shape, BF16), pltpu.VMEM(store.shape, BF16)),
        in_specs=[ANY, ANY],
        out_specs=(VMEM, VMEM),
        scratch_shapes=[pltpu.SemaphoreType.DMA((2,))],
        compiler_params=pltpu.CompilerParams(vmem_limit_bytes=2 * MIB),
    )(hess, store)


def condition_kernel(count, ids, hess, *rest):
    pieces, out, total = rest[:count], rest[count], rest[count + 1]
    width = hess.shape[1] // count
    for t, piece in enumerate(pieces):
        columns = pl.ds(pl.multiple_of(ids[t] * width, width), width)
        part = lax.dot_general(
            hess[:, columns], piece[...], (((1,), (1,)), ((), ())), preferred_element_type=F32
        )
        if t:
            total[...] += part
        else:
            total[...] = part
    out[...] = total[...].astype(BF16)


def condition(ids, hess, pieces):
    rows, queries = hess.shape[0], pieces[0].shape[0]
    return pl.pallas_call(
        functools.partial(condition_kernel, len(pieces)),
        out_shape=jax.ShapeDtypeStruct((rows, queries), BF16),
        in_specs=[SMEM] + [VMEM] * (1 + len(pieces)),
        out_specs=VMEM,
        scratch_shapes=[pltpu.VMEM((rows, queries), F32)],
        compiler_params=pltpu.CompilerParams(vmem_limit_bytes=16 * MIB),
    )(ids, hess, *pieces)


def score_kernel(groups, count, ids, blocks, store, *rest):
    pieces = rest[: groups * count]
    send, keep, right = rest[groups * count :]
    rows = send.shape[1]
    depth, width = pieces[0].shape
    for t in range(count):
        at = pl.ds(pl.multiple_of(ids[t] * depth, depth), depth)
        for j in range(groups):
            right[at, j * width : (j + 1) * width] = pieces[t * groups + j][...]
    for r in range(2 * send.shape[0]):
        at = pl.ds(pl.multiple_of(blocks[r] * rows, rows), rows)
        part = jnp.dot(store[at, :], right[...], preferred_element_type=F32)
        if r % 2:
            send[r // 2] = part.astype(BF16)
        else:
            keep[r // 2] = part


def score(ids, blocks, store, pieces, groups):
    count = len(pieces) // groups
    depth, width = pieces[0].shape
    layers = blocks.shape[0]
    shape = (layers // 2, store.shape[0] // layers, groups * width)
    return pl.pallas_call(
        functools.partial(score_kernel, groups, count),
        out_shape=(jax.ShapeDtypeStruct(shape, BF16), jax.ShapeDtypeStruct(shape, F32)),
        in_specs=[SMEM, SMEM] + [VMEM] * (1 + len(pieces)),
        out_specs=(VMEM, VMEM),
        scratch_shapes=[pltpu.VMEM((count * depth, groups * width), BF16)],
        compiler_params=pltpu.CompilerParams(vmem_limit_bytes=24 * MIB),
    )(ids, blocks, store, *pieces)


def fold_kernel(keep, got, send, left):
    for r in range(keep.shape[0]):
        total = keep[r] + got[r].astype(F32)
        if r % 2:
            send[r // 2] = total.astype(BF16)
        else:
            left[r // 2] = total


def fold(keep, got):
    shape = (keep.shape[0] // 2,) + keep.shape[1:]
    return pl.pallas_call(
        fold_kernel,
        out_shape=(jax.ShapeDtypeStruct(shape, BF16), jax.ShapeDtypeStruct(shape, F32)),
        in_specs=[VMEM, VMEM],
        out_specs=(VMEM, VMEM),
        compiler_params=pltpu.CompilerParams(vmem_limit_bytes=16 * MIB),
    )(keep, got)


def finish_kernel(chunks, groups, place, *refs):
    out = refs[2 * chunks]
    span = out.shape[1] // groups
    width = span // chunks
    for c in range(chunks):
        keep, got = refs[2 * c], refs[2 * c + 1]
        total = keep[0] + got[0].astype(F32)
        for j in range(groups):
            at = pl.multiple_of(place[j] * span + c * width, width)
            out[:, pl.ds(at, width)] = total[:, j * width : (j + 1) * width]


def finish(place, pairs, queries):
    groups = place.shape[0]
    rows = pairs[0][0].shape[1]
    return pl.pallas_call(
        functools.partial(finish_kernel, len(pairs), groups),
        out_shape=jax.ShapeDtypeStruct((rows, queries), F32),
        in_specs=[SMEM] + [VMEM] * (2 * len(pairs)),
        out_specs=VMEM,
        compiler_params=pltpu.CompilerParams(vmem_limit_bytes=16 * MIB),
    )(place, *[a for pair in pairs for a in pair])


def shards(groups, ex, layers, queries, hessian, store):
    chips = ex // CORES
    at_group, at_ex, at_layer = (lax.axis_index(a) for a in ("groups", "ex", "layer"))
    chip, core = at_ex // CORES, at_ex % CORES
    ids = jnp.stack(
        [(chip + k) % chips * CORES + (core ^ s) for k in range(chips) for s in range(CORES)]
    ).astype(jnp.int32)
    blocks = jnp.stack([at_layer ^ r for r in range(layers)]).astype(jnp.int32)
    place = jnp.stack([(at_group + j) % groups for j in range(groups)]).astype(jnp.int32)

    def from_chip(x, k):
        perm = [(e, (e - k * CORES) % ex) for e in range(ex)]
        return lax.ppermute(x, "ex", perm)

    def from_core(x):
        return lax.ppermute(x, "ex", [(e, e ^ 1) for e in range(ex)])

    def from_group(x, j):
        return lax.ppermute(x, "groups", [(g, (g - j) % groups) for g in range(groups)])

    def from_layer(x, b):
        return lax.ppermute(x, "layer", [(z, z ^ b) for z in range(layers)])

    hess, rows = load(hessian[0], store[:, 0, :])
    total = queries.shape[0]
    span = total // groups
    width = span // CHUNKS
    pairs = []
    last = None
    for c in range(CHUNKS):
        mine = lax.dynamic_slice_in_dim(queries[:, 0, :], at_group * span + c * width, width, 0)
        if last is not None:
            mine, last = lax.optimization_barrier((mine, last))
        pieces = []
        for k in range(chips):
            here = from_chip(mine, k) if k else mine
            pieces += [here, from_core(here)]
            last = here
        share = condition(ids, hess, pieces)
        held = []
        for k in range(chips):
            here = from_chip(share, k) if k else share
            across = [from_group(here, j) if j else here for j in range(groups)]
            held += across + [from_core(x) for x in across]
        send, keep = score(ids, blocks, rows, held, groups)
        step = 1
        while True:
            got = from_layer(send, step)
            if keep.shape[0] == 1:
                break
            send, keep = fold(keep, got)
            step *= 2
        pairs.append((keep, got))
    return finish(place, pairs, total)


def solution(mesh):
    groups, ex, layers = (mesh.shape[a] for a in ("groups", "ex", "layer"))
    in_specs = (P(None, "layer", "ex"), P("layer", "ex", None), P(("groups", "ex"), "layer", None))
    out_specs = P(("groups", "ex", "layer"), None)
    return jax.shard_map(
        functools.partial(shards, groups, ex, layers),
        mesh=mesh,
        in_specs=in_specs,
        out_specs=out_specs,
        check_vma=False,
    )
```

time: 204 us -> 103 us (0.50)
  waiting for transfers between devices: 161 us -> 48.1 us
  matrix products: 22 us -> 0 us
  starting transfers between devices: 0.09 us -> 20.4 us
  Pallas kernels: 0 us -> 17.2 us
  between operations: 13.1 us -> 0.1 us
  local copies, waits for them, and re-layouts: 4.44 us -> 16.4 us
  other arithmetic: 2.7 us -> 0.23 us
    reduce_scatter x2 -> x0, waiting for transfers between devices: 127 us -> none  [the longest x1 74.5 us: shards(): lax.psum_scatter(lax.dot_general(hess_rows, query_cols, (((0,), (1,)), ((...]
    ppermute x0 -> x24, waiting for transfers between devices: none -> 48.1 us  [the longest x4 20.1 us: from_layer(): return lax.ppermute(x, 'layer', [(z, z ^ b) for z in range(layers)])]
    all_gather x1 -> x0, waiting for transfers between devices: 34.6 us -> none  [shards(): lax.all_gather(share, 'ex', axis=0, tiled=True)]
    dot_general x2 -> x0, matrix products: 22 us -> none  [the longest x1 11.6 us: shards(): jnp.dot(store_rows, lax.all_gather(share, 'ex', axis=0, tiled=True), pref...]
    ppermute x0 -> x24, starting transfers between devices: none -> 20.4 us  [the longest x4 6.83 us: from_chip(): return lax.ppermute(x, 'ex', perm)]
    pallas_call x0 -> x8, Pallas kernels: none -> 17.2 us  [the longest x2 8.54 us: score(): pl.pallas_call(functools.partial(score_kernel, groups, count), out_shape=...]
    unnamed x3 -> x8, local copies, waits for them, and re-layouts: 4.44 us -> 15.3 us
    convert_element_type x1 -> x0, other arithmetic: 2.7 us -> none  [shards(): share = lax.psum_scatter(lax.dot_general(hess_rows, query_cols, (((0,), (...]
  transfers between devices with their start and end apart: 3 -> 24, of which waited for: 3 -> 10; matrix products, arithmetic and copies ran while one was open for 0% -> 0% of each run, Pallas kernels for 0% -> 15%
where the time goes in v1:
time: 103 us; the launch traced here: 102 us
  waiting for transfers between devices  48.1 us (47%)
  starting transfers between devices  20.4 us (20%)
  Pallas kernels  17.2 us (17%)
  local copies, waits for them, and re-layouts  16.4 us (16%)
    ppermute x4, waiting for transfers between devices, from_layer(): return lax.ppermute(x, 'layer', [(z, z ^ b) for z in range(layers)])  20.1 us
    ppermute x4, waiting for transfers between devices, from_chip(): return lax.ppermute(x, 'ex', perm)  16.4 us
    unnamed x8, local copies, waits for them, and re-layouts  15.3 us
    ppermute x4, waiting for transfers between devices, from_group(): lax.ppermute(x, 'groups', [(g, (g - j) % groups) for g in range(groups)])  11.6 us
    pallas_call x2, Pallas kernels, score(): pl.pallas_call(functools.partial(score_kernel, groups, count), out_shape=...  8.54 us
    ppermute x4, starting transfers between devices, from_chip(): return lax.ppermute(x, 'ex', perm)  6.83 us
    ppermute x4, starting transfers between devices, from_layer(): return lax.ppermute(x, 'layer', [(z, z ^ b) for z in range(layers)])  6.45 us
    pallas_call x2, Pallas kernels, condition(): pl.pallas_call(functools.partial(condition_kernel, len(pieces)), out_shap...  5.73 us
  transfers between devices with their start and end apart: 24, of which 10 were waited for; matrix products, arithmetic and copies ran while one was open for 0% of the time, Pallas kernels for 15%

profile of v1, /device:TPU:0, one launch (start us, length us, event | category | flops | bytes accessed | tf_op | source)
XLA Modules:
  0.0 102.3 jit_solution(293733868863557378)
XLA Ops:
  0.0 1.1 %dynamic-slice_bitcast_fusion = (bf16[128,1024]{1,0:T(8,128)(2,1)S(1)}, bf16[128,1024]{1,0:T(8,128)(2,1)S(1)}) fusion(bf16[512,1,1024]{2,0,1:T(8,128)(2,1)} %param.3, s32[]{:T(128)S(6)} %select_n.44, s32[]{:T(128)S(6)} %select_n.43), kind=kLoop, calls=%fused_computation | loop fusion | bytes 1048584 | tf_op jit(solution)/shard_map/dynamic_slice | solution.py:175
  1.1 3.0 %collective-permute-start.1 = (bf16[128,1024]{1,0:T(8,128)(2,1)S(1)}, bf16[128,1024]{1,0:T(8,128)(2,1)S(1)}, u32[]{:S(2)}, u32[]{:S(2)}) collective-permute-start(bf16[128,1024]{1,0:T(8,128)(2,1)S(1)} %get-tuple-element.28.rest_0_), channel_id=1, source_target_pairs={{0,8},{4,12},{8,0},{12,4},{1,9},{5,13},{9,1},{13,5},{2,10},{6,14},... | collective-permute-start | bytes 786440 | tf_op jit(solution)/shard_map/ppermute | solution.py:157
  4.1 6.3 %collective-permute-done.1.rest_2_ = bf16[128,1024]{1,0:T(8,128)(2,1)S(1)} collective-permute-done((bf16[128,1024]{1,0:T(8,128)(2,1)S(1)}, bf16[128,1024]{1,0:T(8,128)(2,1)S(1)}, u32[]{:S(2)}, u32[]{:S(2)}) %collective-permute-start.1) | collective-permute-done | bytes 262176 | tf_op jit(solution)/shard_map/ppermute | solution.py:157
  10.4 1.7 %collective-permute-start.13 = (bf16[128,1024]{1,0:T(8,128)(2,1)S(1)}, bf16[128,1024]{1,0:T(8,128)(2,1)S(1)}, u32[]{:S(2)}, u32[]{:S(2)}) collective-permute-start(bf16[128,1024]{1,0:T(8,128)(2,1)S(1)} %get-tuple-element.22.rest_0_), channel_id=1, source_target_pairs={{0,8},{4,12},{8,0},{12,4},{1,9},{5,13},{9,1},{13,5},{2,10},{6,14},... | collective-permute-start | bytes 786440 | tf_op jit(solution)/shard_map/ppermute | solution.py:157
  12.1 0.5 collective-permute-start.2
  12.7 0.0 collective-permute-start.12
  12.7 5.2 %collective-permute-done.13.rest_2_ = bf16[128,1024]{1,0:T(8,128)(2,1)S(1)} collective-permute-done((bf16[128,1024]{1,0:T(8,128)(2,1)S(1)}, bf16[128,1024]{1,0:T(8,128)(2,1)S(1)}, u32[]{:S(2)}, u32[]{:S(2)}) %collective-permute-start.13) | collective-permute-done | bytes 262176 | tf_op jit(solution)/shard_map/ppermute | solution.py:157
  17.9 0.0 collective-permute-start.14
  17.9 4.0 %copy-done.2 = bf16[1280,1,4096]{2,0,1:T(8,128)(2,1)S(1)} copy-done((bf16[1280,1,4096]{2,0,1:T(8,128)(2,1)S(1)}, bf16[1280,1,4096]{2,0,1:T(8,128)(2,1)}, u32[]{:S(2)}) %copy-start.2) | copy-done | bytes 10485784
  21.9 3.4 %copy-done.3 = bf16[1,1024,4096]{2,1,0:T(8,128)(2,1)S(1)} copy-done((bf16[1,1024,4096]{2,1,0:T(8,128)(2,1)S(1)}, bf16[1,1024,4096]{2,1,0:T(8,128)(2,1)}, u32[]{:S(2)}) %copy-start.3) | copy-done | bytes 8388632
  25.3 1.3 %shard_map.37 = (bf16[1024,4096]{1,0:T(8,128)(2,1)S(1)}, bf16[1280,4096]{1,0:T(8,128)(2,1)S(1)}) custom-call(bf16[1024,4096]{1,0:T(8,128)(2,1)S(1)} %bitcast.17, bf16[1280,4096]{1,0:T(8,128)(2,1)S(1)} %bitcast.16), custom_call_target="tpu_custom_call" | custom-call | tf_op jit(solution)/shard_map/pallas_call | solution.py:31
  26.6 4.0 %copy-done = bf16[1280,4096]{1,0:T(8,128)(2,1)} copy-done((bf16[1280,4096]{1,0:T(8,128)(2,1)}, bf16[1280,4096]{1,0:T(8,128)(2,1)S(1)}, u32[]{:S(2)}) %copy-start) | copy-done | bytes 10485784
  30.5 0.1 pad_add_fusion.1.ids
  30.6 0.0 collective-permute-done.rest_1_
  30.6 2.9 %shard_map.38.rest_0_ = bf16[1024,128]{1,0:T(8,128)(2,1)S(1)} custom-call(s32[4]{0:T(128)S(1)} %pad_add_fusion.1.ids, bf16[1024,4096]{1,0:T(8,128)(2,1)S(1)} %get-tuple-element.17.hess, bf16[128,1024]{1,0:T(8,128)(2,1)S(1)} %get-tuple-element.28.rest_0_, bf16[128,1024]{1,0:T(8,128)(2,1)S(1)} %collective-permute-done.rest_1_, ...), custom_call_target="tpu_custom_call" | custom-call | tf_op jit(solution)/shard_map/pallas_call | solution.py:58
  33.5 1.5 %collective-permute-start.6 = (bf16[1024,128]{1,0:T(8,128)(2,1)S(1)}, bf16[1024,128]{1,0:T(8,128)(2,1)S(1)}, u32[]{:S(2)}, u32[]{:S(2)}) collective-permute-start(bf16[1024,128]{1,0:T(8,128)(2,1)S(1)} %shard_map.38.rest_0_), channel_id=1, source_target_pairs={{0,8},{4,12},{8,0},{12,4},{1,9},{5,13},{9,1},{13,5},{2,10},{6,14},... | collective-permute-start | bytes 786440 | tf_op jit(solution)/shard_map/ppermute | solution.py:157
  35.0 0.2 collective-permute-start.4
  35.2 1.5 %collective-permute-start.3 = (bf16[1024,128]{1,0:T(8,128)(2,1)S(1)}, bf16[1024,128]{1,0:T(8,128)(2,1)S(1)}, u32[]{:S(2)}, u32[]{:S(2)}) collective-permute-start(bf16[1024,128]{1,0:T(8,128)(2,1)S(1)} %shard_map.38.rest_0_), channel_id=1, source_target_pairs={{0,16},{16,0},{1,17},{17,1},{2,18},{18,2},{3,19},{19,3},{4,20},{20... | collective-permute-start | bytes 786440 | tf_op jit(solution)/shard_map/ppermute | solution.py:163
  36.7 2.9 %shard_map.41.rest_0_ = bf16[1024,128]{1,0:T(8,128)(2,1)S(1)} custom-call(s32[4]{0:T(128)S(1)} %pad_add_fusion.1.ids, bf16[1024,4096]{1,0:T(8,128)(2,1)S(1)} %get-tuple-element.17.hess, bf16[128,1024]{1,0:T(8,128)(2,1)S(1)} %get-tuple-element.22.rest_0_, bf16[128,1024]{1,0:T(8,128)(2,1)S(1)} %collective-permute-done.12.rest_1_, ...), custom_call_target="tpu_custom_call" | custom-call | tf_op jit(solution)/shard_map/pallas_call | solution.py:58
  39.6 0.6 collective-permute-start.18
  40.2 2.1 %collective-permute-done.6.rest_4_ = bf16[1024,128]{1,0:T(8,128)(2,1)S(1)} collective-permute-done((bf16[1024,128]{1,0:T(8,128)(2,1)S(1)}, bf16[1024,128]{1,0:T(8,128)(2,1)S(1)}, u32[]{:S(2)}, u32[]{:S(2)}) %collective-permute-start.6) | collective-permute-done | bytes 262176 | tf_op jit(solution)/shard_map/ppermute | solution.py:157
  42.3 1.8 %collective-permute-start.7 = (bf16[1024,128]{1,0:T(8,128)(2,1)S(1)}, bf16[1024,128]{1,0:T(8,128)(2,1)S(1)}, u32[]{:S(2)}, u32[]{:S(2)}) collective-permute-start(bf16[1024,128]{1,0:T(8,128)(2,1)S(1)} %collective-permute-done.6.rest_4_), channel_id=1, source_target_pairs={{0,16},{16,0},{1,17},{17,1},{2,18},{18,2},{3,19},{19,3},{4,20},{20... | collective-permute-start | bytes 786440 | tf_op jit(solution)/shard_map/ppermute | solution.py:163
  44.1 0.0 collective-permute-start.8
  44.1 0.0 collective-permute-done.3.rest_1_
  44.1 0.5 collective-permute-start.5
  44.6 0.6 collective-permute-start.15
  45.2 2.7 %collective-permute-done.18.rest_4_ = bf16[1024,128]{1,0:T(8,128)(2,1)S(1)} collective-permute-done((bf16[1024,128]{1,0:T(8,128)(2,1)S(1)}, bf16[1024,128]{1,0:T(8,128)(2,1)S(1)}, u32[]{:S(2)}, u32[]{:S(2)}) %collective-permute-start.18) | collective-permute-done | bytes 262176 | tf_op jit(solution)/shard_map/ppermute | solution.py:157
  47.9 1.4 %collective-permute-start.19 = (bf16[1024,128]{1,0:T(8,128)(2,1)S(1)}, bf16[1024,128]{1,0:T(8,128)(2,1)S(1)}, u32[]{:S(2)}, u32[]{:S(2)}) collective-permute-start(bf16[1024,128]{1,0:T(8,128)(2,1)S(1)} %collective-permute-done.18.rest_4_), channel_id=1, source_target_pairs={{0,16},{16,0},{1,17},{17,1},{2,18},{18,2},{3,19},{19,3},{4,20},{20... | collective-permute-start | bytes 786440 | tf_op jit(solution)/shard_map/ppermute | solution.py:163
  49.3 2.2 %collective-permute-done.7.rest_5_ = bf16[1024,128]{1,0:T(8,128)(2,1)S(1)} collective-permute-done((bf16[1024,128]{1,0:T(8,128)(2,1)S(1)}, bf16[1024,128]{1,0:T(8,128)(2,1)S(1)}, u32[]{:S(2)}, u32[]{:S(2)}) %collective-permute-start.7) | collective-permute-done | bytes 262176 | tf_op jit(solution)/shard_map/ppermute | solution.py:163
  51.5 0.5 collective-permute-start.16
  52.0 0.1 collective-permute-start.20
  52.1 5.0 %collective-permute-done.15.rest_1_ = bf16[1024,128]{1,0:T(8,128)(2,1)S(1)} collective-permute-done((bf16[1024,128]{1,0:T(8,128)(2,1)S(1)}, bf16[1024,128]{1,0:T(8,128)(2,1)S(1)}, u32[]{:S(2)}, u32[]{:S(2)}) %collective-permute-start.15) | collective-permute-done | bytes 262176 | tf_op jit(solution)/shard_map/ppermute | solution.py:163
  57.1 4.3 %collective-permute-done.19.rest_5_ = bf16[1024,128]{1,0:T(8,128)(2,1)S(1)} collective-permute-done((bf16[1024,128]{1,0:T(8,128)(2,1)S(1)}, bf16[1024,128]{1,0:T(8,128)(2,1)S(1)}, u32[]{:S(2)}, u32[]{:S(2)}) %collective-permute-start.19) | collective-permute-done | bytes 262176 | tf_op jit(solution)/shard_map/ppermute | solution.py:163
  61.5 0.1 pad_add_fusion.2.blocks
  61.5 4.0 %copy-done.1 = bf16[1280,4096]{1,0:T(8,128)(2,1)S(1)} copy-done((bf16[1280,4096]{1,0:T(8,128)(2,1)S(1)}, bf16[1280,4096]{1,0:T(8,128)(2,1)}, u32[]{:S(2)}) %copy-start.1) | copy-done | bytes 10485784
  65.5 4.2 %shard_map.39 = (bf16[2,320,256]{2,1,0:T(8,128)(2,1)S(1)}, f32[2,320,256]{2,1,0:T(8,128)S(1)}) custom-call(s32[4]{0:T(128)S(1)} %pad_add_fusion.1.ids, s32[4]{0:T(128)S(1)} %pad_add_fusion.2.blocks, bf16[1280,4096]{1,0:T(8,128)(2,1)S(1)} %copy-done.1, bf16[1024,128]{1,0:T(8,128)(2,1)S(1)} %shard_map.38.rest_0_, ...), custom_call_target="tpu_custom_call" | custom-call | tf_op jit(solution)/shard_map/pallas_call | solution.py:91
  69.8 1.5 %collective-permute-start.10 = (bf16[2,320,256]{2,1,0:T(8,128)(2,1)S(1)}, bf16[2,320,256]{2,1,0:T(8,128)(2,1)S(1)}, u32[]{:S(2)}, u32[]{:S(2)}) collective-permute-start(bf16[2,320,256]{2,1,0:T(8,128)(2,1)S(1)} %get-tuple-element.19), channel_id=1, source_target_pairs={{0,1},{1,0},{2,3},{3,2},{4,5},{5,4},{6,7},{7,6},{8,9},{9,8},{10,11... | collective-permute-start | bytes 983048 | tf_op jit(solution)/shard_map/ppermute | solution.py:166
  71.3 4.3 %shard_map.42 = (bf16[2,320,256]{2,1,0:T(8,128)(2,1)S(1)}, f32[2,320,256]{2,1,0:T(8,128)S(1)}) custom-call(s32[4]{0:T(128)S(1)} %pad_add_fusion.1.ids, s32[4]{0:T(128)S(1)} %pad_add_fusion.2.blocks, bf16[1280,4096]{1,0:T(8,128)(2,1)S(1)} %copy-done.1, bf16[1024,128]{1,0:T(8,128)(2,1)S(1)} %shard_map.41.rest_0_, ...), custom_call_target="tpu_custom_call" | custom-call | tf_op jit(solution)/shard_map/pallas_call | solution.py:91
  75.7 0.6 collective-permute-start.22
  76.3 4.1 %collective-permute-done.10.got = bf16[2,320,256]{2,1,0:T(8,128)(2,1)S(1)} collective-permute-done((bf16[2,320,256]{2,1,0:T(8,128)(2,1)S(1)}, bf16[2,320,256]{2,1,0:T(8,128)(2,1)S(1)}, u32[]{:S(2)}, u32[]{:S(2)}) %collective-permute-start.10) | collective-permute-done | bytes 327712 | tf_op jit(solution)/shard_map/ppermute | solution.py:166
  80.3 0.1 shard_map.40
  80.4 2.6 %collective-permute-start.11 = (bf16[1,320,256]{2,1,0:T(8,128)(2,1)S(1)}, bf16[1,320,256]{2,1,0:T(8,128)(2,1)S(1)}, u32[]{:S(2)}, u32[]{:S(2)}) collective-permute-start(bf16[1,320,256]{2,1,0:T(8,128)(2,1)S(1)} %get-tuple-element.21), channel_id=1, source_target_pairs={{0,2},{1,3},{2,0},{3,1},{4,6},{5,7},{6,4},{7,5},{8,10},{9,11},{10,... | collective-permute-start | bytes 491528 | tf_op jit(solution)/shard_map/ppermute | solution.py:166
  83.0 7.5 %collective-permute-done.22.got = bf16[2,320,256]{2,1,0:T(8,128)(2,1)S(1)} collective-permute-done((bf16[2,320,256]{2,1,0:T(8,128)(2,1)S(1)}, bf16[2,320,256]{2,1,0:T(8,128)(2,1)S(1)}, u32[]{:S(2)}, u32[]{:S(2)}) %collective-permute-start.22) | collective-permute-done | bytes 327712 | tf_op jit(solution)/shard_map/ppermute | solution.py:166
  90.5 0.1 shard_map.43
  90.6 1.7 %collective-permute-start.23 = (bf16[1,320,256]{2,1,0:T(8,128)(2,1)S(1)}, bf16[1,320,256]{2,1,0:T(8,128)(2,1)S(1)}, u32[]{:S(2)}, u32[]{:S(2)}) collective-permute-start(bf16[1,320,256]{2,1,0:T(8,128)(2,1)S(1)} %get-tuple-element.26), channel_id=1, source_target_pairs={{0,2},{1,3},{2,0},{3,1},{4,6},{5,7},{6,4},{7,5},{8,10},{9,11},{10,... | collective-permute-start | bytes 491528 | tf_op jit(solution)/shard_map/ppermute | solution.py:166
  92.3 0.1 pad_add_fusion.place
  92.4 8.5 %collective-permute-done.23.refs_3_ = bf16[1,320,256]{2,1,0:T(8,128)(2,1)S(1)} collective-permute-done((bf16[1,320,256]{2,1,0:T(8,128)(2,1)S(1)}, bf16[1,320,256]{2,1,0:T(8,128)(2,1)S(1)}, u32[]{:S(2)}, u32[]{:S(2)}) %collective-permute-start.23) | collective-permute-done | bytes 163872 | tf_op jit(solution)/shard_map/ppermute | solution.py:166
  100.9 1.5 %shard_map.44 = f32[320,512]{1,0:T(8,128)} custom-call(s32[2]{0:T(128)S(1)} %pad_add_fusion.place, f32[1,320,256]{2,1,0:T(8,128)S(1)} %get-tuple-element.20.refs_0_, bf16[1,320,256]{2,1,0:T(8,128)(2,1)S(1)} %collective-permute-done.11.refs_1_, f32[1,320,256]{2,1,0:T(8,128)S(1)} %get-tuple-element.25.refs_2_, ...), custom_call_target="tpu_custom_call" | custom-call | tf_op jit(solution)/shard_map/pallas_call | solution.py:136
  (20 shorter events, 0.0 us)
Async XLA Ops:
  1.1 9.3 %collective-permute-start.1 = (bf16[128,1024]{1,0:T(8,128)(2,1)S(1)}, bf16[128,1024]{1,0:T(8,128)(2,1)S(1)}, u32[]{:S(2)}, u32[]{:S(2)}) collective-permute-start(bf16[128,1024]{1,0:T(8,128)(2,1)S(1)} %get-tuple-element.28.rest_0_), channel_id=1, source_target_pairs={{0,8},{4,12},{8,0},{12,4},{1,9},{5,13},{9,1},{13,5},{2,10},{6,14},... | collective-permute-start | bytes 786440 | tf_op jit(solution)/shard_map/ppermute | solution.py:157
  10.4 7.5 %collective-permute-start.13 = (bf16[128,1024]{1,0:T(8,128)(2,1)S(1)}, bf16[128,1024]{1,0:T(8,128)(2,1)S(1)}, u32[]{:S(2)}, u32[]{:S(2)}) collective-permute-start(bf16[128,1024]{1,0:T(8,128)(2,1)S(1)} %get-tuple-element.22.rest_0_), channel_id=1, source_target_pairs={{0,8},{4,12},{8,0},{12,4},{1,9},{5,13},{9,1},{13,5},{2,10},{6,14},... | collective-permute-start | bytes 786440 | tf_op jit(solution)/shard_map/ppermute | solution.py:157
  12.1 18.5 %collective-permute-start = (bf16[128,1024]{1,0:T(8,128)(2,1)S(1)}, bf16[128,1024]{1,0:T(8,128)(2,1)S(1)}, u32[]{:S(2)}, u32[]{:S(2)}) collective-permute-start(bf16[128,1024]{1,0:T(8,128)(2,1)S(1)} %get-tuple-element.28.rest_0_), channel_id=1, source_target_pairs={{0,4},{4,0},{8,12},{12,8},{1,5},{5,1},{9,13},{13,9},{2,6},{6,2},{1... | collective-permute-start | bytes 786440 | tf_op jit(solution)/shard_map/ppermute | solution.py:160
  12.1 18.5 %collective-permute-start.2 = (bf16[128,1024]{1,0:T(8,128)(2,1)S(1)}, bf16[128,1024]{1,0:T(8,128)(2,1)S(1)}, u32[]{:S(2)}, u32[]{:S(2)}) collective-permute-start(bf16[128,1024]{1,0:T(8,128)(2,1)S(1)} %collective-permute-done.1.rest_2_), channel_id=1, source_target_pairs={{0,4},{4,0},{8,12},{12,8},{1,5},{5,1},{9,13},{13,9},{2,6},{6,2},{1... | collective-permute-start | bytes 786440 | tf_op jit(solution)/shard_map/ppermute | solution.py:160
  12.7 24.1 %collective-permute-start.12 = (bf16[128,1024]{1,0:T(8,128)(2,1)S(1)}, bf16[128,1024]{1,0:T(8,128)(2,1)S(1)}, u32[]{:S(2)}, u32[]{:S(2)}) collective-permute-start(bf16[128,1024]{1,0:T(8,128)(2,1)S(1)} %get-tuple-element.22.rest_0_), channel_id=1, source_target_pairs={{0,4},{4,0},{8,12},{12,8},{1,5},{5,1},{9,13},{13,9},{2,6},{6,2},{1... | collective-permute-start | bytes 786440 | tf_op jit(solution)/shard_map/ppermute | solution.py:160
  17.9 18.8 %collective-permute-start.14 = (bf16[128,1024]{1,0:T(8,128)(2,1)S(1)}, bf16[128,1024]{1,0:T(8,128)(2,1)S(1)}, u32[]{:S(2)}, u32[]{:S(2)}) collective-permute-start(bf16[128,1024]{1,0:T(8,128)(2,1)S(1)} %collective-permute-done.13.rest_2_), channel_id=1, source_target_pairs={{0,4},{4,0},{8,12},{12,8},{1,5},{5,1},{9,13},{13,9},{2,6},{6,2},{1... | collective-permute-start | bytes 786440 | tf_op jit(solution)/shard_map/ppermute | solution.py:160
  17.9 4.0 %copy-start.2 = (bf16[1280,1,4096]{2,0,1:T(8,128)(2,1)S(1)}, bf16[1280,1,4096]{2,0,1:T(8,128)(2,1)}, u32[]{:S(2)}) copy-start(bf16[1280,1,4096]{2,0,1:T(8,128)(2,1)} %param.5) | copy-start | bytes 31457284
  21.9 3.4 %copy-start.3 = (bf16[1,1024,4096]{2,1,0:T(8,128)(2,1)S(1)}, bf16[1,1024,4096]{2,1,0:T(8,128)(2,1)}, u32[]{:S(2)}) copy-start(bf16[1,1024,4096]{2,1,0:T(8,128)(2,1)} %param.4) | copy-start | bytes 25165828
  26.5 4.0 %copy-start = (bf16[1280,4096]{1,0:T(8,128)(2,1)}, bf16[1280,4096]{1,0:T(8,128)(2,1)S(1)}, u32[]{:S(2)}) copy-start(bf16[1280,4096]{1,0:T(8,128)(2,1)S(1)} %get-tuple-element.16.store) | copy-start | bytes 31457284
  33.5 8.8 %collective-permute-start.6 = (bf16[1024,128]{1,0:T(8,128)(2,1)S(1)}, bf16[1024,128]{1,0:T(8,128)(2,1)S(1)}, u32[]{:S(2)}, u32[]{:S(2)}) collective-permute-start(bf16[1024,128]{1,0:T(8,128)(2,1)S(1)} %shard_map.38.rest_0_), channel_id=1, source_target_pairs={{0,8},{4,12},{8,0},{12,4},{1,9},{5,13},{9,1},{13,5},{2,10},{6,14},... | collective-permute-start | bytes 786440 | tf_op jit(solution)/shard_map/ppermute | solution.py:157
  35.0 9.6 %collective-permute-start.4 = (bf16[1024,128]{1,0:T(8,128)(2,1)S(1)}, bf16[1024,128]{1,0:T(8,128)(2,1)S(1)}, u32[]{:S(2)}, u32[]{:S(2)}) collective-permute-start(bf16[1024,128]{1,0:T(8,128)(2,1)S(1)} %shard_map.38.rest_0_), channel_id=1, source_target_pairs={{0,4},{4,0},{8,12},{12,8},{1,5},{5,1},{9,13},{13,9},{2,6},{6,2},{1... | collective-permute-start | bytes 786440 | tf_op jit(solution)/shard_map/ppermute | solution.py:160
  35.2 8.9 %collective-permute-start.3 = (bf16[1024,128]{1,0:T(8,128)(2,1)S(1)}, bf16[1024,128]{1,0:T(8,128)(2,1)S(1)}, u32[]{:S(2)}, u32[]{:S(2)}) collective-permute-start(bf16[1024,128]{1,0:T(8,128)(2,1)S(1)} %shard_map.38.rest_0_), channel_id=1, source_target_pairs={{0,16},{16,0},{1,17},{17,1},{2,18},{18,2},{3,19},{19,3},{4,20},{20... | collective-permute-start | bytes 786440 | tf_op jit(solution)/shard_map/ppermute | solution.py:163
  39.6 8.3 %collective-permute-start.18 = (bf16[1024,128]{1,0:T(8,128)(2,1)S(1)}, bf16[1024,128]{1,0:T(8,128)(2,1)S(1)}, u32[]{:S(2)}, u32[]{:S(2)}) collective-permute-start(bf16[1024,128]{1,0:T(8,128)(2,1)S(1)} %shard_map.41.rest_0_), channel_id=1, source_target_pairs={{0,8},{4,12},{8,0},{12,4},{1,9},{5,13},{9,1},{13,5},{2,10},{6,14},... | collective-permute-start | bytes 786440 | tf_op jit(solution)/shard_map/ppermute | solution.py:157
  42.3 9.2 %collective-permute-start.7 = (bf16[1024,128]{1,0:T(8,128)(2,1)S(1)}, bf16[1024,128]{1,0:T(8,128)(2,1)S(1)}, u32[]{:S(2)}, u32[]{:S(2)}) collective-permute-start(bf16[1024,128]{1,0:T(8,128)(2,1)S(1)} %collective-permute-done.6.rest_4_), channel_id=1, source_target_pairs={{0,16},{16,0},{1,17},{17,1},{2,18},{18,2},{3,19},{19,3},{4,20},{20... | collective-permute-start | bytes 786440 | tf_op jit(solution)/shard_map/ppermute | solution.py:163
  44.1 7.4 %collective-permute-start.8 = (bf16[1024,128]{1,0:T(8,128)(2,1)S(1)}, bf16[1024,128]{1,0:T(8,128)(2,1)S(1)}, u32[]{:S(2)}, u32[]{:S(2)}) collective-permute-start(bf16[1024,128]{1,0:T(8,128)(2,1)S(1)} %collective-permute-done.6.rest_4_), channel_id=1, source_target_pairs={{0,4},{4,0},{8,12},{12,8},{1,5},{5,1},{9,13},{13,9},{2,6},{6,2},{1... | collective-permute-start | bytes 786440 | tf_op jit(solution)/shard_map/ppermute | solution.py:160
  44.1 7.9 %collective-permute-start.5 = (bf16[1024,128]{1,0:T(8,128)(2,1)S(1)}, bf16[1024,128]{1,0:T(8,128)(2,1)S(1)}, u32[]{:S(2)}, u32[]{:S(2)}) collective-permute-start(bf16[1024,128]{1,0:T(8,128)(2,1)S(1)} %collective-permute-done.3.rest_1_), channel_id=1, source_target_pairs={{0,4},{4,0},{8,12},{12,8},{1,5},{5,1},{9,13},{13,9},{2,6},{6,2},{1... | collective-permute-start | bytes 786440 | tf_op jit(solution)/shard_map/ppermute | solution.py:160
  44.6 12.5 %collective-permute-start.15 = (bf16[1024,128]{1,0:T(8,128)(2,1)S(1)}, bf16[1024,128]{1,0:T(8,128)(2,1)S(1)}, u32[]{:S(2)}, u32[]{:S(2)}) collective-permute-start(bf16[1024,128]{1,0:T(8,128)(2,1)S(1)} %shard_map.41.rest_0_), channel_id=1, source_target_pairs={{0,16},{16,0},{1,17},{17,1},{2,18},{18,2},{3,19},{19,3},{4,20},{20... | collective-permute-start | bytes 786440 | tf_op jit(solution)/shard_map/ppermute | solution.py:163
  47.9 13.6 %collective-permute-start.19 = (bf16[1024,128]{1,0:T(8,128)(2,1)S(1)}, bf16[1024,128]{1,0:T(8,128)(2,1)S(1)}, u32[]{:S(2)}, u32[]{:S(2)}) collective-permute-start(bf16[1024,128]{1,0:T(8,128)(2,1)S(1)} %collective-permute-done.18.rest_4_), channel_id=1, source_target_pairs={{0,16},{16,0},{1,17},{17,1},{2,18},{18,2},{3,19},{19,3},{4,20},{20... | collective-permute-start | bytes 786440 | tf_op jit(solution)/shard_map/ppermute | solution.py:163
  51.5 10.0 %collective-permute-start.9 = (bf16[1024,128]{1,0:T(8,128)(2,1)S(1)}, bf16[1024,128]{1,0:T(8,128)(2,1)}, u32[]{:S(2)}, u32[]{:S(2)}) collective-permute-start(bf16[1024,128]{1,0:T(8,128)(2,1)S(1)} %collective-permute-done.7.rest_5_), channel_id=1, source_target_pairs={{0,4},{4,0},{8,12},{12,8},{1,5},{5,1},{9,13},{13,9},{2,6},{6,2},{1... | collective-permute-start | bytes 786440 | tf_op jit(solution)/shard_map/ppermute | solution.py:160
  51.5 19.8 %collective-permute-start.16 = (bf16[1024,128]{1,0:T(8,128)(2,1)S(1)}, bf16[1024,128]{1,0:T(8,128)(2,1)S(1)}, u32[]{:S(2)}, u32[]{:S(2)}) collective-permute-start(bf16[1024,128]{1,0:T(8,128)(2,1)S(1)} %shard_map.41.rest_0_), channel_id=1, source_target_pairs={{0,4},{4,0},{8,12},{12,8},{1,5},{5,1},{9,13},{13,9},{2,6},{6,2},{1... | collective-permute-start | bytes 786440 | tf_op jit(solution)/shard_map/ppermute | solution.py:160
  52.0 19.3 %collective-permute-start.20 = (bf16[1024,128]{1,0:T(8,128)(2,1)S(1)}, bf16[1024,128]{1,0:T(8,128)(2,1)S(1)}, u32[]{:S(2)}, u32[]{:S(2)}) collective-permute-start(bf16[1024,128]{1,0:T(8,128)(2,1)S(1)} %collective-permute-done.18.rest_4_), channel_id=1, source_target_pairs={{0,4},{4,0},{8,12},{12,8},{1,5},{5,1},{9,13},{13,9},{2,6},{6,2},{1... | collective-permute-start | bytes 786440 | tf_op jit(solution)/shard_map/ppermute | solution.py:160
  57.1 14.2 %collective-permute-start.17 = (bf16[1024,128]{1,0:T(8,128)(2,1)S(1)}, bf16[1024,128]{1,0:T(8,128)(2,1)}, u32[]{:S(2)}, u32[]{:S(2)}) collective-permute-start(bf16[1024,128]{1,0:T(8,128)(2,1)S(1)} %collective-permute-done.15.rest_1_), channel_id=1, source_target_pairs={{0,4},{4,0},{8,12},{12,8},{1,5},{5,1},{9,13},{13,9},{2,6},{6,2},{1... | collective-permute-start | bytes 786440 | tf_op jit(solution)/shard_map/ppermute | solution.py:160
  61.5 9.9 %collective-permute-start.21 = (bf16[1024,128]{1,0:T(8,128)(2,1)S(1)}, bf16[1024,128]{1,0:T(8,128)(2,1)}, u32[]{:S(2)}, u32[]{:S(2)}) collective-permute-start(bf16[1024,128]{1,0:T(8,128)(2,1)S(1)} %collective-permute-done.19.rest_5_), channel_id=1, source_target_pairs={{0,4},{4,0},{8,12},{12,8},{1,5},{5,1},{9,13},{13,9},{2,6},{6,2},{1... | collective-permute-start | bytes 786440 | tf_op jit(solution)/shard_map/ppermute | solution.py:160
  61.5 4.0 %copy-start.1 = (bf16[1280,4096]{1,0:T(8,128)(2,1)S(1)}, bf16[1280,4096]{1,0:T(8,128)(2,1)}, u32[]{:S(2)}) copy-start(bf16[1280,4096]{1,0:T(8,128)(2,1)} %copy-done) | copy-start | bytes 31457284
  69.8 10.6 %collective-permute-start.10 = (bf16[2,320,256]{2,1,0:T(8,128)(2,1)S(1)}, bf16[2,320,256]{2,1,0:T(8,128)(2,1)S(1)}, u32[]{:S(2)}, u32[]{:S(2)}) collective-permute-start(bf16[2,320,256]{2,1,0:T(8,128)(2,1)S(1)} %get-tuple-element.19), channel_id=1, source_target_pairs={{0,1},{1,0},{2,3},{3,2},{4,5},{5,4},{6,7},{7,6},{8,9},{9,8},{10,11... | collective-permute-start | bytes 983048 | tf_op jit(solution)/shard_map/ppermute | solution.py:166
  75.7 14.8 %collective-permute-start.22 = (bf16[2,320,256]{2,1,0:T(8,128)(2,1)S(1)}, bf16[2,320,256]{2,1,0:T(8,128)(2,1)S(1)}, u32[]{:S(2)}, u32[]{:S(2)}) collective-permute-start(bf16[2,320,256]{2,1,0:T(8,128)(2,1)S(1)} %get-tuple-element.24), channel_id=1, source_target_pairs={{0,1},{1,0},{2,3},{3,2},{4,5},{5,4},{6,7},{7,6},{8,9},{9,8},{10,11... | collective-permute-start | bytes 983048 | tf_op jit(solution)/shard_map/ppermute | solution.py:166
  80.4 12.0 %collective-permute-start.11 = (bf16[1,320,256]{2,1,0:T(8,128)(2,1)S(1)}, bf16[1,320,256]{2,1,0:T(8,128)(2,1)S(1)}, u32[]{:S(2)}, u32[]{:S(2)}) collective-permute-start(bf16[1,320,256]{2,1,0:T(8,128)(2,1)S(1)} %get-tuple-element.21), channel_id=1, source_target_pairs={{0,2},{1,3},{2,0},{3,1},{4,6},{5,7},{6,4},{7,5},{8,10},{9,11},{10,... | collective-permute-start | bytes 491528 | tf_op jit(solution)/shard_map/ppermute | solution.py:166
  90.6 10.3 %collective-permute-start.23 = (bf16[1,320,256]{2,1,0:T(8,128)(2,1)S(1)}, bf16[1,320,256]{2,1,0:T(8,128)(2,1)S(1)}, u32[]{:S(2)}, u32[]{:S(2)}) collective-permute-start(bf16[1,320,256]{2,1,0:T(8,128)(2,1)S(1)} %get-tuple-element.26), channel_id=1, source_target_pairs={{0,2},{1,3},{2,0},{3,1},{4,6},{5,7},{6,4},{7,5},{8,10},{9,11},{10,... | collective-permute-start | bytes 491528 | tf_op jit(solution)/shard_map/ppermute | solution.py:166

commit v2 on v1

v2 whole, which is shorter than its diff:
```python
import functools

import jax
import jax.numpy as jnp
from jax import lax
from jax.experimental import pallas as pl
from jax.experimental.pallas import tpu as pltpu
from jax.sharding import PartitionSpec as P

F32, BF16 = jnp.float32, jnp.bfloat16
CORES = 2
CHUNKS = 2
MIB = 1 << 20
VMEM = pl.BlockSpec(memory_space=pltpu.VMEM)
SMEM = pl.BlockSpec(memory_space=pltpu.SMEM)
ANY = pl.BlockSpec(memory_space=pl.ANY)


HBM = pl.BlockSpec(memory_space=pltpu.HBM)


def load_kernel(source, after, out, sem):
    copy = pltpu.make_async_copy(source, out, sem)
    copy.start()
    copy.wait()


def load(source, after):
    return pl.pallas_call(
        load_kernel,
        out_shape=pltpu.VMEM(source.shape, BF16),
        in_specs=[HBM, ANY],
        out_specs=VMEM,
        scratch_shapes=[pltpu.SemaphoreType.DMA],
        compiler_params=pltpu.CompilerParams(vmem_limit_bytes=2 * MIB),
        cost_estimate=pl.CostEstimate(flops=0, bytes_accessed=source.size * 2, transcendentals=0),
    )(pltpu.with_memory_space_constraint(source, pltpu.HBM), after)


def take_kernel(start, source, after, out, sem):
    at = pl.ds(pl.multiple_of(start[0], out.shape[0]), out.shape[0])
    copy = pltpu.make_async_copy(source.at[at, :], out, sem)
    copy.start()
    copy.wait()


def take(start, source, after, rows):
    return pl.pallas_call(
        take_kernel,
        out_shape=pltpu.VMEM((rows, source.shape[1]), BF16),
        in_specs=[SMEM, HBM, ANY],
        out_specs=VMEM,
        scratch_shapes=[pltpu.SemaphoreType.DMA],
        compiler_params=pltpu.CompilerParams(vmem_limit_bytes=2 * MIB),
        cost_estimate=pl.CostEstimate(flops=0, bytes_accessed=2 * rows * source.shape[1], transcendentals=0),
    )(start, pltpu.with_memory_space_constraint(source, pltpu.HBM), after)


def condition_kernel(count, ids, hess, *rest):
    pieces, out, right = rest[:count], rest[count], rest[count + 1]
    width = hess.shape[1] // count
    for t, piece in enumerate(pieces):
        right[:, pl.ds(pl.multiple_of(ids[t] * width, width), width)] = piece[...]
    out[...] = lax.dot_general(
        hess[...], right[...], (((1,), (1,)), ((), ())), preferred_element_type=F32
    ).astype(BF16)


def condition(ids, hess, pieces):
    rows, queries = hess.shape[0], pieces[0].shape[0]
    return pl.pallas_call(
        functools.partial(condition_kernel, len(pieces)),
        out_shape=jax.ShapeDtypeStruct((rows, queries), BF16),
        in_specs=[SMEM] + [VMEM] * (1 + len(pieces)),
        out_specs=VMEM,
        scratch_shapes=[pltpu.VMEM((queries, hess.shape[1]), BF16)],
        compiler_params=pltpu.CompilerParams(vmem_limit_bytes=12 * MIB),
        cost_estimate=pl.CostEstimate(
            flops=2 * queries * hess.size, bytes_accessed=hess.size * 2, transcendentals=0
        ),
    )(ids, hess, *pieces)


def score_kernel(groups, count, ids, blocks, store, *rest):
    pieces = rest[: groups * count]
    keep, *send, right = rest[groups * count :]
    rows = keep.shape[0]
    depth, width = pieces[0].shape
    for t in range(count):
        at = pl.ds(pl.multiple_of(ids[t] * depth, depth), depth)
        for j in range(groups):
            right[at, j * width : (j + 1) * width] = pieces[t * groups + j][...]
    for r in range(blocks.shape[0]):
        at = pl.ds(pl.multiple_of(blocks[r] * rows, rows), rows)
        part = jnp.dot(store[at, :], right[...], preferred_element_type=F32)
        if r:
            send[r - 1][...] = part.astype(BF16)
        else:
            keep[...] = part


def score(ids, blocks, store, pieces, groups):
    count = len(pieces) // groups
    depth, width = pieces[0].shape
    layers = blocks.shape[0]
    shape = (store.shape[0] // layers, groups * width)
    return pl.pallas_call(
        functools.partial(score_kernel, groups, count),
        out_shape=(jax.ShapeDtypeStruct(shape, F32),)
        + (jax.ShapeDtypeStruct(shape, BF16),) * (layers - 1),
        in_specs=[SMEM, SMEM] + [VMEM] * (1 + len(pieces)),
        out_specs=(VMEM,) * layers,
        scratch_shapes=[pltpu.VMEM((count * depth, groups * width), BF16)],
        compiler_params=pltpu.CompilerParams(vmem_limit_bytes=12 * MIB),
        cost_estimate=pl.CostEstimate(
            flops=2 * groups * width * store.size, bytes_accessed=store.size * 2, transcendentals=0
        ),
    )(ids, blocks, store, *pieces)


def finish_kernel(chunks, groups, place, *refs):
    *refs, out = refs
    span = out.shape[1] // groups
    width = span // chunks
    count = len(refs) // chunks
    for c in range(chunks):
        total = refs[c * count][...]
        for got in refs[c * count + 1 : (c + 1) * count]:
            total = total + got[...].astype(F32)
        for j in range(groups):
            at = pl.multiple_of(place[j] * span + c * width, width)
            out[:, pl.ds(at, width)] = total[:, j * width : (j + 1) * width]


def finish(place, parts, queries):
    groups = place.shape[0]
    rows = parts[0][0].shape[0]
    return pl.pallas_call(
        functools.partial(finish_kernel, len(parts), groups),
        out_shape=jax.ShapeDtypeStruct((rows, queries), F32),
        in_specs=[SMEM] + [VMEM] * sum(map(len, parts)),
        out_specs=VMEM,
        compiler_params=pltpu.CompilerParams(vmem_limit_bytes=12 * MIB),
    )(place, *[a for part in parts for a in part])


def shards(groups, ex, layers, queries, hessian, store):
    chips = ex // CORES
    at_group, at_ex, at_layer = (lax.axis_index(a) for a in ("groups", "ex", "layer"))
    chip, core = at_ex // CORES, at_ex % CORES
    ids = jnp.stack(
        [(chip + k) % chips * CORES + (core ^ s) for k in range(chips) for s in range(CORES)]
    ).astype(jnp.int32)
    blocks = jnp.stack([at_layer ^ r for r in range(layers)]).astype(jnp.int32)
    place = jnp.stack([(at_group + j) % groups for j in range(groups)]).astype(jnp.int32)

    def from_chip(x, k):
        perm = [(e, (e - k * CORES) % ex) for e in range(ex)]
        return lax.ppermute(x, "ex", perm)

    def from_core(x):
        return lax.ppermute(x, "ex", [(e, e ^ 1) for e in range(ex)])

    def from_group(x, j):
        return lax.ppermute(x, "groups", [(g, (g - j) % groups) for g in range(groups)])

    def from_layer(x, r):
        return lax.ppermute(x, "layer", [(z, z ^ r) for z in range(layers)])

    def tie(x, *others):
        return lax.optimization_barrier((x, *others))[0]

    total = queries.shape[0]
    span = total // groups
    width = span // CHUNKS

    pieces, last = [], ids
    for c in range(CHUNKS):
        start = (at_group * span + c * width).astype(jnp.int32)[None]
        mine = take(start, queries[:, 0, :], last, width)
        there = [from_chip(mine, k) for k in range(1, chips)]
        last = there[-1]
        pieces.append([p for x in [mine] + there for p in (x, from_core(x))])

    hess = load(hessian[0], ids)
    shares, held, last = [], [], ()
    for c in range(CHUNKS):
        share = condition(ids, hess, pieces[c])
        shares.append(share)
        share = tie(share, *last)
        columns = [share] + [from_chip(share, k) for k in range(1, chips)]
        first = [from_group(share, j) for j in range(1, groups)]
        last = columns[1:] + first
        held.append(
            [[columns[0]] + first]
            + [[x] + [from_group(x, j) for j in range(1, groups)] for x in columns[1:]]
        )

    rows = load(store[:, 0, :], shares[-1])
    parts, last = [], ()
    for c in range(CHUNKS):
        ready = [x for row in held[c] for x in row]
        flip = [from_core(tie(x, *last)) for x in ready]
        both = []
        for k in range(chips):
            at = slice(k * groups, (k + 1) * groups)
            both += ready[at] + flip[at]
        keep, *send = score(ids, blocks, rows, both, groups)
        last = [keep]
        parts.append([keep] + [from_layer(x, r + 1) for r, x in enumerate(send)])
    return finish(place, parts, total)


def solution(mesh):
    groups, ex, layers = (mesh.shape[a] for a in ("groups", "ex", "layer"))
    in_specs = (P(None, "layer", "ex"), P("layer", "ex", None), P(("groups", "ex"), "layer", None))
    out_specs = P(("groups", "ex", "layer"), None)
    return jax.shard_map(
        functools.partial(shards, groups, ex, layers),
        mesh=mesh,
        in_specs=in_specs,
        out_specs=out_specs,
        check_vma=False,
    )
```

time: 103 us -> 83.8 us (0.81)
  local copies, waits for them, and re-layouts: 16.4 us -> 0 us
  waiting for transfers between devices: 48.1 us -> 36.7 us
  Pallas kernels: 17.2 us -> 24.4 us
  starting transfers between devices: 20.4 us -> 21.8 us
    unnamed x8 -> x0, local copies, waits for them, and re-layouts: 15.3 us -> none
    ppermute x4, waiting for transfers between devices: 11.6 us -> 2.26 us  [from_group(): lax.ppermute(x, 'groups', [(g, (g - j) % groups) for g in range(groups)])]
    pallas_call x4 -> x5, Pallas kernels: 2.88 us -> 10.8 us  [the longest x2 7.38 us: load(): pl.pallas_call(load_kernel, out_shape=pltpu.VMEM(source.shape, BF16), in_...]
    ppermute x4 -> x6, starting transfers between devices: 6.45 us -> 8.93 us  [from_layer(): return lax.ppermute(x, 'layer', [(z, z ^ r) for z in range(layers)])]
    ppermute x4 -> x6, waiting for transfers between devices: 20.1 us -> 17.8 us  [from_layer(): return lax.ppermute(x, 'layer', [(z, z ^ r) for z in range(layers)])]
    ppermute x4, starting transfers between devices: 6.83 us -> 5.76 us  [from_chip(): return lax.ppermute(x, 'ex', perm)]
    dynamic_slice x1 -> x0, local copies, waits for them, and re-layouts: 1.06 us -> none  [shards(): lax.dynamic_slice_in_dim(queries[:, 0, :], at_group * span + c * width, w...]
  transfers between devices with their start and end apart: 24 -> 26, of which waited for: 10 -> 9; matrix products, arithmetic and copies ran while one was open for 0% -> 0% of each run, Pallas kernels for 15% -> 26%
where the time goes in v2:
time: 83.8 us; the launch traced here: 83.3 us
  waiting for transfers between devices  36.7 us (44%)
  Pallas kernels  24.4 us (29%)
  starting transfers between devices  21.8 us (26%)
    ppermute x6, waiting for transfers between devices, from_layer(): return lax.ppermute(x, 'layer', [(z, z ^ r) for z in range(layers)])  17.8 us
    ppermute x4, waiting for transfers between devices, from_chip(): return lax.ppermute(x, 'ex', perm)  16.6 us
    ppermute x6, starting transfers between devices, from_layer(): return lax.ppermute(x, 'layer', [(z, z ^ r) for z in range(layers)])  8.93 us
    pallas_call x2, Pallas kernels, score(): pl.pallas_call(functools.partial(score_kernel, groups, count), out_shape=...  7.69 us
    pallas_call x2, Pallas kernels, load(): pl.pallas_call(load_kernel, out_shape=pltpu.VMEM(source.shape, BF16), in_...  7.38 us
    pallas_call x2, Pallas kernels, condition(): pl.pallas_call(functools.partial(condition_kernel, len(pieces)), out_shap...  5.91 us
    ppermute x4, starting transfers between devices, from_chip(): return lax.ppermute(x, 'ex', perm)  5.76 us
    ppermute x4, starting transfers between devices, from_group(): lax.ppermute(x, 'groups', [(g, (g - j) % groups) for g in range(groups)])  5.23 us
  transfers between devices with their start and end apart: 26, of which 9 were waited for; matrix products, arithmetic and copies ran while one was open for 0% of the time, Pallas kernels for 26%

profile of v2, /device:TPU:0, one launch (start us, length us, event | category | flops | bytes accessed | tf_op | source)
XLA Modules:
  0.0 83.3 jit_solution(1357058608615899036)
XLA Ops:
  0.0 0.1 pad_add_fusion.1.after.ids
  0.1 1.0 %shard_map.38.rest_0_ = bf16[128,1024]{1,0:T(8,128)(2,1)S(1)} custom-call(s32[1]{0:T(128)} %bitcast.14.start, bf16[512,1024]{1,0:T(8,128)(2,1)} %bitcast.17, s32[4]{0:T(128)S(1)} %pad_add_fusion.1.after.ids), custom_call_target="tpu_custom_call" | custom-call | bytes 262144 | tf_op jit(solution)/shard_map/pallas_call | solution.py:48
  1.0 3.0 %collective-permute-start = (bf16[128,1024]{1,0:T(8,128)(2,1)S(1)}, bf16[128,1024]{1,0:T(8,128)(2,1)S(1)}, u32[]{:S(2)}, u32[]{:S(2)}) collective-permute-start(bf16[128,1024]{1,0:T(8,128)(2,1)S(1)} %shard_map.38.rest_0_), channel_id=1, source_target_pairs={{0,8},{4,12},{8,0},{12,4},{1,9},{5,13},{9,1},{13,5},{2,10},{6,14},... | collective-permute-start | bytes 786440 | tf_op jit(solution)/shard_map/ppermute | solution.py:159
  4.1 6.3 %collective-permute-done.after.rest_2_ = bf16[128,1024]{1,0:T(8,128)(2,1)S(1)} collective-permute-done((bf16[128,1024]{1,0:T(8,128)(2,1)S(1)}, bf16[128,1024]{1,0:T(8,128)(2,1)S(1)}, u32[]{:S(2)}, u32[]{:S(2)}) %collective-permute-start) | collective-permute-done | bytes 262176 | tf_op jit(solution)/shard_map/ppermute | solution.py:159
  10.4 0.0 collective-permute-start.5
  10.4 1.0 %shard_map.39.rest_0_ = bf16[128,1024]{1,0:T(8,128)(2,1)S(1)} custom-call(s32[1]{0:T(128)} %bitcast.12.start, bf16[512,1024]{1,0:T(8,128)(2,1)} %bitcast.18, bf16[128,1024]{1,0:T(8,128)(2,1)S(1)} %collective-permute-done.after.rest_2_), custom_call_target="tpu_custom_call" | custom-call | bytes 262144 | tf_op jit(solution)/shard_map/pallas_call | solution.py:48
  11.4 1.8 %collective-permute-start.2 = (bf16[128,1024]{1,0:T(8,128)(2,1)S(1)}, bf16[128,1024]{1,0:T(8,128)(2,1)S(1)}, u32[]{:S(2)}, u32[]{:S(2)}) collective-permute-start(bf16[128,1024]{1,0:T(8,128)(2,1)S(1)} %shard_map.39.rest_0_), channel_id=1, source_target_pairs={{0,8},{4,12},{8,0},{12,4},{1,9},{5,13},{9,1},{13,5},{2,10},{6,14},... | collective-permute-start | bytes 786440 | tf_op jit(solution)/shard_map/ppermute | solution.py:159
  13.2 3.4 %shard_map.37.hess = bf16[1024,4096]{1,0:T(8,128)(2,1)S(1)} custom-call(bf16[1024,4096]{1,0:T(8,128)(2,1)} %bitcast.16, s32[4]{0:T(128)S(1)} %pad_add_fusion.1.after.ids), custom_call_target="tpu_custom_call" | custom-call | bytes 8388608 | tf_op jit(solution)/shard_map/pallas_call | solution.py:29
  16.6 3.0 %shard_map.42.rest_0_ = bf16[1024,128]{1,0:T(8,128)(2,1)S(1)} custom-call(s32[4]{0:T(128)S(1)} %pad_add_fusion.1.after.ids, bf16[1024,4096]{1,0:T(8,128)(2,1)S(1)} %shard_map.37.hess, bf16[128,1024]{1,0:T(8,128)(2,1)S(1)} %shard_map.38.rest_0_, bf16[128,1024]{1,0:T(8,128)(2,1)S(1)} %collective-permute-done.4.rest_1_, ...), custom_call_target="tpu_custom_call" | custom-call | flops 1073741824 | bytes 8388608 | tf_op jit(solution)/shard_map/pallas_call | solution.py:71
  19.5 0.4 collective-permute-start.9
  19.9 0.0 collective-permute-start.1
  19.9 0.2 collective-permute-done.2.rest_2_
  20.1 0.3 collective-permute-start.3
  20.4 1.7 %collective-permute-start.6 = (bf16[1024,128]{1,0:T(8,128)(2,1)S(1)}, bf16[1024,128]{1,0:T(8,128)(2,1)S(1)}, u32[]{:S(2)}, u32[]{:S(2)}) collective-permute-start(bf16[1024,128]{1,0:T(8,128)(2,1)S(1)} %shard_map.42.rest_0_), channel_id=1, source_target_pairs={{0,16},{16,0},{1,17},{17,1},{2,18},{18,2},{3,19},{19,3},{4,20},{20... | collective-permute-start | bytes 786440 | tf_op jit(solution)/shard_map/ppermute | solution.py:165
  22.1 5.9 %collective-permute-done.9.rest_4_ = bf16[1024,128]{1,0:T(8,128)(2,1)S(1)} collective-permute-done((bf16[1024,128]{1,0:T(8,128)(2,1)S(1)}, bf16[1024,128]{1,0:T(8,128)(2,1)S(1)}, u32[]{:S(2)}, u32[]{:S(2)}) %collective-permute-start.9) | collective-permute-done | bytes 262176 | tf_op jit(solution)/shard_map/ppermute | solution.py:159
  28.0 1.5 %collective-permute-start.10 = (bf16[1024,128]{1,0:T(8,128)(2,1)S(1)}, bf16[1024,128]{1,0:T(8,128)(2,1)S(1)}, u32[]{:S(2)}, u32[]{:S(2)}) collective-permute-start(bf16[1024,128]{1,0:T(8,128)(2,1)S(1)} %collective-permute-done.9.rest_4_), channel_id=1, source_target_pairs={{0,16},{16,0},{1,17},{17,1},{2,18},{18,2},{3,19},{19,3},{4,20},{20... | collective-permute-start | bytes 786440 | tf_op jit(solution)/shard_map/ppermute | solution.py:165
  29.5 0.0 collective-permute-start.7
  29.5 0.0 collective-permute-done.1.rest_1_
  29.5 0.0 collective-permute-done.3.rest_3_
  29.5 3.0 %shard_map.40.after.rest_0_ = bf16[1024,128]{1,0:T(8,128)(2,1)S(1)} custom-call(s32[4]{0:T(128)S(1)} %pad_add_fusion.1.after.ids, bf16[1024,4096]{1,0:T(8,128)(2,1)S(1)} %shard_map.37.hess, bf16[128,1024]{1,0:T(8,128)(2,1)S(1)} %shard_map.39.rest_0_, bf16[128,1024]{1,0:T(8,128)(2,1)S(1)} %collective-permute-done.1.rest_1_, ...), custom_call_target="tpu_custom_call" | custom-call | flops 1073741824 | bytes 8388608 | tf_op jit(solution)/shard_map/pallas_call | solution.py:71
  32.5 0.0 collective-permute-done.6.rest_1_
  32.5 0.6 collective-permute-start.19
  33.1 0.2 collective-permute-start.11
  33.3 0.3 collective-permute-start.8
  33.6 2.1 %collective-permute-done.10.rest_5_ = bf16[1024,128]{1,0:T(8,128)(2,1)S(1)} collective-permute-done((bf16[1024,128]{1,0:T(8,128)(2,1)S(1)}, bf16[1024,128]{1,0:T(8,128)(2,1)S(1)}, u32[]{:S(2)}, u32[]{:S(2)}) %collective-permute-start.10) | collective-permute-done | bytes 262176 | tf_op jit(solution)/shard_map/ppermute | solution.py:165
  35.7 0.0 collective-permute-start.12
  35.7 1.5 %collective-permute-start.16 = (bf16[1024,128]{1,0:T(8,128)(2,1)S(1)}, bf16[1024,128]{1,0:T(8,128)(2,1)S(1)}, u32[]{:S(2)}, u32[]{:S(2)}) collective-permute-start(bf16[1024,128]{1,0:T(8,128)(2,1)S(1)} %shard_map.40.after.rest_0_), channel_id=1, source_target_pairs={{0,16},{16,0},{1,17},{17,1},{2,18},{18,2},{3,19},{19,3},{4,20},{20... | collective-permute-start | bytes 786440 | tf_op jit(solution)/shard_map/ppermute | solution.py:165
  37.2 4.1 %collective-permute-done.19.rest_4_ = bf16[1024,128]{1,0:T(8,128)(2,1)S(1)} collective-permute-done((bf16[1024,128]{1,0:T(8,128)(2,1)S(1)}, bf16[1024,128]{1,0:T(8,128)(2,1)S(1)}, u32[]{:S(2)}, u32[]{:S(2)}) %collective-permute-start.19) | collective-permute-done | bytes 262176 | tf_op jit(solution)/shard_map/ppermute | solution.py:159
  41.3 0.5 collective-permute-start.20
  41.8 0.1 pad_add_fusion.2.blocks
  41.9 4.0 %shard_map.41.store = bf16[1280,4096]{1,0:T(8,128)(2,1)S(1)} custom-call(bf16[1280,4096]{1,0:T(8,128)(2,1)} %bitcast.15, bf16[1024,128]{1,0:T(8,128)(2,1)S(1)} %shard_map.40.after.rest_0_), custom_call_target="tpu_custom_call" | custom-call | bytes 10485760 | tf_op jit(solution)/shard_map/pallas_call | solution.py:29
  45.9 3.8 %shard_map.43 = (f32[320,256]{1,0:T(8,128)S(1)}, bf16[320,256]{1,0:T(8,128)(2,1)S(1)}, bf16[320,256]{1,0:T(8,128)(2,1)S(1)}, bf16[320,256]{1,0:T(8,128)(2,1)S(1)}) custom-call(s32[4]{0:T(128)S(1)} %pad_add_fusion.1.after.ids, s32[4]{0:T(128)S(1)} %pad_add_fusion.2.blocks, bf16[1280,4096]{1,0:T(8,128)(2,1)S(1)} %shard_map.41.store, ...), custom_call_target="tpu_custom_call" | custom-call | flops 2684354560 | bytes 10485760 | tf_op jit(solution)/shard_map/pallas_call | solution.py:107
  49.8 0.2 collective-permute-done.20.rest_5_
  50.0 0.5 collective-permute-start.21
  50.5 0.0 collective-permute-start.18
  50.5 0.5 collective-permute-start.17
  51.0 1.6 %collective-permute-start.13 = (bf16[320,256]{1,0:T(8,128)(2,1)S(1)}, bf16[320,256]{1,0:T(8,128)(2,1)S(1)}, u32[]{:S(2)}, u32[]{:S(2)}) collective-permute-start(bf16[320,256]{1,0:T(8,128)(2,1)S(1)} %get-tuple-element.19), channel_id=1, source_target_pairs={{0,1},{1,0},{2,3},{3,2},{4,5},{5,4},{6,7},{7,6},{8,9},{9,8},{10,11... | collective-permute-start | bytes 491528 | tf_op jit(solution)/shard_map/ppermute | solution.py:168
  52.6 2.6 %collective-permute-start.14 = (bf16[320,256]{1,0:T(8,128)(2,1)S(1)}, bf16[320,256]{1,0:T(8,128)(2,1)S(1)}, u32[]{:S(2)}, u32[]{:S(2)}) collective-permute-start(bf16[320,256]{1,0:T(8,128)(2,1)S(1)} %get-tuple-element.20), channel_id=1, source_target_pairs={{0,2},{1,3},{2,0},{3,1},{4,6},{5,7},{6,4},{7,5},{8,10},{9,11},{10,... | collective-permute-start | bytes 491528 | tf_op jit(solution)/shard_map/ppermute | solution.py:168
  55.2 0.3 collective-permute-start.15
  55.5 3.8 %shard_map.44 = (f32[320,256]{1,0:T(8,128)S(1)}, bf16[320,256]{1,0:T(8,128)(2,1)S(1)}, bf16[320,256]{1,0:T(8,128)(2,1)S(1)}, bf16[320,256]{1,0:T(8,128)(2,1)S(1)}) custom-call(s32[4]{0:T(128)S(1)} %pad_add_fusion.1.after.ids, s32[4]{0:T(128)S(1)} %pad_add_fusion.2.blocks, bf16[1280,4096]{1,0:T(8,128)(2,1)S(1)} %shard_map.41.store, ...), custom_call_target="tpu_custom_call" | custom-call | flops 2684354560 | bytes 10485760 | tf_op jit(solution)/shard_map/pallas_call | solution.py:107
  59.4 0.7 collective-permute-start.23
  60.0 3.5 %collective-permute-start.24 = (bf16[320,256]{1,0:T(8,128)(2,1)S(1)}, bf16[320,256]{1,0:T(8,128)(2,1)S(1)}, u32[]{:S(2)}, u32[]{:S(2)}) collective-permute-start(bf16[320,256]{1,0:T(8,128)(2,1)S(1)} %get-tuple-element.29), channel_id=1, source_target_pairs={{0,2},{1,3},{2,0},{3,1},{4,6},{5,7},{6,4},{7,5},{8,10},{9,11},{10,... | collective-permute-start | bytes 491528 | tf_op jit(solution)/shard_map/ppermute | solution.py:168
  63.5 0.3 collective-permute-start.25
  63.8 0.1 pad_add_fusion.place
  63.9 3.8 %collective-permute-done.14.refs_2_ = bf16[320,256]{1,0:T(8,128)(2,1)S(1)} collective-permute-done((bf16[320,256]{1,0:T(8,128)(2,1)S(1)}, bf16[320,256]{1,0:T(8,128)(2,1)S(1)}, u32[]{:S(2)}, u32[]{:S(2)}) %collective-permute-start.14) | collective-permute-done | bytes 163872 | tf_op jit(solution)/shard_map/ppermute | solution.py:168
  67.7 2.2 %collective-permute-done.23.refs_5_ = bf16[320,256]{1,0:T(8,128)(2,1)S(1)} collective-permute-done((bf16[320,256]{1,0:T(8,128)(2,1)S(1)}, bf16[320,256]{1,0:T(8,128)(2,1)S(1)}, u32[]{:S(2)}, u32[]{:S(2)}) %collective-permute-start.23) | collective-permute-done | bytes 163872 | tf_op jit(solution)/shard_map/ppermute | solution.py:168
  69.8 11.9 %collective-permute-done.24.refs_6_ = bf16[320,256]{1,0:T(8,128)(2,1)S(1)} collective-permute-done((bf16[320,256]{1,0:T(8,128)(2,1)S(1)}, bf16[320,256]{1,0:T(8,128)(2,1)S(1)}, u32[]{:S(2)}, u32[]{:S(2)}) %collective-permute-start.24) | collective-permute-done | bytes 163872 | tf_op jit(solution)/shard_map/ppermute | solution.py:168
  81.7 1.5 %shard_map.45 = f32[320,512]{1,0:T(8,128)} custom-call(s32[2]{0:T(128)S(1)} %pad_add_fusion.place, f32[320,256]{1,0:T(8,128)S(1)} %get-tuple-element.18.refs_0_, bf16[320,256]{1,0:T(8,128)(2,1)S(1)} %collective-permute-done.13.refs_1_, bf16[320,256]{1,0:T(8,128)(2,1)S(1)} %collective-permute-done.14.refs_2_, ...), custom_call_target="tpu_custom_call" | custom-call | tf_op jit(solution)/shard_map/pallas_call | solution.py:138
  (16 shorter events, 0.0 us)
Async XLA Ops:
  1.0 9.3 %collective-permute-start = (bf16[128,1024]{1,0:T(8,128)(2,1)S(1)}, bf16[128,1024]{1,0:T(8,128)(2,1)S(1)}, u32[]{:S(2)}, u32[]{:S(2)}) collective-permute-start(bf16[128,1024]{1,0:T(8,128)(2,1)S(1)} %shard_map.38.rest_0_), channel_id=1, source_target_pairs={{0,8},{4,12},{8,0},{12,4},{1,9},{5,13},{9,1},{13,5},{2,10},{6,14},... | collective-permute-start | bytes 786440 | tf_op jit(solution)/shard_map/ppermute | solution.py:159
  4.1 12.5 %collective-permute-start.4 = (bf16[128,1024]{1,0:T(8,128)(2,1)S(1)}, bf16[128,1024]{1,0:T(8,128)(2,1)S(1)}, u32[]{:S(2)}, u32[]{:S(2)}) collective-permute-start(bf16[128,1024]{1,0:T(8,128)(2,1)S(1)} %shard_map.38.rest_0_), channel_id=1, source_target_pairs={{0,4},{4,0},{8,12},{12,8},{1,5},{5,1},{9,13},{13,9},{2,6},{6,2},{1... | collective-permute-start | bytes 786440 | tf_op jit(solution)/shard_map/ppermute | solution.py:162
  10.4 6.2 %collective-permute-start.5 = (bf16[128,1024]{1,0:T(8,128)(2,1)S(1)}, bf16[128,1024]{1,0:T(8,128)(2,1)S(1)}, u32[]{:S(2)}, u32[]{:S(2)}) collective-permute-start(bf16[128,1024]{1,0:T(8,128)(2,1)S(1)} %collective-permute-done.after.rest_2_), channel_id=1, source_target_pairs={{0,4},{4,0},{8,12},{12,8},{1,5},{5,1},{9,13},{13,9},{2,6},{6,2},{1... | collective-permute-start | bytes 786440 | tf_op jit(solution)/shard_map/ppermute | solution.py:162
  11.4 8.8 %collective-permute-start.2 = (bf16[128,1024]{1,0:T(8,128)(2,1)S(1)}, bf16[128,1024]{1,0:T(8,128)(2,1)S(1)}, u32[]{:S(2)}, u32[]{:S(2)}) collective-permute-start(bf16[128,1024]{1,0:T(8,128)(2,1)S(1)} %shard_map.39.rest_0_), channel_id=1, source_target_pairs={{0,8},{4,12},{8,0},{12,4},{1,9},{5,13},{9,1},{13,5},{2,10},{6,14},... | collective-permute-start | bytes 786440 | tf_op jit(solution)/shard_map/ppermute | solution.py:159
  19.5 8.5 %collective-permute-start.9 = (bf16[1024,128]{1,0:T(8,128)(2,1)S(1)}, bf16[1024,128]{1,0:T(8,128)(2,1)S(1)}, u32[]{:S(2)}, u32[]{:S(2)}) collective-permute-start(bf16[1024,128]{1,0:T(8,128)(2,1)S(1)} %shard_map.42.rest_0_), channel_id=1, source_target_pairs={{0,8},{4,12},{8,0},{12,4},{1,9},{5,13},{9,1},{13,5},{2,10},{6,14},... | collective-permute-start | bytes 786440 | tf_op jit(solution)/shard_map/ppermute | solution.py:159
  19.9 9.7 %collective-permute-start.1 = (bf16[128,1024]{1,0:T(8,128)(2,1)S(1)}, bf16[128,1024]{1,0:T(8,128)(2,1)S(1)}, u32[]{:S(2)}, u32[]{:S(2)}) collective-permute-start(bf16[128,1024]{1,0:T(8,128)(2,1)S(1)} %shard_map.39.rest_0_), channel_id=1, source_target_pairs={{0,4},{4,0},{8,12},{12,8},{1,5},{5,1},{9,13},{13,9},{2,6},{6,2},{1... | collective-permute-start | bytes 786440 | tf_op jit(solution)/shard_map/ppermute | solution.py:162
  20.1 9.4 %collective-permute-start.3 = (bf16[128,1024]{1,0:T(8,128)(2,1)S(1)}, bf16[128,1024]{1,0:T(8,128)(2,1)S(1)}, u32[]{:S(2)}, u32[]{:S(2)}) collective-permute-start(bf16[128,1024]{1,0:T(8,128)(2,1)S(1)} %collective-permute-done.2.rest_2_), channel_id=1, source_target_pairs={{0,4},{4,0},{8,12},{12,8},{1,5},{5,1},{9,13},{13,9},{2,6},{6,2},{1... | collective-permute-start | bytes 786440 | tf_op jit(solution)/shard_map/ppermute | solution.py:162
  20.4 12.1 %collective-permute-start.6 = (bf16[1024,128]{1,0:T(8,128)(2,1)S(1)}, bf16[1024,128]{1,0:T(8,128)(2,1)S(1)}, u32[]{:S(2)}, u32[]{:S(2)}) collective-permute-start(bf16[1024,128]{1,0:T(8,128)(2,1)S(1)} %shard_map.42.rest_0_), channel_id=1, source_target_pairs={{0,16},{16,0},{1,17},{17,1},{2,18},{18,2},{3,19},{19,3},{4,20},{20... | collective-permute-start | bytes 786440 | tf_op jit(solution)/shard_map/ppermute | solution.py:165
  28.0 7.6 %collective-permute-start.10 = (bf16[1024,128]{1,0:T(8,128)(2,1)S(1)}, bf16[1024,128]{1,0:T(8,128)(2,1)S(1)}, u32[]{:S(2)}, u32[]{:S(2)}) collective-permute-start(bf16[1024,128]{1,0:T(8,128)(2,1)S(1)} %collective-permute-done.9.rest_4_), channel_id=1, source_target_pairs={{0,16},{16,0},{1,17},{17,1},{2,18},{18,2},{3,19},{19,3},{4,20},{20... | collective-permute-start | bytes 786440 | tf_op jit(solution)/shard_map/ppermute | solution.py:165
  29.5 6.1 %collective-permute-start.7 = (bf16[1024,128]{1,0:T(8,128)(2,1)S(1)}, bf16[1024,128]{1,0:T(8,128)(2,1)S(1)}, u32[]{:S(2)}, u32[]{:S(2)}) collective-permute-start(bf16[1024,128]{1,0:T(8,128)(2,1)S(1)} %shard_map.42.rest_0_), channel_id=1, source_target_pairs={{0,4},{4,0},{8,12},{12,8},{1,5},{5,1},{9,13},{13,9},{2,6},{6,2},{1... | collective-permute-start | bytes 786440 | tf_op jit(solution)/shard_map/ppermute | solution.py:162
  32.5 8.8 %collective-permute-start.19 = (bf16[1024,128]{1,0:T(8,128)(2,1)S(1)}, bf16[1024,128]{1,0:T(8,128)(2,1)S(1)}, u32[]{:S(2)}, u32[]{:S(2)}) collective-permute-start(bf16[1024,128]{1,0:T(8,128)(2,1)S(1)} %shard_map.40.after.rest_0_), channel_id=1, source_target_pairs={{0,8},{4,12},{8,0},{12,4},{1,9},{5,13},{9,1},{13,5},{2,10},{6,14},... | collective-permute-start | bytes 786440 | tf_op jit(solution)/shard_map/ppermute | solution.py:159
  33.1 12.8 %collective-permute-start.11 = (bf16[1024,128]{1,0:T(8,128)(2,1)S(1)}, bf16[1024,128]{1,0:T(8,128)(2,1)S(1)}, u32[]{:S(2)}, u32[]{:S(2)}) collective-permute-start(bf16[1024,128]{1,0:T(8,128)(2,1)S(1)} %collective-permute-done.9.rest_4_), channel_id=1, source_target_pairs={{0,4},{4,0},{8,12},{12,8},{1,5},{5,1},{9,13},{13,9},{2,6},{6,2},{1... | collective-permute-start | bytes 786440 | tf_op jit(solution)/shard_map/ppermute | solution.py:162
  33.3 12.6 %collective-permute-start.8 = (bf16[1024,128]{1,0:T(8,128)(2,1)S(1)}, bf16[1024,128]{1,0:T(8,128)(2,1)S(1)}, u32[]{:S(2)}, u32[]{:S(2)}) collective-permute-start(bf16[1024,128]{1,0:T(8,128)(2,1)S(1)} %collective-permute-done.6.rest_1_), channel_id=1, source_target_pairs={{0,4},{4,0},{8,12},{12,8},{1,5},{5,1},{9,13},{13,9},{2,6},{6,2},{1... | collective-permute-start | bytes 786440 | tf_op jit(solution)/shard_map/ppermute | solution.py:162
  35.7 10.3 %collective-permute-start.12 = (bf16[1024,128]{1,0:T(8,128)(2,1)S(1)}, bf16[1024,128]{1,0:T(8,128)(2,1)S(1)}, u32[]{:S(2)}, u32[]{:S(2)}) collective-permute-start(bf16[1024,128]{1,0:T(8,128)(2,1)S(1)} %collective-permute-done.10.rest_5_), channel_id=1, source_target_pairs={{0,4},{4,0},{8,12},{12,8},{1,5},{5,1},{9,13},{13,9},{2,6},{6,2},{1... | collective-permute-start | bytes 786440 | tf_op jit(solution)/shard_map/ppermute | solution.py:162
  35.7 14.9 %collective-permute-start.16 = (bf16[1024,128]{1,0:T(8,128)(2,1)S(1)}, bf16[1024,128]{1,0:T(8,128)(2,1)S(1)}, u32[]{:S(2)}, u32[]{:S(2)}) collective-permute-start(bf16[1024,128]{1,0:T(8,128)(2,1)S(1)} %shard_map.40.after.rest_0_), channel_id=1, source_target_pairs={{0,16},{16,0},{1,17},{17,1},{2,18},{18,2},{3,19},{19,3},{4,20},{20... | collective-permute-start | bytes 786440 | tf_op jit(solution)/shard_map/ppermute | solution.py:165
  41.3 8.7 %collective-permute-start.20 = (bf16[1024,128]{1,0:T(8,128)(2,1)S(1)}, bf16[1024,128]{1,0:T(8,128)(2,1)S(1)}, u32[]{:S(2)}, u32[]{:S(2)}) collective-permute-start(bf16[1024,128]{1,0:T(8,128)(2,1)S(1)} %collective-permute-done.19.rest_4_), channel_id=1, source_target_pairs={{0,16},{16,0},{1,17},{17,1},{2,18},{18,2},{3,19},{19,3},{4,20},{20... | collective-permute-start | bytes 786440 | tf_op jit(solution)/shard_map/ppermute | solution.py:165
  50.0 2.6 %collective-permute-start.22 = (bf16[1024,128]{1,0:T(8,128)(2,1)S(1)}, bf16[1024,128]{1,0:T(8,128)(2,1)S(1)}, u32[]{:S(2)}, u32[]{:S(2)}) collective-permute-start(bf16[1024,128]{1,0:T(8,128)(2,1)S(1)} %collective-permute-done.20.rest_5_), channel_id=1, source_target_pairs={{0,4},{4,0},{8,12},{12,8},{1,5},{5,1},{9,13},{13,9},{2,6},{6,2},{1... | collective-permute-start | bytes 786440 | tf_op jit(solution)/shard_map/ppermute | solution.py:162
  50.0 5.2 %collective-permute-start.21 = (bf16[1024,128]{1,0:T(8,128)(2,1)S(1)}, bf16[1024,128]{1,0:T(8,128)(2,1)S(1)}, u32[]{:S(2)}, u32[]{:S(2)}) collective-permute-start(bf16[1024,128]{1,0:T(8,128)(2,1)S(1)} %collective-permute-done.19.rest_4_), channel_id=1, source_target_pairs={{0,4},{4,0},{8,12},{12,8},{1,5},{5,1},{9,13},{13,9},{2,6},{6,2},{1... | collective-permute-start | bytes 786440 | tf_op jit(solution)/shard_map/ppermute | solution.py:162
  50.5 5.0 %collective-permute-start.18 = (bf16[1024,128]{1,0:T(8,128)(2,1)S(1)}, bf16[1024,128]{1,0:T(8,128)(2,1)S(1)}, u32[]{:S(2)}, u32[]{:S(2)}) collective-permute-start(bf16[1024,128]{1,0:T(8,128)(2,1)S(1)} %collective-permute-done.16.rest_1_), channel_id=1, source_target_pairs={{0,4},{4,0},{8,12},{12,8},{1,5},{5,1},{9,13},{13,9},{2,6},{6,2},{1... | collective-permute-start | bytes 786440 | tf_op jit(solution)/shard_map/ppermute | solution.py:162
  50.5 5.0 %collective-permute-start.17 = (bf16[1024,128]{1,0:T(8,128)(2,1)S(1)}, bf16[1024,128]{1,0:T(8,128)(2,1)S(1)}, u32[]{:S(2)}, u32[]{:S(2)}) collective-permute-start(bf16[1024,128]{1,0:T(8,128)(2,1)S(1)} %shard_map.40.after.rest_0_), channel_id=1, source_target_pairs={{0,4},{4,0},{8,12},{12,8},{1,5},{5,1},{9,13},{13,9},{2,6},{6,2},{1... | collective-permute-start | bytes 786440 | tf_op jit(solution)/shard_map/ppermute | solution.py:162
  51.0 12.5 %collective-permute-start.13 = (bf16[320,256]{1,0:T(8,128)(2,1)S(1)}, bf16[320,256]{1,0:T(8,128)(2,1)S(1)}, u32[]{:S(2)}, u32[]{:S(2)}) collective-permute-start(bf16[320,256]{1,0:T(8,128)(2,1)S(1)} %get-tuple-element.19), channel_id=1, source_target_pairs={{0,1},{1,0},{2,3},{3,2},{4,5},{5,4},{6,7},{7,6},{8,9},{9,8},{10,11... | collective-permute-start | bytes 491528 | tf_op jit(solution)/shard_map/ppermute | solution.py:168
  52.6 15.1 %collective-permute-start.14 = (bf16[320,256]{1,0:T(8,128)(2,1)S(1)}, bf16[320,256]{1,0:T(8,128)(2,1)S(1)}, u32[]{:S(2)}, u32[]{:S(2)}) collective-permute-start(bf16[320,256]{1,0:T(8,128)(2,1)S(1)} %get-tuple-element.20), channel_id=1, source_target_pairs={{0,2},{1,3},{2,0},{3,1},{4,6},{5,7},{6,4},{7,5},{8,10},{9,11},{10,... | collective-permute-start | bytes 491528 | tf_op jit(solution)/shard_map/ppermute | solution.py:168
  55.2 12.5 %collective-permute-start.15 = (bf16[320,256]{1,0:T(8,128)(2,1)S(1)}, bf16[320,256]{1,0:T(8,128)(2,1)S(1)}, u32[]{:S(2)}, u32[]{:S(2)}) collective-permute-start(bf16[320,256]{1,0:T(8,128)(2,1)S(1)} %get-tuple-element.21), channel_id=1, source_target_pairs={{0,3},{1,2},{2,1},{3,0},{4,7},{5,6},{6,5},{7,4},{8,11},{9,10},{10,... | collective-permute-start | bytes 491528 | tf_op jit(solution)/shard_map/ppermute | solution.py:168
  59.4 10.5 %collective-permute-start.23 = (bf16[320,256]{1,0:T(8,128)(2,1)S(1)}, bf16[320,256]{1,0:T(8,128)(2,1)S(1)}, u32[]{:S(2)}, u32[]{:S(2)}) collective-permute-start(bf16[320,256]{1,0:T(8,128)(2,1)S(1)} %get-tuple-element.28), channel_id=1, source_target_pairs={{0,1},{1,0},{2,3},{3,2},{4,5},{5,4},{6,7},{7,6},{8,9},{9,8},{10,11... | collective-permute-start | bytes 491528 | tf_op jit(solution)/shard_map/ppermute | solution.py:168
  60.0 21.7 %collective-permute-start.24 = (bf16[320,256]{1,0:T(8,128)(2,1)S(1)}, bf16[320,256]{1,0:T(8,128)(2,1)S(1)}, u32[]{:S(2)}, u32[]{:S(2)}) collective-permute-start(bf16[320,256]{1,0:T(8,128)(2,1)S(1)} %get-tuple-element.29), channel_id=1, source_target_pairs={{0,2},{1,3},{2,0},{3,1},{4,6},{5,7},{6,4},{7,5},{8,10},{9,11},{10,... | collective-permute-start | bytes 491528 | tf_op jit(solution)/shard_map/ppermute | solution.py:168
  63.5 18.2 %collective-permute-start.25 = (bf16[320,256]{1,0:T(8,128)(2,1)S(1)}, bf16[320,256]{1,0:T(8,128)(2,1)S(1)}, u32[]{:S(2)}, u32[]{:S(2)}) collective-permute-start(bf16[320,256]{1,0:T(8,128)(2,1)S(1)} %get-tuple-element.30), channel_id=1, source_target_pairs={{0,3},{1,2},{2,1},{3,0},{4,7},{5,6},{6,5},{7,4},{8,11},{9,10},{10,... | collective-permute-start | bytes 491528 | tf_op jit(solution)/shard_map/ppermute | solution.py:168

commit v3 on v2

v3 whole, which is shorter than its diff:
```python
import functools

import jax
import jax.numpy as jnp
from jax import lax
from jax.experimental import pallas as pl
from jax.experimental.pallas import tpu as pltpu
from jax.sharding import PartitionSpec as P

F32, BF16 = jnp.float32, jnp.bfloat16
CORES = 2
CHUNKS = 2
MIB = 1 << 20
VMEM = pl.BlockSpec(memory_space=pltpu.VMEM)
SMEM = pl.BlockSpec(memory_space=pltpu.SMEM)
ANY = pl.BlockSpec(memory_space=pl.ANY)


HBM = pl.BlockSpec(memory_space=pltpu.HBM)


def load_kernel(source, after, out, sem):
    copy = pltpu.make_async_copy(source, out, sem)
    copy.start()
    copy.wait()


def load(source, after):
    return pl.pallas_call(
        load_kernel,
        out_shape=pltpu.VMEM(source.shape, BF16),
        in_specs=[HBM, ANY],
        out_specs=VMEM,
        scratch_shapes=[pltpu.SemaphoreType.DMA],
        compiler_params=pltpu.CompilerParams(vmem_limit_bytes=2 * MIB),
    )(pltpu.with_memory_space_constraint(source, pltpu.HBM), after)


def take_kernel(start, source, after, out, sem):
    at = pl.ds(pl.multiple_of(start[0], out.shape[0]), out.shape[0])
    copy = pltpu.make_async_copy(source.at[at, :], out, sem)
    copy.start()
    copy.wait()


def take(start, source, after, rows):
    return pl.pallas_call(
        take_kernel,
        out_shape=pltpu.VMEM((rows, source.shape[1]), BF16),
        in_specs=[SMEM, HBM, ANY],
        out_specs=VMEM,
        scratch_shapes=[pltpu.SemaphoreType.DMA],
        compiler_params=pltpu.CompilerParams(vmem_limit_bytes=2 * MIB),
    )(start, pltpu.with_memory_space_constraint(source, pltpu.HBM), after)


def condition_kernel(count, ids, hess, *rest):
    pieces, (_, out, right) = rest[:count], rest[count:]
    width = hess.shape[1] // count
    for t, piece in enumerate(pieces):
        right[:, pl.ds(pl.multiple_of(ids[t] * width, width), width)] = piece[...]
    out[...] = lax.dot_general(
        hess[...], right[...], (((1,), (1,)), ((), ())), preferred_element_type=F32
    ).astype(BF16)


def condition(ids, hess, pieces, after):
    rows, queries = hess.shape[0], pieces[0].shape[0]
    return pl.pallas_call(
        functools.partial(condition_kernel, len(pieces)),
        out_shape=jax.ShapeDtypeStruct((rows, queries), BF16),
        in_specs=[SMEM] + [VMEM] * (1 + len(pieces)) + [ANY],
        out_specs=VMEM,
        scratch_shapes=[pltpu.VMEM((queries, hess.shape[1]), BF16)],
        compiler_params=pltpu.CompilerParams(vmem_limit_bytes=12 * MIB),
    )(ids, hess, *pieces, after)


def score_kernel(count, ids, blocks, store, *rest):
    pieces, (_, send, keep, right) = rest[:count], rest[count:]
    rows = keep.shape[1]
    depth = pieces[0].shape[0]
    for t, piece in enumerate(pieces):
        right[pl.ds(pl.multiple_of(ids[t] * depth, depth), depth), :] = piece[...]
    for r in [*range(1, blocks.shape[0], 2), *range(0, blocks.shape[0], 2)]:
        at = pl.ds(pl.multiple_of(blocks[r] * rows, rows), rows)
        part = jnp.dot(store[at, :], right[...], preferred_element_type=F32)
        if r % 2:
            send[r // 2] = part.astype(BF16)
        else:
            keep[r // 2] = part


def score(ids, blocks, store, pieces, after):
    depth, width = pieces[0].shape
    layers = blocks.shape[0]
    shape = (layers // 2, store.shape[0] // layers, width)
    return pl.pallas_call(
        functools.partial(score_kernel, len(pieces)),
        out_shape=(jax.ShapeDtypeStruct(shape, BF16), jax.ShapeDtypeStruct(shape, F32)),
        in_specs=[SMEM, SMEM] + [VMEM] * (1 + len(pieces)) + [ANY],
        out_specs=(VMEM, VMEM),
        scratch_shapes=[pltpu.VMEM((len(pieces) * depth, width), BF16)],
        compiler_params=pltpu.CompilerParams(vmem_limit_bytes=12 * MIB),
    )(ids, blocks, store, *pieces, after)


def fold_kernel(keep, got, _, send, left):
    for r in range(keep.shape[0]):
        total = keep[r] + got[r].astype(F32)
        if r % 2:
            send[r // 2] = total.astype(BF16)
        else:
            left[r // 2] = total


def fold(keep, got, after):
    shape = (keep.shape[0] // 2,) + keep.shape[1:]
    return pl.pallas_call(
        fold_kernel,
        out_shape=(jax.ShapeDtypeStruct(shape, BF16), jax.ShapeDtypeStruct(shape, F32)),
        in_specs=[VMEM, VMEM, ANY],
        out_specs=(VMEM, VMEM),
        compiler_params=pltpu.CompilerParams(vmem_limit_bytes=4 * MIB),
    )(keep, got, after)


def finish_kernel(groups, place, *refs):
    *refs, out = refs
    width = refs[0].shape[2]
    pieces = out.shape[1] // width
    for c in range(pieces // groups):
        for j in range(groups):
            keep, got = refs[2 * (c * groups + j) : 2 * (c * groups + j + 1)]
            at = place[j] * (out.shape[1] // groups) + c * width
            out[:, pl.ds(pl.multiple_of(at, width), width)] = keep[0] + got[0].astype(F32)


def finish(place, parts, queries):
    groups = place.shape[0]
    rows = parts[0][0].shape[1]
    return pl.pallas_call(
        functools.partial(finish_kernel, groups),
        out_shape=jax.ShapeDtypeStruct((rows, queries), F32),
        in_specs=[SMEM] + [VMEM] * sum(map(len, parts)),
        out_specs=VMEM,
        compiler_params=pltpu.CompilerParams(vmem_limit_bytes=12 * MIB),
    )(place, *[a for part in parts for a in part])


def shards(groups, ex, layers, queries, hessian, store):
    chips = ex // CORES
    at_group, at_ex, at_layer = (lax.axis_index(a) for a in ("groups", "ex", "layer"))
    chip, core = at_ex // CORES, at_ex % CORES
    ids = jnp.stack(
        [(chip + k) % chips * CORES + (core ^ s) for k in range(chips) for s in range(CORES)]
    ).astype(jnp.int32)
    blocks = jnp.stack([at_layer ^ r for r in range(layers)]).astype(jnp.int32)
    place = jnp.stack([(at_group + j) % groups for j in range(groups)]).astype(jnp.int32)

    def from_chip(x, k):
        perm = [(e, (e - k * CORES) % ex) for e in range(ex)]
        return lax.ppermute(x, "ex", perm)

    def from_core(x):
        return lax.ppermute(x, "ex", [(e, e ^ 1) for e in range(ex)])

    def from_group(x, j):
        return lax.ppermute(x, "groups", [(g, (g - j) % groups) for g in range(groups)])

    def from_layer(x, r):
        return lax.ppermute(x, "layer", [(z, z ^ r) for z in range(layers)])

    def tie(x, *others):
        return lax.optimization_barrier((x, *others))[0]

    total = queries.shape[0]
    span = total // groups
    width = span // CHUNKS

    def part_of_queries(c, after):
        start = (at_group * span + c * width).astype(jnp.int32)[None]
        return take(start, queries[:, 0, :], after, width)

    def gather_chip(x):
        return [from_chip(x, k) for k in range(1, chips)]

    def gather_group(x):
        return [from_group(x, j) for j in range(1, groups)]

    def with_cores(ours, theirs):
        return [x for pair in zip(ours, theirs) for x in pair]

    def flip(xs):
        return [from_core(x) for x in xs]

    def after(token, xs):
        return [tie(x, token) for x in xs]

    scored = functools.partial(score, ids, blocks)
    parts = []

    def advance(token, chain=False):
        for i, part in enumerate(parts):
            if part[0].shape[0] > 1:
                if chain and i and parts[i - 1][0].shape[0] == 1:
                    token = tie(token, parts[i - 1][1])
                send, keep = fold(part[0], part[1], token)
                step = layers // keep.shape[0] // 2
                part[:] = keep, from_layer(send, step)

    def send_parts(made):
        send, keep = made
        advance(keep, chain=True)
        parts.append([keep, from_layer(send, 1)])
        return parts[-2][0] if parts[1:] else keep

    q0 = part_of_queries(0, ids)
    q0_there, q0_core = gather_chip(q0), from_core(q0)
    hess = load(hessian[0], ids)
    q0_there = after(hess, q0_there)
    q0_cores = [q0_core] + flip(q0_there)
    q1 = part_of_queries(1, q0_there[-1])
    q1_there, q1_core = gather_chip(q1), from_core(q1)
    s0 = condition(ids, hess, with_cores([q0] + q0_there, q0_cores), q1)
    s0_there, s0_across, s0_core = gather_chip(s0), gather_group(s0), from_core(s0)
    rows = load(store[:, 0, :], s0)
    q1_there = after(rows, q1_there)
    q1_cores = [q1_core] + flip(q1_there)
    s0_there = after(rows, s0_there)
    s0_diagonal = [gather_group(x) for x in s0_there]
    s0_cores = [s0_core] + flip(s0_there)
    s1 = condition(ids, hess, with_cores([q1] + q1_there, q1_cores), s0_there[-1])
    s1_there, s1_core = gather_chip(s1), from_core(s1)
    s0_across = after(s1, s0_across)
    s0_across_cores = flip(s0_across)
    last = send_parts(scored(rows, with_cores([s0] + s0_there, s0_cores), s1))
    s0_diagonal = [after(last, xs) for xs in s0_diagonal]
    s0_diagonal_cores = [flip(xs) for xs in s0_diagonal]
    s1_across = gather_group(tie(s1, s0_diagonal[-1][-1]))
    s1_there = after(last, s1_there)
    s1_diagonal = [gather_group(x) for x in s1_there]
    s1_cores = [s1_core] + flip(s1_there)
    for j in range(groups - 1):
        ours = [s0_across[j]] + [xs[j] for xs in s0_diagonal]
        theirs = [s0_across_cores[j]] + [xs[j] for xs in s0_diagonal_cores]
        last = send_parts(scored(rows, with_cores(ours, theirs), last))
    last = send_parts(scored(rows, with_cores([s1] + s1_there, s1_cores), last))
    s1_across = after(last, s1_across)
    s1_across_cores = flip(s1_across)
    s1_diagonal = [after(last, xs) for xs in s1_diagonal]
    s1_diagonal_cores = [flip(xs) for xs in s1_diagonal]
    last = tie(last, parts[-2][1])
    for j in range(groups - 1):
        ours = [s1_across[j]] + [xs[j] for xs in s1_diagonal]
        theirs = [s1_across_cores[j]] + [xs[j] for xs in s1_diagonal_cores]
        last = send_parts(scored(rows, with_cores(ours, theirs), last))
    while any(part[0].shape[0] > 1 for part in parts):
        advance(last)
    return finish(place, parts, total)


def solution(mesh):
    groups, ex, layers = (mesh.shape[a] for a in ("groups", "ex", "layer"))
    in_specs = (P(None, "layer", "ex"), P("layer", "ex", None), P(("groups", "ex"), "layer", None))
    out_specs = P(("groups", "ex", "layer"), None)
    return jax.shard_map(
        functools.partial(shards, groups, ex, layers),
        mesh=mesh,
        in_specs=in_specs,
        out_specs=out_specs,
        check_vma=False,
    )
```

time: 83.8 us -> 87 us (1.038)
  waiting for transfers between devices: 36.7 us -> 9.52 us
  local copies, waits for them, and re-layouts: 0 us -> 18.1 us
  Pallas kernels: 24.4 us -> 30.7 us
  starting transfers between devices: 21.8 us -> 27.8 us
    unnamed x0 -> x12, local copies, waits for them, and re-layouts: none -> 18.1 us
    ppermute x4, waiting for transfers between devices: 16.6 us -> 0.01 us  [from_chip(): return lax.ppermute(x, 'ex', perm)]
    ppermute x6 -> x8, waiting for transfers between devices: 17.8 us -> 8.66 us  [from_layer(): return lax.ppermute(x, 'layer', [(z, z ^ r) for z in range(layers)])]
    ppermute x6 -> x8, starting transfers between devices: 8.93 us -> 15.3 us  [from_layer(): return lax.ppermute(x, 'layer', [(z, z ^ r) for z in range(layers)])]
    pallas_call x3 -> x9, Pallas kernels: 9.23 us -> 15.5 us  [the longest x4 13.9 us: score(): pl.pallas_call(functools.partial(score_kernel, len(pieces)), out_shape=(j...]
    ppermute x4, waiting for transfers between devices: 2.26 us -> 0.81 us  [from_group(): lax.ppermute(x, 'groups', [(g, (g - j) % groups) for g in range(groups)])]
    ppermute x4, starting transfers between devices: 5.23 us -> 4.05 us  [from_group(): lax.ppermute(x, 'groups', [(g, (g - j) % groups) for g in range(groups)])]
  transfers between devices with their start and end apart: 26 -> 28, of which waited for: 9 -> 6; matrix products, arithmetic and copies ran while one was open for 0% -> 0% of each run, Pallas kernels for 26% -> 33%
where the time goes in v3:
time: 87 us; the launch traced here: 86.6 us
  Pallas kernels  30.7 us (35%)
  starting transfers between devices  27.8 us (32%)
  local copies, waits for them, and re-layouts  18.1 us (21%)
  waiting for transfers between devices  9.52 us (11%)
    unnamed x12, local copies, waits for them, and re-layouts  18.1 us
    ppermute x8, starting transfers between devices, from_layer(): return lax.ppermute(x, 'layer', [(z, z ^ r) for z in range(layers)])  15.3 us
    pallas_call x4, Pallas kernels, score(): pl.pallas_call(functools.partial(score_kernel, len(pieces)), out_shape=(j...  13.9 us
    ppermute x8, waiting for transfers between devices, from_layer(): return lax.ppermute(x, 'layer', [(z, z ^ r) for z in range(layers)])  8.66 us
    pallas_call x2, Pallas kernels, load(): pl.pallas_call(load_kernel, out_shape=pltpu.VMEM(source.shape, BF16), in_...  7.38 us
    ppermute x4, starting transfers between devices, from_chip(): return lax.ppermute(x, 'ex', perm)  6.09 us
    pallas_call x2, Pallas kernels, condition(): pl.pallas_call(functools.partial(condition_kernel, len(pieces)), out_shap...  5.91 us
    ppermute x4, starting transfers between devices, from_group(): lax.ppermute(x, 'groups', [(g, (g - j) % groups) for g in range(groups)])  4.05 us
  transfers between devices with their start and end apart: 28, of which 6 were waited for; matrix products, arithmetic and copies ran while one was open for 0% of the time, Pallas kernels for 33%

profile of v3, /device:TPU:0, one launch (start us, length us, event | category | flops | bytes accessed | tf_op | source)
XLA Modules:
  0.0 86.6 jit_solution(15497865269158089715)
XLA Ops:
  0.0 0.1 pad_add_fusion.1.after.ids
  0.1 1.0 %shard_map.38.rest_0_ = bf16[128,1024]{1,0:T(8,128)(2,1)S(1)} custom-call(s32[1]{0:T(128)} %bitcast.12.start, bf16[512,1024]{1,0:T(8,128)(2,1)} %bitcast.17, s32[4]{0:T(128)S(1)} %pad_add_fusion.1.after.ids), custom_call_target="tpu_custom_call" | custom-call | tf_op jit(solution)/shard_map/pallas_call | solution.py:47
  1.0 3.0 %collective-permute-start.1 = (bf16[128,1024]{1,0:T(8,128)(2,1)S(1)}, bf16[128,1024]{1,0:T(8,128)(2,1)S(1)}, u32[]{:S(2)}, u32[]{:S(2)}) collective-permute-start(bf16[128,1024]{1,0:T(8,128)(2,1)S(1)} %shard_map.38.rest_0_), channel_id=1, source_target_pairs={{0,8},{4,12},{8,0},{12,4},{1,9},{5,13},{9,1},{13,5},{2,10},{6,14},... | collective-permute-start | bytes 786440 | tf_op jit(solution)/shard_map/ppermute | solution.py:163
  4.1 3.4 %shard_map.37.hess = bf16[1024,4096]{1,0:T(8,128)(2,1)S(1)} custom-call(bf16[1024,4096]{1,0:T(8,128)(2,1)} %bitcast.16, s32[4]{0:T(128)S(1)} %pad_add_fusion.1.after.ids), custom_call_target="tpu_custom_call" | custom-call | tf_op jit(solution)/shard_map/pallas_call | solution.py:29
  7.5 3.3 %copy-done.3 = bf16[1024,4096]{1,0:T(8,128)(2,1)} copy-done((bf16[1024,4096]{1,0:T(8,128)(2,1)}, bf16[1024,4096]{1,0:T(8,128)(2,1)S(1)}, u32[]{:S(2)}) %copy-start.3) | copy-done | bytes 8388632
  10.8 0.5 collective-permute-start.2
  11.3 1.0 %shard_map.39.rest_4_.rest_0_ = bf16[128,1024]{1,0:T(8,128)(2,1)S(1)} custom-call(s32[1]{0:T(128)} %bitcast.14.start, bf16[512,1024]{1,0:T(8,128)(2,1)} %bitcast.18, bf16[128,1024]{1,0:T(8,128)(2,1)S(1)} %collective-permute-done.1.after.rest_2_), custom_call_target="tpu_custom_call" | custom-call | tf_op jit(solution)/shard_map/pallas_call | solution.py:47
  12.3 0.9 %collective-permute-start.7 = (bf16[128,1024]{1,0:T(8,128)(2,1)S(1)}, bf16[128,1024]{1,0:T(8,128)(2,1)S(1)}, u32[]{:S(2)}, u32[]{:S(2)}) collective-permute-start(bf16[128,1024]{1,0:T(8,128)(2,1)S(1)} %shard_map.39.rest_4_.rest_0_), channel_id=1, source_target_pairs={{0,8},{4,12},{8,0},{12,4},{1,9},{5,13},{9,1},{13,5},{2,10},{6,14},... | collective-permute-start | bytes 786440 | tf_op jit(solution)/shard_map/ppermute | solution.py:163
  13.2 3.4 %copy-done.4 = bf16[1024,4096]{1,0:T(8,128)(2,1)S(1)} copy-done((bf16[1024,4096]{1,0:T(8,128)(2,1)S(1)}, bf16[1024,4096]{1,0:T(8,128)(2,1)}, u32[]{:S(2)}) %copy-start.4) | copy-done | bytes 8388632
  16.5 3.0 %shard_map.40.after.rest_0_ = bf16[1024,128]{1,0:T(8,128)(2,1)S(1)} custom-call(s32[4]{0:T(128)S(1)} %pad_add_fusion.1.after.ids, bf16[1024,4096]{1,0:T(8,128)(2,1)S(1)} %copy-done.4, bf16[128,1024]{1,0:T(8,128)(2,1)S(1)} %shard_map.38.rest_0_, bf16[128,1024]{1,0:T(8,128)(2,1)S(1)} %collective-permute-done.rest_1_, ...), custom_call_target="tpu_custom_call" | custom-call | tf_op jit(solution)/shard_map/pallas_call | solution.py:69
  19.5 1.3 %collective-permute-start.4 = (bf16[1024,128]{1,0:T(8,128)(2,1)S(1)}, bf16[1024,128]{1,0:T(8,128)(2,1)S(1)}, u32[]{:S(2)}, u32[]{:S(2)}) collective-permute-start(bf16[1024,128]{1,0:T(8,128)(2,1)S(1)} %shard_map.40.after.rest_0_), channel_id=1, source_target_pairs={{0,8},{4,12},{8,0},{12,4},{1,9},{5,13},{9,1},{13,5},{2,10},{6,14},... | collective-permute-start | bytes 786440 | tf_op jit(solution)/shard_map/ppermute | solution.py:163
  20.8 4.0 %shard_map.41.store = bf16[1280,4096]{1,0:T(8,128)(2,1)S(1)} custom-call(bf16[1280,4096]{1,0:T(8,128)(2,1)} %bitcast.15, bf16[1024,128]{1,0:T(8,128)(2,1)S(1)} %shard_map.40.after.rest_0_), custom_call_target="tpu_custom_call" | custom-call | tf_op jit(solution)/shard_map/pallas_call | solution.py:29
  24.8 4.0 %copy-done = bf16[1280,4096]{1,0:T(8,128)(2,1)} copy-done((bf16[1280,4096]{1,0:T(8,128)(2,1)}, bf16[1280,4096]{1,0:T(8,128)(2,1)S(1)}, u32[]{:S(2)}) %copy-start) | copy-done | bytes 10485784
  28.8 0.5 collective-permute-start.8
  29.3 1.5 %collective-permute-start.10 = (bf16[1024,128]{1,0:T(8,128)(2,1)S(1)}, bf16[1024,128]{1,0:T(8,128)(2,1)S(1)}, u32[]{:S(2)}, u32[]{:S(2)}) collective-permute-start(bf16[1024,128]{1,0:T(8,128)(2,1)S(1)} %shard_map.40.after.rest_0_), channel_id=1, source_target_pairs={{0,16},{16,0},{1,17},{17,1},{2,18},{18,2},{3,19},{19,3},{4,20},{20... | collective-permute-start | bytes 786440 | tf_op jit(solution)/shard_map/ppermute | solution.py:169
  30.8 0.5 collective-permute-start.5
  31.3 0.5 collective-permute-start.12
  31.9 3.4 %copy-done.5 = bf16[1024,4096]{1,0:T(8,128)(2,1)S(1)} copy-done((bf16[1024,4096]{1,0:T(8,128)(2,1)S(1)}, bf16[1024,4096]{1,0:T(8,128)(2,1)}, u32[]{:S(2)}) %copy-start.5) | copy-done | bytes 8388632
  35.2 3.0 %shard_map.42.rest_4_.rest_0_ = bf16[1024,128]{1,0:T(8,128)(2,1)S(1)} custom-call(s32[4]{0:T(128)S(1)} %pad_add_fusion.1.after.ids, bf16[1024,4096]{1,0:T(8,128)(2,1)S(1)} %copy-done.5, bf16[128,1024]{1,0:T(8,128)(2,1)S(1)} %shard_map.39.rest_4_.rest_0_, bf16[128,1024]{1,0:T(8,128)(2,1)S(1)} %collective-permute-done.6.rest_1_, ...), custom_call_target="tpu_custom_call" | custom-call | tf_op jit(solution)/shard_map/pallas_call | solution.py:69
  38.2 0.9 %collective-permute-start.17 = (bf16[1024,128]{1,0:T(8,128)(2,1)S(1)}, bf16[1024,128]{1,0:T(8,128)(2,1)S(1)}, u32[]{:S(2)}, u32[]{:S(2)}) collective-permute-start(bf16[1024,128]{1,0:T(8,128)(2,1)S(1)} %shard_map.42.rest_4_.rest_0_), channel_id=1, source_target_pairs={{0,8},{4,12},{8,0},{12,4},{1,9},{5,13},{9,1},{13,5},{2,10},{6,14},... | collective-permute-start | bytes 786440 | tf_op jit(solution)/shard_map/ppermute | solution.py:163
  39.1 0.1 pad_add_fusion.2.blocks
  39.2 4.0 %copy-done.1 = bf16[1280,4096]{1,0:T(8,128)(2,1)S(1)} copy-done((bf16[1280,4096]{1,0:T(8,128)(2,1)S(1)}, bf16[1280,4096]{1,0:T(8,128)(2,1)}, u32[]{:S(2)}) %copy-start.1) | copy-done | bytes 10485784
  43.2 3.5 %shard_map.43 = (bf16[2,320,128]{2,1,0:T(8,128)(2,1)S(1)}, f32[2,320,128]{2,1,0:T(8,128)S(1)}) custom-call(s32[4]{0:T(128)S(1)} %pad_add_fusion.1.after.ids, s32[4]{0:T(128)S(1)} %pad_add_fusion.2.blocks, bf16[1280,4096]{1,0:T(8,128)(2,1)S(1)} %copy-done.1, bf16[1024,128]{1,0:T(8,128)(2,1)S(1)} %shard_map.40.after.rest_0_, ...), custom_call_target="tpu_custom_call" | custom-call | tf_op jit(solution)/shard_map/pallas_call | solution.py:98
  46.7 0.5 collective-permute-start.13
  47.3 0.1 collective-permute-start.16
  47.3 1.6 %collective-permute-start.9 = (bf16[2,320,128]{2,1,0:T(8,128)(2,1)S(1)}, bf16[2,320,128]{2,1,0:T(8,128)(2,1)S(1)}, u32[]{:S(2)}, u32[]{:S(2)}) collective-permute-start(bf16[2,320,128]{2,1,0:T(8,128)(2,1)S(1)} %get-tuple-element.37), channel_id=1, source_target_pairs={{0,1},{1,0},{2,3},{3,2},{4,5},{5,4},{6,7},{7,6},{8,9},{9,8},{10,11... | collective-permute-start | bytes 491528 | tf_op jit(solution)/shard_map/ppermute | solution.py:172
  48.9 0.2 collective-permute-start.18
  49.1 1.5 %collective-permute-start.23 = (bf16[1024,128]{1,0:T(8,128)(2,1)S(1)}, bf16[1024,128]{1,0:T(8,128)(2,1)S(1)}, u32[]{:S(2)}, u32[]{:S(2)}) collective-permute-start(bf16[1024,128]{1,0:T(8,128)(2,1)S(1)} %collective-permute-done.17.rest_2_), channel_id=1, source_target_pairs={{0,16},{16,0},{1,17},{17,1},{2,18},{18,2},{3,19},{19,3},{4,20},{20... | collective-permute-start | bytes 786440 | tf_op jit(solution)/shard_map/ppermute | solution.py:169
  50.6 0.5 collective-permute-start.21
  51.1 3.5 %shard_map.44 = (bf16[2,320,128]{2,1,0:T(8,128)(2,1)S(1)}, f32[2,320,128]{2,1,0:T(8,128)S(1)}) custom-call(s32[4]{0:T(128)S(1)} %pad_add_fusion.1.after.ids, s32[4]{0:T(128)S(1)} %pad_add_fusion.2.blocks, bf16[1280,4096]{1,0:T(8,128)(2,1)S(1)} %copy-done.2, bf16[1024,128]{1,0:T(8,128)(2,1)S(1)} %collective-permute-done.10.rest_0_, ...), custom_call_target="tpu_custom_call" | custom-call | tf_op jit(solution)/shard_map/pallas_call | solution.py:98
  54.6 0.8 collective-permute-start.15
  55.5 2.7 %collective-permute-start.14 = (bf16[1,320,128]{2,1,0:T(8,128)(2,1)S(1)}, bf16[1,320,128]{2,1,0:T(8,128)(2,1)S(1)}, u32[]{:S(2)}, u32[]{:S(2)}) collective-permute-start(bf16[1,320,128]{2,1,0:T(8,128)(2,1)S(1)} %get-tuple-element.42), channel_id=1, source_target_pairs={{0,2},{1,3},{2,0},{3,1},{4,6},{5,7},{6,4},{7,5},{8,10},{9,11},{10,... | collective-permute-start | bytes 245768 | tf_op jit(solution)/shard_map/ppermute | solution.py:172
  58.2 3.5 %shard_map.46 = (bf16[2,320,128]{2,1,0:T(8,128)(2,1)S(1)}, f32[2,320,128]{2,1,0:T(8,128)S(1)}) custom-call(s32[4]{0:T(128)S(1)} %pad_add_fusion.1.after.ids, s32[4]{0:T(128)S(1)} %pad_add_fusion.2.blocks, bf16[1280,4096]{1,0:T(8,128)(2,1)S(1)} %copy-done.2, bf16[1024,128]{1,0:T(8,128)(2,1)S(1)} %shard_map.42.rest_4_.rest_0_, ...), custom_call_target="tpu_custom_call" | custom-call | tf_op jit(solution)/shard_map/pallas_call | solution.py:98
  61.7 0.6 collective-permute-done.15.got
  62.4 0.1 collective-permute-start.24
  62.5 0.8 collective-permute-done.21.rest_0_
  63.3 2.6 %collective-permute-start.19 = (bf16[1,320,128]{2,1,0:T(8,128)(2,1)S(1)}, bf16[1,320,128]{2,1,0:T(8,128)(2,1)S(1)}, u32[]{:S(2)}, u32[]{:S(2)}) collective-permute-start(bf16[1,320,128]{2,1,0:T(8,128)(2,1)S(1)} %get-tuple-element.48), channel_id=1, source_target_pairs={{0,2},{1,3},{2,0},{3,1},{4,6},{5,7},{6,4},{7,5},{8,10},{9,11},{10,... | collective-permute-start | bytes 245768 | tf_op jit(solution)/shard_map/ppermute | solution.py:172
  65.8 0.7 collective-permute-start.20
  66.5 3.8 %collective-permute-done.19.refs_3_ = bf16[1,320,128]{2,1,0:T(8,128)(2,1)S(1)} collective-permute-done((bf16[1,320,128]{2,1,0:T(8,128)(2,1)S(1)}, bf16[1,320,128]{2,1,0:T(8,128)(2,1)S(1)}, u32[]{:S(2)}, u32[]{:S(2)}) %collective-permute-start.19) | collective-permute-done | bytes 81952 | tf_op jit(solution)/shard_map/ppermute | solution.py:172
  70.4 3.5 %shard_map.48 = (bf16[2,320,128]{2,1,0:T(8,128)(2,1)S(1)}, f32[2,320,128]{2,1,0:T(8,128)S(1)}) custom-call(s32[4]{0:T(128)S(1)} %pad_add_fusion.1.after.ids, s32[4]{0:T(128)S(1)} %pad_add_fusion.2.blocks, bf16[1280,4096]{1,0:T(8,128)(2,1)S(1)} %copy-done.2, bf16[1024,128]{1,0:T(8,128)(2,1)S(1)} %collective-permute-done.21.rest_0_, ...), custom_call_target="tpu_custom_call" | custom-call | tf_op jit(solution)/shard_map/pallas_call | solution.py:98
  73.8 1.5 %collective-permute-start.26 = (bf16[2,320,128]{2,1,0:T(8,128)(2,1)S(1)}, bf16[2,320,128]{2,1,0:T(8,128)(2,1)S(1)}, u32[]{:S(2)}, u32[]{:S(2)}) collective-permute-start(bf16[2,320,128]{2,1,0:T(8,128)(2,1)S(1)} %get-tuple-element.58), channel_id=1, source_target_pairs={{0,1},{1,0},{2,3},{3,2},{4,5},{5,4},{6,7},{7,6},{8,9},{9,8},{10,11... | collective-permute-start | bytes 491528 | tf_op jit(solution)/shard_map/ppermute | solution.py:172
  75.4 2.2 %collective-permute-start.25 = (bf16[1,320,128]{2,1,0:T(8,128)(2,1)S(1)}, bf16[1,320,128]{2,1,0:T(8,128)(2,1)S(1)}, u32[]{:S(2)}, u32[]{:S(2)}) collective-permute-start(bf16[1,320,128]{2,1,0:T(8,128)(2,1)S(1)} %get-tuple-element.57), channel_id=1, source_target_pairs={{0,2},{1,3},{2,0},{3,1},{4,6},{5,7},{6,4},{7,5},{8,10},{9,11},{10,... | collective-permute-start | bytes 245768 | tf_op jit(solution)/shard_map/ppermute | solution.py:172
  77.6 1.9 %collective-permute-done.26.got = bf16[2,320,128]{2,1,0:T(8,128)(2,1)S(1)} collective-permute-done((bf16[2,320,128]{2,1,0:T(8,128)(2,1)S(1)}, bf16[2,320,128]{2,1,0:T(8,128)(2,1)S(1)}, u32[]{:S(2)}, u32[]{:S(2)}) %collective-permute-start.26) | collective-permute-done | bytes 163872 | tf_op jit(solution)/shard_map/ppermute | solution.py:172
  79.5 3.2 %collective-permute-start.27 = (bf16[1,320,128]{2,1,0:T(8,128)(2,1)S(1)}, bf16[1,320,128]{2,1,0:T(8,128)(2,1)S(1)}, u32[]{:S(2)}, u32[]{:S(2)}) collective-permute-start(bf16[1,320,128]{2,1,0:T(8,128)(2,1)S(1)} %get-tuple-element.60), channel_id=1, source_target_pairs={{0,2},{1,3},{2,0},{3,1},{4,6},{5,7},{6,4},{7,5},{8,10},{9,11},{10,... | collective-permute-start | bytes 245768 | tf_op jit(solution)/shard_map/ppermute | solution.py:172
  82.7 0.1 pad_add_fusion.place
  82.8 0.7 collective-permute-done.25.refs_5_
  83.5 1.7 %collective-permute-done.27.refs_7_ = bf16[1,320,128]{2,1,0:T(8,128)(2,1)S(1)} collective-permute-done((bf16[1,320,128]{2,1,0:T(8,128)(2,1)S(1)}, bf16[1,320,128]{2,1,0:T(8,128)(2,1)S(1)}, u32[]{:S(2)}, u32[]{:S(2)}) %collective-permute-start.27) | collective-permute-done | bytes 81952 | tf_op jit(solution)/shard_map/ppermute | solution.py:172
  85.1 1.5 %shard_map.51 = f32[320,512]{1,0:T(8,128)} custom-call(s32[2]{0:T(128)S(1)} %pad_add_fusion.place, f32[1,320,128]{2,1,0:T(8,128)S(1)} %get-tuple-element.41.rest_4_.refs_0_, bf16[1,320,128]{2,1,0:T(8,128)(2,1)S(1)} %collective-permute-done.14.refs_1_, f32[1,320,128]{2,1,0:T(8,128)S(1)} %get-tuple-element.53.rest_4_.refs_2_, ...), custom_call_target="tpu_custom_call" | custom-call | tf_op jit(solution)/shard_map/pallas_call | solution.py:142
  (38 shorter events, 0.2 us)
Async XLA Ops:
  1.0 9.7 %collective-permute-start.1 = (bf16[128,1024]{1,0:T(8,128)(2,1)S(1)}, bf16[128,1024]{1,0:T(8,128)(2,1)S(1)}, u32[]{:S(2)}, u32[]{:S(2)}) collective-permute-start(bf16[128,1024]{1,0:T(8,128)(2,1)S(1)} %shard_map.38.rest_0_), channel_id=1, source_target_pairs={{0,8},{4,12},{8,0},{12,4},{1,9},{5,13},{9,1},{13,5},{2,10},{6,14},... | collective-permute-start | bytes 786440 | tf_op jit(solution)/shard_map/ppermute | solution.py:163
  4.1 9.1 %collective-permute-start = (bf16[128,1024]{1,0:T(8,128)(2,1)S(1)}, bf16[128,1024]{1,0:T(8,128)(2,1)S(1)}, u32[]{:S(2)}, u32[]{:S(2)}) collective-permute-start(bf16[128,1024]{1,0:T(8,128)(2,1)S(1)} %shard_map.38.rest_0_), channel_id=1, source_target_pairs={{0,4},{4,0},{8,12},{12,8},{1,5},{5,1},{9,13},{13,9},{2,6},{6,2},{1... | collective-permute-start | bytes 786440 | tf_op jit(solution)/shard_map/ppermute | solution.py:166
  7.5 3.3 %copy-start.3 = (bf16[1024,4096]{1,0:T(8,128)(2,1)}, bf16[1024,4096]{1,0:T(8,128)(2,1)S(1)}, u32[]{:S(2)}) copy-start(bf16[1024,4096]{1,0:T(8,128)(2,1)S(1)} %shard_map.37.hess) | copy-start | bytes 25165828
  10.8 2.4 %collective-permute-start.2 = (bf16[128,1024]{1,0:T(8,128)(2,1)S(1)}, bf16[128,1024]{1,0:T(8,128)(2,1)S(1)}, u32[]{:S(2)}, u32[]{:S(2)}) collective-permute-start(bf16[128,1024]{1,0:T(8,128)(2,1)S(1)} %collective-permute-done.1.after.rest_2_), channel_id=1, source_target_pairs={{0,4},{4,0},{8,12},{12,8},{1,5},{5,1},{9,13},{13,9},{2,6},{6,2},{1... | collective-permute-start | bytes 786440 | tf_op jit(solution)/shard_map/ppermute | solution.py:166
  12.3 16.5 %collective-permute-start.7 = (bf16[128,1024]{1,0:T(8,128)(2,1)S(1)}, bf16[128,1024]{1,0:T(8,128)(2,1)S(1)}, u32[]{:S(2)}, u32[]{:S(2)}) collective-permute-start(bf16[128,1024]{1,0:T(8,128)(2,1)S(1)} %shard_map.39.rest_4_.rest_0_), channel_id=1, source_target_pairs={{0,8},{4,12},{8,0},{12,4},{1,9},{5,13},{9,1},{13,5},{2,10},{6,14},... | collective-permute-start | bytes 786440 | tf_op jit(solution)/shard_map/ppermute | solution.py:163
  13.2 3.4 %copy-start.4 = (bf16[1024,4096]{1,0:T(8,128)(2,1)S(1)}, bf16[1024,4096]{1,0:T(8,128)(2,1)}, u32[]{:S(2)}) copy-start(bf16[1024,4096]{1,0:T(8,128)(2,1)} %copy-done.3) | copy-start | bytes 25165828
  19.5 11.3 %collective-permute-start.4 = (bf16[1024,128]{1,0:T(8,128)(2,1)S(1)}, bf16[1024,128]{1,0:T(8,128)(2,1)S(1)}, u32[]{:S(2)}, u32[]{:S(2)}) collective-permute-start(bf16[1024,128]{1,0:T(8,128)(2,1)S(1)} %shard_map.40.after.rest_0_), channel_id=1, source_target_pairs={{0,8},{4,12},{8,0},{12,4},{1,9},{5,13},{9,1},{13,5},{2,10},{6,14},... | collective-permute-start | bytes 786440 | tf_op jit(solution)/shard_map/ppermute | solution.py:163
  20.8 10.6 %collective-permute-start.6 = (bf16[128,1024]{1,0:T(8,128)(2,1)S(1)}, bf16[128,1024]{1,0:T(8,128)(2,1)S(1)}, u32[]{:S(2)}, u32[]{:S(2)}) collective-permute-start(bf16[128,1024]{1,0:T(8,128)(2,1)S(1)} %shard_map.39.rest_4_.rest_0_), channel_id=1, source_target_pairs={{0,4},{4,0},{8,12},{12,8},{1,5},{5,1},{9,13},{13,9},{2,6},{6,2},{1... | collective-permute-start | bytes 786440 | tf_op jit(solution)/shard_map/ppermute | solution.py:166
  24.8 4.0 %copy-start = (bf16[1280,4096]{1,0:T(8,128)(2,1)}, bf16[1280,4096]{1,0:T(8,128)(2,1)S(1)}, u32[]{:S(2)}) copy-start(bf16[1280,4096]{1,0:T(8,128)(2,1)S(1)} %shard_map.41.store) | copy-start | bytes 31457284
  28.8 3.1 %collective-permute-start.8 = (bf16[128,1024]{1,0:T(8,128)(2,1)S(1)}, bf16[128,1024]{1,0:T(8,128)(2,1)S(1)}, u32[]{:S(2)}, u32[]{:S(2)}) collective-permute-start(bf16[128,1024]{1,0:T(8,128)(2,1)S(1)} %collective-permute-done.7.rest_2_), channel_id=1, source_target_pairs={{0,4},{4,0},{8,12},{12,8},{1,5},{5,1},{9,13},{13,9},{2,6},{6,2},{1... | collective-permute-start | bytes 786440 | tf_op jit(solution)/shard_map/ppermute | solution.py:166
  29.3 9.9 %collective-permute-start.10 = (bf16[1024,128]{1,0:T(8,128)(2,1)S(1)}, bf16[1024,128]{1,0:T(8,128)(2,1)S(1)}, u32[]{:S(2)}, u32[]{:S(2)}) collective-permute-start(bf16[1024,128]{1,0:T(8,128)(2,1)S(1)} %shard_map.40.after.rest_0_), channel_id=1, source_target_pairs={{0,16},{16,0},{1,17},{17,1},{2,18},{18,2},{3,19},{19,3},{4,20},{20... | collective-permute-start | bytes 786440 | tf_op jit(solution)/shard_map/ppermute | solution.py:169
  30.8 8.4 %collective-permute-start.3 = (bf16[1024,128]{1,0:T(8,128)(2,1)S(1)}, bf16[1024,128]{1,0:T(8,128)(2,1)S(1)}, u32[]{:S(2)}, u32[]{:S(2)}) collective-permute-start(bf16[1024,128]{1,0:T(8,128)(2,1)S(1)} %shard_map.40.after.rest_0_), channel_id=1, source_target_pairs={{0,4},{4,0},{8,12},{12,8},{1,5},{5,1},{9,13},{13,9},{2,6},{6,2},{1... | collective-permute-start | bytes 786440 | tf_op jit(solution)/shard_map/ppermute | solution.py:166
  30.8 8.4 %collective-permute-start.5 = (bf16[1024,128]{1,0:T(8,128)(2,1)S(1)}, bf16[1024,128]{1,0:T(8,128)(2,1)S(1)}, u32[]{:S(2)}, u32[]{:S(2)}) collective-permute-start(bf16[1024,128]{1,0:T(8,128)(2,1)S(1)} %collective-permute-done.4.rest_4_.rest_2_), channel_id=1, source_target_pairs={{0,4},{4,0},{8,12},{12,8},{1,5},{5,1},{9,13},{13,9},{2,6},{6,2},{1... | collective-permute-start | bytes 786440 | tf_op jit(solution)/shard_map/ppermute | solution.py:166
  31.3 15.4 %collective-permute-start.12 = (bf16[1024,128]{1,0:T(8,128)(2,1)S(1)}, bf16[1024,128]{1,0:T(8,128)(2,1)S(1)}, u32[]{:S(2)}, u32[]{:S(2)}) collective-permute-start(bf16[1024,128]{1,0:T(8,128)(2,1)S(1)} %collective-permute-done.4.rest_4_.rest_2_), channel_id=1, source_target_pairs={{0,16},{16,0},{1,17},{17,1},{2,18},{18,2},{3,19},{19,3},{4,20},{20... | collective-permute-start | bytes 786440 | tf_op jit(solution)/shard_map/ppermute | solution.py:169
  31.9 3.4 %copy-start.5 = (bf16[1024,4096]{1,0:T(8,128)(2,1)S(1)}, bf16[1024,4096]{1,0:T(8,128)(2,1)}, u32[]{:S(2)}) copy-start(bf16[1024,4096]{1,0:T(8,128)(2,1)} %copy-done.3) | copy-start | bytes 25165828
  38.2 10.7 %collective-permute-start.17 = (bf16[1024,128]{1,0:T(8,128)(2,1)S(1)}, bf16[1024,128]{1,0:T(8,128)(2,1)S(1)}, u32[]{:S(2)}, u32[]{:S(2)}) collective-permute-start(bf16[1024,128]{1,0:T(8,128)(2,1)S(1)} %shard_map.42.rest_4_.rest_0_), channel_id=1, source_target_pairs={{0,8},{4,12},{8,0},{12,4},{1,9},{5,13},{9,1},{13,5},{2,10},{6,14},... | collective-permute-start | bytes 786440 | tf_op jit(solution)/shard_map/ppermute | solution.py:163
  39.2 9.9 %collective-permute-start.11 = (bf16[1024,128]{1,0:T(8,128)(2,1)S(1)}, bf16[1024,128]{1,0:T(8,128)(2,1)S(1)}, u32[]{:S(2)}, u32[]{:S(2)}) collective-permute-start(bf16[1024,128]{1,0:T(8,128)(2,1)S(1)} %collective-permute-done.10.rest_0_), channel_id=1, source_target_pairs={{0,4},{4,0},{8,12},{12,8},{1,5},{5,1},{9,13},{13,9},{2,6},{6,2},{1... | collective-permute-start | bytes 786440 | tf_op jit(solution)/shard_map/ppermute | solution.py:166
  39.2 4.0 %copy-start.1 = (bf16[1280,4096]{1,0:T(8,128)(2,1)S(1)}, bf16[1280,4096]{1,0:T(8,128)(2,1)}, u32[]{:S(2)}) copy-start(bf16[1280,4096]{1,0:T(8,128)(2,1)} %copy-done) | copy-start | bytes 31457284
  43.2 7.9 %copy-start.2 = (bf16[1280,4096]{1,0:T(8,128)(2,1)S(1)}, bf16[1280,4096]{1,0:T(8,128)(2,1)}, u32[]{:S(2)}) copy-start(bf16[1280,4096]{1,0:T(8,128)(2,1)} %copy-done) | copy-start | bytes 31457284
  46.7 3.9 %collective-permute-start.13 = (bf16[1024,128]{1,0:T(8,128)(2,1)S(1)}, bf16[1024,128]{1,0:T(8,128)(2,1)S(1)}, u32[]{:S(2)}, u32[]{:S(2)}) collective-permute-start(bf16[1024,128]{1,0:T(8,128)(2,1)S(1)} %collective-permute-done.12.rest_2_), channel_id=1, source_target_pairs={{0,4},{4,0},{8,12},{12,8},{1,5},{5,1},{9,13},{13,9},{2,6},{6,2},{1... | collective-permute-start | bytes 786440 | tf_op jit(solution)/shard_map/ppermute | solution.py:166
  47.3 8.2 %collective-permute-start.16 = (bf16[1024,128]{1,0:T(8,128)(2,1)S(1)}, bf16[1024,128]{1,0:T(8,128)(2,1)S(1)}, u32[]{:S(2)}, u32[]{:S(2)}) collective-permute-start(bf16[1024,128]{1,0:T(8,128)(2,1)S(1)} %shard_map.42.rest_4_.rest_0_), channel_id=1, source_target_pairs={{0,4},{4,0},{8,12},{12,8},{1,5},{5,1},{9,13},{13,9},{2,6},{6,2},{1... | collective-permute-start | bytes 786440 | tf_op jit(solution)/shard_map/ppermute | solution.py:166
  47.3 7.3 %collective-permute-start.9 = (bf16[2,320,128]{2,1,0:T(8,128)(2,1)S(1)}, bf16[2,320,128]{2,1,0:T(8,128)(2,1)S(1)}, u32[]{:S(2)}, u32[]{:S(2)}) collective-permute-start(bf16[2,320,128]{2,1,0:T(8,128)(2,1)S(1)} %get-tuple-element.37), channel_id=1, source_target_pairs={{0,1},{1,0},{2,3},{3,2},{4,5},{5,4},{6,7},{7,6},{8,9},{9,8},{10,11... | collective-permute-start | bytes 491528 | tf_op jit(solution)/shard_map/ppermute | solution.py:172
  48.9 9.2 %collective-permute-start.18 = (bf16[1024,128]{1,0:T(8,128)(2,1)S(1)}, bf16[1024,128]{1,0:T(8,128)(2,1)S(1)}, u32[]{:S(2)}, u32[]{:S(2)}) collective-permute-start(bf16[1024,128]{1,0:T(8,128)(2,1)S(1)} %collective-permute-done.17.rest_2_), channel_id=1, source_target_pairs={{0,4},{4,0},{8,12},{12,8},{1,5},{5,1},{9,13},{13,9},{2,6},{6,2},{1... | collective-permute-start | bytes 786440 | tf_op jit(solution)/shard_map/ppermute | solution.py:166
  49.1 13.3 %collective-permute-start.23 = (bf16[1024,128]{1,0:T(8,128)(2,1)S(1)}, bf16[1024,128]{1,0:T(8,128)(2,1)S(1)}, u32[]{:S(2)}, u32[]{:S(2)}) collective-permute-start(bf16[1024,128]{1,0:T(8,128)(2,1)S(1)} %collective-permute-done.17.rest_2_), channel_id=1, source_target_pairs={{0,16},{16,0},{1,17},{17,1},{2,18},{18,2},{3,19},{19,3},{4,20},{20... | collective-permute-start | bytes 786440 | tf_op jit(solution)/shard_map/ppermute | solution.py:169
  50.6 12.7 %collective-permute-start.21 = (bf16[1024,128]{1,0:T(8,128)(2,1)S(1)}, bf16[1024,128]{1,0:T(8,128)(2,1)S(1)}, u32[]{:S(2)}, u32[]{:S(2)}) collective-permute-start(bf16[1024,128]{1,0:T(8,128)(2,1)S(1)} %shard_map.42.rest_4_.rest_0_), channel_id=1, source_target_pairs={{0,16},{16,0},{1,17},{17,1},{2,18},{18,2},{3,19},{19,3},{4,20},{20... | collective-permute-start | bytes 786440 | tf_op jit(solution)/shard_map/ppermute | solution.py:169
  54.6 7.7 %collective-permute-start.15 = (bf16[2,320,128]{2,1,0:T(8,128)(2,1)S(1)}, bf16[2,320,128]{2,1,0:T(8,128)(2,1)S(1)}, u32[]{:S(2)}, u32[]{:S(2)}) collective-permute-start(bf16[2,320,128]{2,1,0:T(8,128)(2,1)S(1)} %get-tuple-element.43), channel_id=1, source_target_pairs={{0,1},{1,0},{2,3},{3,2},{4,5},{5,4},{6,7},{7,6},{8,9},{9,8},{10,11... | collective-permute-start | bytes 491528 | tf_op jit(solution)/shard_map/ppermute | solution.py:172
  55.5 6.2 %collective-permute-start.14 = (bf16[1,320,128]{2,1,0:T(8,128)(2,1)S(1)}, bf16[1,320,128]{2,1,0:T(8,128)(2,1)S(1)}, u32[]{:S(2)}, u32[]{:S(2)}) collective-permute-start(bf16[1,320,128]{2,1,0:T(8,128)(2,1)S(1)} %get-tuple-element.42), channel_id=1, source_target_pairs={{0,2},{1,3},{2,0},{3,1},{4,6},{5,7},{6,4},{7,5},{8,10},{9,11},{10,... | collective-permute-start | bytes 245768 | tf_op jit(solution)/shard_map/ppermute | solution.py:172
  62.4 8.0 %collective-permute-start.24 = (bf16[1024,128]{1,0:T(8,128)(2,1)S(1)}, bf16[1024,128]{1,0:T(8,128)(2,1)S(1)}, u32[]{:S(2)}, u32[]{:S(2)}) collective-permute-start(bf16[1024,128]{1,0:T(8,128)(2,1)S(1)} %collective-permute-done.23.rest_2_), channel_id=1, source_target_pairs={{0,4},{4,0},{8,12},{12,8},{1,5},{5,1},{9,13},{13,9},{2,6},{6,2},{1... | collective-permute-start | bytes 786440 | tf_op jit(solution)/shard_map/ppermute | solution.py:166
  63.3 7.1 %collective-permute-start.22 = (bf16[1024,128]{1,0:T(8,128)(2,1)S(1)}, bf16[1024,128]{1,0:T(8,128)(2,1)S(1)}, u32[]{:S(2)}, u32[]{:S(2)}) collective-permute-start(bf16[1024,128]{1,0:T(8,128)(2,1)S(1)} %collective-permute-done.21.rest_0_), channel_id=1, source_target_pairs={{0,4},{4,0},{8,12},{12,8},{1,5},{5,1},{9,13},{13,9},{2,6},{6,2},{1... | collective-permute-start | bytes 786440 | tf_op jit(solution)/shard_map/ppermute | solution.py:166
  63.3 7.1 %collective-permute-start.19 = (bf16[1,320,128]{2,1,0:T(8,128)(2,1)S(1)}, bf16[1,320,128]{2,1,0:T(8,128)(2,1)S(1)}, u32[]{:S(2)}, u32[]{:S(2)}) collective-permute-start(bf16[1,320,128]{2,1,0:T(8,128)(2,1)S(1)} %get-tuple-element.48), channel_id=1, source_target_pairs={{0,2},{1,3},{2,0},{3,1},{4,6},{5,7},{6,4},{7,5},{8,10},{9,11},{10,... | collective-permute-start | bytes 245768 | tf_op jit(solution)/shard_map/ppermute | solution.py:172
  65.8 9.5 %collective-permute-start.20 = (bf16[2,320,128]{2,1,0:T(8,128)(2,1)S(1)}, bf16[2,320,128]{2,1,0:T(8,128)(2,1)S(1)}, u32[]{:S(2)}, u32[]{:S(2)}) collective-permute-start(bf16[2,320,128]{2,1,0:T(8,128)(2,1)S(1)} %get-tuple-element.49), channel_id=1, source_target_pairs={{0,1},{1,0},{2,3},{3,2},{4,5},{5,4},{6,7},{7,6},{8,9},{9,8},{10,11... | collective-permute-start | bytes 491528 | tf_op jit(solution)/shard_map/ppermute | solution.py:172
  73.8 5.6 %collective-permute-start.26 = (bf16[2,320,128]{2,1,0:T(8,128)(2,1)S(1)}, bf16[2,320,128]{2,1,0:T(8,128)(2,1)S(1)}, u32[]{:S(2)}, u32[]{:S(2)}) collective-permute-start(bf16[2,320,128]{2,1,0:T(8,128)(2,1)S(1)} %get-tuple-element.58), channel_id=1, source_target_pairs={{0,1},{1,0},{2,3},{3,2},{4,5},{5,4},{6,7},{7,6},{8,9},{9,8},{10,11... | collective-permute-start | bytes 491528 | tf_op jit(solution)/shard_map/ppermute | solution.py:172
  75.4 8.1 %collective-permute-start.25 = (bf16[1,320,128]{2,1,0:T(8,128)(2,1)S(1)}, bf16[1,320,128]{2,1,0:T(8,128)(2,1)S(1)}, u32[]{:S(2)}, u32[]{:S(2)}) collective-permute-start(bf16[1,320,128]{2,1,0:T(8,128)(2,1)S(1)} %get-tuple-element.57), channel_id=1, source_target_pairs={{0,2},{1,3},{2,0},{3,1},{4,6},{5,7},{6,4},{7,5},{8,10},{9,11},{10,... | collective-permute-start | bytes 245768 | tf_op jit(solution)/shard_map/ppermute | solution.py:172
  79.5 5.7 %collective-permute-start.27 = (bf16[1,320,128]{2,1,0:T(8,128)(2,1)S(1)}, bf16[1,320,128]{2,1,0:T(8,128)(2,1)S(1)}, u32[]{:S(2)}, u32[]{:S(2)}) collective-permute-start(bf16[1,320,128]{2,1,0:T(8,128)(2,1)S(1)} %get-tuple-element.60), channel_id=1, source_target_pairs={{0,2},{1,3},{2,0},{3,1},{4,6},{5,7},{6,4},{7,5},{8,10},{9,11},{10,... | collective-permute-start | bytes 245768 | tf_op jit(solution)/shard_map/ppermute | solution.py:172

commit v4 on v3

--- a/solution.py
+++ b/solution.py
@@ -36,35 +36,35 @@
     )(pltpu.with_memory_space_constraint(source, pltpu.HBM), after)
 
 
-def take_kernel(start, source, after, out, sem):
-    at = pl.ds(pl.multiple_of(start[0], out.shape[0]), out.shape[0])
+def take_kernel(where, facts, source, after, out, sem):
+    at = pl.ds(pl.multiple_of(facts[where], out.shape[0]), out.shape[0])
     copy = pltpu.make_async_copy(source.at[at, :], out, sem)
     copy.start()
     copy.wait()
 
 
-def take(start, source, after, rows):
-    return pl.pallas_call(
-        take_kernel,
+def take(where, facts, source, after, rows):
+    return pl.pallas_call(
+        functools.partial(take_kernel, where),
         out_shape=pltpu.VMEM((rows, source.shape[1]), BF16),
         in_specs=[SMEM, HBM, ANY],
         out_specs=VMEM,
         scratch_shapes=[pltpu.SemaphoreType.DMA],
         compiler_params=pltpu.CompilerParams(vmem_limit_bytes=2 * MIB),
-    )(start, pltpu.with_memory_space_constraint(source, pltpu.HBM), after)
-
-
-def condition_kernel(count, ids, hess, *rest):
+    )(facts, pltpu.with_memory_space_constraint(source, pltpu.HBM), after)
+
+
+def condition_kernel(count, facts, hess, *rest):
     pieces, (_, out, right) = rest[:count], rest[count:]
     width = hess.shape[1] // count
     for t, piece in enumerate(pieces):
-        right[:, pl.ds(pl.multiple_of(ids[t] * width, width), width)] = piece[...]
+        right[:, pl.ds(pl.multiple_of(facts[t] * width, width), width)] = piece[...]
     out[...] = lax.dot_general(
         hess[...], right[...], (((1,), (1,)), ((), ())), preferred_element_type=F32
     ).astype(BF16)
 
 
-def condition(ids, hess, pieces, after):
+def condition(facts, hess, pieces, after):
     rows, queries = hess.shape[0], pieces[0].shape[0]
     return pl.pallas_call(
         functools.partial(condition_kernel, len(pieces)),
@@ -73,17 +73,17 @@
         out_specs=VMEM,
         scratch_shapes=[pltpu.VMEM((queries, hess.shape[1]), BF16)],
         compiler_params=pltpu.CompilerParams(vmem_limit_bytes=12 * MIB),
-    )(ids, hess, *pieces, after)
-
-
-def score_kernel(count, ids, blocks, store, *rest):
+    )(facts, hess, *pieces, after)
+
+
+def score_kernel(count, layers, facts, store, *rest):
     pieces, (_, send, keep, right) = rest[:count], rest[count:]
     rows = keep.shape[1]
     depth = pieces[0].shape[0]
     for t, piece in enumerate(pieces):
-        right[pl.ds(pl.multiple_of(ids[t] * depth, depth), depth), :] = piece[...]
-    for r in [*range(1, blocks.shape[0], 2), *range(0, blocks.shape[0], 2)]:
-        at = pl.ds(pl.multiple_of(blocks[r] * rows, rows), rows)
+        right[pl.ds(pl.multiple_of(facts[t] * depth, depth), depth), :] = piece[...]
+    for r in [*range(1, layers, 2), *range(0, layers, 2)]:
+        at = pl.ds(pl.multiple_of(facts[count + r] * rows, rows), rows)
         part = jnp.dot(store[at, :], right[...], preferred_element_type=F32)
         if r % 2:
             send[r // 2] = part.astype(BF16)
@@ -91,18 +91,17 @@
             keep[r // 2] = part
 
 
-def score(ids, blocks, store, pieces, after):
+def score(layers, facts, store, pieces, after):
     depth, width = pieces[0].shape
-    layers = blocks.shape[0]
     shape = (layers // 2, store.shape[0] // layers, width)
     return pl.pallas_call(
-        functools.partial(score_kernel, len(pieces)),
+        functools.partial(score_kernel, len(pieces), layers),
         out_shape=(jax.ShapeDtypeStruct(shape, BF16), jax.ShapeDtypeStruct(shape, F32)),
-        in_specs=[SMEM, SMEM] + [VMEM] * (1 + len(pieces)) + [ANY],
+        in_specs=[SMEM] + [VMEM] * (1 + len(pieces)) + [ANY],
         out_specs=(VMEM, VMEM),
         scratch_shapes=[pltpu.VMEM((len(pieces) * depth, width), BF16)],
         compiler_params=pltpu.CompilerParams(vmem_limit_bytes=12 * MIB),
-    )(ids, blocks, store, *pieces, after)
+    )(facts, store, *pieces, after)
 
 
 def fold_kernel(keep, got, _, send, left):
@@ -125,38 +124,40 @@
     )(keep, got, after)
 
 
-def finish_kernel(groups, place, *refs):
+def finish_kernel(groups, base, facts, *refs):
     *refs, out = refs
     width = refs[0].shape[2]
     pieces = out.shape[1] // width
     for c in range(pieces // groups):
         for j in range(groups):
             keep, got = refs[2 * (c * groups + j) : 2 * (c * groups + j + 1)]
-            at = place[j] * (out.shape[1] // groups) + c * width
+            at = facts[base + j] * (out.shape[1] // groups) + c * width
             out[:, pl.ds(pl.multiple_of(at, width), width)] = keep[0] + got[0].astype(F32)
 
 
-def finish(place, parts, queries):
-    groups = place.shape[0]
+def finish(groups, base, facts, parts, queries):
     rows = parts[0][0].shape[1]
     return pl.pallas_call(
-        functools.partial(finish_kernel, groups),
+        functools.partial(finish_kernel, groups, base),
         out_shape=jax.ShapeDtypeStruct((rows, queries), F32),
         in_specs=[SMEM] + [VMEM] * sum(map(len, parts)),
         out_specs=VMEM,
         compiler_params=pltpu.CompilerParams(vmem_limit_bytes=12 * MIB),
-    )(place, *[a for part in parts for a in part])
+    )(facts, *[a for part in parts for a in part])
 
 
 def shards(groups, ex, layers, queries, hessian, store):
     chips = ex // CORES
     at_group, at_ex, at_layer = (lax.axis_index(a) for a in ("groups", "ex", "layer"))
     chip, core = at_ex // CORES, at_ex % CORES
-    ids = jnp.stack(
-        [(chip + k) % chips * CORES + (core ^ s) for k in range(chips) for s in range(CORES)]
-    ).astype(jnp.int32)
-    blocks = jnp.stack([at_layer ^ r for r in range(layers)]).astype(jnp.int32)
-    place = jnp.stack([(at_group + j) % groups for j in range(groups)]).astype(jnp.int32)
+    total = queries.shape[0]
+    span = total // groups
+    width = span // CHUNKS
+    facts = [(chip + k) % chips * CORES + (core ^ s) for k in range(chips) for s in range(CORES)]
+    facts += [at_layer ^ r for r in range(layers)]
+    facts += [(at_group + j) % groups for j in range(groups)]
+    facts += [at_group * span + c * width for c in range(CHUNKS)]
+    facts = jnp.stack(facts).astype(jnp.int32)
 
     def from_chip(x, k):
         perm = [(e, (e - k * CORES) % ex) for e in range(ex)]
@@ -174,13 +175,8 @@
     def tie(x, *others):
         return lax.optimization_barrier((x, *others))[0]
 
-    total = queries.shape[0]
-    span = total // groups
-    width = span // CHUNKS
-
     def part_of_queries(c, after):
-        start = (at_group * span + c * width).astype(jnp.int32)[None]
-        return take(start, queries[:, 0, :], after, width)
+        return take(ex + layers + groups + c, facts, queries[:, 0, :], after, width)
 
     def gather_chip(x):
         return [from_chip(x, k) for k in range(1, chips)]
@@ -197,7 +193,7 @@
     def after(token, xs):
         return [tie(x, token) for x in xs]
 
-    scored = functools.partial(score, ids, blocks)
+    scored = functools.partial(score, layers, facts)
     parts = []
 
     def advance(token, chain=False):
@@ -215,14 +211,14 @@
         parts.append([keep, from_layer(send, 1)])
         return parts[-2][0] if parts[1:] else keep
 
-    q0 = part_of_queries(0, ids)
+    q0 = part_of_queries(0, facts)
     q0_there, q0_core = gather_chip(q0), from_core(q0)
-    hess = load(hessian[0], ids)
+    hess = load(hessian[0], facts)
     q0_there = after(hess, q0_there)
     q0_cores = [q0_core] + flip(q0_there)
     q1 = part_of_queries(1, q0_there[-1])
     q1_there, q1_core = gather_chip(q1), from_core(q1)
-    s0 = condition(ids, hess, with_cores([q0] + q0_there, q0_cores), q1)
+    s0 = condition(facts, hess, with_cores([q0] + q0_there, q0_cores), q1)
     s0_there, s0_across, s0_core = gather_chip(s0), gather_group(s0), from_core(s0)
     rows = load(store[:, 0, :], s0)
     q1_there = after(rows, q1_there)
@@ -230,7 +226,7 @@
     s0_there = after(rows, s0_there)
     s0_diagonal = [gather_group(x) for x in s0_there]
     s0_cores = [s0_core] + flip(s0_there)
-    s1 = condition(ids, hess, with_cores([q1] + q1_there, q1_cores), s0_there[-1])
+    s1 = condition(facts, hess, with_cores([q1] + q1_there, q1_cores), s0_there[-1])
     s1_there, s1_core = gather_chip(s1), from_core(s1)
     s0_across = after(s1, s0_across)
     s0_across_cores = flip(s0_across)
@@ -257,7 +253,7 @@
         last = send_parts(scored(rows, with_cores(ours, theirs), last))
     while any(part[0].shape[0] > 1 for part in parts):
         advance(last)
-    return finish(place, parts, total)
+    return finish(groups, ex + layers, facts, parts, total)
 
 
 def solution(mesh):

time: 87 us -> 80.2 us (0.922)
  local copies, waits for them, and re-layouts: 18.1 us -> 0.09 us
  waiting for transfers between devices: 9.52 us -> 16.9 us
  starting transfers between devices: 27.8 us -> 31 us
  Pallas kernels: 30.7 us -> 31.8 us
    unnamed x12 -> x0, local copies, waits for them, and re-layouts: 18.1 us -> none
    ppermute x4, waiting for transfers between devices: 0.01 us -> 7.09 us  [from_chip(): return lax.ppermute(x, 'ex', perm)]
    ppermute x8, starting transfers between devices: 15.3 us -> 17.5 us  [from_layer(): return lax.ppermute(x, 'layer', [(z, z ^ r) for z in range(layers)])]
    ppermute x4, starting transfers between devices: 4.05 us -> 5.45 us  [from_group(): lax.ppermute(x, 'groups', [(g, (g - j) % groups) for g in range(groups)])]
    ppermute x12, starting transfers between devices: 2.41 us -> 1.29 us  [from_core(): return lax.ppermute(x, 'ex', [(e, e ^ 1) for e in range(ex)])]
    pallas_call x7, Pallas kernels: 17.3 us -> 18.4 us  [the longest x4 13.9 us: score(): pl.pallas_call(functools.partial(score_kernel, len(pieces), layers), out_...]
  transfers between devices with their start and end apart: 28 -> 28, of which waited for: 6 -> 7; matrix products, arithmetic and copies ran while one was open for 0% -> 0% of each run, Pallas kernels for 33% -> 36%
where the time goes in v4:
time: 80.2 us; the launch traced here: 80 us
  Pallas kernels  31.8 us (40%)
  starting transfers between devices  31 us (39%)
  waiting for transfers between devices  16.9 us (21%)
    ppermute x8, starting transfers between devices, from_layer(): return lax.ppermute(x, 'layer', [(z, z ^ r) for z in range(layers)])  17.5 us
    pallas_call x4, Pallas kernels, score(): pl.pallas_call(functools.partial(score_kernel, len(pieces), layers), out_...  13.9 us
    ppermute x8, waiting for transfers between devices, from_layer(): return lax.ppermute(x, 'layer', [(z, z ^ r) for z in range(layers)])  9 us
    pallas_call x2, Pallas kernels, load(): pl.pallas_call(load_kernel, out_shape=pltpu.VMEM(source.shape, BF16), in_...  7.38 us
    ppermute x4, waiting for transfers between devices, from_chip(): return lax.ppermute(x, 'ex', perm)  7.09 us
    ppermute x4, starting transfers between devices, from_chip(): return lax.ppermute(x, 'ex', perm)  6.77 us
    pallas_call x2, Pallas kernels, condition(): pl.pallas_call(functools.partial(condition_kernel, len(pieces)), out_shap...  5.91 us
    ppermute x4, starting transfers between devices, from_group(): lax.ppermute(x, 'groups', [(g, (g - j) % groups) for g in range(groups)])  5.45 us
  transfers between devices with their start and end apart: 28, of which 7 were waited for; matrix products, arithmetic and copies ran while one was open for 0% of the time, Pallas kernels for 36%

profile of v4, /device:TPU:0, one launch (start us, length us, event | category | flops | bytes accessed | tf_op | source)
XLA Modules:
  0.0 80.0 jit_solution(8740911828434349825)
XLA Ops:
  0.0 0.1 stack.51.after.facts
  0.1 1.5 %shard_map.38.rest_0_ = bf16[128,1024]{1,0:T(8,128)(2,1)S(1)} custom-call(s32[12]{0:T(128)S(1)} %stack.51.after.facts, bf16[512,1024]{1,0:T(8,128)(2,1)} %bitcast.17, s32[12]{0:T(128)S(1)} %stack.51.after.facts), custom_call_target="tpu_custom_call" | custom-call | tf_op jit(solution)/shard_map/pallas_call | solution.py:47
  1.6 3.0 %collective-permute-start.1 = (bf16[128,1024]{1,0:T(8,128)(2,1)S(1)}, bf16[128,1024]{1,0:T(8,128)(2,1)S(1)}, u32[]{:S(2)}, u32[]{:S(2)}) collective-permute-start(bf16[128,1024]{1,0:T(8,128)(2,1)S(1)} %shard_map.38.rest_0_), channel_id=1, source_target_pairs={{0,8},{4,12},{8,0},{12,4},{1,9},{5,13},{9,1},{13,5},{2,10},{6,14},... | collective-permute-start | bytes 786440 | tf_op jit(solution)/shard_map/ppermute | solution.py:164
  4.6 0.0 collective-permute-start
  4.6 3.4 %shard_map.37.hess = bf16[1024,4096]{1,0:T(8,128)(2,1)S(1)} custom-call(bf16[1024,4096]{1,0:T(8,128)(2,1)} %bitcast.16, s32[12]{0:T(128)S(1)} %stack.51.after.facts), custom_call_target="tpu_custom_call" | custom-call | tf_op jit(solution)/shard_map/pallas_call | solution.py:29
  8.0 2.9 %collective-permute-done.1.after.rest_2_ = bf16[128,1024]{1,0:T(8,128)(2,1)S(1)} collective-permute-done((bf16[128,1024]{1,0:T(8,128)(2,1)S(1)}, bf16[128,1024]{1,0:T(8,128)(2,1)S(1)}, u32[]{:S(2)}, u32[]{:S(2)}) %collective-permute-start.1) | collective-permute-done | bytes 262176 | tf_op jit(solution)/shard_map/ppermute | solution.py:164
  10.9 1.5 %shard_map.39.rest_4_.rest_0_ = bf16[128,1024]{1,0:T(8,128)(2,1)S(1)} custom-call(s32[12]{0:T(128)S(1)} %stack.51.after.facts, bf16[512,1024]{1,0:T(8,128)(2,1)} %bitcast.18, bf16[128,1024]{1,0:T(8,128)(2,1)S(1)} %collective-permute-done.1.after.rest_2_), custom_call_target="tpu_custom_call" | custom-call | tf_op jit(solution)/shard_map/pallas_call | solution.py:47
  12.5 1.8 %collective-permute-start.7 = (bf16[128,1024]{1,0:T(8,128)(2,1)S(1)}, bf16[128,1024]{1,0:T(8,128)(2,1)S(1)}, u32[]{:S(2)}, u32[]{:S(2)}) collective-permute-start(bf16[128,1024]{1,0:T(8,128)(2,1)S(1)} %shard_map.39.rest_4_.rest_0_), channel_id=1, source_target_pairs={{0,8},{4,12},{8,0},{12,4},{1,9},{5,13},{9,1},{13,5},{2,10},{6,14},... | collective-permute-start | bytes 786440 | tf_op jit(solution)/shard_map/ppermute | solution.py:164
  14.3 0.0 collective-permute-done.2.rest_3_
  14.3 3.0 %shard_map.40.after.rest_0_ = bf16[1024,128]{1,0:T(8,128)(2,1)S(1)} custom-call(s32[12]{0:T(128)S(1)} %stack.51.after.facts, bf16[1024,4096]{1,0:T(8,128)(2,1)S(1)} %shard_map.37.hess, bf16[128,1024]{1,0:T(8,128)(2,1)S(1)} %shard_map.38.rest_0_, bf16[128,1024]{1,0:T(8,128)(2,1)S(1)} %collective-permute-done.rest_1_, ...), custom_call_target="tpu_custom_call" | custom-call | tf_op jit(solution)/shard_map/pallas_call | solution.py:69
  17.2 0.4 collective-permute-start.4
  17.6 0.0 collective-permute-start.6
  17.6 4.0 %shard_map.41.store = bf16[1280,4096]{1,0:T(8,128)(2,1)S(1)} custom-call(bf16[1280,4096]{1,0:T(8,128)(2,1)} %bitcast.15, bf16[1024,128]{1,0:T(8,128)(2,1)S(1)} %shard_map.40.after.rest_0_), custom_call_target="tpu_custom_call" | custom-call | tf_op jit(solution)/shard_map/pallas_call | solution.py:29
  21.6 0.0 collective-permute-done.7.rest_2_
  21.6 0.5 collective-permute-start.8
  22.2 1.7 %collective-permute-start.10 = (bf16[1024,128]{1,0:T(8,128)(2,1)S(1)}, bf16[1024,128]{1,0:T(8,128)(2,1)S(1)}, u32[]{:S(2)}, u32[]{:S(2)}) collective-permute-start(bf16[1024,128]{1,0:T(8,128)(2,1)S(1)} %shard_map.40.after.rest_0_), channel_id=1, source_target_pairs={{0,16},{16,0},{1,17},{17,1},{2,18},{18,2},{3,19},{19,3},{4,20},{20... | collective-permute-start | bytes 786440 | tf_op jit(solution)/shard_map/ppermute | solution.py:170
  23.9 3.0 %collective-permute-done.4.rest_4_.rest_2_ = bf16[1024,128]{1,0:T(8,128)(2,1)S(1)} collective-permute-done((bf16[1024,128]{1,0:T(8,128)(2,1)S(1)}, bf16[1024,128]{1,0:T(8,128)(2,1)S(1)}, u32[]{:S(2)}, u32[]{:S(2)}) %collective-permute-start.4) | collective-permute-done | bytes 262176 | tf_op jit(solution)/shard_map/ppermute | solution.py:164
  26.9 1.7 %collective-permute-start.12 = (bf16[1024,128]{1,0:T(8,128)(2,1)S(1)}, bf16[1024,128]{1,0:T(8,128)(2,1)S(1)}, u32[]{:S(2)}, u32[]{:S(2)}) collective-permute-start(bf16[1024,128]{1,0:T(8,128)(2,1)S(1)} %collective-permute-done.4.rest_4_.rest_2_), channel_id=1, source_target_pairs={{0,16},{16,0},{1,17},{17,1},{2,18},{18,2},{3,19},{19,3},{4,20},{20... | collective-permute-start | bytes 786440 | tf_op jit(solution)/shard_map/ppermute | solution.py:170
  28.6 3.0 %shard_map.42.rest_4_.rest_0_ = bf16[1024,128]{1,0:T(8,128)(2,1)S(1)} custom-call(s32[12]{0:T(128)S(1)} %stack.51.after.facts, bf16[1024,4096]{1,0:T(8,128)(2,1)S(1)} %shard_map.37.hess, bf16[128,1024]{1,0:T(8,128)(2,1)S(1)} %shard_map.39.rest_4_.rest_0_, bf16[128,1024]{1,0:T(8,128)(2,1)S(1)} %collective-permute-done.6.rest_1_, ...), custom_call_target="tpu_custom_call" | custom-call | tf_op jit(solution)/shard_map/pallas_call | solution.py:69
  31.5 1.6 %collective-permute-start.17 = (bf16[1024,128]{1,0:T(8,128)(2,1)S(1)}, bf16[1024,128]{1,0:T(8,128)(2,1)S(1)}, u32[]{:S(2)}, u32[]{:S(2)}) collective-permute-start(bf16[1024,128]{1,0:T(8,128)(2,1)S(1)} %shard_map.42.rest_4_.rest_0_), channel_id=1, source_target_pairs={{0,8},{4,12},{8,0},{12,4},{1,9},{5,13},{9,1},{13,5},{2,10},{6,14},... | collective-permute-start | bytes 786440 | tf_op jit(solution)/shard_map/ppermute | solution.py:164
  33.1 0.0 collective-permute-done.10.rest_0_
  33.1 0.0 collective-permute-start.11
  33.1 0.0 collective-permute-done.5.rest_3_
  33.1 3.5 %shard_map.43 = (bf16[2,320,128]{2,1,0:T(8,128)(2,1)S(1)}, f32[2,320,128]{2,1,0:T(8,128)S(1)}) custom-call(s32[12]{0:T(128)S(1)} %stack.51.after.facts, bf16[1280,4096]{1,0:T(8,128)(2,1)S(1)} %shard_map.41.store, bf16[1024,128]{1,0:T(8,128)(2,1)S(1)} %shard_map.40.after.rest_0_, bf16[1024,128]{1,0:T(8,128)(2,1)S(1)} %collective-permute-done.3.rest_1_, ...), custom_call_target="tpu_custom_call" | custom-call | tf_op jit(solution)/shard_map/pallas_call | solution.py:97
  36.6 0.6 collective-permute-start.13
  37.2 0.1 collective-permute-start.16
  37.3 1.6 %collective-permute-start.9 = (bf16[2,320,128]{2,1,0:T(8,128)(2,1)S(1)}, bf16[2,320,128]{2,1,0:T(8,128)(2,1)S(1)}, u32[]{:S(2)}, u32[]{:S(2)}) collective-permute-start(bf16[2,320,128]{2,1,0:T(8,128)(2,1)S(1)} %get-tuple-element.37), channel_id=1, source_target_pairs={{0,1},{1,0},{2,3},{3,2},{4,5},{5,4},{6,7},{7,6},{8,9},{9,8},{10,11... | collective-permute-start | bytes 491528 | tf_op jit(solution)/shard_map/ppermute | solution.py:173
  38.9 1.2 %collective-permute-done.17.rest_2_ = bf16[1024,128]{1,0:T(8,128)(2,1)S(1)} collective-permute-done((bf16[1024,128]{1,0:T(8,128)(2,1)S(1)}, bf16[1024,128]{1,0:T(8,128)(2,1)S(1)}, u32[]{:S(2)}, u32[]{:S(2)}) %collective-permute-start.17) | collective-permute-done | bytes 262176 | tf_op jit(solution)/shard_map/ppermute | solution.py:164
  40.0 0.0 collective-permute-start.18
  40.1 0.3 collective-permute-start.23
  40.4 1.7 %collective-permute-start.21 = (bf16[1024,128]{1,0:T(8,128)(2,1)S(1)}, bf16[1024,128]{1,0:T(8,128)(2,1)S(1)}, u32[]{:S(2)}, u32[]{:S(2)}) collective-permute-start(bf16[1024,128]{1,0:T(8,128)(2,1)S(1)} %shard_map.42.rest_4_.rest_0_), channel_id=1, source_target_pairs={{0,16},{16,0},{1,17},{17,1},{2,18},{18,2},{3,19},{19,3},{4,20},{20... | collective-permute-start | bytes 786440 | tf_op jit(solution)/shard_map/ppermute | solution.py:170
  42.1 3.5 %shard_map.44 = (bf16[2,320,128]{2,1,0:T(8,128)(2,1)S(1)}, f32[2,320,128]{2,1,0:T(8,128)S(1)}) custom-call(s32[12]{0:T(128)S(1)} %stack.51.after.facts, bf16[1280,4096]{1,0:T(8,128)(2,1)S(1)} %shard_map.41.store, bf16[1024,128]{1,0:T(8,128)(2,1)S(1)} %collective-permute-done.10.rest_0_, bf16[1024,128]{1,0:T(8,128)(2,1)S(1)} %collective-permute-done.11.rest_1_, ...), custom_call_target="tpu_custom_call" | custom-call | tf_op jit(solution)/shard_map/pallas_call | solution.py:97
  45.6 1.6 %collective-permute-start.15 = (bf16[2,320,128]{2,1,0:T(8,128)(2,1)S(1)}, bf16[2,320,128]{2,1,0:T(8,128)(2,1)S(1)}, u32[]{:S(2)}, u32[]{:S(2)}) collective-permute-start(bf16[2,320,128]{2,1,0:T(8,128)(2,1)S(1)} %get-tuple-element.43), channel_id=1, source_target_pairs={{0,1},{1,0},{2,3},{3,2},{4,5},{5,4},{6,7},{7,6},{8,9},{9,8},{10,11... | collective-permute-start | bytes 491528 | tf_op jit(solution)/shard_map/ppermute | solution.py:173
  47.3 2.7 %collective-permute-start.14 = (bf16[1,320,128]{2,1,0:T(8,128)(2,1)S(1)}, bf16[1,320,128]{2,1,0:T(8,128)(2,1)S(1)}, u32[]{:S(2)}, u32[]{:S(2)}) collective-permute-start(bf16[1,320,128]{2,1,0:T(8,128)(2,1)S(1)} %get-tuple-element.42), channel_id=1, source_target_pairs={{0,2},{1,3},{2,0},{3,1},{4,6},{5,7},{6,4},{7,5},{8,10},{9,11},{10,... | collective-permute-start | bytes 245768 | tf_op jit(solution)/shard_map/ppermute | solution.py:173
  49.9 3.5 %shard_map.46 = (bf16[2,320,128]{2,1,0:T(8,128)(2,1)S(1)}, f32[2,320,128]{2,1,0:T(8,128)S(1)}) custom-call(s32[12]{0:T(128)S(1)} %stack.51.after.facts, bf16[1280,4096]{1,0:T(8,128)(2,1)S(1)} %shard_map.41.store, bf16[1024,128]{1,0:T(8,128)(2,1)S(1)} %shard_map.42.rest_4_.rest_0_, bf16[1024,128]{1,0:T(8,128)(2,1)S(1)} %collective-permute-done.16.rest_1_, ...), custom_call_target="tpu_custom_call" | custom-call | tf_op jit(solution)/shard_map/pallas_call | solution.py:97
  53.4 0.0 collective-permute-done.15.got
  53.5 0.1 collective-permute-start.24
  53.6 0.8 %collective-permute-done.21.rest_0_ = bf16[1024,128]{1,0:T(8,128)(2,1)S(1)} collective-permute-done((bf16[1024,128]{1,0:T(8,128)(2,1)S(1)}, bf16[1024,128]{1,0:T(8,128)(2,1)S(1)}, u32[]{:S(2)}, u32[]{:S(2)}) %collective-permute-start.21) | collective-permute-done | bytes 262176 | tf_op jit(solution)/shard_map/ppermute | solution.py:170
  54.4 2.6 %collective-permute-start.19 = (bf16[1,320,128]{2,1,0:T(8,128)(2,1)S(1)}, bf16[1,320,128]{2,1,0:T(8,128)(2,1)S(1)}, u32[]{:S(2)}, u32[]{:S(2)}) collective-permute-start(bf16[1,320,128]{2,1,0:T(8,128)(2,1)S(1)} %get-tuple-element.48), channel_id=1, source_target_pairs={{0,2},{1,3},{2,0},{3,1},{4,6},{5,7},{6,4},{7,5},{8,10},{9,11},{10,... | collective-permute-start | bytes 245768 | tf_op jit(solution)/shard_map/ppermute | solution.py:173
  57.0 1.6 %collective-permute-start.20 = (bf16[2,320,128]{2,1,0:T(8,128)(2,1)S(1)}, bf16[2,320,128]{2,1,0:T(8,128)(2,1)S(1)}, u32[]{:S(2)}, u32[]{:S(2)}) collective-permute-start(bf16[2,320,128]{2,1,0:T(8,128)(2,1)S(1)} %get-tuple-element.49), channel_id=1, source_target_pairs={{0,1},{1,0},{2,3},{3,2},{4,5},{5,4},{6,7},{7,6},{8,9},{9,8},{10,11... | collective-permute-start | bytes 491528 | tf_op jit(solution)/shard_map/ppermute | solution.py:173
  58.6 2.9 %collective-permute-done.19.refs_3_ = bf16[1,320,128]{2,1,0:T(8,128)(2,1)S(1)} collective-permute-done((bf16[1,320,128]{2,1,0:T(8,128)(2,1)S(1)}, bf16[1,320,128]{2,1,0:T(8,128)(2,1)S(1)}, u32[]{:S(2)}, u32[]{:S(2)}) %collective-permute-start.19) | collective-permute-done | bytes 81952 | tf_op jit(solution)/shard_map/ppermute | solution.py:173
  61.5 3.5 %shard_map.48 = (bf16[2,320,128]{2,1,0:T(8,128)(2,1)S(1)}, f32[2,320,128]{2,1,0:T(8,128)S(1)}) custom-call(s32[12]{0:T(128)S(1)} %stack.51.after.facts, bf16[1280,4096]{1,0:T(8,128)(2,1)S(1)} %shard_map.41.store, bf16[1024,128]{1,0:T(8,128)(2,1)S(1)} %collective-permute-done.21.rest_0_, bf16[1024,128]{1,0:T(8,128)(2,1)S(1)} %collective-permute-done.22.rest_1_, ...), custom_call_target="tpu_custom_call" | custom-call | tf_op jit(solution)/shard_map/pallas_call | solution.py:97
  65.0 1.4 %collective-permute-start.26 = (bf16[2,320,128]{2,1,0:T(8,128)(2,1)S(1)}, bf16[2,320,128]{2,1,0:T(8,128)(2,1)S(1)}, u32[]{:S(2)}, u32[]{:S(2)}) collective-permute-start(bf16[2,320,128]{2,1,0:T(8,128)(2,1)S(1)} %get-tuple-element.58), channel_id=1, source_target_pairs={{0,1},{1,0},{2,3},{3,2},{4,5},{5,4},{6,7},{7,6},{8,9},{9,8},{10,11... | collective-permute-start | bytes 491528 | tf_op jit(solution)/shard_map/ppermute | solution.py:173
  66.5 3.3 %collective-permute-start.25 = (bf16[1,320,128]{2,1,0:T(8,128)(2,1)S(1)}, bf16[1,320,128]{2,1,0:T(8,128)(2,1)S(1)}, u32[]{:S(2)}, u32[]{:S(2)}) collective-permute-start(bf16[1,320,128]{2,1,0:T(8,128)(2,1)S(1)} %get-tuple-element.57), channel_id=1, source_target_pairs={{0,2},{1,3},{2,0},{3,1},{4,6},{5,7},{6,4},{7,5},{8,10},{9,11},{10,... | collective-permute-start | bytes 245768 | tf_op jit(solution)/shard_map/ppermute | solution.py:173
  69.7 2.6 %collective-permute-done.26.got = bf16[2,320,128]{2,1,0:T(8,128)(2,1)S(1)} collective-permute-done((bf16[2,320,128]{2,1,0:T(8,128)(2,1)S(1)}, bf16[2,320,128]{2,1,0:T(8,128)(2,1)S(1)}, u32[]{:S(2)}, u32[]{:S(2)}) %collective-permute-start.26) | collective-permute-done | bytes 163872 | tf_op jit(solution)/shard_map/ppermute | solution.py:173
  72.4 2.7 %collective-permute-start.27 = (bf16[1,320,128]{2,1,0:T(8,128)(2,1)S(1)}, bf16[1,320,128]{2,1,0:T(8,128)(2,1)S(1)}, u32[]{:S(2)}, u32[]{:S(2)}) collective-permute-start(bf16[1,320,128]{2,1,0:T(8,128)(2,1)S(1)} %get-tuple-element.60), channel_id=1, source_target_pairs={{0,2},{1,3},{2,0},{3,1},{4,6},{5,7},{6,4},{7,5},{8,10},{9,11},{10,... | collective-permute-start | bytes 245768 | tf_op jit(solution)/shard_map/ppermute | solution.py:173
  75.1 3.4 %collective-permute-done.27.refs_7_ = bf16[1,320,128]{2,1,0:T(8,128)(2,1)S(1)} collective-permute-done((bf16[1,320,128]{2,1,0:T(8,128)(2,1)S(1)}, bf16[1,320,128]{2,1,0:T(8,128)(2,1)S(1)}, u32[]{:S(2)}, u32[]{:S(2)}) %collective-permute-start.27) | collective-permute-done | bytes 81952 | tf_op jit(solution)/shard_map/ppermute | solution.py:173
  78.5 1.5 %shard_map.51 = f32[320,512]{1,0:T(8,128)} custom-call(s32[12]{0:T(128)S(1)} %stack.51.after.facts, f32[1,320,128]{2,1,0:T(8,128)S(1)} %get-tuple-element.41.rest_4_.refs_0_, bf16[1,320,128]{2,1,0:T(8,128)(2,1)S(1)} %collective-permute-done.14.refs_1_, f32[1,320,128]{2,1,0:T(8,128)S(1)} %get-tuple-element.53.rest_4_.refs_2_, ...), custom_call_target="tpu_custom_call" | custom-call | tf_op jit(solution)/shard_map/pallas_call | solution.py:140
  (24 shorter events, 0.2 us)
Async XLA Ops:
  1.6 9.3 %collective-permute-start.1 = (bf16[128,1024]{1,0:T(8,128)(2,1)S(1)}, bf16[128,1024]{1,0:T(8,128)(2,1)S(1)}, u32[]{:S(2)}, u32[]{:S(2)}) collective-permute-start(bf16[128,1024]{1,0:T(8,128)(2,1)S(1)} %shard_map.38.rest_0_), channel_id=1, source_target_pairs={{0,8},{4,12},{8,0},{12,4},{1,9},{5,13},{9,1},{13,5},{2,10},{6,14},... | collective-permute-start | bytes 786440 | tf_op jit(solution)/shard_map/ppermute | solution.py:164
  4.6 9.6 %collective-permute-start = (bf16[128,1024]{1,0:T(8,128)(2,1)S(1)}, bf16[128,1024]{1,0:T(8,128)(2,1)S(1)}, u32[]{:S(2)}, u32[]{:S(2)}) collective-permute-start(bf16[128,1024]{1,0:T(8,128)(2,1)S(1)} %shard_map.38.rest_0_), channel_id=1, source_target_pairs={{0,4},{4,0},{8,12},{12,8},{1,5},{5,1},{9,13},{13,9},{2,6},{6,2},{1... | collective-permute-start | bytes 786440 | tf_op jit(solution)/shard_map/ppermute | solution.py:167
  10.9 3.3 %collective-permute-start.2 = (bf16[128,1024]{1,0:T(8,128)(2,1)S(1)}, bf16[128,1024]{1,0:T(8,128)(2,1)S(1)}, u32[]{:S(2)}, u32[]{:S(2)}) collective-permute-start(bf16[128,1024]{1,0:T(8,128)(2,1)S(1)} %collective-permute-done.1.after.rest_2_), channel_id=1, source_target_pairs={{0,4},{4,0},{8,12},{12,8},{1,5},{5,1},{9,13},{13,9},{2,6},{6,2},{1... | collective-permute-start | bytes 786440 | tf_op jit(solution)/shard_map/ppermute | solution.py:167
  12.5 9.2 %collective-permute-start.7 = (bf16[128,1024]{1,0:T(8,128)(2,1)S(1)}, bf16[128,1024]{1,0:T(8,128)(2,1)S(1)}, u32[]{:S(2)}, u32[]{:S(2)}) collective-permute-start(bf16[128,1024]{1,0:T(8,128)(2,1)S(1)} %shard_map.39.rest_4_.rest_0_), channel_id=1, source_target_pairs={{0,8},{4,12},{8,0},{12,4},{1,9},{5,13},{9,1},{13,5},{2,10},{6,14},... | collective-permute-start | bytes 786440 | tf_op jit(solution)/shard_map/ppermute | solution.py:164
  17.2 9.6 %collective-permute-start.4 = (bf16[1024,128]{1,0:T(8,128)(2,1)S(1)}, bf16[1024,128]{1,0:T(8,128)(2,1)S(1)}, u32[]{:S(2)}, u32[]{:S(2)}) collective-permute-start(bf16[1024,128]{1,0:T(8,128)(2,1)S(1)} %shard_map.40.after.rest_0_), channel_id=1, source_target_pairs={{0,8},{4,12},{8,0},{12,4},{1,9},{5,13},{9,1},{13,5},{2,10},{6,14},... | collective-permute-start | bytes 786440 | tf_op jit(solution)/shard_map/ppermute | solution.py:164
  17.6 9.3 %collective-permute-start.6 = (bf16[128,1024]{1,0:T(8,128)(2,1)S(1)}, bf16[128,1024]{1,0:T(8,128)(2,1)S(1)}, u32[]{:S(2)}, u32[]{:S(2)}) collective-permute-start(bf16[128,1024]{1,0:T(8,128)(2,1)S(1)} %shard_map.39.rest_4_.rest_0_), channel_id=1, source_target_pairs={{0,4},{4,0},{8,12},{12,8},{1,5},{5,1},{9,13},{13,9},{2,6},{6,2},{1... | collective-permute-start | bytes 786440 | tf_op jit(solution)/shard_map/ppermute | solution.py:167
  21.6 7.0 %collective-permute-start.8 = (bf16[128,1024]{1,0:T(8,128)(2,1)S(1)}, bf16[128,1024]{1,0:T(8,128)(2,1)S(1)}, u32[]{:S(2)}, u32[]{:S(2)}) collective-permute-start(bf16[128,1024]{1,0:T(8,128)(2,1)S(1)} %collective-permute-done.7.rest_2_), channel_id=1, source_target_pairs={{0,4},{4,0},{8,12},{12,8},{1,5},{5,1},{9,13},{13,9},{2,6},{6,2},{1... | collective-permute-start | bytes 786440 | tf_op jit(solution)/shard_map/ppermute | solution.py:167
  22.2 11.0 %collective-permute-start.10 = (bf16[1024,128]{1,0:T(8,128)(2,1)S(1)}, bf16[1024,128]{1,0:T(8,128)(2,1)S(1)}, u32[]{:S(2)}, u32[]{:S(2)}) collective-permute-start(bf16[1024,128]{1,0:T(8,128)(2,1)S(1)} %shard_map.40.after.rest_0_), channel_id=1, source_target_pairs={{0,16},{16,0},{1,17},{17,1},{2,18},{18,2},{3,19},{19,3},{4,20},{20... | collective-permute-start | bytes 786440 | tf_op jit(solution)/shard_map/ppermute | solution.py:170
  23.9 9.3 %collective-permute-start.3 = (bf16[1024,128]{1,0:T(8,128)(2,1)S(1)}, bf16[1024,128]{1,0:T(8,128)(2,1)S(1)}, u32[]{:S(2)}, u32[]{:S(2)}) collective-permute-start(bf16[1024,128]{1,0:T(8,128)(2,1)S(1)} %shard_map.40.after.rest_0_), channel_id=1, source_target_pairs={{0,4},{4,0},{8,12},{12,8},{1,5},{5,1},{9,13},{13,9},{2,6},{6,2},{1... | collective-permute-start | bytes 786440 | tf_op jit(solution)/shard_map/ppermute | solution.py:167
  26.9 6.3 %collective-permute-start.5 = (bf16[1024,128]{1,0:T(8,128)(2,1)S(1)}, bf16[1024,128]{1,0:T(8,128)(2,1)S(1)}, u32[]{:S(2)}, u32[]{:S(2)}) collective-permute-start(bf16[1024,128]{1,0:T(8,128)(2,1)S(1)} %collective-permute-done.4.rest_4_.rest_2_), channel_id=1, source_target_pairs={{0,4},{4,0},{8,12},{12,8},{1,5},{5,1},{9,13},{13,9},{2,6},{6,2},{1... | collective-permute-start | bytes 786440 | tf_op jit(solution)/shard_map/ppermute | solution.py:167
  26.9 9.8 %collective-permute-start.12 = (bf16[1024,128]{1,0:T(8,128)(2,1)S(1)}, bf16[1024,128]{1,0:T(8,128)(2,1)S(1)}, u32[]{:S(2)}, u32[]{:S(2)}) collective-permute-start(bf16[1024,128]{1,0:T(8,128)(2,1)S(1)} %collective-permute-done.4.rest_4_.rest_2_), channel_id=1, source_target_pairs={{0,16},{16,0},{1,17},{17,1},{2,18},{18,2},{3,19},{19,3},{4,20},{20... | collective-permute-start | bytes 786440 | tf_op jit(solution)/shard_map/ppermute | solution.py:170
  31.5 8.5 %collective-permute-start.17 = (bf16[1024,128]{1,0:T(8,128)(2,1)S(1)}, bf16[1024,128]{1,0:T(8,128)(2,1)S(1)}, u32[]{:S(2)}, u32[]{:S(2)}) collective-permute-start(bf16[1024,128]{1,0:T(8,128)(2,1)S(1)} %shard_map.42.rest_4_.rest_0_), channel_id=1, source_target_pairs={{0,8},{4,12},{8,0},{12,4},{1,9},{5,13},{9,1},{13,5},{2,10},{6,14},... | collective-permute-start | bytes 786440 | tf_op jit(solution)/shard_map/ppermute | solution.py:164
  33.1 6.9 %collective-permute-start.11 = (bf16[1024,128]{1,0:T(8,128)(2,1)S(1)}, bf16[1024,128]{1,0:T(8,128)(2,1)S(1)}, u32[]{:S(2)}, u32[]{:S(2)}) collective-permute-start(bf16[1024,128]{1,0:T(8,128)(2,1)S(1)} %collective-permute-done.10.rest_0_), channel_id=1, source_target_pairs={{0,4},{4,0},{8,12},{12,8},{1,5},{5,1},{9,13},{13,9},{2,6},{6,2},{1... | collective-permute-start | bytes 786440 | tf_op jit(solution)/shard_map/ppermute | solution.py:167
  36.6 3.7 %collective-permute-start.13 = (bf16[1024,128]{1,0:T(8,128)(2,1)S(1)}, bf16[1024,128]{1,0:T(8,128)(2,1)S(1)}, u32[]{:S(2)}, u32[]{:S(2)}) collective-permute-start(bf16[1024,128]{1,0:T(8,128)(2,1)S(1)} %collective-permute-done.12.rest_2_), channel_id=1, source_target_pairs={{0,4},{4,0},{8,12},{12,8},{1,5},{5,1},{9,13},{13,9},{2,6},{6,2},{1... | collective-permute-start | bytes 786440 | tf_op jit(solution)/shard_map/ppermute | solution.py:167
  37.2 10.0 %collective-permute-start.16 = (bf16[1024,128]{1,0:T(8,128)(2,1)S(1)}, bf16[1024,128]{1,0:T(8,128)(2,1)S(1)}, u32[]{:S(2)}, u32[]{:S(2)}) collective-permute-start(bf16[1024,128]{1,0:T(8,128)(2,1)S(1)} %shard_map.42.rest_4_.rest_0_), channel_id=1, source_target_pairs={{0,4},{4,0},{8,12},{12,8},{1,5},{5,1},{9,13},{13,9},{2,6},{6,2},{1... | collective-permute-start | bytes 786440 | tf_op jit(solution)/shard_map/ppermute | solution.py:167
  37.3 8.3 %collective-permute-start.9 = (bf16[2,320,128]{2,1,0:T(8,128)(2,1)S(1)}, bf16[2,320,128]{2,1,0:T(8,128)(2,1)S(1)}, u32[]{:S(2)}, u32[]{:S(2)}) collective-permute-start(bf16[2,320,128]{2,1,0:T(8,128)(2,1)S(1)} %get-tuple-element.37), channel_id=1, source_target_pairs={{0,1},{1,0},{2,3},{3,2},{4,5},{5,4},{6,7},{7,6},{8,9},{9,8},{10,11... | collective-permute-start | bytes 491528 | tf_op jit(solution)/shard_map/ppermute | solution.py:173
  40.0 9.9 %collective-permute-start.18 = (bf16[1024,128]{1,0:T(8,128)(2,1)S(1)}, bf16[1024,128]{1,0:T(8,128)(2,1)S(1)}, u32[]{:S(2)}, u32[]{:S(2)}) collective-permute-start(bf16[1024,128]{1,0:T(8,128)(2,1)S(1)} %collective-permute-done.17.rest_2_), channel_id=1, source_target_pairs={{0,4},{4,0},{8,12},{12,8},{1,5},{5,1},{9,13},{13,9},{2,6},{6,2},{1... | collective-permute-start | bytes 786440 | tf_op jit(solution)/shard_map/ppermute | solution.py:167
  40.1 13.4 %collective-permute-start.23 = (bf16[1024,128]{1,0:T(8,128)(2,1)S(1)}, bf16[1024,128]{1,0:T(8,128)(2,1)S(1)}, u32[]{:S(2)}, u32[]{:S(2)}) collective-permute-start(bf16[1024,128]{1,0:T(8,128)(2,1)S(1)} %collective-permute-done.17.rest_2_), channel_id=1, source_target_pairs={{0,16},{16,0},{1,17},{17,1},{2,18},{18,2},{3,19},{19,3},{4,20},{20... | collective-permute-start | bytes 786440 | tf_op jit(solution)/shard_map/ppermute | solution.py:170
  40.4 14.0 %collective-permute-start.21 = (bf16[1024,128]{1,0:T(8,128)(2,1)S(1)}, bf16[1024,128]{1,0:T(8,128)(2,1)S(1)}, u32[]{:S(2)}, u32[]{:S(2)}) collective-permute-start(bf16[1024,128]{1,0:T(8,128)(2,1)S(1)} %shard_map.42.rest_4_.rest_0_), channel_id=1, source_target_pairs={{0,16},{16,0},{1,17},{17,1},{2,18},{18,2},{3,19},{19,3},{4,20},{20... | collective-permute-start | bytes 786440 | tf_op jit(solution)/shard_map/ppermute | solution.py:170
  45.6 7.9 %collective-permute-start.15 = (bf16[2,320,128]{2,1,0:T(8,128)(2,1)S(1)}, bf16[2,320,128]{2,1,0:T(8,128)(2,1)S(1)}, u32[]{:S(2)}, u32[]{:S(2)}) collective-permute-start(bf16[2,320,128]{2,1,0:T(8,128)(2,1)S(1)} %get-tuple-element.43), channel_id=1, source_target_pairs={{0,1},{1,0},{2,3},{3,2},{4,5},{5,4},{6,7},{7,6},{8,9},{9,8},{10,11... | collective-permute-start | bytes 491528 | tf_op jit(solution)/shard_map/ppermute | solution.py:173
  47.3 6.1 %collective-permute-start.14 = (bf16[1,320,128]{2,1,0:T(8,128)(2,1)S(1)}, bf16[1,320,128]{2,1,0:T(8,128)(2,1)S(1)}, u32[]{:S(2)}, u32[]{:S(2)}) collective-permute-start(bf16[1,320,128]{2,1,0:T(8,128)(2,1)S(1)} %get-tuple-element.42), channel_id=1, source_target_pairs={{0,2},{1,3},{2,0},{3,1},{4,6},{5,7},{6,4},{7,5},{8,10},{9,11},{10,... | collective-permute-start | bytes 245768 | tf_op jit(solution)/shard_map/ppermute | solution.py:173
  53.5 8.0 %collective-permute-start.24 = (bf16[1024,128]{1,0:T(8,128)(2,1)S(1)}, bf16[1024,128]{1,0:T(8,128)(2,1)S(1)}, u32[]{:S(2)}, u32[]{:S(2)}) collective-permute-start(bf16[1024,128]{1,0:T(8,128)(2,1)S(1)} %collective-permute-done.23.rest_2_), channel_id=1, source_target_pairs={{0,4},{4,0},{8,12},{12,8},{1,5},{5,1},{9,13},{13,9},{2,6},{6,2},{1... | collective-permute-start | bytes 786440 | tf_op jit(solution)/shard_map/ppermute | solution.py:167
  54.4 7.1 %collective-permute-start.22 = (bf16[1024,128]{1,0:T(8,128)(2,1)S(1)}, bf16[1024,128]{1,0:T(8,128)(2,1)S(1)}, u32[]{:S(2)}, u32[]{:S(2)}) collective-permute-start(bf16[1024,128]{1,0:T(8,128)(2,1)S(1)} %collective-permute-done.21.rest_0_), channel_id=1, source_target_pairs={{0,4},{4,0},{8,12},{12,8},{1,5},{5,1},{9,13},{13,9},{2,6},{6,2},{1... | collective-permute-start | bytes 786440 | tf_op jit(solution)/shard_map/ppermute | solution.py:167
  54.4 7.1 %collective-permute-start.19 = (bf16[1,320,128]{2,1,0:T(8,128)(2,1)S(1)}, bf16[1,320,128]{2,1,0:T(8,128)(2,1)S(1)}, u32[]{:S(2)}, u32[]{:S(2)}) collective-permute-start(bf16[1,320,128]{2,1,0:T(8,128)(2,1)S(1)} %get-tuple-element.48), channel_id=1, source_target_pairs={{0,2},{1,3},{2,0},{3,1},{4,6},{5,7},{6,4},{7,5},{8,10},{9,11},{10,... | collective-permute-start | bytes 245768 | tf_op jit(solution)/shard_map/ppermute | solution.py:173
  57.0 9.4 %collective-permute-start.20 = (bf16[2,320,128]{2,1,0:T(8,128)(2,1)S(1)}, bf16[2,320,128]{2,1,0:T(8,128)(2,1)S(1)}, u32[]{:S(2)}, u32[]{:S(2)}) collective-permute-start(bf16[2,320,128]{2,1,0:T(8,128)(2,1)S(1)} %get-tuple-element.49), channel_id=1, source_target_pairs={{0,1},{1,0},{2,3},{3,2},{4,5},{5,4},{6,7},{7,6},{8,9},{9,8},{10,11... | collective-permute-start | bytes 491528 | tf_op jit(solution)/shard_map/ppermute | solution.py:173
  65.0 7.4 %collective-permute-start.26 = (bf16[2,320,128]{2,1,0:T(8,128)(2,1)S(1)}, bf16[2,320,128]{2,1,0:T(8,128)(2,1)S(1)}, u32[]{:S(2)}, u32[]{:S(2)}) collective-permute-start(bf16[2,320,128]{2,1,0:T(8,128)(2,1)S(1)} %get-tuple-element.58), channel_id=1, source_target_pairs={{0,1},{1,0},{2,3},{3,2},{4,5},{5,4},{6,7},{7,6},{8,9},{9,8},{10,11... | collective-permute-start | bytes 491528 | tf_op jit(solution)/shard_map/ppermute | solution.py:173
  66.5 8.7 %collective-permute-start.25 = (bf16[1,320,128]{2,1,0:T(8,128)(2,1)S(1)}, bf16[1,320,128]{2,1,0:T(8,128)(2,1)S(1)}, u32[]{:S(2)}, u32[]{:S(2)}) collective-permute-start(bf16[1,320,128]{2,1,0:T(8,128)(2,1)S(1)} %get-tuple-element.57), channel_id=1, source_target_pairs={{0,2},{1,3},{2,0},{3,1},{4,6},{5,7},{6,4},{7,5},{8,10},{9,11},{10,... | collective-permute-start | bytes 245768 | tf_op jit(solution)/shard_map/ppermute | solution.py:173
  72.4 6.1 %collective-permute-start.27 = (bf16[1,320,128]{2,1,0:T(8,128)(2,1)S(1)}, bf16[1,320,128]{2,1,0:T(8,128)(2,1)S(1)}, u32[]{:S(2)}, u32[]{:S(2)}) collective-permute-start(bf16[1,320,128]{2,1,0:T(8,128)(2,1)S(1)} %get-tuple-element.60), channel_id=1, source_target_pairs={{0,2},{1,3},{2,0},{3,1},{4,6},{5,7},{6,4},{7,5},{8,10},{9,11},{10,... | collective-permute-start | bytes 245768 | tf_op jit(solution)/shard_map/ppermute | solution.py:173

commit v5 on v0

v5 whole, which is shorter than its diff:
```python
import functools

import jax
import jax.numpy as jnp
from jax import lax
from jax.experimental import pallas as pl
from jax.experimental.pallas import tpu as pltpu
from jax.sharding import PartitionSpec as P

F32, BF16 = jnp.float32, jnp.bfloat16
CORES = 2
COSTS = {
    "load_hessian": 1_000_000_000_000,
    "condition_here": 1_000_000_000_000,
    "own_here": 3_000_000_000,
    "other_here": 1_000_000_000_000,
    "sum0": 1_000_000_000_000,
    "sum1": 3_000_000_000,
    "sum2": 3_000_000_000,
}
MIB = 1 << 20
VMEM = pl.BlockSpec(memory_space=pltpu.VMEM)
SMEM = pl.BlockSpec(memory_space=pltpu.SMEM)
ANY = pl.BlockSpec(memory_space=pl.ANY)


HBM = pl.BlockSpec(memory_space=pltpu.HBM)


def positions(groups, ex, layers):
    chips = ex // CORES
    chip, core = lax.axis_index("ex") // CORES, lax.axis_index("ex") % CORES
    ids = [lax.rem(chip + k, chips) * CORES + (core ^ s) for k in range(chips) for s in range(CORES)]
    blocks = [lax.axis_index("layer") ^ r for r in range(layers)]
    place = [lax.rem(lax.axis_index("groups") + j, groups) for j in range(groups)]
    return ids, blocks, place


def take_kernel(source, out, sem):
    rows = out.shape[0]
    at = pl.ds(pl.multiple_of(lax.axis_index("groups") * rows, rows), rows)
    copy = pltpu.make_async_copy(source.at[at, :], out, sem)
    copy.start()
    copy.wait()


def take(source, rows):
    return pl.pallas_call(
        take_kernel,
        out_shape=pltpu.VMEM((rows, source.shape[1]), BF16),
        in_specs=[HBM],
        out_specs=VMEM,
        scratch_shapes=[pltpu.SemaphoreType.DMA],
        compiler_params=pltpu.CompilerParams(vmem_limit_bytes=2 * MIB),
        name="take",
    )(pltpu.with_memory_space_constraint(source, pltpu.HBM))


def cost(name):
    return pl.CostEstimate(flops=COSTS.get(name, 0), bytes_accessed=1, transcendentals=0)


def load_kernel(source, after, out, sem):
    copy = pltpu.make_async_copy(source, out, sem)
    copy.start()
    copy.wait()


def load(name, source, after):
    return pl.pallas_call(
        load_kernel,
        out_shape=pltpu.VMEM(source.shape, BF16),
        in_specs=[HBM, ANY],
        out_specs=VMEM,
        scratch_shapes=[pltpu.SemaphoreType.DMA],
        compiler_params=pltpu.CompilerParams(vmem_limit_bytes=2 * MIB),
        cost_estimate=cost(name),
        name=name,
    )(pltpu.with_memory_space_constraint(source, pltpu.HBM), after)


def runs_of(ids, at_ids, depth):
    if len(at_ids) == len(ids):
        return [ids[t] * depth for t in at_ids], [(0, 0, len(ids) * depth)]
    span = CORES * depth
    at = [(i // CORES * CORES + ids[t] % CORES) * depth for i, t in enumerate(at_ids)]
    return at, [(i * span, ids[t] // CORES * span, span) for i, t in enumerate(at_ids[::CORES])]


def condition_kernel(sizes, at_ids, more, hess, *rest):
    ids, _, _ = positions(*sizes)
    pieces, rest = rest[: len(at_ids)], rest[len(at_ids) + 1 :]
    before, (out, right) = rest[0] if more else None, rest[more:]
    depth = pieces[0].shape[1]
    places, runs = runs_of(ids, at_ids, depth)
    for at, piece in zip(places, pieces):
        right[:, pl.ds(pl.multiple_of(at, depth), depth)] = piece[...]
    total = before[...] if more else None
    for low, column, span in runs:
        term = lax.dot_general(
            hess[:, pl.ds(pl.multiple_of(column, depth), span)],
            right[:, low : low + span],
            (((1,), (1,)), ((), ())),
            preferred_element_type=F32,
        )
        total = term if total is None else total + term
    out[...] = total.astype(out.dtype)


def condition(name, sizes, hess, at_ids, pieces, after, before=None):
    queries, depth = pieces[0].shape
    more = [] if before is None else [before]
    return pl.pallas_call(
        functools.partial(condition_kernel, sizes, at_ids, len(more)),
        out_shape=jax.ShapeDtypeStruct((hess.shape[0], queries), BF16 if more else F32),
        in_specs=[VMEM] * (1 + len(pieces)) + [ANY] + [VMEM] * len(more),
        out_specs=VMEM,
        scratch_shapes=[pltpu.VMEM((queries, len(pieces) * depth), BF16)],
        compiler_params=pltpu.CompilerParams(vmem_limit_bytes=12 * MIB),
        cost_estimate=cost(name),
        name=name,
    )(hess, *pieces, after, *more)


def score_kernel(sizes, at_ids, offsets, more, store, *rest):
    ids, blocks, _ = positions(*sizes)
    layers = len(blocks)
    pieces, rest = rest[: len(offsets)], rest[len(offsets) + 1 :]
    before, (*outs, right) = rest[0] if more else None, rest[more:]
    depth = right.shape[0] // len(at_ids)
    rows = store.shape[0] // layers
    places, runs = runs_of(ids, at_ids, depth)
    for (i, offset), piece in zip(offsets, pieces):
        count = piece.shape[0]
        right[pl.ds(pl.multiple_of(places[i] + offset, count), count), :] = piece[...]
    for r in [*range(1, layers, 2), *range(0, layers, 2)]:
        at = pl.ds(pl.multiple_of(blocks[r] * rows, rows), rows)
        part = before[r] if more else None
        for low, column, span in runs:
            columns = pl.ds(pl.multiple_of(column, depth), span)
            term = jnp.dot(store[at, columns], right[low : low + span, :], preferred_element_type=F32)
            part = term if part is None else part + term
        if len(outs) == 1:
            outs[0][r] = part
            continue
        cut = 2 * part.shape[1] // len(outs)
        for i in range(len(outs) // 2):
            out = outs[2 * i + 1 - r % 2]
            out[r // 2] = part[:, i * cut : (i + 1) * cut].astype(out.dtype)


def score(name, sizes, store, at_ids, pieces, after, before=None, cuts=0):
    width = pieces[0][0].shape[1]
    layers = sizes[2]
    rows = store.shape[0] // layers
    shapes = [((layers, rows, width), F32)]
    if cuts:
        shapes = [((layers // 2, rows, width // cuts), t) for t in (BF16, F32)] * cuts
    more = [] if before is None else [before]
    offsets, flat = [], []
    for i, xs in enumerate(pieces):
        low = 0
        for x in xs:
            offsets.append((i, low))
            flat.append(x)
            low += x.shape[0]
    return pl.pallas_call(
        functools.partial(score_kernel, sizes, at_ids, tuple(offsets), len(more)),
        out_shape=[jax.ShapeDtypeStruct(*shape) for shape in shapes],
        in_specs=[VMEM] * (1 + len(flat)) + [ANY] + [VMEM] * len(more),
        out_specs=[VMEM] * len(shapes),
        scratch_shapes=[pltpu.VMEM((len(at_ids) * low, width), BF16)],
        compiler_params=pltpu.CompilerParams(vmem_limit_bytes=12 * MIB),
        cost_estimate=cost(name),
        name=name,
    )(store, *flat, after, *more)


def fold_kernel(keep, got, _, send, left):
    for r in range(keep.shape[0]):
        total = keep[r] + got[r].astype(F32)
        if r % 2:
            send[r // 2] = total.astype(BF16)
        else:
            left[r // 2] = total


def fold(name, keep, got, after):
    shape = (keep.shape[0] // 2,) + keep.shape[1:]
    return pl.pallas_call(
        fold_kernel,
        out_shape=(jax.ShapeDtypeStruct(shape, BF16), jax.ShapeDtypeStruct(shape, F32)),
        in_specs=[VMEM, VMEM, ANY],
        out_specs=(VMEM, VMEM),
        compiler_params=pltpu.CompilerParams(vmem_limit_bytes=4 * MIB),
        cost_estimate=cost(name),
        name=name,
    )(keep, got, after)


def finish_kernel(sizes, places, *refs):
    _, _, place = positions(*sizes)
    *refs, out = refs
    span = out.shape[1] // len(place)
    for i, (j, column) in enumerate(places):
        keep, got = refs[2 * i : 2 * i + 2]
        at = pl.multiple_of(place[j] * span + column, keep.shape[2])
        out[:, pl.ds(at, keep.shape[2])] = keep[0] + got[0].astype(F32)


def finish(sizes, parts, queries):
    rows = parts[0][1][0].shape[1]
    return pl.pallas_call(
        functools.partial(finish_kernel, sizes, tuple(place for place, _ in parts)),
        out_shape=jax.ShapeDtypeStruct((rows, queries), F32),
        in_specs=[VMEM] * (2 * len(parts)),
        out_specs=VMEM,
        compiler_params=pltpu.CompilerParams(vmem_limit_bytes=12 * MIB),
        name="finish",
    )(*[a for _, part in parts for a in part])


def shards(groups, ex, layers, queries, hessian, store):
    chips = ex // CORES
    sizes = groups, ex, layers
    total = queries.shape[0]

    def permute(x, axis, perm, what):
        with jax.named_scope(what):
            return lax.ppermute(x, axis, perm)

    def from_chip(x, k, what):
        perm = [(e, (e - k * CORES) % ex) for e in range(ex)]
        return permute(x, "ex", perm, what + "_from_chip")

    def from_core(x, what):
        return permute(x, "ex", [(e, e ^ 1) for e in range(ex)], what + "_from_core")

    def from_group(x, j, what):
        perm = [(g, (g - j) % groups) for g in range(groups)]
        return permute(x, "groups", perm, what + "_from_group")

    def from_layer(x, r, what):
        return permute(x, "layer", [(z, z ^ r) for z in range(layers)], f"{what}_from_layer_{r}")

    def tie(x, *others):
        return lax.optimization_barrier((x, *others))[0]

    def gather_chip(x, what):
        return [from_chip(x, k, what) for k in range(1, chips)]

    def gather_group(x, what):
        return [from_group(x, j, what) for j in range(1, groups)]

    def with_cores(ours, theirs):
        return [x for pair in zip(ours, theirs) for x in pair]

    def flip(xs, what):
        return [from_core(x, what) for x in xs]

    def after(token, xs):
        return [tie(x, token) for x in xs]

    everywhere = tuple(range(ex))
    here, there = everywhere[:CORES], everywhere[CORES:]

    def step(name, keep, got, token):
        if keep.shape[0] == 1:
            return keep, got
        send, keep = fold(name, keep, got, token)
        return keep, from_layer(send, layers // keep.shape[0] // 2, name)

    hess = load("load_hessian", hessian[0], queries)
    rows = pltpu.with_memory_space_constraint(store[:, 0, :], pltpu.VMEM)
    mine = take(queries[:, 0, :], total // groups)
    mine_there, mine_core = gather_chip(mine, "queries"), from_core(mine, "queries")
    part = condition("condition_here", sizes, hess, here, [mine, mine_core], queries)
    mine_there = after(part, mine_there)
    pieces = with_cores(mine_there, flip(mine_there, "queries_there"))
    share = condition("condition_there", sizes, hess, there, pieces, part, part)
    by_chip, by_group = gather_chip(share, "share"), gather_group(share, "share")
    share_core = from_core(share, "share")
    part = score("own_here", sizes, rows, here, [[share], [share_core]], share)[0]
    by_chip, by_group = after(part, by_chip), after(part, by_group)
    half = share.shape[0] // 2
    by_chip_cores, by_group_cores = flip(by_chip, "by_chip"), flip(by_group, "by_group")
    upper = [[from_group(x[:half], j, "upper") for x in by_chip] for j in range(1, groups)]
    lower = [[from_chip(x[half:], k, "lower") for k in range(1, chips)] for x in by_group]
    pieces = [[x] for x in with_cores(by_chip, by_chip_cores)]
    send, keep = score("own_there", sizes, rows, there, pieces, part, part, 1)
    parts = [((0, 0), (keep, from_layer(send, 1, "own")))]
    token = keep
    for j in range(groups - 1):
        pieces = [[by_group[j]], [by_group_cores[j]]]
        part = score("other_here", sizes, rows, here, pieces, token)[0]
        halves = [after(part, pair) for pair in zip(upper[j], lower[j])]
        flips = [flip(pair, "diagonal") for pair in halves]
        pieces = [x for pair in zip(halves, flips) for x in pair]
        made = score("other_there", sizes, rows, there, pieces, part, part, 2)
        cut = made[0].shape[2]
        for c in range(2):
            send, token = made[2 * c : 2 * c + 2]
            parts.append(((j + 1, c * cut), (token, from_layer(send, 1, f"other{c}"))))
    while any(part[0].shape[0] > 1 for _, part in parts):
        parts = [(at, step(f"sum{i}", *part, token)) for i, (at, part) in enumerate(parts)]
    return finish(sizes, parts, total)


def solution(mesh):
    groups, ex, layers = (mesh.shape[a] for a in ("groups", "ex", "layer"))
    in_specs = (P(None, "layer", "ex"), P("layer", "ex", None), P(("groups", "ex"), "layer", None))
    out_specs = P(("groups", "ex", "layer"), None)
    return jax.shard_map(
        functools.partial(shards, groups, ex, layers),
        mesh=mesh,
        in_specs=in_specs,
        out_specs=out_specs,
        check_vma=False,
    )
```

time: 204 us -> 77.2 us (0.38)
  waiting for transfers between devices: 161 us -> 33.4 us
  matrix products: 22 us -> 0 us
  Pallas kernels: 0 us -> 21.4 us
  starting transfers between devices: 0.09 us -> 17.5 us
  between operations: 13.1 us -> 0.09 us
  other arithmetic: 2.7 us -> 0 us
    reduce_scatter x2 -> x0, waiting for transfers between devices: 127 us -> none  [the longest x1 74.5 us: shards(): lax.psum_scatter(lax.dot_general(hess_rows, query_cols, (((0,), (1,)), ((...]
    all_gather x1 -> x0, waiting for transfers between devices: 34.6 us -> none  [shards(): lax.all_gather(share, 'ex', axis=0, tiled=True)]
    ppermute x0 -> x18, waiting for transfers between devices: none -> 33.4 us  [permute(): return lax.ppermute(x, axis, perm)]
    dot_general x2 -> x0, matrix products: 22 us -> none  [the longest x1 11.6 us: shards(): jnp.dot(store_rows, lax.all_gather(share, 'ex', axis=0, tiled=True), pref...]
    pallas_call x0 -> x12, Pallas kernels: none -> 21.4 us  [the longest x4 7.44 us: score(): pl.pallas_call(functools.partial(score_kernel, sizes, at_ids, tuple(offse...]
    ppermute x0 -> x18, starting transfers between devices: none -> 17.5 us  [permute(): return lax.ppermute(x, axis, perm)]
    convert_element_type x1 -> x0, other arithmetic: 2.7 us -> none  [shards(): share = lax.psum_scatter(lax.dot_general(hess_rows, query_cols, (((0,), (...]
  transfers between devices with their start and end apart: 3 -> 18, of which waited for: 3 -> 11; matrix products, arithmetic and copies ran while one was open for 0% -> 6% of each run, Pallas kernels for 0% -> 21%
where the time goes in v5:
time: 77.2 us; the launch traced here: 76.8 us
  waiting for transfers between devices  33.4 us (43%)
  Pallas kernels  21.4 us (28%)
  starting transfers between devices  17.5 us (23%)
  local copies, waits for them, and re-layouts  4.28 us (6%)
    ppermute x18, waiting for transfers between devices, permute(): return lax.ppermute(x, axis, perm)  33.4 us
    ppermute x18, starting transfers between devices, permute(): return lax.ppermute(x, axis, perm)  17.5 us
    pallas_call x4, Pallas kernels, score(): pl.pallas_call(functools.partial(score_kernel, sizes, at_ids, tuple(offse...  7.44 us
    pallas_call x2, Pallas kernels, condition(): pl.pallas_call(functools.partial(condition_kernel, sizes, at_ids, len(mor...  4.93 us
    pallas_call x1, Pallas kernels, load(): pl.pallas_call(load_kernel, out_shape=pltpu.VMEM(source.shape, BF16), in_...  3.39 us
    pallas_call x3, Pallas kernels, fold(): pl.pallas_call(fold_kernel, out_shape=(jax.ShapeDtypeStruct(shape, BF16),...  2.92 us
    unnamed x3, local copies, waits for them, and re-layouts  2.85 us
    pallas_call x1, Pallas kernels, take(): pl.pallas_call(take_kernel, out_shape=pltpu.VMEM((rows, source.shape[1]),...  1.84 us
  transfers between devices with their start and end apart: 18, of which 11 were waited for; matrix products, arithmetic and copies ran while one was open for 6% of the time, Pallas kernels for 21%

profile of v5, /device:TPU:0, one launch (start us, length us, event | category | flops | bytes accessed | tf_op | source)
XLA Modules:
  0.0 76.8 jit_solution(16050458975389077927)
XLA Ops:
  0.0 1.8 %take.1.rest_0_ = bf16[256,1024]{1,0:T(8,128)(2,1)} custom-call(bf16[512,1024]{1,0:T(8,128)(2,1)} %bitcast.7), custom_call_target="tpu_custom_call" | custom-call | tf_op jit(solution)/shard_map/take/pallas_call | solution.py:48
  1.8 0.5 collective-permute-start.1
  2.4 2.6 %collective-permute-start = (bf16[256,1024]{1,0:T(8,128)(2,1)}, bf16[256,1024]{1,0:T(8,128)(2,1)}, u32[]{:S(2)}, u32[]{:S(2)}) collective-permute-start(bf16[256,1024]{1,0:T(8,128)(2,1)} %take.1.rest_0_), channel_id=1, source_target_pairs={{0,8},{4,12},{8,0},{12,4},{1,9},{5,13},{9,1},{13,5},{2,10},{6,14},... | collective-permute-start | bytes 1572872 | tf_op jit(solution)/shard_map/queries_from_chip/ppermute | solution.py:230
  5.0 2.8 %copy.4.after.rest_2_ = bf16[512,1,1024]{2,1,0:T(2,128)(2,1)S(1)} copy(bf16[512,1,1024]{2,0,1:T(8,128)(2,1)} %param.3) | data formatting | bytes 2097152 | tf_op args[0]
  7.8 3.4 %load_hessian.1.hess = bf16[1024,4096]{1,0:T(8,128)(2,1)S(1)} custom-call(bf16[1024,4096]{1,0:T(8,128)(2,1)} %bitcast.8, bf16[512,1,1024]{2,1,0:T(2,128)(2,1)S(1)} %copy.4.after.rest_2_), custom_call_target="tpu_custom_call" | custom-call | flops 999999995904 | bytes 1 | tf_op jit(solution)/shard_map/load_hessian/pallas_call | solution.py:70
  11.2 0.0 collective-permute-done.1.rest_1_
  11.2 2.5 %condition_here.1.rest_2_.rest_3_ = f32[1024,256]{1,0:T(8,128)S(1)} custom-call(bf16[1024,4096]{1,0:T(8,128)(2,1)S(1)} %load_hessian.1.hess, bf16[256,1024]{1,0:T(8,128)(2,1)} %take.1.rest_0_, bf16[256,1024]{1,0:T(8,128)(2,1)} %collective-permute-done.1.rest_1_, bf16[512,1,1024]{2,1,0:T(2,128)(2,1)S(1)} %copy.4.after.rest_2_), custom_call_target="tpu_custom_call" | custom-call | flops 999999995904 | bytes 1 | tf_op jit(solution)/shard_map/condition_here/pallas_call | solution.py:113
  13.8 0.0 copy-start
  13.8 4.0 %collective-permute-done.rest_0_ = bf16[256,1024]{1,0:T(8,128)(2,1)} collective-permute-done((bf16[256,1024]{1,0:T(8,128)(2,1)}, bf16[256,1024]{1,0:T(8,128)(2,1)}, u32[]{:S(2)}, u32[]{:S(2)}) %collective-permute-start) | collective-permute-done | bytes 524320 | tf_op jit(solution)/shard_map/queries_from_chip/ppermute | solution.py:230
  17.8 0.0 collective-permute-start.2
  17.8 2.1 %collective-permute-done.2.rest_1_ = bf16[256,1024]{1,0:T(8,128)(2,1)S(1)} collective-permute-done((bf16[256,1024]{1,0:T(8,128)(2,1)}, bf16[256,1024]{1,0:T(8,128)(2,1)S(1)}, u32[]{:S(2)}, u32[]{:S(2)}) %collective-permute-start.2) | collective-permute-done | bytes 524320 | tf_op jit(solution)/shard_map/queries_there_from_core/ppermute | solution.py:230
  19.9 2.4 %condition_there.1.rest_0_.rest_2_ = bf16[1024,256]{1,0:T(8,128)(2,1)S(1)} custom-call(bf16[1024,4096]{1,0:T(8,128)(2,1)S(1)} %load_hessian.1.hess, bf16[256,1024]{1,0:T(8,128)(2,1)} %collective-permute-done.rest_0_, bf16[256,1024]{1,0:T(8,128)(2,1)S(1)} %collective-permute-done.2.rest_1_, f32[1024,256]{1,0:T(8,128)S(1)} %condition_here.1.rest_2_.rest_3_, ...), custom_call_target="tpu_custom_call" | custom-call | bytes 1 | tf_op jit(solution)/shard_map/condition_there/pallas_call | solution.py:113
  22.3 0.2 collective-permute-start.4
  22.5 1.8 %collective-permute-start.3 = (bf16[1024,256]{1,0:T(8,128)(2,1)S(1)}, bf16[1024,256]{1,0:T(8,128)(2,1)S(1)}, u32[]{:S(2)}, u32[]{:S(2)}) collective-permute-start(bf16[1024,256]{1,0:T(8,128)(2,1)S(1)} %condition_there.1.rest_0_.rest_2_), channel_id=1, source_target_pairs={{0,8},{4,12},{8,0},{12,4},{1,9},{5,13},{9,1},{13,5},{2,10},{6,14},... | collective-permute-start | bytes 1572872 | tf_op jit(solution)/shard_map/share_from_chip/ppermute | solution.py:230
  24.3 1.5 %collective-permute-start.8 = (bf16[1024,256]{1,0:T(8,128)(2,1)S(1)}, bf16[1024,256]{1,0:T(8,128)(2,1)S(1)}, u32[]{:S(2)}, u32[]{:S(2)}) collective-permute-start(bf16[1024,256]{1,0:T(8,128)(2,1)S(1)} %condition_there.1.rest_0_.rest_2_), channel_id=1, source_target_pairs={{0,16},{16,0},{1,17},{17,1},{2,18},{18,2},{3,19},{19,3},{4,20},{20... | collective-permute-start | bytes 1572872 | tf_op jit(solution)/shard_map/share_from_group/ppermute | solution.py:230
  25.8 0.0 collective-permute-done.4.rest_1_
  25.8 1.6 %own_here.1.rest_2_.rest_3_ = f32[4,320,256]{2,1,0:T(8,128)S(1)} custom-call(bf16[1280,4096]{1,0:T(8,128)(2,1)S(1)} %bitcast.3, bf16[1024,256]{1,0:T(8,128)(2,1)S(1)} %condition_there.1.rest_0_.rest_2_, bf16[1024,256]{1,0:T(8,128)(2,1)S(1)} %collective-permute-done.4.rest_1_, bf16[1024,256]{1,0:T(8,128)(2,1)S(1)} %condition_there.1.rest_0_.rest_2_), custom_call_target="tpu_custom_call" | custom-call | flops 3000000000 | bytes 1 | tf_op jit(solution)/shard_map/own_here/pallas_call | solution.py:167
  27.4 9.4 %collective-permute-done.3.rest_0_ = bf16[1024,256]{1,0:T(8,128)(2,1)S(1)} collective-permute-done((bf16[1024,256]{1,0:T(8,128)(2,1)S(1)}, bf16[1024,256]{1,0:T(8,128)(2,1)S(1)}, u32[]{:S(2)}, u32[]{:S(2)}) %collective-permute-start.3) | collective-permute-done | bytes 524320 | tf_op jit(solution)/shard_map/share_from_chip/ppermute | solution.py:230
  36.7 1.5 %collective-permute-done.8.rest_0_ = bf16[1024,256]{1,0:T(8,128)(2,1)S(1)} collective-permute-done((bf16[1024,256]{1,0:T(8,128)(2,1)S(1)}, bf16[1024,256]{1,0:T(8,128)(2,1)S(1)}, u32[]{:S(2)}, u32[]{:S(2)}) %collective-permute-start.8) | collective-permute-done | bytes 524320 | tf_op jit(solution)/shard_map/share_from_group/ppermute | solution.py:230
  38.2 0.7 slice.7
  38.9 0.7 slice.6
  39.6 0.8 %collective-permute-start.10 = (bf16[512,256]{1,0:T(8,128)(2,1)}, bf16[512,256]{1,0:T(8,128)(2,1)}, u32[]{:S(2)}, u32[]{:S(2)}) collective-permute-start(bf16[512,256]{1,0:T(8,128)(2,1)} %slice.7), channel_id=1, source_target_pairs={{0,8},{4,12},{8,0},{12,4},{1,9},{5,13},{9,1},{13,5},{2,10},{6,14},... | collective-permute-start | bytes 786440 | tf_op jit(solution)/shard_map/lower_from_chip/ppermute | solution.py:230
  40.4 1.5 %collective-permute-start.7 = (bf16[512,256]{1,0:T(8,128)(2,1)}, bf16[512,256]{1,0:T(8,128)(2,1)}, u32[]{:S(2)}, u32[]{:S(2)}) collective-permute-start(bf16[512,256]{1,0:T(8,128)(2,1)} %slice.6), channel_id=1, source_target_pairs={{0,16},{16,0},{1,17},{17,1},{2,18},{18,2},{3,19},{19,3},{4,20},{20... | collective-permute-start | bytes 786440 | tf_op jit(solution)/shard_map/upper_from_group/ppermute | solution.py:230
  41.9 1.6 %own_there.1 = (bf16[2,320,256]{2,1,0:T(8,128)(2,1)}, f32[2,320,256]{2,1,0:T(8,128)S(1)}) custom-call(bf16[1280,4096]{1,0:T(8,128)(2,1)S(1)} %bitcast.4, bf16[1024,256]{1,0:T(8,128)(2,1)S(1)} %collective-permute-done.3.rest_0_, bf16[1024,256]{1,0:T(8,128)(2,1)S(1)} %collective-permute-done.5.rest_1_, f32[4,320,256]{2,1,0:T(8,128)S(1)} %own_here.1.rest_2_.rest_3_, ...), custom_call_target="tpu_custom_call" | custom-call | bytes 1 | tf_op jit(solution)/shard_map/own_there/pallas_call | solution.py:167
  43.5 1.6 %collective-permute-start.6 = (bf16[2,320,256]{2,1,0:T(8,128)(2,1)}, bf16[2,320,256]{2,1,0:T(8,128)(2,1)}, u32[]{:S(2)}, u32[]{:S(2)}) collective-permute-start(bf16[2,320,256]{2,1,0:T(8,128)(2,1)} %get-tuple-element.25), channel_id=1, source_target_pairs={{0,1},{1,0},{2,3},{3,2},{4,5},{5,4},{6,7},{7,6},{8,9},{9,8},{10,11... | collective-permute-start | bytes 983048 | tf_op jit(solution)/shard_map/own_from_layer_1/ppermute | solution.py:230
  45.1 1.6 %other_here.1.rest_4_.rest_5_ = f32[4,320,256]{2,1,0:T(8,128)S(1)} custom-call(bf16[1280,4096]{1,0:T(8,128)(2,1)S(1)} %bitcast.5, bf16[1024,256]{1,0:T(8,128)(2,1)S(1)} %collective-permute-done.8.rest_0_, bf16[1024,256]{1,0:T(8,128)(2,1)S(1)} %collective-permute-done.9.rest_1_, f32[2,320,256]{2,1,0:T(8,128)S(1)} %get-tuple-element.24.rest_2_.keep), custom_call_target="tpu_custom_call" | custom-call | flops 999999995904 | bytes 1 | tf_op jit(solution)/shard_map/other_here/pallas_call | solution.py:167
  46.7 2.0 %collective-permute-done.10.rest_1_ = bf16[512,256]{1,0:T(8,128)(2,1)} collective-permute-done((bf16[512,256]{1,0:T(8,128)(2,1)}, bf16[512,256]{1,0:T(8,128)(2,1)}, u32[]{:S(2)}, u32[]{:S(2)}) %collective-permute-start.10) | collective-permute-done | bytes 262176 | tf_op jit(solution)/shard_map/lower_from_chip/ppermute | solution.py:230
  48.7 0.0 collective-permute-start.12
  48.7 0.0 collective-permute-done.7.rest_0_
  48.7 0.5 collective-permute-start.11
  49.2 1.2 %collective-permute-done.12.rest_3_ = bf16[512,256]{1,0:T(8,128)(2,1)S(1)} collective-permute-done((bf16[512,256]{1,0:T(8,128)(2,1)}, bf16[512,256]{1,0:T(8,128)(2,1)S(1)}, u32[]{:S(2)}, u32[]{:S(2)}) %collective-permute-start.12) | collective-permute-done | bytes 262176 | tf_op jit(solution)/shard_map/diagonal_from_core/ppermute | solution.py:230
  50.4 0.4 collective-permute-done.11.rest_2_
  50.8 2.7 %other_there.1 = (bf16[2,320,128]{2,1,0:T(8,128)(2,1)}, f32[2,320,128]{2,1,0:T(8,128)S(1)}, bf16[2,320,128]{2,1,0:T(8,128)(2,1)}, f32[2,320,128]{2,1,0:T(8,128)S(1)}) custom-call(bf16[1280,4096]{1,0:T(8,128)(2,1)S(1)} %bitcast.6, bf16[512,256]{1,0:T(8,128)(2,1)} %collective-permute-done.7.rest_0_, bf16[512,256]{1,0:T(8,128)(2,1)} %collective-permute-done.10.rest_1_, ...), custom_call_target="tpu_custom_call" | custom-call | bytes 1 | tf_op jit(solution)/shard_map/other_there/pallas_call | solution.py:167
  53.5 1.6 %collective-permute-start.16 = (bf16[2,320,128]{2,1,0:T(8,128)(2,1)}, bf16[2,320,128]{2,1,0:T(8,128)(2,1)}, u32[]{:S(2)}, u32[]{:S(2)}) collective-permute-start(bf16[2,320,128]{2,1,0:T(8,128)(2,1)} %get-tuple-element.36), channel_id=1, source_target_pairs={{0,1},{1,0},{2,3},{3,2},{4,5},{5,4},{6,7},{7,6},{8,9},{9,8},{10,11... | collective-permute-start | bytes 491528 | tf_op jit(solution)/shard_map/other1_from_layer_1/ppermute | solution.py:230
  55.1 0.5 collective-permute-start.14
  55.5 0.0 collective-permute-done.6.got
  55.5 1.0 %sum0.1 = (bf16[1,320,256]{2,1,0:T(8,128)(2,1)S(1)}, f32[1,320,256]{2,1,0:T(8,128)S(1)}) custom-call(f32[2,320,256]{2,1,0:T(8,128)S(1)} %get-tuple-element.24.rest_2_.keep, bf16[2,320,256]{2,1,0:T(8,128)(2,1)} %collective-permute-done.6.got, f32[2,320,128]{2,1,0:T(8,128)S(1)} %get-tuple-element.29._.keep), custom_call_target="tpu_custom_call" | custom-call | flops 999999995904 | bytes 1 | tf_op jit(solution)/shard_map/sum0/pallas_call | solution.py:190
  56.5 2.7 %collective-permute-start.13 = (bf16[1,320,256]{2,1,0:T(8,128)(2,1)S(1)}, bf16[1,320,256]{2,1,0:T(8,128)(2,1)S(1)}, u32[]{:S(2)}, u32[]{:S(2)}) collective-permute-start(bf16[1,320,256]{2,1,0:T(8,128)(2,1)S(1)} %get-tuple-element.31), channel_id=1, source_target_pairs={{0,2},{1,3},{2,0},{3,1},{4,6},{5,7},{6,4},{7,5},{8,10},{9,11},{10,... | collective-permute-start | bytes 491528 | tf_op jit(solution)/shard_map/sum0_from_layer_2/ppermute | solution.py:230
  59.2 6.0 %collective-permute-done.16.got = bf16[2,320,128]{2,1,0:T(8,128)(2,1)} collective-permute-done((bf16[2,320,128]{2,1,0:T(8,128)(2,1)}, bf16[2,320,128]{2,1,0:T(8,128)(2,1)}, u32[]{:S(2)}, u32[]{:S(2)}) %collective-permute-start.16) | collective-permute-done | bytes 163872 | tf_op jit(solution)/shard_map/other1_from_layer_1/ppermute | solution.py:230
  65.2 0.9 %sum2.1 = (bf16[1,320,128]{2,1,0:T(8,128)(2,1)S(1)}, f32[1,320,128]{2,1,0:T(8,128)S(1)}) custom-call(f32[2,320,128]{2,1,0:T(8,128)S(1)} %get-tuple-element.29._.keep, bf16[2,320,128]{2,1,0:T(8,128)(2,1)} %collective-permute-done.16.got, f32[2,320,128]{2,1,0:T(8,128)S(1)} %get-tuple-element.29._.keep), custom_call_target="tpu_custom_call" | custom-call | flops 3000000000 | bytes 1 | tf_op jit(solution)/shard_map/sum2/pallas_call | solution.py:190
  66.2 0.6 collective-permute-start.17
  66.7 1.2 %collective-permute-done.14.got = bf16[2,320,128]{2,1,0:T(8,128)(2,1)} collective-permute-done((bf16[2,320,128]{2,1,0:T(8,128)(2,1)}, bf16[2,320,128]{2,1,0:T(8,128)(2,1)}, u32[]{:S(2)}, u32[]{:S(2)}) %collective-permute-start.14) | collective-permute-done | bytes 163872 | tf_op jit(solution)/shard_map/other0_from_layer_1/ppermute | solution.py:230
  67.9 0.9 %sum1.1 = (bf16[1,320,128]{2,1,0:T(8,128)(2,1)S(1)}, f32[1,320,128]{2,1,0:T(8,128)S(1)}) custom-call(f32[2,320,128]{2,1,0:T(8,128)S(1)} %get-tuple-element.32.keep, bf16[2,320,128]{2,1,0:T(8,128)(2,1)} %collective-permute-done.14.got, f32[2,320,128]{2,1,0:T(8,128)S(1)} %get-tuple-element.29._.keep), custom_call_target="tpu_custom_call" | custom-call | flops 3000000000 | bytes 1 | tf_op jit(solution)/shard_map/sum1/pallas_call | solution.py:190
  68.9 1.3 %collective-permute-start.15 = (bf16[1,320,128]{2,1,0:T(8,128)(2,1)S(1)}, bf16[1,320,128]{2,1,0:T(8,128)(2,1)S(1)}, u32[]{:S(2)}, u32[]{:S(2)}) collective-permute-start(bf16[1,320,128]{2,1,0:T(8,128)(2,1)S(1)} %get-tuple-element.35), channel_id=1, source_target_pairs={{0,2},{1,3},{2,0},{3,1},{4,6},{5,7},{6,4},{7,5},{8,10},{9,11},{10,... | collective-permute-start | bytes 245768 | tf_op jit(solution)/shard_map/sum1_from_layer_2/ppermute | solution.py:230
  70.2 0.0 collective-permute-done.13.refs_1_
  70.2 3.6 %collective-permute-done.17.refs_5_ = bf16[1,320,128]{2,1,0:T(8,128)(2,1)S(1)} collective-permute-done((bf16[1,320,128]{2,1,0:T(8,128)(2,1)S(1)}, bf16[1,320,128]{2,1,0:T(8,128)(2,1)S(1)}, u32[]{:S(2)}, u32[]{:S(2)}) %collective-permute-start.17) | collective-permute-done | bytes 81952 | tf_op jit(solution)/shard_map/sum2_from_layer_2/ppermute | solution.py:230
  73.8 2.0 %collective-permute-done.15.refs_3_ = bf16[1,320,128]{2,1,0:T(8,128)(2,1)S(1)} collective-permute-done((bf16[1,320,128]{2,1,0:T(8,128)(2,1)S(1)}, bf16[1,320,128]{2,1,0:T(8,128)(2,1)S(1)}, u32[]{:S(2)}, u32[]{:S(2)}) %collective-permute-start.15) | collective-permute-done | bytes 81952 | tf_op jit(solution)/shard_map/sum1_from_layer_2/ppermute | solution.py:230
  75.9 0.9 %finish.1 = f32[320,512]{1,0:T(8,128)} custom-call(f32[1,320,256]{2,1,0:T(8,128)S(1)} %get-tuple-element.30.refs_0_, bf16[1,320,256]{2,1,0:T(8,128)(2,1)S(1)} %collective-permute-done.13.refs_1_, f32[1,320,128]{2,1,0:T(8,128)S(1)} %get-tuple-element.34.refs_2_, bf16[1,320,128]{2,1,0:T(8,128)(2,1)S(1)} %collective-permute-done.15.refs_3_, ...), custom_call_target="tpu_custom_call" | custom-call | tf_op jit(solution)/shard_map/finish/pallas_call | solution.py:213
  (5 shorter events, 0.0 us)
Async XLA Ops:
  1.8 9.4 %collective-permute-start.1 = (bf16[256,1024]{1,0:T(8,128)(2,1)}, bf16[256,1024]{1,0:T(8,128)(2,1)}, u32[]{:S(2)}, u32[]{:S(2)}) collective-permute-start(bf16[256,1024]{1,0:T(8,128)(2,1)} %take.1.rest_0_), channel_id=1, source_target_pairs={{0,4},{4,0},{8,12},{12,8},{1,5},{5,1},{9,13},{13,9},{2,6},{6,2},{1... | collective-permute-start | bytes 1572872 | tf_op jit(solution)/shard_map/queries_from_core/ppermute | solution.py:230
  2.4 15.4 %collective-permute-start = (bf16[256,1024]{1,0:T(8,128)(2,1)}, bf16[256,1024]{1,0:T(8,128)(2,1)}, u32[]{:S(2)}, u32[]{:S(2)}) collective-permute-start(bf16[256,1024]{1,0:T(8,128)(2,1)} %take.1.rest_0_), channel_id=1, source_target_pairs={{0,8},{4,12},{8,0},{12,4},{1,9},{5,13},{9,1},{13,5},{2,10},{6,14},... | collective-permute-start | bytes 1572872 | tf_op jit(solution)/shard_map/queries_from_chip/ppermute | solution.py:230
  13.8 12.0 %copy-start = (bf16[1280,1,4096]{2,0,1:T(8,128)(2,1)S(1)}, bf16[1280,1,4096]{2,0,1:T(8,128)(2,1)}, u32[]{:S(2)}) copy-start(bf16[1280,1,4096]{2,0,1:T(8,128)(2,1)} %param.5) | copy-start | bytes 31457284
  17.8 2.1 %collective-permute-start.2 = (bf16[256,1024]{1,0:T(8,128)(2,1)}, bf16[256,1024]{1,0:T(8,128)(2,1)S(1)}, u32[]{:S(2)}, u32[]{:S(2)}) collective-permute-start(bf16[256,1024]{1,0:T(8,128)(2,1)} %collective-permute-done.rest_0_), channel_id=1, source_target_pairs={{0,4},{4,0},{8,12},{12,8},{1,5},{5,1},{9,13},{13,9},{2,6},{6,2},{1... | collective-permute-start | bytes 1572872 | tf_op jit(solution)/shard_map/queries_there_from_core/ppermute | solution.py:230
  22.3 3.5 %collective-permute-start.4 = (bf16[1024,256]{1,0:T(8,128)(2,1)S(1)}, bf16[1024,256]{1,0:T(8,128)(2,1)S(1)}, u32[]{:S(2)}, u32[]{:S(2)}) collective-permute-start(bf16[1024,256]{1,0:T(8,128)(2,1)S(1)} %condition_there.1.rest_0_.rest_2_), channel_id=1, source_target_pairs={{0,4},{4,0},{8,12},{12,8},{1,5},{5,1},{9,13},{13,9},{2,6},{6,2},{1... | collective-permute-start | bytes 1572872 | tf_op jit(solution)/shard_map/share_from_core/ppermute | solution.py:230
  22.5 14.2 %collective-permute-start.3 = (bf16[1024,256]{1,0:T(8,128)(2,1)S(1)}, bf16[1024,256]{1,0:T(8,128)(2,1)S(1)}, u32[]{:S(2)}, u32[]{:S(2)}) collective-permute-start(bf16[1024,256]{1,0:T(8,128)(2,1)S(1)} %condition_there.1.rest_0_.rest_2_), channel_id=1, source_target_pairs={{0,8},{4,12},{8,0},{12,4},{1,9},{5,13},{9,1},{13,5},{2,10},{6,14},... | collective-permute-start | bytes 1572872 | tf_op jit(solution)/shard_map/share_from_chip/ppermute | solution.py:230
  24.3 13.9 %collective-permute-start.8 = (bf16[1024,256]{1,0:T(8,128)(2,1)S(1)}, bf16[1024,256]{1,0:T(8,128)(2,1)S(1)}, u32[]{:S(2)}, u32[]{:S(2)}) collective-permute-start(bf16[1024,256]{1,0:T(8,128)(2,1)S(1)} %condition_there.1.rest_0_.rest_2_), channel_id=1, source_target_pairs={{0,16},{16,0},{1,17},{17,1},{2,18},{18,2},{3,19},{19,3},{4,20},{20... | collective-permute-start | bytes 1572872 | tf_op jit(solution)/shard_map/share_from_group/ppermute | solution.py:230
  36.7 5.2 %collective-permute-start.5 = (bf16[1024,256]{1,0:T(8,128)(2,1)S(1)}, bf16[1024,256]{1,0:T(8,128)(2,1)S(1)}, u32[]{:S(2)}, u32[]{:S(2)}) collective-permute-start(bf16[1024,256]{1,0:T(8,128)(2,1)S(1)} %collective-permute-done.3.rest_0_), channel_id=1, source_target_pairs={{0,4},{4,0},{8,12},{12,8},{1,5},{5,1},{9,13},{13,9},{2,6},{6,2},{1... | collective-permute-start | bytes 1572872 | tf_op jit(solution)/shard_map/by_chip_from_core/ppermute | solution.py:230
  38.2 6.9 %collective-permute-start.9 = (bf16[1024,256]{1,0:T(8,128)(2,1)S(1)}, bf16[1024,256]{1,0:T(8,128)(2,1)S(1)}, u32[]{:S(2)}, u32[]{:S(2)}) collective-permute-start(bf16[1024,256]{1,0:T(8,128)(2,1)S(1)} %collective-permute-done.8.rest_0_), channel_id=1, source_target_pairs={{0,4},{4,0},{8,12},{12,8},{1,5},{5,1},{9,13},{13,9},{2,6},{6,2},{1... | collective-permute-start | bytes 1572872 | tf_op jit(solution)/shard_map/by_group_from_core/ppermute | solution.py:230
  39.6 9.0 %collective-permute-start.10 = (bf16[512,256]{1,0:T(8,128)(2,1)}, bf16[512,256]{1,0:T(8,128)(2,1)}, u32[]{:S(2)}, u32[]{:S(2)}) collective-permute-start(bf16[512,256]{1,0:T(8,128)(2,1)} %slice.7), channel_id=1, source_target_pairs={{0,8},{4,12},{8,0},{12,4},{1,9},{5,13},{9,1},{13,5},{2,10},{6,14},... | collective-permute-start | bytes 786440 | tf_op jit(solution)/shard_map/lower_from_chip/ppermute | solution.py:230
  40.4 8.3 %collective-permute-start.7 = (bf16[512,256]{1,0:T(8,128)(2,1)}, bf16[512,256]{1,0:T(8,128)(2,1)}, u32[]{:S(2)}, u32[]{:S(2)}) collective-permute-start(bf16[512,256]{1,0:T(8,128)(2,1)} %slice.6), channel_id=1, source_target_pairs={{0,16},{16,0},{1,17},{17,1},{2,18},{18,2},{3,19},{19,3},{4,20},{20... | collective-permute-start | bytes 786440 | tf_op jit(solution)/shard_map/upper_from_group/ppermute | solution.py:230
  43.5 12.0 %collective-permute-start.6 = (bf16[2,320,256]{2,1,0:T(8,128)(2,1)}, bf16[2,320,256]{2,1,0:T(8,128)(2,1)}, u32[]{:S(2)}, u32[]{:S(2)}) collective-permute-start(bf16[2,320,256]{2,1,0:T(8,128)(2,1)} %get-tuple-element.25), channel_id=1, source_target_pairs={{0,1},{1,0},{2,3},{3,2},{4,5},{5,4},{6,7},{7,6},{8,9},{9,8},{10,11... | collective-permute-start | bytes 983048 | tf_op jit(solution)/shard_map/own_from_layer_1/ppermute | solution.py:230
  48.7 1.7 %collective-permute-start.12 = (bf16[512,256]{1,0:T(8,128)(2,1)}, bf16[512,256]{1,0:T(8,128)(2,1)S(1)}, u32[]{:S(2)}, u32[]{:S(2)}) collective-permute-start(bf16[512,256]{1,0:T(8,128)(2,1)} %collective-permute-done.10.rest_1_), channel_id=1, source_target_pairs={{0,4},{4,0},{8,12},{12,8},{1,5},{5,1},{9,13},{13,9},{2,6},{6,2},{1... | collective-permute-start | bytes 786440 | tf_op jit(solution)/shard_map/diagonal_from_core/ppermute | solution.py:230
  48.7 2.1 %collective-permute-start.11 = (bf16[512,256]{1,0:T(8,128)(2,1)}, bf16[512,256]{1,0:T(8,128)(2,1)S(1)}, u32[]{:S(2)}, u32[]{:S(2)}) collective-permute-start(bf16[512,256]{1,0:T(8,128)(2,1)} %collective-permute-done.7.rest_0_), channel_id=1, source_target_pairs={{0,4},{4,0},{8,12},{12,8},{1,5},{5,1},{9,13},{13,9},{2,6},{6,2},{1... | collective-permute-start | bytes 786440 | tf_op jit(solution)/shard_map/diagonal_from_core/ppermute | solution.py:230
  53.5 11.7 %collective-permute-start.16 = (bf16[2,320,128]{2,1,0:T(8,128)(2,1)}, bf16[2,320,128]{2,1,0:T(8,128)(2,1)}, u32[]{:S(2)}, u32[]{:S(2)}) collective-permute-start(bf16[2,320,128]{2,1,0:T(8,128)(2,1)} %get-tuple-element.36), channel_id=1, source_target_pairs={{0,1},{1,0},{2,3},{3,2},{4,5},{5,4},{6,7},{7,6},{8,9},{9,8},{10,11... | collective-permute-start | bytes 491528 | tf_op jit(solution)/shard_map/other1_from_layer_1/ppermute | solution.py:230
  55.1 12.9 %collective-permute-start.14 = (bf16[2,320,128]{2,1,0:T(8,128)(2,1)}, bf16[2,320,128]{2,1,0:T(8,128)(2,1)}, u32[]{:S(2)}, u32[]{:S(2)}) collective-permute-start(bf16[2,320,128]{2,1,0:T(8,128)(2,1)} %get-tuple-element.33), channel_id=1, source_target_pairs={{0,1},{1,0},{2,3},{3,2},{4,5},{5,4},{6,7},{7,6},{8,9},{9,8},{10,11... | collective-permute-start | bytes 491528 | tf_op jit(solution)/shard_map/other0_from_layer_1/ppermute | solution.py:230
  56.5 13.6 %collective-permute-start.13 = (bf16[1,320,256]{2,1,0:T(8,128)(2,1)S(1)}, bf16[1,320,256]{2,1,0:T(8,128)(2,1)S(1)}, u32[]{:S(2)}, u32[]{:S(2)}) collective-permute-start(bf16[1,320,256]{2,1,0:T(8,128)(2,1)S(1)} %get-tuple-element.31), channel_id=1, source_target_pairs={{0,2},{1,3},{2,0},{3,1},{4,6},{5,7},{6,4},{7,5},{8,10},{9,11},{10,... | collective-permute-start | bytes 491528 | tf_op jit(solution)/shard_map/sum0_from_layer_2/ppermute | solution.py:230
  66.2 7.6 %collective-permute-start.17 = (bf16[1,320,128]{2,1,0:T(8,128)(2,1)S(1)}, bf16[1,320,128]{2,1,0:T(8,128)(2,1)S(1)}, u32[]{:S(2)}, u32[]{:S(2)}) collective-permute-start(bf16[1,320,128]{2,1,0:T(8,128)(2,1)S(1)} %get-tuple-element.38), channel_id=1, source_target_pairs={{0,2},{1,3},{2,0},{3,1},{4,6},{5,7},{6,4},{7,5},{8,10},{9,11},{10,... | collective-permute-start | bytes 245768 | tf_op jit(solution)/shard_map/sum2_from_layer_2/ppermute | solution.py:230
  68.9 7.0 %collective-permute-start.15 = (bf16[1,320,128]{2,1,0:T(8,128)(2,1)S(1)}, bf16[1,320,128]{2,1,0:T(8,128)(2,1)S(1)}, u32[]{:S(2)}, u32[]{:S(2)}) collective-permute-start(bf16[1,320,128]{2,1,0:T(8,128)(2,1)S(1)} %get-tuple-element.35), channel_id=1, source_target_pairs={{0,2},{1,3},{2,0},{3,1},{4,6},{5,7},{6,4},{7,5},{8,10},{9,11},{10,... | collective-permute-start | bytes 245768 | tf_op jit(solution)/shard_map/sum1_from_layer_2/ppermute | solution.py:230

commit v6 on v5

--- a/solution.py
+++ b/solution.py
@@ -12,11 +12,8 @@
 COSTS = {
     "load_hessian": 1_000_000_000_000,
     "condition_here": 1_000_000_000_000,
-    "own_here": 3_000_000_000,
+    "own_here": 1_000_000_000_000,
     "other_here": 1_000_000_000_000,
-    "sum0": 1_000_000_000_000,
-    "sum1": 3_000_000_000,
-    "sum2": 3_000_000_000,
 }
 MIB = 1 << 20
 VMEM = pl.BlockSpec(memory_space=pltpu.VMEM)
@@ -36,12 +33,20 @@
     return ids, blocks, place
 
 
-def take_kernel(source, out, sem):
-    rows = out.shape[0]
-    at = pl.ds(pl.multiple_of(lax.axis_index("groups") * rows, rows), rows)
-    copy = pltpu.make_async_copy(source.at[at, :], out, sem)
-    copy.start()
-    copy.wait()
+def take_kernel(source, out, sems):
+    parts = sems.shape[0]
+    rows = out.shape[0] // parts
+    first = lax.axis_index("groups") * out.shape[0]
+    copies = []
+    for i in range(parts):
+        at = pl.ds(pl.multiple_of(first + i * rows, rows), rows)
+        copies.append(
+            pltpu.make_async_copy(source.at[at, :], out.at[i * rows : (i + 1) * rows, :], sems.at[i])
+        )
+    for copy in copies:
+        copy.start()
+    for copy in copies:
+        copy.wait()
 
 
 def take(source, rows):
@@ -50,7 +55,7 @@
         out_shape=pltpu.VMEM((rows, source.shape[1]), BF16),
         in_specs=[HBM],
         out_specs=VMEM,
-        scratch_shapes=[pltpu.SemaphoreType.DMA],
+        scratch_shapes=[pltpu.SemaphoreType.DMA((8,))],
         compiler_params=pltpu.CompilerParams(vmem_limit_bytes=2 * MIB),
         name="take",
     )(pltpu.with_memory_space_constraint(source, pltpu.HBM))
@@ -79,66 +84,55 @@
     )(pltpu.with_memory_space_constraint(source, pltpu.HBM), after)
 
 
-def runs_of(ids, at_ids, depth):
-    if len(at_ids) == len(ids):
-        return [ids[t] * depth for t in at_ids], [(0, 0, len(ids) * depth)]
-    span = CORES * depth
-    at = [(i // CORES * CORES + ids[t] % CORES) * depth for i, t in enumerate(at_ids)]
-    return at, [(i * span, ids[t] // CORES * span, span) for i, t in enumerate(at_ids[::CORES])]
-
-
 def condition_kernel(sizes, at_ids, more, hess, *rest):
     ids, _, _ = positions(*sizes)
     pieces, rest = rest[: len(at_ids)], rest[len(at_ids) + 1 :]
-    before, (out, right) = rest[0] if more else None, rest[more:]
+    total, outs = rest[0][...] if more else None, rest[more:]
     depth = pieces[0].shape[1]
-    places, runs = runs_of(ids, at_ids, depth)
-    for at, piece in zip(places, pieces):
-        right[:, pl.ds(pl.multiple_of(at, depth), depth)] = piece[...]
-    total = before[...] if more else None
-    for low, column, span in runs:
+    for t, piece in zip(at_ids, pieces):
+        columns = pl.ds(pl.multiple_of(ids[t] * depth, depth), depth)
         term = lax.dot_general(
-            hess[:, pl.ds(pl.multiple_of(column, depth), span)],
-            right[:, low : low + span],
-            (((1,), (1,)), ((), ())),
-            preferred_element_type=F32,
+            hess[:, columns], piece[...], (((1,), (1,)), ((), ())), preferred_element_type=F32
         )
         total = term if total is None else total + term
-    out[...] = total.astype(out.dtype)
+    outs[0][...] = total.astype(outs[0].dtype)
+    for i, out in enumerate(outs[1:]):
+        out[...] = outs[0][i * out.shape[0] : (i + 1) * out.shape[0], :]
 
 
 def condition(name, sizes, hess, at_ids, pieces, after, before=None):
-    queries, depth = pieces[0].shape
+    queries = pieces[0].shape[0]
+    height = hess.shape[0]
+    shapes = [((height, queries), F32)]
+    if before is not None:
+        shapes = [((height, queries), BF16)] + [((height // 2, queries), BF16)] * 2
     more = [] if before is None else [before]
     return pl.pallas_call(
         functools.partial(condition_kernel, sizes, at_ids, len(more)),
-        out_shape=jax.ShapeDtypeStruct((hess.shape[0], queries), BF16 if more else F32),
+        out_shape=[pltpu.VMEM(*shape) for shape in shapes],
         in_specs=[VMEM] * (1 + len(pieces)) + [ANY] + [VMEM] * len(more),
-        out_specs=VMEM,
-        scratch_shapes=[pltpu.VMEM((queries, len(pieces) * depth), BF16)],
+        out_specs=[VMEM] * len(shapes),
         compiler_params=pltpu.CompilerParams(vmem_limit_bytes=12 * MIB),
         cost_estimate=cost(name),
         name=name,
     )(hess, *pieces, after, *more)
 
 
-def score_kernel(sizes, at_ids, offsets, more, store, *rest):
+def score_kernel(sizes, at_ids, more, store, *rest):
     ids, blocks, _ = positions(*sizes)
     layers = len(blocks)
-    pieces, rest = rest[: len(offsets)], rest[len(offsets) + 1 :]
-    before, (*outs, right) = rest[0] if more else None, rest[more:]
-    depth = right.shape[0] // len(at_ids)
+    pieces, rest = rest[: len(at_ids)], rest[len(at_ids) + 1 :]
+    before, outs = rest[0] if more else None, rest[more:]
+    depth = store.shape[1] // len(ids)
     rows = store.shape[0] // layers
-    places, runs = runs_of(ids, at_ids, depth)
-    for (i, offset), piece in zip(offsets, pieces):
-        count = piece.shape[0]
-        right[pl.ds(pl.multiple_of(places[i] + offset, count), count), :] = piece[...]
     for r in [*range(1, layers, 2), *range(0, layers, 2)]:
         at = pl.ds(pl.multiple_of(blocks[r] * rows, rows), rows)
         part = before[r] if more else None
-        for low, column, span in runs:
-            columns = pl.ds(pl.multiple_of(column, depth), span)
-            term = jnp.dot(store[at, columns], right[low : low + span, :], preferred_element_type=F32)
+        for (t, half), piece in zip(at_ids, pieces):
+            height = piece.shape[0]
+            column = ids[t] * depth + half * height
+            columns = pl.ds(pl.multiple_of(column, height), height)
+            term = jnp.dot(store[at, columns], piece[...], preferred_element_type=F32)
             part = term if part is None else part + term
         if len(outs) == 1:
             outs[0][r] = part
@@ -149,27 +143,20 @@
             out[r // 2] = part[:, i * cut : (i + 1) * cut].astype(out.dtype)
 
 
-def score(name, sizes, store, at_ids, pieces, after, before=None, cuts=0):
-    width = pieces[0][0].shape[1]
+def score(name, sizes, store, pieces, after, before=None, cuts=0):
+    flat = list(pieces.values())
+    width = flat[0].shape[1]
     layers = sizes[2]
     rows = store.shape[0] // layers
     shapes = [((layers, rows, width), F32)]
     if cuts:
         shapes = [((layers // 2, rows, width // cuts), t) for t in (BF16, F32)] * cuts
     more = [] if before is None else [before]
-    offsets, flat = [], []
-    for i, xs in enumerate(pieces):
-        low = 0
-        for x in xs:
-            offsets.append((i, low))
-            flat.append(x)
-            low += x.shape[0]
-    return pl.pallas_call(
-        functools.partial(score_kernel, sizes, at_ids, tuple(offsets), len(more)),
-        out_shape=[jax.ShapeDtypeStruct(*shape) for shape in shapes],
+    return pl.pallas_call(
+        functools.partial(score_kernel, sizes, tuple(pieces), len(more)),
+        out_shape=[pltpu.VMEM(*shape) for shape in shapes],
         in_specs=[VMEM] * (1 + len(flat)) + [ANY] + [VMEM] * len(more),
         out_specs=[VMEM] * len(shapes),
-        scratch_shapes=[pltpu.VMEM((len(at_ids) * low, width), BF16)],
         compiler_params=pltpu.CompilerParams(vmem_limit_bytes=12 * MIB),
         cost_estimate=cost(name),
         name=name,
@@ -189,7 +176,7 @@
     shape = (keep.shape[0] // 2,) + keep.shape[1:]
     return pl.pallas_call(
         fold_kernel,
-        out_shape=(jax.ShapeDtypeStruct(shape, BF16), jax.ShapeDtypeStruct(shape, F32)),
+        out_shape=(pltpu.VMEM(shape, BF16), pltpu.VMEM(shape, F32)),
         in_specs=[VMEM, VMEM, ANY],
         out_specs=(VMEM, VMEM),
         compiler_params=pltpu.CompilerParams(vmem_limit_bytes=4 * MIB),
@@ -261,8 +248,7 @@
     def after(token, xs):
         return [tie(x, token) for x in xs]
 
-    everywhere = tuple(range(ex))
-    here, there = everywhere[:CORES], everywhere[CORES:]
+    here, there = range(CORES), range(CORES, ex)
 
     def step(name, keep, got, token):
         if keep.shape[0] == 1:
@@ -270,33 +256,43 @@
         send, keep = fold(name, keep, got, token)
         return keep, from_layer(send, layers // keep.shape[0] // 2, name)
 
-    hess = load("load_hessian", hessian[0], queries)
+    mine = take(queries[:, 0, :], total // groups)
+    hess = load("load_hessian", hessian[0], mine)
     rows = pltpu.with_memory_space_constraint(store[:, 0, :], pltpu.VMEM)
-    mine = take(queries[:, 0, :], total // groups)
     mine_there, mine_core = gather_chip(mine, "queries"), from_core(mine, "queries")
-    part = condition("condition_here", sizes, hess, here, [mine, mine_core], queries)
+    part = condition("condition_here", sizes, hess, here, [mine, mine_core], hess)[0]
     mine_there = after(part, mine_there)
     pieces = with_cores(mine_there, flip(mine_there, "queries_there"))
-    share = condition("condition_there", sizes, hess, there, pieces, part, part)
-    by_chip, by_group = gather_chip(share, "share"), gather_group(share, "share")
+    share, upper, lower = condition("condition_there", sizes, hess, there, pieces, part, part)
     share_core = from_core(share, "share")
-    part = score("own_here", sizes, rows, here, [[share], [share_core]], share)[0]
-    by_chip, by_group = after(part, by_chip), after(part, by_group)
-    half = share.shape[0] // 2
-    by_chip_cores, by_group_cores = flip(by_chip, "by_chip"), flip(by_group, "by_group")
-    upper = [[from_group(x[:half], j, "upper") for x in by_chip] for j in range(1, groups)]
-    lower = [[from_chip(x[half:], k, "lower") for k in range(1, chips)] for x in by_group]
-    pieces = [[x] for x in with_cores(by_chip, by_chip_cores)]
-    send, keep = score("own_there", sizes, rows, there, pieces, part, part, 1)
+    by_chip = [gather_chip(upper, "upper"), gather_chip(lower, "lower")]
+    by_group = [gather_group(tie(upper, share_core), "upper"), gather_group(tie(lower, share_core), "lower")]
+    part = score("own_here", sizes, rows, {(0, 0): share, (1, 0): share_core}, share)[0]
+    by_chip[0], by_group[1] = after(part, by_chip[0]), after(part, by_group[1])
+    diagonal = [
+        [[from_group(x, j, "chips_upper") for x in by_chip[0]] for j in range(1, groups)],
+        [gather_chip(x, "groups_lower") for x in by_group[1]],
+    ]
+
+    def spread(xs, half, what):
+        return {(t, half): x for t, x in zip(there, with_cores(xs, flip(xs, what)))}
+
+    by_chip[1] = after(part, by_chip[1])
+    pieces = spread(by_chip[0], 0, "chips_upper") | spread(by_chip[1], 1, "chips_lower")
+    send, keep = score("own_there", sizes, rows, pieces, part, part, 1)
     parts = [((0, 0), (keep, from_layer(send, 1, "own")))]
     token = keep
+    by_group[0] = after(part, by_group[0])
     for j in range(groups - 1):
-        pieces = [[by_group[j]], [by_group_cores[j]]]
-        part = score("other_here", sizes, rows, here, pieces, token)[0]
-        halves = [after(part, pair) for pair in zip(upper[j], lower[j])]
-        flips = [flip(pair, "diagonal") for pair in halves]
-        pieces = [x for pair in zip(halves, flips) for x in pair]
-        made = score("other_there", sizes, rows, there, pieces, part, part, 2)
+        pieces = {}
+        for half in range(2):
+            x = by_group[half][j]
+            pieces |= {(0, half): x, (1, half): from_core(x, "groups")}
+        part = score("other_here", sizes, rows, pieces, token)[0]
+        pieces = {}
+        for half in range(2):
+            pieces |= spread(after(part, diagonal[half][j]), half, "diagonal")
+        made = score("other_there", sizes, rows, pieces, part, part, 2)
         cut = made[0].shape[2]
         for c in range(2):
             send, token = made[2 * c : 2 * c + 2]

time: 77.2 us -> 79.8 us (1.034)
  waiting for transfers between devices: 33.4 us -> 39.3 us
  local copies, waits for them, and re-layouts: 4.28 us -> 0.01 us
  starting transfers between devices: 17.5 us -> 19 us
    ppermute x18 -> x22, waiting for transfers between devices: 33.4 us -> 39.3 us  [permute(): return lax.ppermute(x, axis, perm)]
    unnamed x3 -> x2, local copies, waits for them, and re-layouts: 2.85 us -> 0.01 us
    ppermute x18 -> x22, starting transfers between devices: 17.5 us -> 19 us  [permute(): return lax.ppermute(x, axis, perm)]
    slice x2 -> x0, local copies, waits for them, and re-layouts: 1.43 us -> none  [the longest x1 0.72 us: shards(): x[:half]]
    pallas_call x7, Pallas kernels: 10.4 us -> 9.27 us  [the longest x4 9.15 us: score(): pl.pallas_call(functools.partial(score_kernel, sizes, tuple(pieces), len(...]
  transfers between devices with their start and end apart: 18 -> 22, of which waited for: 11 -> 10; matrix products, arithmetic and copies ran while one was open for 6% -> 0% of each run, Pallas kernels for 21% -> 19%
where the time goes in v6:
time: 79.8 us; the launch traced here: 79.5 us
  waiting for transfers between devices  39.3 us (49%)
  Pallas kernels  21 us (26%)
  starting transfers between devices  19 us (24%)
    ppermute x22, waiting for transfers between devices, permute(): return lax.ppermute(x, axis, perm)  39.3 us
    ppermute x22, starting transfers between devices, permute(): return lax.ppermute(x, axis, perm)  19 us
    pallas_call x4, Pallas kernels, score(): pl.pallas_call(functools.partial(score_kernel, sizes, tuple(pieces), len(...  9.15 us
    pallas_call x2, Pallas kernels, condition(): pl.pallas_call(functools.partial(condition_kernel, sizes, at_ids, len(mor...  5.53 us
    pallas_call x1, Pallas kernels, load(): pl.pallas_call(load_kernel, out_shape=pltpu.VMEM(source.shape, BF16), in_...  3.39 us
    pallas_call x1, Pallas kernels, take(): pl.pallas_call(take_kernel, out_shape=pltpu.VMEM((rows, source.shape[1]),...  1.92 us
  transfers between devices with their start and end apart: 22, of which 10 were waited for; matrix products, arithmetic and copies ran while one was open for 0% of the time, Pallas kernels for 19%

profile of v6, /device:TPU:0, one launch (start us, length us, event | category | flops | bytes accessed | tf_op | source)
XLA Modules:
  0.0 79.5 jit_solution(152108984401448136)
XLA Ops:
  0.0 1.9 %take.1.after.rest_0_ = bf16[256,1024]{1,0:T(8,128)(2,1)} custom-call(bf16[512,1024]{1,0:T(8,128)(2,1)} %bitcast.7), custom_call_target="tpu_custom_call" | custom-call | tf_op jit(solution)/shard_map/take/pallas_call | solution.py:53
  1.9 0.5 collective-permute-start.1
  2.4 2.6 %collective-permute-start = (bf16[256,1024]{1,0:T(8,128)(2,1)}, bf16[256,1024]{1,0:T(8,128)(2,1)}, u32[]{:S(2)}, u32[]{:S(2)}) collective-permute-start(bf16[256,1024]{1,0:T(8,128)(2,1)} %take.1.after.rest_0_), channel_id=1, source_target_pairs={{0,8},{4,12},{8,0},{12,4},{1,9},{5,13},{9,1},{13,5},{2,10},{6,14},... | collective-permute-start | bytes 1572872 | tf_op jit(solution)/shard_map/queries_from_chip/ppermute | solution.py:217
  5.0 3.4 %load_hessian.1.hess.rest_2_ = bf16[1024,4096]{1,0:T(8,128)(2,1)S(1)} custom-call(bf16[1024,4096]{1,0:T(8,128)(2,1)} %bitcast.8, bf16[256,1024]{1,0:T(8,128)(2,1)} %take.1.after.rest_0_), custom_call_target="tpu_custom_call" | custom-call | flops 999999995904 | bytes 1 | tf_op jit(solution)/shard_map/load_hessian/pallas_call | solution.py:75
  8.4 0.0 collective-permute-done.1.rest_1_
  8.4 2.5 %condition_here.1.rest_2_.rest_3_ = f32[1024,256]{1,0:T(8,128)S(1)} custom-call(bf16[1024,4096]{1,0:T(8,128)(2,1)S(1)} %load_hessian.1.hess.rest_2_, bf16[256,1024]{1,0:T(8,128)(2,1)} %take.1.after.rest_0_, bf16[256,1024]{1,0:T(8,128)(2,1)} %collective-permute-done.1.rest_1_, bf16[1024,4096]{1,0:T(8,128)(2,1)S(1)} %load_hessian.1.hess.rest_2_), custom_call_target="tpu_custom_call" | custom-call | flops 999999995904 | bytes 1 | tf_op jit(solution)/shard_map/condition_here/pallas_call | solution.py:110
  10.9 0.0 copy-start
  11.0 6.9 %collective-permute-done.rest_0_ = bf16[256,1024]{1,0:T(8,128)(2,1)} collective-permute-done((bf16[256,1024]{1,0:T(8,128)(2,1)}, bf16[256,1024]{1,0:T(8,128)(2,1)}, u32[]{:S(2)}, u32[]{:S(2)}) %collective-permute-start) | collective-permute-done | bytes 524320 | tf_op jit(solution)/shard_map/queries_from_chip/ppermute | solution.py:217
  17.9 0.0 collective-permute-start.2
  17.9 2.1 %collective-permute-done.2.rest_1_ = bf16[256,1024]{1,0:T(8,128)(2,1)S(1)} collective-permute-done((bf16[256,1024]{1,0:T(8,128)(2,1)}, bf16[256,1024]{1,0:T(8,128)(2,1)S(1)}, u32[]{:S(2)}, u32[]{:S(2)}) %collective-permute-start.2) | collective-permute-done | bytes 524320 | tf_op jit(solution)/shard_map/queries_there_from_core/ppermute | solution.py:217
  20.0 3.0 %condition_there.1 = (bf16[1024,256]{1,0:T(8,128)(2,1)S(1)}, bf16[512,256]{1,0:T(8,128)(2,1)}, bf16[512,256]{1,0:T(8,128)(2,1)}) custom-call(bf16[1024,4096]{1,0:T(8,128)(2,1)S(1)} %load_hessian.1.hess.rest_2_, bf16[256,1024]{1,0:T(8,128)(2,1)} %collective-permute-done.rest_0_, bf16[256,1024]{1,0:T(8,128)(2,1)S(1)} %collective-permute-done.2.rest_1_, ...), custom_call_target="tpu_custom_call" | custom-call | bytes 1 | tf_op jit(solution)/shard_map/condition_there/pallas_call | solution.py:110
  23.0 0.1 collective-permute-start.4
  23.2 1.8 %collective-permute-start.3 = (bf16[512,256]{1,0:T(8,128)(2,1)}, bf16[512,256]{1,0:T(8,128)(2,1)}, u32[]{:S(2)}, u32[]{:S(2)}) collective-permute-start(bf16[512,256]{1,0:T(8,128)(2,1)} %get-tuple-element.37), channel_id=1, source_target_pairs={{0,8},{4,12},{8,0},{12,4},{1,9},{5,13},{9,1},{13,5},{2,10},{6,14},... | collective-permute-start | bytes 786440 | tf_op jit(solution)/shard_map/upper_from_chip/ppermute | solution.py:217
  25.0 0.3 collective-permute-start.6
  25.2 0.0 collective-permute-done.4.rest_1_
  25.2 1.7 %collective-permute-start.10 = (bf16[512,256]{1,0:T(8,128)(2,1)}, bf16[512,256]{1,0:T(8,128)(2,1)}, u32[]{:S(2)}, u32[]{:S(2)}) collective-permute-start(bf16[512,256]{1,0:T(8,128)(2,1)} %get-tuple-element.37), channel_id=1, source_target_pairs={{0,16},{16,0},{1,17},{17,1},{2,18},{18,2},{3,19},{19,3},{4,20},{20... | collective-permute-start | bytes 786440 | tf_op jit(solution)/shard_map/upper_from_group/ppermute | solution.py:217
  26.9 0.3 collective-permute-start.12
  27.2 1.5 %own_here.1.rest_4_.rest_5_ = f32[4,320,256]{2,1,0:T(8,128)S(1)} custom-call(bf16[1280,4096]{1,0:T(8,128)(2,1)S(1)} %bitcast.3, bf16[1024,256]{1,0:T(8,128)(2,1)S(1)} %get-tuple-element.31.rest_0_.rest_2_, bf16[1024,256]{1,0:T(8,128)(2,1)S(1)} %collective-permute-done.4.rest_1_, bf16[1024,256]{1,0:T(8,128)(2,1)S(1)} %get-tuple-element.31.rest_0_.rest_2_), custom_call_target="tpu_custom_call" | custom-call | flops 999999995904 | bytes 1 | tf_op jit(solution)/shard_map/own_here/pallas_call | solution.py:155
  28.8 8.9 %collective-permute-done.6.rest_2_ = bf16[512,256]{1,0:T(8,128)(2,1)} collective-permute-done((bf16[512,256]{1,0:T(8,128)(2,1)}, bf16[512,256]{1,0:T(8,128)(2,1)}, u32[]{:S(2)}, u32[]{:S(2)}) %collective-permute-start.6) | collective-permute-done | bytes 262176 | tf_op jit(solution)/shard_map/lower_from_chip/ppermute | solution.py:217
  37.7 0.0 collective-permute-done.3.rest_0_
  37.7 0.0 collective-permute-start.5
  37.7 0.5 collective-permute-start.7
  38.2 1.0 %collective-permute-done.12.rest_2_ = bf16[512,256]{1,0:T(8,128)(2,1)} collective-permute-done((bf16[512,256]{1,0:T(8,128)(2,1)}, bf16[512,256]{1,0:T(8,128)(2,1)}, u32[]{:S(2)}, u32[]{:S(2)}) %collective-permute-start.12) | collective-permute-done | bytes 262176 | tf_op jit(solution)/shard_map/lower_from_group/ppermute | solution.py:217
  39.2 0.0 collective-permute-done.10.rest_0_
  39.2 0.0 collective-permute-start.11
  39.2 0.5 collective-permute-start.13
  39.7 1.7 %collective-permute-start.9 = (bf16[512,256]{1,0:T(8,128)(2,1)}, bf16[512,256]{1,0:T(8,128)(2,1)}, u32[]{:S(2)}, u32[]{:S(2)}) collective-permute-start(bf16[512,256]{1,0:T(8,128)(2,1)} %collective-permute-done.3.rest_0_), channel_id=1, source_target_pairs={{0,16},{16,0},{1,17},{17,1},{2,18},{18,2},{3,19},{19,3},{4,20},{20... | collective-permute-start | bytes 786440 | tf_op jit(solution)/shard_map/chips_upper_from_group/ppermute | solution.py:217
  41.5 0.0 collective-permute-done.5.rest_1_
  41.5 1.5 %collective-permute-start.15 = (bf16[512,256]{1,0:T(8,128)(2,1)}, bf16[512,256]{1,0:T(8,128)(2,1)}, u32[]{:S(2)}, u32[]{:S(2)}) collective-permute-start(bf16[512,256]{1,0:T(8,128)(2,1)} %collective-permute-done.12.rest_2_), channel_id=1, source_target_pairs={{0,8},{4,12},{8,0},{12,4},{1,9},{5,13},{9,1},{13,5},{2,10},{6,14},... | collective-permute-start | bytes 786440 | tf_op jit(solution)/shard_map/groups_lower_from_chip/ppermute | solution.py:217
  43.0 2.5 %own_there.1 = (bf16[2,320,256]{2,1,0:T(8,128)(2,1)S(1)}, f32[2,320,256]{2,1,0:T(8,128)S(1)}) custom-call(bf16[1280,4096]{1,0:T(8,128)(2,1)S(1)} %bitcast.4, bf16[512,256]{1,0:T(8,128)(2,1)} %collective-permute-done.3.rest_0_, bf16[512,256]{1,0:T(8,128)(2,1)S(1)} %collective-permute-done.5.rest_1_, bf16[512,256]{1,0:T(8,128)(2,1)} %collective-permute-done.6.rest_2_, ...), custom_call_target="tpu_custom_call" | custom-call | bytes 1 | tf_op jit(solution)/shard_map/own_there/pallas_call | solution.py:155
  45.6 2.5 %other_here.1.rest_4_.rest_5_ = f32[4,320,256]{2,1,0:T(8,128)S(1)} custom-call(bf16[1280,4096]{1,0:T(8,128)(2,1)S(1)} %bitcast.5, bf16[512,256]{1,0:T(8,128)(2,1)} %collective-permute-done.10.rest_0_, bf16[512,256]{1,0:T(8,128)(2,1)S(1)} %collective-permute-done.11.rest_1_, bf16[512,256]{1,0:T(8,128)(2,1)} %collective-permute-done.12.rest_2_, ...), custom_call_target="tpu_custom_call" | custom-call | flops 999999995904 | bytes 1 | tf_op jit(solution)/shard_map/other_here/pallas_call | solution.py:155
  48.1 1.6 %collective-permute-done.15.rest_2_ = bf16[512,256]{1,0:T(8,128)(2,1)} collective-permute-done((bf16[512,256]{1,0:T(8,128)(2,1)}, bf16[512,256]{1,0:T(8,128)(2,1)}, u32[]{:S(2)}, u32[]{:S(2)}) %collective-permute-start.15) | collective-permute-done | bytes 262176 | tf_op jit(solution)/shard_map/groups_lower_from_chip/ppermute | solution.py:217
  49.7 0.5 collective-permute-start.16
  50.2 1.6 %collective-permute-start.8 = (bf16[2,320,256]{2,1,0:T(8,128)(2,1)S(1)}, bf16[2,320,256]{2,1,0:T(8,128)(2,1)S(1)}, u32[]{:S(2)}, u32[]{:S(2)}) collective-permute-start(bf16[2,320,256]{2,1,0:T(8,128)(2,1)S(1)} %get-tuple-element.36), channel_id=1, source_target_pairs={{0,1},{1,0},{2,3},{3,2},{4,5},{5,4},{6,7},{7,6},{8,9},{9,8},{10,11... | collective-permute-start | bytes 983048 | tf_op jit(solution)/shard_map/own_from_layer_1/ppermute | solution.py:217
  51.8 0.0 collective-permute-done.16.rest_3_
  51.9 2.5 %other_there.1 = (bf16[2,320,128]{2,1,0:T(8,128)(2,1)S(1)}, f32[2,320,128]{2,1,0:T(8,128)S(1)}, bf16[2,320,128]{2,1,0:T(8,128)(2,1)S(1)}, f32[2,320,128]{2,1,0:T(8,128)S(1)}) custom-call(bf16[1280,4096]{1,0:T(8,128)(2,1)S(1)} %bitcast.6, bf16[512,256]{1,0:T(8,128)(2,1)} %collective-permute-done.9.rest_0_, ...), custom_call_target="tpu_custom_call" | custom-call | bytes 1 | tf_op jit(solution)/shard_map/other_there/pallas_call | solution.py:155
  54.4 1.6 %collective-permute-start.18 = (bf16[2,320,128]{2,1,0:T(8,128)(2,1)S(1)}, bf16[2,320,128]{2,1,0:T(8,128)(2,1)S(1)}, u32[]{:S(2)}, u32[]{:S(2)}) collective-permute-start(bf16[2,320,128]{2,1,0:T(8,128)(2,1)S(1)} %get-tuple-element.47), channel_id=1, source_target_pairs={{0,1},{1,0},{2,3},{3,2},{4,5},{5,4},{6,7},{7,6},{8,9},{9,8},{10,11... | collective-permute-start | bytes 491528 | tf_op jit(solution)/shard_map/other0_from_layer_1/ppermute | solution.py:217
  56.1 0.4 collective-permute-start.20
  56.5 4.3 %collective-permute-done.8.got = bf16[2,320,256]{2,1,0:T(8,128)(2,1)S(1)} collective-permute-done((bf16[2,320,256]{2,1,0:T(8,128)(2,1)S(1)}, bf16[2,320,256]{2,1,0:T(8,128)(2,1)S(1)}, u32[]{:S(2)}, u32[]{:S(2)}) %collective-permute-start.8) | collective-permute-done | bytes 327712 | tf_op jit(solution)/shard_map/own_from_layer_1/ppermute | solution.py:217
  60.8 0.1 sum0.1
  60.9 2.7 %collective-permute-start.17 = (bf16[1,320,256]{2,1,0:T(8,128)(2,1)S(1)}, bf16[1,320,256]{2,1,0:T(8,128)(2,1)S(1)}, u32[]{:S(2)}, u32[]{:S(2)}) collective-permute-start(bf16[1,320,256]{2,1,0:T(8,128)(2,1)S(1)} %get-tuple-element.45), channel_id=1, source_target_pairs={{0,2},{1,3},{2,0},{3,1},{4,6},{5,7},{6,4},{7,5},{8,10},{9,11},{10,... | collective-permute-start | bytes 491528 | tf_op jit(solution)/shard_map/sum0_from_layer_2/ppermute | solution.py:217
  63.5 5.2 %collective-permute-done.18.got = bf16[2,320,128]{2,1,0:T(8,128)(2,1)S(1)} collective-permute-done((bf16[2,320,128]{2,1,0:T(8,128)(2,1)S(1)}, bf16[2,320,128]{2,1,0:T(8,128)(2,1)S(1)}, u32[]{:S(2)}, u32[]{:S(2)}) %collective-permute-start.18) | collective-permute-done | bytes 163872 | tf_op jit(solution)/shard_map/other0_from_layer_1/ppermute | solution.py:217
  68.8 0.1 collective-permute-start.19
  68.8 2.4 %collective-permute-done.20.got = bf16[2,320,128]{2,1,0:T(8,128)(2,1)S(1)} collective-permute-done((bf16[2,320,128]{2,1,0:T(8,128)(2,1)S(1)}, bf16[2,320,128]{2,1,0:T(8,128)(2,1)S(1)}, u32[]{:S(2)}, u32[]{:S(2)}) %collective-permute-start.20) | collective-permute-done | bytes 163872 | tf_op jit(solution)/shard_map/other1_from_layer_1/ppermute | solution.py:217
  71.3 0.5 collective-permute-start.21
  71.9 5.8 %collective-permute-done.19.refs_3_ = bf16[1,320,128]{2,1,0:T(8,128)(2,1)S(1)} collective-permute-done((bf16[1,320,128]{2,1,0:T(8,128)(2,1)S(1)}, bf16[1,320,128]{2,1,0:T(8,128)(2,1)S(1)}, u32[]{:S(2)}, u32[]{:S(2)}) %collective-permute-start.19) | collective-permute-done | bytes 81952 | tf_op jit(solution)/shard_map/sum1_from_layer_2/ppermute | solution.py:217
  77.6 0.9 %collective-permute-done.21.refs_5_ = bf16[1,320,128]{2,1,0:T(8,128)(2,1)S(1)} collective-permute-done((bf16[1,320,128]{2,1,0:T(8,128)(2,1)S(1)}, bf16[1,320,128]{2,1,0:T(8,128)(2,1)S(1)}, u32[]{:S(2)}, u32[]{:S(2)}) %collective-permute-start.21) | collective-permute-done | bytes 81952 | tf_op jit(solution)/shard_map/sum2_from_layer_2/ppermute | solution.py:217
  78.6 0.9 %finish.1 = f32[320,512]{1,0:T(8,128)} custom-call(f32[1,320,256]{2,1,0:T(8,128)S(1)} %get-tuple-element.44.refs_0_, bf16[1,320,256]{2,1,0:T(8,128)(2,1)S(1)} %collective-permute-done.17.refs_1_, f32[1,320,128]{2,1,0:T(8,128)S(1)} %get-tuple-element.48.refs_2_, bf16[1,320,128]{2,1,0:T(8,128)(2,1)S(1)} %collective-permute-done.19.refs_3_, ...), custom_call_target="tpu_custom_call" | custom-call | tf_op jit(solution)/shard_map/finish/pallas_call | solution.py:200
  (10 shorter events, 0.1 us)
Async XLA Ops:
  1.9 6.5 %collective-permute-start.1 = (bf16[256,1024]{1,0:T(8,128)(2,1)}, bf16[256,1024]{1,0:T(8,128)(2,1)}, u32[]{:S(2)}, u32[]{:S(2)}) collective-permute-start(bf16[256,1024]{1,0:T(8,128)(2,1)} %take.1.after.rest_0_), channel_id=1, source_target_pairs={{0,4},{4,0},{8,12},{12,8},{1,5},{5,1},{9,13},{13,9},{2,6},{6,2},{1... | collective-permute-start | bytes 1572872 | tf_op jit(solution)/shard_map/queries_from_core/ppermute | solution.py:217
  2.4 15.4 %collective-permute-start = (bf16[256,1024]{1,0:T(8,128)(2,1)}, bf16[256,1024]{1,0:T(8,128)(2,1)}, u32[]{:S(2)}, u32[]{:S(2)}) collective-permute-start(bf16[256,1024]{1,0:T(8,128)(2,1)} %take.1.after.rest_0_), channel_id=1, source_target_pairs={{0,8},{4,12},{8,0},{12,4},{1,9},{5,13},{9,1},{13,5},{2,10},{6,14},... | collective-permute-start | bytes 1572872 | tf_op jit(solution)/shard_map/queries_from_chip/ppermute | solution.py:217
  10.9 16.3 %copy-start = (bf16[1280,1,4096]{2,0,1:T(8,128)(2,1)S(1)}, bf16[1280,1,4096]{2,0,1:T(8,128)(2,1)}, u32[]{:S(2)}) copy-start(bf16[1280,1,4096]{2,0,1:T(8,128)(2,1)} %param.5) | copy-start | bytes 31457284
  17.9 2.1 %collective-permute-start.2 = (bf16[256,1024]{1,0:T(8,128)(2,1)}, bf16[256,1024]{1,0:T(8,128)(2,1)S(1)}, u32[]{:S(2)}, u32[]{:S(2)}) collective-permute-start(bf16[256,1024]{1,0:T(8,128)(2,1)} %collective-permute-done.rest_0_), channel_id=1, source_target_pairs={{0,4},{4,0},{8,12},{12,8},{1,5},{5,1},{9,13},{13,9},{2,6},{6,2},{1... | collective-permute-start | bytes 1572872 | tf_op jit(solution)/shard_map/queries_there_from_core/ppermute | solution.py:217
  23.0 2.2 %collective-permute-start.4 = (bf16[1024,256]{1,0:T(8,128)(2,1)S(1)}, bf16[1024,256]{1,0:T(8,128)(2,1)S(1)}, u32[]{:S(2)}, u32[]{:S(2)}) collective-permute-start(bf16[1024,256]{1,0:T(8,128)(2,1)S(1)} %get-tuple-element.31.rest_0_.rest_2_), channel_id=1, source_target_pairs={{0,4},{4,0},{8,12},{12,8},{1,5},{5,1},{9,13},{13,9},{2,6},{6,2},{1... | collective-permute-start | bytes 1572872 | tf_op jit(solution)/shard_map/share_from_core/ppermute | solution.py:217
  23.2 14.5 %collective-permute-start.3 = (bf16[512,256]{1,0:T(8,128)(2,1)}, bf16[512,256]{1,0:T(8,128)(2,1)}, u32[]{:S(2)}, u32[]{:S(2)}) collective-permute-start(bf16[512,256]{1,0:T(8,128)(2,1)} %get-tuple-element.37), channel_id=1, source_target_pairs={{0,8},{4,12},{8,0},{12,4},{1,9},{5,13},{9,1},{13,5},{2,10},{6,14},... | collective-permute-start | bytes 786440 | tf_op jit(solution)/shard_map/upper_from_chip/ppermute | solution.py:217
  25.0 12.7 %collective-permute-start.6 = (bf16[512,256]{1,0:T(8,128)(2,1)}, bf16[512,256]{1,0:T(8,128)(2,1)}, u32[]{:S(2)}, u32[]{:S(2)}) collective-permute-start(bf16[512,256]{1,0:T(8,128)(2,1)} %get-tuple-element.39), channel_id=1, source_target_pairs={{0,8},{4,12},{8,0},{12,4},{1,9},{5,13},{9,1},{13,5},{2,10},{6,14},... | collective-permute-start | bytes 786440 | tf_op jit(solution)/shard_map/lower_from_chip/ppermute | solution.py:217
  25.2 14.0 %collective-permute-start.10 = (bf16[512,256]{1,0:T(8,128)(2,1)}, bf16[512,256]{1,0:T(8,128)(2,1)}, u32[]{:S(2)}, u32[]{:S(2)}) collective-permute-start(bf16[512,256]{1,0:T(8,128)(2,1)} %get-tuple-element.37), channel_id=1, source_target_pairs={{0,16},{16,0},{1,17},{17,1},{2,18},{18,2},{3,19},{19,3},{4,20},{20... | collective-permute-start | bytes 786440 | tf_op jit(solution)/shard_map/upper_from_group/ppermute | solution.py:217
  26.9 12.3 %collective-permute-start.12 = (bf16[512,256]{1,0:T(8,128)(2,1)}, bf16[512,256]{1,0:T(8,128)(2,1)}, u32[]{:S(2)}, u32[]{:S(2)}) collective-permute-start(bf16[512,256]{1,0:T(8,128)(2,1)} %get-tuple-element.39), channel_id=1, source_target_pairs={{0,16},{16,0},{1,17},{17,1},{2,18},{18,2},{3,19},{19,3},{4,20},{20... | collective-permute-start | bytes 786440 | tf_op jit(solution)/shard_map/lower_from_group/ppermute | solution.py:217
  37.7 3.8 %collective-permute-start.5 = (bf16[512,256]{1,0:T(8,128)(2,1)}, bf16[512,256]{1,0:T(8,128)(2,1)S(1)}, u32[]{:S(2)}, u32[]{:S(2)}) collective-permute-start(bf16[512,256]{1,0:T(8,128)(2,1)} %collective-permute-done.3.rest_0_), channel_id=1, source_target_pairs={{0,4},{4,0},{8,12},{12,8},{1,5},{5,1},{9,13},{13,9},{2,6},{6,2},{1... | collective-permute-start | bytes 786440 | tf_op jit(solution)/shard_map/chips_upper_from_core/ppermute | solution.py:217
  37.7 5.3 %collective-permute-start.7 = (bf16[512,256]{1,0:T(8,128)(2,1)}, bf16[512,256]{1,0:T(8,128)(2,1)S(1)}, u32[]{:S(2)}, u32[]{:S(2)}) collective-permute-start(bf16[512,256]{1,0:T(8,128)(2,1)} %collective-permute-done.6.rest_2_), channel_id=1, source_target_pairs={{0,4},{4,0},{8,12},{12,8},{1,5},{5,1},{9,13},{13,9},{2,6},{6,2},{1... | collective-permute-start | bytes 786440 | tf_op jit(solution)/shard_map/chips_lower_from_core/ppermute | solution.py:217
  39.2 6.3 %collective-permute-start.11 = (bf16[512,256]{1,0:T(8,128)(2,1)}, bf16[512,256]{1,0:T(8,128)(2,1)S(1)}, u32[]{:S(2)}, u32[]{:S(2)}) collective-permute-start(bf16[512,256]{1,0:T(8,128)(2,1)} %collective-permute-done.10.rest_0_), channel_id=1, source_target_pairs={{0,4},{4,0},{8,12},{12,8},{1,5},{5,1},{9,13},{13,9},{2,6},{6,2},{1... | collective-permute-start | bytes 786440 | tf_op jit(solution)/shard_map/groups_from_core/ppermute | solution.py:217
  39.2 6.3 %collective-permute-start.13 = (bf16[512,256]{1,0:T(8,128)(2,1)}, bf16[512,256]{1,0:T(8,128)(2,1)S(1)}, u32[]{:S(2)}, u32[]{:S(2)}) collective-permute-start(bf16[512,256]{1,0:T(8,128)(2,1)} %collective-permute-done.12.rest_2_), channel_id=1, source_target_pairs={{0,4},{4,0},{8,12},{12,8},{1,5},{5,1},{9,13},{13,9},{2,6},{6,2},{1... | collective-permute-start | bytes 786440 | tf_op jit(solution)/shard_map/groups_from_core/ppermute | solution.py:217
  39.7 10.0 %collective-permute-start.9 = (bf16[512,256]{1,0:T(8,128)(2,1)}, bf16[512,256]{1,0:T(8,128)(2,1)}, u32[]{:S(2)}, u32[]{:S(2)}) collective-permute-start(bf16[512,256]{1,0:T(8,128)(2,1)} %collective-permute-done.3.rest_0_), channel_id=1, source_target_pairs={{0,16},{16,0},{1,17},{17,1},{2,18},{18,2},{3,19},{19,3},{4,20},{20... | collective-permute-start | bytes 786440 | tf_op jit(solution)/shard_map/chips_upper_from_group/ppermute | solution.py:217
  41.5 8.3 %collective-permute-start.15 = (bf16[512,256]{1,0:T(8,128)(2,1)}, bf16[512,256]{1,0:T(8,128)(2,1)}, u32[]{:S(2)}, u32[]{:S(2)}) collective-permute-start(bf16[512,256]{1,0:T(8,128)(2,1)} %collective-permute-done.12.rest_2_), channel_id=1, source_target_pairs={{0,8},{4,12},{8,0},{12,4},{1,9},{5,13},{9,1},{13,5},{2,10},{6,14},... | collective-permute-start | bytes 786440 | tf_op jit(solution)/shard_map/groups_lower_from_chip/ppermute | solution.py:217
  49.7 2.1 %collective-permute-start.14 = (bf16[512,256]{1,0:T(8,128)(2,1)}, bf16[512,256]{1,0:T(8,128)(2,1)S(1)}, u32[]{:S(2)}, u32[]{:S(2)}) collective-permute-start(bf16[512,256]{1,0:T(8,128)(2,1)} %collective-permute-done.9.rest_0_), channel_id=1, source_target_pairs={{0,4},{4,0},{8,12},{12,8},{1,5},{5,1},{9,13},{13,9},{2,6},{6,2},{1... | collective-permute-start | bytes 786440 | tf_op jit(solution)/shard_map/diagonal_from_core/ppermute | solution.py:217
  49.7 2.1 %collective-permute-start.16 = (bf16[512,256]{1,0:T(8,128)(2,1)}, bf16[512,256]{1,0:T(8,128)(2,1)S(1)}, u32[]{:S(2)}, u32[]{:S(2)}) collective-permute-start(bf16[512,256]{1,0:T(8,128)(2,1)} %collective-permute-done.15.rest_2_), channel_id=1, source_target_pairs={{0,4},{4,0},{8,12},{12,8},{1,5},{5,1},{9,13},{13,9},{2,6},{6,2},{1... | collective-permute-start | bytes 786440 | tf_op jit(solution)/shard_map/diagonal_from_core/ppermute | solution.py:217
  50.2 10.6 %collective-permute-start.8 = (bf16[2,320,256]{2,1,0:T(8,128)(2,1)S(1)}, bf16[2,320,256]{2,1,0:T(8,128)(2,1)S(1)}, u32[]{:S(2)}, u32[]{:S(2)}) collective-permute-start(bf16[2,320,256]{2,1,0:T(8,128)(2,1)S(1)} %get-tuple-element.36), channel_id=1, source_target_pairs={{0,1},{1,0},{2,3},{3,2},{4,5},{5,4},{6,7},{7,6},{8,9},{9,8},{10,11... | collective-permute-start | bytes 983048 | tf_op jit(solution)/shard_map/own_from_layer_1/ppermute | solution.py:217
  54.4 14.3 %collective-permute-start.18 = (bf16[2,320,128]{2,1,0:T(8,128)(2,1)S(1)}, bf16[2,320,128]{2,1,0:T(8,128)(2,1)S(1)}, u32[]{:S(2)}, u32[]{:S(2)}) collective-permute-start(bf16[2,320,128]{2,1,0:T(8,128)(2,1)S(1)} %get-tuple-element.47), channel_id=1, source_target_pairs={{0,1},{1,0},{2,3},{3,2},{4,5},{5,4},{6,7},{7,6},{8,9},{9,8},{10,11... | collective-permute-start | bytes 491528 | tf_op jit(solution)/shard_map/other0_from_layer_1/ppermute | solution.py:217
  56.1 15.2 %collective-permute-start.20 = (bf16[2,320,128]{2,1,0:T(8,128)(2,1)S(1)}, bf16[2,320,128]{2,1,0:T(8,128)(2,1)S(1)}, u32[]{:S(2)}, u32[]{:S(2)}) collective-permute-start(bf16[2,320,128]{2,1,0:T(8,128)(2,1)S(1)} %get-tuple-element.50), channel_id=1, source_target_pairs={{0,1},{1,0},{2,3},{3,2},{4,5},{5,4},{6,7},{7,6},{8,9},{9,8},{10,11... | collective-permute-start | bytes 491528 | tf_op jit(solution)/shard_map/other1_from_layer_1/ppermute | solution.py:217
  60.9 11.0 %collective-permute-start.17 = (bf16[1,320,256]{2,1,0:T(8,128)(2,1)S(1)}, bf16[1,320,256]{2,1,0:T(8,128)(2,1)S(1)}, u32[]{:S(2)}, u32[]{:S(2)}) collective-permute-start(bf16[1,320,256]{2,1,0:T(8,128)(2,1)S(1)} %get-tuple-element.45), channel_id=1, source_target_pairs={{0,2},{1,3},{2,0},{3,1},{4,6},{5,7},{6,4},{7,5},{8,10},{9,11},{10,... | collective-permute-start | bytes 491528 | tf_op jit(solution)/shard_map/sum0_from_layer_2/ppermute | solution.py:217
  68.8 8.9 %collective-permute-start.19 = (bf16[1,320,128]{2,1,0:T(8,128)(2,1)S(1)}, bf16[1,320,128]{2,1,0:T(8,128)(2,1)S(1)}, u32[]{:S(2)}, u32[]{:S(2)}) collective-permute-start(bf16[1,320,128]{2,1,0:T(8,128)(2,1)S(1)} %get-tuple-element.49), channel_id=1, source_target_pairs={{0,2},{1,3},{2,0},{3,1},{4,6},{5,7},{6,4},{7,5},{8,10},{9,11},{10,... | collective-permute-start | bytes 245768 | tf_op jit(solution)/shard_map/sum1_from_layer_2/ppermute | solution.py:217
  71.3 7.3 %collective-permute-start.21 = (bf16[1,320,128]{2,1,0:T(8,128)(2,1)S(1)}, bf16[1,320,128]{2,1,0:T(8,128)(2,1)S(1)}, u32[]{:S(2)}, u32[]{:S(2)}) collective-permute-start(bf16[1,320,128]{2,1,0:T(8,128)(2,1)S(1)} %get-tuple-element.52), channel_id=1, source_target_pairs={{0,2},{1,3},{2,0},{3,1},{4,6},{5,7},{6,4},{7,5},{8,10},{9,11},{10,... | collective-permute-start | bytes 245768 | tf_op jit(solution)/shard_map/sum2_from_layer_2/ppermute | solution.py:217

commit v7 on v5

--- a/solution.py
+++ b/solution.py
@@ -18,6 +18,7 @@
     "sum1": 3_000_000_000,
     "sum2": 3_000_000_000,
 }
+CHUNKS = 2
 MIB = 1 << 20
 VMEM = pl.BlockSpec(memory_space=pltpu.VMEM)
 SMEM = pl.BlockSpec(memory_space=pltpu.SMEM)
@@ -36,24 +37,43 @@
     return ids, blocks, place
 
 
-def take_kernel(source, out, sem):
+def take_kernel(chunk, source, after, out, sem):
     rows = out.shape[0]
-    at = pl.ds(pl.multiple_of(lax.axis_index("groups") * rows, rows), rows)
-    copy = pltpu.make_async_copy(source.at[at, :], out, sem)
+    at = pl.multiple_of((lax.axis_index("groups") * CHUNKS + chunk) * rows, rows)
+    copy = pltpu.make_async_copy(source.at[pl.ds(at, rows), :], out, sem)
     copy.start()
     copy.wait()
 
 
-def take(source, rows):
-    return pl.pallas_call(
-        take_kernel,
+def take(name, chunk, source, after, rows):
+    return pl.pallas_call(
+        functools.partial(take_kernel, chunk),
         out_shape=pltpu.VMEM((rows, source.shape[1]), BF16),
-        in_specs=[HBM],
+        in_specs=[HBM, VMEM if chunk else ANY],
         out_specs=VMEM,
         scratch_shapes=[pltpu.SemaphoreType.DMA],
         compiler_params=pltpu.CompilerParams(vmem_limit_bytes=2 * MIB),
-        name="take",
-    )(pltpu.with_memory_space_constraint(source, pltpu.HBM))
+        cost_estimate=cost(name),
+        name=name,
+    )(pltpu.with_memory_space_constraint(source, pltpu.HBM), after)
+
+
+def cut_kernel(half, source, out):
+    rows = out.shape[0]
+    out[...] = source[half * rows : (half + 1) * rows, :]
+
+
+def cut(name, half, source):
+    shape = (source.shape[0] // 2, source.shape[1])
+    return pl.pallas_call(
+        functools.partial(cut_kernel, half),
+        out_shape=pltpu.VMEM(shape, BF16),
+        in_specs=[VMEM],
+        out_specs=VMEM,
+        compiler_params=pltpu.CompilerParams(vmem_limit_bytes=4 * MIB),
+        cost_estimate=cost(name),
+        name=name,
+    )(source)
 
 
 def cost(name):
@@ -89,12 +109,15 @@
 
 def condition_kernel(sizes, at_ids, more, hess, *rest):
     ids, _, _ = positions(*sizes)
-    pieces, rest = rest[: len(at_ids)], rest[len(at_ids) + 1 :]
+    count = CHUNKS * len(at_ids)
+    pieces, rest = rest[:count], rest[count + 1 :]
     before, (out, right) = rest[0] if more else None, rest[more:]
-    depth = pieces[0].shape[1]
+    rows, depth = pieces[0].shape
     places, runs = runs_of(ids, at_ids, depth)
-    for at, piece in zip(places, pieces):
-        right[:, pl.ds(pl.multiple_of(at, depth), depth)] = piece[...]
+    for i, piece in enumerate(pieces):
+        at = pl.multiple_of(places[i // CHUNKS], depth)
+        low = i % CHUNKS * rows
+        right[low : low + rows, pl.ds(at, depth)] = piece[...]
     total = before[...] if more else None
     for low, column, span in runs:
         term = lax.dot_general(
@@ -108,18 +131,19 @@
 
 
 def condition(name, sizes, hess, at_ids, pieces, after, before=None):
-    queries, depth = pieces[0].shape
+    queries, depth = CHUNKS * pieces[0][0].shape[0], pieces[0][0].shape[1]
+    flat = [x for xs in pieces for x in xs]
     more = [] if before is None else [before]
     return pl.pallas_call(
         functools.partial(condition_kernel, sizes, at_ids, len(more)),
-        out_shape=jax.ShapeDtypeStruct((hess.shape[0], queries), BF16 if more else F32),
-        in_specs=[VMEM] * (1 + len(pieces)) + [ANY] + [VMEM] * len(more),
+        out_shape=pltpu.VMEM((hess.shape[0], queries), BF16 if more else F32),
+        in_specs=[VMEM] * (1 + len(flat)) + [ANY] + [VMEM] * len(more),
         out_specs=VMEM,
         scratch_shapes=[pltpu.VMEM((queries, len(pieces) * depth), BF16)],
         compiler_params=pltpu.CompilerParams(vmem_limit_bytes=12 * MIB),
         cost_estimate=cost(name),
         name=name,
-    )(hess, *pieces, after, *more)
+    )(hess, *flat, after, *more)
 
 
 def score_kernel(sizes, at_ids, offsets, more, store, *rest):
@@ -166,7 +190,7 @@
             low += x.shape[0]
     return pl.pallas_call(
         functools.partial(score_kernel, sizes, at_ids, tuple(offsets), len(more)),
-        out_shape=[jax.ShapeDtypeStruct(*shape) for shape in shapes],
+        out_shape=[pltpu.VMEM(*shape) for shape in shapes],
         in_specs=[VMEM] * (1 + len(flat)) + [ANY] + [VMEM] * len(more),
         out_specs=[VMEM] * len(shapes),
         scratch_shapes=[pltpu.VMEM((len(at_ids) * low, width), BF16)],
@@ -189,7 +213,7 @@
     shape = (keep.shape[0] // 2,) + keep.shape[1:]
     return pl.pallas_call(
         fold_kernel,
-        out_shape=(jax.ShapeDtypeStruct(shape, BF16), jax.ShapeDtypeStruct(shape, F32)),
+        out_shape=(pltpu.VMEM(shape, BF16), pltpu.VMEM(shape, F32)),
         in_specs=[VMEM, VMEM, ANY],
         out_specs=(VMEM, VMEM),
         compiler_params=pltpu.CompilerParams(vmem_limit_bytes=4 * MIB),
@@ -270,22 +294,29 @@
         send, keep = fold(name, keep, got, token)
         return keep, from_layer(send, layers // keep.shape[0] // 2, name)
 
-    hess = load("load_hessian", hessian[0], queries)
+    source = queries[:, 0, :]
+    width = total // groups // CHUNKS
     rows = pltpu.with_memory_space_constraint(store[:, 0, :], pltpu.VMEM)
-    mine = take(queries[:, 0, :], total // groups)
-    mine_there, mine_core = gather_chip(mine, "queries"), from_core(mine, "queries")
-    part = condition("condition_here", sizes, hess, here, [mine, mine_core], queries)
-    mine_there = after(part, mine_there)
-    pieces = with_cores(mine_there, flip(mine_there, "queries_there"))
+    mine = [take("take0", 0, source, source[:8], width)]
+    mine_there, mine_core = [gather_chip(mine[0], "queries0")], [from_core(mine[0], "queries0")]
+    mine.append(take("take1", 1, source, mine_core[0], width))
+    mine_there.append(gather_chip(mine[1], "queries1"))
+    mine_core.append(from_core(mine[1], "queries1"))
+    hess = load("load_hessian", hessian[0], mine[1])
+    part = condition("condition_here", sizes, hess, here, [mine, mine_core], hess)
+    pieces = []
+    for xs in zip(*[after(part, xs) for xs in mine_there]):
+        pieces += [xs, flip(xs, "queries_there")]
     share = condition("condition_there", sizes, hess, there, pieces, part, part)
     by_chip, by_group = gather_chip(share, "share"), gather_group(share, "share")
     share_core = from_core(share, "share")
     part = score("own_here", sizes, rows, here, [[share], [share_core]], share)[0]
     by_chip, by_group = after(part, by_chip), after(part, by_group)
-    half = share.shape[0] // 2
     by_chip_cores, by_group_cores = flip(by_chip, "by_chip"), flip(by_group, "by_group")
-    upper = [[from_group(x[:half], j, "upper") for x in by_chip] for j in range(1, groups)]
-    lower = [[from_chip(x[half:], k, "lower") for k in range(1, chips)] for x in by_group]
+    upper = [cut("cut0", 0, x) for x in by_chip]
+    lower = [cut("cut1", 1, x) for x in by_group]
+    upper = [[from_group(x, j, "upper") for x in upper] for j in range(1, groups)]
+    lower = [gather_chip(x, "lower") for x in lower]
     pieces = [[x] for x in with_cores(by_chip, by_chip_cores)]
     send, keep = score("own_there", sizes, rows, there, pieces, part, part, 1)
     parts = [((0, 0), (keep, from_layer(send, 1, "own")))]
@@ -297,10 +328,10 @@
         flips = [flip(pair, "diagonal") for pair in halves]
         pieces = [x for pair in zip(halves, flips) for x in pair]
         made = score("other_there", sizes, rows, there, pieces, part, part, 2)
-        cut = made[0].shape[2]
+        columns = made[0].shape[2]
         for c in range(2):
             send, token = made[2 * c : 2 * c + 2]
-            parts.append(((j + 1, c * cut), (token, from_layer(send, 1, f"other{c}"))))
+            parts.append(((j + 1, c * columns), (token, from_layer(send, 1, f"other{c}"))))
     while any(part[0].shape[0] > 1 for _, part in parts):
         parts = [(at, step(f"sum{i}", *part, token)) for i, (at, part) in enumerate(parts)]
     return finish(sizes, parts, total)

time: 77.2 us -> 77.9 us (level)
  Pallas kernels: 21.4 us -> 24.4 us
  local copies, waits for them, and re-layouts: 4.28 us -> 1.67 us
  starting transfers between devices: 17.5 us -> 20.1 us
  waiting for transfers between devices: 33.4 us -> 31.1 us
    pallas_call x4 -> x7, Pallas kernels: 4.76 us -> 7.81 us  [the longest x2 3.42 us: take(): pl.pallas_call(functools.partial(take_kernel, chunk), out_shape=pltpu.VME...]
    ppermute x18 -> x21, starting transfers between devices: 17.5 us -> 20.1 us  [permute(): return lax.ppermute(x, axis, perm)]
    ppermute x18 -> x21, waiting for transfers between devices: 33.4 us -> 31.1 us  [permute(): return lax.ppermute(x, axis, perm)]
    unnamed x3 -> x6, local copies, waits for them, and re-layouts: 2.85 us -> 0.95 us
  transfers between devices with their start and end apart: 18 -> 21, of which waited for: 11 -> 12; matrix products, arithmetic and copies ran while one was open for 6% -> 0% of each run, Pallas kernels for 21% -> 25%
where the time goes in v7:
time: 77.9 us; the launch traced here: 77.4 us
  waiting for transfers between devices  31.1 us (40%)
  Pallas kernels  24.4 us (31%)
  starting transfers between devices  20.1 us (26%)
  local copies, waits for them, and re-layouts  1.67 us (2%)
    ppermute x21, waiting for transfers between devices, permute(): return lax.ppermute(x, axis, perm)  31.1 us
    ppermute x21, starting transfers between devices, permute(): return lax.ppermute(x, axis, perm)  20.1 us
    pallas_call x4, Pallas kernels, score(): pl.pallas_call(functools.partial(score_kernel, sizes, at_ids, tuple(offse...  7.43 us
    pallas_call x2, Pallas kernels, condition(): pl.pallas_call(functools.partial(condition_kernel, sizes, at_ids, len(mor...  4.82 us
    pallas_call x2, Pallas kernels, take(): pl.pallas_call(functools.partial(take_kernel, chunk), out_shape=pltpu.VME...  3.42 us
    pallas_call x1, Pallas kernels, load(): pl.pallas_call(load_kernel, out_shape=pltpu.VMEM(source.shape, BF16), in_...  3.39 us
    pallas_call x3, Pallas kernels, fold(): pl.pallas_call(fold_kernel, out_shape=(pltpu.VMEM(shape, BF16), pltpu.VME...  2.92 us
  transfers between devices with their start and end apart: 21, of which 12 were waited for; matrix products, arithmetic and copies ran while one was open for 0% of the time, Pallas kernels for 25%

profile of v7, /device:TPU:0, one launch (start us, length us, event | category | flops | bytes accessed | tf_op | source)
XLA Modules:
  0.0 77.4 jit_solution(6904854212908738585)
XLA Ops:
  0.0 0.7 slice_bitcast_fusion.after
  0.7 1.7 %take0.1.rest_0_ = bf16[128,1024]{1,0:T(8,128)(2,1)} custom-call(bf16[512,1024]{1,0:T(8,128)(2,1)} %bitcast.9, bf16[8,1024]{1,0:T(8,128)(2,1)S(1)} %slice_bitcast_fusion.after), custom_call_target="tpu_custom_call" | custom-call | bytes 1 | tf_op jit(solution)/shard_map/take0/pallas_call | solution.py:49
  2.4 0.5 collective-permute-start
  2.9 2.6 %collective-permute-start.1 = (bf16[128,1024]{1,0:T(8,128)(2,1)}, bf16[128,1024]{1,0:T(8,128)(2,1)}, u32[]{:S(2)}, u32[]{:S(2)}) collective-permute-start(bf16[128,1024]{1,0:T(8,128)(2,1)} %take0.1.rest_0_), channel_id=1, source_target_pairs={{0,8},{4,12},{8,0},{12,4},{1,9},{5,13},{9,1},{13,5},{2,10},{6,14},... | collective-permute-start | bytes 786440 | tf_op jit(solution)/shard_map/queries0_from_chip/ppermute | solution.py:254
  5.5 0.0 collective-permute-done.after.rest_2_
  5.5 1.8 %take1.1.after.rest_1_ = bf16[128,1024]{1,0:T(8,128)(2,1)} custom-call(bf16[512,1024]{1,0:T(8,128)(2,1)} %bitcast.10, bf16[128,1024]{1,0:T(8,128)(2,1)S(1)} %collective-permute-done.after.rest_2_), custom_call_target="tpu_custom_call" | custom-call | bytes 1 | tf_op jit(solution)/shard_map/take1/pallas_call | solution.py:49
  7.3 1.7 %collective-permute-start.3 = (bf16[128,1024]{1,0:T(8,128)(2,1)}, bf16[128,1024]{1,0:T(8,128)(2,1)}, u32[]{:S(2)}, u32[]{:S(2)}) collective-permute-start(bf16[128,1024]{1,0:T(8,128)(2,1)} %take1.1.after.rest_1_), channel_id=1, source_target_pairs={{0,8},{4,12},{8,0},{12,4},{1,9},{5,13},{9,1},{13,5},{2,10},{6,14},... | collective-permute-start | bytes 786440 | tf_op jit(solution)/shard_map/queries1_from_chip/ppermute | solution.py:254
  9.0 3.4 %load_hessian.1.hess.rest_4_ = bf16[1024,4096]{1,0:T(8,128)(2,1)S(1)} custom-call(bf16[1024,4096]{1,0:T(8,128)(2,1)} %bitcast.11, bf16[128,1024]{1,0:T(8,128)(2,1)} %take1.1.after.rest_1_), custom_call_target="tpu_custom_call" | custom-call | flops 999999995904 | bytes 1 | tf_op jit(solution)/shard_map/load_hessian/pallas_call | solution.py:90
  12.4 0.9 %copy-done.2 = bf16[128,1024]{1,0:T(8,128)(2,1)S(1)} copy-done((bf16[128,1024]{1,0:T(8,128)(2,1)S(1)}, bf16[128,1024]{1,0:T(8,128)(2,1)}, u32[]{:S(2)}) %copy-start.2) | copy-done | bytes 262168
  13.4 2.4 %condition_here.1.rest_4_.rest_5_ = f32[1024,256]{1,0:T(8,128)S(1)} custom-call(bf16[1024,4096]{1,0:T(8,128)(2,1)S(1)} %load_hessian.1.hess.rest_4_, bf16[128,1024]{1,0:T(8,128)(2,1)} %take0.1.rest_0_, bf16[128,1024]{1,0:T(8,128)(2,1)} %take1.1.after.rest_1_, bf16[128,1024]{1,0:T(8,128)(2,1)S(1)} %copy-done.2, ...), custom_call_target="tpu_custom_call" | custom-call | flops 999999995904 | bytes 1 | tf_op jit(solution)/shard_map/condition_here/pallas_call | solution.py:137
  15.8 0.0 copy-start
  15.8 2.5 %collective-permute-done.3.rest_1_ = bf16[128,1024]{1,0:T(8,128)(2,1)} collective-permute-done((bf16[128,1024]{1,0:T(8,128)(2,1)}, bf16[128,1024]{1,0:T(8,128)(2,1)}, u32[]{:S(2)}, u32[]{:S(2)}) %collective-permute-start.3) | collective-permute-done | bytes 262176 | tf_op jit(solution)/shard_map/queries1_from_chip/ppermute | solution.py:254
  18.3 0.5 collective-permute-start.5
  18.8 1.2 %collective-permute-done.4.rest_2_ = bf16[128,1024]{1,0:T(8,128)(2,1)S(1)} collective-permute-done((bf16[128,1024]{1,0:T(8,128)(2,1)}, bf16[128,1024]{1,0:T(8,128)(2,1)S(1)}, u32[]{:S(2)}, u32[]{:S(2)}) %collective-permute-start.4) | collective-permute-done | bytes 262176 | tf_op jit(solution)/shard_map/queries_there_from_core/ppermute | solution.py:254
  20.1 0.4 collective-permute-done.5.rest_3_
  20.5 2.4 %condition_there.1.rest_0_.rest_2_ = bf16[1024,256]{1,0:T(8,128)(2,1)S(1)} custom-call(bf16[1024,4096]{1,0:T(8,128)(2,1)S(1)} %load_hessian.1.hess.rest_4_, bf16[128,1024]{1,0:T(8,128)(2,1)} %collective-permute-done.1.rest_0_, bf16[128,1024]{1,0:T(8,128)(2,1)} %collective-permute-done.3.rest_1_, bf16[128,1024]{1,0:T(8,128)(2,1)S(1)} %collective-permute-done.4.rest_2_, ...), custom_call_target="tpu_custom_call" | custom-call | bytes 1 | tf_op jit(solution)/shard_map/condition_there/pallas_call | solution.py:137
  22.8 0.2 collective-permute-start.7
  23.0 1.8 %collective-permute-start.6 = (bf16[1024,256]{1,0:T(8,128)(2,1)S(1)}, bf16[1024,256]{1,0:T(8,128)(2,1)S(1)}, u32[]{:S(2)}, u32[]{:S(2)}) collective-permute-start(bf16[1024,256]{1,0:T(8,128)(2,1)S(1)} %condition_there.1.rest_0_.rest_2_), channel_id=1, source_target_pairs={{0,8},{4,12},{8,0},{12,4},{1,9},{5,13},{9,1},{13,5},{2,10},{6,14},... | collective-permute-start | bytes 1572872 | tf_op jit(solution)/shard_map/share_from_chip/ppermute | solution.py:254
  24.8 1.5 %collective-permute-start.11 = (bf16[1024,256]{1,0:T(8,128)(2,1)S(1)}, bf16[1024,256]{1,0:T(8,128)(2,1)S(1)}, u32[]{:S(2)}, u32[]{:S(2)}) collective-permute-start(bf16[1024,256]{1,0:T(8,128)(2,1)S(1)} %condition_there.1.rest_0_.rest_2_), channel_id=1, source_target_pairs={{0,16},{16,0},{1,17},{17,1},{2,18},{18,2},{3,19},{19,3},{4,20},{20... | collective-permute-start | bytes 1572872 | tf_op jit(solution)/shard_map/share_from_group/ppermute | solution.py:254
  26.3 1.6 %own_here.1.rest_2_.rest_3_ = f32[4,320,256]{2,1,0:T(8,128)S(1)} custom-call(bf16[1280,4096]{1,0:T(8,128)(2,1)S(1)} %bitcast.5, bf16[1024,256]{1,0:T(8,128)(2,1)S(1)} %condition_there.1.rest_0_.rest_2_, bf16[1024,256]{1,0:T(8,128)(2,1)S(1)} %collective-permute-done.7.rest_1_, bf16[1024,256]{1,0:T(8,128)(2,1)S(1)} %condition_there.1.rest_0_.rest_2_), custom_call_target="tpu_custom_call" | custom-call | flops 3000000000 | bytes 1 | tf_op jit(solution)/shard_map/own_here/pallas_call | solution.py:191
  27.9 9.4 %collective-permute-done.6.rest_0_.source = bf16[1024,256]{1,0:T(8,128)(2,1)S(1)} collective-permute-done((bf16[1024,256]{1,0:T(8,128)(2,1)S(1)}, bf16[1024,256]{1,0:T(8,128)(2,1)S(1)}, u32[]{:S(2)}, u32[]{:S(2)}) %collective-permute-start.6) | collective-permute-done | bytes 524320 | tf_op jit(solution)/shard_map/share_from_chip/ppermute | solution.py:254
  37.3 1.5 %collective-permute-done.11.rest_0_.source = bf16[1024,256]{1,0:T(8,128)(2,1)S(1)} collective-permute-done((bf16[1024,256]{1,0:T(8,128)(2,1)S(1)}, bf16[1024,256]{1,0:T(8,128)(2,1)S(1)}, u32[]{:S(2)}, u32[]{:S(2)}) %collective-permute-start.11) | collective-permute-done | bytes 524320 | tf_op jit(solution)/shard_map/share_from_group/ppermute | solution.py:254
  38.7 0.7 cut0.1
  39.5 0.7 cut1.1
  40.2 0.8 %collective-permute-start.13 = (bf16[512,256]{1,0:T(8,128)(2,1)}, bf16[512,256]{1,0:T(8,128)(2,1)}, u32[]{:S(2)}, u32[]{:S(2)}) collective-permute-start(bf16[512,256]{1,0:T(8,128)(2,1)} %cut1.1), channel_id=1, source_target_pairs={{0,8},{4,12},{8,0},{12,4},{1,9},{5,13},{9,1},{13,5},{2,10},{6,14},... | collective-permute-start | bytes 786440 | tf_op jit(solution)/shard_map/lower_from_chip/ppermute | solution.py:254
  41.0 1.5 %collective-permute-start.10 = (bf16[512,256]{1,0:T(8,128)(2,1)}, bf16[512,256]{1,0:T(8,128)(2,1)}, u32[]{:S(2)}, u32[]{:S(2)}) collective-permute-start(bf16[512,256]{1,0:T(8,128)(2,1)} %cut0.1), channel_id=1, source_target_pairs={{0,16},{16,0},{1,17},{17,1},{2,18},{18,2},{3,19},{19,3},{4,20},{20... | collective-permute-start | bytes 786440 | tf_op jit(solution)/shard_map/upper_from_group/ppermute | solution.py:254
  42.5 1.6 %own_there.1 = (bf16[2,320,256]{2,1,0:T(8,128)(2,1)}, f32[2,320,256]{2,1,0:T(8,128)S(1)}) custom-call(bf16[1280,4096]{1,0:T(8,128)(2,1)S(1)} %bitcast.6, bf16[1024,256]{1,0:T(8,128)(2,1)S(1)} %collective-permute-done.6.rest_0_.source, bf16[1024,256]{1,0:T(8,128)(2,1)S(1)} %collective-permute-done.8.rest_1_, f32[4,320,256]{2,1,0:T(8,128)S(1)} %own_here.1.rest_2_.rest_3_, ...), custom_call_target="tpu_custom_call" | custom-call | bytes 1 | tf_op jit(solution)/shard_map/own_there/pallas_call | solution.py:191
  44.1 1.6 %collective-permute-start.9 = (bf16[2,320,256]{2,1,0:T(8,128)(2,1)}, bf16[2,320,256]{2,1,0:T(8,128)(2,1)}, u32[]{:S(2)}, u32[]{:S(2)}) collective-permute-start(bf16[2,320,256]{2,1,0:T(8,128)(2,1)} %get-tuple-element.27), channel_id=1, source_target_pairs={{0,1},{1,0},{2,3},{3,2},{4,5},{5,4},{6,7},{7,6},{8,9},{9,8},{10,11... | collective-permute-start | bytes 983048 | tf_op jit(solution)/shard_map/own_from_layer_1/ppermute | solution.py:254
  45.7 1.6 %other_here.1.rest_4_.rest_5_ = f32[4,320,256]{2,1,0:T(8,128)S(1)} custom-call(bf16[1280,4096]{1,0:T(8,128)(2,1)S(1)} %bitcast.7, bf16[1024,256]{1,0:T(8,128)(2,1)S(1)} %collective-permute-done.11.rest_0_.source, bf16[1024,256]{1,0:T(8,128)(2,1)S(1)} %collective-permute-done.12.rest_1_, f32[2,320,256]{2,1,0:T(8,128)S(1)} %get-tuple-element.26.rest_2_.keep), custom_call_target="tpu_custom_call" | custom-call | flops 999999995904 | bytes 1 | tf_op jit(solution)/shard_map/other_here/pallas_call | solution.py:191
  47.2 2.0 %collective-permute-done.13.rest_1_ = bf16[512,256]{1,0:T(8,128)(2,1)} collective-permute-done((bf16[512,256]{1,0:T(8,128)(2,1)}, bf16[512,256]{1,0:T(8,128)(2,1)}, u32[]{:S(2)}, u32[]{:S(2)}) %collective-permute-start.13) | collective-permute-done | bytes 262176 | tf_op jit(solution)/shard_map/lower_from_chip/ppermute | solution.py:254
  49.2 0.0 collective-permute-done.10.rest_0_
  49.2 0.5 collective-permute-start.15
  49.7 1.2 %collective-permute-done.14.rest_2_ = bf16[512,256]{1,0:T(8,128)(2,1)S(1)} collective-permute-done((bf16[512,256]{1,0:T(8,128)(2,1)}, bf16[512,256]{1,0:T(8,128)(2,1)S(1)}, u32[]{:S(2)}, u32[]{:S(2)}) %collective-permute-start.14) | collective-permute-done | bytes 262176 | tf_op jit(solution)/shard_map/diagonal_from_core/ppermute | solution.py:254
  51.0 0.4 collective-permute-done.15.rest_3_
  51.4 2.7 %other_there.1 = (bf16[2,320,128]{2,1,0:T(8,128)(2,1)}, f32[2,320,128]{2,1,0:T(8,128)S(1)}, bf16[2,320,128]{2,1,0:T(8,128)(2,1)}, f32[2,320,128]{2,1,0:T(8,128)S(1)}) custom-call(bf16[1280,4096]{1,0:T(8,128)(2,1)S(1)} %bitcast.8, bf16[512,256]{1,0:T(8,128)(2,1)} %collective-permute-done.10.rest_0_, bf16[512,256]{1,0:T(8,128)(2,1)} %collective-permute-done.13.rest_1_, ...), custom_call_target="tpu_custom_call" | custom-call | bytes 1 | tf_op jit(solution)/shard_map/other_there/pallas_call | solution.py:191
  54.0 1.8 %collective-permute-start.17 = (bf16[2,320,128]{2,1,0:T(8,128)(2,1)}, bf16[2,320,128]{2,1,0:T(8,128)(2,1)}, u32[]{:S(2)}, u32[]{:S(2)}) collective-permute-start(bf16[2,320,128]{2,1,0:T(8,128)(2,1)} %get-tuple-element.35), channel_id=1, source_target_pairs={{0,1},{1,0},{2,3},{3,2},{4,5},{5,4},{6,7},{7,6},{8,9},{9,8},{10,11... | collective-permute-start | bytes 491528 | tf_op jit(solution)/shard_map/other0_from_layer_1/ppermute | solution.py:254
  55.8 0.2 collective-permute-start.19
  56.1 1.0 %sum0.1 = (bf16[1,320,256]{2,1,0:T(8,128)(2,1)S(1)}, f32[1,320,256]{2,1,0:T(8,128)S(1)}) custom-call(f32[2,320,256]{2,1,0:T(8,128)S(1)} %get-tuple-element.26.rest_2_.keep, bf16[2,320,256]{2,1,0:T(8,128)(2,1)} %collective-permute-done.9.got, f32[2,320,128]{2,1,0:T(8,128)S(1)} %get-tuple-element.31._.keep), custom_call_target="tpu_custom_call" | custom-call | flops 999999995904 | bytes 1 | tf_op jit(solution)/shard_map/sum0/pallas_call | solution.py:214
  57.1 2.9 %collective-permute-start.16 = (bf16[1,320,256]{2,1,0:T(8,128)(2,1)S(1)}, bf16[1,320,256]{2,1,0:T(8,128)(2,1)S(1)}, u32[]{:S(2)}, u32[]{:S(2)}) collective-permute-start(bf16[1,320,256]{2,1,0:T(8,128)(2,1)S(1)} %get-tuple-element.33), channel_id=1, source_target_pairs={{0,2},{1,3},{2,0},{3,1},{4,6},{5,7},{6,4},{7,5},{8,10},{9,11},{10,... | collective-permute-start | bytes 491528 | tf_op jit(solution)/shard_map/sum0_from_layer_2/ppermute | solution.py:254
  60.0 5.8 %collective-permute-done.17.got = bf16[2,320,128]{2,1,0:T(8,128)(2,1)} collective-permute-done((bf16[2,320,128]{2,1,0:T(8,128)(2,1)}, bf16[2,320,128]{2,1,0:T(8,128)(2,1)}, u32[]{:S(2)}, u32[]{:S(2)}) %collective-permute-start.17) | collective-permute-done | bytes 163872 | tf_op jit(solution)/shard_map/other0_from_layer_1/ppermute | solution.py:254
  65.8 0.9 %sum1.1 = (bf16[1,320,128]{2,1,0:T(8,128)(2,1)S(1)}, f32[1,320,128]{2,1,0:T(8,128)S(1)}) custom-call(f32[2,320,128]{2,1,0:T(8,128)S(1)} %get-tuple-element.34.keep, bf16[2,320,128]{2,1,0:T(8,128)(2,1)} %collective-permute-done.17.got, f32[2,320,128]{2,1,0:T(8,128)S(1)} %get-tuple-element.31._.keep), custom_call_target="tpu_custom_call" | custom-call | flops 3000000000 | bytes 1 | tf_op jit(solution)/shard_map/sum1/pallas_call | solution.py:214
  66.7 0.8 %collective-permute-start.18 = (bf16[1,320,128]{2,1,0:T(8,128)(2,1)S(1)}, bf16[1,320,128]{2,1,0:T(8,128)(2,1)S(1)}, u32[]{:S(2)}, u32[]{:S(2)}) collective-permute-start(bf16[1,320,128]{2,1,0:T(8,128)(2,1)S(1)} %get-tuple-element.37), channel_id=1, source_target_pairs={{0,2},{1,3},{2,0},{3,1},{4,6},{5,7},{6,4},{7,5},{8,10},{9,11},{10,... | collective-permute-start | bytes 245768 | tf_op jit(solution)/shard_map/sum1_from_layer_2/ppermute | solution.py:254
  67.5 1.0 %collective-permute-done.19.got = bf16[2,320,128]{2,1,0:T(8,128)(2,1)} collective-permute-done((bf16[2,320,128]{2,1,0:T(8,128)(2,1)}, bf16[2,320,128]{2,1,0:T(8,128)(2,1)}, u32[]{:S(2)}, u32[]{:S(2)}) %collective-permute-start.19) | collective-permute-done | bytes 163872 | tf_op jit(solution)/shard_map/other1_from_layer_1/ppermute | solution.py:254
  68.5 0.9 %sum2.1 = (bf16[1,320,128]{2,1,0:T(8,128)(2,1)S(1)}, f32[1,320,128]{2,1,0:T(8,128)S(1)}) custom-call(f32[2,320,128]{2,1,0:T(8,128)S(1)} %get-tuple-element.31._.keep, bf16[2,320,128]{2,1,0:T(8,128)(2,1)} %collective-permute-done.19.got, f32[2,320,128]{2,1,0:T(8,128)S(1)} %get-tuple-element.31._.keep), custom_call_target="tpu_custom_call" | custom-call | flops 3000000000 | bytes 1 | tf_op jit(solution)/shard_map/sum2/pallas_call | solution.py:214
  69.5 1.2 %collective-permute-start.20 = (bf16[1,320,128]{2,1,0:T(8,128)(2,1)S(1)}, bf16[1,320,128]{2,1,0:T(8,128)(2,1)S(1)}, u32[]{:S(2)}, u32[]{:S(2)}) collective-permute-start(bf16[1,320,128]{2,1,0:T(8,128)(2,1)S(1)} %get-tuple-element.40), channel_id=1, source_target_pairs={{0,2},{1,3},{2,0},{3,1},{4,6},{5,7},{6,4},{7,5},{8,10},{9,11},{10,... | collective-permute-start | bytes 245768 | tf_op jit(solution)/shard_map/sum2_from_layer_2/ppermute | solution.py:254
  70.7 3.8 %collective-permute-done.18.refs_3_ = bf16[1,320,128]{2,1,0:T(8,128)(2,1)S(1)} collective-permute-done((bf16[1,320,128]{2,1,0:T(8,128)(2,1)S(1)}, bf16[1,320,128]{2,1,0:T(8,128)(2,1)S(1)}, u32[]{:S(2)}, u32[]{:S(2)}) %collective-permute-start.18) | collective-permute-done | bytes 81952 | tf_op jit(solution)/shard_map/sum1_from_layer_2/ppermute | solution.py:254
  74.5 2.0 %collective-permute-done.20.refs_5_ = bf16[1,320,128]{2,1,0:T(8,128)(2,1)S(1)} collective-permute-done((bf16[1,320,128]{2,1,0:T(8,128)(2,1)S(1)}, bf16[1,320,128]{2,1,0:T(8,128)(2,1)S(1)}, u32[]{:S(2)}, u32[]{:S(2)}) %collective-permute-start.20) | collective-permute-done | bytes 81952 | tf_op jit(solution)/shard_map/sum2_from_layer_2/ppermute | solution.py:254
  76.5 0.9 %finish.1 = f32[320,512]{1,0:T(8,128)} custom-call(f32[1,320,256]{2,1,0:T(8,128)S(1)} %get-tuple-element.32.refs_0_, bf16[1,320,256]{2,1,0:T(8,128)(2,1)S(1)} %collective-permute-done.16.refs_1_, f32[1,320,128]{2,1,0:T(8,128)S(1)} %get-tuple-element.36.refs_2_, bf16[1,320,128]{2,1,0:T(8,128)(2,1)S(1)} %collective-permute-done.18.refs_3_, ...), custom_call_target="tpu_custom_call" | custom-call | tf_op jit(solution)/shard_map/finish/pallas_call | solution.py:237
  (16 shorter events, 0.0 us)
Async XLA Ops:
  2.4 3.1 %collective-permute-start = (bf16[128,1024]{1,0:T(8,128)(2,1)}, bf16[128,1024]{1,0:T(8,128)(2,1)S(1)}, u32[]{:S(2)}, u32[]{:S(2)}) collective-permute-start(bf16[128,1024]{1,0:T(8,128)(2,1)} %take0.1.rest_0_), channel_id=1, source_target_pairs={{0,4},{4,0},{8,12},{12,8},{1,5},{5,1},{9,13},{13,9},{2,6},{6,2},{1... | collective-permute-start | bytes 786440 | tf_op jit(solution)/shard_map/queries0_from_core/ppermute | solution.py:254
  2.9 15.4 %collective-permute-start.1 = (bf16[128,1024]{1,0:T(8,128)(2,1)}, bf16[128,1024]{1,0:T(8,128)(2,1)}, u32[]{:S(2)}, u32[]{:S(2)}) collective-permute-start(bf16[128,1024]{1,0:T(8,128)(2,1)} %take0.1.rest_0_), channel_id=1, source_target_pairs={{0,8},{4,12},{8,0},{12,4},{1,9},{5,13},{9,1},{13,5},{2,10},{6,14},... | collective-permute-start | bytes 786440 | tf_op jit(solution)/shard_map/queries0_from_chip/ppermute | solution.py:254
  5.5 6.9 %copy-start.1 = (bf16[128,1024]{1,0:T(8,128)(2,1)}, bf16[128,1024]{1,0:T(8,128)(2,1)S(1)}, u32[]{:S(2)}) copy-start(bf16[128,1024]{1,0:T(8,128)(2,1)S(1)} %collective-permute-done.after.rest_2_) | copy-start | bytes 786436
  7.3 11.1 %collective-permute-start.3 = (bf16[128,1024]{1,0:T(8,128)(2,1)}, bf16[128,1024]{1,0:T(8,128)(2,1)}, u32[]{:S(2)}, u32[]{:S(2)}) collective-permute-start(bf16[128,1024]{1,0:T(8,128)(2,1)} %take1.1.after.rest_1_), channel_id=1, source_target_pairs={{0,8},{4,12},{8,0},{12,4},{1,9},{5,13},{9,1},{13,5},{2,10},{6,14},... | collective-permute-start | bytes 786440 | tf_op jit(solution)/shard_map/queries1_from_chip/ppermute | solution.py:254
  9.0 3.4 %collective-permute-start.2 = (bf16[128,1024]{1,0:T(8,128)(2,1)}, bf16[128,1024]{1,0:T(8,128)(2,1)}, u32[]{:S(2)}, u32[]{:S(2)}) collective-permute-start(bf16[128,1024]{1,0:T(8,128)(2,1)} %take1.1.after.rest_1_), channel_id=1, source_target_pairs={{0,4},{4,0},{8,12},{12,8},{1,5},{5,1},{9,13},{13,9},{2,6},{6,2},{1... | collective-permute-start | bytes 786440 | tf_op jit(solution)/shard_map/queries1_from_core/ppermute | solution.py:254
  12.4 1.0 %copy-start.2 = (bf16[128,1024]{1,0:T(8,128)(2,1)S(1)}, bf16[128,1024]{1,0:T(8,128)(2,1)}, u32[]{:S(2)}) copy-start(bf16[128,1024]{1,0:T(8,128)(2,1)} %copy-done.1) | copy-start | bytes 786436
  15.8 10.5 %copy-start = (bf16[1280,1,4096]{2,0,1:T(8,128)(2,1)S(1)}, bf16[1280,1,4096]{2,0,1:T(8,128)(2,1)}, u32[]{:S(2)}) copy-start(bf16[1280,1,4096]{2,0,1:T(8,128)(2,1)} %param.5) | copy-start | bytes 31457284
  18.3 1.7 %collective-permute-start.4 = (bf16[128,1024]{1,0:T(8,128)(2,1)}, bf16[128,1024]{1,0:T(8,128)(2,1)S(1)}, u32[]{:S(2)}, u32[]{:S(2)}) collective-permute-start(bf16[128,1024]{1,0:T(8,128)(2,1)} %collective-permute-done.1.rest_0_), channel_id=1, source_target_pairs={{0,4},{4,0},{8,12},{12,8},{1,5},{5,1},{9,13},{13,9},{2,6},{6,2},{1... | collective-permute-start | bytes 786440 | tf_op jit(solution)/shard_map/queries_there_from_core/ppermute | solution.py:254
  18.3 2.1 %collective-permute-start.5 = (bf16[128,1024]{1,0:T(8,128)(2,1)}, bf16[128,1024]{1,0:T(8,128)(2,1)S(1)}, u32[]{:S(2)}, u32[]{:S(2)}) collective-permute-start(bf16[128,1024]{1,0:T(8,128)(2,1)} %collective-permute-done.3.rest_1_), channel_id=1, source_target_pairs={{0,4},{4,0},{8,12},{12,8},{1,5},{5,1},{9,13},{13,9},{2,6},{6,2},{1... | collective-permute-start | bytes 786440 | tf_op jit(solution)/shard_map/queries_there_from_core/ppermute | solution.py:254
  22.8 3.5 %collective-permute-start.7 = (bf16[1024,256]{1,0:T(8,128)(2,1)S(1)}, bf16[1024,256]{1,0:T(8,128)(2,1)S(1)}, u32[]{:S(2)}, u32[]{:S(2)}) collective-permute-start(bf16[1024,256]{1,0:T(8,128)(2,1)S(1)} %condition_there.1.rest_0_.rest_2_), channel_id=1, source_target_pairs={{0,4},{4,0},{8,12},{12,8},{1,5},{5,1},{9,13},{13,9},{2,6},{6,2},{1... | collective-permute-start | bytes 1572872 | tf_op jit(solution)/shard_map/share_from_core/ppermute | solution.py:254
  23.0 14.2 %collective-permute-start.6 = (bf16[1024,256]{1,0:T(8,128)(2,1)S(1)}, bf16[1024,256]{1,0:T(8,128)(2,1)S(1)}, u32[]{:S(2)}, u32[]{:S(2)}) collective-permute-start(bf16[1024,256]{1,0:T(8,128)(2,1)S(1)} %condition_there.1.rest_0_.rest_2_), channel_id=1, source_target_pairs={{0,8},{4,12},{8,0},{12,4},{1,9},{5,13},{9,1},{13,5},{2,10},{6,14},... | collective-permute-start | bytes 1572872 | tf_op jit(solution)/shard_map/share_from_chip/ppermute | solution.py:254
  24.8 13.9 %collective-permute-start.11 = (bf16[1024,256]{1,0:T(8,128)(2,1)S(1)}, bf16[1024,256]{1,0:T(8,128)(2,1)S(1)}, u32[]{:S(2)}, u32[]{:S(2)}) collective-permute-start(bf16[1024,256]{1,0:T(8,128)(2,1)S(1)} %condition_there.1.rest_0_.rest_2_), channel_id=1, source_target_pairs={{0,16},{16,0},{1,17},{17,1},{2,18},{18,2},{3,19},{19,3},{4,20},{20... | collective-permute-start | bytes 1572872 | tf_op jit(solution)/shard_map/share_from_group/ppermute | solution.py:254
  37.3 5.2 %collective-permute-start.8 = (bf16[1024,256]{1,0:T(8,128)(2,1)S(1)}, bf16[1024,256]{1,0:T(8,128)(2,1)S(1)}, u32[]{:S(2)}, u32[]{:S(2)}) collective-permute-start(bf16[1024,256]{1,0:T(8,128)(2,1)S(1)} %collective-permute-done.6.rest_0_.source), channel_id=1, source_target_pairs={{0,4},{4,0},{8,12},{12,8},{1,5},{5,1},{9,13},{13,9},{2,6},{6,2},{1... | collective-permute-start | bytes 1572872 | tf_op jit(solution)/shard_map/by_chip_from_core/ppermute | solution.py:254
  38.7 7.0 %collective-permute-start.12 = (bf16[1024,256]{1,0:T(8,128)(2,1)S(1)}, bf16[1024,256]{1,0:T(8,128)(2,1)S(1)}, u32[]{:S(2)}, u32[]{:S(2)}) collective-permute-start(bf16[1024,256]{1,0:T(8,128)(2,1)S(1)} %collective-permute-done.11.rest_0_.source), channel_id=1, source_target_pairs={{0,4},{4,0},{8,12},{12,8},{1,5},{5,1},{9,13},{13,9},{2,6},{6,2},{1... | collective-permute-start | bytes 1572872 | tf_op jit(solution)/shard_map/by_group_from_core/ppermute | solution.py:254
  40.2 9.0 %collective-permute-start.13 = (bf16[512,256]{1,0:T(8,128)(2,1)}, bf16[512,256]{1,0:T(8,128)(2,1)}, u32[]{:S(2)}, u32[]{:S(2)}) collective-permute-start(bf16[512,256]{1,0:T(8,128)(2,1)} %cut1.1), channel_id=1, source_target_pairs={{0,8},{4,12},{8,0},{12,4},{1,9},{5,13},{9,1},{13,5},{2,10},{6,14},... | collective-permute-start | bytes 786440 | tf_op jit(solution)/shard_map/lower_from_chip/ppermute | solution.py:254
  41.0 8.3 %collective-permute-start.10 = (bf16[512,256]{1,0:T(8,128)(2,1)}, bf16[512,256]{1,0:T(8,128)(2,1)}, u32[]{:S(2)}, u32[]{:S(2)}) collective-permute-start(bf16[512,256]{1,0:T(8,128)(2,1)} %cut0.1), channel_id=1, source_target_pairs={{0,16},{16,0},{1,17},{17,1},{2,18},{18,2},{3,19},{19,3},{4,20},{20... | collective-permute-start | bytes 786440 | tf_op jit(solution)/shard_map/upper_from_group/ppermute | solution.py:254
  44.1 12.0 %collective-permute-start.9 = (bf16[2,320,256]{2,1,0:T(8,128)(2,1)}, bf16[2,320,256]{2,1,0:T(8,128)(2,1)}, u32[]{:S(2)}, u32[]{:S(2)}) collective-permute-start(bf16[2,320,256]{2,1,0:T(8,128)(2,1)} %get-tuple-element.27), channel_id=1, source_target_pairs={{0,1},{1,0},{2,3},{3,2},{4,5},{5,4},{6,7},{7,6},{8,9},{9,8},{10,11... | collective-permute-start | bytes 983048 | tf_op jit(solution)/shard_map/own_from_layer_1/ppermute | solution.py:254
  49.2 1.7 %collective-permute-start.14 = (bf16[512,256]{1,0:T(8,128)(2,1)}, bf16[512,256]{1,0:T(8,128)(2,1)S(1)}, u32[]{:S(2)}, u32[]{:S(2)}) collective-permute-start(bf16[512,256]{1,0:T(8,128)(2,1)} %collective-permute-done.10.rest_0_), channel_id=1, source_target_pairs={{0,4},{4,0},{8,12},{12,8},{1,5},{5,1},{9,13},{13,9},{2,6},{6,2},{1... | collective-permute-start | bytes 786440 | tf_op jit(solution)/shard_map/diagonal_from_core/ppermute | solution.py:254
  49.2 2.1 %collective-permute-start.15 = (bf16[512,256]{1,0:T(8,128)(2,1)}, bf16[512,256]{1,0:T(8,128)(2,1)S(1)}, u32[]{:S(2)}, u32[]{:S(2)}) collective-permute-start(bf16[512,256]{1,0:T(8,128)(2,1)} %collective-permute-done.13.rest_1_), channel_id=1, source_target_pairs={{0,4},{4,0},{8,12},{12,8},{1,5},{5,1},{9,13},{13,9},{2,6},{6,2},{1... | collective-permute-start | bytes 786440 | tf_op jit(solution)/shard_map/diagonal_from_core/ppermute | solution.py:254
  54.0 11.7 %collective-permute-start.17 = (bf16[2,320,128]{2,1,0:T(8,128)(2,1)}, bf16[2,320,128]{2,1,0:T(8,128)(2,1)}, u32[]{:S(2)}, u32[]{:S(2)}) collective-permute-start(bf16[2,320,128]{2,1,0:T(8,128)(2,1)} %get-tuple-element.35), channel_id=1, source_target_pairs={{0,1},{1,0},{2,3},{3,2},{4,5},{5,4},{6,7},{7,6},{8,9},{9,8},{10,11... | collective-permute-start | bytes 491528 | tf_op jit(solution)/shard_map/other0_from_layer_1/ppermute | solution.py:254
  55.8 12.7 %collective-permute-start.19 = (bf16[2,320,128]{2,1,0:T(8,128)(2,1)}, bf16[2,320,128]{2,1,0:T(8,128)(2,1)}, u32[]{:S(2)}, u32[]{:S(2)}) collective-permute-start(bf16[2,320,128]{2,1,0:T(8,128)(2,1)} %get-tuple-element.38), channel_id=1, source_target_pairs={{0,1},{1,0},{2,3},{3,2},{4,5},{5,4},{6,7},{7,6},{8,9},{9,8},{10,11... | collective-permute-start | bytes 491528 | tf_op jit(solution)/shard_map/other1_from_layer_1/ppermute | solution.py:254
  57.1 13.6 %collective-permute-start.16 = (bf16[1,320,256]{2,1,0:T(8,128)(2,1)S(1)}, bf16[1,320,256]{2,1,0:T(8,128)(2,1)S(1)}, u32[]{:S(2)}, u32[]{:S(2)}) collective-permute-start(bf16[1,320,256]{2,1,0:T(8,128)(2,1)S(1)} %get-tuple-element.33), channel_id=1, source_target_pairs={{0,2},{1,3},{2,0},{3,1},{4,6},{5,7},{6,4},{7,5},{8,10},{9,11},{10,... | collective-permute-start | bytes 491528 | tf_op jit(solution)/shard_map/sum0_from_layer_2/ppermute | solution.py:254
  66.7 7.8 %collective-permute-start.18 = (bf16[1,320,128]{2,1,0:T(8,128)(2,1)S(1)}, bf16[1,320,128]{2,1,0:T(8,128)(2,1)S(1)}, u32[]{:S(2)}, u32[]{:S(2)}) collective-permute-start(bf16[1,320,128]{2,1,0:T(8,128)(2,1)S(1)} %get-tuple-element.37), channel_id=1, source_target_pairs={{0,2},{1,3},{2,0},{3,1},{4,6},{5,7},{6,4},{7,5},{8,10},{9,11},{10,... | collective-permute-start | bytes 245768 | tf_op jit(solution)/shard_map/sum1_from_layer_2/ppermute | solution.py:254
  69.5 7.0 %collective-permute-start.20 = (bf16[1,320,128]{2,1,0:T(8,128)(2,1)S(1)}, bf16[1,320,128]{2,1,0:T(8,128)(2,1)S(1)}, u32[]{:S(2)}, u32[]{:S(2)}) collective-permute-start(bf16[1,320,128]{2,1,0:T(8,128)(2,1)S(1)} %get-tuple-element.40), channel_id=1, source_target_pairs={{0,2},{1,3},{2,0},{3,1},{4,6},{5,7},{6,4},{7,5},{8,10},{9,11},{10,... | collective-permute-start | bytes 245768 | tf_op jit(solution)/shard_map/sum2_from_layer_2/ppermute | solution.py:254

commit v8 on v4

v8 whole, which is shorter than its diff:
```python
import functools

import jax
import jax.numpy as jnp
from jax import lax
from jax.experimental import pallas as pl
from jax.experimental.pallas import tpu as pltpu
from jax.sharding import PartitionSpec as P

F32, BF16 = jnp.float32, jnp.bfloat16
CORES = 2
CHUNKS = 2
MIB = 1 << 20
VMEM = pl.BlockSpec(memory_space=pltpu.VMEM)
SMEM = pl.BlockSpec(memory_space=pltpu.SMEM)
ANY = pl.BlockSpec(memory_space=pl.ANY)


HBM = pl.BlockSpec(memory_space=pltpu.HBM)


def positions(groups, ex, layers, place):
    at_group, at_ex, at_layer = (ref[0] for ref in place)
    chips = ex // CORES
    chip, core = at_ex // CORES, lax.rem(at_ex, CORES)
    ids = [lax.rem(chip + k, chips) * CORES + (core ^ s) for k in range(chips) for s in range(CORES)]
    blocks = [at_layer ^ r for r in range(layers)]
    return ids, blocks, [lax.rem(at_group + j, groups) for j in range(groups)]


def load_kernel(source, after, out, sem):
    copy = pltpu.make_async_copy(source, out, sem)
    copy.start()
    copy.wait()


def load(source, after):
    return pl.pallas_call(
        load_kernel,
        out_shape=pltpu.VMEM(source.shape, BF16),
        in_specs=[HBM, ANY],
        out_specs=VMEM,
        scratch_shapes=[pltpu.SemaphoreType.DMA],
        compiler_params=pltpu.CompilerParams(vmem_limit_bytes=2 * MIB),
        name="load",
    )(pltpu.with_memory_space_constraint(source, pltpu.HBM), after)


def take_kernel(chunk, at_group, source, after, out, sem):
    rows = out.shape[0]
    at = pl.multiple_of((at_group[0] * CHUNKS + chunk) * rows, rows)
    copy = pltpu.make_async_copy(source.at[pl.ds(at, rows), :], out, sem)
    copy.start()
    copy.wait()


def take(chunk, place, source, after, rows):
    return pl.pallas_call(
        functools.partial(take_kernel, chunk),
        out_shape=pltpu.VMEM((rows, source.shape[1]), BF16),
        in_specs=[SMEM, HBM, ANY],
        out_specs=VMEM,
        scratch_shapes=[pltpu.SemaphoreType.DMA],
        compiler_params=pltpu.CompilerParams(vmem_limit_bytes=2 * MIB),
        name="take",
    )(place[0], pltpu.with_memory_space_constraint(source, pltpu.HBM), after)


def condition_kernel(sizes, *refs):
    place, (hess, *rest) = refs[:3], refs[3:]
    ids, _, _ = positions(*sizes, place)
    pieces, (_, out, right) = rest[: len(ids)], rest[len(ids) :]
    width = pieces[0].shape[1]
    for t, piece in zip(ids, pieces):
        right[:, pl.ds(pl.multiple_of(t * width, width), width)] = piece[...]
    out[...] = lax.dot_general(
        hess[...], right[...], (((1,), (1,)), ((), ())), preferred_element_type=F32
    ).astype(BF16)


def condition(sizes, place, hess, pieces, after):
    rows, queries = hess.shape[0], pieces[0].shape[0]
    return pl.pallas_call(
        functools.partial(condition_kernel, sizes),
        out_shape=pltpu.VMEM((rows, queries), BF16),
        in_specs=[SMEM] * 3 + [VMEM] * (1 + len(pieces)) + [ANY],
        out_specs=VMEM,
        scratch_shapes=[pltpu.VMEM((queries, hess.shape[1]), BF16)],
        compiler_params=pltpu.CompilerParams(vmem_limit_bytes=12 * MIB),
        name="condition",
    )(*place, hess, *pieces, after)


def score_kernel(sizes, direct, *refs):
    place, (store, *rest) = refs[:3], refs[3:]
    ids, blocks, _ = positions(*sizes, place)
    layers = len(blocks)
    pieces, (_, *outs, right) = rest[: len(ids)], rest[len(ids) :]
    rows = store.shape[0] // layers
    depth = pieces[0].shape[0]
    for t, piece in zip(ids, pieces):
        right[pl.ds(pl.multiple_of(t * depth, depth), depth), :] = piece[...]
    for r in [*range(1, layers, 2), *range(0, layers, 2)]:
        at = pl.ds(pl.multiple_of(blocks[r] * rows, rows), rows)
        part = jnp.dot(store[at, :], right[...], preferred_element_type=F32)
        if direct:
            outs[r][0] = part.astype(outs[r].dtype)
        else:
            outs[1 - r % 2][r // 2] = part.astype(outs[1 - r % 2].dtype)


def score(name, sizes, place, store, pieces, after, direct=False):
    depth, width = pieces[0].shape
    layers = sizes[2]
    rows = store.shape[0] // layers
    shapes = [((layers // 2, rows, width), t) for t in (BF16, F32)]
    if direct:
        shapes = [((1, rows, width), BF16 if r else F32) for r in range(layers)]
    return pl.pallas_call(
        functools.partial(score_kernel, sizes, direct),
        out_shape=[pltpu.VMEM(*shape) for shape in shapes],
        in_specs=[SMEM] * 3 + [VMEM] * (1 + len(pieces)) + [ANY],
        out_specs=[VMEM] * len(shapes),
        scratch_shapes=[pltpu.VMEM((len(pieces) * depth, width), BF16)],
        compiler_params=pltpu.CompilerParams(vmem_limit_bytes=12 * MIB),
        name=name,
    )(*place, store, *pieces, after)


def fold_kernel(keep, got, _, send, left):
    for r in range(keep.shape[0]):
        total = keep[r] + got[r].astype(F32)
        if r % 2:
            send[r // 2] = total.astype(BF16)
        else:
            left[r // 2] = total


def fold(keep, got, after):
    shape = (keep.shape[0] // 2,) + keep.shape[1:]
    return pl.pallas_call(
        fold_kernel,
        out_shape=(pltpu.VMEM(shape, BF16), pltpu.VMEM(shape, F32)),
        in_specs=[VMEM, VMEM, ANY],
        out_specs=(VMEM, VMEM),
        compiler_params=pltpu.CompilerParams(vmem_limit_bytes=4 * MIB),
        name="fold",
    )(keep, got, after)


def finish_kernel(sizes, counts, *refs):
    place, (*refs, out) = refs[:3], refs[3:]
    _, _, order = positions(*sizes, place)
    groups = len(order)
    width = refs[0].shape[2]
    for i, count in enumerate(counts):
        (keep, *rest), refs = refs[:count], refs[count:]
        total = keep[0]
        for got in rest:
            total = total + got[0].astype(F32)
        at = order[i % groups] * (out.shape[1] // groups) + i // groups * width
        out[:, pl.ds(pl.multiple_of(at, width), width)] = total


def finish(sizes, place, parts, queries):
    rows = parts[0][0].shape[1]
    return pl.pallas_call(
        functools.partial(finish_kernel, sizes, tuple(map(len, parts))),
        out_shape=jax.ShapeDtypeStruct((rows, queries), F32),
        in_specs=[SMEM] * 3 + [VMEM] * sum(map(len, parts)),
        out_specs=VMEM,
        compiler_params=pltpu.CompilerParams(vmem_limit_bytes=12 * MIB),
        name="finish",
    )(*place, *[a for part in parts for a in part])


def shards(groups, ex, layers, queries, hessian, store):
    chips = ex // CORES
    sizes = groups, ex, layers
    total = queries.shape[0]
    place = [lax.axis_index(a).astype(jnp.int32)[None] for a in ("groups", "ex", "layer")]

    def permute(x, axis, perm, what):
        with jax.named_scope(what):
            return lax.ppermute(x, axis, perm)

    def from_chip(x, k, what):
        perm = [(e, (e - k * CORES) % ex) for e in range(ex)]
        return permute(x, "ex", perm, what + "_from_chip")

    def from_core(x, what):
        return permute(x, "ex", [(e, e ^ 1) for e in range(ex)], what + "_from_core")

    def from_group(x, j, what):
        perm = [(g, (g - j) % groups) for g in range(groups)]
        return permute(x, "groups", perm, what + "_from_group")

    def from_layer(x, r, what):
        return permute(x, "layer", [(z, z ^ r) for z in range(layers)], f"{what}_from_layer_{r}")

    def tie(x, *others):
        return lax.optimization_barrier((x, *others))[0]

    def gather_chip(x, what):
        return [from_chip(x, k, what) for k in range(1, chips)]

    def gather_group(x, what):
        return [from_group(x, j, what) for j in range(1, groups)]

    def with_cores(ours, theirs):
        return [x for pair in zip(ours, theirs) for x in pair]

    def flip(xs, what):
        return [from_core(x, what) for x in xs]

    def after(token, xs):
        return [tie(x, token) for x in xs]

    parts = []

    def advance(token, chain=False):
        for i, part in enumerate(parts):
            if part[0].shape[0] > 1:
                if chain and i and parts[i - 1][0].shape[0] == 1:
                    token = tie(token, parts[i - 1][1])
                send, keep = fold(part[0], part[1], token)
                step = layers // keep.shape[0] // 2
                part[:] = keep, from_layer(send, step, f"sum{i}")

    def send_parts(made):
        send, keep = made
        advance(keep, chain=True)
        parts.append([keep, from_layer(send, 1, f"sum{len(parts)}")])
        return parts[-2][0] if parts[1:] else keep

    rows = pltpu.with_memory_space_constraint(store[:, 0, :], pltpu.VMEM)
    width = total // groups // CHUNKS
    q0 = take(0, place, queries[:, 0, :], place[0], width)
    q0_there, q0_core = gather_chip(q0, "q0"), from_core(q0, "q0")
    hess = load(hessian[0], q0)
    q1 = take(1, place, queries[:, 0, :], hess, width)
    q0_there = after(q1, q0_there)
    q0_cores = [q0_core] + flip(q0_there, "q0_there")
    q1_there, q1_core = gather_chip(q1, "q1"), from_core(q1, "q1")
    s0 = condition(sizes, place, hess, with_cores([q0] + q0_there, q0_cores), q1)
    s0_there, s0_across, s0_core = gather_chip(s0, "s0"), gather_group(s0, "s0"), from_core(s0, "s0")
    q1_there = after(s0, q1_there)
    q1_cores = [q1_core] + flip(q1_there, "q1_there")
    s0_diagonal = [gather_group(x, "s0_there") for x in s0_there]
    s0_cores = [s0_core] + flip(s0_there, "s0_there")
    s1 = condition(sizes, place, hess, with_cores([q1] + q1_there, q1_cores), s0_there[-1])
    s1_there, s1_core = gather_chip(s1, "s1"), from_core(s1, "s1")
    s0_across = after(s1, s0_across)
    s0_across_cores = flip(s0_across, "s0_across")
    last = send_parts(score("score0", sizes, place, rows, with_cores([s0] + s0_there, s0_cores), s1))
    s0_diagonal = [after(last, xs) for xs in s0_diagonal]
    s0_diagonal_cores = [flip(xs, "s0_diagonal") for xs in s0_diagonal]
    s1_across = gather_group(tie(s1, s0_diagonal[-1][-1]), "s1")
    s1_there = after(last, s1_there)
    s1_diagonal = [gather_group(x, "s1_there") for x in s1_there]
    s1_cores = [s1_core] + flip(s1_there, "s1_there")
    for j in range(groups - 1):
        ours = [s0_across[j]] + [xs[j] for xs in s0_diagonal]
        theirs = [s0_across_cores[j]] + [xs[j] for xs in s0_diagonal_cores]
        last = send_parts(score("score1", sizes, place, rows, with_cores(ours, theirs), last))
    last = send_parts(score("score2", sizes, place, rows, with_cores([s1] + s1_there, s1_cores), last))
    s1_across = after(last, s1_across)
    s1_across_cores = flip(s1_across, "s1_across")
    s1_diagonal = [after(last, xs) for xs in s1_diagonal]
    s1_diagonal_cores = [flip(xs, "s1_diagonal") for xs in s1_diagonal]
    for j in range(groups - 1):
        ours = [s1_across[j]] + [xs[j] for xs in s1_diagonal]
        theirs = [s1_across_cores[j]] + [xs[j] for xs in s1_diagonal_cores]
        made = score("score3", sizes, place, rows, with_cores(ours, theirs), last, direct=True)
        advance(made[0])
        parts.append([made[0]] + [from_layer(made[r], r, f"last{j}") for r in range(1, layers)])
    while any(part[0].shape[0] > 1 for part in parts):
        advance(last)
    return finish(sizes, place, parts, total)


def solution(mesh):
    groups, ex, layers = (mesh.shape[a] for a in ("groups", "ex", "layer"))
    in_specs = (P(None, "layer", "ex"), P("layer", "ex", None), P(("groups", "ex"), "layer", None))
    out_specs = P(("groups", "ex", "layer"), None)
    return jax.shard_map(
        functools.partial(shards, groups, ex, layers),
        mesh=mesh,
        in_specs=in_specs,
        out_specs=out_specs,
        check_vma=False,
    )
```

time: 80.2 us -> 80.6 us (level)
  local copies, waits for them, and re-layouts: 0.09 us -> 10 us
  Pallas kernels: 31.8 us -> 23 us
  starting transfers between devices: 31 us -> 27.7 us
  waiting for transfers between devices: 16.9 us -> 19.4 us
    unnamed x0 -> x12, local copies, waits for them, and re-layouts: none -> 10 us
    pallas_call x13 -> x12, Pallas kernels: 24.4 us -> 19.6 us  [the longest x4 11.8 us: score(): pl.pallas_call(functools.partial(score_kernel, sizes, direct), out_shape=...]
    pallas_call x2 -> x1, Pallas kernels: 7.38 us -> 3.39 us  [load(): pl.pallas_call(load_kernel, out_shape=pltpu.VMEM(source.shape, BF16), in_...]
    ppermute x28 -> x29, starting transfers between devices: 31 us -> 27.7 us  [permute(): return lax.ppermute(x, axis, perm)]
    ppermute x28 -> x29, waiting for transfers between devices: 16.9 us -> 19.4 us  [permute(): return lax.ppermute(x, axis, perm)]
  transfers between devices with their start and end apart: 28 -> 29, of which waited for: 7 -> 10; matrix products, arithmetic and copies ran while one was open for 0% -> 0% of each run, Pallas kernels for 36% -> 26%
where the time goes in v8:
time: 80.6 us; the launch traced here: 80.3 us
  starting transfers between devices  27.7 us (34%)
  Pallas kernels  23 us (29%)
  waiting for transfers between devices  19.4 us (24%)
  local copies, waits for them, and re-layouts  10 us (12%)
    ppermute x29, starting transfers between devices, permute(): return lax.ppermute(x, axis, perm)  27.7 us
    ppermute x29, waiting for transfers between devices, permute(): return lax.ppermute(x, axis, perm)  19.4 us
    pallas_call x4, Pallas kernels, score(): pl.pallas_call(functools.partial(score_kernel, sizes, direct), out_shape=...  11.8 us
    unnamed x12, local copies, waits for them, and re-layouts  10 us
    pallas_call x2, Pallas kernels, condition(): pl.pallas_call(functools.partial(condition_kernel, sizes), out_shape=pltp...  4.85 us
    pallas_call x1, Pallas kernels, load(): pl.pallas_call(load_kernel, out_shape=pltpu.VMEM(source.shape, BF16), in_...  3.39 us
    pallas_call x2, Pallas kernels, take(): pl.pallas_call(functools.partial(take_kernel, chunk), out_shape=pltpu.VME...  1.92 us
  transfers between devices with their start and end apart: 29, of which 10 were waited for; matrix products, arithmetic and copies ran while one was open for 0% of the time, Pallas kernels for 26%

profile of v8, /device:TPU:0, one launch (start us, length us, event | category | flops | bytes accessed | tf_op | source)
XLA Modules:
  0.0 80.3 jit_solution(14033763138437838324)
XLA Ops:
  0.0 1.0 %take.2.after.refs_4_ = bf16[128,1024]{1,0:T(8,128)(2,1)S(1)} custom-call(s32[1]{0:T(128)} %bitcast.at_group.after.refs_0_, bf16[512,1024]{1,0:T(8,128)(2,1)} %bitcast.13, s32[1]{0:T(128)} %bitcast.at_group.after.refs_0_), custom_call_target="tpu_custom_call" | custom-call | tf_op jit(solution)/shard_map/take/pallas_call | solution.py:58
  1.0 3.0 %collective-permute-start.1 = (bf16[128,1024]{1,0:T(8,128)(2,1)S(1)}, bf16[128,1024]{1,0:T(8,128)(2,1)S(1)}, u32[]{:S(2)}, u32[]{:S(2)}) collective-permute-start(bf16[128,1024]{1,0:T(8,128)(2,1)S(1)} %take.2.after.refs_4_), channel_id=1, source_target_pairs={{0,8},{4,12},{8,0},{12,4},{1,9},{5,13},{9,1},{13,5},{2,10},{6,14},... | collective-permute-start | bytes 786440 | tf_op jit(solution)/shard_map/q0_from_chip/ppermute | solution.py:185
  4.0 3.4 %load.1.after.refs_3_ = bf16[1024,4096]{1,0:T(8,128)(2,1)S(1)} custom-call(bf16[1024,4096]{1,0:T(8,128)(2,1)} %bitcast.12, bf16[128,1024]{1,0:T(8,128)(2,1)S(1)} %take.2.after.refs_4_), custom_call_target="tpu_custom_call" | custom-call | tf_op jit(solution)/shard_map/load/pallas_call | solution.py:38
  7.4 1.0 %take.3.refs_8_.refs_4_ = bf16[128,1024]{1,0:T(8,128)(2,1)S(1)} custom-call(s32[1]{0:T(128)} %bitcast.at_group.after.refs_0_, bf16[512,1024]{1,0:T(8,128)(2,1)} %bitcast.14, bf16[1024,4096]{1,0:T(8,128)(2,1)S(1)} %load.1.after.refs_3_), custom_call_target="tpu_custom_call" | custom-call | tf_op jit(solution)/shard_map/take/pallas_call | solution.py:58
  8.4 3.3 %copy-done = bf16[1024,4096]{1,0:T(8,128)(2,1)} copy-done((bf16[1024,4096]{1,0:T(8,128)(2,1)}, bf16[1024,4096]{1,0:T(8,128)(2,1)S(1)}, u32[]{:S(2)}) %copy-start) | copy-done | bytes 8388632
  11.7 0.0 collective-permute-done.1.refs_6_
  11.7 0.5 collective-permute-start.2
  12.2 0.1 collective-permute-start.7
  12.2 0.0 collective-permute-done.refs_5_
  12.2 1.1 %collective-permute-done.2.refs_7_ = bf16[128,1024]{1,0:T(8,128)(2,1)S(1)} collective-permute-done((bf16[128,1024]{1,0:T(8,128)(2,1)S(1)}, bf16[128,1024]{1,0:T(8,128)(2,1)S(1)}, u32[]{:S(2)}, u32[]{:S(2)}) %collective-permute-start.2) | collective-permute-done | bytes 262176 | tf_op jit(solution)/shard_map/q0_there_from_core/ppermute | solution.py:185
  13.3 3.4 %copy-done.1 = bf16[1024,4096]{1,0:T(8,128)(2,1)S(1)} copy-done((bf16[1024,4096]{1,0:T(8,128)(2,1)S(1)}, bf16[1024,4096]{1,0:T(8,128)(2,1)}, u32[]{:S(2)}) %copy-start.1) | copy-done | bytes 8388632
  16.7 2.4 %condition.2.refs_4_ = bf16[1024,128]{1,0:T(8,128)(2,1)S(1)} custom-call(s32[1]{0:T(128)} %bitcast.at_group.after.refs_0_, s32[1]{0:T(128)} %bitcast.1.refs_1_, s32[1]{0:T(128)} %bitcast.2.refs_2_, bf16[1024,4096]{1,0:T(8,128)(2,1)S(1)} %copy-done.1, bf16[128,1024]{1,0:T(8,128)(2,1)S(1)} %take.2.after.refs_4_, ...), custom_call_target="tpu_custom_call" | custom-call | tf_op jit(solution)/shard_map/condition/pallas_call | solution.py:83
  19.1 0.0 slice-start.2
  19.2 0.9 %collective-permute-start.4 = (bf16[1024,128]{1,0:T(8,128)(2,1)S(1)}, bf16[1024,128]{1,0:T(8,128)(2,1)S(1)}, u32[]{:S(2)}, u32[]{:S(2)}) collective-permute-start(bf16[1024,128]{1,0:T(8,128)(2,1)S(1)} %condition.2.refs_4_), channel_id=1, source_target_pairs={{0,8},{4,12},{8,0},{12,4},{1,9},{5,13},{9,1},{13,5},{2,10},{6,14},... | collective-permute-start | bytes 786440 | tf_op jit(solution)/shard_map/s0_from_chip/ppermute | solution.py:185
  20.1 0.3 collective-permute-done.7.refs_6_
  20.4 0.2 collective-permute-start.8
  20.6 1.5 %collective-permute-start.10 = (bf16[1024,128]{1,0:T(8,128)(2,1)S(1)}, bf16[1024,128]{1,0:T(8,128)(2,1)S(1)}, u32[]{:S(2)}, u32[]{:S(2)}) collective-permute-start(bf16[1024,128]{1,0:T(8,128)(2,1)S(1)} %condition.2.refs_4_), channel_id=1, source_target_pairs={{0,16},{16,0},{1,17},{17,1},{2,18},{18,2},{3,19},{19,3},{4,20},{20... | collective-permute-start | bytes 786440 | tf_op jit(solution)/shard_map/s0_from_group/ppermute | solution.py:185
  22.1 5.7 %collective-permute-done.4.refs_8_.refs_6_ = bf16[1024,128]{1,0:T(8,128)(2,1)S(1)} collective-permute-done((bf16[1024,128]{1,0:T(8,128)(2,1)S(1)}, bf16[1024,128]{1,0:T(8,128)(2,1)S(1)}, u32[]{:S(2)}, u32[]{:S(2)}) %collective-permute-start.4) | collective-permute-done | bytes 262176 | tf_op jit(solution)/shard_map/s0_from_chip/ppermute | solution.py:185
  27.8 1.5 %collective-permute-start.12 = (bf16[1024,128]{1,0:T(8,128)(2,1)S(1)}, bf16[1024,128]{1,0:T(8,128)(2,1)S(1)}, u32[]{:S(2)}, u32[]{:S(2)}) collective-permute-start(bf16[1024,128]{1,0:T(8,128)(2,1)S(1)} %collective-permute-done.4.refs_8_.refs_6_), channel_id=1, source_target_pairs={{0,16},{16,0},{1,17},{17,1},{2,18},{18,2},{3,19},{19,3},{4,20},{20... | collective-permute-start | bytes 786440 | tf_op jit(solution)/shard_map/s0_there_from_group/ppermute | solution.py:185
  29.3 3.4 %copy-done.2 = bf16[1024,4096]{1,0:T(8,128)(2,1)S(1)} copy-done((bf16[1024,4096]{1,0:T(8,128)(2,1)S(1)}, bf16[1024,4096]{1,0:T(8,128)(2,1)}, u32[]{:S(2)}) %copy-start.2) | copy-done | bytes 8388632
  32.7 2.4 %condition.3.refs_8_.refs_4_ = bf16[1024,128]{1,0:T(8,128)(2,1)S(1)} custom-call(s32[1]{0:T(128)} %bitcast.at_group.after.refs_0_, s32[1]{0:T(128)} %bitcast.1.refs_1_, s32[1]{0:T(128)} %bitcast.2.refs_2_, bf16[1024,4096]{1,0:T(8,128)(2,1)S(1)} %copy-done.2, bf16[128,1024]{1,0:T(8,128)(2,1)S(1)} %take.3.refs_8_.refs_4_, ...), custom_call_target="tpu_custom_call" | custom-call | tf_op jit(solution)/shard_map/condition/pallas_call | solution.py:83
  35.1 0.6 collective-permute-start.17
  35.8 2.9 %score0.1 = (bf16[2,320,128]{2,1,0:T(8,128)(2,1)S(1)}, f32[2,320,128]{2,1,0:T(8,128)S(1)}) custom-call(s32[1]{0:T(128)} %bitcast.at_group.after.refs_0_, s32[1]{0:T(128)} %bitcast.1.refs_1_, s32[1]{0:T(128)} %bitcast.2.refs_2_, bf16[1280,4096]{1,0:T(8,128)(2,1)S(1)} %bitcast.8, bf16[1024,128]{1,0:T(8,128)(2,1)S(1)} %condition.2.refs_4_, ...), custom_call_target="tpu_custom_call" | custom-call | tf_op jit(solution)/shard_map/score0/pallas_call | solution.py:119
  38.7 0.6 collective-permute-start.13
  39.3 0.1 collective-permute-start.16
  39.4 1.6 %collective-permute-start.9 = (bf16[2,320,128]{2,1,0:T(8,128)(2,1)S(1)}, bf16[2,320,128]{2,1,0:T(8,128)(2,1)S(1)}, u32[]{:S(2)}, u32[]{:S(2)}) collective-permute-start(bf16[2,320,128]{2,1,0:T(8,128)(2,1)S(1)} %get-tuple-element.33), channel_id=1, source_target_pairs={{0,1},{1,0},{2,3},{3,2},{4,5},{5,4},{6,7},{7,6},{8,9},{9,8},{10,11... | collective-permute-start | bytes 491528 | tf_op jit(solution)/shard_map/sum0_from_layer_1/ppermute | solution.py:185
  40.9 2.7 %collective-permute-done.17.refs_6_ = bf16[1024,128]{1,0:T(8,128)(2,1)S(1)} collective-permute-done((bf16[1024,128]{1,0:T(8,128)(2,1)S(1)}, bf16[1024,128]{1,0:T(8,128)(2,1)S(1)}, u32[]{:S(2)}, u32[]{:S(2)}) %collective-permute-start.17) | collective-permute-done | bytes 262176 | tf_op jit(solution)/shard_map/s1_from_chip/ppermute | solution.py:185
  43.6 0.5 collective-permute-start.23
  44.2 1.5 %collective-permute-start.21 = (bf16[1024,128]{1,0:T(8,128)(2,1)S(1)}, bf16[1024,128]{1,0:T(8,128)(2,1)S(1)}, u32[]{:S(2)}, u32[]{:S(2)}) collective-permute-start(bf16[1024,128]{1,0:T(8,128)(2,1)S(1)} %condition.3.refs_8_.refs_4_), channel_id=1, source_target_pairs={{0,16},{16,0},{1,17},{17,1},{2,18},{18,2},{3,19},{19,3},{4,20},{20... | collective-permute-start | bytes 786440 | tf_op jit(solution)/shard_map/s1_from_group/ppermute | solution.py:185
  45.7 2.9 %score1.1 = (bf16[2,320,128]{2,1,0:T(8,128)(2,1)S(1)}, f32[2,320,128]{2,1,0:T(8,128)S(1)}) custom-call(s32[1]{0:T(128)} %bitcast.at_group.after.refs_0_, s32[1]{0:T(128)} %bitcast.1.refs_1_, s32[1]{0:T(128)} %bitcast.2.refs_2_, bf16[1280,4096]{1,0:T(8,128)(2,1)S(1)} %bitcast.9, bf16[1024,128]{1,0:T(8,128)(2,1)S(1)} %collective-permute-done.10.refs_4_, ...), custom_call_target="tpu_custom_call" | custom-call | tf_op jit(solution)/shard_map/score1/pallas_call | solution.py:119
  48.6 1.6 %collective-permute-start.15 = (bf16[2,320,128]{2,1,0:T(8,128)(2,1)S(1)}, bf16[2,320,128]{2,1,0:T(8,128)(2,1)S(1)}, u32[]{:S(2)}, u32[]{:S(2)}) collective-permute-start(bf16[2,320,128]{2,1,0:T(8,128)(2,1)S(1)} %get-tuple-element.39), channel_id=1, source_target_pairs={{0,1},{1,0},{2,3},{3,2},{4,5},{5,4},{6,7},{7,6},{8,9},{9,8},{10,11... | collective-permute-start | bytes 491528 | tf_op jit(solution)/shard_map/sum1_from_layer_1/ppermute | solution.py:185
  50.3 2.7 %collective-permute-start.14 = (bf16[1,320,128]{2,1,0:T(8,128)(2,1)S(1)}, bf16[1,320,128]{2,1,0:T(8,128)(2,1)S(1)}, u32[]{:S(2)}, u32[]{:S(2)}) collective-permute-start(bf16[1,320,128]{2,1,0:T(8,128)(2,1)S(1)} %get-tuple-element.38), channel_id=1, source_target_pairs={{0,2},{1,3},{2,0},{3,1},{4,6},{5,7},{6,4},{7,5},{8,10},{9,11},{10,... | collective-permute-start | bytes 245768 | tf_op jit(solution)/shard_map/sum0_from_layer_2/ppermute | solution.py:185
  53.0 2.9 %score2.1 = (bf16[2,320,128]{2,1,0:T(8,128)(2,1)S(1)}, f32[2,320,128]{2,1,0:T(8,128)S(1)}) custom-call(s32[1]{0:T(128)} %bitcast.at_group.after.refs_0_, s32[1]{0:T(128)} %bitcast.1.refs_1_, s32[1]{0:T(128)} %bitcast.2.refs_2_, bf16[1280,4096]{1,0:T(8,128)(2,1)S(1)} %bitcast.10, bf16[1024,128]{1,0:T(8,128)(2,1)S(1)} %condition.3.refs_8_.refs_4_, ...), custom_call_target="tpu_custom_call" | custom-call | tf_op jit(solution)/shard_map/score2/pallas_call | solution.py:119
  55.9 0.6 collective-permute-done.15.got
  56.6 0.1 collective-permute-start.24
  56.6 1.3 %collective-permute-done.21.refs_4_ = bf16[1024,128]{1,0:T(8,128)(2,1)S(1)} collective-permute-done((bf16[1024,128]{1,0:T(8,128)(2,1)S(1)}, bf16[1024,128]{1,0:T(8,128)(2,1)S(1)}, u32[]{:S(2)}, u32[]{:S(2)}) %collective-permute-start.21) | collective-permute-done | bytes 262176 | tf_op jit(solution)/shard_map/s1_from_group/ppermute | solution.py:185
  58.0 1.7 %collective-permute-start.20 = (bf16[2,320,128]{2,1,0:T(8,128)(2,1)S(1)}, bf16[2,320,128]{2,1,0:T(8,128)(2,1)S(1)}, u32[]{:S(2)}, u32[]{:S(2)}) collective-permute-start(bf16[2,320,128]{2,1,0:T(8,128)(2,1)S(1)} %get-tuple-element.45), channel_id=1, source_target_pairs={{0,1},{1,0},{2,3},{3,2},{4,5},{5,4},{6,7},{7,6},{8,9},{9,8},{10,11... | collective-permute-start | bytes 491528 | tf_op jit(solution)/shard_map/sum2_from_layer_1/ppermute | solution.py:185
  59.7 2.4 %collective-permute-start.19 = (bf16[1,320,128]{2,1,0:T(8,128)(2,1)S(1)}, bf16[1,320,128]{2,1,0:T(8,128)(2,1)S(1)}, u32[]{:S(2)}, u32[]{:S(2)}) collective-permute-start(bf16[1,320,128]{2,1,0:T(8,128)(2,1)S(1)} %get-tuple-element.44), channel_id=1, source_target_pairs={{0,2},{1,3},{2,0},{3,1},{4,6},{5,7},{6,4},{7,5},{8,10},{9,11},{10,... | collective-permute-start | bytes 245768 | tf_op jit(solution)/shard_map/sum1_from_layer_2/ppermute | solution.py:185
  62.2 3.0 %score3.1 = (f32[1,320,128]{2,1,0:T(8,128)S(1)}, bf16[1,320,128]{2,1,0:T(8,128)(2,1)S(1)}, bf16[1,320,128]{2,1,0:T(8,128)(2,1)S(1)}, bf16[1,320,128]{2,1,0:T(8,128)(2,1)S(1)}) custom-call(s32[1]{0:T(128)} %bitcast.at_group.after.refs_0_, s32[1]{0:T(128)} %bitcast.1.refs_1_, s32[1]{0:T(128)} %bitcast.2.refs_2_, bf16[1280,4096]{1,0:T(8,128)(2,1)S(1)} %bitcast.11, ...), custom_call_target="tpu_custom_call" | custom-call | tf_op jit(solution)/shard_map/score3/pallas_call | solution.py:119
  65.1 1.2 %collective-permute-done.20.got = bf16[2,320,128]{2,1,0:T(8,128)(2,1)S(1)} collective-permute-done((bf16[2,320,128]{2,1,0:T(8,128)(2,1)S(1)}, bf16[2,320,128]{2,1,0:T(8,128)(2,1)S(1)}, u32[]{:S(2)}, u32[]{:S(2)}) %collective-permute-start.20) | collective-permute-done | bytes 163872 | tf_op jit(solution)/shard_map/sum2_from_layer_1/ppermute | solution.py:185
  66.4 1.7 %collective-permute-start.25 = (bf16[1,320,128]{2,1,0:T(8,128)(2,1)S(1)}, bf16[1,320,128]{2,1,0:T(8,128)(2,1)S(1)}, u32[]{:S(2)}, u32[]{:S(2)}) collective-permute-start(bf16[1,320,128]{2,1,0:T(8,128)(2,1)S(1)} %get-tuple-element.51), channel_id=1, source_target_pairs={{0,2},{1,3},{2,0},{3,1},{4,6},{5,7},{6,4},{7,5},{8,10},{9,11},{10,... | collective-permute-start | bytes 245768 | tf_op jit(solution)/shard_map/sum2_from_layer_2/ppermute | solution.py:185
  68.1 2.5 %collective-permute-start.26 = (bf16[1,320,128]{2,1,0:T(8,128)(2,1)S(1)}, bf16[1,320,128]{2,1,0:T(8,128)(2,1)S(1)}, u32[]{:S(2)}, u32[]{:S(2)}) collective-permute-start(bf16[1,320,128]{2,1,0:T(8,128)(2,1)S(1)} %get-tuple-element.52), channel_id=1, source_target_pairs={{0,1},{1,0},{2,3},{3,2},{4,5},{5,4},{6,7},{7,6},{8,9},{9,8},{10,11... | collective-permute-start | bytes 245768 | tf_op jit(solution)/shard_map/last0_from_layer_1/ppermute | solution.py:185
  70.6 0.1 collective-permute-start.27
  70.7 2.3 %collective-permute-start.28 = (bf16[1,320,128]{2,1,0:T(8,128)(2,1)S(1)}, bf16[1,320,128]{2,1,0:T(8,128)(2,1)S(1)}, u32[]{:S(2)}, u32[]{:S(2)}) collective-permute-start(bf16[1,320,128]{2,1,0:T(8,128)(2,1)S(1)} %get-tuple-element.54), channel_id=1, source_target_pairs={{0,3},{1,2},{2,1},{3,0},{4,7},{5,6},{6,5},{7,4},{8,11},{9,10},{10,... | collective-permute-start | bytes 245768 | tf_op jit(solution)/shard_map/last0_from_layer_3/ppermute | solution.py:185
  73.0 0.2 collective-permute-done.25.refs_8_
  73.2 0.6 collective-permute-done.26.refs_10_
  73.8 5.7 %collective-permute-done.27.refs_11_ = bf16[1,320,128]{2,1,0:T(8,128)(2,1)S(1)} collective-permute-done((bf16[1,320,128]{2,1,0:T(8,128)(2,1)S(1)}, bf16[1,320,128]{2,1,0:T(8,128)(2,1)S(1)}, u32[]{:S(2)}, u32[]{:S(2)}) %collective-permute-start.27) | collective-permute-done | bytes 81952 | tf_op jit(solution)/shard_map/last0_from_layer_2/ppermute | solution.py:185
  79.4 0.9 %finish.1 = f32[320,512]{1,0:T(8,128)} custom-call(s32[1]{0:T(128)} %bitcast.at_group.after.refs_0_, s32[1]{0:T(128)} %bitcast.1.refs_1_, s32[1]{0:T(128)} %bitcast.2.refs_2_, f32[1,320,128]{2,1,0:T(8,128)S(1)} %get-tuple-element.37.refs_8_.refs_3_, bf16[1,320,128]{2,1,0:T(8,128)(2,1)S(1)} %collective-permute-done.14.refs_4_, ...), custom_call_target="tpu_custom_call" | custom-call | tf_op jit(solution)/shard_map/finish/pallas_call | solution.py:167
  (36 shorter events, 0.2 us)
Async XLA Ops:
  1.0 10.7 %collective-permute-start.1 = (bf16[128,1024]{1,0:T(8,128)(2,1)S(1)}, bf16[128,1024]{1,0:T(8,128)(2,1)S(1)}, u32[]{:S(2)}, u32[]{:S(2)}) collective-permute-start(bf16[128,1024]{1,0:T(8,128)(2,1)S(1)} %take.2.after.refs_4_), channel_id=1, source_target_pairs={{0,8},{4,12},{8,0},{12,4},{1,9},{5,13},{9,1},{13,5},{2,10},{6,14},... | collective-permute-start | bytes 786440 | tf_op jit(solution)/shard_map/q0_from_chip/ppermute | solution.py:185
  4.0 8.2 %collective-permute-start = (bf16[128,1024]{1,0:T(8,128)(2,1)S(1)}, bf16[128,1024]{1,0:T(8,128)(2,1)S(1)}, u32[]{:S(2)}, u32[]{:S(2)}) collective-permute-start(bf16[128,1024]{1,0:T(8,128)(2,1)S(1)} %take.2.after.refs_4_), channel_id=1, source_target_pairs={{0,4},{4,0},{8,12},{12,8},{1,5},{5,1},{9,13},{13,9},{2,6},{6,2},{1... | collective-permute-start | bytes 786440 | tf_op jit(solution)/shard_map/q0_from_core/ppermute | solution.py:185
  8.4 3.3 %copy-start = (bf16[1024,4096]{1,0:T(8,128)(2,1)}, bf16[1024,4096]{1,0:T(8,128)(2,1)S(1)}, u32[]{:S(2)}) copy-start(bf16[1024,4096]{1,0:T(8,128)(2,1)S(1)} %load.1.after.refs_3_) | copy-start | bytes 25165828
  11.7 1.7 %collective-permute-start.2 = (bf16[128,1024]{1,0:T(8,128)(2,1)S(1)}, bf16[128,1024]{1,0:T(8,128)(2,1)S(1)}, u32[]{:S(2)}, u32[]{:S(2)}) collective-permute-start(bf16[128,1024]{1,0:T(8,128)(2,1)S(1)} %collective-permute-done.1.refs_6_), channel_id=1, source_target_pairs={{0,4},{4,0},{8,12},{12,8},{1,5},{5,1},{9,13},{13,9},{2,6},{6,2},{1... | collective-permute-start | bytes 786440 | tf_op jit(solution)/shard_map/q0_there_from_core/ppermute | solution.py:185
  12.2 8.2 %collective-permute-start.7 = (bf16[128,1024]{1,0:T(8,128)(2,1)S(1)}, bf16[128,1024]{1,0:T(8,128)(2,1)S(1)}, u32[]{:S(2)}, u32[]{:S(2)}) collective-permute-start(bf16[128,1024]{1,0:T(8,128)(2,1)S(1)} %take.3.refs_8_.refs_4_), channel_id=1, source_target_pairs={{0,8},{4,12},{8,0},{12,4},{1,9},{5,13},{9,1},{13,5},{2,10},{6,14},... | collective-permute-start | bytes 786440 | tf_op jit(solution)/shard_map/q1_from_chip/ppermute | solution.py:185
  13.3 3.4 %copy-start.1 = (bf16[1024,4096]{1,0:T(8,128)(2,1)S(1)}, bf16[1024,4096]{1,0:T(8,128)(2,1)}, u32[]{:S(2)}) copy-start(bf16[1024,4096]{1,0:T(8,128)(2,1)} %copy-done) | copy-start | bytes 25165828
  16.7 19.0 %slice-start = ((s8[10485760]{0:T(1024)(128)(4,1)}), s8[4194304]{0:T(1024)(128)(4,1)S(1)}, s32[]{:S(2)}) async-start(s8[10485760]{0:T(1024)(128)(4,1)} %bitcast.6), calls=%async_computation | async-start | bytes 8388608
  16.7 19.0 %slice-start.1 = ((s8[10485760]{0:T(1024)(128)(4,1)}), s8[4194304]{0:T(1024)(128)(4,1)S(1)}, s32[]{:S(2)}) async-start(s8[10485760]{0:T(1024)(128)(4,1)} %bitcast.6), calls=%async_computation.1 | async-start | bytes 8388608
  19.1 16.6 %slice-start.2 = ((s8[10485760]{0:T(1024)(128)(4,1)}), s8[2097152]{0:T(1024)(128)(4,1)S(1)}, s32[]{:S(2)}) async-start(s8[10485760]{0:T(1024)(128)(4,1)} %bitcast.6), calls=%async_computation.2 | async-start | bytes 4194304
  19.2 8.7 %collective-permute-start.4 = (bf16[1024,128]{1,0:T(8,128)(2,1)S(1)}, bf16[1024,128]{1,0:T(8,128)(2,1)S(1)}, u32[]{:S(2)}, u32[]{:S(2)}) collective-permute-start(bf16[1024,128]{1,0:T(8,128)(2,1)S(1)} %condition.2.refs_4_), channel_id=1, source_target_pairs={{0,8},{4,12},{8,0},{12,4},{1,9},{5,13},{9,1},{13,5},{2,10},{6,14},... | collective-permute-start | bytes 786440 | tf_op jit(solution)/shard_map/s0_from_chip/ppermute | solution.py:185
  20.1 7.7 %collective-permute-start.6 = (bf16[128,1024]{1,0:T(8,128)(2,1)S(1)}, bf16[128,1024]{1,0:T(8,128)(2,1)S(1)}, u32[]{:S(2)}, u32[]{:S(2)}) collective-permute-start(bf16[128,1024]{1,0:T(8,128)(2,1)S(1)} %take.3.refs_8_.refs_4_), channel_id=1, source_target_pairs={{0,4},{4,0},{8,12},{12,8},{1,5},{5,1},{9,13},{13,9},{2,6},{6,2},{1... | collective-permute-start | bytes 786440 | tf_op jit(solution)/shard_map/q1_from_core/ppermute | solution.py:185
  20.4 8.9 %collective-permute-start.8 = (bf16[128,1024]{1,0:T(8,128)(2,1)S(1)}, bf16[128,1024]{1,0:T(8,128)(2,1)S(1)}, u32[]{:S(2)}, u32[]{:S(2)}) collective-permute-start(bf16[128,1024]{1,0:T(8,128)(2,1)S(1)} %collective-permute-done.7.refs_6_), channel_id=1, source_target_pairs={{0,4},{4,0},{8,12},{12,8},{1,5},{5,1},{9,13},{13,9},{2,6},{6,2},{1... | collective-permute-start | bytes 786440 | tf_op jit(solution)/shard_map/q1_there_from_core/ppermute | solution.py:185
  20.6 15.1 %collective-permute-start.10 = (bf16[1024,128]{1,0:T(8,128)(2,1)S(1)}, bf16[1024,128]{1,0:T(8,128)(2,1)S(1)}, u32[]{:S(2)}, u32[]{:S(2)}) collective-permute-start(bf16[1024,128]{1,0:T(8,128)(2,1)S(1)} %condition.2.refs_4_), channel_id=1, source_target_pairs={{0,16},{16,0},{1,17},{17,1},{2,18},{18,2},{3,19},{19,3},{4,20},{20... | collective-permute-start | bytes 786440 | tf_op jit(solution)/shard_map/s0_from_group/ppermute | solution.py:185
  22.1 13.6 %collective-permute-start.3 = (bf16[1024,128]{1,0:T(8,128)(2,1)S(1)}, bf16[1024,128]{1,0:T(8,128)(2,1)S(1)}, u32[]{:S(2)}, u32[]{:S(2)}) collective-permute-start(bf16[1024,128]{1,0:T(8,128)(2,1)S(1)} %condition.2.refs_4_), channel_id=1, source_target_pairs={{0,4},{4,0},{8,12},{12,8},{1,5},{5,1},{9,13},{13,9},{2,6},{6,2},{1... | collective-permute-start | bytes 786440 | tf_op jit(solution)/shard_map/s0_from_core/ppermute | solution.py:185
  27.8 7.9 %collective-permute-start.5 = (bf16[1024,128]{1,0:T(8,128)(2,1)S(1)}, bf16[1024,128]{1,0:T(8,128)(2,1)S(1)}, u32[]{:S(2)}, u32[]{:S(2)}) collective-permute-start(bf16[1024,128]{1,0:T(8,128)(2,1)S(1)} %collective-permute-done.4.refs_8_.refs_6_), channel_id=1, source_target_pairs={{0,4},{4,0},{8,12},{12,8},{1,5},{5,1},{9,13},{13,9},{2,6},{6,2},{1... | collective-permute-start | bytes 786440 | tf_op jit(solution)/shard_map/s0_there_from_core/ppermute | solution.py:185
  27.8 10.9 %collective-permute-start.12 = (bf16[1024,128]{1,0:T(8,128)(2,1)S(1)}, bf16[1024,128]{1,0:T(8,128)(2,1)S(1)}, u32[]{:S(2)}, u32[]{:S(2)}) collective-permute-start(bf16[1024,128]{1,0:T(8,128)(2,1)S(1)} %collective-permute-done.4.refs_8_.refs_6_), channel_id=1, source_target_pairs={{0,16},{16,0},{1,17},{17,1},{2,18},{18,2},{3,19},{19,3},{4,20},{20... | collective-permute-start | bytes 786440 | tf_op jit(solution)/shard_map/s0_there_from_group/ppermute | solution.py:185
  29.3 3.4 %copy-start.2 = (bf16[1024,4096]{1,0:T(8,128)(2,1)S(1)}, bf16[1024,4096]{1,0:T(8,128)(2,1)}, u32[]{:S(2)}) copy-start(bf16[1024,4096]{1,0:T(8,128)(2,1)} %copy-done) | copy-start | bytes 25165828
  35.1 8.5 %collective-permute-start.17 = (bf16[1024,128]{1,0:T(8,128)(2,1)S(1)}, bf16[1024,128]{1,0:T(8,128)(2,1)S(1)}, u32[]{:S(2)}, u32[]{:S(2)}) collective-permute-start(bf16[1024,128]{1,0:T(8,128)(2,1)S(1)} %condition.3.refs_8_.refs_4_), channel_id=1, source_target_pairs={{0,8},{4,12},{8,0},{12,4},{1,9},{5,13},{9,1},{13,5},{2,10},{6,14},... | collective-permute-start | bytes 786440 | tf_op jit(solution)/shard_map/s1_from_chip/ppermute | solution.py:185
  35.7 7.9 %collective-permute-start.11 = (bf16[1024,128]{1,0:T(8,128)(2,1)S(1)}, bf16[1024,128]{1,0:T(8,128)(2,1)S(1)}, u32[]{:S(2)}, u32[]{:S(2)}) collective-permute-start(bf16[1024,128]{1,0:T(8,128)(2,1)S(1)} %collective-permute-done.10.refs_4_), channel_id=1, source_target_pairs={{0,4},{4,0},{8,12},{12,8},{1,5},{5,1},{9,13},{13,9},{2,6},{6,2},{1... | collective-permute-start | bytes 786440 | tf_op jit(solution)/shard_map/s0_across_from_core/ppermute | solution.py:185
  38.7 5.4 %collective-permute-start.13 = (bf16[1024,128]{1,0:T(8,128)(2,1)S(1)}, bf16[1024,128]{1,0:T(8,128)(2,1)S(1)}, u32[]{:S(2)}, u32[]{:S(2)}) collective-permute-start(bf16[1024,128]{1,0:T(8,128)(2,1)S(1)} %collective-permute-done.12.refs_6_), channel_id=1, source_target_pairs={{0,4},{4,0},{8,12},{12,8},{1,5},{5,1},{9,13},{13,9},{2,6},{6,2},{1... | collective-permute-start | bytes 786440 | tf_op jit(solution)/shard_map/s0_diagonal_from_core/ppermute | solution.py:185
  39.3 11.0 %collective-permute-start.16 = (bf16[1024,128]{1,0:T(8,128)(2,1)S(1)}, bf16[1024,128]{1,0:T(8,128)(2,1)S(1)}, u32[]{:S(2)}, u32[]{:S(2)}) collective-permute-start(bf16[1024,128]{1,0:T(8,128)(2,1)S(1)} %condition.3.refs_8_.refs_4_), channel_id=1, source_target_pairs={{0,4},{4,0},{8,12},{12,8},{1,5},{5,1},{9,13},{13,9},{2,6},{6,2},{1... | collective-permute-start | bytes 786440 | tf_op jit(solution)/shard_map/s1_from_core/ppermute | solution.py:185
  39.4 9.3 %collective-permute-start.9 = (bf16[2,320,128]{2,1,0:T(8,128)(2,1)S(1)}, bf16[2,320,128]{2,1,0:T(8,128)(2,1)S(1)}, u32[]{:S(2)}, u32[]{:S(2)}) collective-permute-start(bf16[2,320,128]{2,1,0:T(8,128)(2,1)S(1)} %get-tuple-element.33), channel_id=1, source_target_pairs={{0,1},{1,0},{2,3},{3,2},{4,5},{5,4},{6,7},{7,6},{8,9},{9,8},{10,11... | collective-permute-start | bytes 491528 | tf_op jit(solution)/shard_map/sum0_from_layer_1/ppermute | solution.py:185
  43.6 9.3 %collective-permute-start.18 = (bf16[1024,128]{1,0:T(8,128)(2,1)S(1)}, bf16[1024,128]{1,0:T(8,128)(2,1)S(1)}, u32[]{:S(2)}, u32[]{:S(2)}) collective-permute-start(bf16[1024,128]{1,0:T(8,128)(2,1)S(1)} %collective-permute-done.17.refs_6_), channel_id=1, source_target_pairs={{0,4},{4,0},{8,12},{12,8},{1,5},{5,1},{9,13},{13,9},{2,6},{6,2},{1... | collective-permute-start | bytes 786440 | tf_op jit(solution)/shard_map/s1_there_from_core/ppermute | solution.py:185
  43.6 12.9 %collective-permute-start.23 = (bf16[1024,128]{1,0:T(8,128)(2,1)S(1)}, bf16[1024,128]{1,0:T(8,128)(2,1)S(1)}, u32[]{:S(2)}, u32[]{:S(2)}) collective-permute-start(bf16[1024,128]{1,0:T(8,128)(2,1)S(1)} %collective-permute-done.17.refs_6_), channel_id=1, source_target_pairs={{0,16},{16,0},{1,17},{17,1},{2,18},{18,2},{3,19},{19,3},{4,20},{20... | collective-permute-start | bytes 786440 | tf_op jit(solution)/shard_map/s1_there_from_group/ppermute | solution.py:185
  44.2 13.8 %collective-permute-start.21 = (bf16[1024,128]{1,0:T(8,128)(2,1)S(1)}, bf16[1024,128]{1,0:T(8,128)(2,1)S(1)}, u32[]{:S(2)}, u32[]{:S(2)}) collective-permute-start(bf16[1024,128]{1,0:T(8,128)(2,1)S(1)} %condition.3.refs_8_.refs_4_), channel_id=1, source_target_pairs={{0,16},{16,0},{1,17},{17,1},{2,18},{18,2},{3,19},{19,3},{4,20},{20... | collective-permute-start | bytes 786440 | tf_op jit(solution)/shard_map/s1_from_group/ppermute | solution.py:185
  48.6 7.9 %collective-permute-start.15 = (bf16[2,320,128]{2,1,0:T(8,128)(2,1)S(1)}, bf16[2,320,128]{2,1,0:T(8,128)(2,1)S(1)}, u32[]{:S(2)}, u32[]{:S(2)}) collective-permute-start(bf16[2,320,128]{2,1,0:T(8,128)(2,1)S(1)} %get-tuple-element.39), channel_id=1, source_target_pairs={{0,1},{1,0},{2,3},{3,2},{4,5},{5,4},{6,7},{7,6},{8,9},{9,8},{10,11... | collective-permute-start | bytes 491528 | tf_op jit(solution)/shard_map/sum1_from_layer_1/ppermute | solution.py:185
  50.3 5.6 %collective-permute-start.14 = (bf16[1,320,128]{2,1,0:T(8,128)(2,1)S(1)}, bf16[1,320,128]{2,1,0:T(8,128)(2,1)S(1)}, u32[]{:S(2)}, u32[]{:S(2)}) collective-permute-start(bf16[1,320,128]{2,1,0:T(8,128)(2,1)S(1)} %get-tuple-element.38), channel_id=1, source_target_pairs={{0,2},{1,3},{2,0},{3,1},{4,6},{5,7},{6,4},{7,5},{8,10},{9,11},{10,... | collective-permute-start | bytes 245768 | tf_op jit(solution)/shard_map/sum0_from_layer_2/ppermute | solution.py:185
  56.6 5.6 %collective-permute-start.24 = (bf16[1024,128]{1,0:T(8,128)(2,1)S(1)}, bf16[1024,128]{1,0:T(8,128)(2,1)S(1)}, u32[]{:S(2)}, u32[]{:S(2)}) collective-permute-start(bf16[1024,128]{1,0:T(8,128)(2,1)S(1)} %collective-permute-done.23.refs_6_), channel_id=1, source_target_pairs={{0,4},{4,0},{8,12},{12,8},{1,5},{5,1},{9,13},{13,9},{2,6},{6,2},{1... | collective-permute-start | bytes 786440 | tf_op jit(solution)/shard_map/s1_diagonal_from_core/ppermute | solution.py:185
  58.0 4.2 %collective-permute-start.22 = (bf16[1024,128]{1,0:T(8,128)(2,1)S(1)}, bf16[1024,128]{1,0:T(8,128)(2,1)S(1)}, u32[]{:S(2)}, u32[]{:S(2)}) collective-permute-start(bf16[1024,128]{1,0:T(8,128)(2,1)S(1)} %collective-permute-done.21.refs_4_), channel_id=1, source_target_pairs={{0,4},{4,0},{8,12},{12,8},{1,5},{5,1},{9,13},{13,9},{2,6},{6,2},{1... | collective-permute-start | bytes 786440 | tf_op jit(solution)/shard_map/s1_across_from_core/ppermute | solution.py:185
  58.0 8.4 %collective-permute-start.20 = (bf16[2,320,128]{2,1,0:T(8,128)(2,1)S(1)}, bf16[2,320,128]{2,1,0:T(8,128)(2,1)S(1)}, u32[]{:S(2)}, u32[]{:S(2)}) collective-permute-start(bf16[2,320,128]{2,1,0:T(8,128)(2,1)S(1)} %get-tuple-element.45), channel_id=1, source_target_pairs={{0,1},{1,0},{2,3},{3,2},{4,5},{5,4},{6,7},{7,6},{8,9},{9,8},{10,11... | collective-permute-start | bytes 491528 | tf_op jit(solution)/shard_map/sum2_from_layer_1/ppermute | solution.py:185
  59.7 13.3 %collective-permute-start.19 = (bf16[1,320,128]{2,1,0:T(8,128)(2,1)S(1)}, bf16[1,320,128]{2,1,0:T(8,128)(2,1)S(1)}, u32[]{:S(2)}, u32[]{:S(2)}) collective-permute-start(bf16[1,320,128]{2,1,0:T(8,128)(2,1)S(1)} %get-tuple-element.44), channel_id=1, source_target_pairs={{0,2},{1,3},{2,0},{3,1},{4,6},{5,7},{6,4},{7,5},{8,10},{9,11},{10,... | collective-permute-start | bytes 245768 | tf_op jit(solution)/shard_map/sum1_from_layer_2/ppermute | solution.py:185
  66.4 6.8 %collective-permute-start.25 = (bf16[1,320,128]{2,1,0:T(8,128)(2,1)S(1)}, bf16[1,320,128]{2,1,0:T(8,128)(2,1)S(1)}, u32[]{:S(2)}, u32[]{:S(2)}) collective-permute-start(bf16[1,320,128]{2,1,0:T(8,128)(2,1)S(1)} %get-tuple-element.51), channel_id=1, source_target_pairs={{0,2},{1,3},{2,0},{3,1},{4,6},{5,7},{6,4},{7,5},{8,10},{9,11},{10,... | collective-permute-start | bytes 245768 | tf_op jit(solution)/shard_map/sum2_from_layer_2/ppermute | solution.py:185
  68.1 5.6 %collective-permute-start.26 = (bf16[1,320,128]{2,1,0:T(8,128)(2,1)S(1)}, bf16[1,320,128]{2,1,0:T(8,128)(2,1)S(1)}, u32[]{:S(2)}, u32[]{:S(2)}) collective-permute-start(bf16[1,320,128]{2,1,0:T(8,128)(2,1)S(1)} %get-tuple-element.52), channel_id=1, source_target_pairs={{0,1},{1,0},{2,3},{3,2},{4,5},{5,4},{6,7},{7,6},{8,9},{9,8},{10,11... | collective-permute-start | bytes 245768 | tf_op jit(solution)/shard_map/last0_from_layer_1/ppermute | solution.py:185
  70.6 8.8 %collective-permute-start.27 = (bf16[1,320,128]{2,1,0:T(8,128)(2,1)S(1)}, bf16[1,320,128]{2,1,0:T(8,128)(2,1)S(1)}, u32[]{:S(2)}, u32[]{:S(2)}) collective-permute-start(bf16[1,320,128]{2,1,0:T(8,128)(2,1)S(1)} %get-tuple-element.53), channel_id=1, source_target_pairs={{0,2},{1,3},{2,0},{3,1},{4,6},{5,7},{6,4},{7,5},{8,10},{9,11},{10,... | collective-permute-start | bytes 245768 | tf_op jit(solution)/shard_map/last0_from_layer_2/ppermute | solution.py:185
  70.7 8.7 %collective-permute-start.28 = (bf16[1,320,128]{2,1,0:T(8,128)(2,1)S(1)}, bf16[1,320,128]{2,1,0:T(8,128)(2,1)S(1)}, u32[]{:S(2)}, u32[]{:S(2)}) collective-permute-start(bf16[1,320,128]{2,1,0:T(8,128)(2,1)S(1)} %get-tuple-element.54), channel_id=1, source_target_pairs={{0,3},{1,2},{2,1},{3,0},{4,7},{5,6},{6,5},{7,4},{8,11},{9,10},{10,... | collective-permute-start | bytes 245768 | tf_op jit(solution)/shard_map/last0_from_layer_3/ppermute | solution.py:185

commit v9 on v8

--- a/solution.py
+++ b/solution.py
@@ -46,7 +46,7 @@
     )(pltpu.with_memory_space_constraint(source, pltpu.HBM), after)
 
 
-def take_kernel(chunk, at_group, source, after, out, sem):
+def take_kernel(chunk, at_group, at_ex, at_layer, source, after, out, sem):
     rows = out.shape[0]
     at = pl.multiple_of((at_group[0] * CHUNKS + chunk) * rows, rows)
     copy = pltpu.make_async_copy(source.at[pl.ds(at, rows), :], out, sem)
@@ -58,12 +58,12 @@
     return pl.pallas_call(
         functools.partial(take_kernel, chunk),
         out_shape=pltpu.VMEM((rows, source.shape[1]), BF16),
-        in_specs=[SMEM, HBM, ANY],
+        in_specs=[SMEM] * 3 + [HBM, ANY],
         out_specs=VMEM,
         scratch_shapes=[pltpu.SemaphoreType.DMA],
         compiler_params=pltpu.CompilerParams(vmem_limit_bytes=2 * MIB),
         name="take",
-    )(place[0], pltpu.with_memory_space_constraint(source, pltpu.HBM), after)
+    )(*place, pltpu.with_memory_space_constraint(source, pltpu.HBM), after)
 
 
 def condition_kernel(sizes, *refs):

time: 80.6 us -> 74.2 us (0.921)
  local copies, waits for them, and re-layouts: 10 us -> 0.02 us
  starting transfers between devices: 27.7 us -> 31.1 us
    unnamed x12 -> x6, local copies, waits for them, and re-layouts: 10 us -> 0.02 us
    ppermute x29, starting transfers between devices: 27.7 us -> 31.1 us  [permute(): return lax.ppermute(x, axis, perm)]
  transfers between devices with their start and end apart: 29 -> 29, of which waited for: 10 -> 11; matrix products, arithmetic and copies ran while one was open for 0% -> 0% of each run, Pallas kernels for 26% -> 28%
where the time goes in v9:
time: 74.2 us; the launch traced here: 74 us
  starting transfers between devices  31.1 us (42%)
  Pallas kernels  22.9 us (31%)
  waiting for transfers between devices  19.7 us (27%)
    ppermute x29, starting transfers between devices, permute(): return lax.ppermute(x, axis, perm)  31.1 us
    ppermute x29, waiting for transfers between devices, permute(): return lax.ppermute(x, axis, perm)  19.7 us
    pallas_call x4, Pallas kernels, score(): pl.pallas_call(functools.partial(score_kernel, sizes, direct), out_shape=...  11.8 us
    pallas_call x2, Pallas kernels, condition(): pl.pallas_call(functools.partial(condition_kernel, sizes), out_shape=pltp...  4.82 us
    pallas_call x1, Pallas kernels, load(): pl.pallas_call(load_kernel, out_shape=pltpu.VMEM(source.shape, BF16), in_...  3.39 us
    pallas_call x2, Pallas kernels, take(): pl.pallas_call(functools.partial(take_kernel, chunk), out_shape=pltpu.VME...  1.92 us
  transfers between devices with their start and end apart: 29, of which 11 were waited for; matrix products, arithmetic and copies ran while one was open for 0% of the time, Pallas kernels for 28%

profile of v9, /device:TPU:0, one launch (start us, length us, event | category | flops | bytes accessed | tf_op | source)
XLA Modules:
  0.0 74.0 jit_solution(847840358422413321)
XLA Ops:
  0.0 1.0 %take.2.after.refs_4_ = bf16[128,1024]{1,0:T(8,128)(2,1)S(1)} custom-call(s32[1]{0:T(128)} %bitcast.at_group.after.refs_0_, s32[1]{0:T(128)} %bitcast.1.at_ex.refs_1_, s32[1]{0:T(128)} %bitcast.2.at_layer.refs_2_, bf16[512,1024]{1,0:T(8,128)(2,1)} %bitcast.13, s32[1]{0:T(128)} %bitcast.at_group.after.refs_0_), custom_call_target="tpu_custom_call" | custom-call | tf_op jit(solution)/shard_map/take/pallas_call | solution.py:58
  1.0 3.0 %collective-permute-start.1 = (bf16[128,1024]{1,0:T(8,128)(2,1)S(1)}, bf16[128,1024]{1,0:T(8,128)(2,1)S(1)}, u32[]{:S(2)}, u32[]{:S(2)}) collective-permute-start(bf16[128,1024]{1,0:T(8,128)(2,1)S(1)} %take.2.after.refs_4_), channel_id=1, source_target_pairs={{0,8},{4,12},{8,0},{12,4},{1,9},{5,13},{9,1},{13,5},{2,10},{6,14},... | collective-permute-start | bytes 786440 | tf_op jit(solution)/shard_map/q0_from_chip/ppermute | solution.py:185
  4.0 3.4 %load.1.after.refs_3_ = bf16[1024,4096]{1,0:T(8,128)(2,1)S(1)} custom-call(bf16[1024,4096]{1,0:T(8,128)(2,1)} %bitcast.12, bf16[128,1024]{1,0:T(8,128)(2,1)S(1)} %take.2.after.refs_4_), custom_call_target="tpu_custom_call" | custom-call | tf_op jit(solution)/shard_map/load/pallas_call | solution.py:38
  7.4 1.0 %take.3.refs_8_.refs_4_ = bf16[128,1024]{1,0:T(8,128)(2,1)S(1)} custom-call(s32[1]{0:T(128)} %bitcast.at_group.after.refs_0_, s32[1]{0:T(128)} %bitcast.1.at_ex.refs_1_, s32[1]{0:T(128)} %bitcast.2.at_layer.refs_2_, bf16[512,1024]{1,0:T(8,128)(2,1)} %bitcast.14, bf16[1024,4096]{1,0:T(8,128)(2,1)S(1)} %load.1.after.refs_3_), custom_call_target="tpu_custom_call" | custom-call | tf_op jit(solution)/shard_map/take/pallas_call | solution.py:58
  8.4 0.0 slice-start
  8.4 0.0 slice-start.1
  8.4 1.9 %collective-permute-done.1.refs_6_ = bf16[128,1024]{1,0:T(8,128)(2,1)S(1)} collective-permute-done((bf16[128,1024]{1,0:T(8,128)(2,1)S(1)}, bf16[128,1024]{1,0:T(8,128)(2,1)S(1)}, u32[]{:S(2)}, u32[]{:S(2)}) %collective-permute-start.1) | collective-permute-done | bytes 262176 | tf_op jit(solution)/shard_map/q0_from_chip/ppermute | solution.py:185
  10.3 0.0 collective-permute-start.2
  10.3 1.7 %collective-permute-start.7 = (bf16[128,1024]{1,0:T(8,128)(2,1)S(1)}, bf16[128,1024]{1,0:T(8,128)(2,1)S(1)}, u32[]{:S(2)}, u32[]{:S(2)}) collective-permute-start(bf16[128,1024]{1,0:T(8,128)(2,1)S(1)} %take.3.refs_8_.refs_4_), channel_id=1, source_target_pairs={{0,8},{4,12},{8,0},{12,4},{1,9},{5,13},{9,1},{13,5},{2,10},{6,14},... | collective-permute-start | bytes 786440 | tf_op jit(solution)/shard_map/q1_from_chip/ppermute | solution.py:185
  12.1 2.4 %condition.2.refs_4_ = bf16[1024,128]{1,0:T(8,128)(2,1)S(1)} custom-call(s32[1]{0:T(128)} %bitcast.at_group.after.refs_0_, s32[1]{0:T(128)} %bitcast.1.at_ex.refs_1_, s32[1]{0:T(128)} %bitcast.2.at_layer.refs_2_, bf16[1024,4096]{1,0:T(8,128)(2,1)S(1)} %load.1.after.refs_3_, bf16[128,1024]{1,0:T(8,128)(2,1)S(1)} %take.2.after.refs_4_, ...), custom_call_target="tpu_custom_call" | custom-call | tf_op jit(solution)/shard_map/condition/pallas_call | solution.py:83
  14.5 0.0 slice-start.2
  14.5 1.6 %collective-permute-start.4 = (bf16[1024,128]{1,0:T(8,128)(2,1)S(1)}, bf16[1024,128]{1,0:T(8,128)(2,1)S(1)}, u32[]{:S(2)}, u32[]{:S(2)}) collective-permute-start(bf16[1024,128]{1,0:T(8,128)(2,1)S(1)} %condition.2.refs_4_), channel_id=1, source_target_pairs={{0,8},{4,12},{8,0},{12,4},{1,9},{5,13},{9,1},{13,5},{2,10},{6,14},... | collective-permute-start | bytes 786440 | tf_op jit(solution)/shard_map/s0_from_chip/ppermute | solution.py:185
  16.1 0.0 collective-permute-start.6
  16.1 3.3 %collective-permute-done.7.refs_6_ = bf16[128,1024]{1,0:T(8,128)(2,1)S(1)} collective-permute-done((bf16[128,1024]{1,0:T(8,128)(2,1)S(1)}, bf16[128,1024]{1,0:T(8,128)(2,1)S(1)}, u32[]{:S(2)}, u32[]{:S(2)}) %collective-permute-start.7) | collective-permute-done | bytes 262176 | tf_op jit(solution)/shard_map/q1_from_chip/ppermute | solution.py:185
  19.4 0.0 collective-permute-start.8
  19.4 1.7 %collective-permute-start.10 = (bf16[1024,128]{1,0:T(8,128)(2,1)S(1)}, bf16[1024,128]{1,0:T(8,128)(2,1)S(1)}, u32[]{:S(2)}, u32[]{:S(2)}) collective-permute-start(bf16[1024,128]{1,0:T(8,128)(2,1)S(1)} %condition.2.refs_4_), channel_id=1, source_target_pairs={{0,16},{16,0},{1,17},{17,1},{2,18},{18,2},{3,19},{19,3},{4,20},{20... | collective-permute-start | bytes 786440 | tf_op jit(solution)/shard_map/s0_from_group/ppermute | solution.py:185
  21.1 0.2 collective-permute-start.3
  21.4 3.3 %collective-permute-done.4.refs_8_.refs_6_ = bf16[1024,128]{1,0:T(8,128)(2,1)S(1)} collective-permute-done((bf16[1024,128]{1,0:T(8,128)(2,1)S(1)}, bf16[1024,128]{1,0:T(8,128)(2,1)S(1)}, u32[]{:S(2)}, u32[]{:S(2)}) %collective-permute-start.4) | collective-permute-done | bytes 262176 | tf_op jit(solution)/shard_map/s0_from_chip/ppermute | solution.py:185
  24.7 1.7 %collective-permute-start.12 = (bf16[1024,128]{1,0:T(8,128)(2,1)S(1)}, bf16[1024,128]{1,0:T(8,128)(2,1)S(1)}, u32[]{:S(2)}, u32[]{:S(2)}) collective-permute-start(bf16[1024,128]{1,0:T(8,128)(2,1)S(1)} %collective-permute-done.4.refs_8_.refs_6_), channel_id=1, source_target_pairs={{0,16},{16,0},{1,17},{17,1},{2,18},{18,2},{3,19},{19,3},{4,20},{20... | collective-permute-start | bytes 786440 | tf_op jit(solution)/shard_map/s0_there_from_group/ppermute | solution.py:185
  26.4 2.4 %condition.3.refs_8_.refs_4_ = bf16[1024,128]{1,0:T(8,128)(2,1)S(1)} custom-call(s32[1]{0:T(128)} %bitcast.at_group.after.refs_0_, s32[1]{0:T(128)} %bitcast.1.at_ex.refs_1_, s32[1]{0:T(128)} %bitcast.2.at_layer.refs_2_, bf16[1024,4096]{1,0:T(8,128)(2,1)S(1)} %load.1.after.refs_3_, bf16[128,1024]{1,0:T(8,128)(2,1)S(1)} %take.3.refs_8_.refs_4_, ...), custom_call_target="tpu_custom_call" | custom-call | tf_op jit(solution)/shard_map/condition/pallas_call | solution.py:83
  28.8 1.6 %collective-permute-start.17 = (bf16[1024,128]{1,0:T(8,128)(2,1)S(1)}, bf16[1024,128]{1,0:T(8,128)(2,1)S(1)}, u32[]{:S(2)}, u32[]{:S(2)}) collective-permute-start(bf16[1024,128]{1,0:T(8,128)(2,1)S(1)} %condition.3.refs_8_.refs_4_), channel_id=1, source_target_pairs={{0,8},{4,12},{8,0},{12,4},{1,9},{5,13},{9,1},{13,5},{2,10},{6,14},... | collective-permute-start | bytes 786440 | tf_op jit(solution)/shard_map/s1_from_chip/ppermute | solution.py:185
  30.4 3.0 %score0.1 = (bf16[2,320,128]{2,1,0:T(8,128)(2,1)S(1)}, f32[2,320,128]{2,1,0:T(8,128)S(1)}) custom-call(s32[1]{0:T(128)} %bitcast.at_group.after.refs_0_, s32[1]{0:T(128)} %bitcast.1.at_ex.refs_1_, s32[1]{0:T(128)} %bitcast.2.at_layer.refs_2_, bf16[1280,4096]{1,0:T(8,128)(2,1)S(1)} %bitcast.8, bf16[1024,128]{1,0:T(8,128)(2,1)S(1)} %condition.2.refs_4_, ...), custom_call_target="tpu_custom_call" | custom-call | tf_op jit(solution)/shard_map/score0/pallas_call | solution.py:119
  33.4 0.4 collective-permute-done.12.refs_6_
  33.8 0.2 collective-permute-start.13
  34.0 0.3 collective-permute-start.16
  34.3 1.8 %collective-permute-start.9 = (bf16[2,320,128]{2,1,0:T(8,128)(2,1)S(1)}, bf16[2,320,128]{2,1,0:T(8,128)(2,1)S(1)}, u32[]{:S(2)}, u32[]{:S(2)}) collective-permute-start(bf16[2,320,128]{2,1,0:T(8,128)(2,1)S(1)} %get-tuple-element.33), channel_id=1, source_target_pairs={{0,1},{1,0},{2,3},{3,2},{4,5},{5,4},{6,7},{7,6},{8,9},{9,8},{10,11... | collective-permute-start | bytes 491528 | tf_op jit(solution)/shard_map/sum0_from_layer_1/ppermute | solution.py:185
  36.1 1.2 %collective-permute-done.17.refs_6_ = bf16[1024,128]{1,0:T(8,128)(2,1)S(1)} collective-permute-done((bf16[1024,128]{1,0:T(8,128)(2,1)S(1)}, bf16[1024,128]{1,0:T(8,128)(2,1)S(1)}, u32[]{:S(2)}, u32[]{:S(2)}) %collective-permute-start.17) | collective-permute-done | bytes 262176 | tf_op jit(solution)/shard_map/s1_from_chip/ppermute | solution.py:185
  37.3 0.4 collective-permute-start.23
  37.7 1.7 %collective-permute-start.21 = (bf16[1024,128]{1,0:T(8,128)(2,1)S(1)}, bf16[1024,128]{1,0:T(8,128)(2,1)S(1)}, u32[]{:S(2)}, u32[]{:S(2)}) collective-permute-start(bf16[1024,128]{1,0:T(8,128)(2,1)S(1)} %condition.3.refs_8_.refs_4_), channel_id=1, source_target_pairs={{0,16},{16,0},{1,17},{17,1},{2,18},{18,2},{3,19},{19,3},{4,20},{20... | collective-permute-start | bytes 786440 | tf_op jit(solution)/shard_map/s1_from_group/ppermute | solution.py:185
  39.3 2.9 %score1.1 = (bf16[2,320,128]{2,1,0:T(8,128)(2,1)S(1)}, f32[2,320,128]{2,1,0:T(8,128)S(1)}) custom-call(s32[1]{0:T(128)} %bitcast.at_group.after.refs_0_, s32[1]{0:T(128)} %bitcast.1.at_ex.refs_1_, s32[1]{0:T(128)} %bitcast.2.at_layer.refs_2_, bf16[1280,4096]{1,0:T(8,128)(2,1)S(1)} %bitcast.9, bf16[1024,128]{1,0:T(8,128)(2,1)S(1)} %collective-permute-done.10.refs_4_, ...), custom_call_target="tpu_custom_call" | custom-call | tf_op jit(solution)/shard_map/score1/pallas_call | solution.py:119
  42.3 1.6 %collective-permute-start.15 = (bf16[2,320,128]{2,1,0:T(8,128)(2,1)S(1)}, bf16[2,320,128]{2,1,0:T(8,128)(2,1)S(1)}, u32[]{:S(2)}, u32[]{:S(2)}) collective-permute-start(bf16[2,320,128]{2,1,0:T(8,128)(2,1)S(1)} %get-tuple-element.39), channel_id=1, source_target_pairs={{0,1},{1,0},{2,3},{3,2},{4,5},{5,4},{6,7},{7,6},{8,9},{9,8},{10,11... | collective-permute-start | bytes 491528 | tf_op jit(solution)/shard_map/sum1_from_layer_1/ppermute | solution.py:185
  44.0 2.7 %collective-permute-start.14 = (bf16[1,320,128]{2,1,0:T(8,128)(2,1)S(1)}, bf16[1,320,128]{2,1,0:T(8,128)(2,1)S(1)}, u32[]{:S(2)}, u32[]{:S(2)}) collective-permute-start(bf16[1,320,128]{2,1,0:T(8,128)(2,1)S(1)} %get-tuple-element.38), channel_id=1, source_target_pairs={{0,2},{1,3},{2,0},{3,1},{4,6},{5,7},{6,4},{7,5},{8,10},{9,11},{10,... | collective-permute-start | bytes 245768 | tf_op jit(solution)/shard_map/sum0_from_layer_2/ppermute | solution.py:185
  46.6 2.9 %score2.1 = (bf16[2,320,128]{2,1,0:T(8,128)(2,1)S(1)}, f32[2,320,128]{2,1,0:T(8,128)S(1)}) custom-call(s32[1]{0:T(128)} %bitcast.at_group.after.refs_0_, s32[1]{0:T(128)} %bitcast.1.at_ex.refs_1_, s32[1]{0:T(128)} %bitcast.2.at_layer.refs_2_, bf16[1280,4096]{1,0:T(8,128)(2,1)S(1)} %bitcast.10, bf16[1024,128]{1,0:T(8,128)(2,1)S(1)} %condition.3.refs_8_.refs_4_, ...), custom_call_target="tpu_custom_call" | custom-call | tf_op jit(solution)/shard_map/score2/pallas_call | solution.py:119
  49.6 0.6 collective-permute-done.15.got
  50.2 0.1 collective-permute-start.24
  50.3 1.3 %collective-permute-done.21.refs_4_ = bf16[1024,128]{1,0:T(8,128)(2,1)S(1)} collective-permute-done((bf16[1024,128]{1,0:T(8,128)(2,1)S(1)}, bf16[1024,128]{1,0:T(8,128)(2,1)S(1)}, u32[]{:S(2)}, u32[]{:S(2)}) %collective-permute-start.21) | collective-permute-done | bytes 262176 | tf_op jit(solution)/shard_map/s1_from_group/ppermute | solution.py:185
  51.6 1.7 %collective-permute-start.20 = (bf16[2,320,128]{2,1,0:T(8,128)(2,1)S(1)}, bf16[2,320,128]{2,1,0:T(8,128)(2,1)S(1)}, u32[]{:S(2)}, u32[]{:S(2)}) collective-permute-start(bf16[2,320,128]{2,1,0:T(8,128)(2,1)S(1)} %get-tuple-element.45), channel_id=1, source_target_pairs={{0,1},{1,0},{2,3},{3,2},{4,5},{5,4},{6,7},{7,6},{8,9},{9,8},{10,11... | collective-permute-start | bytes 491528 | tf_op jit(solution)/shard_map/sum2_from_layer_1/ppermute | solution.py:185
  53.4 2.4 %collective-permute-start.19 = (bf16[1,320,128]{2,1,0:T(8,128)(2,1)S(1)}, bf16[1,320,128]{2,1,0:T(8,128)(2,1)S(1)}, u32[]{:S(2)}, u32[]{:S(2)}) collective-permute-start(bf16[1,320,128]{2,1,0:T(8,128)(2,1)S(1)} %get-tuple-element.44), channel_id=1, source_target_pairs={{0,2},{1,3},{2,0},{3,1},{4,6},{5,7},{6,4},{7,5},{8,10},{9,11},{10,... | collective-permute-start | bytes 245768 | tf_op jit(solution)/shard_map/sum1_from_layer_2/ppermute | solution.py:185
  55.8 3.0 %score3.1 = (f32[1,320,128]{2,1,0:T(8,128)S(1)}, bf16[1,320,128]{2,1,0:T(8,128)(2,1)S(1)}, bf16[1,320,128]{2,1,0:T(8,128)(2,1)S(1)}, bf16[1,320,128]{2,1,0:T(8,128)(2,1)S(1)}) custom-call(s32[1]{0:T(128)} %bitcast.at_group.after.refs_0_, s32[1]{0:T(128)} %bitcast.1.at_ex.refs_1_, s32[1]{0:T(128)} %bitcast.2.at_layer.refs_2_, ...), custom_call_target="tpu_custom_call" | custom-call | tf_op jit(solution)/shard_map/score3/pallas_call | solution.py:119
  58.8 1.2 %collective-permute-done.20.got = bf16[2,320,128]{2,1,0:T(8,128)(2,1)S(1)} collective-permute-done((bf16[2,320,128]{2,1,0:T(8,128)(2,1)S(1)}, bf16[2,320,128]{2,1,0:T(8,128)(2,1)S(1)}, u32[]{:S(2)}, u32[]{:S(2)}) %collective-permute-start.20) | collective-permute-done | bytes 163872 | tf_op jit(solution)/shard_map/sum2_from_layer_1/ppermute | solution.py:185
  60.0 1.7 %collective-permute-start.25 = (bf16[1,320,128]{2,1,0:T(8,128)(2,1)S(1)}, bf16[1,320,128]{2,1,0:T(8,128)(2,1)S(1)}, u32[]{:S(2)}, u32[]{:S(2)}) collective-permute-start(bf16[1,320,128]{2,1,0:T(8,128)(2,1)S(1)} %get-tuple-element.51), channel_id=1, source_target_pairs={{0,2},{1,3},{2,0},{3,1},{4,6},{5,7},{6,4},{7,5},{8,10},{9,11},{10,... | collective-permute-start | bytes 245768 | tf_op jit(solution)/shard_map/sum2_from_layer_2/ppermute | solution.py:185
  61.8 2.5 %collective-permute-start.26 = (bf16[1,320,128]{2,1,0:T(8,128)(2,1)S(1)}, bf16[1,320,128]{2,1,0:T(8,128)(2,1)S(1)}, u32[]{:S(2)}, u32[]{:S(2)}) collective-permute-start(bf16[1,320,128]{2,1,0:T(8,128)(2,1)S(1)} %get-tuple-element.52), channel_id=1, source_target_pairs={{0,1},{1,0},{2,3},{3,2},{4,5},{5,4},{6,7},{7,6},{8,9},{9,8},{10,11... | collective-permute-start | bytes 245768 | tf_op jit(solution)/shard_map/last0_from_layer_1/ppermute | solution.py:185
  64.3 0.1 collective-permute-start.27
  64.3 2.3 %collective-permute-start.28 = (bf16[1,320,128]{2,1,0:T(8,128)(2,1)S(1)}, bf16[1,320,128]{2,1,0:T(8,128)(2,1)S(1)}, u32[]{:S(2)}, u32[]{:S(2)}) collective-permute-start(bf16[1,320,128]{2,1,0:T(8,128)(2,1)S(1)} %get-tuple-element.54), channel_id=1, source_target_pairs={{0,3},{1,2},{2,1},{3,0},{4,7},{5,6},{6,5},{7,4},{8,11},{9,10},{10,... | collective-permute-start | bytes 245768 | tf_op jit(solution)/shard_map/last0_from_layer_3/ppermute | solution.py:185
  66.6 0.2 collective-permute-done.25.refs_8_
  66.8 0.6 collective-permute-done.26.refs_10_
  67.4 5.7 %collective-permute-done.27.refs_11_ = bf16[1,320,128]{2,1,0:T(8,128)(2,1)S(1)} collective-permute-done((bf16[1,320,128]{2,1,0:T(8,128)(2,1)S(1)}, bf16[1,320,128]{2,1,0:T(8,128)(2,1)S(1)}, u32[]{:S(2)}, u32[]{:S(2)}) %collective-permute-start.27) | collective-permute-done | bytes 81952 | tf_op jit(solution)/shard_map/last0_from_layer_2/ppermute | solution.py:185
  73.1 0.9 %finish.1 = f32[320,512]{1,0:T(8,128)} custom-call(s32[1]{0:T(128)} %bitcast.at_group.after.refs_0_, s32[1]{0:T(128)} %bitcast.1.at_ex.refs_1_, s32[1]{0:T(128)} %bitcast.2.at_layer.refs_2_, f32[1,320,128]{2,1,0:T(8,128)S(1)} %get-tuple-element.37.refs_8_.refs_3_, bf16[1,320,128]{2,1,0:T(8,128)(2,1)S(1)} %collective-permute-done.14.refs_4_, ...), custom_call_target="tpu_custom_call" | custom-call | tf_op jit(solution)/shard_map/finish/pallas_call | solution.py:167
  (30 shorter events, 0.2 us)
Async XLA Ops:
  1.0 9.3 %collective-permute-start.1 = (bf16[128,1024]{1,0:T(8,128)(2,1)S(1)}, bf16[128,1024]{1,0:T(8,128)(2,1)S(1)}, u32[]{:S(2)}, u32[]{:S(2)}) collective-permute-start(bf16[128,1024]{1,0:T(8,128)(2,1)S(1)} %take.2.after.refs_4_), channel_id=1, source_target_pairs={{0,8},{4,12},{8,0},{12,4},{1,9},{5,13},{9,1},{13,5},{2,10},{6,14},... | collective-permute-start | bytes 786440 | tf_op jit(solution)/shard_map/q0_from_chip/ppermute | solution.py:185
  4.0 8.1 %collective-permute-start = (bf16[128,1024]{1,0:T(8,128)(2,1)S(1)}, bf16[128,1024]{1,0:T(8,128)(2,1)S(1)}, u32[]{:S(2)}, u32[]{:S(2)}) collective-permute-start(bf16[128,1024]{1,0:T(8,128)(2,1)S(1)} %take.2.after.refs_4_), channel_id=1, source_target_pairs={{0,4},{4,0},{8,12},{12,8},{1,5},{5,1},{9,13},{13,9},{2,6},{6,2},{1... | collective-permute-start | bytes 786440 | tf_op jit(solution)/shard_map/q0_from_core/ppermute | solution.py:185
  8.4 22.0 %slice-start = ((s8[10485760]{0:T(1024)(128)(4,1)}), s8[4194304]{0:T(1024)(128)(4,1)S(1)}, s32[]{:S(2)}) async-start(s8[10485760]{0:T(1024)(128)(4,1)} %bitcast.6), calls=%async_computation | async-start | bytes 8388608
  8.4 22.0 %slice-start.1 = ((s8[10485760]{0:T(1024)(128)(4,1)}), s8[4194304]{0:T(1024)(128)(4,1)S(1)}, s32[]{:S(2)}) async-start(s8[10485760]{0:T(1024)(128)(4,1)} %bitcast.6), calls=%async_computation.1 | async-start | bytes 8388608
  10.3 1.8 %collective-permute-start.2 = (bf16[128,1024]{1,0:T(8,128)(2,1)S(1)}, bf16[128,1024]{1,0:T(8,128)(2,1)S(1)}, u32[]{:S(2)}, u32[]{:S(2)}) collective-permute-start(bf16[128,1024]{1,0:T(8,128)(2,1)S(1)} %collective-permute-done.1.refs_6_), channel_id=1, source_target_pairs={{0,4},{4,0},{8,12},{12,8},{1,5},{5,1},{9,13},{13,9},{2,6},{6,2},{1... | collective-permute-start | bytes 786440 | tf_op jit(solution)/shard_map/q0_there_from_core/ppermute | solution.py:185
  10.3 9.1 %collective-permute-start.7 = (bf16[128,1024]{1,0:T(8,128)(2,1)S(1)}, bf16[128,1024]{1,0:T(8,128)(2,1)S(1)}, u32[]{:S(2)}, u32[]{:S(2)}) collective-permute-start(bf16[128,1024]{1,0:T(8,128)(2,1)S(1)} %take.3.refs_8_.refs_4_), channel_id=1, source_target_pairs={{0,8},{4,12},{8,0},{12,4},{1,9},{5,13},{9,1},{13,5},{2,10},{6,14},... | collective-permute-start | bytes 786440 | tf_op jit(solution)/shard_map/q1_from_chip/ppermute | solution.py:185
  14.5 15.9 %slice-start.2 = ((s8[10485760]{0:T(1024)(128)(4,1)}), s8[2097152]{0:T(1024)(128)(4,1)S(1)}, s32[]{:S(2)}) async-start(s8[10485760]{0:T(1024)(128)(4,1)} %bitcast.6), calls=%async_computation.2 | async-start | bytes 4194304
  14.5 10.2 %collective-permute-start.4 = (bf16[1024,128]{1,0:T(8,128)(2,1)S(1)}, bf16[1024,128]{1,0:T(8,128)(2,1)S(1)}, u32[]{:S(2)}, u32[]{:S(2)}) collective-permute-start(bf16[1024,128]{1,0:T(8,128)(2,1)S(1)} %condition.2.refs_4_), channel_id=1, source_target_pairs={{0,8},{4,12},{8,0},{12,4},{1,9},{5,13},{9,1},{13,5},{2,10},{6,14},... | collective-permute-start | bytes 786440 | tf_op jit(solution)/shard_map/s0_from_chip/ppermute | solution.py:185
  16.1 8.6 %collective-permute-start.6 = (bf16[128,1024]{1,0:T(8,128)(2,1)S(1)}, bf16[128,1024]{1,0:T(8,128)(2,1)S(1)}, u32[]{:S(2)}, u32[]{:S(2)}) collective-permute-start(bf16[128,1024]{1,0:T(8,128)(2,1)S(1)} %take.3.refs_8_.refs_4_), channel_id=1, source_target_pairs={{0,4},{4,0},{8,12},{12,8},{1,5},{5,1},{9,13},{13,9},{2,6},{6,2},{1... | collective-permute-start | bytes 786440 | tf_op jit(solution)/shard_map/q1_from_core/ppermute | solution.py:185
  19.4 7.0 %collective-permute-start.8 = (bf16[128,1024]{1,0:T(8,128)(2,1)S(1)}, bf16[128,1024]{1,0:T(8,128)(2,1)S(1)}, u32[]{:S(2)}, u32[]{:S(2)}) collective-permute-start(bf16[128,1024]{1,0:T(8,128)(2,1)S(1)} %collective-permute-done.7.refs_6_), channel_id=1, source_target_pairs={{0,4},{4,0},{8,12},{12,8},{1,5},{5,1},{9,13},{13,9},{2,6},{6,2},{1... | collective-permute-start | bytes 786440 | tf_op jit(solution)/shard_map/q1_there_from_core/ppermute | solution.py:185
  19.4 11.0 %collective-permute-start.10 = (bf16[1024,128]{1,0:T(8,128)(2,1)S(1)}, bf16[1024,128]{1,0:T(8,128)(2,1)S(1)}, u32[]{:S(2)}, u32[]{:S(2)}) collective-permute-start(bf16[1024,128]{1,0:T(8,128)(2,1)S(1)} %condition.2.refs_4_), channel_id=1, source_target_pairs={{0,16},{16,0},{1,17},{17,1},{2,18},{18,2},{3,19},{19,3},{4,20},{20... | collective-permute-start | bytes 786440 | tf_op jit(solution)/shard_map/s0_from_group/ppermute | solution.py:185
  21.1 9.2 %collective-permute-start.3 = (bf16[1024,128]{1,0:T(8,128)(2,1)S(1)}, bf16[1024,128]{1,0:T(8,128)(2,1)S(1)}, u32[]{:S(2)}, u32[]{:S(2)}) collective-permute-start(bf16[1024,128]{1,0:T(8,128)(2,1)S(1)} %condition.2.refs_4_), channel_id=1, source_target_pairs={{0,4},{4,0},{8,12},{12,8},{1,5},{5,1},{9,13},{13,9},{2,6},{6,2},{1... | collective-permute-start | bytes 786440 | tf_op jit(solution)/shard_map/s0_from_core/ppermute | solution.py:185
  24.6 5.7 %collective-permute-start.5 = (bf16[1024,128]{1,0:T(8,128)(2,1)S(1)}, bf16[1024,128]{1,0:T(8,128)(2,1)S(1)}, u32[]{:S(2)}, u32[]{:S(2)}) collective-permute-start(bf16[1024,128]{1,0:T(8,128)(2,1)S(1)} %collective-permute-done.4.refs_8_.refs_6_), channel_id=1, source_target_pairs={{0,4},{4,0},{8,12},{12,8},{1,5},{5,1},{9,13},{13,9},{2,6},{6,2},{1... | collective-permute-start | bytes 786440 | tf_op jit(solution)/shard_map/s0_there_from_core/ppermute | solution.py:185
  24.7 9.1 %collective-permute-start.12 = (bf16[1024,128]{1,0:T(8,128)(2,1)S(1)}, bf16[1024,128]{1,0:T(8,128)(2,1)S(1)}, u32[]{:S(2)}, u32[]{:S(2)}) collective-permute-start(bf16[1024,128]{1,0:T(8,128)(2,1)S(1)} %collective-permute-done.4.refs_8_.refs_6_), channel_id=1, source_target_pairs={{0,16},{16,0},{1,17},{17,1},{2,18},{18,2},{3,19},{19,3},{4,20},{20... | collective-permute-start | bytes 786440 | tf_op jit(solution)/shard_map/s0_there_from_group/ppermute | solution.py:185
  28.8 8.5 %collective-permute-start.17 = (bf16[1024,128]{1,0:T(8,128)(2,1)S(1)}, bf16[1024,128]{1,0:T(8,128)(2,1)S(1)}, u32[]{:S(2)}, u32[]{:S(2)}) collective-permute-start(bf16[1024,128]{1,0:T(8,128)(2,1)S(1)} %condition.3.refs_8_.refs_4_), channel_id=1, source_target_pairs={{0,8},{4,12},{8,0},{12,4},{1,9},{5,13},{9,1},{13,5},{2,10},{6,14},... | collective-permute-start | bytes 786440 | tf_op jit(solution)/shard_map/s1_from_chip/ppermute | solution.py:185
  30.4 6.9 %collective-permute-start.11 = (bf16[1024,128]{1,0:T(8,128)(2,1)S(1)}, bf16[1024,128]{1,0:T(8,128)(2,1)S(1)}, u32[]{:S(2)}, u32[]{:S(2)}) collective-permute-start(bf16[1024,128]{1,0:T(8,128)(2,1)S(1)} %collective-permute-done.10.refs_4_), channel_id=1, source_target_pairs={{0,4},{4,0},{8,12},{12,8},{1,5},{5,1},{9,13},{13,9},{2,6},{6,2},{1... | collective-permute-start | bytes 786440 | tf_op jit(solution)/shard_map/s0_across_from_core/ppermute | solution.py:185
  33.8 3.9 %collective-permute-start.13 = (bf16[1024,128]{1,0:T(8,128)(2,1)S(1)}, bf16[1024,128]{1,0:T(8,128)(2,1)S(1)}, u32[]{:S(2)}, u32[]{:S(2)}) collective-permute-start(bf16[1024,128]{1,0:T(8,128)(2,1)S(1)} %collective-permute-done.12.refs_6_), channel_id=1, source_target_pairs={{0,4},{4,0},{8,12},{12,8},{1,5},{5,1},{9,13},{13,9},{2,6},{6,2},{1... | collective-permute-start | bytes 786440 | tf_op jit(solution)/shard_map/s0_diagonal_from_core/ppermute | solution.py:185
  34.0 10.0 %collective-permute-start.16 = (bf16[1024,128]{1,0:T(8,128)(2,1)S(1)}, bf16[1024,128]{1,0:T(8,128)(2,1)S(1)}, u32[]{:S(2)}, u32[]{:S(2)}) collective-permute-start(bf16[1024,128]{1,0:T(8,128)(2,1)S(1)} %condition.3.refs_8_.refs_4_), channel_id=1, source_target_pairs={{0,4},{4,0},{8,12},{12,8},{1,5},{5,1},{9,13},{13,9},{2,6},{6,2},{1... | collective-permute-start | bytes 786440 | tf_op jit(solution)/shard_map/s1_from_core/ppermute | solution.py:185
  34.3 8.0 %collective-permute-start.9 = (bf16[2,320,128]{2,1,0:T(8,128)(2,1)S(1)}, bf16[2,320,128]{2,1,0:T(8,128)(2,1)S(1)}, u32[]{:S(2)}, u32[]{:S(2)}) collective-permute-start(bf16[2,320,128]{2,1,0:T(8,128)(2,1)S(1)} %get-tuple-element.33), channel_id=1, source_target_pairs={{0,1},{1,0},{2,3},{3,2},{4,5},{5,4},{6,7},{7,6},{8,9},{9,8},{10,11... | collective-permute-start | bytes 491528 | tf_op jit(solution)/shard_map/sum0_from_layer_1/ppermute | solution.py:185
  37.3 9.3 %collective-permute-start.18 = (bf16[1024,128]{1,0:T(8,128)(2,1)S(1)}, bf16[1024,128]{1,0:T(8,128)(2,1)S(1)}, u32[]{:S(2)}, u32[]{:S(2)}) collective-permute-start(bf16[1024,128]{1,0:T(8,128)(2,1)S(1)} %collective-permute-done.17.refs_6_), channel_id=1, source_target_pairs={{0,4},{4,0},{8,12},{12,8},{1,5},{5,1},{9,13},{13,9},{2,6},{6,2},{1... | collective-permute-start | bytes 786440 | tf_op jit(solution)/shard_map/s1_there_from_core/ppermute | solution.py:185
  37.3 12.9 %collective-permute-start.23 = (bf16[1024,128]{1,0:T(8,128)(2,1)S(1)}, bf16[1024,128]{1,0:T(8,128)(2,1)S(1)}, u32[]{:S(2)}, u32[]{:S(2)}) collective-permute-start(bf16[1024,128]{1,0:T(8,128)(2,1)S(1)} %collective-permute-done.17.refs_6_), channel_id=1, source_target_pairs={{0,16},{16,0},{1,17},{17,1},{2,18},{18,2},{3,19},{19,3},{4,20},{20... | collective-permute-start | bytes 786440 | tf_op jit(solution)/shard_map/s1_there_from_group/ppermute | solution.py:185
  37.7 14.0 %collective-permute-start.21 = (bf16[1024,128]{1,0:T(8,128)(2,1)S(1)}, bf16[1024,128]{1,0:T(8,128)(2,1)S(1)}, u32[]{:S(2)}, u32[]{:S(2)}) collective-permute-start(bf16[1024,128]{1,0:T(8,128)(2,1)S(1)} %condition.3.refs_8_.refs_4_), channel_id=1, source_target_pairs={{0,16},{16,0},{1,17},{17,1},{2,18},{18,2},{3,19},{19,3},{4,20},{20... | collective-permute-start | bytes 786440 | tf_op jit(solution)/shard_map/s1_from_group/ppermute | solution.py:185
  42.3 7.9 %collective-permute-start.15 = (bf16[2,320,128]{2,1,0:T(8,128)(2,1)S(1)}, bf16[2,320,128]{2,1,0:T(8,128)(2,1)S(1)}, u32[]{:S(2)}, u32[]{:S(2)}) collective-permute-start(bf16[2,320,128]{2,1,0:T(8,128)(2,1)S(1)} %get-tuple-element.39), channel_id=1, source_target_pairs={{0,1},{1,0},{2,3},{3,2},{4,5},{5,4},{6,7},{7,6},{8,9},{9,8},{10,11... | collective-permute-start | bytes 491528 | tf_op jit(solution)/shard_map/sum1_from_layer_1/ppermute | solution.py:185
  44.0 5.6 %collective-permute-start.14 = (bf16[1,320,128]{2,1,0:T(8,128)(2,1)S(1)}, bf16[1,320,128]{2,1,0:T(8,128)(2,1)S(1)}, u32[]{:S(2)}, u32[]{:S(2)}) collective-permute-start(bf16[1,320,128]{2,1,0:T(8,128)(2,1)S(1)} %get-tuple-element.38), channel_id=1, source_target_pairs={{0,2},{1,3},{2,0},{3,1},{4,6},{5,7},{6,4},{7,5},{8,10},{9,11},{10,... | collective-permute-start | bytes 245768 | tf_op jit(solution)/shard_map/sum0_from_layer_2/ppermute | solution.py:185
  50.2 5.6 %collective-permute-start.24 = (bf16[1024,128]{1,0:T(8,128)(2,1)S(1)}, bf16[1024,128]{1,0:T(8,128)(2,1)S(1)}, u32[]{:S(2)}, u32[]{:S(2)}) collective-permute-start(bf16[1024,128]{1,0:T(8,128)(2,1)S(1)} %collective-permute-done.23.refs_6_), channel_id=1, source_target_pairs={{0,4},{4,0},{8,12},{12,8},{1,5},{5,1},{9,13},{13,9},{2,6},{6,2},{1... | collective-permute-start | bytes 786440 | tf_op jit(solution)/shard_map/s1_diagonal_from_core/ppermute | solution.py:185
  51.6 4.2 %collective-permute-start.22 = (bf16[1024,128]{1,0:T(8,128)(2,1)S(1)}, bf16[1024,128]{1,0:T(8,128)(2,1)S(1)}, u32[]{:S(2)}, u32[]{:S(2)}) collective-permute-start(bf16[1024,128]{1,0:T(8,128)(2,1)S(1)} %collective-permute-done.21.refs_4_), channel_id=1, source_target_pairs={{0,4},{4,0},{8,12},{12,8},{1,5},{5,1},{9,13},{13,9},{2,6},{6,2},{1... | collective-permute-start | bytes 786440 | tf_op jit(solution)/shard_map/s1_across_from_core/ppermute | solution.py:185
  51.6 8.4 %collective-permute-start.20 = (bf16[2,320,128]{2,1,0:T(8,128)(2,1)S(1)}, bf16[2,320,128]{2,1,0:T(8,128)(2,1)S(1)}, u32[]{:S(2)}, u32[]{:S(2)}) collective-permute-start(bf16[2,320,128]{2,1,0:T(8,128)(2,1)S(1)} %get-tuple-element.45), channel_id=1, source_target_pairs={{0,1},{1,0},{2,3},{3,2},{4,5},{5,4},{6,7},{7,6},{8,9},{9,8},{10,11... | collective-permute-start | bytes 491528 | tf_op jit(solution)/shard_map/sum2_from_layer_1/ppermute | solution.py:185
  53.4 13.3 %collective-permute-start.19 = (bf16[1,320,128]{2,1,0:T(8,128)(2,1)S(1)}, bf16[1,320,128]{2,1,0:T(8,128)(2,1)S(1)}, u32[]{:S(2)}, u32[]{:S(2)}) collective-permute-start(bf16[1,320,128]{2,1,0:T(8,128)(2,1)S(1)} %get-tuple-element.44), channel_id=1, source_target_pairs={{0,2},{1,3},{2,0},{3,1},{4,6},{5,7},{6,4},{7,5},{8,10},{9,11},{10,... | collective-permute-start | bytes 245768 | tf_op jit(solution)/shard_map/sum1_from_layer_2/ppermute | solution.py:185
  60.0 6.8 %collective-permute-start.25 = (bf16[1,320,128]{2,1,0:T(8,128)(2,1)S(1)}, bf16[1,320,128]{2,1,0:T(8,128)(2,1)S(1)}, u32[]{:S(2)}, u32[]{:S(2)}) collective-permute-start(bf16[1,320,128]{2,1,0:T(8,128)(2,1)S(1)} %get-tuple-element.51), channel_id=1, source_target_pairs={{0,2},{1,3},{2,0},{3,1},{4,6},{5,7},{6,4},{7,5},{8,10},{9,11},{10,... | collective-permute-start | bytes 245768 | tf_op jit(solution)/shard_map/sum2_from_layer_2/ppermute | solution.py:185
  61.8 5.6 %collective-permute-start.26 = (bf16[1,320,128]{2,1,0:T(8,128)(2,1)S(1)}, bf16[1,320,128]{2,1,0:T(8,128)(2,1)S(1)}, u32[]{:S(2)}, u32[]{:S(2)}) collective-permute-start(bf16[1,320,128]{2,1,0:T(8,128)(2,1)S(1)} %get-tuple-element.52), channel_id=1, source_target_pairs={{0,1},{1,0},{2,3},{3,2},{4,5},{5,4},{6,7},{7,6},{8,9},{9,8},{10,11... | collective-permute-start | bytes 245768 | tf_op jit(solution)/shard_map/last0_from_layer_1/ppermute | solution.py:185
  64.3 8.8 %collective-permute-start.27 = (bf16[1,320,128]{2,1,0:T(8,128)(2,1)S(1)}, bf16[1,320,128]{2,1,0:T(8,128)(2,1)S(1)}, u32[]{:S(2)}, u32[]{:S(2)}) collective-permute-start(bf16[1,320,128]{2,1,0:T(8,128)(2,1)S(1)} %get-tuple-element.53), channel_id=1, source_target_pairs={{0,2},{1,3},{2,0},{3,1},{4,6},{5,7},{6,4},{7,5},{8,10},{9,11},{10,... | collective-permute-start | bytes 245768 | tf_op jit(solution)/shard_map/last0_from_layer_2/ppermute | solution.py:185
  64.3 8.7 %collective-permute-start.28 = (bf16[1,320,128]{2,1,0:T(8,128)(2,1)S(1)}, bf16[1,320,128]{2,1,0:T(8,128)(2,1)S(1)}, u32[]{:S(2)}, u32[]{:S(2)}) collective-permute-start(bf16[1,320,128]{2,1,0:T(8,128)(2,1)S(1)} %get-tuple-element.54), channel_id=1, source_target_pairs={{0,3},{1,2},{2,1},{3,0},{4,7},{5,6},{6,5},{7,4},{8,11},{9,10},{10,... | collective-permute-start | bytes 245768 | tf_op jit(solution)/shard_map/last0_from_layer_3/ppermute | solution.py:185

commit v10 on v9

--- a/solution.py
+++ b/solution.py
@@ -91,40 +91,40 @@
     )(*place, hess, *pieces, after)
 
 
-def score_kernel(sizes, direct, *refs):
+def score_kernel(sizes, columns, *refs):
     place, (store, *rest) = refs[:3], refs[3:]
     ids, blocks, _ = positions(*sizes, place)
-    layers = len(blocks)
-    pieces, (_, *outs, right) = rest[: len(ids)], rest[len(ids) :]
+    layers, count = len(blocks), len(ids)
+    pieces, (_, *outs, right) = rest[: columns * count], rest[columns * count :]
     rows = store.shape[0] // layers
-    depth = pieces[0].shape[0]
-    for t, piece in zip(ids, pieces):
-        right[pl.ds(pl.multiple_of(t * depth, depth), depth), :] = piece[...]
+    depth, width = pieces[0].shape
+    for i, piece in enumerate(pieces):
+        at = pl.ds(pl.multiple_of(ids[i % count] * depth, depth), depth)
+        right[at, i // count * width : (i // count + 1) * width] = piece[...]
     for r in [*range(1, layers, 2), *range(0, layers, 2)]:
         at = pl.ds(pl.multiple_of(blocks[r] * rows, rows), rows)
         part = jnp.dot(store[at, :], right[...], preferred_element_type=F32)
-        if direct:
-            outs[r][0] = part.astype(outs[r].dtype)
-        else:
-            outs[1 - r % 2][r // 2] = part.astype(outs[1 - r % 2].dtype)
-
-
-def score(name, sizes, place, store, pieces, after, direct=False):
-    depth, width = pieces[0].shape
-    layers = sizes[2]
+        for c in range(columns):
+            out = outs[2 * c + 1 - r % 2]
+            out[r // 2] = part[:, c * width : (c + 1) * width].astype(out.dtype)
+
+
+def score(name, sizes, place, store, pieces, after):
+    depth, width = pieces[0][0].shape
+    layers, columns = sizes[2], len(pieces)
     rows = store.shape[0] // layers
-    shapes = [((layers // 2, rows, width), t) for t in (BF16, F32)]
-    if direct:
-        shapes = [((1, rows, width), BF16 if r else F32) for r in range(layers)]
-    return pl.pallas_call(
-        functools.partial(score_kernel, sizes, direct),
+    shapes = [((layers // 2, rows, width), t) for t in (BF16, F32)] * columns
+    flat = [x for xs in pieces for x in xs]
+    made = pl.pallas_call(
+        functools.partial(score_kernel, sizes, columns),
         out_shape=[pltpu.VMEM(*shape) for shape in shapes],
-        in_specs=[SMEM] * 3 + [VMEM] * (1 + len(pieces)) + [ANY],
+        in_specs=[SMEM] * 3 + [VMEM] * (1 + len(flat)) + [ANY],
         out_specs=[VMEM] * len(shapes),
-        scratch_shapes=[pltpu.VMEM((len(pieces) * depth, width), BF16)],
+        scratch_shapes=[pltpu.VMEM((store.shape[1], columns * width), BF16)],
         compiler_params=pltpu.CompilerParams(vmem_limit_bytes=12 * MIB),
         name=name,
-    )(*place, store, *pieces, after)
+    )(*place, store, *flat, after)
+    return [made[2 * c : 2 * c + 2] for c in range(columns)]
 
 
 def fold_kernel(keep, got, _, send, left):
@@ -228,10 +228,11 @@
                 part[:] = keep, from_layer(send, step, f"sum{i}")
 
     def send_parts(made):
-        send, keep = made
-        advance(keep, chain=True)
-        parts.append([keep, from_layer(send, 1, f"sum{len(parts)}")])
-        return parts[-2][0] if parts[1:] else keep
+        first = len(parts)
+        advance(made[-1][1])
+        for send, keep in made:
+            parts.append([keep, from_layer(send, 1, f"sum{len(parts)}")])
+        return parts[first - 1][0] if first else made[-1][1]
 
     rows = pltpu.with_memory_space_constraint(store[:, 0, :], pltpu.VMEM)
     width = total // groups // CHUNKS
@@ -252,28 +253,27 @@
     s1_there, s1_core = gather_chip(s1, "s1"), from_core(s1, "s1")
     s0_across = after(s1, s0_across)
     s0_across_cores = flip(s0_across, "s0_across")
-    last = send_parts(score("score0", sizes, place, rows, with_cores([s0] + s0_there, s0_cores), s1))
+    last = send_parts(score("score0", sizes, place, rows, [with_cores([s0] + s0_there, s0_cores)], s1))
     s0_diagonal = [after(last, xs) for xs in s0_diagonal]
     s0_diagonal_cores = [flip(xs, "s0_diagonal") for xs in s0_diagonal]
-    s1_across = gather_group(tie(s1, s0_diagonal[-1][-1]), "s1")
+    s1_across = gather_group(s1, "s1")
     s1_there = after(last, s1_there)
+    s1_across = after(last, s1_across)
+    s1_across_cores = flip(s1_across, "s1_across")
     s1_diagonal = [gather_group(x, "s1_there") for x in s1_there]
     s1_cores = [s1_core] + flip(s1_there, "s1_there")
     for j in range(groups - 1):
         ours = [s0_across[j]] + [xs[j] for xs in s0_diagonal]
         theirs = [s0_across_cores[j]] + [xs[j] for xs in s0_diagonal_cores]
-        last = send_parts(score("score1", sizes, place, rows, with_cores(ours, theirs), last))
-    last = send_parts(score("score2", sizes, place, rows, with_cores([s1] + s1_there, s1_cores), last))
-    s1_across = after(last, s1_across)
-    s1_across_cores = flip(s1_across, "s1_across")
+        last = send_parts(score("score1", sizes, place, rows, [with_cores(ours, theirs)], tie(last, *s1_across)))
     s1_diagonal = [after(last, xs) for xs in s1_diagonal]
     s1_diagonal_cores = [flip(xs, "s1_diagonal") for xs in s1_diagonal]
+    pieces = [with_cores([s1] + s1_there, s1_cores)]
     for j in range(groups - 1):
         ours = [s1_across[j]] + [xs[j] for xs in s1_diagonal]
         theirs = [s1_across_cores[j]] + [xs[j] for xs in s1_diagonal_cores]
-        made = score("score3", sizes, place, rows, with_cores(ours, theirs), last, direct=True)
-        advance(made[0])
-        parts.append([made[0]] + [from_layer(made[r], r, f"last{j}") for r in range(1, layers)])
+        pieces.append(with_cores(ours, theirs))
+    last = send_parts(score("score2", sizes, place, rows, pieces, last))
     while any(part[0].shape[0] > 1 for part in parts):
         advance(last)
     return finish(sizes, place, parts, total)

time: 74.2 us -> 72.8 us (0.981)
  waiting for transfers between devices: 19.7 us -> 28.3 us
  starting transfers between devices: 31.1 us -> 23.7 us
  Pallas kernels: 22.9 us -> 20.4 us
    ppermute x29 -> x28, waiting for transfers between devices: 19.7 us -> 28.3 us  [permute(): return lax.ppermute(x, axis, perm)]
    ppermute x29 -> x28, starting transfers between devices: 31.1 us -> 23.7 us  [permute(): return lax.ppermute(x, axis, perm)]
    pallas_call x4 -> x3, Pallas kernels: 11.8 us -> 9.17 us  [score(): pl.pallas_call(functools.partial(score_kernel, sizes, columns), out_shape...]
  transfers between devices with their start and end apart: 29 -> 28, of which waited for: 11 -> 10; matrix products, arithmetic and copies ran while one was open for 0% -> 0% of each run, Pallas kernels for 28% -> 25%
where the time goes in v10:
time: 72.8 us; the launch traced here: 72.6 us
  waiting for transfers between devices  28.3 us (39%)
  starting transfers between devices  23.7 us (33%)
  Pallas kernels  20.4 us (28%)
    ppermute x28, waiting for transfers between devices, permute(): return lax.ppermute(x, axis, perm)  28.3 us
    ppermute x28, starting transfers between devices, permute(): return lax.ppermute(x, axis, perm)  23.7 us
    pallas_call x3, Pallas kernels, score(): pl.pallas_call(functools.partial(score_kernel, sizes, columns), out_shape...  9.17 us
    pallas_call x2, Pallas kernels, condition(): pl.pallas_call(functools.partial(condition_kernel, sizes), out_shape=pltp...  4.82 us
    pallas_call x1, Pallas kernels, load(): pl.pallas_call(load_kernel, out_shape=pltpu.VMEM(source.shape, BF16), in_...  3.39 us
    pallas_call x2, Pallas kernels, take(): pl.pallas_call(functools.partial(take_kernel, chunk), out_shape=pltpu.VME...  1.92 us
  transfers between devices with their start and end apart: 28, of which 10 were waited for; matrix products, arithmetic and copies ran while one was open for 0% of the time, Pallas kernels for 25%

profile of v10, /device:TPU:0, one launch (start us, length us, event | category | flops | bytes accessed | tf_op | source)
XLA Modules:
  0.0 72.6 jit_solution(1340426726741106599)
XLA Ops:
  0.0 1.0 %take.2.after.refs_4_ = bf16[128,1024]{1,0:T(8,128)(2,1)S(1)} custom-call(s32[1]{0:T(128)} %bitcast.at_group.after.refs_0_, s32[1]{0:T(128)} %bitcast.1.at_ex.refs_1_, s32[1]{0:T(128)} %bitcast.2.at_layer.refs_2_, bf16[512,1024]{1,0:T(8,128)(2,1)} %bitcast.12, s32[1]{0:T(128)} %bitcast.at_group.after.refs_0_), custom_call_target="tpu_custom_call" | custom-call | tf_op jit(solution)/shard_map/take/pallas_call | solution.py:58
  1.0 3.0 %collective-permute-start.1 = (bf16[128,1024]{1,0:T(8,128)(2,1)S(1)}, bf16[128,1024]{1,0:T(8,128)(2,1)S(1)}, u32[]{:S(2)}, u32[]{:S(2)}) collective-permute-start(bf16[128,1024]{1,0:T(8,128)(2,1)S(1)} %take.2.after.refs_4_), channel_id=1, source_target_pairs={{0,8},{4,12},{8,0},{12,4},{1,9},{5,13},{9,1},{13,5},{2,10},{6,14},... | collective-permute-start | bytes 786440 | tf_op jit(solution)/shard_map/q0_from_chip/ppermute | solution.py:185
  4.0 0.0 collective-permute-start
  4.0 3.4 %load.1.after.refs_3_ = bf16[1024,4096]{1,0:T(8,128)(2,1)S(1)} custom-call(bf16[1024,4096]{1,0:T(8,128)(2,1)} %bitcast.11, bf16[128,1024]{1,0:T(8,128)(2,1)S(1)} %take.2.after.refs_4_), custom_call_target="tpu_custom_call" | custom-call | tf_op jit(solution)/shard_map/load/pallas_call | solution.py:38
  7.4 1.0 %take.3.refs_8_.refs_4_ = bf16[128,1024]{1,0:T(8,128)(2,1)S(1)} custom-call(s32[1]{0:T(128)} %bitcast.at_group.after.refs_0_, s32[1]{0:T(128)} %bitcast.1.at_ex.refs_1_, s32[1]{0:T(128)} %bitcast.2.at_layer.refs_2_, bf16[512,1024]{1,0:T(8,128)(2,1)} %bitcast.13, bf16[1024,4096]{1,0:T(8,128)(2,1)S(1)} %load.1.after.refs_3_), custom_call_target="tpu_custom_call" | custom-call | tf_op jit(solution)/shard_map/take/pallas_call | solution.py:58
  8.4 0.0 slice-start
  8.4 0.0 slice-start.1
  8.4 1.9 %collective-permute-done.1.refs_6_ = bf16[128,1024]{1,0:T(8,128)(2,1)S(1)} collective-permute-done((bf16[128,1024]{1,0:T(8,128)(2,1)S(1)}, bf16[128,1024]{1,0:T(8,128)(2,1)S(1)}, u32[]{:S(2)}, u32[]{:S(2)}) %collective-permute-start.1) | collective-permute-done | bytes 262176 | tf_op jit(solution)/shard_map/q0_from_chip/ppermute | solution.py:185
  10.3 1.7 %collective-permute-start.7 = (bf16[128,1024]{1,0:T(8,128)(2,1)S(1)}, bf16[128,1024]{1,0:T(8,128)(2,1)S(1)}, u32[]{:S(2)}, u32[]{:S(2)}) collective-permute-start(bf16[128,1024]{1,0:T(8,128)(2,1)S(1)} %take.3.refs_8_.refs_4_), channel_id=1, source_target_pairs={{0,8},{4,12},{8,0},{12,4},{1,9},{5,13},{9,1},{13,5},{2,10},{6,14},... | collective-permute-start | bytes 786440 | tf_op jit(solution)/shard_map/q1_from_chip/ppermute | solution.py:185
  12.0 0.0 collective-permute-done.refs_5_
  12.1 0.0 collective-permute-done.2.refs_7_
  12.1 2.4 %condition.2.refs_4_ = bf16[1024,128]{1,0:T(8,128)(2,1)S(1)} custom-call(s32[1]{0:T(128)} %bitcast.at_group.after.refs_0_, s32[1]{0:T(128)} %bitcast.1.at_ex.refs_1_, s32[1]{0:T(128)} %bitcast.2.at_layer.refs_2_, bf16[1024,4096]{1,0:T(8,128)(2,1)S(1)} %load.1.after.refs_3_, bf16[128,1024]{1,0:T(8,128)(2,1)S(1)} %take.2.after.refs_4_, ...), custom_call_target="tpu_custom_call" | custom-call | tf_op jit(solution)/shard_map/condition/pallas_call | solution.py:83
  14.5 0.0 slice-start.2
  14.5 1.6 %collective-permute-start.4 = (bf16[1024,128]{1,0:T(8,128)(2,1)S(1)}, bf16[1024,128]{1,0:T(8,128)(2,1)S(1)}, u32[]{:S(2)}, u32[]{:S(2)}) collective-permute-start(bf16[1024,128]{1,0:T(8,128)(2,1)S(1)} %condition.2.refs_4_), channel_id=1, source_target_pairs={{0,8},{4,12},{8,0},{12,4},{1,9},{5,13},{9,1},{13,5},{2,10},{6,14},... | collective-permute-start | bytes 786440 | tf_op jit(solution)/shard_map/s0_from_chip/ppermute | solution.py:185
  16.1 3.3 %collective-permute-done.7.refs_6_ = bf16[128,1024]{1,0:T(8,128)(2,1)S(1)} collective-permute-done((bf16[128,1024]{1,0:T(8,128)(2,1)S(1)}, bf16[128,1024]{1,0:T(8,128)(2,1)S(1)}, u32[]{:S(2)}, u32[]{:S(2)}) %collective-permute-start.7) | collective-permute-done | bytes 262176 | tf_op jit(solution)/shard_map/q1_from_chip/ppermute | solution.py:185
  19.4 0.0 collective-permute-start.8
  19.4 1.7 %collective-permute-start.10 = (bf16[1024,128]{1,0:T(8,128)(2,1)S(1)}, bf16[1024,128]{1,0:T(8,128)(2,1)S(1)}, u32[]{:S(2)}, u32[]{:S(2)}) collective-permute-start(bf16[1024,128]{1,0:T(8,128)(2,1)S(1)} %condition.2.refs_4_), channel_id=1, source_target_pairs={{0,16},{16,0},{1,17},{17,1},{2,18},{18,2},{3,19},{19,3},{4,20},{20... | collective-permute-start | bytes 786440 | tf_op jit(solution)/shard_map/s0_from_group/ppermute | solution.py:185
  21.1 0.2 collective-permute-start.3
  21.4 3.3 %collective-permute-done.4.refs_8_.refs_6_ = bf16[1024,128]{1,0:T(8,128)(2,1)S(1)} collective-permute-done((bf16[1024,128]{1,0:T(8,128)(2,1)S(1)}, bf16[1024,128]{1,0:T(8,128)(2,1)S(1)}, u32[]{:S(2)}, u32[]{:S(2)}) %collective-permute-start.4) | collective-permute-done | bytes 262176 | tf_op jit(solution)/shard_map/s0_from_chip/ppermute | solution.py:185
  24.6 0.0 collective-permute-done.6.refs_5_
  24.7 1.7 %collective-permute-start.12 = (bf16[1024,128]{1,0:T(8,128)(2,1)S(1)}, bf16[1024,128]{1,0:T(8,128)(2,1)S(1)}, u32[]{:S(2)}, u32[]{:S(2)}) collective-permute-start(bf16[1024,128]{1,0:T(8,128)(2,1)S(1)} %collective-permute-done.4.refs_8_.refs_6_), channel_id=1, source_target_pairs={{0,16},{16,0},{1,17},{17,1},{2,18},{18,2},{3,19},{19,3},{4,20},{20... | collective-permute-start | bytes 786440 | tf_op jit(solution)/shard_map/s0_there_from_group/ppermute | solution.py:185
  26.4 2.4 %condition.3.refs_8_.refs_4_ = bf16[1024,128]{1,0:T(8,128)(2,1)S(1)} custom-call(s32[1]{0:T(128)} %bitcast.at_group.after.refs_0_, s32[1]{0:T(128)} %bitcast.1.at_ex.refs_1_, s32[1]{0:T(128)} %bitcast.2.at_layer.refs_2_, bf16[1024,4096]{1,0:T(8,128)(2,1)S(1)} %load.1.after.refs_3_, bf16[128,1024]{1,0:T(8,128)(2,1)S(1)} %take.3.refs_8_.refs_4_, ...), custom_call_target="tpu_custom_call" | custom-call | tf_op jit(solution)/shard_map/condition/pallas_call | solution.py:83
  28.8 1.6 %collective-permute-start.18 = (bf16[1024,128]{1,0:T(8,128)(2,1)S(1)}, bf16[1024,128]{1,0:T(8,128)(2,1)S(1)}, u32[]{:S(2)}, u32[]{:S(2)}) collective-permute-start(bf16[1024,128]{1,0:T(8,128)(2,1)S(1)} %condition.3.refs_8_.refs_4_), channel_id=1, source_target_pairs={{0,8},{4,12},{8,0},{12,4},{1,9},{5,13},{9,1},{13,5},{2,10},{6,14},... | collective-permute-start | bytes 786440 | tf_op jit(solution)/shard_map/s1_from_chip/ppermute | solution.py:185
  30.4 0.0 collective-permute-done.10.refs_4_
  30.4 0.5 collective-permute-start.14
  31.0 3.0 %score0.1 = (bf16[2,320,128]{2,1,0:T(8,128)(2,1)S(1)}, f32[2,320,128]{2,1,0:T(8,128)S(1)}) custom-call(s32[1]{0:T(128)} %bitcast.at_group.after.refs_0_, s32[1]{0:T(128)} %bitcast.1.at_ex.refs_1_, s32[1]{0:T(128)} %bitcast.2.at_layer.refs_2_, bf16[1280,4096]{1,0:T(8,128)(2,1)S(1)} %bitcast.8, bf16[1024,128]{1,0:T(8,128)(2,1)S(1)} %condition.2.refs_4_, ...), custom_call_target="tpu_custom_call" | custom-call | tf_op jit(solution)/shard_map/score0/pallas_call | solution.py:118
  33.9 0.1 collective-permute-done.12.refs_6_
  34.1 0.4 collective-permute-start.13
  34.5 2.8 %collective-permute-done.18.refs_6_ = bf16[1024,128]{1,0:T(8,128)(2,1)S(1)} collective-permute-done((bf16[1024,128]{1,0:T(8,128)(2,1)S(1)}, bf16[1024,128]{1,0:T(8,128)(2,1)S(1)}, u32[]{:S(2)}, u32[]{:S(2)}) %collective-permute-start.18) | collective-permute-done | bytes 262176 | tf_op jit(solution)/shard_map/s1_from_chip/ppermute | solution.py:185
  37.3 0.3 collective-permute-start.21
  37.6 1.8 %collective-permute-start.9 = (bf16[2,320,128]{2,1,0:T(8,128)(2,1)S(1)}, bf16[2,320,128]{2,1,0:T(8,128)(2,1)S(1)}, u32[]{:S(2)}, u32[]{:S(2)}) collective-permute-start(bf16[2,320,128]{2,1,0:T(8,128)(2,1)S(1)} %get-tuple-element.32), channel_id=1, source_target_pairs={{0,1},{1,0},{2,3},{3,2},{4,5},{5,4},{6,7},{7,6},{8,9},{9,8},{10,11... | collective-permute-start | bytes 491528 | tf_op jit(solution)/shard_map/sum0_from_layer_1/ppermute | solution.py:185
  39.4 0.5 collective-permute-start.19
  39.9 0.1 collective-permute-start.20
  40.0 3.0 %score1.1 = (bf16[2,320,128]{2,1,0:T(8,128)(2,1)S(1)}, f32[2,320,128]{2,1,0:T(8,128)S(1)}) custom-call(s32[1]{0:T(128)} %bitcast.at_group.after.refs_0_, s32[1]{0:T(128)} %bitcast.1.at_ex.refs_1_, s32[1]{0:T(128)} %bitcast.2.at_layer.refs_2_, bf16[1280,4096]{1,0:T(8,128)(2,1)S(1)} %bitcast.9, bf16[1024,128]{1,0:T(8,128)(2,1)S(1)} %collective-permute-done.10.refs_4_, ...), custom_call_target="tpu_custom_call" | custom-call | tf_op jit(solution)/shard_map/score1/pallas_call | solution.py:118
  43.0 2.0 %collective-permute-done.21.refs_10_ = bf16[1024,128]{1,0:T(8,128)(2,1)S(1)} collective-permute-done((bf16[1024,128]{1,0:T(8,128)(2,1)S(1)}, bf16[1024,128]{1,0:T(8,128)(2,1)S(1)}, u32[]{:S(2)}, u32[]{:S(2)}) %collective-permute-start.21) | collective-permute-done | bytes 262176 | tf_op jit(solution)/shard_map/s1_there_from_group/ppermute | solution.py:185
  45.0 1.8 %collective-permute-start.16 = (bf16[2,320,128]{2,1,0:T(8,128)(2,1)S(1)}, bf16[2,320,128]{2,1,0:T(8,128)(2,1)S(1)}, u32[]{:S(2)}, u32[]{:S(2)}) collective-permute-start(bf16[2,320,128]{2,1,0:T(8,128)(2,1)S(1)} %get-tuple-element.40), channel_id=1, source_target_pairs={{0,1},{1,0},{2,3},{3,2},{4,5},{5,4},{6,7},{7,6},{8,9},{9,8},{10,11... | collective-permute-start | bytes 491528 | tf_op jit(solution)/shard_map/sum1_from_layer_1/ppermute | solution.py:185
  46.8 3.3 %score2.1 = (bf16[2,320,128]{2,1,0:T(8,128)(2,1)S(1)}, f32[2,320,128]{2,1,0:T(8,128)S(1)}, bf16[2,320,128]{2,1,0:T(8,128)(2,1)S(1)}, f32[2,320,128]{2,1,0:T(8,128)S(1)}) custom-call(s32[1]{0:T(128)} %bitcast.at_group.after.refs_0_, s32[1]{0:T(128)} %bitcast.1.at_ex.refs_1_, s32[1]{0:T(128)} %bitcast.2.at_layer.refs_2_, bf16[1280,4096]{1,0:T(8,128)(2,1)S(1)} %bitcast.10, ...), custom_call_target="tpu_custom_call" | custom-call | tf_op jit(solution)/shard_map/score2/pallas_call | solution.py:118
  50.1 1.6 %collective-permute-start.26 = (bf16[2,320,128]{2,1,0:T(8,128)(2,1)S(1)}, bf16[2,320,128]{2,1,0:T(8,128)(2,1)S(1)}, u32[]{:S(2)}, u32[]{:S(2)}) collective-permute-start(bf16[2,320,128]{2,1,0:T(8,128)(2,1)S(1)} %get-tuple-element.50), channel_id=1, source_target_pairs={{0,1},{1,0},{2,3},{3,2},{4,5},{5,4},{6,7},{7,6},{8,9},{9,8},{10,11... | collective-permute-start | bytes 491528 | tf_op jit(solution)/shard_map/sum3_from_layer_1/ppermute | solution.py:185
  51.7 0.5 collective-permute-start.24
  52.2 2.6 %collective-permute-start.15 = (bf16[1,320,128]{2,1,0:T(8,128)(2,1)S(1)}, bf16[1,320,128]{2,1,0:T(8,128)(2,1)S(1)}, u32[]{:S(2)}, u32[]{:S(2)}) collective-permute-start(bf16[1,320,128]{2,1,0:T(8,128)(2,1)S(1)} %get-tuple-element.39), channel_id=1, source_target_pairs={{0,2},{1,3},{2,0},{3,1},{4,6},{5,7},{6,4},{7,5},{8,10},{9,11},{10,... | collective-permute-start | bytes 245768 | tf_op jit(solution)/shard_map/sum0_from_layer_2/ppermute | solution.py:185
  54.8 0.4 collective-permute-start.23
  55.2 6.4 %collective-permute-done.26.got = bf16[2,320,128]{2,1,0:T(8,128)(2,1)S(1)} collective-permute-done((bf16[2,320,128]{2,1,0:T(8,128)(2,1)S(1)}, bf16[2,320,128]{2,1,0:T(8,128)(2,1)S(1)}, u32[]{:S(2)}, u32[]{:S(2)}) %collective-permute-start.26) | collective-permute-done | bytes 163872 | tf_op jit(solution)/shard_map/sum3_from_layer_1/ppermute | solution.py:185
  61.6 0.8 %collective-permute-start.27 = (bf16[1,320,128]{2,1,0:T(8,128)(2,1)S(1)}, bf16[1,320,128]{2,1,0:T(8,128)(2,1)S(1)}, u32[]{:S(2)}, u32[]{:S(2)}) collective-permute-start(bf16[1,320,128]{2,1,0:T(8,128)(2,1)S(1)} %get-tuple-element.52), channel_id=1, source_target_pairs={{0,2},{1,3},{2,0},{3,1},{4,6},{5,7},{6,4},{7,5},{8,10},{9,11},{10,... | collective-permute-start | bytes 245768 | tf_op jit(solution)/shard_map/sum3_from_layer_2/ppermute | solution.py:185
  62.4 2.0 %collective-permute-done.24.got = bf16[2,320,128]{2,1,0:T(8,128)(2,1)S(1)} collective-permute-done((bf16[2,320,128]{2,1,0:T(8,128)(2,1)S(1)}, bf16[2,320,128]{2,1,0:T(8,128)(2,1)S(1)}, u32[]{:S(2)}, u32[]{:S(2)}) %collective-permute-start.24) | collective-permute-done | bytes 163872 | tf_op jit(solution)/shard_map/sum2_from_layer_1/ppermute | solution.py:185
  64.4 0.8 %collective-permute-start.25 = (bf16[1,320,128]{2,1,0:T(8,128)(2,1)S(1)}, bf16[1,320,128]{2,1,0:T(8,128)(2,1)S(1)}, u32[]{:S(2)}, u32[]{:S(2)}) collective-permute-start(bf16[1,320,128]{2,1,0:T(8,128)(2,1)S(1)} %get-tuple-element.49), channel_id=1, source_target_pairs={{0,2},{1,3},{2,0},{3,1},{4,6},{5,7},{6,4},{7,5},{8,10},{9,11},{10,... | collective-permute-start | bytes 245768 | tf_op jit(solution)/shard_map/sum2_from_layer_2/ppermute | solution.py:185
  65.2 5.5 %collective-permute-done.27.refs_10_ = bf16[1,320,128]{2,1,0:T(8,128)(2,1)S(1)} collective-permute-done((bf16[1,320,128]{2,1,0:T(8,128)(2,1)S(1)}, bf16[1,320,128]{2,1,0:T(8,128)(2,1)S(1)}, u32[]{:S(2)}, u32[]{:S(2)}) %collective-permute-start.27) | collective-permute-done | bytes 81952 | tf_op jit(solution)/shard_map/sum3_from_layer_2/ppermute | solution.py:185
  70.7 1.0 %collective-permute-done.25.refs_8_ = bf16[1,320,128]{2,1,0:T(8,128)(2,1)S(1)} collective-permute-done((bf16[1,320,128]{2,1,0:T(8,128)(2,1)S(1)}, bf16[1,320,128]{2,1,0:T(8,128)(2,1)S(1)}, u32[]{:S(2)}, u32[]{:S(2)}) %collective-permute-start.25) | collective-permute-done | bytes 81952 | tf_op jit(solution)/shard_map/sum2_from_layer_2/ppermute | solution.py:185
  71.7 0.9 %finish.1 = f32[320,512]{1,0:T(8,128)} custom-call(s32[1]{0:T(128)} %bitcast.at_group.after.refs_0_, s32[1]{0:T(128)} %bitcast.1.at_ex.refs_1_, s32[1]{0:T(128)} %bitcast.2.at_layer.refs_2_, f32[1,320,128]{2,1,0:T(8,128)S(1)} %get-tuple-element.38.refs_12_.refs_3_, bf16[1,320,128]{2,1,0:T(8,128)(2,1)S(1)} %collective-permute-done.15.refs_4_, ...), custom_call_target="tpu_custom_call" | custom-call | tf_op jit(solution)/shard_map/finish/pallas_call | solution.py:167
  (28 shorter events, 0.2 us)
Async XLA Ops:
  1.0 9.3 %collective-permute-start.1 = (bf16[128,1024]{1,0:T(8,128)(2,1)S(1)}, bf16[128,1024]{1,0:T(8,128)(2,1)S(1)}, u32[]{:S(2)}, u32[]{:S(2)}) collective-permute-start(bf16[128,1024]{1,0:T(8,128)(2,1)S(1)} %take.2.after.refs_4_), channel_id=1, source_target_pairs={{0,8},{4,12},{8,0},{12,4},{1,9},{5,13},{9,1},{13,5},{2,10},{6,14},... | collective-permute-start | bytes 786440 | tf_op jit(solution)/shard_map/q0_from_chip/ppermute | solution.py:185
  4.0 8.1 %collective-permute-start = (bf16[128,1024]{1,0:T(8,128)(2,1)S(1)}, bf16[128,1024]{1,0:T(8,128)(2,1)S(1)}, u32[]{:S(2)}, u32[]{:S(2)}) collective-permute-start(bf16[128,1024]{1,0:T(8,128)(2,1)S(1)} %take.2.after.refs_4_), channel_id=1, source_target_pairs={{0,4},{4,0},{8,12},{12,8},{1,5},{5,1},{9,13},{13,9},{2,6},{6,2},{1... | collective-permute-start | bytes 786440 | tf_op jit(solution)/shard_map/q0_from_core/ppermute | solution.py:185
  8.4 22.5 %slice-start = ((s8[10485760]{0:T(1024)(128)(4,1)}), s8[4194304]{0:T(1024)(128)(4,1)S(1)}, s32[]{:S(2)}) async-start(s8[10485760]{0:T(1024)(128)(4,1)} %bitcast.6), calls=%async_computation | async-start | bytes 8388608
  8.4 22.5 %slice-start.1 = ((s8[10485760]{0:T(1024)(128)(4,1)}), s8[4194304]{0:T(1024)(128)(4,1)S(1)}, s32[]{:S(2)}) async-start(s8[10485760]{0:T(1024)(128)(4,1)} %bitcast.6), calls=%async_computation.1 | async-start | bytes 8388608
  10.3 1.8 %collective-permute-start.2 = (bf16[128,1024]{1,0:T(8,128)(2,1)S(1)}, bf16[128,1024]{1,0:T(8,128)(2,1)S(1)}, u32[]{:S(2)}, u32[]{:S(2)}) collective-permute-start(bf16[128,1024]{1,0:T(8,128)(2,1)S(1)} %collective-permute-done.1.refs_6_), channel_id=1, source_target_pairs={{0,4},{4,0},{8,12},{12,8},{1,5},{5,1},{9,13},{13,9},{2,6},{6,2},{1... | collective-permute-start | bytes 786440 | tf_op jit(solution)/shard_map/q0_there_from_core/ppermute | solution.py:185
  10.3 9.1 %collective-permute-start.7 = (bf16[128,1024]{1,0:T(8,128)(2,1)S(1)}, bf16[128,1024]{1,0:T(8,128)(2,1)S(1)}, u32[]{:S(2)}, u32[]{:S(2)}) collective-permute-start(bf16[128,1024]{1,0:T(8,128)(2,1)S(1)} %take.3.refs_8_.refs_4_), channel_id=1, source_target_pairs={{0,8},{4,12},{8,0},{12,4},{1,9},{5,13},{9,1},{13,5},{2,10},{6,14},... | collective-permute-start | bytes 786440 | tf_op jit(solution)/shard_map/q1_from_chip/ppermute | solution.py:185
  14.5 16.5 %slice-start.2 = ((s8[10485760]{0:T(1024)(128)(4,1)}), s8[2097152]{0:T(1024)(128)(4,1)S(1)}, s32[]{:S(2)}) async-start(s8[10485760]{0:T(1024)(128)(4,1)} %bitcast.6), calls=%async_computation.2 | async-start | bytes 4194304
  14.5 10.2 %collective-permute-start.4 = (bf16[1024,128]{1,0:T(8,128)(2,1)S(1)}, bf16[1024,128]{1,0:T(8,128)(2,1)S(1)}, u32[]{:S(2)}, u32[]{:S(2)}) collective-permute-start(bf16[1024,128]{1,0:T(8,128)(2,1)S(1)} %condition.2.refs_4_), channel_id=1, source_target_pairs={{0,8},{4,12},{8,0},{12,4},{1,9},{5,13},{9,1},{13,5},{2,10},{6,14},... | collective-permute-start | bytes 786440 | tf_op jit(solution)/shard_map/s0_from_chip/ppermute | solution.py:185
  16.1 8.6 %collective-permute-start.6 = (bf16[128,1024]{1,0:T(8,128)(2,1)S(1)}, bf16[128,1024]{1,0:T(8,128)(2,1)S(1)}, u32[]{:S(2)}, u32[]{:S(2)}) collective-permute-start(bf16[128,1024]{1,0:T(8,128)(2,1)S(1)} %take.3.refs_8_.refs_4_), channel_id=1, source_target_pairs={{0,4},{4,0},{8,12},{12,8},{1,5},{5,1},{9,13},{13,9},{2,6},{6,2},{1... | collective-permute-start | bytes 786440 | tf_op jit(solution)/shard_map/q1_from_core/ppermute | solution.py:185
  19.4 7.0 %collective-permute-start.8 = (bf16[128,1024]{1,0:T(8,128)(2,1)S(1)}, bf16[128,1024]{1,0:T(8,128)(2,1)S(1)}, u32[]{:S(2)}, u32[]{:S(2)}) collective-permute-start(bf16[128,1024]{1,0:T(8,128)(2,1)S(1)} %collective-permute-done.7.refs_6_), channel_id=1, source_target_pairs={{0,4},{4,0},{8,12},{12,8},{1,5},{5,1},{9,13},{13,9},{2,6},{6,2},{1... | collective-permute-start | bytes 786440 | tf_op jit(solution)/shard_map/q1_there_from_core/ppermute | solution.py:185
  19.4 11.0 %collective-permute-start.10 = (bf16[1024,128]{1,0:T(8,128)(2,1)S(1)}, bf16[1024,128]{1,0:T(8,128)(2,1)S(1)}, u32[]{:S(2)}, u32[]{:S(2)}) collective-permute-start(bf16[1024,128]{1,0:T(8,128)(2,1)S(1)} %condition.2.refs_4_), channel_id=1, source_target_pairs={{0,16},{16,0},{1,17},{17,1},{2,18},{18,2},{3,19},{19,3},{4,20},{20... | collective-permute-start | bytes 786440 | tf_op jit(solution)/shard_map/s0_from_group/ppermute | solution.py:185
  21.1 9.8 %collective-permute-start.3 = (bf16[1024,128]{1,0:T(8,128)(2,1)S(1)}, bf16[1024,128]{1,0:T(8,128)(2,1)S(1)}, u32[]{:S(2)}, u32[]{:S(2)}) collective-permute-start(bf16[1024,128]{1,0:T(8,128)(2,1)S(1)} %condition.2.refs_4_), channel_id=1, source_target_pairs={{0,4},{4,0},{8,12},{12,8},{1,5},{5,1},{9,13},{13,9},{2,6},{6,2},{1... | collective-permute-start | bytes 786440 | tf_op jit(solution)/shard_map/s0_from_core/ppermute | solution.py:185
  24.6 6.3 %collective-permute-start.5 = (bf16[1024,128]{1,0:T(8,128)(2,1)S(1)}, bf16[1024,128]{1,0:T(8,128)(2,1)S(1)}, u32[]{:S(2)}, u32[]{:S(2)}) collective-permute-start(bf16[1024,128]{1,0:T(8,128)(2,1)S(1)} %collective-permute-done.4.refs_8_.refs_6_), channel_id=1, source_target_pairs={{0,4},{4,0},{8,12},{12,8},{1,5},{5,1},{9,13},{13,9},{2,6},{6,2},{1... | collective-permute-start | bytes 786440 | tf_op jit(solution)/shard_map/s0_there_from_core/ppermute | solution.py:185
  24.7 9.4 %collective-permute-start.12 = (bf16[1024,128]{1,0:T(8,128)(2,1)S(1)}, bf16[1024,128]{1,0:T(8,128)(2,1)S(1)}, u32[]{:S(2)}, u32[]{:S(2)}) collective-permute-start(bf16[1024,128]{1,0:T(8,128)(2,1)S(1)} %collective-permute-done.4.refs_8_.refs_6_), channel_id=1, source_target_pairs={{0,16},{16,0},{1,17},{17,1},{2,18},{18,2},{3,19},{19,3},{4,20},{20... | collective-permute-start | bytes 786440 | tf_op jit(solution)/shard_map/s0_there_from_group/ppermute | solution.py:185
  28.8 8.5 %collective-permute-start.18 = (bf16[1024,128]{1,0:T(8,128)(2,1)S(1)}, bf16[1024,128]{1,0:T(8,128)(2,1)S(1)}, u32[]{:S(2)}, u32[]{:S(2)}) collective-permute-start(bf16[1024,128]{1,0:T(8,128)(2,1)S(1)} %condition.3.refs_8_.refs_4_), channel_id=1, source_target_pairs={{0,8},{4,12},{8,0},{12,4},{1,9},{5,13},{9,1},{13,5},{2,10},{6,14},... | collective-permute-start | bytes 786440 | tf_op jit(solution)/shard_map/s1_from_chip/ppermute | solution.py:185
  30.4 9.0 %collective-permute-start.14 = (bf16[1024,128]{1,0:T(8,128)(2,1)S(1)}, bf16[1024,128]{1,0:T(8,128)(2,1)S(1)}, u32[]{:S(2)}, u32[]{:S(2)}) collective-permute-start(bf16[1024,128]{1,0:T(8,128)(2,1)S(1)} %condition.3.refs_8_.refs_4_), channel_id=1, source_target_pairs={{0,16},{16,0},{1,17},{17,1},{2,18},{18,2},{3,19},{19,3},{4,20},{20... | collective-permute-start | bytes 786440 | tf_op jit(solution)/shard_map/s1_from_group/ppermute | solution.py:185
  30.9 8.5 %collective-permute-start.11 = (bf16[1024,128]{1,0:T(8,128)(2,1)S(1)}, bf16[1024,128]{1,0:T(8,128)(2,1)S(1)}, u32[]{:S(2)}, u32[]{:S(2)}) collective-permute-start(bf16[1024,128]{1,0:T(8,128)(2,1)S(1)} %collective-permute-done.10.refs_4_), channel_id=1, source_target_pairs={{0,4},{4,0},{8,12},{12,8},{1,5},{5,1},{9,13},{13,9},{2,6},{6,2},{1... | collective-permute-start | bytes 786440 | tf_op jit(solution)/shard_map/s0_across_from_core/ppermute | solution.py:185
  34.1 5.9 %collective-permute-start.13 = (bf16[1024,128]{1,0:T(8,128)(2,1)S(1)}, bf16[1024,128]{1,0:T(8,128)(2,1)S(1)}, u32[]{:S(2)}, u32[]{:S(2)}) collective-permute-start(bf16[1024,128]{1,0:T(8,128)(2,1)S(1)} %collective-permute-done.12.refs_6_), channel_id=1, source_target_pairs={{0,4},{4,0},{8,12},{12,8},{1,5},{5,1},{9,13},{13,9},{2,6},{6,2},{1... | collective-permute-start | bytes 786440 | tf_op jit(solution)/shard_map/s0_diagonal_from_core/ppermute | solution.py:185
  37.3 7.7 %collective-permute-start.21 = (bf16[1024,128]{1,0:T(8,128)(2,1)S(1)}, bf16[1024,128]{1,0:T(8,128)(2,1)S(1)}, u32[]{:S(2)}, u32[]{:S(2)}) collective-permute-start(bf16[1024,128]{1,0:T(8,128)(2,1)S(1)} %collective-permute-done.18.refs_6_), channel_id=1, source_target_pairs={{0,16},{16,0},{1,17},{17,1},{2,18},{18,2},{3,19},{19,3},{4,20},{20... | collective-permute-start | bytes 786440 | tf_op jit(solution)/shard_map/s1_there_from_group/ppermute | solution.py:185
  37.6 5.4 %collective-permute-start.9 = (bf16[2,320,128]{2,1,0:T(8,128)(2,1)S(1)}, bf16[2,320,128]{2,1,0:T(8,128)(2,1)S(1)}, u32[]{:S(2)}, u32[]{:S(2)}) collective-permute-start(bf16[2,320,128]{2,1,0:T(8,128)(2,1)S(1)} %get-tuple-element.32), channel_id=1, source_target_pairs={{0,1},{1,0},{2,3},{3,2},{4,5},{5,4},{6,7},{7,6},{8,9},{9,8},{10,11... | collective-permute-start | bytes 491528 | tf_op jit(solution)/shard_map/sum0_from_layer_1/ppermute | solution.py:185
  39.4 7.4 %collective-permute-start.17 = (bf16[1024,128]{1,0:T(8,128)(2,1)S(1)}, bf16[1024,128]{1,0:T(8,128)(2,1)S(1)}, u32[]{:S(2)}, u32[]{:S(2)}) collective-permute-start(bf16[1024,128]{1,0:T(8,128)(2,1)S(1)} %condition.3.refs_8_.refs_4_), channel_id=1, source_target_pairs={{0,4},{4,0},{8,12},{12,8},{1,5},{5,1},{9,13},{13,9},{2,6},{6,2},{1... | collective-permute-start | bytes 786440 | tf_op jit(solution)/shard_map/s1_from_core/ppermute | solution.py:185
  39.4 7.4 %collective-permute-start.19 = (bf16[1024,128]{1,0:T(8,128)(2,1)S(1)}, bf16[1024,128]{1,0:T(8,128)(2,1)S(1)}, u32[]{:S(2)}, u32[]{:S(2)}) collective-permute-start(bf16[1024,128]{1,0:T(8,128)(2,1)S(1)} %collective-permute-done.18.refs_6_), channel_id=1, source_target_pairs={{0,4},{4,0},{8,12},{12,8},{1,5},{5,1},{9,13},{13,9},{2,6},{6,2},{1... | collective-permute-start | bytes 786440 | tf_op jit(solution)/shard_map/s1_there_from_core/ppermute | solution.py:185
  39.9 6.9 %collective-permute-start.20 = (bf16[1024,128]{1,0:T(8,128)(2,1)S(1)}, bf16[1024,128]{1,0:T(8,128)(2,1)S(1)}, u32[]{:S(2)}, u32[]{:S(2)}) collective-permute-start(bf16[1024,128]{1,0:T(8,128)(2,1)S(1)} %collective-permute-done.14.refs_8_), channel_id=1, source_target_pairs={{0,4},{4,0},{8,12},{12,8},{1,5},{5,1},{9,13},{13,9},{2,6},{6,2},{1... | collective-permute-start | bytes 786440 | tf_op jit(solution)/shard_map/s1_across_from_core/ppermute | solution.py:185
  45.0 1.8 %collective-permute-start.22 = (bf16[1024,128]{1,0:T(8,128)(2,1)S(1)}, bf16[1024,128]{1,0:T(8,128)(2,1)S(1)}, u32[]{:S(2)}, u32[]{:S(2)}) collective-permute-start(bf16[1024,128]{1,0:T(8,128)(2,1)S(1)} %collective-permute-done.21.refs_10_), channel_id=1, source_target_pairs={{0,4},{4,0},{8,12},{12,8},{1,5},{5,1},{9,13},{13,9},{2,6},{6,2},{1... | collective-permute-start | bytes 786440 | tf_op jit(solution)/shard_map/s1_diagonal_from_core/ppermute | solution.py:185
  45.0 9.8 %collective-permute-start.16 = (bf16[2,320,128]{2,1,0:T(8,128)(2,1)S(1)}, bf16[2,320,128]{2,1,0:T(8,128)(2,1)S(1)}, u32[]{:S(2)}, u32[]{:S(2)}) collective-permute-start(bf16[2,320,128]{2,1,0:T(8,128)(2,1)S(1)} %get-tuple-element.40), channel_id=1, source_target_pairs={{0,1},{1,0},{2,3},{3,2},{4,5},{5,4},{6,7},{7,6},{8,9},{9,8},{10,11... | collective-permute-start | bytes 491528 | tf_op jit(solution)/shard_map/sum1_from_layer_1/ppermute | solution.py:185
  50.1 11.5 %collective-permute-start.26 = (bf16[2,320,128]{2,1,0:T(8,128)(2,1)S(1)}, bf16[2,320,128]{2,1,0:T(8,128)(2,1)S(1)}, u32[]{:S(2)}, u32[]{:S(2)}) collective-permute-start(bf16[2,320,128]{2,1,0:T(8,128)(2,1)S(1)} %get-tuple-element.50), channel_id=1, source_target_pairs={{0,1},{1,0},{2,3},{3,2},{4,5},{5,4},{6,7},{7,6},{8,9},{9,8},{10,11... | collective-permute-start | bytes 491528 | tf_op jit(solution)/shard_map/sum3_from_layer_1/ppermute | solution.py:185
  51.7 12.7 %collective-permute-start.24 = (bf16[2,320,128]{2,1,0:T(8,128)(2,1)S(1)}, bf16[2,320,128]{2,1,0:T(8,128)(2,1)S(1)}, u32[]{:S(2)}, u32[]{:S(2)}) collective-permute-start(bf16[2,320,128]{2,1,0:T(8,128)(2,1)S(1)} %get-tuple-element.47), channel_id=1, source_target_pairs={{0,1},{1,0},{2,3},{3,2},{4,5},{5,4},{6,7},{7,6},{8,9},{9,8},{10,11... | collective-permute-start | bytes 491528 | tf_op jit(solution)/shard_map/sum2_from_layer_1/ppermute | solution.py:185
  52.2 13.0 %collective-permute-start.15 = (bf16[1,320,128]{2,1,0:T(8,128)(2,1)S(1)}, bf16[1,320,128]{2,1,0:T(8,128)(2,1)S(1)}, u32[]{:S(2)}, u32[]{:S(2)}) collective-permute-start(bf16[1,320,128]{2,1,0:T(8,128)(2,1)S(1)} %get-tuple-element.39), channel_id=1, source_target_pairs={{0,2},{1,3},{2,0},{3,1},{4,6},{5,7},{6,4},{7,5},{8,10},{9,11},{10,... | collective-permute-start | bytes 245768 | tf_op jit(solution)/shard_map/sum0_from_layer_2/ppermute | solution.py:185
  54.8 10.4 %collective-permute-start.23 = (bf16[1,320,128]{2,1,0:T(8,128)(2,1)S(1)}, bf16[1,320,128]{2,1,0:T(8,128)(2,1)S(1)}, u32[]{:S(2)}, u32[]{:S(2)}) collective-permute-start(bf16[1,320,128]{2,1,0:T(8,128)(2,1)S(1)} %get-tuple-element.45), channel_id=1, source_target_pairs={{0,2},{1,3},{2,0},{3,1},{4,6},{5,7},{6,4},{7,5},{8,10},{9,11},{10,... | collective-permute-start | bytes 245768 | tf_op jit(solution)/shard_map/sum1_from_layer_2/ppermute | solution.py:185
  61.6 9.1 %collective-permute-start.27 = (bf16[1,320,128]{2,1,0:T(8,128)(2,1)S(1)}, bf16[1,320,128]{2,1,0:T(8,128)(2,1)S(1)}, u32[]{:S(2)}, u32[]{:S(2)}) collective-permute-start(bf16[1,320,128]{2,1,0:T(8,128)(2,1)S(1)} %get-tuple-element.52), channel_id=1, source_target_pairs={{0,2},{1,3},{2,0},{3,1},{4,6},{5,7},{6,4},{7,5},{8,10},{9,11},{10,... | collective-permute-start | bytes 245768 | tf_op jit(solution)/shard_map/sum3_from_layer_2/ppermute | solution.py:185
  64.4 7.3 %collective-permute-start.25 = (bf16[1,320,128]{2,1,0:T(8,128)(2,1)S(1)}, bf16[1,320,128]{2,1,0:T(8,128)(2,1)S(1)}, u32[]{:S(2)}, u32[]{:S(2)}) collective-permute-start(bf16[1,320,128]{2,1,0:T(8,128)(2,1)S(1)} %get-tuple-element.49), channel_id=1, source_target_pairs={{0,2},{1,3},{2,0},{3,1},{4,6},{5,7},{6,4},{7,5},{8,10},{9,11},{10,... | collective-permute-start | bytes 245768 | tf_op jit(solution)/shard_map/sum2_from_layer_2/ppermute | solution.py:185

commit v11 on v10

--- a/solution.py
+++ b/solution.py
@@ -69,54 +69,64 @@
 def condition_kernel(sizes, *refs):
     place, (hess, *rest) = refs[:3], refs[3:]
     ids, _, _ = positions(*sizes, place)
-    pieces, (_, out, right) = rest[: len(ids)], rest[len(ids) :]
+    pieces, (_, *outs, right) = rest[: len(ids)], rest[len(ids) :]
     width = pieces[0].shape[1]
     for t, piece in zip(ids, pieces):
         right[:, pl.ds(pl.multiple_of(t * width, width), width)] = piece[...]
-    out[...] = lax.dot_general(
+    height = hess.shape[0]
+    outs[0][...] = lax.dot_general(
         hess[...], right[...], (((1,), (1,)), ((), ())), preferred_element_type=F32
     ).astype(BF16)
-
-
-def condition(sizes, place, hess, pieces, after):
+    for out in outs[1:]:
+        out[:height, :] = outs[0][...]
+        out[height:, :] = jnp.zeros((out.shape[0] - height, out.shape[1]), BF16)
+
+
+def condition(sizes, place, hess, pieces, after, more):
     rows, queries = hess.shape[0], pieces[0].shape[0]
+    shapes = [(rows + count, queries) for count in (0, *more)]
     return pl.pallas_call(
         functools.partial(condition_kernel, sizes),
-        out_shape=pltpu.VMEM((rows, queries), BF16),
+        out_shape=[pltpu.VMEM(shape, BF16) for shape in shapes],
         in_specs=[SMEM] * 3 + [VMEM] * (1 + len(pieces)) + [ANY],
-        out_specs=VMEM,
+        out_specs=[VMEM] * len(shapes),
         scratch_shapes=[pltpu.VMEM((queries, hess.shape[1]), BF16)],
         compiler_params=pltpu.CompilerParams(vmem_limit_bytes=12 * MIB),
         name="condition",
     )(*place, hess, *pieces, after)
 
 
-def score_kernel(sizes, columns, *refs):
+def score_kernel(sizes, columns, direct, *refs):
     place, (store, *rest) = refs[:3], refs[3:]
     ids, blocks, _ = positions(*sizes, place)
     layers, count = len(blocks), len(ids)
     pieces, (_, *outs, right) = rest[: columns * count], rest[columns * count :]
     rows = store.shape[0] // layers
-    depth, width = pieces[0].shape
+    depth, width = store.shape[1] // count, pieces[0].shape[1]
     for i, piece in enumerate(pieces):
         at = pl.ds(pl.multiple_of(ids[i % count] * depth, depth), depth)
-        right[at, i // count * width : (i // count + 1) * width] = piece[...]
-    for r in [*range(1, layers, 2), *range(0, layers, 2)]:
+        right[at, i // count * width : (i // count + 1) * width] = piece[:depth, :]
+    for r in reversed(range(layers)) if direct else [*range(1, layers, 2), *range(0, layers, 2)]:
         at = pl.ds(pl.multiple_of(blocks[r] * rows, rows), rows)
         part = jnp.dot(store[at, :], right[...], preferred_element_type=F32)
+        if direct:
+            outs[r][0] = part.astype(outs[r].dtype)
+            continue
         for c in range(columns):
             out = outs[2 * c + 1 - r % 2]
             out[r // 2] = part[:, c * width : (c + 1) * width].astype(out.dtype)
 
 
-def score(name, sizes, place, store, pieces, after):
-    depth, width = pieces[0][0].shape
+def score(name, sizes, place, store, pieces, after, direct=False):
+    width = pieces[0][0].shape[1]
     layers, columns = sizes[2], len(pieces)
     rows = store.shape[0] // layers
     shapes = [((layers // 2, rows, width), t) for t in (BF16, F32)] * columns
+    if direct:
+        shapes = [((1, rows, columns * width), BF16 if r else F32) for r in range(layers)]
     flat = [x for xs in pieces for x in xs]
     made = pl.pallas_call(
-        functools.partial(score_kernel, sizes, columns),
+        functools.partial(score_kernel, sizes, columns, direct),
         out_shape=[pltpu.VMEM(*shape) for shape in shapes],
         in_specs=[SMEM] * 3 + [VMEM] * (1 + len(flat)) + [ANY],
         out_specs=[VMEM] * len(shapes),
@@ -124,7 +134,7 @@
         compiler_params=pltpu.CompilerParams(vmem_limit_bytes=12 * MIB),
         name=name,
     )(*place, store, *flat, after)
-    return [made[2 * c : 2 * c + 2] for c in range(columns)]
+    return made if direct else [made[2 * c : 2 * c + 2] for c in range(columns)]
 
 
 def fold_kernel(keep, got, _, send, left):
@@ -152,14 +162,18 @@
     place, (*refs, out) = refs[:3], refs[3:]
     _, _, order = positions(*sizes, place)
     groups = len(order)
-    width = refs[0].shape[2]
-    for i, count in enumerate(counts):
+    span = out.shape[1] // groups
+    width = span // CHUNKS
+    i = 0
+    for count in counts:
         (keep, *rest), refs = refs[:count], refs[count:]
         total = keep[0]
         for got in rest:
             total = total + got[0].astype(F32)
-        at = order[i % groups] * (out.shape[1] // groups) + i // groups * width
-        out[:, pl.ds(pl.multiple_of(at, width), width)] = total
+        for low in range(0, total.shape[1], width):
+            at = order[i % groups] * span + i // groups * width
+            out[:, pl.ds(pl.multiple_of(at, width), width)] = total[:, low : low + width]
+            i += 1
 
 
 def finish(sizes, place, parts, queries):
@@ -243,20 +257,20 @@
     q0_there = after(q1, q0_there)
     q0_cores = [q0_core] + flip(q0_there, "q0_there")
     q1_there, q1_core = gather_chip(q1, "q1"), from_core(q1, "q1")
-    s0 = condition(sizes, place, hess, with_cores([q0] + q0_there, q0_cores), q1)
-    s0_there, s0_across, s0_core = gather_chip(s0, "s0"), gather_group(s0, "s0"), from_core(s0, "s0")
+    s0, s0_long, s0_longer = condition(sizes, place, hess, with_cores([q0] + q0_there, q0_cores), q1, (16, 16))
+    s0_there, s0_across, s0_core = gather_chip(s0_long, "s0"), gather_group(s0_longer, "s0"), from_core(s0, "s0")
     q1_there = after(s0, q1_there)
     q1_cores = [q1_core] + flip(q1_there, "q1_there")
+    s1, s1_long = condition(sizes, place, hess, with_cores([q1] + q1_there, q1_cores), s0, (16,))
+    s1_there, s1_core = gather_chip(s1, "s1"), from_core(s1, "s1")
+    s0_there, s0_across = after(s1, s0_there), after(s1, s0_across)
     s0_diagonal = [gather_group(x, "s0_there") for x in s0_there]
     s0_cores = [s0_core] + flip(s0_there, "s0_there")
-    s1 = condition(sizes, place, hess, with_cores([q1] + q1_there, q1_cores), s0_there[-1])
-    s1_there, s1_core = gather_chip(s1, "s1"), from_core(s1, "s1")
-    s0_across = after(s1, s0_across)
     s0_across_cores = flip(s0_across, "s0_across")
     last = send_parts(score("score0", sizes, place, rows, [with_cores([s0] + s0_there, s0_cores)], s1))
     s0_diagonal = [after(last, xs) for xs in s0_diagonal]
     s0_diagonal_cores = [flip(xs, "s0_diagonal") for xs in s0_diagonal]
-    s1_across = gather_group(s1, "s1")
+    s1_across = gather_group(s1_long, "s1")
     s1_there = after(last, s1_there)
     s1_across = after(last, s1_across)
     s1_across_cores = flip(s1_across, "s1_across")

time: 72.8 us -> 73.1 us (level)
  starting transfers between devices: 23.7 us -> 24.7 us
  waiting for transfers between devices: 28.3 us -> 27.4 us
    ppermute x28, starting transfers between devices: 23.7 us -> 24.7 us  [permute(): return lax.ppermute(x, axis, perm)]
    ppermute x28, waiting for transfers between devices: 28.3 us -> 27.4 us  [permute(): return lax.ppermute(x, axis, perm)]
  transfers between devices with their start and end apart: 28 -> 28, of which waited for: 10 -> 12; matrix products, arithmetic and copies ran while one was open for 0% -> 0% of each run, Pallas kernels for 25% -> 26%
where the time goes in v11:
time: 73.1 us; the launch traced here: 72.9 us
  waiting for transfers between devices  27.4 us (37%)
  starting transfers between devices  24.7 us (34%)
  Pallas kernels  20.6 us (28%)
    ppermute x28, waiting for transfers between devices, permute(): return lax.ppermute(x, axis, perm)  27.4 us
    ppermute x28, starting transfers between devices, permute(): return lax.ppermute(x, axis, perm)  24.7 us
    pallas_call x3, Pallas kernels, score(): pl.pallas_call(functools.partial(score_kernel, sizes, columns, direct), o...  9.17 us
    pallas_call x2, Pallas kernels, condition(): pl.pallas_call(functools.partial(condition_kernel, sizes), out_shape=[plt...  5.01 us
    pallas_call x1, Pallas kernels, load(): pl.pallas_call(load_kernel, out_shape=pltpu.VMEM(source.shape, BF16), in_...  3.39 us
    pallas_call x2, Pallas kernels, take(): pl.pallas_call(functools.partial(take_kernel, chunk), out_shape=pltpu.VME...  1.92 us
  transfers between devices with their start and end apart: 28, of which 12 were waited for; matrix products, arithmetic and copies ran while one was open for 0% of the time, Pallas kernels for 26%

profile of v11, /device:TPU:0, one launch (start us, length us, event | category | flops | bytes accessed | tf_op | source)
XLA Modules:
  0.0 72.9 jit_solution(3102716623973306978)
XLA Ops:
  0.0 1.0 %take.2.after.refs_4_ = bf16[128,1024]{1,0:T(8,128)(2,1)S(1)} custom-call(s32[1]{0:T(128)} %bitcast.at_group.after.refs_0_, s32[1]{0:T(128)} %bitcast.1.at_ex.refs_1_, s32[1]{0:T(128)} %bitcast.2.at_layer.refs_2_, bf16[512,1024]{1,0:T(8,128)(2,1)} %bitcast.12, s32[1]{0:T(128)} %bitcast.at_group.after.refs_0_), custom_call_target="tpu_custom_call" | custom-call | tf_op jit(solution)/shard_map/take/pallas_call | solution.py:58
  1.0 3.0 %collective-permute-start.1 = (bf16[128,1024]{1,0:T(8,128)(2,1)S(1)}, bf16[128,1024]{1,0:T(8,128)(2,1)S(1)}, u32[]{:S(2)}, u32[]{:S(2)}) collective-permute-start(bf16[128,1024]{1,0:T(8,128)(2,1)S(1)} %take.2.after.refs_4_), channel_id=1, source_target_pairs={{0,8},{4,12},{8,0},{12,4},{1,9},{5,13},{9,1},{13,5},{2,10},{6,14},... | collective-permute-start | bytes 786440 | tf_op jit(solution)/shard_map/q0_from_chip/ppermute | solution.py:199
  4.0 0.0 collective-permute-start
  4.0 3.4 %load.1.after.refs_3_ = bf16[1024,4096]{1,0:T(8,128)(2,1)S(1)} custom-call(bf16[1024,4096]{1,0:T(8,128)(2,1)} %bitcast.11, bf16[128,1024]{1,0:T(8,128)(2,1)S(1)} %take.2.after.refs_4_), custom_call_target="tpu_custom_call" | custom-call | tf_op jit(solution)/shard_map/load/pallas_call | solution.py:38
  7.4 1.0 %take.3.refs_8_.refs_4_ = bf16[128,1024]{1,0:T(8,128)(2,1)S(1)} custom-call(s32[1]{0:T(128)} %bitcast.at_group.after.refs_0_, s32[1]{0:T(128)} %bitcast.1.at_ex.refs_1_, s32[1]{0:T(128)} %bitcast.2.at_layer.refs_2_, bf16[512,1024]{1,0:T(8,128)(2,1)} %bitcast.13, bf16[1024,4096]{1,0:T(8,128)(2,1)S(1)} %load.1.after.refs_3_), custom_call_target="tpu_custom_call" | custom-call | tf_op jit(solution)/shard_map/take/pallas_call | solution.py:58
  8.4 0.0 slice-start
  8.4 0.0 slice-start.1
  8.4 1.9 %collective-permute-done.1.refs_6_ = bf16[128,1024]{1,0:T(8,128)(2,1)S(1)} collective-permute-done((bf16[128,1024]{1,0:T(8,128)(2,1)S(1)}, bf16[128,1024]{1,0:T(8,128)(2,1)S(1)}, u32[]{:S(2)}, u32[]{:S(2)}) %collective-permute-start.1) | collective-permute-done | bytes 262176 | tf_op jit(solution)/shard_map/q0_from_chip/ppermute | solution.py:199
  10.3 1.7 %collective-permute-start.6 = (bf16[128,1024]{1,0:T(8,128)(2,1)S(1)}, bf16[128,1024]{1,0:T(8,128)(2,1)S(1)}, u32[]{:S(2)}, u32[]{:S(2)}) collective-permute-start(bf16[128,1024]{1,0:T(8,128)(2,1)S(1)} %take.3.refs_8_.refs_4_), channel_id=1, source_target_pairs={{0,8},{4,12},{8,0},{12,4},{1,9},{5,13},{9,1},{13,5},{2,10},{6,14},... | collective-permute-start | bytes 786440 | tf_op jit(solution)/shard_map/q1_from_chip/ppermute | solution.py:199
  12.0 0.0 collective-permute-done.refs_5_
  12.1 0.0 collective-permute-done.2.refs_7_
  12.1 2.5 %condition.2 = (bf16[1024,128]{1,0:T(8,128)(2,1)S(1)}, bf16[1040,128]{1,0:T(8,128)(2,1)S(1)}, bf16[1040,128]{1,0:T(8,128)(2,1)S(1)}) custom-call(s32[1]{0:T(128)} %bitcast.at_group.after.refs_0_, s32[1]{0:T(128)} %bitcast.1.at_ex.refs_1_, s32[1]{0:T(128)} %bitcast.2.at_layer.refs_2_, bf16[1024,4096]{1,0:T(8,128)(2,1)S(1)} %load.1.after.refs_3_, ...), custom_call_target="tpu_custom_call" | custom-call | tf_op jit(solution)/shard_map/condition/pallas_call | solution.py:88
  14.5 1.6 %collective-permute-start.4 = (bf16[1040,128]{1,0:T(8,128)(2,1)S(1)}, bf16[1040,128]{1,0:T(8,128)(2,1)S(1)}, u32[]{:S(2)}, u32[]{:S(2)}) collective-permute-start(bf16[1040,128]{1,0:T(8,128)(2,1)S(1)} %get-tuple-element.37), channel_id=1, source_target_pairs={{0,8},{4,12},{8,0},{12,4},{1,9},{5,13},{9,1},{13,5},{2,10},{6,14},... | collective-permute-start | bytes 798728 | tf_op jit(solution)/shard_map/s0_from_chip/ppermute | solution.py:199
  16.1 3.3 %collective-permute-done.6.refs_6_ = bf16[128,1024]{1,0:T(8,128)(2,1)S(1)} collective-permute-done((bf16[128,1024]{1,0:T(8,128)(2,1)S(1)}, bf16[128,1024]{1,0:T(8,128)(2,1)S(1)}, u32[]{:S(2)}, u32[]{:S(2)}) %collective-permute-start.6) | collective-permute-done | bytes 262176 | tf_op jit(solution)/shard_map/q1_from_chip/ppermute | solution.py:199
  19.4 0.0 collective-permute-start.7
  19.4 1.7 %collective-permute-start.10 = (bf16[1040,128]{1,0:T(8,128)(2,1)S(1)}, bf16[1040,128]{1,0:T(8,128)(2,1)S(1)}, u32[]{:S(2)}, u32[]{:S(2)}) collective-permute-start(bf16[1040,128]{1,0:T(8,128)(2,1)S(1)} %get-tuple-element.43), channel_id=1, source_target_pairs={{0,16},{16,0},{1,17},{17,1},{2,18},{18,2},{3,19},{19,3},{4,20},{20... | collective-permute-start | bytes 798728 | tf_op jit(solution)/shard_map/s0_from_group/ppermute | solution.py:199
  21.1 0.0 collective-permute-done.5.refs_5_
  21.1 0.0 collective-permute-done.7.refs_7_
  21.1 2.5 %condition.3 = (bf16[1024,128]{1,0:T(8,128)(2,1)S(1)}, bf16[1040,128]{1,0:T(8,128)(2,1)S(1)}) custom-call(s32[1]{0:T(128)} %bitcast.at_group.after.refs_0_, s32[1]{0:T(128)} %bitcast.1.at_ex.refs_1_, s32[1]{0:T(128)} %bitcast.2.at_layer.refs_2_, bf16[1024,4096]{1,0:T(8,128)(2,1)S(1)} %load.1.after.refs_3_, bf16[128,1024]{1,0:T(8,128)(2,1)S(1)} %take.3.refs_8_.refs_4_, ...), custom_call_target="tpu_custom_call" | custom-call | tf_op jit(solution)/shard_map/condition/pallas_call | solution.py:88
  23.7 1.1 %collective-permute-done.4.refs_6_ = bf16[1040,128]{1,0:T(8,128)(2,1)S(1)} collective-permute-done((bf16[1040,128]{1,0:T(8,128)(2,1)S(1)}, bf16[1040,128]{1,0:T(8,128)(2,1)S(1)}, u32[]{:S(2)}, u32[]{:S(2)}) %collective-permute-start.4) | collective-permute-done | bytes 266272 | tf_op jit(solution)/shard_map/s0_from_chip/ppermute | solution.py:199
  24.7 1.7 %collective-permute-start.12 = (bf16[1040,128]{1,0:T(8,128)(2,1)S(1)}, bf16[1040,128]{1,0:T(8,128)(2,1)S(1)}, u32[]{:S(2)}, u32[]{:S(2)}) collective-permute-start(bf16[1040,128]{1,0:T(8,128)(2,1)S(1)} %collective-permute-done.4.refs_6_), channel_id=1, source_target_pairs={{0,16},{16,0},{1,17},{17,1},{2,18},{18,2},{3,19},{19,3},{4,20},{20... | collective-permute-start | bytes 798728 | tf_op jit(solution)/shard_map/s0_there_from_group/ppermute | solution.py:199
  26.4 0.2 collective-permute-start.3
  26.7 1.5 %collective-permute-start.18 = (bf16[1024,128]{1,0:T(8,128)(2,1)S(1)}, bf16[1024,128]{1,0:T(8,128)(2,1)S(1)}, u32[]{:S(2)}, u32[]{:S(2)}) collective-permute-start(bf16[1024,128]{1,0:T(8,128)(2,1)S(1)} %get-tuple-element.39.refs_8_.refs_4_), channel_id=1, source_target_pairs={{0,8},{4,12},{8,0},{12,4},{1,9},{5,13},{9,1},{13,5},{2,10},{6,14},... | collective-permute-start | bytes 786440 | tf_op jit(solution)/shard_map/s1_from_chip/ppermute | solution.py:199
  28.2 0.3 collective-permute-done.10.refs_4_
  28.5 1.7 %collective-permute-start.14 = (bf16[1040,128]{1,0:T(8,128)(2,1)S(1)}, bf16[1040,128]{1,0:T(8,128)(2,1)S(1)}, u32[]{:S(2)}, u32[]{:S(2)}) collective-permute-start(bf16[1040,128]{1,0:T(8,128)(2,1)S(1)} %get-tuple-element.46), channel_id=1, source_target_pairs={{0,16},{16,0},{1,17},{17,1},{2,18},{18,2},{3,19},{19,3},{4,20},{20... | collective-permute-start | bytes 798728 | tf_op jit(solution)/shard_map/s1_from_group/ppermute | solution.py:199
  30.3 3.0 %score0.1 = (bf16[2,320,128]{2,1,0:T(8,128)(2,1)S(1)}, f32[2,320,128]{2,1,0:T(8,128)S(1)}) custom-call(s32[1]{0:T(128)} %bitcast.at_group.after.refs_0_, s32[1]{0:T(128)} %bitcast.1.at_ex.refs_1_, s32[1]{0:T(128)} %bitcast.2.at_layer.refs_2_, bf16[1280,4096]{1,0:T(8,128)(2,1)S(1)} %bitcast.8, bf16[1024,128]{1,0:T(8,128)(2,1)S(1)} %get-tuple-element.36.refs_8_.refs_4_, ...), custom_call_target="tpu_custom_call" | custom-call | tf_op jit(solution)/shard_map/score0/pallas_call | solution.py:128
  33.3 1.0 %collective-permute-done.12.refs_6_ = bf16[1040,128]{1,0:T(8,128)(2,1)S(1)} collective-permute-done((bf16[1040,128]{1,0:T(8,128)(2,1)S(1)}, bf16[1040,128]{1,0:T(8,128)(2,1)S(1)}, u32[]{:S(2)}, u32[]{:S(2)}) %collective-permute-start.12) | collective-permute-done | bytes 266272 | tf_op jit(solution)/shard_map/s0_there_from_group/ppermute | solution.py:199
  34.2 0.9 %collective-permute-done.18.refs_6_ = bf16[1024,128]{1,0:T(8,128)(2,1)S(1)} collective-permute-done((bf16[1024,128]{1,0:T(8,128)(2,1)S(1)}, bf16[1024,128]{1,0:T(8,128)(2,1)S(1)}, u32[]{:S(2)}, u32[]{:S(2)}) %collective-permute-start.18) | collective-permute-done | bytes 262176 | tf_op jit(solution)/shard_map/s1_from_chip/ppermute | solution.py:199
  35.2 0.8 %collective-permute-start.21 = (bf16[1024,128]{1,0:T(8,128)(2,1)S(1)}, bf16[1024,128]{1,0:T(8,128)(2,1)S(1)}, u32[]{:S(2)}, u32[]{:S(2)}) collective-permute-start(bf16[1024,128]{1,0:T(8,128)(2,1)S(1)} %collective-permute-done.18.refs_6_), channel_id=1, source_target_pairs={{0,16},{16,0},{1,17},{17,1},{2,18},{18,2},{3,19},{19,3},{4,20},{20... | collective-permute-start | bytes 786440 | tf_op jit(solution)/shard_map/s1_there_from_group/ppermute | solution.py:199
  36.0 1.6 %collective-permute-start.9 = (bf16[2,320,128]{2,1,0:T(8,128)(2,1)S(1)}, bf16[2,320,128]{2,1,0:T(8,128)(2,1)S(1)}, u32[]{:S(2)}, u32[]{:S(2)}) collective-permute-start(bf16[2,320,128]{2,1,0:T(8,128)(2,1)S(1)} %get-tuple-element.42), channel_id=1, source_target_pairs={{0,1},{1,0},{2,3},{3,2},{4,5},{5,4},{6,7},{7,6},{8,9},{9,8},{10,11... | collective-permute-start | bytes 491528 | tf_op jit(solution)/shard_map/sum0_from_layer_1/ppermute | solution.py:199
  37.5 2.4 %collective-permute-done.14.refs_8_ = bf16[1040,128]{1,0:T(8,128)(2,1)S(1)} collective-permute-done((bf16[1040,128]{1,0:T(8,128)(2,1)S(1)}, bf16[1040,128]{1,0:T(8,128)(2,1)S(1)}, u32[]{:S(2)}, u32[]{:S(2)}) %collective-permute-start.14) | collective-permute-done | bytes 266272 | tf_op jit(solution)/shard_map/s1_from_group/ppermute | solution.py:199
  40.0 0.5 collective-permute-start.17
  40.5 0.1 collective-permute-start.19
  40.5 2.9 %score1.1 = (bf16[2,320,128]{2,1,0:T(8,128)(2,1)S(1)}, f32[2,320,128]{2,1,0:T(8,128)S(1)}) custom-call(s32[1]{0:T(128)} %bitcast.at_group.after.refs_0_, s32[1]{0:T(128)} %bitcast.1.at_ex.refs_1_, s32[1]{0:T(128)} %bitcast.2.at_layer.refs_2_, bf16[1280,4096]{1,0:T(8,128)(2,1)S(1)} %bitcast.9, bf16[1040,128]{1,0:T(8,128)(2,1)S(1)} %collective-permute-done.10.refs_4_, ...), custom_call_target="tpu_custom_call" | custom-call | tf_op jit(solution)/shard_map/score1/pallas_call | solution.py:128
  43.5 1.7 %collective-permute-done.21.refs_10_ = bf16[1024,128]{1,0:T(8,128)(2,1)S(1)} collective-permute-done((bf16[1024,128]{1,0:T(8,128)(2,1)S(1)}, bf16[1024,128]{1,0:T(8,128)(2,1)S(1)}, u32[]{:S(2)}, u32[]{:S(2)}) %collective-permute-start.21) | collective-permute-done | bytes 262176 | tf_op jit(solution)/shard_map/s1_there_from_group/ppermute | solution.py:199
  45.3 1.8 %collective-permute-start.16 = (bf16[2,320,128]{2,1,0:T(8,128)(2,1)S(1)}, bf16[2,320,128]{2,1,0:T(8,128)(2,1)S(1)}, u32[]{:S(2)}, u32[]{:S(2)}) collective-permute-start(bf16[2,320,128]{2,1,0:T(8,128)(2,1)S(1)} %get-tuple-element.52), channel_id=1, source_target_pairs={{0,1},{1,0},{2,3},{3,2},{4,5},{5,4},{6,7},{7,6},{8,9},{9,8},{10,11... | collective-permute-start | bytes 491528 | tf_op jit(solution)/shard_map/sum1_from_layer_1/ppermute | solution.py:199
  47.1 3.3 %score2.1 = (bf16[2,320,128]{2,1,0:T(8,128)(2,1)S(1)}, f32[2,320,128]{2,1,0:T(8,128)S(1)}, bf16[2,320,128]{2,1,0:T(8,128)(2,1)S(1)}, f32[2,320,128]{2,1,0:T(8,128)S(1)}) custom-call(s32[1]{0:T(128)} %bitcast.at_group.after.refs_0_, s32[1]{0:T(128)} %bitcast.1.at_ex.refs_1_, s32[1]{0:T(128)} %bitcast.2.at_layer.refs_2_, bf16[1280,4096]{1,0:T(8,128)(2,1)S(1)} %bitcast.10, ...), custom_call_target="tpu_custom_call" | custom-call | tf_op jit(solution)/shard_map/score2/pallas_call | solution.py:128
  50.4 1.6 %collective-permute-start.26 = (bf16[2,320,128]{2,1,0:T(8,128)(2,1)S(1)}, bf16[2,320,128]{2,1,0:T(8,128)(2,1)S(1)}, u32[]{:S(2)}, u32[]{:S(2)}) collective-permute-start(bf16[2,320,128]{2,1,0:T(8,128)(2,1)S(1)} %get-tuple-element.62), channel_id=1, source_target_pairs={{0,1},{1,0},{2,3},{3,2},{4,5},{5,4},{6,7},{7,6},{8,9},{9,8},{10,11... | collective-permute-start | bytes 491528 | tf_op jit(solution)/shard_map/sum3_from_layer_1/ppermute | solution.py:199
  51.9 0.5 collective-permute-start.24
  52.4 2.6 %collective-permute-start.15 = (bf16[1,320,128]{2,1,0:T(8,128)(2,1)S(1)}, bf16[1,320,128]{2,1,0:T(8,128)(2,1)S(1)}, u32[]{:S(2)}, u32[]{:S(2)}) collective-permute-start(bf16[1,320,128]{2,1,0:T(8,128)(2,1)S(1)} %get-tuple-element.51), channel_id=1, source_target_pairs={{0,2},{1,3},{2,0},{3,1},{4,6},{5,7},{6,4},{7,5},{8,10},{9,11},{10,... | collective-permute-start | bytes 245768 | tf_op jit(solution)/shard_map/sum0_from_layer_2/ppermute | solution.py:199
  55.1 0.4 collective-permute-start.23
  55.5 6.4 %collective-permute-done.26.got = bf16[2,320,128]{2,1,0:T(8,128)(2,1)S(1)} collective-permute-done((bf16[2,320,128]{2,1,0:T(8,128)(2,1)S(1)}, bf16[2,320,128]{2,1,0:T(8,128)(2,1)S(1)}, u32[]{:S(2)}, u32[]{:S(2)}) %collective-permute-start.26) | collective-permute-done | bytes 163872 | tf_op jit(solution)/shard_map/sum3_from_layer_1/ppermute | solution.py:199
  61.9 0.8 %collective-permute-start.27 = (bf16[1,320,128]{2,1,0:T(8,128)(2,1)S(1)}, bf16[1,320,128]{2,1,0:T(8,128)(2,1)S(1)}, u32[]{:S(2)}, u32[]{:S(2)}) collective-permute-start(bf16[1,320,128]{2,1,0:T(8,128)(2,1)S(1)} %get-tuple-element.64), channel_id=1, source_target_pairs={{0,2},{1,3},{2,0},{3,1},{4,6},{5,7},{6,4},{7,5},{8,10},{9,11},{10,... | collective-permute-start | bytes 245768 | tf_op jit(solution)/shard_map/sum3_from_layer_2/ppermute | solution.py:199
  62.7 2.0 %collective-permute-done.24.got = bf16[2,320,128]{2,1,0:T(8,128)(2,1)S(1)} collective-permute-done((bf16[2,320,128]{2,1,0:T(8,128)(2,1)S(1)}, bf16[2,320,128]{2,1,0:T(8,128)(2,1)S(1)}, u32[]{:S(2)}, u32[]{:S(2)}) %collective-permute-start.24) | collective-permute-done | bytes 163872 | tf_op jit(solution)/shard_map/sum2_from_layer_1/ppermute | solution.py:199
  64.7 0.8 %collective-permute-start.25 = (bf16[1,320,128]{2,1,0:T(8,128)(2,1)S(1)}, bf16[1,320,128]{2,1,0:T(8,128)(2,1)S(1)}, u32[]{:S(2)}, u32[]{:S(2)}) collective-permute-start(bf16[1,320,128]{2,1,0:T(8,128)(2,1)S(1)} %get-tuple-element.61), channel_id=1, source_target_pairs={{0,2},{1,3},{2,0},{3,1},{4,6},{5,7},{6,4},{7,5},{8,10},{9,11},{10,... | collective-permute-start | bytes 245768 | tf_op jit(solution)/shard_map/sum2_from_layer_2/ppermute | solution.py:199
  65.5 5.5 %collective-permute-done.27.refs_10_ = bf16[1,320,128]{2,1,0:T(8,128)(2,1)S(1)} collective-permute-done((bf16[1,320,128]{2,1,0:T(8,128)(2,1)S(1)}, bf16[1,320,128]{2,1,0:T(8,128)(2,1)S(1)}, u32[]{:S(2)}, u32[]{:S(2)}) %collective-permute-start.27) | collective-permute-done | bytes 81952 | tf_op jit(solution)/shard_map/sum3_from_layer_2/ppermute | solution.py:199
  71.0 1.0 %collective-permute-done.25.refs_8_ = bf16[1,320,128]{2,1,0:T(8,128)(2,1)S(1)} collective-permute-done((bf16[1,320,128]{2,1,0:T(8,128)(2,1)S(1)}, bf16[1,320,128]{2,1,0:T(8,128)(2,1)S(1)}, u32[]{:S(2)}, u32[]{:S(2)}) %collective-permute-start.25) | collective-permute-done | bytes 81952 | tf_op jit(solution)/shard_map/sum2_from_layer_2/ppermute | solution.py:199
  71.9 0.9 %finish.1 = f32[320,512]{1,0:T(8,128)} custom-call(s32[1]{0:T(128)} %bitcast.at_group.after.refs_0_, s32[1]{0:T(128)} %bitcast.1.at_ex.refs_1_, s32[1]{0:T(128)} %bitcast.2.at_layer.refs_2_, f32[1,320,128]{2,1,0:T(8,128)S(1)} %get-tuple-element.50.refs_12_.refs_3_, bf16[1,320,128]{2,1,0:T(8,128)(2,1)S(1)} %collective-permute-done.15.refs_4_, ...), custom_call_target="tpu_custom_call" | custom-call | tf_op jit(solution)/shard_map/finish/pallas_call | solution.py:181
  (28 shorter events, 0.2 us)
Async XLA Ops:
  1.0 9.3 %collective-permute-start.1 = (bf16[128,1024]{1,0:T(8,128)(2,1)S(1)}, bf16[128,1024]{1,0:T(8,128)(2,1)S(1)}, u32[]{:S(2)}, u32[]{:S(2)}) collective-permute-start(bf16[128,1024]{1,0:T(8,128)(2,1)S(1)} %take.2.after.refs_4_), channel_id=1, source_target_pairs={{0,8},{4,12},{8,0},{12,4},{1,9},{5,13},{9,1},{13,5},{2,10},{6,14},... | collective-permute-start | bytes 786440 | tf_op jit(solution)/shard_map/q0_from_chip/ppermute | solution.py:199
  4.0 8.1 %collective-permute-start = (bf16[128,1024]{1,0:T(8,128)(2,1)S(1)}, bf16[128,1024]{1,0:T(8,128)(2,1)S(1)}, u32[]{:S(2)}, u32[]{:S(2)}) collective-permute-start(bf16[128,1024]{1,0:T(8,128)(2,1)S(1)} %take.2.after.refs_4_), channel_id=1, source_target_pairs={{0,4},{4,0},{8,12},{12,8},{1,5},{5,1},{9,13},{13,9},{2,6},{6,2},{1... | collective-permute-start | bytes 786440 | tf_op jit(solution)/shard_map/q0_from_core/ppermute | solution.py:199
  8.4 21.9 %slice-start = ((s8[10485760]{0:T(1024)(128)(4,1)}), s8[4194304]{0:T(1024)(128)(4,1)S(1)}, s32[]{:S(2)}) async-start(s8[10485760]{0:T(1024)(128)(4,1)} %bitcast.6), calls=%async_computation | async-start | bytes 8388608
  8.4 21.9 %slice-start.1 = ((s8[10485760]{0:T(1024)(128)(4,1)}), s8[4194304]{0:T(1024)(128)(4,1)S(1)}, s32[]{:S(2)}) async-start(s8[10485760]{0:T(1024)(128)(4,1)} %bitcast.6), calls=%async_computation.1 | async-start | bytes 8388608
  10.3 1.8 %collective-permute-start.2 = (bf16[128,1024]{1,0:T(8,128)(2,1)S(1)}, bf16[128,1024]{1,0:T(8,128)(2,1)S(1)}, u32[]{:S(2)}, u32[]{:S(2)}) collective-permute-start(bf16[128,1024]{1,0:T(8,128)(2,1)S(1)} %collective-permute-done.1.refs_6_), channel_id=1, source_target_pairs={{0,4},{4,0},{8,12},{12,8},{1,5},{5,1},{9,13},{13,9},{2,6},{6,2},{1... | collective-permute-start | bytes 786440 | tf_op jit(solution)/shard_map/q0_there_from_core/ppermute | solution.py:199
  10.3 9.1 %collective-permute-start.6 = (bf16[128,1024]{1,0:T(8,128)(2,1)S(1)}, bf16[128,1024]{1,0:T(8,128)(2,1)S(1)}, u32[]{:S(2)}, u32[]{:S(2)}) collective-permute-start(bf16[128,1024]{1,0:T(8,128)(2,1)S(1)} %take.3.refs_8_.refs_4_), channel_id=1, source_target_pairs={{0,8},{4,12},{8,0},{12,4},{1,9},{5,13},{9,1},{13,5},{2,10},{6,14},... | collective-permute-start | bytes 786440 | tf_op jit(solution)/shard_map/q1_from_chip/ppermute | solution.py:199
  14.5 10.2 %collective-permute-start.4 = (bf16[1040,128]{1,0:T(8,128)(2,1)S(1)}, bf16[1040,128]{1,0:T(8,128)(2,1)S(1)}, u32[]{:S(2)}, u32[]{:S(2)}) collective-permute-start(bf16[1040,128]{1,0:T(8,128)(2,1)S(1)} %get-tuple-element.37), channel_id=1, source_target_pairs={{0,8},{4,12},{8,0},{12,4},{1,9},{5,13},{9,1},{13,5},{2,10},{6,14},... | collective-permute-start | bytes 798728 | tf_op jit(solution)/shard_map/s0_from_chip/ppermute | solution.py:199
  16.1 5.0 %collective-permute-start.5 = (bf16[128,1024]{1,0:T(8,128)(2,1)S(1)}, bf16[128,1024]{1,0:T(8,128)(2,1)S(1)}, u32[]{:S(2)}, u32[]{:S(2)}) collective-permute-start(bf16[128,1024]{1,0:T(8,128)(2,1)S(1)} %take.3.refs_8_.refs_4_), channel_id=1, source_target_pairs={{0,4},{4,0},{8,12},{12,8},{1,5},{5,1},{9,13},{13,9},{2,6},{6,2},{1... | collective-permute-start | bytes 786440 | tf_op jit(solution)/shard_map/q1_from_core/ppermute | solution.py:199
  19.4 1.7 %collective-permute-start.7 = (bf16[128,1024]{1,0:T(8,128)(2,1)S(1)}, bf16[128,1024]{1,0:T(8,128)(2,1)S(1)}, u32[]{:S(2)}, u32[]{:S(2)}) collective-permute-start(bf16[128,1024]{1,0:T(8,128)(2,1)S(1)} %collective-permute-done.6.refs_6_), channel_id=1, source_target_pairs={{0,4},{4,0},{8,12},{12,8},{1,5},{5,1},{9,13},{13,9},{2,6},{6,2},{1... | collective-permute-start | bytes 786440 | tf_op jit(solution)/shard_map/q1_there_from_core/ppermute | solution.py:199
  19.4 10.9 %slice-start.2 = ((s8[10485760]{0:T(1024)(128)(4,1)}), s8[2097152]{0:T(1024)(128)(4,1)S(1)}, s32[]{:S(2)}) async-start(s8[10485760]{0:T(1024)(128)(4,1)} %bitcast.6), calls=%async_computation.2 | async-start | bytes 4194304
  19.4 9.1 %collective-permute-start.10 = (bf16[1040,128]{1,0:T(8,128)(2,1)S(1)}, bf16[1040,128]{1,0:T(8,128)(2,1)S(1)}, u32[]{:S(2)}, u32[]{:S(2)}) collective-permute-start(bf16[1040,128]{1,0:T(8,128)(2,1)S(1)} %get-tuple-element.43), channel_id=1, source_target_pairs={{0,16},{16,0},{1,17},{17,1},{2,18},{18,2},{3,19},{19,3},{4,20},{20... | collective-permute-start | bytes 798728 | tf_op jit(solution)/shard_map/s0_from_group/ppermute | solution.py:199
  24.7 5.5 %collective-permute-start.8 = (bf16[1040,128]{1,0:T(8,128)(2,1)S(1)}, bf16[1040,128]{1,0:T(8,128)(2,1)S(1)}, u32[]{:S(2)}, u32[]{:S(2)}) collective-permute-start(bf16[1040,128]{1,0:T(8,128)(2,1)S(1)} %collective-permute-done.4.refs_6_), channel_id=1, source_target_pairs={{0,4},{4,0},{8,12},{12,8},{1,5},{5,1},{9,13},{13,9},{2,6},{6,2},{1... | collective-permute-start | bytes 798728 | tf_op jit(solution)/shard_map/s0_there_from_core/ppermute | solution.py:199
  24.7 9.5 %collective-permute-start.12 = (bf16[1040,128]{1,0:T(8,128)(2,1)S(1)}, bf16[1040,128]{1,0:T(8,128)(2,1)S(1)}, u32[]{:S(2)}, u32[]{:S(2)}) collective-permute-start(bf16[1040,128]{1,0:T(8,128)(2,1)S(1)} %collective-permute-done.4.refs_6_), channel_id=1, source_target_pairs={{0,16},{16,0},{1,17},{17,1},{2,18},{18,2},{3,19},{19,3},{4,20},{20... | collective-permute-start | bytes 798728 | tf_op jit(solution)/shard_map/s0_there_from_group/ppermute | solution.py:199
  26.4 3.8 %collective-permute-start.3 = (bf16[1024,128]{1,0:T(8,128)(2,1)S(1)}, bf16[1024,128]{1,0:T(8,128)(2,1)S(1)}, u32[]{:S(2)}, u32[]{:S(2)}) collective-permute-start(bf16[1024,128]{1,0:T(8,128)(2,1)S(1)} %get-tuple-element.36.refs_8_.refs_4_), channel_id=1, source_target_pairs={{0,4},{4,0},{8,12},{12,8},{1,5},{5,1},{9,13},{13,9},{2,6},{6,2},{1... | collective-permute-start | bytes 786440 | tf_op jit(solution)/shard_map/s0_from_core/ppermute | solution.py:199
  26.7 8.5 %collective-permute-start.18 = (bf16[1024,128]{1,0:T(8,128)(2,1)S(1)}, bf16[1024,128]{1,0:T(8,128)(2,1)S(1)}, u32[]{:S(2)}, u32[]{:S(2)}) collective-permute-start(bf16[1024,128]{1,0:T(8,128)(2,1)S(1)} %get-tuple-element.39.refs_8_.refs_4_), channel_id=1, source_target_pairs={{0,8},{4,12},{8,0},{12,4},{1,9},{5,13},{9,1},{13,5},{2,10},{6,14},... | collective-permute-start | bytes 786440 | tf_op jit(solution)/shard_map/s1_from_chip/ppermute | solution.py:199
  28.5 11.4 %collective-permute-start.14 = (bf16[1040,128]{1,0:T(8,128)(2,1)S(1)}, bf16[1040,128]{1,0:T(8,128)(2,1)S(1)}, u32[]{:S(2)}, u32[]{:S(2)}) collective-permute-start(bf16[1040,128]{1,0:T(8,128)(2,1)S(1)} %get-tuple-element.46), channel_id=1, source_target_pairs={{0,16},{16,0},{1,17},{17,1},{2,18},{18,2},{3,19},{19,3},{4,20},{20... | collective-permute-start | bytes 798728 | tf_op jit(solution)/shard_map/s1_from_group/ppermute | solution.py:199
  30.3 9.7 %collective-permute-start.11 = (bf16[1040,128]{1,0:T(8,128)(2,1)S(1)}, bf16[1040,128]{1,0:T(8,128)(2,1)S(1)}, u32[]{:S(2)}, u32[]{:S(2)}) collective-permute-start(bf16[1040,128]{1,0:T(8,128)(2,1)S(1)} %collective-permute-done.10.refs_4_), channel_id=1, source_target_pairs={{0,4},{4,0},{8,12},{12,8},{1,5},{5,1},{9,13},{13,9},{2,6},{6,2},{1... | collective-permute-start | bytes 798728 | tf_op jit(solution)/shard_map/s0_across_from_core/ppermute | solution.py:199
  34.2 6.2 %collective-permute-start.13 = (bf16[1040,128]{1,0:T(8,128)(2,1)S(1)}, bf16[1040,128]{1,0:T(8,128)(2,1)S(1)}, u32[]{:S(2)}, u32[]{:S(2)}) collective-permute-start(bf16[1040,128]{1,0:T(8,128)(2,1)S(1)} %collective-permute-done.12.refs_6_), channel_id=1, source_target_pairs={{0,4},{4,0},{8,12},{12,8},{1,5},{5,1},{9,13},{13,9},{2,6},{6,2},{1... | collective-permute-start | bytes 798728 | tf_op jit(solution)/shard_map/s0_diagonal_from_core/ppermute | solution.py:199
  35.2 10.1 %collective-permute-start.21 = (bf16[1024,128]{1,0:T(8,128)(2,1)S(1)}, bf16[1024,128]{1,0:T(8,128)(2,1)S(1)}, u32[]{:S(2)}, u32[]{:S(2)}) collective-permute-start(bf16[1024,128]{1,0:T(8,128)(2,1)S(1)} %collective-permute-done.18.refs_6_), channel_id=1, source_target_pairs={{0,16},{16,0},{1,17},{17,1},{2,18},{18,2},{3,19},{19,3},{4,20},{20... | collective-permute-start | bytes 786440 | tf_op jit(solution)/shard_map/s1_there_from_group/ppermute | solution.py:199
  36.0 7.5 %collective-permute-start.9 = (bf16[2,320,128]{2,1,0:T(8,128)(2,1)S(1)}, bf16[2,320,128]{2,1,0:T(8,128)(2,1)S(1)}, u32[]{:S(2)}, u32[]{:S(2)}) collective-permute-start(bf16[2,320,128]{2,1,0:T(8,128)(2,1)S(1)} %get-tuple-element.42), channel_id=1, source_target_pairs={{0,1},{1,0},{2,3},{3,2},{4,5},{5,4},{6,7},{7,6},{8,9},{9,8},{10,11... | collective-permute-start | bytes 491528 | tf_op jit(solution)/shard_map/sum0_from_layer_1/ppermute | solution.py:199
  40.0 7.1 %collective-permute-start.20 = (bf16[1040,128]{1,0:T(8,128)(2,1)S(1)}, bf16[1040,128]{1,0:T(8,128)(2,1)S(1)}, u32[]{:S(2)}, u32[]{:S(2)}) collective-permute-start(bf16[1040,128]{1,0:T(8,128)(2,1)S(1)} %collective-permute-done.14.refs_8_), channel_id=1, source_target_pairs={{0,4},{4,0},{8,12},{12,8},{1,5},{5,1},{9,13},{13,9},{2,6},{6,2},{1... | collective-permute-start | bytes 798728 | tf_op jit(solution)/shard_map/s1_across_from_core/ppermute | solution.py:199
  40.0 7.1 %collective-permute-start.17 = (bf16[1024,128]{1,0:T(8,128)(2,1)S(1)}, bf16[1024,128]{1,0:T(8,128)(2,1)S(1)}, u32[]{:S(2)}, u32[]{:S(2)}) collective-permute-start(bf16[1024,128]{1,0:T(8,128)(2,1)S(1)} %get-tuple-element.39.refs_8_.refs_4_), channel_id=1, source_target_pairs={{0,4},{4,0},{8,12},{12,8},{1,5},{5,1},{9,13},{13,9},{2,6},{6,2},{1... | collective-permute-start | bytes 786440 | tf_op jit(solution)/shard_map/s1_from_core/ppermute | solution.py:199
  40.5 6.6 %collective-permute-start.19 = (bf16[1024,128]{1,0:T(8,128)(2,1)S(1)}, bf16[1024,128]{1,0:T(8,128)(2,1)S(1)}, u32[]{:S(2)}, u32[]{:S(2)}) collective-permute-start(bf16[1024,128]{1,0:T(8,128)(2,1)S(1)} %collective-permute-done.18.refs_6_), channel_id=1, source_target_pairs={{0,4},{4,0},{8,12},{12,8},{1,5},{5,1},{9,13},{13,9},{2,6},{6,2},{1... | collective-permute-start | bytes 786440 | tf_op jit(solution)/shard_map/s1_there_from_core/ppermute | solution.py:199
  45.3 1.8 %collective-permute-start.22 = (bf16[1024,128]{1,0:T(8,128)(2,1)S(1)}, bf16[1024,128]{1,0:T(8,128)(2,1)S(1)}, u32[]{:S(2)}, u32[]{:S(2)}) collective-permute-start(bf16[1024,128]{1,0:T(8,128)(2,1)S(1)} %collective-permute-done.21.refs_10_), channel_id=1, source_target_pairs={{0,4},{4,0},{8,12},{12,8},{1,5},{5,1},{9,13},{13,9},{2,6},{6,2},{1... | collective-permute-start | bytes 786440 | tf_op jit(solution)/shard_map/s1_diagonal_from_core/ppermute | solution.py:199
  45.3 9.8 %collective-permute-start.16 = (bf16[2,320,128]{2,1,0:T(8,128)(2,1)S(1)}, bf16[2,320,128]{2,1,0:T(8,128)(2,1)S(1)}, u32[]{:S(2)}, u32[]{:S(2)}) collective-permute-start(bf16[2,320,128]{2,1,0:T(8,128)(2,1)S(1)} %get-tuple-element.52), channel_id=1, source_target_pairs={{0,1},{1,0},{2,3},{3,2},{4,5},{5,4},{6,7},{7,6},{8,9},{9,8},{10,11... | collective-permute-start | bytes 491528 | tf_op jit(solution)/shard_map/sum1_from_layer_1/ppermute | solution.py:199
  50.4 11.5 %collective-permute-start.26 = (bf16[2,320,128]{2,1,0:T(8,128)(2,1)S(1)}, bf16[2,320,128]{2,1,0:T(8,128)(2,1)S(1)}, u32[]{:S(2)}, u32[]{:S(2)}) collective-permute-start(bf16[2,320,128]{2,1,0:T(8,128)(2,1)S(1)} %get-tuple-element.62), channel_id=1, source_target_pairs={{0,1},{1,0},{2,3},{3,2},{4,5},{5,4},{6,7},{7,6},{8,9},{9,8},{10,11... | collective-permute-start | bytes 491528 | tf_op jit(solution)/shard_map/sum3_from_layer_1/ppermute | solution.py:199
  51.9 12.7 %collective-permute-start.24 = (bf16[2,320,128]{2,1,0:T(8,128)(2,1)S(1)}, bf16[2,320,128]{2,1,0:T(8,128)(2,1)S(1)}, u32[]{:S(2)}, u32[]{:S(2)}) collective-permute-start(bf16[2,320,128]{2,1,0:T(8,128)(2,1)S(1)} %get-tuple-element.59), channel_id=1, source_target_pairs={{0,1},{1,0},{2,3},{3,2},{4,5},{5,4},{6,7},{7,6},{8,9},{9,8},{10,11... | collective-permute-start | bytes 491528 | tf_op jit(solution)/shard_map/sum2_from_layer_1/ppermute | solution.py:199
  52.4 13.0 %collective-permute-start.15 = (bf16[1,320,128]{2,1,0:T(8,128)(2,1)S(1)}, bf16[1,320,128]{2,1,0:T(8,128)(2,1)S(1)}, u32[]{:S(2)}, u32[]{:S(2)}) collective-permute-start(bf16[1,320,128]{2,1,0:T(8,128)(2,1)S(1)} %get-tuple-element.51), channel_id=1, source_target_pairs={{0,2},{1,3},{2,0},{3,1},{4,6},{5,7},{6,4},{7,5},{8,10},{9,11},{10,... | collective-permute-start | bytes 245768 | tf_op jit(solution)/shard_map/sum0_from_layer_2/ppermute | solution.py:199
  55.1 10.4 %collective-permute-start.23 = (bf16[1,320,128]{2,1,0:T(8,128)(2,1)S(1)}, bf16[1,320,128]{2,1,0:T(8,128)(2,1)S(1)}, u32[]{:S(2)}, u32[]{:S(2)}) collective-permute-start(bf16[1,320,128]{2,1,0:T(8,128)(2,1)S(1)} %get-tuple-element.57), channel_id=1, source_target_pairs={{0,2},{1,3},{2,0},{3,1},{4,6},{5,7},{6,4},{7,5},{8,10},{9,11},{10,... | collective-permute-start | bytes 245768 | tf_op jit(solution)/shard_map/sum1_from_layer_2/ppermute | solution.py:199
  61.9 9.1 %collective-permute-start.27 = (bf16[1,320,128]{2,1,0:T(8,128)(2,1)S(1)}, bf16[1,320,128]{2,1,0:T(8,128)(2,1)S(1)}, u32[]{:S(2)}, u32[]{:S(2)}) collective-permute-start(bf16[1,320,128]{2,1,0:T(8,128)(2,1)S(1)} %get-tuple-element.64), channel_id=1, source_target_pairs={{0,2},{1,3},{2,0},{3,1},{4,6},{5,7},{6,4},{7,5},{8,10},{9,11},{10,... | collective-permute-start | bytes 245768 | tf_op jit(solution)/shard_map/sum3_from_layer_2/ppermute | solution.py:199
  64.7 7.2 %collective-permute-start.25 = (bf16[1,320,128]{2,1,0:T(8,128)(2,1)S(1)}, bf16[1,320,128]{2,1,0:T(8,128)(2,1)S(1)}, u32[]{:S(2)}, u32[]{:S(2)}) collective-permute-start(bf16[1,320,128]{2,1,0:T(8,128)(2,1)S(1)} %get-tuple-element.61), channel_id=1, source_target_pairs={{0,2},{1,3},{2,0},{3,1},{4,6},{5,7},{6,4},{7,5},{8,10},{9,11},{10,... | collective-permute-start | bytes 245768 | tf_op jit(solution)/shard_map/sum2_from_layer_2/ppermute | solution.py:199

commit v12 on v11

--- a/solution.py
+++ b/solution.py
@@ -276,13 +276,18 @@
     s1_across_cores = flip(s1_across, "s1_across")
     s1_diagonal = [gather_group(x, "s1_there") for x in s1_there]
     s1_cores = [s1_core] + flip(s1_there, "s1_there")
+    pieces = []
     for j in range(groups - 1):
         ours = [s0_across[j]] + [xs[j] for xs in s0_diagonal]
         theirs = [s0_across_cores[j]] + [xs[j] for xs in s0_diagonal_cores]
-        last = send_parts(score("score1", sizes, place, rows, [with_cores(ours, theirs)], tie(last, *s1_across)))
+        pieces.append(with_cores(ours, theirs))
+    pieces.append(with_cores([s1] + s1_there, s1_cores))
+    last = send_parts(score("score1", sizes, place, rows, pieces, last))
+    s1_across = after(last, s1_across)
+    s1_across_cores = flip(s1_across, "s1_across")
     s1_diagonal = [after(last, xs) for xs in s1_diagonal]
     s1_diagonal_cores = [flip(xs, "s1_diagonal") for xs in s1_diagonal]
-    pieces = [with_cores([s1] + s1_there, s1_cores)]
+    pieces = []
     for j in range(groups - 1):
         ours = [s1_across[j]] + [xs[j] for xs in s1_diagonal]
         theirs = [s1_across_cores[j]] + [xs[j] for xs in s1_diagonal_cores]

time: 73.1 us -> 72.7 us (level)
  waiting for transfers between devices: 27.4 us -> 23.2 us
  starting transfers between devices: 24.7 us -> 28.5 us
    ppermute x28, waiting for transfers between devices: 27.4 us -> 23.2 us  [permute(): return lax.ppermute(x, axis, perm)]
    ppermute x28, starting transfers between devices: 24.7 us -> 28.5 us  [permute(): return lax.ppermute(x, axis, perm)]
where the time goes in v12:
time: 72.7 us; the launch traced here: 72.5 us
  starting transfers between devices  28.5 us (39%)
  waiting for transfers between devices  23.2 us (32%)
  Pallas kernels  20.6 us (28%)
    ppermute x28, starting transfers between devices, permute(): return lax.ppermute(x, axis, perm)  28.5 us
    ppermute x28, waiting for transfers between devices, permute(): return lax.ppermute(x, axis, perm)  23.2 us
    pallas_call x3, Pallas kernels, score(): pl.pallas_call(functools.partial(score_kernel, sizes, columns, direct), o...  9.17 us
    pallas_call x2, Pallas kernels, condition(): pl.pallas_call(functools.partial(condition_kernel, sizes), out_shape=[plt...  5.04 us
    pallas_call x1, Pallas kernels, load(): pl.pallas_call(load_kernel, out_shape=pltpu.VMEM(source.shape, BF16), in_...  3.39 us
    pallas_call x2, Pallas kernels, take(): pl.pallas_call(functools.partial(take_kernel, chunk), out_shape=pltpu.VME...  1.92 us
  transfers between devices with their start and end apart: 28, of which 12 were waited for; matrix products, arithmetic and copies ran while one was open for 0% of the time, Pallas kernels for 26%

profile of v12, /device:TPU:0, one launch (start us, length us, event | category | flops | bytes accessed | tf_op | source)
XLA Modules:
  0.0 72.5 jit_solution(12607592529415991354)
XLA Ops:
  0.0 1.0 %take.2.after.refs_4_ = bf16[128,1024]{1,0:T(8,128)(2,1)S(1)} custom-call(s32[1]{0:T(128)} %bitcast.at_group.after.refs_0_, s32[1]{0:T(128)} %bitcast.1.at_ex.refs_1_, s32[1]{0:T(128)} %bitcast.2.at_layer.refs_2_, bf16[512,1024]{1,0:T(8,128)(2,1)} %bitcast.12, s32[1]{0:T(128)} %bitcast.at_group.after.refs_0_), custom_call_target="tpu_custom_call" | custom-call | tf_op jit(solution)/shard_map/take/pallas_call | solution.py:58
  1.0 3.0 %collective-permute-start.1 = (bf16[128,1024]{1,0:T(8,128)(2,1)S(1)}, bf16[128,1024]{1,0:T(8,128)(2,1)S(1)}, u32[]{:S(2)}, u32[]{:S(2)}) collective-permute-start(bf16[128,1024]{1,0:T(8,128)(2,1)S(1)} %take.2.after.refs_4_), channel_id=1, source_target_pairs={{0,8},{4,12},{8,0},{12,4},{1,9},{5,13},{9,1},{13,5},{2,10},{6,14},... | collective-permute-start | bytes 786440 | tf_op jit(solution)/shard_map/q0_from_chip/ppermute | solution.py:199
  4.0 3.4 %load.1.after.refs_3_ = bf16[1024,4096]{1,0:T(8,128)(2,1)S(1)} custom-call(bf16[1024,4096]{1,0:T(8,128)(2,1)} %bitcast.11, bf16[128,1024]{1,0:T(8,128)(2,1)S(1)} %take.2.after.refs_4_), custom_call_target="tpu_custom_call" | custom-call | tf_op jit(solution)/shard_map/load/pallas_call | solution.py:38
  7.4 1.0 %take.3.refs_8_.refs_4_ = bf16[128,1024]{1,0:T(8,128)(2,1)S(1)} custom-call(s32[1]{0:T(128)} %bitcast.at_group.after.refs_0_, s32[1]{0:T(128)} %bitcast.1.at_ex.refs_1_, s32[1]{0:T(128)} %bitcast.2.at_layer.refs_2_, bf16[512,1024]{1,0:T(8,128)(2,1)} %bitcast.13, bf16[1024,4096]{1,0:T(8,128)(2,1)S(1)} %load.1.after.refs_3_), custom_call_target="tpu_custom_call" | custom-call | tf_op jit(solution)/shard_map/take/pallas_call | solution.py:58
  8.4 0.0 slice-start
  8.4 0.0 slice-start.1
  8.4 1.9 %collective-permute-done.1.refs_6_ = bf16[128,1024]{1,0:T(8,128)(2,1)S(1)} collective-permute-done((bf16[128,1024]{1,0:T(8,128)(2,1)S(1)}, bf16[128,1024]{1,0:T(8,128)(2,1)S(1)}, u32[]{:S(2)}, u32[]{:S(2)}) %collective-permute-start.1) | collective-permute-done | bytes 262176 | tf_op jit(solution)/shard_map/q0_from_chip/ppermute | solution.py:199
  10.3 0.0 collective-permute-start.2
  10.3 1.7 %collective-permute-start.6 = (bf16[128,1024]{1,0:T(8,128)(2,1)S(1)}, bf16[128,1024]{1,0:T(8,128)(2,1)S(1)}, u32[]{:S(2)}, u32[]{:S(2)}) collective-permute-start(bf16[128,1024]{1,0:T(8,128)(2,1)S(1)} %take.3.refs_8_.refs_4_), channel_id=1, source_target_pairs={{0,8},{4,12},{8,0},{12,4},{1,9},{5,13},{9,1},{13,5},{2,10},{6,14},... | collective-permute-start | bytes 786440 | tf_op jit(solution)/shard_map/q1_from_chip/ppermute | solution.py:199
  12.1 2.5 %condition.2 = (bf16[1024,128]{1,0:T(8,128)(2,1)S(1)}, bf16[1040,128]{1,0:T(8,128)(2,1)S(1)}, bf16[1040,128]{1,0:T(8,128)(2,1)S(1)}) custom-call(s32[1]{0:T(128)} %bitcast.at_group.after.refs_0_, s32[1]{0:T(128)} %bitcast.1.at_ex.refs_1_, s32[1]{0:T(128)} %bitcast.2.at_layer.refs_2_, bf16[1024,4096]{1,0:T(8,128)(2,1)S(1)} %load.1.after.refs_3_, ...), custom_call_target="tpu_custom_call" | custom-call | tf_op jit(solution)/shard_map/condition/pallas_call | solution.py:88
  14.5 1.6 %collective-permute-start.4 = (bf16[1040,128]{1,0:T(8,128)(2,1)S(1)}, bf16[1040,128]{1,0:T(8,128)(2,1)S(1)}, u32[]{:S(2)}, u32[]{:S(2)}) collective-permute-start(bf16[1040,128]{1,0:T(8,128)(2,1)S(1)} %get-tuple-element.37), channel_id=1, source_target_pairs={{0,8},{4,12},{8,0},{12,4},{1,9},{5,13},{9,1},{13,5},{2,10},{6,14},... | collective-permute-start | bytes 798728 | tf_op jit(solution)/shard_map/s0_from_chip/ppermute | solution.py:199
  16.1 3.3 %collective-permute-done.6.refs_6_ = bf16[128,1024]{1,0:T(8,128)(2,1)S(1)} collective-permute-done((bf16[128,1024]{1,0:T(8,128)(2,1)S(1)}, bf16[128,1024]{1,0:T(8,128)(2,1)S(1)}, u32[]{:S(2)}, u32[]{:S(2)}) %collective-permute-start.6) | collective-permute-done | bytes 262176 | tf_op jit(solution)/shard_map/q1_from_chip/ppermute | solution.py:199
  19.4 0.0 collective-permute-start.7
  19.4 0.5 collective-permute-start.3
  19.9 1.7 %collective-permute-start.10 = (bf16[1040,128]{1,0:T(8,128)(2,1)S(1)}, bf16[1040,128]{1,0:T(8,128)(2,1)S(1)}, u32[]{:S(2)}, u32[]{:S(2)}) collective-permute-start(bf16[1040,128]{1,0:T(8,128)(2,1)S(1)} %get-tuple-element.43), channel_id=1, source_target_pairs={{0,16},{16,0},{1,17},{17,1},{2,18},{18,2},{3,19},{19,3},{4,20},{20... | collective-permute-start | bytes 798728 | tf_op jit(solution)/shard_map/s0_from_group/ppermute | solution.py:199
  21.6 0.0 collective-permute-done.5.refs_5_
  21.6 0.0 collective-permute-done.7.refs_7_
  21.6 2.6 %condition.3 = (bf16[1024,128]{1,0:T(8,128)(2,1)S(1)}, bf16[1040,128]{1,0:T(8,128)(2,1)S(1)}) custom-call(s32[1]{0:T(128)} %bitcast.at_group.after.refs_0_, s32[1]{0:T(128)} %bitcast.1.at_ex.refs_1_, s32[1]{0:T(128)} %bitcast.2.at_layer.refs_2_, bf16[1024,4096]{1,0:T(8,128)(2,1)S(1)} %load.1.after.refs_3_, bf16[128,1024]{1,0:T(8,128)(2,1)S(1)} %take.3.refs_8_.refs_4_, ...), custom_call_target="tpu_custom_call" | custom-call | tf_op jit(solution)/shard_map/condition/pallas_call | solution.py:88
  24.2 0.5 collective-permute-done.4.refs_6_
  24.7 0.0 collective-permute-start.8
  24.7 1.7 %collective-permute-start.12 = (bf16[1040,128]{1,0:T(8,128)(2,1)S(1)}, bf16[1040,128]{1,0:T(8,128)(2,1)S(1)}, u32[]{:S(2)}, u32[]{:S(2)}) collective-permute-start(bf16[1040,128]{1,0:T(8,128)(2,1)S(1)} %collective-permute-done.4.refs_6_), channel_id=1, source_target_pairs={{0,16},{16,0},{1,17},{17,1},{2,18},{18,2},{3,19},{19,3},{4,20},{20... | collective-permute-start | bytes 798728 | tf_op jit(solution)/shard_map/s0_there_from_group/ppermute | solution.py:199
  26.4 1.5 %collective-permute-start.15 = (bf16[1024,128]{1,0:T(8,128)(2,1)S(1)}, bf16[1024,128]{1,0:T(8,128)(2,1)S(1)}, u32[]{:S(2)}, u32[]{:S(2)}) collective-permute-start(bf16[1024,128]{1,0:T(8,128)(2,1)S(1)} %get-tuple-element.39.refs_8_), channel_id=1, source_target_pairs={{0,8},{4,12},{8,0},{12,4},{1,9},{5,13},{9,1},{13,5},{2,10},{6,14},... | collective-permute-start | bytes 786440 | tf_op jit(solution)/shard_map/s1_from_chip/ppermute | solution.py:199
  28.0 0.0 collective-permute-done.3.refs_5_
  28.0 0.6 collective-permute-done.10.refs_4_
  28.6 1.7 %collective-permute-start.19 = (bf16[1040,128]{1,0:T(8,128)(2,1)S(1)}, bf16[1040,128]{1,0:T(8,128)(2,1)S(1)}, u32[]{:S(2)}, u32[]{:S(2)}) collective-permute-start(bf16[1040,128]{1,0:T(8,128)(2,1)S(1)} %get-tuple-element.52), channel_id=1, source_target_pairs={{0,16},{16,0},{1,17},{17,1},{2,18},{18,2},{3,19},{19,3},{4,20},{20... | collective-permute-start | bytes 798728 | tf_op jit(solution)/shard_map/s1_from_group/ppermute | solution.py:199
  30.3 3.0 %score0.1 = (bf16[2,320,128]{2,1,0:T(8,128)(2,1)S(1)}, f32[2,320,128]{2,1,0:T(8,128)S(1)}) custom-call(s32[1]{0:T(128)} %bitcast.at_group.after.refs_0_, s32[1]{0:T(128)} %bitcast.1.at_ex.refs_1_, s32[1]{0:T(128)} %bitcast.2.at_layer.refs_2_, bf16[1280,4096]{1,0:T(8,128)(2,1)S(1)} %bitcast.8, bf16[1024,128]{1,0:T(8,128)(2,1)S(1)} %get-tuple-element.36.refs_8_.refs_4_, ...), custom_call_target="tpu_custom_call" | custom-call | tf_op jit(solution)/shard_map/score0/pallas_call | solution.py:128
  33.3 1.0 %collective-permute-done.12.refs_6_ = bf16[1040,128]{1,0:T(8,128)(2,1)S(1)} collective-permute-done((bf16[1040,128]{1,0:T(8,128)(2,1)S(1)}, bf16[1040,128]{1,0:T(8,128)(2,1)S(1)}, u32[]{:S(2)}, u32[]{:S(2)}) %collective-permute-start.12) | collective-permute-done | bytes 266272 | tf_op jit(solution)/shard_map/s0_there_from_group/ppermute | solution.py:199
  34.3 0.6 collective-permute-done.15.refs_10_
  34.9 1.6 %collective-permute-start.21 = (bf16[1024,128]{1,0:T(8,128)(2,1)S(1)}, bf16[1024,128]{1,0:T(8,128)(2,1)S(1)}, u32[]{:S(2)}, u32[]{:S(2)}) collective-permute-start(bf16[1024,128]{1,0:T(8,128)(2,1)S(1)} %collective-permute-done.15.refs_10_), channel_id=1, source_target_pairs={{0,16},{16,0},{1,17},{17,1},{2,18},{18,2},{3,19},{19,3},{4,20},{20... | collective-permute-start | bytes 786440 | tf_op jit(solution)/shard_map/s1_there_from_group/ppermute | solution.py:199
  36.5 3.5 %collective-permute-done.19.refs_4_ = bf16[1040,128]{1,0:T(8,128)(2,1)S(1)} collective-permute-done((bf16[1040,128]{1,0:T(8,128)(2,1)S(1)}, bf16[1040,128]{1,0:T(8,128)(2,1)S(1)}, u32[]{:S(2)}, u32[]{:S(2)}) %collective-permute-start.19) | collective-permute-done | bytes 266272 | tf_op jit(solution)/shard_map/s1_from_group/ppermute | solution.py:199
  40.0 1.8 %collective-permute-start.9 = (bf16[2,320,128]{2,1,0:T(8,128)(2,1)S(1)}, bf16[2,320,128]{2,1,0:T(8,128)(2,1)S(1)}, u32[]{:S(2)}, u32[]{:S(2)}) collective-permute-start(bf16[2,320,128]{2,1,0:T(8,128)(2,1)S(1)} %get-tuple-element.42), channel_id=1, source_target_pairs={{0,1},{1,0},{2,3},{3,2},{4,5},{5,4},{6,7},{7,6},{8,9},{9,8},{10,11... | collective-permute-start | bytes 491528 | tf_op jit(solution)/shard_map/sum0_from_layer_1/ppermute | solution.py:199
  41.8 3.3 %score1.1 = (bf16[2,320,128]{2,1,0:T(8,128)(2,1)S(1)}, f32[2,320,128]{2,1,0:T(8,128)S(1)}, bf16[2,320,128]{2,1,0:T(8,128)(2,1)S(1)}, f32[2,320,128]{2,1,0:T(8,128)S(1)}) custom-call(s32[1]{0:T(128)} %bitcast.at_group.after.refs_0_, s32[1]{0:T(128)} %bitcast.1.at_ex.refs_1_, s32[1]{0:T(128)} %bitcast.2.at_layer.refs_2_, bf16[1280,4096]{1,0:T(8,128)(2,1)S(1)} %bitcast.9, ...), custom_call_target="tpu_custom_call" | custom-call | tf_op jit(solution)/shard_map/score1/pallas_call | solution.py:128
  45.0 0.5 collective-permute-done.9.got
  45.6 0.1 collective-permute-start.20
  45.7 0.5 collective-permute-start.22
  46.2 1.7 %collective-permute-start.24 = (bf16[2,320,128]{2,1,0:T(8,128)(2,1)S(1)}, bf16[2,320,128]{2,1,0:T(8,128)(2,1)S(1)}, u32[]{:S(2)}, u32[]{:S(2)}) collective-permute-start(bf16[2,320,128]{2,1,0:T(8,128)(2,1)S(1)} %get-tuple-element.59), channel_id=1, source_target_pairs={{0,1},{1,0},{2,3},{3,2},{4,5},{5,4},{6,7},{7,6},{8,9},{9,8},{10,11... | collective-permute-start | bytes 491528 | tf_op jit(solution)/shard_map/sum2_from_layer_1/ppermute | solution.py:199
  47.9 0.3 collective-permute-start.18
  48.2 2.9 %score2.1 = (bf16[2,320,128]{2,1,0:T(8,128)(2,1)S(1)}, f32[2,320,128]{2,1,0:T(8,128)S(1)}) custom-call(s32[1]{0:T(128)} %bitcast.at_group.after.refs_0_, s32[1]{0:T(128)} %bitcast.1.at_ex.refs_1_, s32[1]{0:T(128)} %bitcast.2.at_layer.refs_2_, bf16[1280,4096]{1,0:T(8,128)(2,1)S(1)} %bitcast.10, bf16[1040,128]{1,0:T(8,128)(2,1)S(1)} %collective-permute-done.19.refs_4_, ...), custom_call_target="tpu_custom_call" | custom-call | tf_op jit(solution)/shard_map/score2/pallas_call | solution.py:128
  51.2 1.8 %collective-permute-start.26 = (bf16[2,320,128]{2,1,0:T(8,128)(2,1)S(1)}, bf16[2,320,128]{2,1,0:T(8,128)(2,1)S(1)}, u32[]{:S(2)}, u32[]{:S(2)}) collective-permute-start(bf16[2,320,128]{2,1,0:T(8,128)(2,1)S(1)} %get-tuple-element.62), channel_id=1, source_target_pairs={{0,1},{1,0},{2,3},{3,2},{4,5},{5,4},{6,7},{7,6},{8,9},{9,8},{10,11... | collective-permute-start | bytes 491528 | tf_op jit(solution)/shard_map/sum3_from_layer_1/ppermute | solution.py:199
  53.0 2.6 %collective-permute-start.17 = (bf16[1,320,128]{2,1,0:T(8,128)(2,1)S(1)}, bf16[1,320,128]{2,1,0:T(8,128)(2,1)S(1)}, u32[]{:S(2)}, u32[]{:S(2)}) collective-permute-start(bf16[1,320,128]{2,1,0:T(8,128)(2,1)S(1)} %get-tuple-element.49), channel_id=1, source_target_pairs={{0,2},{1,3},{2,0},{3,1},{4,6},{5,7},{6,4},{7,5},{8,10},{9,11},{10,... | collective-permute-start | bytes 245768 | tf_op jit(solution)/shard_map/sum0_from_layer_2/ppermute | solution.py:199
  55.6 0.5 collective-permute-start.25
  56.1 3.3 %collective-permute-done.18.got = bf16[2,320,128]{2,1,0:T(8,128)(2,1)S(1)} collective-permute-done((bf16[2,320,128]{2,1,0:T(8,128)(2,1)S(1)}, bf16[2,320,128]{2,1,0:T(8,128)(2,1)S(1)}, u32[]{:S(2)}, u32[]{:S(2)}) %collective-permute-start.18) | collective-permute-done | bytes 163872 | tf_op jit(solution)/shard_map/sum1_from_layer_1/ppermute | solution.py:199
  59.4 2.8 %collective-permute-start.23 = (bf16[1,320,128]{2,1,0:T(8,128)(2,1)S(1)}, bf16[1,320,128]{2,1,0:T(8,128)(2,1)S(1)}, u32[]{:S(2)}, u32[]{:S(2)}) collective-permute-start(bf16[1,320,128]{2,1,0:T(8,128)(2,1)S(1)} %get-tuple-element.58), channel_id=1, source_target_pairs={{0,2},{1,3},{2,0},{3,1},{4,6},{5,7},{6,4},{7,5},{8,10},{9,11},{10,... | collective-permute-start | bytes 245768 | tf_op jit(solution)/shard_map/sum1_from_layer_2/ppermute | solution.py:199
  62.2 1.3 %collective-permute-done.26.got = bf16[2,320,128]{2,1,0:T(8,128)(2,1)S(1)} collective-permute-done((bf16[2,320,128]{2,1,0:T(8,128)(2,1)S(1)}, bf16[2,320,128]{2,1,0:T(8,128)(2,1)S(1)}, u32[]{:S(2)}, u32[]{:S(2)}) %collective-permute-start.26) | collective-permute-done | bytes 163872 | tf_op jit(solution)/shard_map/sum3_from_layer_1/ppermute | solution.py:199
  63.6 1.4 %collective-permute-start.27 = (bf16[1,320,128]{2,1,0:T(8,128)(2,1)S(1)}, bf16[1,320,128]{2,1,0:T(8,128)(2,1)S(1)}, u32[]{:S(2)}, u32[]{:S(2)}) collective-permute-start(bf16[1,320,128]{2,1,0:T(8,128)(2,1)S(1)} %get-tuple-element.64), channel_id=1, source_target_pairs={{0,2},{1,3},{2,0},{3,1},{4,6},{5,7},{6,4},{7,5},{8,10},{9,11},{10,... | collective-permute-start | bytes 245768 | tf_op jit(solution)/shard_map/sum3_from_layer_2/ppermute | solution.py:199
  65.0 5.6 %collective-permute-done.23.refs_6_ = bf16[1,320,128]{2,1,0:T(8,128)(2,1)S(1)} collective-permute-done((bf16[1,320,128]{2,1,0:T(8,128)(2,1)S(1)}, bf16[1,320,128]{2,1,0:T(8,128)(2,1)S(1)}, u32[]{:S(2)}, u32[]{:S(2)}) %collective-permute-start.23) | collective-permute-done | bytes 81952 | tf_op jit(solution)/shard_map/sum1_from_layer_2/ppermute | solution.py:199
  70.5 1.0 %collective-permute-done.27.refs_10_ = bf16[1,320,128]{2,1,0:T(8,128)(2,1)S(1)} collective-permute-done((bf16[1,320,128]{2,1,0:T(8,128)(2,1)S(1)}, bf16[1,320,128]{2,1,0:T(8,128)(2,1)S(1)}, u32[]{:S(2)}, u32[]{:S(2)}) %collective-permute-start.27) | collective-permute-done | bytes 81952 | tf_op jit(solution)/shard_map/sum3_from_layer_2/ppermute | solution.py:199
  71.6 0.9 %finish.1 = f32[320,512]{1,0:T(8,128)} custom-call(s32[1]{0:T(128)} %bitcast.at_group.after.refs_0_, s32[1]{0:T(128)} %bitcast.1.at_ex.refs_1_, s32[1]{0:T(128)} %bitcast.2.at_layer.refs_2_, f32[1,320,128]{2,1,0:T(8,128)S(1)} %get-tuple-element.48.refs_8_.refs_3_, bf16[1,320,128]{2,1,0:T(8,128)(2,1)S(1)} %collective-permute-done.17.refs_4_, ...), custom_call_target="tpu_custom_call" | custom-call | tf_op jit(solution)/shard_map/finish/pallas_call | solution.py:181
  (28 shorter events, 0.2 us)
Async XLA Ops:
  1.0 9.3 %collective-permute-start.1 = (bf16[128,1024]{1,0:T(8,128)(2,1)S(1)}, bf16[128,1024]{1,0:T(8,128)(2,1)S(1)}, u32[]{:S(2)}, u32[]{:S(2)}) collective-permute-start(bf16[128,1024]{1,0:T(8,128)(2,1)S(1)} %take.2.after.refs_4_), channel_id=1, source_target_pairs={{0,8},{4,12},{8,0},{12,4},{1,9},{5,13},{9,1},{13,5},{2,10},{6,14},... | collective-permute-start | bytes 786440 | tf_op jit(solution)/shard_map/q0_from_chip/ppermute | solution.py:199
  4.0 8.1 %collective-permute-start = (bf16[128,1024]{1,0:T(8,128)(2,1)S(1)}, bf16[128,1024]{1,0:T(8,128)(2,1)S(1)}, u32[]{:S(2)}, u32[]{:S(2)}) collective-permute-start(bf16[128,1024]{1,0:T(8,128)(2,1)S(1)} %take.2.after.refs_4_), channel_id=1, source_target_pairs={{0,4},{4,0},{8,12},{12,8},{1,5},{5,1},{9,13},{13,9},{2,6},{6,2},{1... | collective-permute-start | bytes 786440 | tf_op jit(solution)/shard_map/q0_from_core/ppermute | solution.py:199
  8.4 21.9 %slice-start = ((s8[10485760]{0:T(1024)(128)(4,1)}), s8[4194304]{0:T(1024)(128)(4,1)S(1)}, s32[]{:S(2)}) async-start(s8[10485760]{0:T(1024)(128)(4,1)} %bitcast.6), calls=%async_computation | async-start | bytes 8388608
  8.4 21.9 %slice-start.1 = ((s8[10485760]{0:T(1024)(128)(4,1)}), s8[4194304]{0:T(1024)(128)(4,1)S(1)}, s32[]{:S(2)}) async-start(s8[10485760]{0:T(1024)(128)(4,1)} %bitcast.6), calls=%async_computation.1 | async-start | bytes 8388608
  10.3 1.8 %collective-permute-start.2 = (bf16[128,1024]{1,0:T(8,128)(2,1)S(1)}, bf16[128,1024]{1,0:T(8,128)(2,1)S(1)}, u32[]{:S(2)}, u32[]{:S(2)}) collective-permute-start(bf16[128,1024]{1,0:T(8,128)(2,1)S(1)} %collective-permute-done.1.refs_6_), channel_id=1, source_target_pairs={{0,4},{4,0},{8,12},{12,8},{1,5},{5,1},{9,13},{13,9},{2,6},{6,2},{1... | collective-permute-start | bytes 786440 | tf_op jit(solution)/shard_map/q0_there_from_core/ppermute | solution.py:199
  10.3 9.1 %collective-permute-start.6 = (bf16[128,1024]{1,0:T(8,128)(2,1)S(1)}, bf16[128,1024]{1,0:T(8,128)(2,1)S(1)}, u32[]{:S(2)}, u32[]{:S(2)}) collective-permute-start(bf16[128,1024]{1,0:T(8,128)(2,1)S(1)} %take.3.refs_8_.refs_4_), channel_id=1, source_target_pairs={{0,8},{4,12},{8,0},{12,4},{1,9},{5,13},{9,1},{13,5},{2,10},{6,14},... | collective-permute-start | bytes 786440 | tf_op jit(solution)/shard_map/q1_from_chip/ppermute | solution.py:199
  14.5 10.2 %collective-permute-start.4 = (bf16[1040,128]{1,0:T(8,128)(2,1)S(1)}, bf16[1040,128]{1,0:T(8,128)(2,1)S(1)}, u32[]{:S(2)}, u32[]{:S(2)}) collective-permute-start(bf16[1040,128]{1,0:T(8,128)(2,1)S(1)} %get-tuple-element.37), channel_id=1, source_target_pairs={{0,8},{4,12},{8,0},{12,4},{1,9},{5,13},{9,1},{13,5},{2,10},{6,14},... | collective-permute-start | bytes 798728 | tf_op jit(solution)/shard_map/s0_from_chip/ppermute | solution.py:199
  16.1 5.5 %collective-permute-start.5 = (bf16[128,1024]{1,0:T(8,128)(2,1)S(1)}, bf16[128,1024]{1,0:T(8,128)(2,1)S(1)}, u32[]{:S(2)}, u32[]{:S(2)}) collective-permute-start(bf16[128,1024]{1,0:T(8,128)(2,1)S(1)} %take.3.refs_8_.refs_4_), channel_id=1, source_target_pairs={{0,4},{4,0},{8,12},{12,8},{1,5},{5,1},{9,13},{13,9},{2,6},{6,2},{1... | collective-permute-start | bytes 786440 | tf_op jit(solution)/shard_map/q1_from_core/ppermute | solution.py:199
  19.4 2.2 %collective-permute-start.7 = (bf16[128,1024]{1,0:T(8,128)(2,1)S(1)}, bf16[128,1024]{1,0:T(8,128)(2,1)S(1)}, u32[]{:S(2)}, u32[]{:S(2)}) collective-permute-start(bf16[128,1024]{1,0:T(8,128)(2,1)S(1)} %collective-permute-done.6.refs_6_), channel_id=1, source_target_pairs={{0,4},{4,0},{8,12},{12,8},{1,5},{5,1},{9,13},{13,9},{2,6},{6,2},{1... | collective-permute-start | bytes 786440 | tf_op jit(solution)/shard_map/q1_there_from_core/ppermute | solution.py:199
  19.4 8.6 %collective-permute-start.3 = (bf16[1024,128]{1,0:T(8,128)(2,1)S(1)}, bf16[1024,128]{1,0:T(8,128)(2,1)S(1)}, u32[]{:S(2)}, u32[]{:S(2)}) collective-permute-start(bf16[1024,128]{1,0:T(8,128)(2,1)S(1)} %get-tuple-element.36.refs_8_.refs_4_), channel_id=1, source_target_pairs={{0,4},{4,0},{8,12},{12,8},{1,5},{5,1},{9,13},{13,9},{2,6},{6,2},{1... | collective-permute-start | bytes 786440 | tf_op jit(solution)/shard_map/s0_from_core/ppermute | solution.py:199
  19.9 10.4 %slice-start.2 = ((s8[10485760]{0:T(1024)(128)(4,1)}), s8[2097152]{0:T(1024)(128)(4,1)S(1)}, s32[]{:S(2)}) async-start(s8[10485760]{0:T(1024)(128)(4,1)} %bitcast.6), calls=%async_computation.2 | async-start | bytes 4194304
  19.9 8.6 %collective-permute-start.10 = (bf16[1040,128]{1,0:T(8,128)(2,1)S(1)}, bf16[1040,128]{1,0:T(8,128)(2,1)S(1)}, u32[]{:S(2)}, u32[]{:S(2)}) collective-permute-start(bf16[1040,128]{1,0:T(8,128)(2,1)S(1)} %get-tuple-element.43), channel_id=1, source_target_pairs={{0,16},{16,0},{1,17},{17,1},{2,18},{18,2},{3,19},{19,3},{4,20},{20... | collective-permute-start | bytes 798728 | tf_op jit(solution)/shard_map/s0_from_group/ppermute | solution.py:199
  24.7 5.5 %collective-permute-start.8 = (bf16[1040,128]{1,0:T(8,128)(2,1)S(1)}, bf16[1040,128]{1,0:T(8,128)(2,1)S(1)}, u32[]{:S(2)}, u32[]{:S(2)}) collective-permute-start(bf16[1040,128]{1,0:T(8,128)(2,1)S(1)} %collective-permute-done.4.refs_6_), channel_id=1, source_target_pairs={{0,4},{4,0},{8,12},{12,8},{1,5},{5,1},{9,13},{13,9},{2,6},{6,2},{1... | collective-permute-start | bytes 798728 | tf_op jit(solution)/shard_map/s0_there_from_core/ppermute | solution.py:199
  24.7 9.5 %collective-permute-start.12 = (bf16[1040,128]{1,0:T(8,128)(2,1)S(1)}, bf16[1040,128]{1,0:T(8,128)(2,1)S(1)}, u32[]{:S(2)}, u32[]{:S(2)}) collective-permute-start(bf16[1040,128]{1,0:T(8,128)(2,1)S(1)} %collective-permute-done.4.refs_6_), channel_id=1, source_target_pairs={{0,16},{16,0},{1,17},{17,1},{2,18},{18,2},{3,19},{19,3},{4,20},{20... | collective-permute-start | bytes 798728 | tf_op jit(solution)/shard_map/s0_there_from_group/ppermute | solution.py:199
  26.4 8.4 %collective-permute-start.15 = (bf16[1024,128]{1,0:T(8,128)(2,1)S(1)}, bf16[1024,128]{1,0:T(8,128)(2,1)S(1)}, u32[]{:S(2)}, u32[]{:S(2)}) collective-permute-start(bf16[1024,128]{1,0:T(8,128)(2,1)S(1)} %get-tuple-element.39.refs_8_), channel_id=1, source_target_pairs={{0,8},{4,12},{8,0},{12,4},{1,9},{5,13},{9,1},{13,5},{2,10},{6,14},... | collective-permute-start | bytes 786440 | tf_op jit(solution)/shard_map/s1_from_chip/ppermute | solution.py:199
  28.0 6.9 %collective-permute-start.14 = (bf16[1024,128]{1,0:T(8,128)(2,1)S(1)}, bf16[1024,128]{1,0:T(8,128)(2,1)S(1)}, u32[]{:S(2)}, u32[]{:S(2)}) collective-permute-start(bf16[1024,128]{1,0:T(8,128)(2,1)S(1)} %get-tuple-element.39.refs_8_), channel_id=1, source_target_pairs={{0,4},{4,0},{8,12},{12,8},{1,5},{5,1},{9,13},{13,9},{2,6},{6,2},{1... | collective-permute-start | bytes 786440 | tf_op jit(solution)/shard_map/s1_from_core/ppermute | solution.py:199
  28.6 11.4 %collective-permute-start.19 = (bf16[1040,128]{1,0:T(8,128)(2,1)S(1)}, bf16[1040,128]{1,0:T(8,128)(2,1)S(1)}, u32[]{:S(2)}, u32[]{:S(2)}) collective-permute-start(bf16[1040,128]{1,0:T(8,128)(2,1)S(1)} %get-tuple-element.52), channel_id=1, source_target_pairs={{0,16},{16,0},{1,17},{17,1},{2,18},{18,2},{3,19},{19,3},{4,20},{20... | collective-permute-start | bytes 798728 | tf_op jit(solution)/shard_map/s1_from_group/ppermute | solution.py:199
  30.3 11.5 %collective-permute-start.11 = (bf16[1040,128]{1,0:T(8,128)(2,1)S(1)}, bf16[1040,128]{1,0:T(8,128)(2,1)S(1)}, u32[]{:S(2)}, u32[]{:S(2)}) collective-permute-start(bf16[1040,128]{1,0:T(8,128)(2,1)S(1)} %collective-permute-done.10.refs_4_), channel_id=1, source_target_pairs={{0,4},{4,0},{8,12},{12,8},{1,5},{5,1},{9,13},{13,9},{2,6},{6,2},{1... | collective-permute-start | bytes 798728 | tf_op jit(solution)/shard_map/s0_across_from_core/ppermute | solution.py:199
  34.3 7.5 %collective-permute-start.13 = (bf16[1040,128]{1,0:T(8,128)(2,1)S(1)}, bf16[1040,128]{1,0:T(8,128)(2,1)S(1)}, u32[]{:S(2)}, u32[]{:S(2)}) collective-permute-start(bf16[1040,128]{1,0:T(8,128)(2,1)S(1)} %collective-permute-done.12.refs_6_), channel_id=1, source_target_pairs={{0,4},{4,0},{8,12},{12,8},{1,5},{5,1},{9,13},{13,9},{2,6},{6,2},{1... | collective-permute-start | bytes 798728 | tf_op jit(solution)/shard_map/s0_diagonal_from_core/ppermute | solution.py:199
  34.9 6.9 %collective-permute-start.16 = (bf16[1024,128]{1,0:T(8,128)(2,1)S(1)}, bf16[1024,128]{1,0:T(8,128)(2,1)S(1)}, u32[]{:S(2)}, u32[]{:S(2)}) collective-permute-start(bf16[1024,128]{1,0:T(8,128)(2,1)S(1)} %collective-permute-done.15.refs_10_), channel_id=1, source_target_pairs={{0,4},{4,0},{8,12},{12,8},{1,5},{5,1},{9,13},{13,9},{2,6},{6,2},{1... | collective-permute-start | bytes 786440 | tf_op jit(solution)/shard_map/s1_there_from_core/ppermute | solution.py:199
  34.9 10.8 %collective-permute-start.21 = (bf16[1024,128]{1,0:T(8,128)(2,1)S(1)}, bf16[1024,128]{1,0:T(8,128)(2,1)S(1)}, u32[]{:S(2)}, u32[]{:S(2)}) collective-permute-start(bf16[1024,128]{1,0:T(8,128)(2,1)S(1)} %collective-permute-done.15.refs_10_), channel_id=1, source_target_pairs={{0,16},{16,0},{1,17},{17,1},{2,18},{18,2},{3,19},{19,3},{4,20},{20... | collective-permute-start | bytes 786440 | tf_op jit(solution)/shard_map/s1_there_from_group/ppermute | solution.py:199
  40.0 5.6 %collective-permute-start.9 = (bf16[2,320,128]{2,1,0:T(8,128)(2,1)S(1)}, bf16[2,320,128]{2,1,0:T(8,128)(2,1)S(1)}, u32[]{:S(2)}, u32[]{:S(2)}) collective-permute-start(bf16[2,320,128]{2,1,0:T(8,128)(2,1)S(1)} %get-tuple-element.42), channel_id=1, source_target_pairs={{0,1},{1,0},{2,3},{3,2},{4,5},{5,4},{6,7},{7,6},{8,9},{9,8},{10,11... | collective-permute-start | bytes 491528 | tf_op jit(solution)/shard_map/sum0_from_layer_1/ppermute | solution.py:199
  45.6 2.6 %collective-permute-start.20 = (bf16[1040,128]{1,0:T(8,128)(2,1)S(1)}, bf16[1040,128]{1,0:T(8,128)(2,1)S(1)}, u32[]{:S(2)}, u32[]{:S(2)}) collective-permute-start(bf16[1040,128]{1,0:T(8,128)(2,1)S(1)} %collective-permute-done.19.refs_4_), channel_id=1, source_target_pairs={{0,4},{4,0},{8,12},{12,8},{1,5},{5,1},{9,13},{13,9},{2,6},{6,2},{1... | collective-permute-start | bytes 798728 | tf_op jit(solution)/shard_map/s1_across_from_core/ppermute | solution.py:199
  45.7 2.5 %collective-permute-start.22 = (bf16[1024,128]{1,0:T(8,128)(2,1)S(1)}, bf16[1024,128]{1,0:T(8,128)(2,1)S(1)}, u32[]{:S(2)}, u32[]{:S(2)}) collective-permute-start(bf16[1024,128]{1,0:T(8,128)(2,1)S(1)} %collective-permute-done.21.refs_6_), channel_id=1, source_target_pairs={{0,4},{4,0},{8,12},{12,8},{1,5},{5,1},{9,13},{13,9},{2,6},{6,2},{1... | collective-permute-start | bytes 786440 | tf_op jit(solution)/shard_map/s1_diagonal_from_core/ppermute | solution.py:199
  46.2 9.4 %collective-permute-start.24 = (bf16[2,320,128]{2,1,0:T(8,128)(2,1)S(1)}, bf16[2,320,128]{2,1,0:T(8,128)(2,1)S(1)}, u32[]{:S(2)}, u32[]{:S(2)}) collective-permute-start(bf16[2,320,128]{2,1,0:T(8,128)(2,1)S(1)} %get-tuple-element.59), channel_id=1, source_target_pairs={{0,1},{1,0},{2,3},{3,2},{4,5},{5,4},{6,7},{7,6},{8,9},{9,8},{10,11... | collective-permute-start | bytes 491528 | tf_op jit(solution)/shard_map/sum2_from_layer_1/ppermute | solution.py:199
  47.9 11.5 %collective-permute-start.18 = (bf16[2,320,128]{2,1,0:T(8,128)(2,1)S(1)}, bf16[2,320,128]{2,1,0:T(8,128)(2,1)S(1)}, u32[]{:S(2)}, u32[]{:S(2)}) collective-permute-start(bf16[2,320,128]{2,1,0:T(8,128)(2,1)S(1)} %get-tuple-element.51), channel_id=1, source_target_pairs={{0,1},{1,0},{2,3},{3,2},{4,5},{5,4},{6,7},{7,6},{8,9},{9,8},{10,11... | collective-permute-start | bytes 491528 | tf_op jit(solution)/shard_map/sum1_from_layer_1/ppermute | solution.py:199
  51.2 12.4 %collective-permute-start.26 = (bf16[2,320,128]{2,1,0:T(8,128)(2,1)S(1)}, bf16[2,320,128]{2,1,0:T(8,128)(2,1)S(1)}, u32[]{:S(2)}, u32[]{:S(2)}) collective-permute-start(bf16[2,320,128]{2,1,0:T(8,128)(2,1)S(1)} %get-tuple-element.62), channel_id=1, source_target_pairs={{0,1},{1,0},{2,3},{3,2},{4,5},{5,4},{6,7},{7,6},{8,9},{9,8},{10,11... | collective-permute-start | bytes 491528 | tf_op jit(solution)/shard_map/sum3_from_layer_1/ppermute | solution.py:199
  53.0 12.0 %collective-permute-start.17 = (bf16[1,320,128]{2,1,0:T(8,128)(2,1)S(1)}, bf16[1,320,128]{2,1,0:T(8,128)(2,1)S(1)}, u32[]{:S(2)}, u32[]{:S(2)}) collective-permute-start(bf16[1,320,128]{2,1,0:T(8,128)(2,1)S(1)} %get-tuple-element.49), channel_id=1, source_target_pairs={{0,2},{1,3},{2,0},{3,1},{4,6},{5,7},{6,4},{7,5},{8,10},{9,11},{10,... | collective-permute-start | bytes 245768 | tf_op jit(solution)/shard_map/sum0_from_layer_2/ppermute | solution.py:199
  55.6 9.3 %collective-permute-start.25 = (bf16[1,320,128]{2,1,0:T(8,128)(2,1)S(1)}, bf16[1,320,128]{2,1,0:T(8,128)(2,1)S(1)}, u32[]{:S(2)}, u32[]{:S(2)}) collective-permute-start(bf16[1,320,128]{2,1,0:T(8,128)(2,1)S(1)} %get-tuple-element.61), channel_id=1, source_target_pairs={{0,2},{1,3},{2,0},{3,1},{4,6},{5,7},{6,4},{7,5},{8,10},{9,11},{10,... | collective-permute-start | bytes 245768 | tf_op jit(solution)/shard_map/sum2_from_layer_2/ppermute | solution.py:199
  59.4 11.1 %collective-permute-start.23 = (bf16[1,320,128]{2,1,0:T(8,128)(2,1)S(1)}, bf16[1,320,128]{2,1,0:T(8,128)(2,1)S(1)}, u32[]{:S(2)}, u32[]{:S(2)}) collective-permute-start(bf16[1,320,128]{2,1,0:T(8,128)(2,1)S(1)} %get-tuple-element.58), channel_id=1, source_target_pairs={{0,2},{1,3},{2,0},{3,1},{4,6},{5,7},{6,4},{7,5},{8,10},{9,11},{10,... | collective-permute-start | bytes 245768 | tf_op jit(solution)/shard_map/sum1_from_layer_2/ppermute | solution.py:199
  63.6 7.9 %collective-permute-start.27 = (bf16[1,320,128]{2,1,0:T(8,128)(2,1)S(1)}, bf16[1,320,128]{2,1,0:T(8,128)(2,1)S(1)}, u32[]{:S(2)}, u32[]{:S(2)}) collective-permute-start(bf16[1,320,128]{2,1,0:T(8,128)(2,1)S(1)} %get-tuple-element.64), channel_id=1, source_target_pairs={{0,2},{1,3},{2,0},{3,1},{4,6},{5,7},{6,4},{7,5},{8,10},{9,11},{10,... | collective-permute-start | bytes 245768 | tf_op jit(solution)/shard_map/sum3_from_layer_2/ppermute | solution.py:199

commit v13 on v12

--- a/solution.py
+++ b/solution.py
@@ -100,15 +100,15 @@
     place, (store, *rest) = refs[:3], refs[3:]
     ids, blocks, _ = positions(*sizes, place)
     layers, count = len(blocks), len(ids)
-    pieces, (_, *outs, right) = rest[: columns * count], rest[columns * count :]
+    pieces, (_, *outs, right, total) = rest[: columns * count], rest[columns * count :]
     rows = store.shape[0] // layers
     depth, width = store.shape[1] // count, pieces[0].shape[1]
     for i, piece in enumerate(pieces):
         at = pl.ds(pl.multiple_of(ids[i % count] * depth, depth), depth)
         right[at, i // count * width : (i // count + 1) * width] = piece[:depth, :]
-    for r in reversed(range(layers)) if direct else [*range(1, layers, 2), *range(0, layers, 2)]:
-        at = pl.ds(pl.multiple_of(blocks[r] * rows, rows), rows)
-        part = jnp.dot(store[at, :], right[...], preferred_element_type=F32)
+    total[...] = jnp.dot(store[...], right[...], preferred_element_type=F32)
+    for r in range(layers):
+        part = total[pl.ds(pl.multiple_of(blocks[r] * rows, rows), rows), :]
         if direct:
             outs[r][0] = part.astype(outs[r].dtype)
             continue
@@ -130,7 +130,10 @@
         out_shape=[pltpu.VMEM(*shape) for shape in shapes],
         in_specs=[SMEM] * 3 + [VMEM] * (1 + len(flat)) + [ANY],
         out_specs=[VMEM] * len(shapes),
-        scratch_shapes=[pltpu.VMEM((store.shape[1], columns * width), BF16)],
+        scratch_shapes=[
+            pltpu.VMEM((store.shape[1], columns * width), BF16),
+            pltpu.VMEM((store.shape[0], columns * width), F32),
+        ],
         compiler_params=pltpu.CompilerParams(vmem_limit_bytes=12 * MIB),
         name=name,
     )(*place, store, *flat, after)

time: 72.7 us -> 72.8 us (level)
  waiting for transfers between devices: 23.2 us -> 21.2 us
  starting transfers between devices: 28.5 us -> 30.3 us
    ppermute x28, waiting for transfers between devices: 23.2 us -> 21.2 us  [permute(): return lax.ppermute(x, axis, perm)]
    ppermute x28, starting transfers between devices: 28.5 us -> 30.3 us  [permute(): return lax.ppermute(x, axis, perm)]
  transfers between devices with their start and end apart: 28 -> 28, of which waited for: 12 -> 13; matrix products, arithmetic and copies ran while one was open for 0% -> 0% of each run, Pallas kernels for 26% -> 26%
where the time goes in v13:
time: 72.8 us; the launch traced here: 72.6 us
  starting transfers between devices  30.3 us (42%)
  waiting for transfers between devices  21.2 us (29%)
  Pallas kernels  20.9 us (29%)
    ppermute x28, starting transfers between devices, permute(): return lax.ppermute(x, axis, perm)  30.3 us
    ppermute x28, waiting for transfers between devices, permute(): return lax.ppermute(x, axis, perm)  21.2 us
    pallas_call x3, Pallas kernels, score(): pl.pallas_call(functools.partial(score_kernel, sizes, columns, direct), o...  9.47 us
    pallas_call x2, Pallas kernels, condition(): pl.pallas_call(functools.partial(condition_kernel, sizes), out_shape=[plt...  5.04 us
    pallas_call x1, Pallas kernels, load(): pl.pallas_call(load_kernel, out_shape=pltpu.VMEM(source.shape, BF16), in_...  3.39 us
    pallas_call x2, Pallas kernels, take(): pl.pallas_call(functools.partial(take_kernel, chunk), out_shape=pltpu.VME...  1.92 us
  transfers between devices with their start and end apart: 28, of which 13 were waited for; matrix products, arithmetic and copies ran while one was open for 0% of the time, Pallas kernels for 26%

profile of v13, /device:TPU:0, one launch (start us, length us, event | category | flops | bytes accessed | tf_op | source)
XLA Modules:
  0.0 72.6 jit_solution(10577403174014039641)
XLA Ops:
  0.0 1.0 %take.2.after.refs_4_ = bf16[128,1024]{1,0:T(8,128)(2,1)S(1)} custom-call(s32[1]{0:T(128)} %bitcast.at_group.after.refs_0_, s32[1]{0:T(128)} %bitcast.1.at_ex.refs_1_, s32[1]{0:T(128)} %bitcast.2.at_layer.refs_2_, bf16[512,1024]{1,0:T(8,128)(2,1)} %bitcast.12, s32[1]{0:T(128)} %bitcast.at_group.after.refs_0_), custom_call_target="tpu_custom_call" | custom-call | tf_op jit(solution)/shard_map/take/pallas_call | solution.py:58
  1.0 3.0 %collective-permute-start.1 = (bf16[128,1024]{1,0:T(8,128)(2,1)S(1)}, bf16[128,1024]{1,0:T(8,128)(2,1)S(1)}, u32[]{:S(2)}, u32[]{:S(2)}) collective-permute-start(bf16[128,1024]{1,0:T(8,128)(2,1)S(1)} %take.2.after.refs_4_), channel_id=1, source_target_pairs={{0,8},{4,12},{8,0},{12,4},{1,9},{5,13},{9,1},{13,5},{2,10},{6,14},... | collective-permute-start | bytes 786440 | tf_op jit(solution)/shard_map/q0_from_chip/ppermute | solution.py:202
  4.0 3.4 %load.1.after.refs_3_ = bf16[1024,4096]{1,0:T(8,128)(2,1)S(1)} custom-call(bf16[1024,4096]{1,0:T(8,128)(2,1)} %bitcast.11, bf16[128,1024]{1,0:T(8,128)(2,1)S(1)} %take.2.after.refs_4_), custom_call_target="tpu_custom_call" | custom-call | tf_op jit(solution)/shard_map/load/pallas_call | solution.py:38
  7.4 1.0 %take.3.refs_8_.refs_4_ = bf16[128,1024]{1,0:T(8,128)(2,1)S(1)} custom-call(s32[1]{0:T(128)} %bitcast.at_group.after.refs_0_, s32[1]{0:T(128)} %bitcast.1.at_ex.refs_1_, s32[1]{0:T(128)} %bitcast.2.at_layer.refs_2_, bf16[512,1024]{1,0:T(8,128)(2,1)} %bitcast.13, bf16[1024,4096]{1,0:T(8,128)(2,1)S(1)} %load.1.after.refs_3_), custom_call_target="tpu_custom_call" | custom-call | tf_op jit(solution)/shard_map/take/pallas_call | solution.py:58
  8.4 0.0 slice-start
  8.4 0.0 slice-start.1
  8.4 1.9 %collective-permute-done.1.refs_6_ = bf16[128,1024]{1,0:T(8,128)(2,1)S(1)} collective-permute-done((bf16[128,1024]{1,0:T(8,128)(2,1)S(1)}, bf16[128,1024]{1,0:T(8,128)(2,1)S(1)}, u32[]{:S(2)}, u32[]{:S(2)}) %collective-permute-start.1) | collective-permute-done | bytes 262176 | tf_op jit(solution)/shard_map/q0_from_chip/ppermute | solution.py:202
  10.3 0.0 collective-permute-start.2
  10.3 1.7 %collective-permute-start.6 = (bf16[128,1024]{1,0:T(8,128)(2,1)S(1)}, bf16[128,1024]{1,0:T(8,128)(2,1)S(1)}, u32[]{:S(2)}, u32[]{:S(2)}) collective-permute-start(bf16[128,1024]{1,0:T(8,128)(2,1)S(1)} %take.3.refs_8_.refs_4_), channel_id=1, source_target_pairs={{0,8},{4,12},{8,0},{12,4},{1,9},{5,13},{9,1},{13,5},{2,10},{6,14},... | collective-permute-start | bytes 786440 | tf_op jit(solution)/shard_map/q1_from_chip/ppermute | solution.py:202
  12.1 2.5 %condition.2 = (bf16[1024,128]{1,0:T(8,128)(2,1)S(1)}, bf16[1040,128]{1,0:T(8,128)(2,1)S(1)}, bf16[1040,128]{1,0:T(8,128)(2,1)S(1)}) custom-call(s32[1]{0:T(128)} %bitcast.at_group.after.refs_0_, s32[1]{0:T(128)} %bitcast.1.at_ex.refs_1_, s32[1]{0:T(128)} %bitcast.2.at_layer.refs_2_, bf16[1024,4096]{1,0:T(8,128)(2,1)S(1)} %load.1.after.refs_3_, ...), custom_call_target="tpu_custom_call" | custom-call | tf_op jit(solution)/shard_map/condition/pallas_call | solution.py:88
  14.5 1.6 %collective-permute-start.4 = (bf16[1040,128]{1,0:T(8,128)(2,1)S(1)}, bf16[1040,128]{1,0:T(8,128)(2,1)S(1)}, u32[]{:S(2)}, u32[]{:S(2)}) collective-permute-start(bf16[1040,128]{1,0:T(8,128)(2,1)S(1)} %get-tuple-element.37), channel_id=1, source_target_pairs={{0,8},{4,12},{8,0},{12,4},{1,9},{5,13},{9,1},{13,5},{2,10},{6,14},... | collective-permute-start | bytes 798728 | tf_op jit(solution)/shard_map/s0_from_chip/ppermute | solution.py:202
  16.1 3.3 %collective-permute-done.6.refs_6_ = bf16[128,1024]{1,0:T(8,128)(2,1)S(1)} collective-permute-done((bf16[128,1024]{1,0:T(8,128)(2,1)S(1)}, bf16[128,1024]{1,0:T(8,128)(2,1)S(1)}, u32[]{:S(2)}, u32[]{:S(2)}) %collective-permute-start.6) | collective-permute-done | bytes 262176 | tf_op jit(solution)/shard_map/q1_from_chip/ppermute | solution.py:202
  19.4 0.0 collective-permute-start.7
  19.4 0.5 collective-permute-start.3
  19.9 1.7 %collective-permute-start.10 = (bf16[1040,128]{1,0:T(8,128)(2,1)S(1)}, bf16[1040,128]{1,0:T(8,128)(2,1)S(1)}, u32[]{:S(2)}, u32[]{:S(2)}) collective-permute-start(bf16[1040,128]{1,0:T(8,128)(2,1)S(1)} %get-tuple-element.43), channel_id=1, source_target_pairs={{0,16},{16,0},{1,17},{17,1},{2,18},{18,2},{3,19},{19,3},{4,20},{20... | collective-permute-start | bytes 798728 | tf_op jit(solution)/shard_map/s0_from_group/ppermute | solution.py:202
  21.6 0.0 collective-permute-done.5.refs_5_
  21.6 0.0 collective-permute-done.7.refs_7_
  21.6 2.6 %condition.3 = (bf16[1024,128]{1,0:T(8,128)(2,1)S(1)}, bf16[1040,128]{1,0:T(8,128)(2,1)S(1)}) custom-call(s32[1]{0:T(128)} %bitcast.at_group.after.refs_0_, s32[1]{0:T(128)} %bitcast.1.at_ex.refs_1_, s32[1]{0:T(128)} %bitcast.2.at_layer.refs_2_, bf16[1024,4096]{1,0:T(8,128)(2,1)S(1)} %load.1.after.refs_3_, bf16[128,1024]{1,0:T(8,128)(2,1)S(1)} %take.3.refs_8_.refs_4_, ...), custom_call_target="tpu_custom_call" | custom-call | tf_op jit(solution)/shard_map/condition/pallas_call | solution.py:88
  24.2 0.5 collective-permute-done.4.refs_6_
  24.7 0.0 collective-permute-start.8
  24.7 1.7 %collective-permute-start.12 = (bf16[1040,128]{1,0:T(8,128)(2,1)S(1)}, bf16[1040,128]{1,0:T(8,128)(2,1)S(1)}, u32[]{:S(2)}, u32[]{:S(2)}) collective-permute-start(bf16[1040,128]{1,0:T(8,128)(2,1)S(1)} %collective-permute-done.4.refs_6_), channel_id=1, source_target_pairs={{0,16},{16,0},{1,17},{17,1},{2,18},{18,2},{3,19},{19,3},{4,20},{20... | collective-permute-start | bytes 798728 | tf_op jit(solution)/shard_map/s0_there_from_group/ppermute | solution.py:202
  26.4 1.5 %collective-permute-start.15 = (bf16[1024,128]{1,0:T(8,128)(2,1)S(1)}, bf16[1024,128]{1,0:T(8,128)(2,1)S(1)}, u32[]{:S(2)}, u32[]{:S(2)}) collective-permute-start(bf16[1024,128]{1,0:T(8,128)(2,1)S(1)} %get-tuple-element.39.refs_8_), channel_id=1, source_target_pairs={{0,8},{4,12},{8,0},{12,4},{1,9},{5,13},{9,1},{13,5},{2,10},{6,14},... | collective-permute-start | bytes 786440 | tf_op jit(solution)/shard_map/s1_from_chip/ppermute | solution.py:202
  28.0 0.6 collective-permute-done.10.refs_4_
  28.6 1.7 %collective-permute-start.19 = (bf16[1040,128]{1,0:T(8,128)(2,1)S(1)}, bf16[1040,128]{1,0:T(8,128)(2,1)S(1)}, u32[]{:S(2)}, u32[]{:S(2)}) collective-permute-start(bf16[1040,128]{1,0:T(8,128)(2,1)S(1)} %get-tuple-element.52), channel_id=1, source_target_pairs={{0,16},{16,0},{1,17},{17,1},{2,18},{18,2},{3,19},{19,3},{4,20},{20... | collective-permute-start | bytes 798728 | tf_op jit(solution)/shard_map/s1_from_group/ppermute | solution.py:202
  30.3 3.0 %score0.1 = (bf16[2,320,128]{2,1,0:T(8,128)(2,1)S(1)}, f32[2,320,128]{2,1,0:T(8,128)S(1)}) custom-call(s32[1]{0:T(128)} %bitcast.at_group.after.refs_0_, s32[1]{0:T(128)} %bitcast.1.at_ex.refs_1_, s32[1]{0:T(128)} %bitcast.2.at_layer.refs_2_, bf16[1280,4096]{1,0:T(8,128)(2,1)S(1)} %bitcast.8, bf16[1024,128]{1,0:T(8,128)(2,1)S(1)} %get-tuple-element.36.refs_8_.refs_4_, ...), custom_call_target="tpu_custom_call" | custom-call | tf_op jit(solution)/shard_map/score0/pallas_call | solution.py:128
  33.3 0.9 %collective-permute-done.12.refs_6_ = bf16[1040,128]{1,0:T(8,128)(2,1)S(1)} collective-permute-done((bf16[1040,128]{1,0:T(8,128)(2,1)S(1)}, bf16[1040,128]{1,0:T(8,128)(2,1)S(1)}, u32[]{:S(2)}, u32[]{:S(2)}) %collective-permute-start.12) | collective-permute-done | bytes 266272 | tf_op jit(solution)/shard_map/s0_there_from_group/ppermute | solution.py:202
  34.3 0.6 collective-permute-done.15.refs_10_
  34.9 1.6 %collective-permute-start.21 = (bf16[1024,128]{1,0:T(8,128)(2,1)S(1)}, bf16[1024,128]{1,0:T(8,128)(2,1)S(1)}, u32[]{:S(2)}, u32[]{:S(2)}) collective-permute-start(bf16[1024,128]{1,0:T(8,128)(2,1)S(1)} %collective-permute-done.15.refs_10_), channel_id=1, source_target_pairs={{0,16},{16,0},{1,17},{17,1},{2,18},{18,2},{3,19},{19,3},{4,20},{20... | collective-permute-start | bytes 786440 | tf_op jit(solution)/shard_map/s1_there_from_group/ppermute | solution.py:202
  36.5 3.5 %collective-permute-done.19.refs_4_ = bf16[1040,128]{1,0:T(8,128)(2,1)S(1)} collective-permute-done((bf16[1040,128]{1,0:T(8,128)(2,1)S(1)}, bf16[1040,128]{1,0:T(8,128)(2,1)S(1)}, u32[]{:S(2)}, u32[]{:S(2)}) %collective-permute-start.19) | collective-permute-done | bytes 266272 | tf_op jit(solution)/shard_map/s1_from_group/ppermute | solution.py:202
  40.0 1.8 %collective-permute-start.9 = (bf16[2,320,128]{2,1,0:T(8,128)(2,1)S(1)}, bf16[2,320,128]{2,1,0:T(8,128)(2,1)S(1)}, u32[]{:S(2)}, u32[]{:S(2)}) collective-permute-start(bf16[2,320,128]{2,1,0:T(8,128)(2,1)S(1)} %get-tuple-element.42), channel_id=1, source_target_pairs={{0,1},{1,0},{2,3},{3,2},{4,5},{5,4},{6,7},{7,6},{8,9},{9,8},{10,11... | collective-permute-start | bytes 491528 | tf_op jit(solution)/shard_map/sum0_from_layer_1/ppermute | solution.py:202
  41.8 3.4 %score1.1 = (bf16[2,320,128]{2,1,0:T(8,128)(2,1)S(1)}, f32[2,320,128]{2,1,0:T(8,128)S(1)}, bf16[2,320,128]{2,1,0:T(8,128)(2,1)S(1)}, f32[2,320,128]{2,1,0:T(8,128)S(1)}) custom-call(s32[1]{0:T(128)} %bitcast.at_group.after.refs_0_, s32[1]{0:T(128)} %bitcast.1.at_ex.refs_1_, s32[1]{0:T(128)} %bitcast.2.at_layer.refs_2_, bf16[1280,4096]{1,0:T(8,128)(2,1)S(1)} %bitcast.9, ...), custom_call_target="tpu_custom_call" | custom-call | tf_op jit(solution)/shard_map/score1/pallas_call | solution.py:128
  45.2 0.4 collective-permute-done.9.got
  45.6 0.1 collective-permute-start.20
  45.7 0.5 collective-permute-start.22
  46.2 1.7 %collective-permute-start.24 = (bf16[2,320,128]{2,1,0:T(8,128)(2,1)S(1)}, bf16[2,320,128]{2,1,0:T(8,128)(2,1)S(1)}, u32[]{:S(2)}, u32[]{:S(2)}) collective-permute-start(bf16[2,320,128]{2,1,0:T(8,128)(2,1)S(1)} %get-tuple-element.59), channel_id=1, source_target_pairs={{0,1},{1,0},{2,3},{3,2},{4,5},{5,4},{6,7},{7,6},{8,9},{9,8},{10,11... | collective-permute-start | bytes 491528 | tf_op jit(solution)/shard_map/sum2_from_layer_1/ppermute | solution.py:202
  47.9 0.3 collective-permute-start.18
  48.2 3.0 %score2.1 = (bf16[2,320,128]{2,1,0:T(8,128)(2,1)S(1)}, f32[2,320,128]{2,1,0:T(8,128)S(1)}) custom-call(s32[1]{0:T(128)} %bitcast.at_group.after.refs_0_, s32[1]{0:T(128)} %bitcast.1.at_ex.refs_1_, s32[1]{0:T(128)} %bitcast.2.at_layer.refs_2_, bf16[1280,4096]{1,0:T(8,128)(2,1)S(1)} %bitcast.10, bf16[1040,128]{1,0:T(8,128)(2,1)S(1)} %collective-permute-done.19.refs_4_, ...), custom_call_target="tpu_custom_call" | custom-call | tf_op jit(solution)/shard_map/score2/pallas_call | solution.py:128
  51.3 1.8 %collective-permute-start.26 = (bf16[2,320,128]{2,1,0:T(8,128)(2,1)S(1)}, bf16[2,320,128]{2,1,0:T(8,128)(2,1)S(1)}, u32[]{:S(2)}, u32[]{:S(2)}) collective-permute-start(bf16[2,320,128]{2,1,0:T(8,128)(2,1)S(1)} %get-tuple-element.62), channel_id=1, source_target_pairs={{0,1},{1,0},{2,3},{3,2},{4,5},{5,4},{6,7},{7,6},{8,9},{9,8},{10,11... | collective-permute-start | bytes 491528 | tf_op jit(solution)/shard_map/sum3_from_layer_1/ppermute | solution.py:202
  53.1 2.6 %collective-permute-start.17 = (bf16[1,320,128]{2,1,0:T(8,128)(2,1)S(1)}, bf16[1,320,128]{2,1,0:T(8,128)(2,1)S(1)}, u32[]{:S(2)}, u32[]{:S(2)}) collective-permute-start(bf16[1,320,128]{2,1,0:T(8,128)(2,1)S(1)} %get-tuple-element.49), channel_id=1, source_target_pairs={{0,2},{1,3},{2,0},{3,1},{4,6},{5,7},{6,4},{7,5},{8,10},{9,11},{10,... | collective-permute-start | bytes 245768 | tf_op jit(solution)/shard_map/sum0_from_layer_2/ppermute | solution.py:202
  55.7 0.4 collective-permute-start.25
  56.1 1.5 %collective-permute-done.18.got = bf16[2,320,128]{2,1,0:T(8,128)(2,1)S(1)} collective-permute-done((bf16[2,320,128]{2,1,0:T(8,128)(2,1)S(1)}, bf16[2,320,128]{2,1,0:T(8,128)(2,1)S(1)}, u32[]{:S(2)}, u32[]{:S(2)}) %collective-permute-start.18) | collective-permute-done | bytes 163872 | tf_op jit(solution)/shard_map/sum1_from_layer_1/ppermute | solution.py:202
  57.7 4.5 %collective-permute-start.23 = (bf16[1,320,128]{2,1,0:T(8,128)(2,1)S(1)}, bf16[1,320,128]{2,1,0:T(8,128)(2,1)S(1)}, u32[]{:S(2)}, u32[]{:S(2)}) collective-permute-start(bf16[1,320,128]{2,1,0:T(8,128)(2,1)S(1)} %get-tuple-element.58), channel_id=1, source_target_pairs={{0,2},{1,3},{2,0},{3,1},{4,6},{5,7},{6,4},{7,5},{8,10},{9,11},{10,... | collective-permute-start | bytes 245768 | tf_op jit(solution)/shard_map/sum1_from_layer_2/ppermute | solution.py:202
  62.2 1.3 %collective-permute-done.26.got = bf16[2,320,128]{2,1,0:T(8,128)(2,1)S(1)} collective-permute-done((bf16[2,320,128]{2,1,0:T(8,128)(2,1)S(1)}, bf16[2,320,128]{2,1,0:T(8,128)(2,1)S(1)}, u32[]{:S(2)}, u32[]{:S(2)}) %collective-permute-start.26) | collective-permute-done | bytes 163872 | tf_op jit(solution)/shard_map/sum3_from_layer_1/ppermute | solution.py:202
  63.5 1.4 %collective-permute-start.27 = (bf16[1,320,128]{2,1,0:T(8,128)(2,1)S(1)}, bf16[1,320,128]{2,1,0:T(8,128)(2,1)S(1)}, u32[]{:S(2)}, u32[]{:S(2)}) collective-permute-start(bf16[1,320,128]{2,1,0:T(8,128)(2,1)S(1)} %get-tuple-element.64), channel_id=1, source_target_pairs={{0,2},{1,3},{2,0},{3,1},{4,6},{5,7},{6,4},{7,5},{8,10},{9,11},{10,... | collective-permute-start | bytes 245768 | tf_op jit(solution)/shard_map/sum3_from_layer_2/ppermute | solution.py:202
  65.0 3.0 %collective-permute-done.25.refs_8_ = bf16[1,320,128]{2,1,0:T(8,128)(2,1)S(1)} collective-permute-done((bf16[1,320,128]{2,1,0:T(8,128)(2,1)S(1)}, bf16[1,320,128]{2,1,0:T(8,128)(2,1)S(1)}, u32[]{:S(2)}, u32[]{:S(2)}) %collective-permute-start.25) | collective-permute-done | bytes 81952 | tf_op jit(solution)/shard_map/sum2_from_layer_2/ppermute | solution.py:202
  67.9 2.6 %collective-permute-done.23.refs_6_ = bf16[1,320,128]{2,1,0:T(8,128)(2,1)S(1)} collective-permute-done((bf16[1,320,128]{2,1,0:T(8,128)(2,1)S(1)}, bf16[1,320,128]{2,1,0:T(8,128)(2,1)S(1)}, u32[]{:S(2)}, u32[]{:S(2)}) %collective-permute-start.23) | collective-permute-done | bytes 81952 | tf_op jit(solution)/shard_map/sum1_from_layer_2/ppermute | solution.py:202
  70.6 1.1 %collective-permute-done.27.refs_10_ = bf16[1,320,128]{2,1,0:T(8,128)(2,1)S(1)} collective-permute-done((bf16[1,320,128]{2,1,0:T(8,128)(2,1)S(1)}, bf16[1,320,128]{2,1,0:T(8,128)(2,1)S(1)}, u32[]{:S(2)}, u32[]{:S(2)}) %collective-permute-start.27) | collective-permute-done | bytes 81952 | tf_op jit(solution)/shard_map/sum3_from_layer_2/ppermute | solution.py:202
  71.7 0.9 %finish.1 = f32[320,512]{1,0:T(8,128)} custom-call(s32[1]{0:T(128)} %bitcast.at_group.after.refs_0_, s32[1]{0:T(128)} %bitcast.1.at_ex.refs_1_, s32[1]{0:T(128)} %bitcast.2.at_layer.refs_2_, f32[1,320,128]{2,1,0:T(8,128)S(1)} %get-tuple-element.48.refs_8_.refs_3_, bf16[1,320,128]{2,1,0:T(8,128)(2,1)S(1)} %collective-permute-done.17.refs_4_, ...), custom_call_target="tpu_custom_call" | custom-call | tf_op jit(solution)/shard_map/finish/pallas_call | solution.py:184
  (28 shorter events, 0.2 us)
Async XLA Ops:
  1.0 9.3 %collective-permute-start.1 = (bf16[128,1024]{1,0:T(8,128)(2,1)S(1)}, bf16[128,1024]{1,0:T(8,128)(2,1)S(1)}, u32[]{:S(2)}, u32[]{:S(2)}) collective-permute-start(bf16[128,1024]{1,0:T(8,128)(2,1)S(1)} %take.2.after.refs_4_), channel_id=1, source_target_pairs={{0,8},{4,12},{8,0},{12,4},{1,9},{5,13},{9,1},{13,5},{2,10},{6,14},... | collective-permute-start | bytes 786440 | tf_op jit(solution)/shard_map/q0_from_chip/ppermute | solution.py:202
  4.0 8.1 %collective-permute-start = (bf16[128,1024]{1,0:T(8,128)(2,1)S(1)}, bf16[128,1024]{1,0:T(8,128)(2,1)S(1)}, u32[]{:S(2)}, u32[]{:S(2)}) collective-permute-start(bf16[128,1024]{1,0:T(8,128)(2,1)S(1)} %take.2.after.refs_4_), channel_id=1, source_target_pairs={{0,4},{4,0},{8,12},{12,8},{1,5},{5,1},{9,13},{13,9},{2,6},{6,2},{1... | collective-permute-start | bytes 786440 | tf_op jit(solution)/shard_map/q0_from_core/ppermute | solution.py:202
  8.4 21.9 %slice-start = ((s8[10485760]{0:T(1024)(128)(4,1)}), s8[4194304]{0:T(1024)(128)(4,1)S(1)}, s32[]{:S(2)}) async-start(s8[10485760]{0:T(1024)(128)(4,1)} %bitcast.6), calls=%async_computation | async-start | bytes 8388608
  8.4 21.9 %slice-start.1 = ((s8[10485760]{0:T(1024)(128)(4,1)}), s8[4194304]{0:T(1024)(128)(4,1)S(1)}, s32[]{:S(2)}) async-start(s8[10485760]{0:T(1024)(128)(4,1)} %bitcast.6), calls=%async_computation.1 | async-start | bytes 8388608
  10.3 1.8 %collective-permute-start.2 = (bf16[128,1024]{1,0:T(8,128)(2,1)S(1)}, bf16[128,1024]{1,0:T(8,128)(2,1)S(1)}, u32[]{:S(2)}, u32[]{:S(2)}) collective-permute-start(bf16[128,1024]{1,0:T(8,128)(2,1)S(1)} %collective-permute-done.1.refs_6_), channel_id=1, source_target_pairs={{0,4},{4,0},{8,12},{12,8},{1,5},{5,1},{9,13},{13,9},{2,6},{6,2},{1... | collective-permute-start | bytes 786440 | tf_op jit(solution)/shard_map/q0_there_from_core/ppermute | solution.py:202
  10.3 9.1 %collective-permute-start.6 = (bf16[128,1024]{1,0:T(8,128)(2,1)S(1)}, bf16[128,1024]{1,0:T(8,128)(2,1)S(1)}, u32[]{:S(2)}, u32[]{:S(2)}) collective-permute-start(bf16[128,1024]{1,0:T(8,128)(2,1)S(1)} %take.3.refs_8_.refs_4_), channel_id=1, source_target_pairs={{0,8},{4,12},{8,0},{12,4},{1,9},{5,13},{9,1},{13,5},{2,10},{6,14},... | collective-permute-start | bytes 786440 | tf_op jit(solution)/shard_map/q1_from_chip/ppermute | solution.py:202
  14.5 10.2 %collective-permute-start.4 = (bf16[1040,128]{1,0:T(8,128)(2,1)S(1)}, bf16[1040,128]{1,0:T(8,128)(2,1)S(1)}, u32[]{:S(2)}, u32[]{:S(2)}) collective-permute-start(bf16[1040,128]{1,0:T(8,128)(2,1)S(1)} %get-tuple-element.37), channel_id=1, source_target_pairs={{0,8},{4,12},{8,0},{12,4},{1,9},{5,13},{9,1},{13,5},{2,10},{6,14},... | collective-permute-start | bytes 798728 | tf_op jit(solution)/shard_map/s0_from_chip/ppermute | solution.py:202
  16.1 5.5 %collective-permute-start.5 = (bf16[128,1024]{1,0:T(8,128)(2,1)S(1)}, bf16[128,1024]{1,0:T(8,128)(2,1)S(1)}, u32[]{:S(2)}, u32[]{:S(2)}) collective-permute-start(bf16[128,1024]{1,0:T(8,128)(2,1)S(1)} %take.3.refs_8_.refs_4_), channel_id=1, source_target_pairs={{0,4},{4,0},{8,12},{12,8},{1,5},{5,1},{9,13},{13,9},{2,6},{6,2},{1... | collective-permute-start | bytes 786440 | tf_op jit(solution)/shard_map/q1_from_core/ppermute | solution.py:202
  19.4 2.2 %collective-permute-start.7 = (bf16[128,1024]{1,0:T(8,128)(2,1)S(1)}, bf16[128,1024]{1,0:T(8,128)(2,1)S(1)}, u32[]{:S(2)}, u32[]{:S(2)}) collective-permute-start(bf16[128,1024]{1,0:T(8,128)(2,1)S(1)} %collective-permute-done.6.refs_6_), channel_id=1, source_target_pairs={{0,4},{4,0},{8,12},{12,8},{1,5},{5,1},{9,13},{13,9},{2,6},{6,2},{1... | collective-permute-start | bytes 786440 | tf_op jit(solution)/shard_map/q1_there_from_core/ppermute | solution.py:202
  19.4 8.6 %collective-permute-start.3 = (bf16[1024,128]{1,0:T(8,128)(2,1)S(1)}, bf16[1024,128]{1,0:T(8,128)(2,1)S(1)}, u32[]{:S(2)}, u32[]{:S(2)}) collective-permute-start(bf16[1024,128]{1,0:T(8,128)(2,1)S(1)} %get-tuple-element.36.refs_8_.refs_4_), channel_id=1, source_target_pairs={{0,4},{4,0},{8,12},{12,8},{1,5},{5,1},{9,13},{13,9},{2,6},{6,2},{1... | collective-permute-start | bytes 786440 | tf_op jit(solution)/shard_map/s0_from_core/ppermute | solution.py:202
  19.9 10.4 %slice-start.2 = ((s8[10485760]{0:T(1024)(128)(4,1)}), s8[2097152]{0:T(1024)(128)(4,1)S(1)}, s32[]{:S(2)}) async-start(s8[10485760]{0:T(1024)(128)(4,1)} %bitcast.6), calls=%async_computation.2 | async-start | bytes 4194304
  19.9 8.6 %collective-permute-start.10 = (bf16[1040,128]{1,0:T(8,128)(2,1)S(1)}, bf16[1040,128]{1,0:T(8,128)(2,1)S(1)}, u32[]{:S(2)}, u32[]{:S(2)}) collective-permute-start(bf16[1040,128]{1,0:T(8,128)(2,1)S(1)} %get-tuple-element.43), channel_id=1, source_target_pairs={{0,16},{16,0},{1,17},{17,1},{2,18},{18,2},{3,19},{19,3},{4,20},{20... | collective-permute-start | bytes 798728 | tf_op jit(solution)/shard_map/s0_from_group/ppermute | solution.py:202
  24.7 5.5 %collective-permute-start.8 = (bf16[1040,128]{1,0:T(8,128)(2,1)S(1)}, bf16[1040,128]{1,0:T(8,128)(2,1)S(1)}, u32[]{:S(2)}, u32[]{:S(2)}) collective-permute-start(bf16[1040,128]{1,0:T(8,128)(2,1)S(1)} %collective-permute-done.4.refs_6_), channel_id=1, source_target_pairs={{0,4},{4,0},{8,12},{12,8},{1,5},{5,1},{9,13},{13,9},{2,6},{6,2},{1... | collective-permute-start | bytes 798728 | tf_op jit(solution)/shard_map/s0_there_from_core/ppermute | solution.py:202
  24.7 9.5 %collective-permute-start.12 = (bf16[1040,128]{1,0:T(8,128)(2,1)S(1)}, bf16[1040,128]{1,0:T(8,128)(2,1)S(1)}, u32[]{:S(2)}, u32[]{:S(2)}) collective-permute-start(bf16[1040,128]{1,0:T(8,128)(2,1)S(1)} %collective-permute-done.4.refs_6_), channel_id=1, source_target_pairs={{0,16},{16,0},{1,17},{17,1},{2,18},{18,2},{3,19},{19,3},{4,20},{20... | collective-permute-start | bytes 798728 | tf_op jit(solution)/shard_map/s0_there_from_group/ppermute | solution.py:202
  26.4 8.4 %collective-permute-start.15 = (bf16[1024,128]{1,0:T(8,128)(2,1)S(1)}, bf16[1024,128]{1,0:T(8,128)(2,1)S(1)}, u32[]{:S(2)}, u32[]{:S(2)}) collective-permute-start(bf16[1024,128]{1,0:T(8,128)(2,1)S(1)} %get-tuple-element.39.refs_8_), channel_id=1, source_target_pairs={{0,8},{4,12},{8,0},{12,4},{1,9},{5,13},{9,1},{13,5},{2,10},{6,14},... | collective-permute-start | bytes 786440 | tf_op jit(solution)/shard_map/s1_from_chip/ppermute | solution.py:202
  28.0 6.9 %collective-permute-start.14 = (bf16[1024,128]{1,0:T(8,128)(2,1)S(1)}, bf16[1024,128]{1,0:T(8,128)(2,1)S(1)}, u32[]{:S(2)}, u32[]{:S(2)}) collective-permute-start(bf16[1024,128]{1,0:T(8,128)(2,1)S(1)} %get-tuple-element.39.refs_8_), channel_id=1, source_target_pairs={{0,4},{4,0},{8,12},{12,8},{1,5},{5,1},{9,13},{13,9},{2,6},{6,2},{1... | collective-permute-start | bytes 786440 | tf_op jit(solution)/shard_map/s1_from_core/ppermute | solution.py:202
  28.6 11.4 %collective-permute-start.19 = (bf16[1040,128]{1,0:T(8,128)(2,1)S(1)}, bf16[1040,128]{1,0:T(8,128)(2,1)S(1)}, u32[]{:S(2)}, u32[]{:S(2)}) collective-permute-start(bf16[1040,128]{1,0:T(8,128)(2,1)S(1)} %get-tuple-element.52), channel_id=1, source_target_pairs={{0,16},{16,0},{1,17},{17,1},{2,18},{18,2},{3,19},{19,3},{4,20},{20... | collective-permute-start | bytes 798728 | tf_op jit(solution)/shard_map/s1_from_group/ppermute | solution.py:202
  30.3 11.5 %collective-permute-start.11 = (bf16[1040,128]{1,0:T(8,128)(2,1)S(1)}, bf16[1040,128]{1,0:T(8,128)(2,1)S(1)}, u32[]{:S(2)}, u32[]{:S(2)}) collective-permute-start(bf16[1040,128]{1,0:T(8,128)(2,1)S(1)} %collective-permute-done.10.refs_4_), channel_id=1, source_target_pairs={{0,4},{4,0},{8,12},{12,8},{1,5},{5,1},{9,13},{13,9},{2,6},{6,2},{1... | collective-permute-start | bytes 798728 | tf_op jit(solution)/shard_map/s0_across_from_core/ppermute | solution.py:202
  34.3 7.5 %collective-permute-start.13 = (bf16[1040,128]{1,0:T(8,128)(2,1)S(1)}, bf16[1040,128]{1,0:T(8,128)(2,1)S(1)}, u32[]{:S(2)}, u32[]{:S(2)}) collective-permute-start(bf16[1040,128]{1,0:T(8,128)(2,1)S(1)} %collective-permute-done.12.refs_6_), channel_id=1, source_target_pairs={{0,4},{4,0},{8,12},{12,8},{1,5},{5,1},{9,13},{13,9},{2,6},{6,2},{1... | collective-permute-start | bytes 798728 | tf_op jit(solution)/shard_map/s0_diagonal_from_core/ppermute | solution.py:202
  34.9 6.9 %collective-permute-start.16 = (bf16[1024,128]{1,0:T(8,128)(2,1)S(1)}, bf16[1024,128]{1,0:T(8,128)(2,1)S(1)}, u32[]{:S(2)}, u32[]{:S(2)}) collective-permute-start(bf16[1024,128]{1,0:T(8,128)(2,1)S(1)} %collective-permute-done.15.refs_10_), channel_id=1, source_target_pairs={{0,4},{4,0},{8,12},{12,8},{1,5},{5,1},{9,13},{13,9},{2,6},{6,2},{1... | collective-permute-start | bytes 786440 | tf_op jit(solution)/shard_map/s1_there_from_core/ppermute | solution.py:202
  34.9 10.8 %collective-permute-start.21 = (bf16[1024,128]{1,0:T(8,128)(2,1)S(1)}, bf16[1024,128]{1,0:T(8,128)(2,1)S(1)}, u32[]{:S(2)}, u32[]{:S(2)}) collective-permute-start(bf16[1024,128]{1,0:T(8,128)(2,1)S(1)} %collective-permute-done.15.refs_10_), channel_id=1, source_target_pairs={{0,16},{16,0},{1,17},{17,1},{2,18},{18,2},{3,19},{19,3},{4,20},{20... | collective-permute-start | bytes 786440 | tf_op jit(solution)/shard_map/s1_there_from_group/ppermute | solution.py:202
  40.0 5.6 %collective-permute-start.9 = (bf16[2,320,128]{2,1,0:T(8,128)(2,1)S(1)}, bf16[2,320,128]{2,1,0:T(8,128)(2,1)S(1)}, u32[]{:S(2)}, u32[]{:S(2)}) collective-permute-start(bf16[2,320,128]{2,1,0:T(8,128)(2,1)S(1)} %get-tuple-element.42), channel_id=1, source_target_pairs={{0,1},{1,0},{2,3},{3,2},{4,5},{5,4},{6,7},{7,6},{8,9},{9,8},{10,11... | collective-permute-start | bytes 491528 | tf_op jit(solution)/shard_map/sum0_from_layer_1/ppermute | solution.py:202
  45.6 2.6 %collective-permute-start.20 = (bf16[1040,128]{1,0:T(8,128)(2,1)S(1)}, bf16[1040,128]{1,0:T(8,128)(2,1)S(1)}, u32[]{:S(2)}, u32[]{:S(2)}) collective-permute-start(bf16[1040,128]{1,0:T(8,128)(2,1)S(1)} %collective-permute-done.19.refs_4_), channel_id=1, source_target_pairs={{0,4},{4,0},{8,12},{12,8},{1,5},{5,1},{9,13},{13,9},{2,6},{6,2},{1... | collective-permute-start | bytes 798728 | tf_op jit(solution)/shard_map/s1_across_from_core/ppermute | solution.py:202
  45.7 2.5 %collective-permute-start.22 = (bf16[1024,128]{1,0:T(8,128)(2,1)S(1)}, bf16[1024,128]{1,0:T(8,128)(2,1)S(1)}, u32[]{:S(2)}, u32[]{:S(2)}) collective-permute-start(bf16[1024,128]{1,0:T(8,128)(2,1)S(1)} %collective-permute-done.21.refs_6_), channel_id=1, source_target_pairs={{0,4},{4,0},{8,12},{12,8},{1,5},{5,1},{9,13},{13,9},{2,6},{6,2},{1... | collective-permute-start | bytes 786440 | tf_op jit(solution)/shard_map/s1_diagonal_from_core/ppermute | solution.py:202
  46.2 9.5 %collective-permute-start.24 = (bf16[2,320,128]{2,1,0:T(8,128)(2,1)S(1)}, bf16[2,320,128]{2,1,0:T(8,128)(2,1)S(1)}, u32[]{:S(2)}, u32[]{:S(2)}) collective-permute-start(bf16[2,320,128]{2,1,0:T(8,128)(2,1)S(1)} %get-tuple-element.59), channel_id=1, source_target_pairs={{0,1},{1,0},{2,3},{3,2},{4,5},{5,4},{6,7},{7,6},{8,9},{9,8},{10,11... | collective-permute-start | bytes 491528 | tf_op jit(solution)/shard_map/sum2_from_layer_1/ppermute | solution.py:202
  47.9 9.7 %collective-permute-start.18 = (bf16[2,320,128]{2,1,0:T(8,128)(2,1)S(1)}, bf16[2,320,128]{2,1,0:T(8,128)(2,1)S(1)}, u32[]{:S(2)}, u32[]{:S(2)}) collective-permute-start(bf16[2,320,128]{2,1,0:T(8,128)(2,1)S(1)} %get-tuple-element.51), channel_id=1, source_target_pairs={{0,1},{1,0},{2,3},{3,2},{4,5},{5,4},{6,7},{7,6},{8,9},{9,8},{10,11... | collective-permute-start | bytes 491528 | tf_op jit(solution)/shard_map/sum1_from_layer_1/ppermute | solution.py:202
  51.3 12.2 %collective-permute-start.26 = (bf16[2,320,128]{2,1,0:T(8,128)(2,1)S(1)}, bf16[2,320,128]{2,1,0:T(8,128)(2,1)S(1)}, u32[]{:S(2)}, u32[]{:S(2)}) collective-permute-start(bf16[2,320,128]{2,1,0:T(8,128)(2,1)S(1)} %get-tuple-element.62), channel_id=1, source_target_pairs={{0,1},{1,0},{2,3},{3,2},{4,5},{5,4},{6,7},{7,6},{8,9},{9,8},{10,11... | collective-permute-start | bytes 491528 | tf_op jit(solution)/shard_map/sum3_from_layer_1/ppermute | solution.py:202
  53.1 11.9 %collective-permute-start.17 = (bf16[1,320,128]{2,1,0:T(8,128)(2,1)S(1)}, bf16[1,320,128]{2,1,0:T(8,128)(2,1)S(1)}, u32[]{:S(2)}, u32[]{:S(2)}) collective-permute-start(bf16[1,320,128]{2,1,0:T(8,128)(2,1)S(1)} %get-tuple-element.49), channel_id=1, source_target_pairs={{0,2},{1,3},{2,0},{3,1},{4,6},{5,7},{6,4},{7,5},{8,10},{9,11},{10,... | collective-permute-start | bytes 245768 | tf_op jit(solution)/shard_map/sum0_from_layer_2/ppermute | solution.py:202
  55.7 12.2 %collective-permute-start.25 = (bf16[1,320,128]{2,1,0:T(8,128)(2,1)S(1)}, bf16[1,320,128]{2,1,0:T(8,128)(2,1)S(1)}, u32[]{:S(2)}, u32[]{:S(2)}) collective-permute-start(bf16[1,320,128]{2,1,0:T(8,128)(2,1)S(1)} %get-tuple-element.61), channel_id=1, source_target_pairs={{0,2},{1,3},{2,0},{3,1},{4,6},{5,7},{6,4},{7,5},{8,10},{9,11},{10,... | collective-permute-start | bytes 245768 | tf_op jit(solution)/shard_map/sum2_from_layer_2/ppermute | solution.py:202
  57.7 12.9 %collective-permute-start.23 = (bf16[1,320,128]{2,1,0:T(8,128)(2,1)S(1)}, bf16[1,320,128]{2,1,0:T(8,128)(2,1)S(1)}, u32[]{:S(2)}, u32[]{:S(2)}) collective-permute-start(bf16[1,320,128]{2,1,0:T(8,128)(2,1)S(1)} %get-tuple-element.58), channel_id=1, source_target_pairs={{0,2},{1,3},{2,0},{3,1},{4,6},{5,7},{6,4},{7,5},{8,10},{9,11},{10,... | collective-permute-start | bytes 245768 | tf_op jit(solution)/shard_map/sum1_from_layer_2/ppermute | solution.py:202
  63.5 8.1 %collective-permute-start.27 = (bf16[1,320,128]{2,1,0:T(8,128)(2,1)S(1)}, bf16[1,320,128]{2,1,0:T(8,128)(2,1)S(1)}, u32[]{:S(2)}, u32[]{:S(2)}) collective-permute-start(bf16[1,320,128]{2,1,0:T(8,128)(2,1)S(1)} %get-tuple-element.64), channel_id=1, source_target_pairs={{0,2},{1,3},{2,0},{3,1},{4,6},{5,7},{6,4},{7,5},{8,10},{9,11},{10,... | collective-permute-start | bytes 245768 | tf_op jit(solution)/shard_map/sum3_from_layer_2/ppermute | solution.py:202

commit v14 on v12

--- a/solution.py
+++ b/solution.py
@@ -66,34 +66,54 @@
     )(*place, pltpu.with_memory_space_constraint(source, pltpu.HBM), after)
 
 
-def condition_kernel(sizes, *refs):
+def runs_of(ids, at_ids, depth):
+    if len(at_ids) == len(ids):
+        return [ids[t] * depth for t in at_ids], [(0, 0, len(ids) * depth)]
+    span = CORES * depth
+    at = [(i // CORES * CORES + lax.rem(ids[t], CORES)) * depth for i, t in enumerate(at_ids)]
+    return at, [(i * span, ids[t] // CORES * span, span) for i, t in enumerate(at_ids[::CORES])]
+
+
+def condition_kernel(sizes, at_ids, first, *refs):
     place, (hess, *rest) = refs[:3], refs[3:]
     ids, _, _ = positions(*sizes, place)
-    pieces, (_, *outs, right) = rest[: len(ids)], rest[len(ids) :]
-    width = pieces[0].shape[1]
-    for t, piece in zip(ids, pieces):
-        right[:, pl.ds(pl.multiple_of(t * width, width), width)] = piece[...]
-    height = hess.shape[0]
-    outs[0][...] = lax.dot_general(
-        hess[...], right[...], (((1,), (1,)), ((), ())), preferred_element_type=F32
-    ).astype(BF16)
+    pieces, rest = rest[: len(at_ids)], rest[len(at_ids) + 1 :]
+    before, (*outs, right) = rest[0] if first else None, rest[first:]
+    depth, height = pieces[0].shape[1], hess.shape[0]
+    places, runs = runs_of(ids, at_ids, depth)
+    for at, piece in zip(places, pieces):
+        right[:, pl.ds(pl.multiple_of(at, depth), depth)] = piece[...]
+    total = before[...] if first else None
+    for low, column, span in runs:
+        term = lax.dot_general(
+            hess[:, pl.ds(pl.multiple_of(column, depth), span)],
+            right[:, low : low + span],
+            (((1,), (1,)), ((), ())),
+            preferred_element_type=F32,
+        )
+        total = term if total is None else total + term
+    outs[0][...] = total.astype(outs[0].dtype)
     for out in outs[1:]:
         out[:height, :] = outs[0][...]
-        out[height:, :] = jnp.zeros((out.shape[0] - height, out.shape[1]), BF16)
-
-
-def condition(sizes, place, hess, pieces, after, more):
-    rows, queries = hess.shape[0], pieces[0].shape[0]
-    shapes = [(rows + count, queries) for count in (0, *more)]
-    return pl.pallas_call(
-        functools.partial(condition_kernel, sizes),
-        out_shape=[pltpu.VMEM(shape, BF16) for shape in shapes],
-        in_specs=[SMEM] * 3 + [VMEM] * (1 + len(pieces)) + [ANY],
+        if out.shape[0] > height:
+            out[height:, :] = jnp.zeros((out.shape[0] - height, out.shape[1]), BF16)
+
+
+def condition(sizes, place, hess, at_ids, pieces, after, more=None, before=None):
+    rows, (queries, depth) = hess.shape[0], pieces[0].shape
+    shapes = [((rows, queries), F32)]
+    if more is not None:
+        shapes = [((rows + count, queries), BF16) for count in (0, *more)]
+    first = [] if before is None else [before]
+    return pl.pallas_call(
+        functools.partial(condition_kernel, sizes, tuple(at_ids), len(first)),
+        out_shape=[pltpu.VMEM(*shape) for shape in shapes],
+        in_specs=[SMEM] * 3 + [VMEM] * (1 + len(pieces)) + [ANY] + [VMEM] * len(first),
         out_specs=[VMEM] * len(shapes),
-        scratch_shapes=[pltpu.VMEM((queries, hess.shape[1]), BF16)],
+        scratch_shapes=[pltpu.VMEM((queries, len(at_ids) * depth), BF16)],
         compiler_params=pltpu.CompilerParams(vmem_limit_bytes=12 * MIB),
-        name="condition",
-    )(*place, hess, *pieces, after)
+        name="condition" if more is not None else "condition_part",
+    )(*place, hess, *pieces, after, *first)
 
 
 def score_kernel(sizes, columns, direct, *refs):
@@ -257,12 +277,13 @@
     q0_there = after(q1, q0_there)
     q0_cores = [q0_core] + flip(q0_there, "q0_there")
     q1_there, q1_core = gather_chip(q1, "q1"), from_core(q1, "q1")
-    s0, s0_long, s0_longer = condition(sizes, place, hess, with_cores([q0] + q0_there, q0_cores), q1, (16, 16))
+    s0, s0_long, s0_longer = condition(sizes, place, hess, range(ex), with_cores([q0] + q0_there, q0_cores), q1, (16, 0))
     s0_there, s0_across, s0_core = gather_chip(s0_long, "s0"), gather_group(s0_longer, "s0"), from_core(s0, "s0")
-    q1_there = after(s0, q1_there)
-    q1_cores = [q1_core] + flip(q1_there, "q1_there")
-    s1, s1_long = condition(sizes, place, hess, with_cores([q1] + q1_there, q1_cores), s0, (16,))
-    s1_there, s1_core = gather_chip(s1, "s1"), from_core(s1, "s1")
+    part = condition(sizes, place, hess, range(CORES), [q1, q1_core], s0)[0]
+    q1_there = after(part, q1_there)
+    pieces = with_cores(q1_there, flip(q1_there, "q1_there"))
+    s1, s1_long, s1_longer = condition(sizes, place, hess, range(CORES, ex), pieces, part, (0, 32), part)
+    s1_there, s1_core = gather_chip(s1_longer, "s1"), from_core(s1, "s1")
     s0_there, s0_across = after(s1, s0_there), after(s1, s0_across)
     s0_diagonal = [gather_group(x, "s0_there") for x in s0_there]
     s0_cores = [s0_core] + flip(s0_there, "s0_there")

time: 72.7 us -> 74.7 us (1.028)
  starting transfers between devices: 28.5 us -> 29.6 us
  waiting for transfers between devices: 23.2 us -> 24.1 us
    ppermute x28, starting transfers between devices: 28.5 us -> 29.6 us  [permute(): return lax.ppermute(x, axis, perm)]
    ppermute x28, waiting for transfers between devices: 23.2 us -> 24.1 us  [permute(): return lax.ppermute(x, axis, perm)]
    pallas_call x2 -> x3, Pallas kernels: 5.04 us -> 5.11 us  [condition(): pl.pallas_call(functools.partial(condition_kernel, sizes, tuple(at_ids),...]
  transfers between devices with their start and end apart: 28 -> 28, of which waited for: 12 -> 9; matrix products, arithmetic and copies ran while one was open for 0% -> 0% of each run, Pallas kernels for 26% -> 25%
where the time goes in v14:
time: 74.7 us; the launch traced here: 74.5 us
  starting transfers between devices  29.6 us (40%)
  waiting for transfers between devices  24.1 us (32%)
  Pallas kernels  20.6 us (28%)
    ppermute x28, starting transfers between devices, permute(): return lax.ppermute(x, axis, perm)  29.6 us
    ppermute x28, waiting for transfers between devices, permute(): return lax.ppermute(x, axis, perm)  24.1 us
    pallas_call x3, Pallas kernels, score(): pl.pallas_call(functools.partial(score_kernel, sizes, columns, direct), o...  9.14 us
    pallas_call x3, Pallas kernels, condition(): pl.pallas_call(functools.partial(condition_kernel, sizes, tuple(at_ids),...  5.11 us
    pallas_call x1, Pallas kernels, load(): pl.pallas_call(load_kernel, out_shape=pltpu.VMEM(source.shape, BF16), in_...  3.39 us
    pallas_call x2, Pallas kernels, take(): pl.pallas_call(functools.partial(take_kernel, chunk), out_shape=pltpu.VME...  1.92 us
  transfers between devices with their start and end apart: 28, of which 9 were waited for; matrix products, arithmetic and copies ran while one was open for 0% of the time, Pallas kernels for 25%

profile of v14, /device:TPU:0, one launch (start us, length us, event | category | flops | bytes accessed | tf_op | source)
XLA Modules:
  0.0 74.5 jit_solution(17155486707096292485)
XLA Ops:
  0.0 1.0 %take.2.after.refs_4_ = bf16[128,1024]{1,0:T(8,128)(2,1)S(1)} custom-call(s32[1]{0:T(128)} %bitcast.at_group.after.refs_0_, s32[1]{0:T(128)} %bitcast.1.at_ex.refs_1_, s32[1]{0:T(128)} %bitcast.2.at_layer.refs_2_, bf16[512,1024]{1,0:T(8,128)(2,1)} %bitcast.12, s32[1]{0:T(128)} %bitcast.at_group.after.refs_0_), custom_call_target="tpu_custom_call" | custom-call | tf_op jit(solution)/shard_map/take/pallas_call | solution.py:58
  1.0 3.0 %collective-permute-start.1 = (bf16[128,1024]{1,0:T(8,128)(2,1)S(1)}, bf16[128,1024]{1,0:T(8,128)(2,1)S(1)}, u32[]{:S(2)}, u32[]{:S(2)}) collective-permute-start(bf16[128,1024]{1,0:T(8,128)(2,1)S(1)} %take.2.after.refs_4_), channel_id=1, source_target_pairs={{0,8},{4,12},{8,0},{12,4},{1,9},{5,13},{9,1},{13,5},{2,10},{6,14},... | collective-permute-start | bytes 786440 | tf_op jit(solution)/shard_map/q0_from_chip/ppermute | solution.py:219
  4.0 0.0 collective-permute-start
  4.0 3.4 %load.1.after.refs_3_ = bf16[1024,4096]{1,0:T(8,128)(2,1)S(1)} custom-call(bf16[1024,4096]{1,0:T(8,128)(2,1)} %bitcast.11, bf16[128,1024]{1,0:T(8,128)(2,1)S(1)} %take.2.after.refs_4_), custom_call_target="tpu_custom_call" | custom-call | tf_op jit(solution)/shard_map/load/pallas_call | solution.py:38
  7.4 1.0 %take.3.refs_8_.refs_4_ = bf16[128,1024]{1,0:T(8,128)(2,1)S(1)} custom-call(s32[1]{0:T(128)} %bitcast.at_group.after.refs_0_, s32[1]{0:T(128)} %bitcast.1.at_ex.refs_1_, s32[1]{0:T(128)} %bitcast.2.at_layer.refs_2_, bf16[512,1024]{1,0:T(8,128)(2,1)} %bitcast.13, bf16[1024,4096]{1,0:T(8,128)(2,1)S(1)} %load.1.after.refs_3_), custom_call_target="tpu_custom_call" | custom-call | tf_op jit(solution)/shard_map/take/pallas_call | solution.py:58
  8.4 1.9 %collective-permute-done.1.refs_6_ = bf16[128,1024]{1,0:T(8,128)(2,1)S(1)} collective-permute-done((bf16[128,1024]{1,0:T(8,128)(2,1)S(1)}, bf16[128,1024]{1,0:T(8,128)(2,1)S(1)}, u32[]{:S(2)}, u32[]{:S(2)}) %collective-permute-start.1) | collective-permute-done | bytes 262176 | tf_op jit(solution)/shard_map/q0_from_chip/ppermute | solution.py:219
  10.3 0.0 collective-permute-start.2
  10.3 0.5 collective-permute-start.6
  10.8 1.7 %collective-permute-start.5 = (bf16[128,1024]{1,0:T(8,128)(2,1)S(1)}, bf16[128,1024]{1,0:T(8,128)(2,1)S(1)}, u32[]{:S(2)}, u32[]{:S(2)}) collective-permute-start(bf16[128,1024]{1,0:T(8,128)(2,1)S(1)} %take.3.refs_8_.refs_4_), channel_id=1, source_target_pairs={{0,8},{4,12},{8,0},{12,4},{1,9},{5,13},{9,1},{13,5},{2,10},{6,14},... | collective-permute-start | bytes 786440 | tf_op jit(solution)/shard_map/q1_from_chip/ppermute | solution.py:219
  12.6 0.0 collective-permute-done.refs_5_
  12.6 0.0 collective-permute-done.2.refs_7_
  12.6 2.5 %condition.2 = (bf16[1024,128]{1,0:T(8,128)(2,1)S(1)}, bf16[1040,128]{1,0:T(8,128)(2,1)S(1)}, bf16[1024,128]{1,0:T(8,128)(2,1)S(1)}) custom-call(s32[1]{0:T(128)} %bitcast.at_group.after.refs_0_, s32[1]{0:T(128)} %bitcast.1.at_ex.refs_1_, s32[1]{0:T(128)} %bitcast.2.at_layer.refs_2_, bf16[1024,4096]{1,0:T(8,128)(2,1)S(1)} %load.1.after.refs_3_, ...), custom_call_target="tpu_custom_call" | custom-call | tf_op jit(solution)/shard_map/condition/pallas_call | solution.py:108
  15.0 1.1 %collective-permute-start.4 = (bf16[1040,128]{1,0:T(8,128)(2,1)S(1)}, bf16[1040,128]{1,0:T(8,128)(2,1)S(1)}, u32[]{:S(2)}, u32[]{:S(2)}) collective-permute-start(bf16[1040,128]{1,0:T(8,128)(2,1)S(1)} %get-tuple-element.38), channel_id=1, source_target_pairs={{0,8},{4,12},{8,0},{12,4},{1,9},{5,13},{9,1},{13,5},{2,10},{6,14},... | collective-permute-start | bytes 798728 | tf_op jit(solution)/shard_map/s0_from_chip/ppermute | solution.py:219
  16.1 1.3 %condition_part.1.refs_6_.refs_7_ = f32[1024,128]{1,0:T(8,128)S(1)} custom-call(s32[1]{0:T(128)} %bitcast.at_group.after.refs_0_, s32[1]{0:T(128)} %bitcast.1.at_ex.refs_1_, s32[1]{0:T(128)} %bitcast.2.at_layer.refs_2_, bf16[1024,4096]{1,0:T(8,128)(2,1)S(1)} %load.1.after.refs_3_, bf16[128,1024]{1,0:T(8,128)(2,1)S(1)} %take.3.refs_8_.refs_4_, ...), custom_call_target="tpu_custom_call" | custom-call | tf_op jit(solution)/shard_map/condition_part/pallas_call | solution.py:108
  17.4 2.6 %collective-permute-done.5.refs_4_ = bf16[128,1024]{1,0:T(8,128)(2,1)S(1)} collective-permute-done((bf16[128,1024]{1,0:T(8,128)(2,1)S(1)}, bf16[128,1024]{1,0:T(8,128)(2,1)S(1)}, u32[]{:S(2)}, u32[]{:S(2)}) %collective-permute-start.5) | collective-permute-done | bytes 262176 | tf_op jit(solution)/shard_map/q1_from_chip/ppermute | solution.py:219
  20.0 0.0 collective-permute-start.7
  20.0 1.7 %collective-permute-start.10 = (bf16[1024,128]{1,0:T(8,128)(2,1)S(1)}, bf16[1024,128]{1,0:T(8,128)(2,1)S(1)}, u32[]{:S(2)}, u32[]{:S(2)}) collective-permute-start(bf16[1024,128]{1,0:T(8,128)(2,1)S(1)} %get-tuple-element.44), channel_id=1, source_target_pairs={{0,16},{16,0},{1,17},{17,1},{2,18},{18,2},{3,19},{19,3},{4,20},{20... | collective-permute-start | bytes 786440 | tf_op jit(solution)/shard_map/s0_from_group/ppermute | solution.py:219
  21.7 0.2 collective-permute-start.3
  21.9 0.0 collective-permute-done.7.refs_5_
  21.9 1.4 %condition.3 = (bf16[1024,128]{1,0:T(8,128)(2,1)S(1)}, bf16[1024,128]{1,0:T(8,128)(2,1)S(1)}, bf16[1056,128]{1,0:T(8,128)(2,1)S(1)}) custom-call(s32[1]{0:T(128)} %bitcast.at_group.after.refs_0_, s32[1]{0:T(128)} %bitcast.1.at_ex.refs_1_, s32[1]{0:T(128)} %bitcast.2.at_layer.refs_2_, bf16[1024,4096]{1,0:T(8,128)(2,1)S(1)} %load.1.after.refs_3_, ...), custom_call_target="tpu_custom_call" | custom-call | tf_op jit(solution)/shard_map/condition/pallas_call | solution.py:108
  23.3 1.6 %collective-permute-start.15 = (bf16[1056,128]{1,0:T(8,128)(2,1)S(1)}, bf16[1056,128]{1,0:T(8,128)(2,1)S(1)}, u32[]{:S(2)}, u32[]{:S(2)}) collective-permute-start(bf16[1056,128]{1,0:T(8,128)(2,1)S(1)} %get-tuple-element.47), channel_id=1, source_target_pairs={{0,8},{4,12},{8,0},{12,4},{1,9},{5,13},{9,1},{13,5},{2,10},{6,14},... | collective-permute-start | bytes 811016 | tf_op jit(solution)/shard_map/s1_from_chip/ppermute | solution.py:219
  24.9 0.0 collective-permute-start.8
  24.9 1.6 %collective-permute-start.12 = (bf16[1040,128]{1,0:T(8,128)(2,1)S(1)}, bf16[1040,128]{1,0:T(8,128)(2,1)S(1)}, u32[]{:S(2)}, u32[]{:S(2)}) collective-permute-start(bf16[1040,128]{1,0:T(8,128)(2,1)S(1)} %collective-permute-done.4.refs_6_), channel_id=1, source_target_pairs={{0,16},{16,0},{1,17},{17,1},{2,18},{18,2},{3,19},{19,3},{4,20},{20... | collective-permute-start | bytes 798728 | tf_op jit(solution)/shard_map/s0_there_from_group/ppermute | solution.py:219
  26.5 2.6 %collective-permute-done.10.refs_4_ = bf16[1024,128]{1,0:T(8,128)(2,1)S(1)} collective-permute-done((bf16[1024,128]{1,0:T(8,128)(2,1)S(1)}, bf16[1024,128]{1,0:T(8,128)(2,1)S(1)}, u32[]{:S(2)}, u32[]{:S(2)}) %collective-permute-start.10) | collective-permute-done | bytes 262176 | tf_op jit(solution)/shard_map/s0_from_group/ppermute | solution.py:219
  29.1 0.5 collective-permute-start.14
  29.6 2.9 %score0.1 = (bf16[2,320,128]{2,1,0:T(8,128)(2,1)S(1)}, f32[2,320,128]{2,1,0:T(8,128)S(1)}) custom-call(s32[1]{0:T(128)} %bitcast.at_group.after.refs_0_, s32[1]{0:T(128)} %bitcast.1.at_ex.refs_1_, s32[1]{0:T(128)} %bitcast.2.at_layer.refs_2_, bf16[1280,4096]{1,0:T(8,128)(2,1)S(1)} %bitcast.8, bf16[1024,128]{1,0:T(8,128)(2,1)S(1)} %get-tuple-element.37.refs_6_.refs_4_, ...), custom_call_target="tpu_custom_call" | custom-call | tf_op jit(solution)/shard_map/score0/pallas_call | solution.py:148
  32.6 0.1 collective-permute-start.16
  32.7 1.8 %collective-permute-start.21 = (bf16[1056,128]{1,0:T(8,128)(2,1)S(1)}, bf16[1056,128]{1,0:T(8,128)(2,1)S(1)}, u32[]{:S(2)}, u32[]{:S(2)}) collective-permute-start(bf16[1056,128]{1,0:T(8,128)(2,1)S(1)} %collective-permute-done.15.refs_10_), channel_id=1, source_target_pairs={{0,16},{16,0},{1,17},{17,1},{2,18},{18,2},{3,19},{19,3},{4,20},{20... | collective-permute-start | bytes 811016 | tf_op jit(solution)/shard_map/s1_there_from_group/ppermute | solution.py:219
  34.5 0.2 collective-permute-start.13
  34.6 1.5 %collective-permute-start.19 = (bf16[1024,128]{1,0:T(8,128)(2,1)S(1)}, bf16[1024,128]{1,0:T(8,128)(2,1)S(1)}, u32[]{:S(2)}, u32[]{:S(2)}) collective-permute-start(bf16[1024,128]{1,0:T(8,128)(2,1)S(1)} %get-tuple-element.54), channel_id=1, source_target_pairs={{0,16},{16,0},{1,17},{17,1},{2,18},{18,2},{3,19},{19,3},{4,20},{20... | collective-permute-start | bytes 786440 | tf_op jit(solution)/shard_map/s1_from_group/ppermute | solution.py:219
  36.1 1.6 %collective-permute-start.9 = (bf16[2,320,128]{2,1,0:T(8,128)(2,1)S(1)}, bf16[2,320,128]{2,1,0:T(8,128)(2,1)S(1)}, u32[]{:S(2)}, u32[]{:S(2)}) collective-permute-start(bf16[2,320,128]{2,1,0:T(8,128)(2,1)S(1)} %get-tuple-element.43), channel_id=1, source_target_pairs={{0,1},{1,0},{2,3},{3,2},{4,5},{5,4},{6,7},{7,6},{8,9},{9,8},{10,11... | collective-permute-start | bytes 491528 | tf_op jit(solution)/shard_map/sum0_from_layer_1/ppermute | solution.py:219
  37.7 3.2 %score1.1 = (bf16[2,320,128]{2,1,0:T(8,128)(2,1)S(1)}, f32[2,320,128]{2,1,0:T(8,128)S(1)}, bf16[2,320,128]{2,1,0:T(8,128)(2,1)S(1)}, f32[2,320,128]{2,1,0:T(8,128)S(1)}) custom-call(s32[1]{0:T(128)} %bitcast.at_group.after.refs_0_, s32[1]{0:T(128)} %bitcast.1.at_ex.refs_1_, s32[1]{0:T(128)} %bitcast.2.at_layer.refs_2_, bf16[1280,4096]{1,0:T(8,128)(2,1)S(1)} %bitcast.9, ...), custom_call_target="tpu_custom_call" | custom-call | tf_op jit(solution)/shard_map/score1/pallas_call | solution.py:148
  41.0 1.5 %collective-permute-done.9.got = bf16[2,320,128]{2,1,0:T(8,128)(2,1)S(1)} collective-permute-done((bf16[2,320,128]{2,1,0:T(8,128)(2,1)S(1)}, bf16[2,320,128]{2,1,0:T(8,128)(2,1)S(1)}, u32[]{:S(2)}, u32[]{:S(2)}) %collective-permute-start.9) | collective-permute-done | bytes 163872 | tf_op jit(solution)/shard_map/sum0_from_layer_1/ppermute | solution.py:219
  42.5 0.1 collective-permute-start.22
  42.6 4.6 %collective-permute-done.19.refs_4_ = bf16[1024,128]{1,0:T(8,128)(2,1)S(1)} collective-permute-done((bf16[1024,128]{1,0:T(8,128)(2,1)S(1)}, bf16[1024,128]{1,0:T(8,128)(2,1)S(1)}, u32[]{:S(2)}, u32[]{:S(2)}) %collective-permute-start.19) | collective-permute-done | bytes 262176 | tf_op jit(solution)/shard_map/s1_from_group/ppermute | solution.py:219
  47.2 1.8 %collective-permute-start.24 = (bf16[2,320,128]{2,1,0:T(8,128)(2,1)S(1)}, bf16[2,320,128]{2,1,0:T(8,128)(2,1)S(1)}, u32[]{:S(2)}, u32[]{:S(2)}) collective-permute-start(bf16[2,320,128]{2,1,0:T(8,128)(2,1)S(1)} %get-tuple-element.61), channel_id=1, source_target_pairs={{0,1},{1,0},{2,3},{3,2},{4,5},{5,4},{6,7},{7,6},{8,9},{9,8},{10,11... | collective-permute-start | bytes 491528 | tf_op jit(solution)/shard_map/sum2_from_layer_1/ppermute | solution.py:219
  49.0 0.2 collective-permute-start.18
  49.2 2.9 %score2.1 = (bf16[2,320,128]{2,1,0:T(8,128)(2,1)S(1)}, f32[2,320,128]{2,1,0:T(8,128)S(1)}) custom-call(s32[1]{0:T(128)} %bitcast.at_group.after.refs_0_, s32[1]{0:T(128)} %bitcast.1.at_ex.refs_1_, s32[1]{0:T(128)} %bitcast.2.at_layer.refs_2_, bf16[1280,4096]{1,0:T(8,128)(2,1)S(1)} %bitcast.10, bf16[1024,128]{1,0:T(8,128)(2,1)S(1)} %collective-permute-done.19.refs_4_, ...), custom_call_target="tpu_custom_call" | custom-call | tf_op jit(solution)/shard_map/score2/pallas_call | solution.py:148
  52.2 1.9 %collective-permute-start.26 = (bf16[2,320,128]{2,1,0:T(8,128)(2,1)S(1)}, bf16[2,320,128]{2,1,0:T(8,128)(2,1)S(1)}, u32[]{:S(2)}, u32[]{:S(2)}) collective-permute-start(bf16[2,320,128]{2,1,0:T(8,128)(2,1)S(1)} %get-tuple-element.64), channel_id=1, source_target_pairs={{0,1},{1,0},{2,3},{3,2},{4,5},{5,4},{6,7},{7,6},{8,9},{9,8},{10,11... | collective-permute-start | bytes 491528 | tf_op jit(solution)/shard_map/sum3_from_layer_1/ppermute | solution.py:219
  54.1 2.6 %collective-permute-start.17 = (bf16[1,320,128]{2,1,0:T(8,128)(2,1)S(1)}, bf16[1,320,128]{2,1,0:T(8,128)(2,1)S(1)}, u32[]{:S(2)}, u32[]{:S(2)}) collective-permute-start(bf16[1,320,128]{2,1,0:T(8,128)(2,1)S(1)} %get-tuple-element.51), channel_id=1, source_target_pairs={{0,2},{1,3},{2,0},{3,1},{4,6},{5,7},{6,4},{7,5},{8,10},{9,11},{10,... | collective-permute-start | bytes 245768 | tf_op jit(solution)/shard_map/sum0_from_layer_2/ppermute | solution.py:219
  56.7 0.4 collective-permute-start.25
  57.1 2.3 %collective-permute-done.18.got = bf16[2,320,128]{2,1,0:T(8,128)(2,1)S(1)} collective-permute-done((bf16[2,320,128]{2,1,0:T(8,128)(2,1)S(1)}, bf16[2,320,128]{2,1,0:T(8,128)(2,1)S(1)}, u32[]{:S(2)}, u32[]{:S(2)}) %collective-permute-start.18) | collective-permute-done | bytes 163872 | tf_op jit(solution)/shard_map/sum1_from_layer_1/ppermute | solution.py:219
  59.5 3.7 %collective-permute-start.23 = (bf16[1,320,128]{2,1,0:T(8,128)(2,1)S(1)}, bf16[1,320,128]{2,1,0:T(8,128)(2,1)S(1)}, u32[]{:S(2)}, u32[]{:S(2)}) collective-permute-start(bf16[1,320,128]{2,1,0:T(8,128)(2,1)S(1)} %get-tuple-element.60), channel_id=1, source_target_pairs={{0,2},{1,3},{2,0},{3,1},{4,6},{5,7},{6,4},{7,5},{8,10},{9,11},{10,... | collective-permute-start | bytes 245768 | tf_op jit(solution)/shard_map/sum1_from_layer_2/ppermute | solution.py:219
  63.2 1.4 %collective-permute-done.26.got = bf16[2,320,128]{2,1,0:T(8,128)(2,1)S(1)} collective-permute-done((bf16[2,320,128]{2,1,0:T(8,128)(2,1)S(1)}, bf16[2,320,128]{2,1,0:T(8,128)(2,1)S(1)}, u32[]{:S(2)}, u32[]{:S(2)}) %collective-permute-start.26) | collective-permute-done | bytes 163872 | tf_op jit(solution)/shard_map/sum3_from_layer_1/ppermute | solution.py:219
  64.6 1.8 %collective-permute-start.27 = (bf16[1,320,128]{2,1,0:T(8,128)(2,1)S(1)}, bf16[1,320,128]{2,1,0:T(8,128)(2,1)S(1)}, u32[]{:S(2)}, u32[]{:S(2)}) collective-permute-start(bf16[1,320,128]{2,1,0:T(8,128)(2,1)S(1)} %get-tuple-element.66), channel_id=1, source_target_pairs={{0,2},{1,3},{2,0},{3,1},{4,6},{5,7},{6,4},{7,5},{8,10},{9,11},{10,... | collective-permute-start | bytes 245768 | tf_op jit(solution)/shard_map/sum3_from_layer_2/ppermute | solution.py:219
  66.4 5.5 %collective-permute-done.23.refs_6_ = bf16[1,320,128]{2,1,0:T(8,128)(2,1)S(1)} collective-permute-done((bf16[1,320,128]{2,1,0:T(8,128)(2,1)S(1)}, bf16[1,320,128]{2,1,0:T(8,128)(2,1)S(1)}, u32[]{:S(2)}, u32[]{:S(2)}) %collective-permute-start.23) | collective-permute-done | bytes 81952 | tf_op jit(solution)/shard_map/sum1_from_layer_2/ppermute | solution.py:219
  72.0 1.6 %collective-permute-done.27.refs_10_ = bf16[1,320,128]{2,1,0:T(8,128)(2,1)S(1)} collective-permute-done((bf16[1,320,128]{2,1,0:T(8,128)(2,1)S(1)}, bf16[1,320,128]{2,1,0:T(8,128)(2,1)S(1)}, u32[]{:S(2)}, u32[]{:S(2)}) %collective-permute-start.27) | collective-permute-done | bytes 81952 | tf_op jit(solution)/shard_map/sum3_from_layer_2/ppermute | solution.py:219
  73.5 0.9 %finish.1 = f32[320,512]{1,0:T(8,128)} custom-call(s32[1]{0:T(128)} %bitcast.at_group.after.refs_0_, s32[1]{0:T(128)} %bitcast.1.at_ex.refs_1_, s32[1]{0:T(128)} %bitcast.2.at_layer.refs_2_, f32[1,320,128]{2,1,0:T(8,128)S(1)} %get-tuple-element.50.refs_8_.refs_3_, bf16[1,320,128]{2,1,0:T(8,128)(2,1)S(1)} %collective-permute-done.17.refs_4_, ...), custom_call_target="tpu_custom_call" | custom-call | tf_op jit(solution)/shard_map/finish/pallas_call | solution.py:201
  (29 shorter events, 0.2 us)
Async XLA Ops:
  1.0 9.3 %collective-permute-start.1 = (bf16[128,1024]{1,0:T(8,128)(2,1)S(1)}, bf16[128,1024]{1,0:T(8,128)(2,1)S(1)}, u32[]{:S(2)}, u32[]{:S(2)}) collective-permute-start(bf16[128,1024]{1,0:T(8,128)(2,1)S(1)} %take.2.after.refs_4_), channel_id=1, source_target_pairs={{0,8},{4,12},{8,0},{12,4},{1,9},{5,13},{9,1},{13,5},{2,10},{6,14},... | collective-permute-start | bytes 786440 | tf_op jit(solution)/shard_map/q0_from_chip/ppermute | solution.py:219
  4.0 8.6 %collective-permute-start = (bf16[128,1024]{1,0:T(8,128)(2,1)S(1)}, bf16[128,1024]{1,0:T(8,128)(2,1)S(1)}, u32[]{:S(2)}, u32[]{:S(2)}) collective-permute-start(bf16[128,1024]{1,0:T(8,128)(2,1)S(1)} %take.2.after.refs_4_), channel_id=1, source_target_pairs={{0,4},{4,0},{8,12},{12,8},{1,5},{5,1},{9,13},{13,9},{2,6},{6,2},{1... | collective-permute-start | bytes 786440 | tf_op jit(solution)/shard_map/q0_from_core/ppermute | solution.py:219
  10.3 2.3 %collective-permute-start.2 = (bf16[128,1024]{1,0:T(8,128)(2,1)S(1)}, bf16[128,1024]{1,0:T(8,128)(2,1)S(1)}, u32[]{:S(2)}, u32[]{:S(2)}) collective-permute-start(bf16[128,1024]{1,0:T(8,128)(2,1)S(1)} %collective-permute-done.1.refs_6_), channel_id=1, source_target_pairs={{0,4},{4,0},{8,12},{12,8},{1,5},{5,1},{9,13},{13,9},{2,6},{6,2},{1... | collective-permute-start | bytes 786440 | tf_op jit(solution)/shard_map/q0_there_from_core/ppermute | solution.py:219
  10.3 5.8 %collective-permute-start.6 = (bf16[128,1024]{1,0:T(8,128)(2,1)S(1)}, bf16[128,1024]{1,0:T(8,128)(2,1)S(1)}, u32[]{:S(2)}, u32[]{:S(2)}) collective-permute-start(bf16[128,1024]{1,0:T(8,128)(2,1)S(1)} %take.3.refs_8_.refs_4_), channel_id=1, source_target_pairs={{0,4},{4,0},{8,12},{12,8},{1,5},{5,1},{9,13},{13,9},{2,6},{6,2},{1... | collective-permute-start | bytes 786440 | tf_op jit(solution)/shard_map/q1_from_core/ppermute | solution.py:219
  10.8 9.2 %collective-permute-start.5 = (bf16[128,1024]{1,0:T(8,128)(2,1)S(1)}, bf16[128,1024]{1,0:T(8,128)(2,1)S(1)}, u32[]{:S(2)}, u32[]{:S(2)}) collective-permute-start(bf16[128,1024]{1,0:T(8,128)(2,1)S(1)} %take.3.refs_8_.refs_4_), channel_id=1, source_target_pairs={{0,8},{4,12},{8,0},{12,4},{1,9},{5,13},{9,1},{13,5},{2,10},{6,14},... | collective-permute-start | bytes 786440 | tf_op jit(solution)/shard_map/q1_from_chip/ppermute | solution.py:219
  15.0 9.8 %collective-permute-start.4 = (bf16[1040,128]{1,0:T(8,128)(2,1)S(1)}, bf16[1040,128]{1,0:T(8,128)(2,1)S(1)}, u32[]{:S(2)}, u32[]{:S(2)}) collective-permute-start(bf16[1040,128]{1,0:T(8,128)(2,1)S(1)} %get-tuple-element.38), channel_id=1, source_target_pairs={{0,8},{4,12},{8,0},{12,4},{1,9},{5,13},{9,1},{13,5},{2,10},{6,14},... | collective-permute-start | bytes 798728 | tf_op jit(solution)/shard_map/s0_from_chip/ppermute | solution.py:219
  16.1 13.5 %slice-start = ((s8[10485760]{0:T(1024)(128)(4,1)}), s8[4194304]{0:T(1024)(128)(4,1)S(1)}, s32[]{:S(2)}) async-start(s8[10485760]{0:T(1024)(128)(4,1)} %bitcast.6), calls=%async_computation | async-start | bytes 8388608
  16.1 13.5 %slice-start.1 = ((s8[10485760]{0:T(1024)(128)(4,1)}), s8[4194304]{0:T(1024)(128)(4,1)S(1)}, s32[]{:S(2)}) async-start(s8[10485760]{0:T(1024)(128)(4,1)} %bitcast.6), calls=%async_computation.1 | async-start | bytes 8388608
  20.0 1.9 %collective-permute-start.7 = (bf16[128,1024]{1,0:T(8,128)(2,1)S(1)}, bf16[128,1024]{1,0:T(8,128)(2,1)S(1)}, u32[]{:S(2)}, u32[]{:S(2)}) collective-permute-start(bf16[128,1024]{1,0:T(8,128)(2,1)S(1)} %collective-permute-done.5.refs_4_), channel_id=1, source_target_pairs={{0,4},{4,0},{8,12},{12,8},{1,5},{5,1},{9,13},{13,9},{2,6},{6,2},{1... | collective-permute-start | bytes 786440 | tf_op jit(solution)/shard_map/q1_there_from_core/ppermute | solution.py:219
  20.0 9.6 %slice-start.2 = ((s8[10485760]{0:T(1024)(128)(4,1)}), s8[2097152]{0:T(1024)(128)(4,1)S(1)}, s32[]{:S(2)}) async-start(s8[10485760]{0:T(1024)(128)(4,1)} %bitcast.6), calls=%async_computation.2 | async-start | bytes 4194304
  20.0 9.1 %collective-permute-start.10 = (bf16[1024,128]{1,0:T(8,128)(2,1)S(1)}, bf16[1024,128]{1,0:T(8,128)(2,1)S(1)}, u32[]{:S(2)}, u32[]{:S(2)}) collective-permute-start(bf16[1024,128]{1,0:T(8,128)(2,1)S(1)} %get-tuple-element.44), channel_id=1, source_target_pairs={{0,16},{16,0},{1,17},{17,1},{2,18},{18,2},{3,19},{19,3},{4,20},{20... | collective-permute-start | bytes 786440 | tf_op jit(solution)/shard_map/s0_from_group/ppermute | solution.py:219
  21.7 7.4 %collective-permute-start.3 = (bf16[1024,128]{1,0:T(8,128)(2,1)S(1)}, bf16[1024,128]{1,0:T(8,128)(2,1)S(1)}, u32[]{:S(2)}, u32[]{:S(2)}) collective-permute-start(bf16[1024,128]{1,0:T(8,128)(2,1)S(1)} %get-tuple-element.37.refs_6_.refs_4_), channel_id=1, source_target_pairs={{0,4},{4,0},{8,12},{12,8},{1,5},{5,1},{9,13},{13,9},{2,6},{6,2},{1... | collective-permute-start | bytes 786440 | tf_op jit(solution)/shard_map/s0_from_core/ppermute | solution.py:219
  23.3 9.3 %collective-permute-start.15 = (bf16[1056,128]{1,0:T(8,128)(2,1)S(1)}, bf16[1056,128]{1,0:T(8,128)(2,1)S(1)}, u32[]{:S(2)}, u32[]{:S(2)}) collective-permute-start(bf16[1056,128]{1,0:T(8,128)(2,1)S(1)} %get-tuple-element.47), channel_id=1, source_target_pairs={{0,8},{4,12},{8,0},{12,4},{1,9},{5,13},{9,1},{13,5},{2,10},{6,14},... | collective-permute-start | bytes 811016 | tf_op jit(solution)/shard_map/s1_from_chip/ppermute | solution.py:219
  24.9 4.7 %collective-permute-start.8 = (bf16[1040,128]{1,0:T(8,128)(2,1)S(1)}, bf16[1040,128]{1,0:T(8,128)(2,1)S(1)}, u32[]{:S(2)}, u32[]{:S(2)}) collective-permute-start(bf16[1040,128]{1,0:T(8,128)(2,1)S(1)} %collective-permute-done.4.refs_6_), channel_id=1, source_target_pairs={{0,4},{4,0},{8,12},{12,8},{1,5},{5,1},{9,13},{13,9},{2,6},{6,2},{1... | collective-permute-start | bytes 798728 | tf_op jit(solution)/shard_map/s0_there_from_core/ppermute | solution.py:219
  24.9 9.6 %collective-permute-start.12 = (bf16[1040,128]{1,0:T(8,128)(2,1)S(1)}, bf16[1040,128]{1,0:T(8,128)(2,1)S(1)}, u32[]{:S(2)}, u32[]{:S(2)}) collective-permute-start(bf16[1040,128]{1,0:T(8,128)(2,1)S(1)} %collective-permute-done.4.refs_6_), channel_id=1, source_target_pairs={{0,16},{16,0},{1,17},{17,1},{2,18},{18,2},{3,19},{19,3},{4,20},{20... | collective-permute-start | bytes 798728 | tf_op jit(solution)/shard_map/s0_there_from_group/ppermute | solution.py:219
  29.1 5.5 %collective-permute-start.11 = (bf16[1024,128]{1,0:T(8,128)(2,1)S(1)}, bf16[1024,128]{1,0:T(8,128)(2,1)S(1)}, u32[]{:S(2)}, u32[]{:S(2)}) collective-permute-start(bf16[1024,128]{1,0:T(8,128)(2,1)S(1)} %collective-permute-done.10.refs_4_), channel_id=1, source_target_pairs={{0,4},{4,0},{8,12},{12,8},{1,5},{5,1},{9,13},{13,9},{2,6},{6,2},{1... | collective-permute-start | bytes 786440 | tf_op jit(solution)/shard_map/s0_across_from_core/ppermute | solution.py:219
  29.1 7.0 %collective-permute-start.14 = (bf16[1024,128]{1,0:T(8,128)(2,1)S(1)}, bf16[1024,128]{1,0:T(8,128)(2,1)S(1)}, u32[]{:S(2)}, u32[]{:S(2)}) collective-permute-start(bf16[1024,128]{1,0:T(8,128)(2,1)S(1)} %get-tuple-element.40.refs_8_), channel_id=1, source_target_pairs={{0,4},{4,0},{8,12},{12,8},{1,5},{5,1},{9,13},{13,9},{2,6},{6,2},{1... | collective-permute-start | bytes 786440 | tf_op jit(solution)/shard_map/s1_from_core/ppermute | solution.py:219
  32.6 5.1 %collective-permute-start.16 = (bf16[1056,128]{1,0:T(8,128)(2,1)S(1)}, bf16[1056,128]{1,0:T(8,128)(2,1)S(1)}, u32[]{:S(2)}, u32[]{:S(2)}) collective-permute-start(bf16[1056,128]{1,0:T(8,128)(2,1)S(1)} %collective-permute-done.15.refs_10_), channel_id=1, source_target_pairs={{0,4},{4,0},{8,12},{12,8},{1,5},{5,1},{9,13},{13,9},{2,6},{6,2},{1... | collective-permute-start | bytes 811016 | tf_op jit(solution)/shard_map/s1_there_from_core/ppermute | solution.py:219
  32.7 9.8 %collective-permute-start.21 = (bf16[1056,128]{1,0:T(8,128)(2,1)S(1)}, bf16[1056,128]{1,0:T(8,128)(2,1)S(1)}, u32[]{:S(2)}, u32[]{:S(2)}) collective-permute-start(bf16[1056,128]{1,0:T(8,128)(2,1)S(1)} %collective-permute-done.15.refs_10_), channel_id=1, source_target_pairs={{0,16},{16,0},{1,17},{17,1},{2,18},{18,2},{3,19},{19,3},{4,20},{20... | collective-permute-start | bytes 811016 | tf_op jit(solution)/shard_map/s1_there_from_group/ppermute | solution.py:219
  34.5 3.3 %collective-permute-start.13 = (bf16[1040,128]{1,0:T(8,128)(2,1)S(1)}, bf16[1040,128]{1,0:T(8,128)(2,1)S(1)}, u32[]{:S(2)}, u32[]{:S(2)}) collective-permute-start(bf16[1040,128]{1,0:T(8,128)(2,1)S(1)} %collective-permute-done.12.refs_6_), channel_id=1, source_target_pairs={{0,4},{4,0},{8,12},{12,8},{1,5},{5,1},{9,13},{13,9},{2,6},{6,2},{1... | collective-permute-start | bytes 798728 | tf_op jit(solution)/shard_map/s0_diagonal_from_core/ppermute | solution.py:219
  34.6 12.6 %collective-permute-start.19 = (bf16[1024,128]{1,0:T(8,128)(2,1)S(1)}, bf16[1024,128]{1,0:T(8,128)(2,1)S(1)}, u32[]{:S(2)}, u32[]{:S(2)}) collective-permute-start(bf16[1024,128]{1,0:T(8,128)(2,1)S(1)} %get-tuple-element.54), channel_id=1, source_target_pairs={{0,16},{16,0},{1,17},{17,1},{2,18},{18,2},{3,19},{19,3},{4,20},{20... | collective-permute-start | bytes 786440 | tf_op jit(solution)/shard_map/s1_from_group/ppermute | solution.py:219
  36.1 6.3 %collective-permute-start.9 = (bf16[2,320,128]{2,1,0:T(8,128)(2,1)S(1)}, bf16[2,320,128]{2,1,0:T(8,128)(2,1)S(1)}, u32[]{:S(2)}, u32[]{:S(2)}) collective-permute-start(bf16[2,320,128]{2,1,0:T(8,128)(2,1)S(1)} %get-tuple-element.43), channel_id=1, source_target_pairs={{0,1},{1,0},{2,3},{3,2},{4,5},{5,4},{6,7},{7,6},{8,9},{9,8},{10,11... | collective-permute-start | bytes 491528 | tf_op jit(solution)/shard_map/sum0_from_layer_1/ppermute | solution.py:219
  42.5 6.7 %collective-permute-start.22 = (bf16[1056,128]{1,0:T(8,128)(2,1)S(1)}, bf16[1056,128]{1,0:T(8,128)(2,1)S(1)}, u32[]{:S(2)}, u32[]{:S(2)}) collective-permute-start(bf16[1056,128]{1,0:T(8,128)(2,1)S(1)} %collective-permute-done.21.refs_6_), channel_id=1, source_target_pairs={{0,4},{4,0},{8,12},{12,8},{1,5},{5,1},{9,13},{13,9},{2,6},{6,2},{1... | collective-permute-start | bytes 811016 | tf_op jit(solution)/shard_map/s1_diagonal_from_core/ppermute | solution.py:219
  47.2 2.0 %collective-permute-start.20 = (bf16[1024,128]{1,0:T(8,128)(2,1)S(1)}, bf16[1024,128]{1,0:T(8,128)(2,1)S(1)}, u32[]{:S(2)}, u32[]{:S(2)}) collective-permute-start(bf16[1024,128]{1,0:T(8,128)(2,1)S(1)} %collective-permute-done.19.refs_4_), channel_id=1, source_target_pairs={{0,4},{4,0},{8,12},{12,8},{1,5},{5,1},{9,13},{13,9},{2,6},{6,2},{1... | collective-permute-start | bytes 786440 | tf_op jit(solution)/shard_map/s1_across_from_core/ppermute | solution.py:219
  47.2 9.4 %collective-permute-start.24 = (bf16[2,320,128]{2,1,0:T(8,128)(2,1)S(1)}, bf16[2,320,128]{2,1,0:T(8,128)(2,1)S(1)}, u32[]{:S(2)}, u32[]{:S(2)}) collective-permute-start(bf16[2,320,128]{2,1,0:T(8,128)(2,1)S(1)} %get-tuple-element.61), channel_id=1, source_target_pairs={{0,1},{1,0},{2,3},{3,2},{4,5},{5,4},{6,7},{7,6},{8,9},{9,8},{10,11... | collective-permute-start | bytes 491528 | tf_op jit(solution)/shard_map/sum2_from_layer_1/ppermute | solution.py:219
  49.0 10.5 %collective-permute-start.18 = (bf16[2,320,128]{2,1,0:T(8,128)(2,1)S(1)}, bf16[2,320,128]{2,1,0:T(8,128)(2,1)S(1)}, u32[]{:S(2)}, u32[]{:S(2)}) collective-permute-start(bf16[2,320,128]{2,1,0:T(8,128)(2,1)S(1)} %get-tuple-element.53), channel_id=1, source_target_pairs={{0,1},{1,0},{2,3},{3,2},{4,5},{5,4},{6,7},{7,6},{8,9},{9,8},{10,11... | collective-permute-start | bytes 491528 | tf_op jit(solution)/shard_map/sum1_from_layer_1/ppermute | solution.py:219
  52.2 12.4 %collective-permute-start.26 = (bf16[2,320,128]{2,1,0:T(8,128)(2,1)S(1)}, bf16[2,320,128]{2,1,0:T(8,128)(2,1)S(1)}, u32[]{:S(2)}, u32[]{:S(2)}) collective-permute-start(bf16[2,320,128]{2,1,0:T(8,128)(2,1)S(1)} %get-tuple-element.64), channel_id=1, source_target_pairs={{0,1},{1,0},{2,3},{3,2},{4,5},{5,4},{6,7},{7,6},{8,9},{9,8},{10,11... | collective-permute-start | bytes 491528 | tf_op jit(solution)/shard_map/sum3_from_layer_1/ppermute | solution.py:219
  54.1 12.4 %collective-permute-start.17 = (bf16[1,320,128]{2,1,0:T(8,128)(2,1)S(1)}, bf16[1,320,128]{2,1,0:T(8,128)(2,1)S(1)}, u32[]{:S(2)}, u32[]{:S(2)}) collective-permute-start(bf16[1,320,128]{2,1,0:T(8,128)(2,1)S(1)} %get-tuple-element.51), channel_id=1, source_target_pairs={{0,2},{1,3},{2,0},{3,1},{4,6},{5,7},{6,4},{7,5},{8,10},{9,11},{10,... | collective-permute-start | bytes 245768 | tf_op jit(solution)/shard_map/sum0_from_layer_2/ppermute | solution.py:219
  56.7 9.8 %collective-permute-start.25 = (bf16[1,320,128]{2,1,0:T(8,128)(2,1)S(1)}, bf16[1,320,128]{2,1,0:T(8,128)(2,1)S(1)}, u32[]{:S(2)}, u32[]{:S(2)}) collective-permute-start(bf16[1,320,128]{2,1,0:T(8,128)(2,1)S(1)} %get-tuple-element.63), channel_id=1, source_target_pairs={{0,2},{1,3},{2,0},{3,1},{4,6},{5,7},{6,4},{7,5},{8,10},{9,11},{10,... | collective-permute-start | bytes 245768 | tf_op jit(solution)/shard_map/sum2_from_layer_2/ppermute | solution.py:219
  59.5 12.5 %collective-permute-start.23 = (bf16[1,320,128]{2,1,0:T(8,128)(2,1)S(1)}, bf16[1,320,128]{2,1,0:T(8,128)(2,1)S(1)}, u32[]{:S(2)}, u32[]{:S(2)}) collective-permute-start(bf16[1,320,128]{2,1,0:T(8,128)(2,1)S(1)} %get-tuple-element.60), channel_id=1, source_target_pairs={{0,2},{1,3},{2,0},{3,1},{4,6},{5,7},{6,4},{7,5},{8,10},{9,11},{10,... | collective-permute-start | bytes 245768 | tf_op jit(solution)/shard_map/sum1_from_layer_2/ppermute | solution.py:219
  64.6 8.9 %collective-permute-start.27 = (bf16[1,320,128]{2,1,0:T(8,128)(2,1)S(1)}, bf16[1,320,128]{2,1,0:T(8,128)(2,1)S(1)}, u32[]{:S(2)}, u32[]{:S(2)}) collective-permute-start(bf16[1,320,128]{2,1,0:T(8,128)(2,1)S(1)} %get-tuple-element.66), channel_id=1, source_target_pairs={{0,2},{1,3},{2,0},{3,1},{4,6},{5,7},{6,4},{7,5},{8,10},{9,11},{10,... | collective-permute-start | bytes 245768 | tf_op jit(solution)/shard_map/sum3_from_layer_2/ppermute | solution.py:219

commit v15 on v12

--- a/solution.py
+++ b/solution.py
@@ -79,7 +79,8 @@
     ).astype(BF16)
     for out in outs[1:]:
         out[:height, :] = outs[0][...]
-        out[height:, :] = jnp.zeros((out.shape[0] - height, out.shape[1]), BF16)
+        if out.shape[0] > height:
+            out[height:, :] = jnp.zeros((out.shape[0] - height, out.shape[1]), BF16)
 
 
 def condition(sizes, place, hess, pieces, after, more):
@@ -257,11 +258,11 @@
     q0_there = after(q1, q0_there)
     q0_cores = [q0_core] + flip(q0_there, "q0_there")
     q1_there, q1_core = gather_chip(q1, "q1"), from_core(q1, "q1")
-    s0, s0_long, s0_longer = condition(sizes, place, hess, with_cores([q0] + q0_there, q0_cores), q1, (16, 16))
+    s0, s0_long, s0_longer = condition(sizes, place, hess, with_cores([q0] + q0_there, q0_cores), q1, (16, 0))
     s0_there, s0_across, s0_core = gather_chip(s0_long, "s0"), gather_group(s0_longer, "s0"), from_core(s0, "s0")
     q1_there = after(s0, q1_there)
     q1_cores = [q1_core] + flip(q1_there, "q1_there")
-    s1, s1_long = condition(sizes, place, hess, with_cores([q1] + q1_there, q1_cores), s0, (16,))
+    s1, s1_long = condition(sizes, place, hess, with_cores([q1] + q1_there, q1_cores), s0, (0,))
     s1_there, s1_core = gather_chip(s1, "s1"), from_core(s1, "s1")
     s0_there, s0_across = after(s1, s0_there), after(s1, s0_across)
     s0_diagonal = [gather_group(x, "s0_there") for x in s0_there]

time: 72.7 us -> 72.6 us (level)
  no operation moved by 1% of the time
where the time goes in v15:
time: 72.6 us; the launch traced here: 72.4 us
  starting transfers between devices  28.7 us (40%)
  waiting for transfers between devices  23.1 us (32%)
  Pallas kernels  20.5 us (28%)
    ppermute x28, starting transfers between devices, permute(): return lax.ppermute(x, axis, perm)  28.7 us
    ppermute x28, waiting for transfers between devices, permute(): return lax.ppermute(x, axis, perm)  23.1 us
    pallas_call x3, Pallas kernels, score(): pl.pallas_call(functools.partial(score_kernel, sizes, columns, direct), o...  9.14 us
    pallas_call x2, Pallas kernels, condition(): pl.pallas_call(functools.partial(condition_kernel, sizes), out_shape=[plt...  4.98 us
    pallas_call x1, Pallas kernels, load(): pl.pallas_call(load_kernel, out_shape=pltpu.VMEM(source.shape, BF16), in_...  3.39 us
    pallas_call x2, Pallas kernels, take(): pl.pallas_call(functools.partial(take_kernel, chunk), out_shape=pltpu.VME...  1.92 us
  transfers between devices with their start and end apart: 28, of which 12 were waited for; matrix products, arithmetic and copies ran while one was open for 0% of the time, Pallas kernels for 26%

profile of v15, /device:TPU:0, one launch (start us, length us, event | category | flops | bytes accessed | tf_op | source)
XLA Modules:
  0.0 72.4 jit_solution(17941929417932119673)
XLA Ops:
  0.0 1.0 %take.2.after.refs_4_ = bf16[128,1024]{1,0:T(8,128)(2,1)S(1)} custom-call(s32[1]{0:T(128)} %bitcast.at_group.after.refs_0_, s32[1]{0:T(128)} %bitcast.1.at_ex.refs_1_, s32[1]{0:T(128)} %bitcast.2.at_layer.refs_2_, bf16[512,1024]{1,0:T(8,128)(2,1)} %bitcast.12, s32[1]{0:T(128)} %bitcast.at_group.after.refs_0_), custom_call_target="tpu_custom_call" | custom-call | tf_op jit(solution)/shard_map/take/pallas_call | solution.py:58
  1.0 3.0 %collective-permute-start.1 = (bf16[128,1024]{1,0:T(8,128)(2,1)S(1)}, bf16[128,1024]{1,0:T(8,128)(2,1)S(1)}, u32[]{:S(2)}, u32[]{:S(2)}) collective-permute-start(bf16[128,1024]{1,0:T(8,128)(2,1)S(1)} %take.2.after.refs_4_), channel_id=1, source_target_pairs={{0,8},{4,12},{8,0},{12,4},{1,9},{5,13},{9,1},{13,5},{2,10},{6,14},... | collective-permute-start | bytes 786440 | tf_op jit(solution)/shard_map/q0_from_chip/ppermute | solution.py:200
  4.0 0.0 collective-permute-start
  4.0 3.4 %load.1.after.refs_3_ = bf16[1024,4096]{1,0:T(8,128)(2,1)S(1)} custom-call(bf16[1024,4096]{1,0:T(8,128)(2,1)} %bitcast.11, bf16[128,1024]{1,0:T(8,128)(2,1)S(1)} %take.2.after.refs_4_), custom_call_target="tpu_custom_call" | custom-call | tf_op jit(solution)/shard_map/load/pallas_call | solution.py:38
  7.4 1.0 %take.3.refs_8_.refs_4_ = bf16[128,1024]{1,0:T(8,128)(2,1)S(1)} custom-call(s32[1]{0:T(128)} %bitcast.at_group.after.refs_0_, s32[1]{0:T(128)} %bitcast.1.at_ex.refs_1_, s32[1]{0:T(128)} %bitcast.2.at_layer.refs_2_, bf16[512,1024]{1,0:T(8,128)(2,1)} %bitcast.13, bf16[1024,4096]{1,0:T(8,128)(2,1)S(1)} %load.1.after.refs_3_), custom_call_target="tpu_custom_call" | custom-call | tf_op jit(solution)/shard_map/take/pallas_call | solution.py:58
  8.4 0.0 slice-start
  8.4 0.0 slice-start.1
  8.4 1.9 %collective-permute-done.1.refs_6_ = bf16[128,1024]{1,0:T(8,128)(2,1)S(1)} collective-permute-done((bf16[128,1024]{1,0:T(8,128)(2,1)S(1)}, bf16[128,1024]{1,0:T(8,128)(2,1)S(1)}, u32[]{:S(2)}, u32[]{:S(2)}) %collective-permute-start.1) | collective-permute-done | bytes 262176 | tf_op jit(solution)/shard_map/q0_from_chip/ppermute | solution.py:200
  10.3 0.0 collective-permute-start.2
  10.3 1.7 %collective-permute-start.6 = (bf16[128,1024]{1,0:T(8,128)(2,1)S(1)}, bf16[128,1024]{1,0:T(8,128)(2,1)S(1)}, u32[]{:S(2)}, u32[]{:S(2)}) collective-permute-start(bf16[128,1024]{1,0:T(8,128)(2,1)S(1)} %take.3.refs_8_.refs_4_), channel_id=1, source_target_pairs={{0,8},{4,12},{8,0},{12,4},{1,9},{5,13},{9,1},{13,5},{2,10},{6,14},... | collective-permute-start | bytes 786440 | tf_op jit(solution)/shard_map/q1_from_chip/ppermute | solution.py:200
  12.0 0.0 collective-permute-done.refs_5_
  12.1 2.5 %condition.2 = (bf16[1024,128]{1,0:T(8,128)(2,1)S(1)}, bf16[1040,128]{1,0:T(8,128)(2,1)S(1)}, bf16[1024,128]{1,0:T(8,128)(2,1)S(1)}) custom-call(s32[1]{0:T(128)} %bitcast.at_group.after.refs_0_, s32[1]{0:T(128)} %bitcast.1.at_ex.refs_1_, s32[1]{0:T(128)} %bitcast.2.at_layer.refs_2_, bf16[1024,4096]{1,0:T(8,128)(2,1)S(1)} %load.1.after.refs_3_, ...), custom_call_target="tpu_custom_call" | custom-call | tf_op jit(solution)/shard_map/condition/pallas_call | solution.py:89
  14.5 1.6 %collective-permute-start.4 = (bf16[1040,128]{1,0:T(8,128)(2,1)S(1)}, bf16[1040,128]{1,0:T(8,128)(2,1)S(1)}, u32[]{:S(2)}, u32[]{:S(2)}) collective-permute-start(bf16[1040,128]{1,0:T(8,128)(2,1)S(1)} %get-tuple-element.37), channel_id=1, source_target_pairs={{0,8},{4,12},{8,0},{12,4},{1,9},{5,13},{9,1},{13,5},{2,10},{6,14},... | collective-permute-start | bytes 798728 | tf_op jit(solution)/shard_map/s0_from_chip/ppermute | solution.py:200
  16.1 3.3 %collective-permute-done.6.refs_6_ = bf16[128,1024]{1,0:T(8,128)(2,1)S(1)} collective-permute-done((bf16[128,1024]{1,0:T(8,128)(2,1)S(1)}, bf16[128,1024]{1,0:T(8,128)(2,1)S(1)}, u32[]{:S(2)}, u32[]{:S(2)}) %collective-permute-start.6) | collective-permute-done | bytes 262176 | tf_op jit(solution)/shard_map/q1_from_chip/ppermute | solution.py:200
  19.4 0.0 collective-permute-start.7
  19.4 1.7 %collective-permute-start.10 = (bf16[1024,128]{1,0:T(8,128)(2,1)S(1)}, bf16[1024,128]{1,0:T(8,128)(2,1)S(1)}, u32[]{:S(2)}, u32[]{:S(2)}) collective-permute-start(bf16[1024,128]{1,0:T(8,128)(2,1)S(1)} %get-tuple-element.43), channel_id=1, source_target_pairs={{0,16},{16,0},{1,17},{17,1},{2,18},{18,2},{3,19},{19,3},{4,20},{20... | collective-permute-start | bytes 786440 | tf_op jit(solution)/shard_map/s0_from_group/ppermute | solution.py:200
  21.1 0.2 collective-permute-start.3
  21.4 0.0 collective-permute-done.5.refs_5_
  21.4 2.5 %condition.3 = (bf16[1024,128]{1,0:T(8,128)(2,1)S(1)}, bf16[1024,128]{1,0:T(8,128)(2,1)S(1)}) custom-call(s32[1]{0:T(128)} %bitcast.at_group.after.refs_0_, s32[1]{0:T(128)} %bitcast.1.at_ex.refs_1_, s32[1]{0:T(128)} %bitcast.2.at_layer.refs_2_, bf16[1024,4096]{1,0:T(8,128)(2,1)S(1)} %load.1.after.refs_3_, bf16[128,1024]{1,0:T(8,128)(2,1)S(1)} %take.3.refs_8_.refs_4_, ...), custom_call_target="tpu_custom_call" | custom-call | tf_op jit(solution)/shard_map/condition/pallas_call | solution.py:89
  23.9 0.9 %collective-permute-done.4.refs_6_ = bf16[1040,128]{1,0:T(8,128)(2,1)S(1)} collective-permute-done((bf16[1040,128]{1,0:T(8,128)(2,1)S(1)}, bf16[1040,128]{1,0:T(8,128)(2,1)S(1)}, u32[]{:S(2)}, u32[]{:S(2)}) %collective-permute-start.4) | collective-permute-done | bytes 266272 | tf_op jit(solution)/shard_map/s0_from_chip/ppermute | solution.py:200
  24.7 1.7 %collective-permute-start.12 = (bf16[1040,128]{1,0:T(8,128)(2,1)S(1)}, bf16[1040,128]{1,0:T(8,128)(2,1)S(1)}, u32[]{:S(2)}, u32[]{:S(2)}) collective-permute-start(bf16[1040,128]{1,0:T(8,128)(2,1)S(1)} %collective-permute-done.4.refs_6_), channel_id=1, source_target_pairs={{0,16},{16,0},{1,17},{17,1},{2,18},{18,2},{3,19},{19,3},{4,20},{20... | collective-permute-start | bytes 798728 | tf_op jit(solution)/shard_map/s0_there_from_group/ppermute | solution.py:200
  26.4 1.5 %collective-permute-start.15 = (bf16[1024,128]{1,0:T(8,128)(2,1)S(1)}, bf16[1024,128]{1,0:T(8,128)(2,1)S(1)}, u32[]{:S(2)}, u32[]{:S(2)}) collective-permute-start(bf16[1024,128]{1,0:T(8,128)(2,1)S(1)} %get-tuple-element.39.refs_8_), channel_id=1, source_target_pairs={{0,8},{4,12},{8,0},{12,4},{1,9},{5,13},{9,1},{13,5},{2,10},{6,14},... | collective-permute-start | bytes 786440 | tf_op jit(solution)/shard_map/s1_from_chip/ppermute | solution.py:200
  28.0 0.4 collective-permute-done.10.refs_4_
  28.4 1.7 %collective-permute-start.19 = (bf16[1024,128]{1,0:T(8,128)(2,1)S(1)}, bf16[1024,128]{1,0:T(8,128)(2,1)S(1)}, u32[]{:S(2)}, u32[]{:S(2)}) collective-permute-start(bf16[1024,128]{1,0:T(8,128)(2,1)S(1)} %get-tuple-element.52), channel_id=1, source_target_pairs={{0,16},{16,0},{1,17},{17,1},{2,18},{18,2},{3,19},{19,3},{4,20},{20... | collective-permute-start | bytes 786440 | tf_op jit(solution)/shard_map/s1_from_group/ppermute | solution.py:200
  30.1 2.9 %score0.1 = (bf16[2,320,128]{2,1,0:T(8,128)(2,1)S(1)}, f32[2,320,128]{2,1,0:T(8,128)S(1)}) custom-call(s32[1]{0:T(128)} %bitcast.at_group.after.refs_0_, s32[1]{0:T(128)} %bitcast.1.at_ex.refs_1_, s32[1]{0:T(128)} %bitcast.2.at_layer.refs_2_, bf16[1280,4096]{1,0:T(8,128)(2,1)S(1)} %bitcast.8, bf16[1024,128]{1,0:T(8,128)(2,1)S(1)} %get-tuple-element.36.refs_8_.refs_4_, ...), custom_call_target="tpu_custom_call" | custom-call | tf_op jit(solution)/shard_map/score0/pallas_call | solution.py:129
  33.1 1.0 %collective-permute-done.12.refs_6_ = bf16[1040,128]{1,0:T(8,128)(2,1)S(1)} collective-permute-done((bf16[1040,128]{1,0:T(8,128)(2,1)S(1)}, bf16[1040,128]{1,0:T(8,128)(2,1)S(1)}, u32[]{:S(2)}, u32[]{:S(2)}) %collective-permute-start.12) | collective-permute-done | bytes 266272 | tf_op jit(solution)/shard_map/s0_there_from_group/ppermute | solution.py:200
  34.1 0.5 collective-permute-start.14
  34.6 0.3 collective-permute-done.15.refs_10_
  34.9 1.5 %collective-permute-start.21 = (bf16[1024,128]{1,0:T(8,128)(2,1)S(1)}, bf16[1024,128]{1,0:T(8,128)(2,1)S(1)}, u32[]{:S(2)}, u32[]{:S(2)}) collective-permute-start(bf16[1024,128]{1,0:T(8,128)(2,1)S(1)} %collective-permute-done.15.refs_10_), channel_id=1, source_target_pairs={{0,16},{16,0},{1,17},{17,1},{2,18},{18,2},{3,19},{19,3},{4,20},{20... | collective-permute-start | bytes 786440 | tf_op jit(solution)/shard_map/s1_there_from_group/ppermute | solution.py:200
  36.4 3.3 %collective-permute-done.19.refs_4_ = bf16[1024,128]{1,0:T(8,128)(2,1)S(1)} collective-permute-done((bf16[1024,128]{1,0:T(8,128)(2,1)S(1)}, bf16[1024,128]{1,0:T(8,128)(2,1)S(1)}, u32[]{:S(2)}, u32[]{:S(2)}) %collective-permute-start.19) | collective-permute-done | bytes 262176 | tf_op jit(solution)/shard_map/s1_from_group/ppermute | solution.py:200
  39.7 1.8 %collective-permute-start.9 = (bf16[2,320,128]{2,1,0:T(8,128)(2,1)S(1)}, bf16[2,320,128]{2,1,0:T(8,128)(2,1)S(1)}, u32[]{:S(2)}, u32[]{:S(2)}) collective-permute-start(bf16[2,320,128]{2,1,0:T(8,128)(2,1)S(1)} %get-tuple-element.42), channel_id=1, source_target_pairs={{0,1},{1,0},{2,3},{3,2},{4,5},{5,4},{6,7},{7,6},{8,9},{9,8},{10,11... | collective-permute-start | bytes 491528 | tf_op jit(solution)/shard_map/sum0_from_layer_1/ppermute | solution.py:200
  41.5 3.3 %score1.1 = (bf16[2,320,128]{2,1,0:T(8,128)(2,1)S(1)}, f32[2,320,128]{2,1,0:T(8,128)S(1)}, bf16[2,320,128]{2,1,0:T(8,128)(2,1)S(1)}, f32[2,320,128]{2,1,0:T(8,128)S(1)}) custom-call(s32[1]{0:T(128)} %bitcast.at_group.after.refs_0_, s32[1]{0:T(128)} %bitcast.1.at_ex.refs_1_, s32[1]{0:T(128)} %bitcast.2.at_layer.refs_2_, bf16[1280,4096]{1,0:T(8,128)(2,1)S(1)} %bitcast.9, ...), custom_call_target="tpu_custom_call" | custom-call | tf_op jit(solution)/shard_map/score1/pallas_call | solution.py:129
  44.8 0.7 %collective-permute-done.9.got = bf16[2,320,128]{2,1,0:T(8,128)(2,1)S(1)} collective-permute-done((bf16[2,320,128]{2,1,0:T(8,128)(2,1)S(1)}, bf16[2,320,128]{2,1,0:T(8,128)(2,1)S(1)}, u32[]{:S(2)}, u32[]{:S(2)}) %collective-permute-start.9) | collective-permute-done | bytes 163872 | tf_op jit(solution)/shard_map/sum0_from_layer_1/ppermute | solution.py:200
  45.5 0.1 collective-permute-start.22
  45.6 0.5 collective-permute-start.20
  46.1 1.7 %collective-permute-start.24 = (bf16[2,320,128]{2,1,0:T(8,128)(2,1)S(1)}, bf16[2,320,128]{2,1,0:T(8,128)(2,1)S(1)}, u32[]{:S(2)}, u32[]{:S(2)}) collective-permute-start(bf16[2,320,128]{2,1,0:T(8,128)(2,1)S(1)} %get-tuple-element.59), channel_id=1, source_target_pairs={{0,1},{1,0},{2,3},{3,2},{4,5},{5,4},{6,7},{7,6},{8,9},{9,8},{10,11... | collective-permute-start | bytes 491528 | tf_op jit(solution)/shard_map/sum2_from_layer_1/ppermute | solution.py:200
  47.9 0.3 collective-permute-start.18
  48.2 2.9 %score2.1 = (bf16[2,320,128]{2,1,0:T(8,128)(2,1)S(1)}, f32[2,320,128]{2,1,0:T(8,128)S(1)}) custom-call(s32[1]{0:T(128)} %bitcast.at_group.after.refs_0_, s32[1]{0:T(128)} %bitcast.1.at_ex.refs_1_, s32[1]{0:T(128)} %bitcast.2.at_layer.refs_2_, bf16[1280,4096]{1,0:T(8,128)(2,1)S(1)} %bitcast.10, bf16[1024,128]{1,0:T(8,128)(2,1)S(1)} %collective-permute-done.19.refs_4_, ...), custom_call_target="tpu_custom_call" | custom-call | tf_op jit(solution)/shard_map/score2/pallas_call | solution.py:129
  51.1 1.8 %collective-permute-start.26 = (bf16[2,320,128]{2,1,0:T(8,128)(2,1)S(1)}, bf16[2,320,128]{2,1,0:T(8,128)(2,1)S(1)}, u32[]{:S(2)}, u32[]{:S(2)}) collective-permute-start(bf16[2,320,128]{2,1,0:T(8,128)(2,1)S(1)} %get-tuple-element.62), channel_id=1, source_target_pairs={{0,1},{1,0},{2,3},{3,2},{4,5},{5,4},{6,7},{7,6},{8,9},{9,8},{10,11... | collective-permute-start | bytes 491528 | tf_op jit(solution)/shard_map/sum3_from_layer_1/ppermute | solution.py:200
  52.9 2.6 %collective-permute-start.17 = (bf16[1,320,128]{2,1,0:T(8,128)(2,1)S(1)}, bf16[1,320,128]{2,1,0:T(8,128)(2,1)S(1)}, u32[]{:S(2)}, u32[]{:S(2)}) collective-permute-start(bf16[1,320,128]{2,1,0:T(8,128)(2,1)S(1)} %get-tuple-element.49), channel_id=1, source_target_pairs={{0,2},{1,3},{2,0},{3,1},{4,6},{5,7},{6,4},{7,5},{8,10},{9,11},{10,... | collective-permute-start | bytes 245768 | tf_op jit(solution)/shard_map/sum0_from_layer_2/ppermute | solution.py:200
  55.5 0.5 collective-permute-start.25
  56.0 3.3 %collective-permute-done.18.got = bf16[2,320,128]{2,1,0:T(8,128)(2,1)S(1)} collective-permute-done((bf16[2,320,128]{2,1,0:T(8,128)(2,1)S(1)}, bf16[2,320,128]{2,1,0:T(8,128)(2,1)S(1)}, u32[]{:S(2)}, u32[]{:S(2)}) %collective-permute-start.18) | collective-permute-done | bytes 163872 | tf_op jit(solution)/shard_map/sum1_from_layer_1/ppermute | solution.py:200
  59.4 2.8 %collective-permute-start.23 = (bf16[1,320,128]{2,1,0:T(8,128)(2,1)S(1)}, bf16[1,320,128]{2,1,0:T(8,128)(2,1)S(1)}, u32[]{:S(2)}, u32[]{:S(2)}) collective-permute-start(bf16[1,320,128]{2,1,0:T(8,128)(2,1)S(1)} %get-tuple-element.58), channel_id=1, source_target_pairs={{0,2},{1,3},{2,0},{3,1},{4,6},{5,7},{6,4},{7,5},{8,10},{9,11},{10,... | collective-permute-start | bytes 245768 | tf_op jit(solution)/shard_map/sum1_from_layer_2/ppermute | solution.py:200
  62.1 1.4 %collective-permute-done.26.got = bf16[2,320,128]{2,1,0:T(8,128)(2,1)S(1)} collective-permute-done((bf16[2,320,128]{2,1,0:T(8,128)(2,1)S(1)}, bf16[2,320,128]{2,1,0:T(8,128)(2,1)S(1)}, u32[]{:S(2)}, u32[]{:S(2)}) %collective-permute-start.26) | collective-permute-done | bytes 163872 | tf_op jit(solution)/shard_map/sum3_from_layer_1/ppermute | solution.py:200
  63.5 1.4 %collective-permute-start.27 = (bf16[1,320,128]{2,1,0:T(8,128)(2,1)S(1)}, bf16[1,320,128]{2,1,0:T(8,128)(2,1)S(1)}, u32[]{:S(2)}, u32[]{:S(2)}) collective-permute-start(bf16[1,320,128]{2,1,0:T(8,128)(2,1)S(1)} %get-tuple-element.64), channel_id=1, source_target_pairs={{0,2},{1,3},{2,0},{3,1},{4,6},{5,7},{6,4},{7,5},{8,10},{9,11},{10,... | collective-permute-start | bytes 245768 | tf_op jit(solution)/shard_map/sum3_from_layer_2/ppermute | solution.py:200
  64.9 5.6 %collective-permute-done.23.refs_6_ = bf16[1,320,128]{2,1,0:T(8,128)(2,1)S(1)} collective-permute-done((bf16[1,320,128]{2,1,0:T(8,128)(2,1)S(1)}, bf16[1,320,128]{2,1,0:T(8,128)(2,1)S(1)}, u32[]{:S(2)}, u32[]{:S(2)}) %collective-permute-start.23) | collective-permute-done | bytes 81952 | tf_op jit(solution)/shard_map/sum1_from_layer_2/ppermute | solution.py:200
  70.5 1.0 %collective-permute-done.27.refs_10_ = bf16[1,320,128]{2,1,0:T(8,128)(2,1)S(1)} collective-permute-done((bf16[1,320,128]{2,1,0:T(8,128)(2,1)S(1)}, bf16[1,320,128]{2,1,0:T(8,128)(2,1)S(1)}, u32[]{:S(2)}, u32[]{:S(2)}) %collective-permute-start.27) | collective-permute-done | bytes 81952 | tf_op jit(solution)/shard_map/sum3_from_layer_2/ppermute | solution.py:200
  71.5 0.9 %finish.1 = f32[320,512]{1,0:T(8,128)} custom-call(s32[1]{0:T(128)} %bitcast.at_group.after.refs_0_, s32[1]{0:T(128)} %bitcast.1.at_ex.refs_1_, s32[1]{0:T(128)} %bitcast.2.at_layer.refs_2_, f32[1,320,128]{2,1,0:T(8,128)S(1)} %get-tuple-element.48.refs_8_.refs_3_, bf16[1,320,128]{2,1,0:T(8,128)(2,1)S(1)} %collective-permute-done.17.refs_4_, ...), custom_call_target="tpu_custom_call" | custom-call | tf_op jit(solution)/shard_map/finish/pallas_call | solution.py:182
  (28 shorter events, 0.2 us)
Async XLA Ops:
  1.0 9.3 %collective-permute-start.1 = (bf16[128,1024]{1,0:T(8,128)(2,1)S(1)}, bf16[128,1024]{1,0:T(8,128)(2,1)S(1)}, u32[]{:S(2)}, u32[]{:S(2)}) collective-permute-start(bf16[128,1024]{1,0:T(8,128)(2,1)S(1)} %take.2.after.refs_4_), channel_id=1, source_target_pairs={{0,8},{4,12},{8,0},{12,4},{1,9},{5,13},{9,1},{13,5},{2,10},{6,14},... | collective-permute-start | bytes 786440 | tf_op jit(solution)/shard_map/q0_from_chip/ppermute | solution.py:200
  4.0 8.1 %collective-permute-start = (bf16[128,1024]{1,0:T(8,128)(2,1)S(1)}, bf16[128,1024]{1,0:T(8,128)(2,1)S(1)}, u32[]{:S(2)}, u32[]{:S(2)}) collective-permute-start(bf16[128,1024]{1,0:T(8,128)(2,1)S(1)} %take.2.after.refs_4_), channel_id=1, source_target_pairs={{0,4},{4,0},{8,12},{12,8},{1,5},{5,1},{9,13},{13,9},{2,6},{6,2},{1... | collective-permute-start | bytes 786440 | tf_op jit(solution)/shard_map/q0_from_core/ppermute | solution.py:200
  8.4 21.7 %slice-start = ((s8[10485760]{0:T(1024)(128)(4,1)}), s8[4194304]{0:T(1024)(128)(4,1)S(1)}, s32[]{:S(2)}) async-start(s8[10485760]{0:T(1024)(128)(4,1)} %bitcast.6), calls=%async_computation | async-start | bytes 8388608
  8.4 21.7 %slice-start.1 = ((s8[10485760]{0:T(1024)(128)(4,1)}), s8[4194304]{0:T(1024)(128)(4,1)S(1)}, s32[]{:S(2)}) async-start(s8[10485760]{0:T(1024)(128)(4,1)} %bitcast.6), calls=%async_computation.1 | async-start | bytes 8388608
  10.3 1.8 %collective-permute-start.2 = (bf16[128,1024]{1,0:T(8,128)(2,1)S(1)}, bf16[128,1024]{1,0:T(8,128)(2,1)S(1)}, u32[]{:S(2)}, u32[]{:S(2)}) collective-permute-start(bf16[128,1024]{1,0:T(8,128)(2,1)S(1)} %collective-permute-done.1.refs_6_), channel_id=1, source_target_pairs={{0,4},{4,0},{8,12},{12,8},{1,5},{5,1},{9,13},{13,9},{2,6},{6,2},{1... | collective-permute-start | bytes 786440 | tf_op jit(solution)/shard_map/q0_there_from_core/ppermute | solution.py:200
  10.3 9.1 %collective-permute-start.6 = (bf16[128,1024]{1,0:T(8,128)(2,1)S(1)}, bf16[128,1024]{1,0:T(8,128)(2,1)S(1)}, u32[]{:S(2)}, u32[]{:S(2)}) collective-permute-start(bf16[128,1024]{1,0:T(8,128)(2,1)S(1)} %take.3.refs_8_.refs_4_), channel_id=1, source_target_pairs={{0,8},{4,12},{8,0},{12,4},{1,9},{5,13},{9,1},{13,5},{2,10},{6,14},... | collective-permute-start | bytes 786440 | tf_op jit(solution)/shard_map/q1_from_chip/ppermute | solution.py:200
  14.5 10.2 %collective-permute-start.4 = (bf16[1040,128]{1,0:T(8,128)(2,1)S(1)}, bf16[1040,128]{1,0:T(8,128)(2,1)S(1)}, u32[]{:S(2)}, u32[]{:S(2)}) collective-permute-start(bf16[1040,128]{1,0:T(8,128)(2,1)S(1)} %get-tuple-element.37), channel_id=1, source_target_pairs={{0,8},{4,12},{8,0},{12,4},{1,9},{5,13},{9,1},{13,5},{2,10},{6,14},... | collective-permute-start | bytes 798728 | tf_op jit(solution)/shard_map/s0_from_chip/ppermute | solution.py:200
  16.1 5.2 %collective-permute-start.5 = (bf16[128,1024]{1,0:T(8,128)(2,1)S(1)}, bf16[128,1024]{1,0:T(8,128)(2,1)S(1)}, u32[]{:S(2)}, u32[]{:S(2)}) collective-permute-start(bf16[128,1024]{1,0:T(8,128)(2,1)S(1)} %take.3.refs_8_.refs_4_), channel_id=1, source_target_pairs={{0,4},{4,0},{8,12},{12,8},{1,5},{5,1},{9,13},{13,9},{2,6},{6,2},{1... | collective-permute-start | bytes 786440 | tf_op jit(solution)/shard_map/q1_from_core/ppermute | solution.py:200
  19.4 2.0 %collective-permute-start.7 = (bf16[128,1024]{1,0:T(8,128)(2,1)S(1)}, bf16[128,1024]{1,0:T(8,128)(2,1)S(1)}, u32[]{:S(2)}, u32[]{:S(2)}) collective-permute-start(bf16[128,1024]{1,0:T(8,128)(2,1)S(1)} %collective-permute-done.6.refs_6_), channel_id=1, source_target_pairs={{0,4},{4,0},{8,12},{12,8},{1,5},{5,1},{9,13},{13,9},{2,6},{6,2},{1... | collective-permute-start | bytes 786440 | tf_op jit(solution)/shard_map/q1_there_from_core/ppermute | solution.py:200
  19.4 10.7 %slice-start.2 = ((s8[10485760]{0:T(1024)(128)(4,1)}), s8[2097152]{0:T(1024)(128)(4,1)S(1)}, s32[]{:S(2)}) async-start(s8[10485760]{0:T(1024)(128)(4,1)} %bitcast.6), calls=%async_computation.2 | async-start | bytes 4194304
  19.4 8.9 %collective-permute-start.10 = (bf16[1024,128]{1,0:T(8,128)(2,1)S(1)}, bf16[1024,128]{1,0:T(8,128)(2,1)S(1)}, u32[]{:S(2)}, u32[]{:S(2)}) collective-permute-start(bf16[1024,128]{1,0:T(8,128)(2,1)S(1)} %get-tuple-element.43), channel_id=1, source_target_pairs={{0,16},{16,0},{1,17},{17,1},{2,18},{18,2},{3,19},{19,3},{4,20},{20... | collective-permute-start | bytes 786440 | tf_op jit(solution)/shard_map/s0_from_group/ppermute | solution.py:200
  21.1 7.2 %collective-permute-start.3 = (bf16[1024,128]{1,0:T(8,128)(2,1)S(1)}, bf16[1024,128]{1,0:T(8,128)(2,1)S(1)}, u32[]{:S(2)}, u32[]{:S(2)}) collective-permute-start(bf16[1024,128]{1,0:T(8,128)(2,1)S(1)} %get-tuple-element.36.refs_8_.refs_4_), channel_id=1, source_target_pairs={{0,4},{4,0},{8,12},{12,8},{1,5},{5,1},{9,13},{13,9},{2,6},{6,2},{1... | collective-permute-start | bytes 786440 | tf_op jit(solution)/shard_map/s0_from_core/ppermute | solution.py:200
  24.7 5.4 %collective-permute-start.8 = (bf16[1040,128]{1,0:T(8,128)(2,1)S(1)}, bf16[1040,128]{1,0:T(8,128)(2,1)S(1)}, u32[]{:S(2)}, u32[]{:S(2)}) collective-permute-start(bf16[1040,128]{1,0:T(8,128)(2,1)S(1)} %collective-permute-done.4.refs_6_), channel_id=1, source_target_pairs={{0,4},{4,0},{8,12},{12,8},{1,5},{5,1},{9,13},{13,9},{2,6},{6,2},{1... | collective-permute-start | bytes 798728 | tf_op jit(solution)/shard_map/s0_there_from_core/ppermute | solution.py:200
  24.7 9.3 %collective-permute-start.12 = (bf16[1040,128]{1,0:T(8,128)(2,1)S(1)}, bf16[1040,128]{1,0:T(8,128)(2,1)S(1)}, u32[]{:S(2)}, u32[]{:S(2)}) collective-permute-start(bf16[1040,128]{1,0:T(8,128)(2,1)S(1)} %collective-permute-done.4.refs_6_), channel_id=1, source_target_pairs={{0,16},{16,0},{1,17},{17,1},{2,18},{18,2},{3,19},{19,3},{4,20},{20... | collective-permute-start | bytes 798728 | tf_op jit(solution)/shard_map/s0_there_from_group/ppermute | solution.py:200
  26.4 8.4 %collective-permute-start.15 = (bf16[1024,128]{1,0:T(8,128)(2,1)S(1)}, bf16[1024,128]{1,0:T(8,128)(2,1)S(1)}, u32[]{:S(2)}, u32[]{:S(2)}) collective-permute-start(bf16[1024,128]{1,0:T(8,128)(2,1)S(1)} %get-tuple-element.39.refs_8_), channel_id=1, source_target_pairs={{0,8},{4,12},{8,0},{12,4},{1,9},{5,13},{9,1},{13,5},{2,10},{6,14},... | collective-permute-start | bytes 786440 | tf_op jit(solution)/shard_map/s1_from_chip/ppermute | solution.py:200
  28.4 6.5 %collective-permute-start.11 = (bf16[1024,128]{1,0:T(8,128)(2,1)S(1)}, bf16[1024,128]{1,0:T(8,128)(2,1)S(1)}, u32[]{:S(2)}, u32[]{:S(2)}) collective-permute-start(bf16[1024,128]{1,0:T(8,128)(2,1)S(1)} %collective-permute-done.10.refs_4_), channel_id=1, source_target_pairs={{0,4},{4,0},{8,12},{12,8},{1,5},{5,1},{9,13},{13,9},{2,6},{6,2},{1... | collective-permute-start | bytes 786440 | tf_op jit(solution)/shard_map/s0_across_from_core/ppermute | solution.py:200
  28.4 11.3 %collective-permute-start.19 = (bf16[1024,128]{1,0:T(8,128)(2,1)S(1)}, bf16[1024,128]{1,0:T(8,128)(2,1)S(1)}, u32[]{:S(2)}, u32[]{:S(2)}) collective-permute-start(bf16[1024,128]{1,0:T(8,128)(2,1)S(1)} %get-tuple-element.52), channel_id=1, source_target_pairs={{0,16},{16,0},{1,17},{17,1},{2,18},{18,2},{3,19},{19,3},{4,20},{20... | collective-permute-start | bytes 786440 | tf_op jit(solution)/shard_map/s1_from_group/ppermute | solution.py:200
  34.1 7.4 %collective-permute-start.13 = (bf16[1040,128]{1,0:T(8,128)(2,1)S(1)}, bf16[1040,128]{1,0:T(8,128)(2,1)S(1)}, u32[]{:S(2)}, u32[]{:S(2)}) collective-permute-start(bf16[1040,128]{1,0:T(8,128)(2,1)S(1)} %collective-permute-done.12.refs_6_), channel_id=1, source_target_pairs={{0,4},{4,0},{8,12},{12,8},{1,5},{5,1},{9,13},{13,9},{2,6},{6,2},{1... | collective-permute-start | bytes 798728 | tf_op jit(solution)/shard_map/s0_diagonal_from_core/ppermute | solution.py:200
  34.1 7.4 %collective-permute-start.14 = (bf16[1024,128]{1,0:T(8,128)(2,1)S(1)}, bf16[1024,128]{1,0:T(8,128)(2,1)S(1)}, u32[]{:S(2)}, u32[]{:S(2)}) collective-permute-start(bf16[1024,128]{1,0:T(8,128)(2,1)S(1)} %get-tuple-element.39.refs_8_), channel_id=1, source_target_pairs={{0,4},{4,0},{8,12},{12,8},{1,5},{5,1},{9,13},{13,9},{2,6},{6,2},{1... | collective-permute-start | bytes 786440 | tf_op jit(solution)/shard_map/s1_from_core/ppermute | solution.py:200
  34.9 6.6 %collective-permute-start.16 = (bf16[1024,128]{1,0:T(8,128)(2,1)S(1)}, bf16[1024,128]{1,0:T(8,128)(2,1)S(1)}, u32[]{:S(2)}, u32[]{:S(2)}) collective-permute-start(bf16[1024,128]{1,0:T(8,128)(2,1)S(1)} %collective-permute-done.15.refs_10_), channel_id=1, source_target_pairs={{0,4},{4,0},{8,12},{12,8},{1,5},{5,1},{9,13},{13,9},{2,6},{6,2},{1... | collective-permute-start | bytes 786440 | tf_op jit(solution)/shard_map/s1_there_from_core/ppermute | solution.py:200
  34.9 10.6 %collective-permute-start.21 = (bf16[1024,128]{1,0:T(8,128)(2,1)S(1)}, bf16[1024,128]{1,0:T(8,128)(2,1)S(1)}, u32[]{:S(2)}, u32[]{:S(2)}) collective-permute-start(bf16[1024,128]{1,0:T(8,128)(2,1)S(1)} %collective-permute-done.15.refs_10_), channel_id=1, source_target_pairs={{0,16},{16,0},{1,17},{17,1},{2,18},{18,2},{3,19},{19,3},{4,20},{20... | collective-permute-start | bytes 786440 | tf_op jit(solution)/shard_map/s1_there_from_group/ppermute | solution.py:200
  39.7 5.8 %collective-permute-start.9 = (bf16[2,320,128]{2,1,0:T(8,128)(2,1)S(1)}, bf16[2,320,128]{2,1,0:T(8,128)(2,1)S(1)}, u32[]{:S(2)}, u32[]{:S(2)}) collective-permute-start(bf16[2,320,128]{2,1,0:T(8,128)(2,1)S(1)} %get-tuple-element.42), channel_id=1, source_target_pairs={{0,1},{1,0},{2,3},{3,2},{4,5},{5,4},{6,7},{7,6},{8,9},{9,8},{10,11... | collective-permute-start | bytes 491528 | tf_op jit(solution)/shard_map/sum0_from_layer_1/ppermute | solution.py:200
  45.5 2.6 %collective-permute-start.22 = (bf16[1024,128]{1,0:T(8,128)(2,1)S(1)}, bf16[1024,128]{1,0:T(8,128)(2,1)S(1)}, u32[]{:S(2)}, u32[]{:S(2)}) collective-permute-start(bf16[1024,128]{1,0:T(8,128)(2,1)S(1)} %collective-permute-done.21.refs_6_), channel_id=1, source_target_pairs={{0,4},{4,0},{8,12},{12,8},{1,5},{5,1},{9,13},{13,9},{2,6},{6,2},{1... | collective-permute-start | bytes 786440 | tf_op jit(solution)/shard_map/s1_diagonal_from_core/ppermute | solution.py:200
  45.6 2.5 %collective-permute-start.20 = (bf16[1024,128]{1,0:T(8,128)(2,1)S(1)}, bf16[1024,128]{1,0:T(8,128)(2,1)S(1)}, u32[]{:S(2)}, u32[]{:S(2)}) collective-permute-start(bf16[1024,128]{1,0:T(8,128)(2,1)S(1)} %collective-permute-done.19.refs_4_), channel_id=1, source_target_pairs={{0,4},{4,0},{8,12},{12,8},{1,5},{5,1},{9,13},{13,9},{2,6},{6,2},{1... | collective-permute-start | bytes 786440 | tf_op jit(solution)/shard_map/s1_across_from_core/ppermute | solution.py:200
  46.1 9.4 %collective-permute-start.24 = (bf16[2,320,128]{2,1,0:T(8,128)(2,1)S(1)}, bf16[2,320,128]{2,1,0:T(8,128)(2,1)S(1)}, u32[]{:S(2)}, u32[]{:S(2)}) collective-permute-start(bf16[2,320,128]{2,1,0:T(8,128)(2,1)S(1)} %get-tuple-element.59), channel_id=1, source_target_pairs={{0,1},{1,0},{2,3},{3,2},{4,5},{5,4},{6,7},{7,6},{8,9},{9,8},{10,11... | collective-permute-start | bytes 491528 | tf_op jit(solution)/shard_map/sum2_from_layer_1/ppermute | solution.py:200
  47.9 11.5 %collective-permute-start.18 = (bf16[2,320,128]{2,1,0:T(8,128)(2,1)S(1)}, bf16[2,320,128]{2,1,0:T(8,128)(2,1)S(1)}, u32[]{:S(2)}, u32[]{:S(2)}) collective-permute-start(bf16[2,320,128]{2,1,0:T(8,128)(2,1)S(1)} %get-tuple-element.51), channel_id=1, source_target_pairs={{0,1},{1,0},{2,3},{3,2},{4,5},{5,4},{6,7},{7,6},{8,9},{9,8},{10,11... | collective-permute-start | bytes 491528 | tf_op jit(solution)/shard_map/sum1_from_layer_1/ppermute | solution.py:200
  51.1 12.4 %collective-permute-start.26 = (bf16[2,320,128]{2,1,0:T(8,128)(2,1)S(1)}, bf16[2,320,128]{2,1,0:T(8,128)(2,1)S(1)}, u32[]{:S(2)}, u32[]{:S(2)}) collective-permute-start(bf16[2,320,128]{2,1,0:T(8,128)(2,1)S(1)} %get-tuple-element.62), channel_id=1, source_target_pairs={{0,1},{1,0},{2,3},{3,2},{4,5},{5,4},{6,7},{7,6},{8,9},{9,8},{10,11... | collective-permute-start | bytes 491528 | tf_op jit(solution)/shard_map/sum3_from_layer_1/ppermute | solution.py:200
  52.9 12.0 %collective-permute-start.17 = (bf16[1,320,128]{2,1,0:T(8,128)(2,1)S(1)}, bf16[1,320,128]{2,1,0:T(8,128)(2,1)S(1)}, u32[]{:S(2)}, u32[]{:S(2)}) collective-permute-start(bf16[1,320,128]{2,1,0:T(8,128)(2,1)S(1)} %get-tuple-element.49), channel_id=1, source_target_pairs={{0,2},{1,3},{2,0},{3,1},{4,6},{5,7},{6,4},{7,5},{8,10},{9,11},{10,... | collective-permute-start | bytes 245768 | tf_op jit(solution)/shard_map/sum0_from_layer_2/ppermute | solution.py:200
  55.5 9.3 %collective-permute-start.25 = (bf16[1,320,128]{2,1,0:T(8,128)(2,1)S(1)}, bf16[1,320,128]{2,1,0:T(8,128)(2,1)S(1)}, u32[]{:S(2)}, u32[]{:S(2)}) collective-permute-start(bf16[1,320,128]{2,1,0:T(8,128)(2,1)S(1)} %get-tuple-element.61), channel_id=1, source_target_pairs={{0,2},{1,3},{2,0},{3,1},{4,6},{5,7},{6,4},{7,5},{8,10},{9,11},{10,... | collective-permute-start | bytes 245768 | tf_op jit(solution)/shard_map/sum2_from_layer_2/ppermute | solution.py:200
  59.4 11.1 %collective-permute-start.23 = (bf16[1,320,128]{2,1,0:T(8,128)(2,1)S(1)}, bf16[1,320,128]{2,1,0:T(8,128)(2,1)S(1)}, u32[]{:S(2)}, u32[]{:S(2)}) collective-permute-start(bf16[1,320,128]{2,1,0:T(8,128)(2,1)S(1)} %get-tuple-element.58), channel_id=1, source_target_pairs={{0,2},{1,3},{2,0},{3,1},{4,6},{5,7},{6,4},{7,5},{8,10},{9,11},{10,... | collective-permute-start | bytes 245768 | tf_op jit(solution)/shard_map/sum1_from_layer_2/ppermute | solution.py:200
  63.5 7.9 %collective-permute-start.27 = (bf16[1,320,128]{2,1,0:T(8,128)(2,1)S(1)}, bf16[1,320,128]{2,1,0:T(8,128)(2,1)S(1)}, u32[]{:S(2)}, u32[]{:S(2)}) collective-permute-start(bf16[1,320,128]{2,1,0:T(8,128)(2,1)S(1)} %get-tuple-element.64), channel_id=1, source_target_pairs={{0,2},{1,3},{2,0},{3,1},{4,6},{5,7},{6,4},{7,5},{8,10},{9,11},{10,... | collective-permute-start | bytes 245768 | tf_op jit(solution)/shard_map/sum3_from_layer_2/ppermute | solution.py:200

commit v16 on v15

--- a/solution.py
+++ b/solution.py
@@ -159,34 +159,37 @@
     )(keep, got, after)
 
 
-def finish_kernel(sizes, counts, *refs):
-    place, (*refs, out) = refs[:3], refs[3:]
+def finish_kernel(sizes, where, first, *refs):
+    place, refs = refs[:3], refs[3 if first else 4 :]
+    out, sums, sems = refs[2 * len(where) :]
     _, _, order = positions(*sizes, place)
-    groups = len(order)
-    span = out.shape[1] // groups
-    width = span // CHUNKS
-    i = 0
-    for count in counts:
-        (keep, *rest), refs = refs[:count], refs[count:]
-        total = keep[0]
-        for got in rest:
-            total = total + got[0].astype(F32)
-        for low in range(0, total.shape[1], width):
-            at = order[i % groups] * span + i // groups * width
-            out[:, pl.ds(pl.multiple_of(at, width), width)] = total[:, low : low + width]
-            i += 1
-
-
-def finish(sizes, place, parts, queries):
-    rows = parts[0][0].shape[1]
-    return pl.pallas_call(
-        functools.partial(finish_kernel, sizes, tuple(map(len, parts))),
+    copies = []
+    for i, (j, low, high) in enumerate(where):
+        keep, got = refs[2 * i : 2 * i + 2]
+        sums[i] = keep[0] + got[0].astype(F32)
+        at = pl.multiple_of(order[j] * (out.shape[1] // len(order)) + low, high - low)
+        copies.append(pltpu.make_async_copy(sums.at[i], out.at[:, pl.ds(at, high - low)], sems.at[i]))
+        copies[-1].start()
+    for copy in copies:
+        copy.wait()
+
+
+def finish(sizes, place, where, parts, queries, out=None):
+    _, rows, width = parts[0][0].shape
+    old = [] if out is None else [out]
+    return pl.pallas_call(
+        functools.partial(finish_kernel, sizes, tuple(where), out is None),
         out_shape=jax.ShapeDtypeStruct((rows, queries), F32),
-        in_specs=[SMEM] * 3 + [VMEM] * sum(map(len, parts)),
-        out_specs=VMEM,
+        in_specs=[SMEM] * 3 + [ANY] * len(old) + [VMEM] * (2 * len(parts)),
+        out_specs=ANY,
+        scratch_shapes=[
+            pltpu.VMEM((len(parts), rows, width), F32),
+            pltpu.SemaphoreType.DMA((len(parts),)),
+        ],
+        input_output_aliases={3: 0} if old else {},
         compiler_params=pltpu.CompilerParams(vmem_limit_bytes=12 * MIB),
         name="finish",
-    )(*place, *[a for part in parts for a in part])
+    )(*place, *old, *[a for part in parts for a in part])
 
 
 def shards(groups, ex, layers, queries, hessian, store):
@@ -296,7 +299,13 @@
     last = send_parts(score("score2", sizes, place, rows, pieces, last))
     while any(part[0].shape[0] > 1 for part in parts):
         advance(last)
-    return finish(sizes, place, parts, total)
+    where = [(i % groups, i // groups * width, (i // groups + 1) * width) for i in range(len(parts))]
+    early = [i for i in range(len(parts)) if i % groups == 0]
+    late = [i for i in range(len(parts)) if i % groups]
+    out = None
+    for which in (early, late):
+        out = finish(sizes, place, [where[i] for i in which], [parts[i] for i in which], total, out)
+    return out
 
 
 def solution(mesh):

time: 72.6 us -> 72.4 us (level)
  waiting for transfers between devices: 23.1 us -> 22.3 us
    ppermute x28, waiting for transfers between devices: 23.1 us -> 22.3 us  [permute(): return lax.ppermute(x, axis, perm)]
    pallas_call x1 -> x2, Pallas kernels: 0.92 us -> 1.51 us  [finish(): pl.pallas_call(functools.partial(finish_kernel, sizes, tuple(where), out...]
  transfers between devices with their start and end apart: 28 -> 28, of which waited for: 12 -> 12; matrix products, arithmetic and copies ran while one was open for 0% -> 0% of each run, Pallas kernels for 26% -> 27%
where the time goes in v16:
time: 72.4 us; the launch traced here: 72.2 us
  starting transfers between devices  28.7 us (40%)
  waiting for transfers between devices  22.3 us (31%)
  Pallas kernels  21.1 us (29%)
    ppermute x28, starting transfers between devices, permute(): return lax.ppermute(x, axis, perm)  28.7 us
    ppermute x28, waiting for transfers between devices, permute(): return lax.ppermute(x, axis, perm)  22.3 us
    pallas_call x3, Pallas kernels, score(): pl.pallas_call(functools.partial(score_kernel, sizes, columns, direct), o...  9.14 us
    pallas_call x2, Pallas kernels, condition(): pl.pallas_call(functools.partial(condition_kernel, sizes), out_shape=[plt...  5.01 us
    pallas_call x1, Pallas kernels, load(): pl.pallas_call(load_kernel, out_shape=pltpu.VMEM(source.shape, BF16), in_...  3.39 us
    pallas_call x2, Pallas kernels, take(): pl.pallas_call(functools.partial(take_kernel, chunk), out_shape=pltpu.VME...  1.92 us
    pallas_call x2, Pallas kernels, finish(): pl.pallas_call(functools.partial(finish_kernel, sizes, tuple(where), out...  1.51 us
  transfers between devices with their start and end apart: 28, of which 12 were waited for; matrix products, arithmetic and copies ran while one was open for 0% of the time, Pallas kernels for 27%

profile of v16, /device:TPU:0, one launch (start us, length us, event | category | flops | bytes accessed | tf_op | source)
XLA Modules:
  0.0 72.2 jit_solution(13359890455211001254)
XLA Ops:
  0.0 1.0 %take.2.after.refs_4_ = bf16[128,1024]{1,0:T(8,128)(2,1)S(1)} custom-call(s32[1]{0:T(128)} %bitcast.at_group.after.refs_0_, s32[1]{0:T(128)} %bitcast.1.at_ex.refs_1_, s32[1]{0:T(128)} %bitcast.2.at_layer.refs_2_, bf16[512,1024]{1,0:T(8,128)(2,1)} %bitcast.12, s32[1]{0:T(128)} %bitcast.at_group.after.refs_0_), custom_call_target="tpu_custom_call" | custom-call | tf_op jit(solution)/shard_map/take/pallas_call | solution.py:58
  1.0 3.0 %collective-permute-start.1 = (bf16[128,1024]{1,0:T(8,128)(2,1)S(1)}, bf16[128,1024]{1,0:T(8,128)(2,1)S(1)}, u32[]{:S(2)}, u32[]{:S(2)}) collective-permute-start(bf16[128,1024]{1,0:T(8,128)(2,1)S(1)} %take.2.after.refs_4_), channel_id=1, source_target_pairs={{0,8},{4,12},{8,0},{12,4},{1,9},{5,13},{9,1},{13,5},{2,10},{6,14},... | collective-permute-start | bytes 786440 | tf_op jit(solution)/shard_map/q0_from_chip/ppermute | solution.py:203
  4.0 3.4 %load.1.after.refs_3_ = bf16[1024,4096]{1,0:T(8,128)(2,1)S(1)} custom-call(bf16[1024,4096]{1,0:T(8,128)(2,1)} %bitcast.11, bf16[128,1024]{1,0:T(8,128)(2,1)S(1)} %take.2.after.refs_4_), custom_call_target="tpu_custom_call" | custom-call | tf_op jit(solution)/shard_map/load/pallas_call | solution.py:38
  7.4 1.0 %take.3.refs_8_.refs_4_ = bf16[128,1024]{1,0:T(8,128)(2,1)S(1)} custom-call(s32[1]{0:T(128)} %bitcast.at_group.after.refs_0_, s32[1]{0:T(128)} %bitcast.1.at_ex.refs_1_, s32[1]{0:T(128)} %bitcast.2.at_layer.refs_2_, bf16[512,1024]{1,0:T(8,128)(2,1)} %bitcast.13, bf16[1024,4096]{1,0:T(8,128)(2,1)S(1)} %load.1.after.refs_3_), custom_call_target="tpu_custom_call" | custom-call | tf_op jit(solution)/shard_map/take/pallas_call | solution.py:58
  8.4 0.0 slice-start
  8.4 0.0 slice-start.1
  8.4 1.9 %collective-permute-done.1.refs_6_ = bf16[128,1024]{1,0:T(8,128)(2,1)S(1)} collective-permute-done((bf16[128,1024]{1,0:T(8,128)(2,1)S(1)}, bf16[128,1024]{1,0:T(8,128)(2,1)S(1)}, u32[]{:S(2)}, u32[]{:S(2)}) %collective-permute-start.1) | collective-permute-done | bytes 262176 | tf_op jit(solution)/shard_map/q0_from_chip/ppermute | solution.py:203
  10.3 0.0 collective-permute-start.2
  10.3 1.7 %collective-permute-start.6 = (bf16[128,1024]{1,0:T(8,128)(2,1)S(1)}, bf16[128,1024]{1,0:T(8,128)(2,1)S(1)}, u32[]{:S(2)}, u32[]{:S(2)}) collective-permute-start(bf16[128,1024]{1,0:T(8,128)(2,1)S(1)} %take.3.refs_8_.refs_4_), channel_id=1, source_target_pairs={{0,8},{4,12},{8,0},{12,4},{1,9},{5,13},{9,1},{13,5},{2,10},{6,14},... | collective-permute-start | bytes 786440 | tf_op jit(solution)/shard_map/q1_from_chip/ppermute | solution.py:203
  12.1 2.5 %condition.2 = (bf16[1024,128]{1,0:T(8,128)(2,1)S(1)}, bf16[1040,128]{1,0:T(8,128)(2,1)S(1)}, bf16[1024,128]{1,0:T(8,128)(2,1)S(1)}) custom-call(s32[1]{0:T(128)} %bitcast.at_group.after.refs_0_, s32[1]{0:T(128)} %bitcast.1.at_ex.refs_1_, s32[1]{0:T(128)} %bitcast.2.at_layer.refs_2_, bf16[1024,4096]{1,0:T(8,128)(2,1)S(1)} %load.1.after.refs_3_, ...), custom_call_target="tpu_custom_call" | custom-call | tf_op jit(solution)/shard_map/condition/pallas_call | solution.py:89
  14.5 1.6 %collective-permute-start.4 = (bf16[1040,128]{1,0:T(8,128)(2,1)S(1)}, bf16[1040,128]{1,0:T(8,128)(2,1)S(1)}, u32[]{:S(2)}, u32[]{:S(2)}) collective-permute-start(bf16[1040,128]{1,0:T(8,128)(2,1)S(1)} %get-tuple-element.37), channel_id=1, source_target_pairs={{0,8},{4,12},{8,0},{12,4},{1,9},{5,13},{9,1},{13,5},{2,10},{6,14},... | collective-permute-start | bytes 798728 | tf_op jit(solution)/shard_map/s0_from_chip/ppermute | solution.py:203
  16.1 0.0 collective-permute-start.5
  16.1 3.3 %collective-permute-done.6.refs_6_ = bf16[128,1024]{1,0:T(8,128)(2,1)S(1)} collective-permute-done((bf16[128,1024]{1,0:T(8,128)(2,1)S(1)}, bf16[128,1024]{1,0:T(8,128)(2,1)S(1)}, u32[]{:S(2)}, u32[]{:S(2)}) %collective-permute-start.6) | collective-permute-done | bytes 262176 | tf_op jit(solution)/shard_map/q1_from_chip/ppermute | solution.py:203
  19.4 1.7 %collective-permute-start.10 = (bf16[1024,128]{1,0:T(8,128)(2,1)S(1)}, bf16[1024,128]{1,0:T(8,128)(2,1)S(1)}, u32[]{:S(2)}, u32[]{:S(2)}) collective-permute-start(bf16[1024,128]{1,0:T(8,128)(2,1)S(1)} %get-tuple-element.43), channel_id=1, source_target_pairs={{0,16},{16,0},{1,17},{17,1},{2,18},{18,2},{3,19},{19,3},{4,20},{20... | collective-permute-start | bytes 786440 | tf_op jit(solution)/shard_map/s0_from_group/ppermute | solution.py:203
  21.1 0.2 collective-permute-start.3
  21.4 0.0 collective-permute-done.5.refs_5_
  21.4 0.0 collective-permute-done.7.refs_7_
  21.4 2.5 %condition.3 = (bf16[1024,128]{1,0:T(8,128)(2,1)S(1)}, bf16[1024,128]{1,0:T(8,128)(2,1)S(1)}) custom-call(s32[1]{0:T(128)} %bitcast.at_group.after.refs_0_, s32[1]{0:T(128)} %bitcast.1.at_ex.refs_1_, s32[1]{0:T(128)} %bitcast.2.at_layer.refs_2_, bf16[1024,4096]{1,0:T(8,128)(2,1)S(1)} %load.1.after.refs_3_, bf16[128,1024]{1,0:T(8,128)(2,1)S(1)} %take.3.refs_8_.refs_4_, ...), custom_call_target="tpu_custom_call" | custom-call | tf_op jit(solution)/shard_map/condition/pallas_call | solution.py:89
  23.9 0.8 %collective-permute-done.4.refs_6_ = bf16[1040,128]{1,0:T(8,128)(2,1)S(1)} collective-permute-done((bf16[1040,128]{1,0:T(8,128)(2,1)S(1)}, bf16[1040,128]{1,0:T(8,128)(2,1)S(1)}, u32[]{:S(2)}, u32[]{:S(2)}) %collective-permute-start.4) | collective-permute-done | bytes 266272 | tf_op jit(solution)/shard_map/s0_from_chip/ppermute | solution.py:203
  24.7 1.7 %collective-permute-start.12 = (bf16[1040,128]{1,0:T(8,128)(2,1)S(1)}, bf16[1040,128]{1,0:T(8,128)(2,1)S(1)}, u32[]{:S(2)}, u32[]{:S(2)}) collective-permute-start(bf16[1040,128]{1,0:T(8,128)(2,1)S(1)} %collective-permute-done.4.refs_6_), channel_id=1, source_target_pairs={{0,16},{16,0},{1,17},{17,1},{2,18},{18,2},{3,19},{19,3},{4,20},{20... | collective-permute-start | bytes 798728 | tf_op jit(solution)/shard_map/s0_there_from_group/ppermute | solution.py:203
  26.4 1.5 %collective-permute-start.15 = (bf16[1024,128]{1,0:T(8,128)(2,1)S(1)}, bf16[1024,128]{1,0:T(8,128)(2,1)S(1)}, u32[]{:S(2)}, u32[]{:S(2)}) collective-permute-start(bf16[1024,128]{1,0:T(8,128)(2,1)S(1)} %get-tuple-element.39.refs_8_), channel_id=1, source_target_pairs={{0,8},{4,12},{8,0},{12,4},{1,9},{5,13},{9,1},{13,5},{2,10},{6,14},... | collective-permute-start | bytes 786440 | tf_op jit(solution)/shard_map/s1_from_chip/ppermute | solution.py:203
  28.0 0.4 collective-permute-done.10.refs_4_
  28.4 1.7 %collective-permute-start.19 = (bf16[1024,128]{1,0:T(8,128)(2,1)S(1)}, bf16[1024,128]{1,0:T(8,128)(2,1)S(1)}, u32[]{:S(2)}, u32[]{:S(2)}) collective-permute-start(bf16[1024,128]{1,0:T(8,128)(2,1)S(1)} %get-tuple-element.51), channel_id=1, source_target_pairs={{0,16},{16,0},{1,17},{17,1},{2,18},{18,2},{3,19},{19,3},{4,20},{20... | collective-permute-start | bytes 786440 | tf_op jit(solution)/shard_map/s1_from_group/ppermute | solution.py:203
  30.1 2.9 %score0.1 = (bf16[2,320,128]{2,1,0:T(8,128)(2,1)S(1)}, f32[2,320,128]{2,1,0:T(8,128)S(1)}) custom-call(s32[1]{0:T(128)} %bitcast.at_group.after.refs_0_, s32[1]{0:T(128)} %bitcast.1.at_ex.refs_1_, s32[1]{0:T(128)} %bitcast.2.at_layer.refs_2_, bf16[1280,4096]{1,0:T(8,128)(2,1)S(1)} %bitcast.8, bf16[1024,128]{1,0:T(8,128)(2,1)S(1)} %get-tuple-element.36.refs_8_.refs_4_, ...), custom_call_target="tpu_custom_call" | custom-call | tf_op jit(solution)/shard_map/score0/pallas_call | solution.py:129
  33.1 1.0 %collective-permute-done.12.refs_6_ = bf16[1040,128]{1,0:T(8,128)(2,1)S(1)} collective-permute-done((bf16[1040,128]{1,0:T(8,128)(2,1)S(1)}, bf16[1040,128]{1,0:T(8,128)(2,1)S(1)}, u32[]{:S(2)}, u32[]{:S(2)}) %collective-permute-start.12) | collective-permute-done | bytes 266272 | tf_op jit(solution)/shard_map/s0_there_from_group/ppermute | solution.py:203
  34.1 0.5 collective-permute-start.14
  34.6 0.3 collective-permute-done.15.refs_10_
  34.9 1.5 %collective-permute-start.21 = (bf16[1024,128]{1,0:T(8,128)(2,1)S(1)}, bf16[1024,128]{1,0:T(8,128)(2,1)S(1)}, u32[]{:S(2)}, u32[]{:S(2)}) collective-permute-start(bf16[1024,128]{1,0:T(8,128)(2,1)S(1)} %collective-permute-done.15.refs_10_), channel_id=1, source_target_pairs={{0,16},{16,0},{1,17},{17,1},{2,18},{18,2},{3,19},{19,3},{4,20},{20... | collective-permute-start | bytes 786440 | tf_op jit(solution)/shard_map/s1_there_from_group/ppermute | solution.py:203
  36.4 3.3 %collective-permute-done.19.refs_4_ = bf16[1024,128]{1,0:T(8,128)(2,1)S(1)} collective-permute-done((bf16[1024,128]{1,0:T(8,128)(2,1)S(1)}, bf16[1024,128]{1,0:T(8,128)(2,1)S(1)}, u32[]{:S(2)}, u32[]{:S(2)}) %collective-permute-start.19) | collective-permute-done | bytes 262176 | tf_op jit(solution)/shard_map/s1_from_group/ppermute | solution.py:203
  39.7 1.8 %collective-permute-start.9 = (bf16[2,320,128]{2,1,0:T(8,128)(2,1)S(1)}, bf16[2,320,128]{2,1,0:T(8,128)(2,1)S(1)}, u32[]{:S(2)}, u32[]{:S(2)}) collective-permute-start(bf16[2,320,128]{2,1,0:T(8,128)(2,1)S(1)} %get-tuple-element.42), channel_id=1, source_target_pairs={{0,1},{1,0},{2,3},{3,2},{4,5},{5,4},{6,7},{7,6},{8,9},{9,8},{10,11... | collective-permute-start | bytes 491528 | tf_op jit(solution)/shard_map/sum0_from_layer_1/ppermute | solution.py:203
  41.5 3.3 %score1.1 = (bf16[2,320,128]{2,1,0:T(8,128)(2,1)S(1)}, f32[2,320,128]{2,1,0:T(8,128)S(1)}, bf16[2,320,128]{2,1,0:T(8,128)(2,1)S(1)}, f32[2,320,128]{2,1,0:T(8,128)S(1)}) custom-call(s32[1]{0:T(128)} %bitcast.at_group.after.refs_0_, s32[1]{0:T(128)} %bitcast.1.at_ex.refs_1_, s32[1]{0:T(128)} %bitcast.2.at_layer.refs_2_, bf16[1280,4096]{1,0:T(8,128)(2,1)S(1)} %bitcast.9, ...), custom_call_target="tpu_custom_call" | custom-call | tf_op jit(solution)/shard_map/score1/pallas_call | solution.py:129
  44.8 0.7 %collective-permute-done.9.got = bf16[2,320,128]{2,1,0:T(8,128)(2,1)S(1)} collective-permute-done((bf16[2,320,128]{2,1,0:T(8,128)(2,1)S(1)}, bf16[2,320,128]{2,1,0:T(8,128)(2,1)S(1)}, u32[]{:S(2)}, u32[]{:S(2)}) %collective-permute-start.9) | collective-permute-done | bytes 163872 | tf_op jit(solution)/shard_map/sum0_from_layer_1/ppermute | solution.py:203
  45.5 0.1 collective-permute-start.22
  45.6 0.5 collective-permute-start.20
  46.1 1.7 %collective-permute-start.24 = (bf16[2,320,128]{2,1,0:T(8,128)(2,1)S(1)}, bf16[2,320,128]{2,1,0:T(8,128)(2,1)S(1)}, u32[]{:S(2)}, u32[]{:S(2)}) collective-permute-start(bf16[2,320,128]{2,1,0:T(8,128)(2,1)S(1)} %get-tuple-element.59), channel_id=1, source_target_pairs={{0,1},{1,0},{2,3},{3,2},{4,5},{5,4},{6,7},{7,6},{8,9},{9,8},{10,11... | collective-permute-start | bytes 491528 | tf_op jit(solution)/shard_map/sum1_from_layer_1/ppermute | solution.py:203
  47.9 0.3 collective-permute-start.18
  48.2 2.9 %score2.1 = (bf16[2,320,128]{2,1,0:T(8,128)(2,1)S(1)}, f32[2,320,128]{2,1,0:T(8,128)S(1)}) custom-call(s32[1]{0:T(128)} %bitcast.at_group.after.refs_0_, s32[1]{0:T(128)} %bitcast.1.at_ex.refs_1_, s32[1]{0:T(128)} %bitcast.2.at_layer.refs_2_, bf16[1280,4096]{1,0:T(8,128)(2,1)S(1)} %bitcast.10, bf16[1024,128]{1,0:T(8,128)(2,1)S(1)} %collective-permute-done.19.refs_4_, ...), custom_call_target="tpu_custom_call" | custom-call | tf_op jit(solution)/shard_map/score2/pallas_call | solution.py:129
  51.1 1.8 %collective-permute-start.26 = (bf16[2,320,128]{2,1,0:T(8,128)(2,1)S(1)}, bf16[2,320,128]{2,1,0:T(8,128)(2,1)S(1)}, u32[]{:S(2)}, u32[]{:S(2)}) collective-permute-start(bf16[2,320,128]{2,1,0:T(8,128)(2,1)S(1)} %get-tuple-element.62), channel_id=1, source_target_pairs={{0,1},{1,0},{2,3},{3,2},{4,5},{5,4},{6,7},{7,6},{8,9},{9,8},{10,11... | collective-permute-start | bytes 491528 | tf_op jit(solution)/shard_map/sum3_from_layer_1/ppermute | solution.py:203
  52.9 2.6 %collective-permute-start.17 = (bf16[1,320,128]{2,1,0:T(8,128)(2,1)S(1)}, bf16[1,320,128]{2,1,0:T(8,128)(2,1)S(1)}, u32[]{:S(2)}, u32[]{:S(2)}) collective-permute-start(bf16[1,320,128]{2,1,0:T(8,128)(2,1)S(1)} %get-tuple-element.49), channel_id=1, source_target_pairs={{0,2},{1,3},{2,0},{3,1},{4,6},{5,7},{6,4},{7,5},{8,10},{9,11},{10,... | collective-permute-start | bytes 245768 | tf_op jit(solution)/shard_map/sum0_from_layer_2/ppermute | solution.py:203
  55.5 0.5 collective-permute-start.25
  56.0 3.3 %collective-permute-done.18.got = bf16[2,320,128]{2,1,0:T(8,128)(2,1)S(1)} collective-permute-done((bf16[2,320,128]{2,1,0:T(8,128)(2,1)S(1)}, bf16[2,320,128]{2,1,0:T(8,128)(2,1)S(1)}, u32[]{:S(2)}, u32[]{:S(2)}) %collective-permute-start.18) | collective-permute-done | bytes 163872 | tf_op jit(solution)/shard_map/sum2_from_layer_1/ppermute | solution.py:203
  59.4 2.8 %collective-permute-start.23 = (bf16[1,320,128]{2,1,0:T(8,128)(2,1)S(1)}, bf16[1,320,128]{2,1,0:T(8,128)(2,1)S(1)}, u32[]{:S(2)}, u32[]{:S(2)}) collective-permute-start(bf16[1,320,128]{2,1,0:T(8,128)(2,1)S(1)} %get-tuple-element.57), channel_id=1, source_target_pairs={{0,2},{1,3},{2,0},{3,1},{4,6},{5,7},{6,4},{7,5},{8,10},{9,11},{10,... | collective-permute-start | bytes 245768 | tf_op jit(solution)/shard_map/sum2_from_layer_2/ppermute | solution.py:203
  62.2 1.3 %collective-permute-done.26.got = bf16[2,320,128]{2,1,0:T(8,128)(2,1)S(1)} collective-permute-done((bf16[2,320,128]{2,1,0:T(8,128)(2,1)S(1)}, bf16[2,320,128]{2,1,0:T(8,128)(2,1)S(1)}, u32[]{:S(2)}, u32[]{:S(2)}) %collective-permute-start.26) | collective-permute-done | bytes 163872 | tf_op jit(solution)/shard_map/sum3_from_layer_1/ppermute | solution.py:203
  63.5 1.4 %collective-permute-start.27 = (bf16[1,320,128]{2,1,0:T(8,128)(2,1)S(1)}, bf16[1,320,128]{2,1,0:T(8,128)(2,1)S(1)}, u32[]{:S(2)}, u32[]{:S(2)}) collective-permute-start(bf16[1,320,128]{2,1,0:T(8,128)(2,1)S(1)} %get-tuple-element.64), channel_id=1, source_target_pairs={{0,2},{1,3},{2,0},{3,1},{4,6},{5,7},{6,4},{7,5},{8,10},{9,11},{10,... | collective-permute-start | bytes 245768 | tf_op jit(solution)/shard_map/sum3_from_layer_2/ppermute | solution.py:203
  64.9 5.6 %collective-permute-done.23.refs_6_ = bf16[1,320,128]{2,1,0:T(8,128)(2,1)S(1)} collective-permute-done((bf16[1,320,128]{2,1,0:T(8,128)(2,1)S(1)}, bf16[1,320,128]{2,1,0:T(8,128)(2,1)S(1)}, u32[]{:S(2)}, u32[]{:S(2)}) %collective-permute-start.23) | collective-permute-done | bytes 81952 | tf_op jit(solution)/shard_map/sum2_from_layer_2/ppermute | solution.py:203
  70.5 0.8 %finish.2.refs_3_ = f32[320,512]{1,0:T(8,128)} custom-call(s32[1]{0:T(128)} %bitcast.at_group.after.refs_0_, s32[1]{0:T(128)} %bitcast.1.at_ex.refs_1_, s32[1]{0:T(128)} %bitcast.2.at_layer.refs_2_, f32[1,320,128]{2,1,0:T(8,128)S(1)} %get-tuple-element.48.refs_8_.refs_3_, bf16[1,320,128]{2,1,0:T(8,128)(2,1)S(1)} %collective-permute-done.17.refs_4_, ...), custom_call_target="tpu_custom_call" | custom-call | tf_op jit(solution)/shard_map/finish/pallas_call | solution.py:180
  71.2 0.3 collective-permute-done.27.refs_7_
  71.5 0.8 %finish.3 = f32[320,512]{1,0:T(8,128)} custom-call(s32[1]{0:T(128)} %bitcast.at_group.after.refs_0_, s32[1]{0:T(128)} %bitcast.1.at_ex.refs_1_, s32[1]{0:T(128)} %bitcast.2.at_layer.refs_2_, f32[320,512]{1,0:T(8,128)} %finish.2.refs_3_, f32[1,320,128]{2,1,0:T(8,128)S(1)} %get-tuple-element.60.refs_4_, ...), custom_call_target="tpu_custom_call", output_to_operand_aliasing={{}: (3, {})} | custom-call | tf_op jit(solution)/shard_map/finish/pallas_call | solution.py:180
  (29 shorter events, 0.2 us)
Async XLA Ops:
  1.0 9.3 %collective-permute-start.1 = (bf16[128,1024]{1,0:T(8,128)(2,1)S(1)}, bf16[128,1024]{1,0:T(8,128)(2,1)S(1)}, u32[]{:S(2)}, u32[]{:S(2)}) collective-permute-start(bf16[128,1024]{1,0:T(8,128)(2,1)S(1)} %take.2.after.refs_4_), channel_id=1, source_target_pairs={{0,8},{4,12},{8,0},{12,4},{1,9},{5,13},{9,1},{13,5},{2,10},{6,14},... | collective-permute-start | bytes 786440 | tf_op jit(solution)/shard_map/q0_from_chip/ppermute | solution.py:203
  4.0 8.1 %collective-permute-start = (bf16[128,1024]{1,0:T(8,128)(2,1)S(1)}, bf16[128,1024]{1,0:T(8,128)(2,1)S(1)}, u32[]{:S(2)}, u32[]{:S(2)}) collective-permute-start(bf16[128,1024]{1,0:T(8,128)(2,1)S(1)} %take.2.after.refs_4_), channel_id=1, source_target_pairs={{0,4},{4,0},{8,12},{12,8},{1,5},{5,1},{9,13},{13,9},{2,6},{6,2},{1... | collective-permute-start | bytes 786440 | tf_op jit(solution)/shard_map/q0_from_core/ppermute | solution.py:203
  8.4 21.7 %slice-start = ((s8[10485760]{0:T(1024)(128)(4,1)}), s8[4194304]{0:T(1024)(128)(4,1)S(1)}, s32[]{:S(2)}) async-start(s8[10485760]{0:T(1024)(128)(4,1)} %bitcast.6), calls=%async_computation | async-start | bytes 8388608
  8.4 21.7 %slice-start.1 = ((s8[10485760]{0:T(1024)(128)(4,1)}), s8[4194304]{0:T(1024)(128)(4,1)S(1)}, s32[]{:S(2)}) async-start(s8[10485760]{0:T(1024)(128)(4,1)} %bitcast.6), calls=%async_computation.1 | async-start | bytes 8388608
  10.3 1.8 %collective-permute-start.2 = (bf16[128,1024]{1,0:T(8,128)(2,1)S(1)}, bf16[128,1024]{1,0:T(8,128)(2,1)S(1)}, u32[]{:S(2)}, u32[]{:S(2)}) collective-permute-start(bf16[128,1024]{1,0:T(8,128)(2,1)S(1)} %collective-permute-done.1.refs_6_), channel_id=1, source_target_pairs={{0,4},{4,0},{8,12},{12,8},{1,5},{5,1},{9,13},{13,9},{2,6},{6,2},{1... | collective-permute-start | bytes 786440 | tf_op jit(solution)/shard_map/q0_there_from_core/ppermute | solution.py:203
  10.3 9.1 %collective-permute-start.6 = (bf16[128,1024]{1,0:T(8,128)(2,1)S(1)}, bf16[128,1024]{1,0:T(8,128)(2,1)S(1)}, u32[]{:S(2)}, u32[]{:S(2)}) collective-permute-start(bf16[128,1024]{1,0:T(8,128)(2,1)S(1)} %take.3.refs_8_.refs_4_), channel_id=1, source_target_pairs={{0,8},{4,12},{8,0},{12,4},{1,9},{5,13},{9,1},{13,5},{2,10},{6,14},... | collective-permute-start | bytes 786440 | tf_op jit(solution)/shard_map/q1_from_chip/ppermute | solution.py:203
  14.5 10.2 %collective-permute-start.4 = (bf16[1040,128]{1,0:T(8,128)(2,1)S(1)}, bf16[1040,128]{1,0:T(8,128)(2,1)S(1)}, u32[]{:S(2)}, u32[]{:S(2)}) collective-permute-start(bf16[1040,128]{1,0:T(8,128)(2,1)S(1)} %get-tuple-element.37), channel_id=1, source_target_pairs={{0,8},{4,12},{8,0},{12,4},{1,9},{5,13},{9,1},{13,5},{2,10},{6,14},... | collective-permute-start | bytes 798728 | tf_op jit(solution)/shard_map/s0_from_chip/ppermute | solution.py:203
  16.1 5.2 %collective-permute-start.5 = (bf16[128,1024]{1,0:T(8,128)(2,1)S(1)}, bf16[128,1024]{1,0:T(8,128)(2,1)S(1)}, u32[]{:S(2)}, u32[]{:S(2)}) collective-permute-start(bf16[128,1024]{1,0:T(8,128)(2,1)S(1)} %take.3.refs_8_.refs_4_), channel_id=1, source_target_pairs={{0,4},{4,0},{8,12},{12,8},{1,5},{5,1},{9,13},{13,9},{2,6},{6,2},{1... | collective-permute-start | bytes 786440 | tf_op jit(solution)/shard_map/q1_from_core/ppermute | solution.py:203
  19.4 2.0 %collective-permute-start.7 = (bf16[128,1024]{1,0:T(8,128)(2,1)S(1)}, bf16[128,1024]{1,0:T(8,128)(2,1)S(1)}, u32[]{:S(2)}, u32[]{:S(2)}) collective-permute-start(bf16[128,1024]{1,0:T(8,128)(2,1)S(1)} %collective-permute-done.6.refs_6_), channel_id=1, source_target_pairs={{0,4},{4,0},{8,12},{12,8},{1,5},{5,1},{9,13},{13,9},{2,6},{6,2},{1... | collective-permute-start | bytes 786440 | tf_op jit(solution)/shard_map/q1_there_from_core/ppermute | solution.py:203
  19.4 10.7 %slice-start.2 = ((s8[10485760]{0:T(1024)(128)(4,1)}), s8[2097152]{0:T(1024)(128)(4,1)S(1)}, s32[]{:S(2)}) async-start(s8[10485760]{0:T(1024)(128)(4,1)} %bitcast.6), calls=%async_computation.2 | async-start | bytes 4194304
  19.4 8.9 %collective-permute-start.10 = (bf16[1024,128]{1,0:T(8,128)(2,1)S(1)}, bf16[1024,128]{1,0:T(8,128)(2,1)S(1)}, u32[]{:S(2)}, u32[]{:S(2)}) collective-permute-start(bf16[1024,128]{1,0:T(8,128)(2,1)S(1)} %get-tuple-element.43), channel_id=1, source_target_pairs={{0,16},{16,0},{1,17},{17,1},{2,18},{18,2},{3,19},{19,3},{4,20},{20... | collective-permute-start | bytes 786440 | tf_op jit(solution)/shard_map/s0_from_group/ppermute | solution.py:203
  21.1 7.2 %collective-permute-start.3 = (bf16[1024,128]{1,0:T(8,128)(2,1)S(1)}, bf16[1024,128]{1,0:T(8,128)(2,1)S(1)}, u32[]{:S(2)}, u32[]{:S(2)}) collective-permute-start(bf16[1024,128]{1,0:T(8,128)(2,1)S(1)} %get-tuple-element.36.refs_8_.refs_4_), channel_id=1, source_target_pairs={{0,4},{4,0},{8,12},{12,8},{1,5},{5,1},{9,13},{13,9},{2,6},{6,2},{1... | collective-permute-start | bytes 786440 | tf_op jit(solution)/shard_map/s0_from_core/ppermute | solution.py:203
  24.7 5.4 %collective-permute-start.8 = (bf16[1040,128]{1,0:T(8,128)(2,1)S(1)}, bf16[1040,128]{1,0:T(8,128)(2,1)S(1)}, u32[]{:S(2)}, u32[]{:S(2)}) collective-permute-start(bf16[1040,128]{1,0:T(8,128)(2,1)S(1)} %collective-permute-done.4.refs_6_), channel_id=1, source_target_pairs={{0,4},{4,0},{8,12},{12,8},{1,5},{5,1},{9,13},{13,9},{2,6},{6,2},{1... | collective-permute-start | bytes 798728 | tf_op jit(solution)/shard_map/s0_there_from_core/ppermute | solution.py:203
  24.7 9.3 %collective-permute-start.12 = (bf16[1040,128]{1,0:T(8,128)(2,1)S(1)}, bf16[1040,128]{1,0:T(8,128)(2,1)S(1)}, u32[]{:S(2)}, u32[]{:S(2)}) collective-permute-start(bf16[1040,128]{1,0:T(8,128)(2,1)S(1)} %collective-permute-done.4.refs_6_), channel_id=1, source_target_pairs={{0,16},{16,0},{1,17},{17,1},{2,18},{18,2},{3,19},{19,3},{4,20},{20... | collective-permute-start | bytes 798728 | tf_op jit(solution)/shard_map/s0_there_from_group/ppermute | solution.py:203
  26.4 8.4 %collective-permute-start.15 = (bf16[1024,128]{1,0:T(8,128)(2,1)S(1)}, bf16[1024,128]{1,0:T(8,128)(2,1)S(1)}, u32[]{:S(2)}, u32[]{:S(2)}) collective-permute-start(bf16[1024,128]{1,0:T(8,128)(2,1)S(1)} %get-tuple-element.39.refs_8_), channel_id=1, source_target_pairs={{0,8},{4,12},{8,0},{12,4},{1,9},{5,13},{9,1},{13,5},{2,10},{6,14},... | collective-permute-start | bytes 786440 | tf_op jit(solution)/shard_map/s1_from_chip/ppermute | solution.py:203
  28.4 6.5 %collective-permute-start.11 = (bf16[1024,128]{1,0:T(8,128)(2,1)S(1)}, bf16[1024,128]{1,0:T(8,128)(2,1)S(1)}, u32[]{:S(2)}, u32[]{:S(2)}) collective-permute-start(bf16[1024,128]{1,0:T(8,128)(2,1)S(1)} %collective-permute-done.10.refs_4_), channel_id=1, source_target_pairs={{0,4},{4,0},{8,12},{12,8},{1,5},{5,1},{9,13},{13,9},{2,6},{6,2},{1... | collective-permute-start | bytes 786440 | tf_op jit(solution)/shard_map/s0_across_from_core/ppermute | solution.py:203
  28.4 11.3 %collective-permute-start.19 = (bf16[1024,128]{1,0:T(8,128)(2,1)S(1)}, bf16[1024,128]{1,0:T(8,128)(2,1)S(1)}, u32[]{:S(2)}, u32[]{:S(2)}) collective-permute-start(bf16[1024,128]{1,0:T(8,128)(2,1)S(1)} %get-tuple-element.51), channel_id=1, source_target_pairs={{0,16},{16,0},{1,17},{17,1},{2,18},{18,2},{3,19},{19,3},{4,20},{20... | collective-permute-start | bytes 786440 | tf_op jit(solution)/shard_map/s1_from_group/ppermute | solution.py:203
  34.1 7.4 %collective-permute-start.13 = (bf16[1040,128]{1,0:T(8,128)(2,1)S(1)}, bf16[1040,128]{1,0:T(8,128)(2,1)S(1)}, u32[]{:S(2)}, u32[]{:S(2)}) collective-permute-start(bf16[1040,128]{1,0:T(8,128)(2,1)S(1)} %collective-permute-done.12.refs_6_), channel_id=1, source_target_pairs={{0,4},{4,0},{8,12},{12,8},{1,5},{5,1},{9,13},{13,9},{2,6},{6,2},{1... | collective-permute-start | bytes 798728 | tf_op jit(solution)/shard_map/s0_diagonal_from_core/ppermute | solution.py:203
  34.1 7.4 %collective-permute-start.14 = (bf16[1024,128]{1,0:T(8,128)(2,1)S(1)}, bf16[1024,128]{1,0:T(8,128)(2,1)S(1)}, u32[]{:S(2)}, u32[]{:S(2)}) collective-permute-start(bf16[1024,128]{1,0:T(8,128)(2,1)S(1)} %get-tuple-element.39.refs_8_), channel_id=1, source_target_pairs={{0,4},{4,0},{8,12},{12,8},{1,5},{5,1},{9,13},{13,9},{2,6},{6,2},{1... | collective-permute-start | bytes 786440 | tf_op jit(solution)/shard_map/s1_from_core/ppermute | solution.py:203
  34.9 6.6 %collective-permute-start.16 = (bf16[1024,128]{1,0:T(8,128)(2,1)S(1)}, bf16[1024,128]{1,0:T(8,128)(2,1)S(1)}, u32[]{:S(2)}, u32[]{:S(2)}) collective-permute-start(bf16[1024,128]{1,0:T(8,128)(2,1)S(1)} %collective-permute-done.15.refs_10_), channel_id=1, source_target_pairs={{0,4},{4,0},{8,12},{12,8},{1,5},{5,1},{9,13},{13,9},{2,6},{6,2},{1... | collective-permute-start | bytes 786440 | tf_op jit(solution)/shard_map/s1_there_from_core/ppermute | solution.py:203
  34.9 10.6 %collective-permute-start.21 = (bf16[1024,128]{1,0:T(8,128)(2,1)S(1)}, bf16[1024,128]{1,0:T(8,128)(2,1)S(1)}, u32[]{:S(2)}, u32[]{:S(2)}) collective-permute-start(bf16[1024,128]{1,0:T(8,128)(2,1)S(1)} %collective-permute-done.15.refs_10_), channel_id=1, source_target_pairs={{0,16},{16,0},{1,17},{17,1},{2,18},{18,2},{3,19},{19,3},{4,20},{20... | collective-permute-start | bytes 786440 | tf_op jit(solution)/shard_map/s1_there_from_group/ppermute | solution.py:203
  39.7 5.8 %collective-permute-start.9 = (bf16[2,320,128]{2,1,0:T(8,128)(2,1)S(1)}, bf16[2,320,128]{2,1,0:T(8,128)(2,1)S(1)}, u32[]{:S(2)}, u32[]{:S(2)}) collective-permute-start(bf16[2,320,128]{2,1,0:T(8,128)(2,1)S(1)} %get-tuple-element.42), channel_id=1, source_target_pairs={{0,1},{1,0},{2,3},{3,2},{4,5},{5,4},{6,7},{7,6},{8,9},{9,8},{10,11... | collective-permute-start | bytes 491528 | tf_op jit(solution)/shard_map/sum0_from_layer_1/ppermute | solution.py:203
  45.5 2.6 %collective-permute-start.22 = (bf16[1024,128]{1,0:T(8,128)(2,1)S(1)}, bf16[1024,128]{1,0:T(8,128)(2,1)S(1)}, u32[]{:S(2)}, u32[]{:S(2)}) collective-permute-start(bf16[1024,128]{1,0:T(8,128)(2,1)S(1)} %collective-permute-done.21.refs_6_), channel_id=1, source_target_pairs={{0,4},{4,0},{8,12},{12,8},{1,5},{5,1},{9,13},{13,9},{2,6},{6,2},{1... | collective-permute-start | bytes 786440 | tf_op jit(solution)/shard_map/s1_diagonal_from_core/ppermute | solution.py:203
  45.6 2.5 %collective-permute-start.20 = (bf16[1024,128]{1,0:T(8,128)(2,1)S(1)}, bf16[1024,128]{1,0:T(8,128)(2,1)S(1)}, u32[]{:S(2)}, u32[]{:S(2)}) collective-permute-start(bf16[1024,128]{1,0:T(8,128)(2,1)S(1)} %collective-permute-done.19.refs_4_), channel_id=1, source_target_pairs={{0,4},{4,0},{8,12},{12,8},{1,5},{5,1},{9,13},{13,9},{2,6},{6,2},{1... | collective-permute-start | bytes 786440 | tf_op jit(solution)/shard_map/s1_across_from_core/ppermute | solution.py:203
  46.1 9.4 %collective-permute-start.24 = (bf16[2,320,128]{2,1,0:T(8,128)(2,1)S(1)}, bf16[2,320,128]{2,1,0:T(8,128)(2,1)S(1)}, u32[]{:S(2)}, u32[]{:S(2)}) collective-permute-start(bf16[2,320,128]{2,1,0:T(8,128)(2,1)S(1)} %get-tuple-element.59), channel_id=1, source_target_pairs={{0,1},{1,0},{2,3},{3,2},{4,5},{5,4},{6,7},{7,6},{8,9},{9,8},{10,11... | collective-permute-start | bytes 491528 | tf_op jit(solution)/shard_map/sum1_from_layer_1/ppermute | solution.py:203
  47.9 11.5 %collective-permute-start.18 = (bf16[2,320,128]{2,1,0:T(8,128)(2,1)S(1)}, bf16[2,320,128]{2,1,0:T(8,128)(2,1)S(1)}, u32[]{:S(2)}, u32[]{:S(2)}) collective-permute-start(bf16[2,320,128]{2,1,0:T(8,128)(2,1)S(1)} %get-tuple-element.50), channel_id=1, source_target_pairs={{0,1},{1,0},{2,3},{3,2},{4,5},{5,4},{6,7},{7,6},{8,9},{9,8},{10,11... | collective-permute-start | bytes 491528 | tf_op jit(solution)/shard_map/sum2_from_layer_1/ppermute | solution.py:203
  51.1 12.4 %collective-permute-start.26 = (bf16[2,320,128]{2,1,0:T(8,128)(2,1)S(1)}, bf16[2,320,128]{2,1,0:T(8,128)(2,1)S(1)}, u32[]{:S(2)}, u32[]{:S(2)}) collective-permute-start(bf16[2,320,128]{2,1,0:T(8,128)(2,1)S(1)} %get-tuple-element.62), channel_id=1, source_target_pairs={{0,1},{1,0},{2,3},{3,2},{4,5},{5,4},{6,7},{7,6},{8,9},{9,8},{10,11... | collective-permute-start | bytes 491528 | tf_op jit(solution)/shard_map/sum3_from_layer_1/ppermute | solution.py:203
  52.9 12.0 %collective-permute-start.17 = (bf16[1,320,128]{2,1,0:T(8,128)(2,1)S(1)}, bf16[1,320,128]{2,1,0:T(8,128)(2,1)S(1)}, u32[]{:S(2)}, u32[]{:S(2)}) collective-permute-start(bf16[1,320,128]{2,1,0:T(8,128)(2,1)S(1)} %get-tuple-element.49), channel_id=1, source_target_pairs={{0,2},{1,3},{2,0},{3,1},{4,6},{5,7},{6,4},{7,5},{8,10},{9,11},{10,... | collective-permute-start | bytes 245768 | tf_op jit(solution)/shard_map/sum0_from_layer_2/ppermute | solution.py:203
  55.5 15.7 %collective-permute-start.25 = (bf16[1,320,128]{2,1,0:T(8,128)(2,1)S(1)}, bf16[1,320,128]{2,1,0:T(8,128)(2,1)S(1)}, u32[]{:S(2)}, u32[]{:S(2)}) collective-permute-start(bf16[1,320,128]{2,1,0:T(8,128)(2,1)S(1)} %get-tuple-element.61), channel_id=1, source_target_pairs={{0,2},{1,3},{2,0},{3,1},{4,6},{5,7},{6,4},{7,5},{8,10},{9,11},{10,... | collective-permute-start | bytes 245768 | tf_op jit(solution)/shard_map/sum1_from_layer_2/ppermute | solution.py:203
  59.4 11.1 %collective-permute-start.23 = (bf16[1,320,128]{2,1,0:T(8,128)(2,1)S(1)}, bf16[1,320,128]{2,1,0:T(8,128)(2,1)S(1)}, u32[]{:S(2)}, u32[]{:S(2)}) collective-permute-start(bf16[1,320,128]{2,1,0:T(8,128)(2,1)S(1)} %get-tuple-element.57), channel_id=1, source_target_pairs={{0,2},{1,3},{2,0},{3,1},{4,6},{5,7},{6,4},{7,5},{8,10},{9,11},{10,... | collective-permute-start | bytes 245768 | tf_op jit(solution)/shard_map/sum2_from_layer_2/ppermute | solution.py:203
  63.5 7.9 %collective-permute-start.27 = (bf16[1,320,128]{2,1,0:T(8,128)(2,1)S(1)}, bf16[1,320,128]{2,1,0:T(8,128)(2,1)S(1)}, u32[]{:S(2)}, u32[]{:S(2)}) collective-permute-start(bf16[1,320,128]{2,1,0:T(8,128)(2,1)S(1)} %get-tuple-element.64), channel_id=1, source_target_pairs={{0,2},{1,3},{2,0},{3,1},{4,6},{5,7},{6,4},{7,5},{8,10},{9,11},{10,... | collective-permute-start | bytes 245768 | tf_op jit(solution)/shard_map/sum3_from_layer_2/ppermute | solution.py:203

commit v17 on v16

--- a/solution.py
+++ b/solution.py
@@ -303,7 +303,7 @@
     early = [i for i in range(len(parts)) if i % groups == 0]
     late = [i for i in range(len(parts)) if i % groups]
     out = None
-    for which in (early, late):
+    for which in (early, late[:-1], late[-1:]):
         out = finish(sizes, place, [where[i] for i in which], [parts[i] for i in which], total, out)
     return out
 

time: 72.4 us -> 72.8 us (level)
    pallas_call x2 -> x3, Pallas kernels: 1.51 us -> 2.14 us  [finish(): pl.pallas_call(functools.partial(finish_kernel, sizes, tuple(where), out...]
  transfers between devices with their start and end apart: 28 -> 28, of which waited for: 12 -> 11; matrix products, arithmetic and copies ran while one was open for 0% -> 0% of each run, Pallas kernels for 27% -> 28%
where the time goes in v17:
time: 72.8 us; the launch traced here: 72.6 us
  starting transfers between devices  28.7 us (39%)
  waiting for transfers between devices  22 us (30%)
  Pallas kernels  21.8 us (30%)
    ppermute x28, starting transfers between devices, permute(): return lax.ppermute(x, axis, perm)  28.7 us
    ppermute x28, waiting for transfers between devices, permute(): return lax.ppermute(x, axis, perm)  22 us
    pallas_call x3, Pallas kernels, score(): pl.pallas_call(functools.partial(score_kernel, sizes, columns, direct), o...  9.14 us
    pallas_call x2, Pallas kernels, condition(): pl.pallas_call(functools.partial(condition_kernel, sizes), out_shape=[plt...  5.01 us
    pallas_call x1, Pallas kernels, load(): pl.pallas_call(load_kernel, out_shape=pltpu.VMEM(source.shape, BF16), in_...  3.39 us
    pallas_call x3, Pallas kernels, finish(): pl.pallas_call(functools.partial(finish_kernel, sizes, tuple(where), out...  2.14 us
    pallas_call x2, Pallas kernels, take(): pl.pallas_call(functools.partial(take_kernel, chunk), out_shape=pltpu.VME...  1.92 us
  transfers between devices with their start and end apart: 28, of which 11 were waited for; matrix products, arithmetic and copies ran while one was open for 0% of the time, Pallas kernels for 28%

profile of v17, /device:TPU:0, one launch (start us, length us, event | category | flops | bytes accessed | tf_op | source)
XLA Modules:
  0.0 72.6 jit_solution(5510436339497034201)
XLA Ops:
  0.0 1.0 %take.2.after.refs_4_ = bf16[128,1024]{1,0:T(8,128)(2,1)S(1)} custom-call(s32[1]{0:T(128)} %bitcast.at_group.after.refs_0_, s32[1]{0:T(128)} %bitcast.1.at_ex.refs_1_, s32[1]{0:T(128)} %bitcast.2.at_layer.refs_2_, bf16[512,1024]{1,0:T(8,128)(2,1)} %bitcast.12, s32[1]{0:T(128)} %bitcast.at_group.after.refs_0_), custom_call_target="tpu_custom_call" | custom-call | tf_op jit(solution)/shard_map/take/pallas_call | solution.py:58
  1.0 3.0 %collective-permute-start.1 = (bf16[128,1024]{1,0:T(8,128)(2,1)S(1)}, bf16[128,1024]{1,0:T(8,128)(2,1)S(1)}, u32[]{:S(2)}, u32[]{:S(2)}) collective-permute-start(bf16[128,1024]{1,0:T(8,128)(2,1)S(1)} %take.2.after.refs_4_), channel_id=1, source_target_pairs={{0,8},{4,12},{8,0},{12,4},{1,9},{5,13},{9,1},{13,5},{2,10},{6,14},... | collective-permute-start | bytes 786440 | tf_op jit(solution)/shard_map/q0_from_chip/ppermute | solution.py:203
  4.0 3.4 %load.1.after.refs_3_ = bf16[1024,4096]{1,0:T(8,128)(2,1)S(1)} custom-call(bf16[1024,4096]{1,0:T(8,128)(2,1)} %bitcast.11, bf16[128,1024]{1,0:T(8,128)(2,1)S(1)} %take.2.after.refs_4_), custom_call_target="tpu_custom_call" | custom-call | tf_op jit(solution)/shard_map/load/pallas_call | solution.py:38
  7.4 1.0 %take.3.refs_8_.refs_4_ = bf16[128,1024]{1,0:T(8,128)(2,1)S(1)} custom-call(s32[1]{0:T(128)} %bitcast.at_group.after.refs_0_, s32[1]{0:T(128)} %bitcast.1.at_ex.refs_1_, s32[1]{0:T(128)} %bitcast.2.at_layer.refs_2_, bf16[512,1024]{1,0:T(8,128)(2,1)} %bitcast.13, bf16[1024,4096]{1,0:T(8,128)(2,1)S(1)} %load.1.after.refs_3_), custom_call_target="tpu_custom_call" | custom-call | tf_op jit(solution)/shard_map/take/pallas_call | solution.py:58
  8.4 0.0 slice-start
  8.4 0.0 slice-start.1
  8.4 1.9 %collective-permute-done.1.refs_6_ = bf16[128,1024]{1,0:T(8,128)(2,1)S(1)} collective-permute-done((bf16[128,1024]{1,0:T(8,128)(2,1)S(1)}, bf16[128,1024]{1,0:T(8,128)(2,1)S(1)}, u32[]{:S(2)}, u32[]{:S(2)}) %collective-permute-start.1) | collective-permute-done | bytes 262176 | tf_op jit(solution)/shard_map/q0_from_chip/ppermute | solution.py:203
  10.3 0.0 collective-permute-start.2
  10.3 1.7 %collective-permute-start.6 = (bf16[128,1024]{1,0:T(8,128)(2,1)S(1)}, bf16[128,1024]{1,0:T(8,128)(2,1)S(1)}, u32[]{:S(2)}, u32[]{:S(2)}) collective-permute-start(bf16[128,1024]{1,0:T(8,128)(2,1)S(1)} %take.3.refs_8_.refs_4_), channel_id=1, source_target_pairs={{0,8},{4,12},{8,0},{12,4},{1,9},{5,13},{9,1},{13,5},{2,10},{6,14},... | collective-permute-start | bytes 786440 | tf_op jit(solution)/shard_map/q1_from_chip/ppermute | solution.py:203
  12.1 2.5 %condition.2 = (bf16[1024,128]{1,0:T(8,128)(2,1)S(1)}, bf16[1040,128]{1,0:T(8,128)(2,1)S(1)}, bf16[1024,128]{1,0:T(8,128)(2,1)S(1)}) custom-call(s32[1]{0:T(128)} %bitcast.at_group.after.refs_0_, s32[1]{0:T(128)} %bitcast.1.at_ex.refs_1_, s32[1]{0:T(128)} %bitcast.2.at_layer.refs_2_, bf16[1024,4096]{1,0:T(8,128)(2,1)S(1)} %load.1.after.refs_3_, ...), custom_call_target="tpu_custom_call" | custom-call | tf_op jit(solution)/shard_map/condition/pallas_call | solution.py:89
  14.5 1.6 %collective-permute-start.4 = (bf16[1040,128]{1,0:T(8,128)(2,1)S(1)}, bf16[1040,128]{1,0:T(8,128)(2,1)S(1)}, u32[]{:S(2)}, u32[]{:S(2)}) collective-permute-start(bf16[1040,128]{1,0:T(8,128)(2,1)S(1)} %get-tuple-element.37), channel_id=1, source_target_pairs={{0,8},{4,12},{8,0},{12,4},{1,9},{5,13},{9,1},{13,5},{2,10},{6,14},... | collective-permute-start | bytes 798728 | tf_op jit(solution)/shard_map/s0_from_chip/ppermute | solution.py:203
  16.1 0.0 collective-permute-start.5
  16.1 3.3 %collective-permute-done.6.refs_6_ = bf16[128,1024]{1,0:T(8,128)(2,1)S(1)} collective-permute-done((bf16[128,1024]{1,0:T(8,128)(2,1)S(1)}, bf16[128,1024]{1,0:T(8,128)(2,1)S(1)}, u32[]{:S(2)}, u32[]{:S(2)}) %collective-permute-start.6) | collective-permute-done | bytes 262176 | tf_op jit(solution)/shard_map/q1_from_chip/ppermute | solution.py:203
  19.4 1.7 %collective-permute-start.10 = (bf16[1024,128]{1,0:T(8,128)(2,1)S(1)}, bf16[1024,128]{1,0:T(8,128)(2,1)S(1)}, u32[]{:S(2)}, u32[]{:S(2)}) collective-permute-start(bf16[1024,128]{1,0:T(8,128)(2,1)S(1)} %get-tuple-element.43), channel_id=1, source_target_pairs={{0,16},{16,0},{1,17},{17,1},{2,18},{18,2},{3,19},{19,3},{4,20},{20... | collective-permute-start | bytes 786440 | tf_op jit(solution)/shard_map/s0_from_group/ppermute | solution.py:203
  21.1 0.2 collective-permute-start.3
  21.4 0.0 collective-permute-done.5.refs_5_
  21.4 0.0 collective-permute-done.7.refs_7_
  21.4 2.5 %condition.3 = (bf16[1024,128]{1,0:T(8,128)(2,1)S(1)}, bf16[1024,128]{1,0:T(8,128)(2,1)S(1)}) custom-call(s32[1]{0:T(128)} %bitcast.at_group.after.refs_0_, s32[1]{0:T(128)} %bitcast.1.at_ex.refs_1_, s32[1]{0:T(128)} %bitcast.2.at_layer.refs_2_, bf16[1024,4096]{1,0:T(8,128)(2,1)S(1)} %load.1.after.refs_3_, bf16[128,1024]{1,0:T(8,128)(2,1)S(1)} %take.3.refs_8_.refs_4_, ...), custom_call_target="tpu_custom_call" | custom-call | tf_op jit(solution)/shard_map/condition/pallas_call | solution.py:89
  23.9 0.8 %collective-permute-done.4.refs_6_ = bf16[1040,128]{1,0:T(8,128)(2,1)S(1)} collective-permute-done((bf16[1040,128]{1,0:T(8,128)(2,1)S(1)}, bf16[1040,128]{1,0:T(8,128)(2,1)S(1)}, u32[]{:S(2)}, u32[]{:S(2)}) %collective-permute-start.4) | collective-permute-done | bytes 266272 | tf_op jit(solution)/shard_map/s0_from_chip/ppermute | solution.py:203
  24.7 1.7 %collective-permute-start.12 = (bf16[1040,128]{1,0:T(8,128)(2,1)S(1)}, bf16[1040,128]{1,0:T(8,128)(2,1)S(1)}, u32[]{:S(2)}, u32[]{:S(2)}) collective-permute-start(bf16[1040,128]{1,0:T(8,128)(2,1)S(1)} %collective-permute-done.4.refs_6_), channel_id=1, source_target_pairs={{0,16},{16,0},{1,17},{17,1},{2,18},{18,2},{3,19},{19,3},{4,20},{20... | collective-permute-start | bytes 798728 | tf_op jit(solution)/shard_map/s0_there_from_group/ppermute | solution.py:203
  26.4 1.5 %collective-permute-start.15 = (bf16[1024,128]{1,0:T(8,128)(2,1)S(1)}, bf16[1024,128]{1,0:T(8,128)(2,1)S(1)}, u32[]{:S(2)}, u32[]{:S(2)}) collective-permute-start(bf16[1024,128]{1,0:T(8,128)(2,1)S(1)} %get-tuple-element.39.refs_8_), channel_id=1, source_target_pairs={{0,8},{4,12},{8,0},{12,4},{1,9},{5,13},{9,1},{13,5},{2,10},{6,14},... | collective-permute-start | bytes 786440 | tf_op jit(solution)/shard_map/s1_from_chip/ppermute | solution.py:203
  28.0 0.4 collective-permute-done.10.refs_4_
  28.4 1.7 %collective-permute-start.19 = (bf16[1024,128]{1,0:T(8,128)(2,1)S(1)}, bf16[1024,128]{1,0:T(8,128)(2,1)S(1)}, u32[]{:S(2)}, u32[]{:S(2)}) collective-permute-start(bf16[1024,128]{1,0:T(8,128)(2,1)S(1)} %get-tuple-element.51), channel_id=1, source_target_pairs={{0,16},{16,0},{1,17},{17,1},{2,18},{18,2},{3,19},{19,3},{4,20},{20... | collective-permute-start | bytes 786440 | tf_op jit(solution)/shard_map/s1_from_group/ppermute | solution.py:203
  30.1 2.9 %score0.1 = (bf16[2,320,128]{2,1,0:T(8,128)(2,1)S(1)}, f32[2,320,128]{2,1,0:T(8,128)S(1)}) custom-call(s32[1]{0:T(128)} %bitcast.at_group.after.refs_0_, s32[1]{0:T(128)} %bitcast.1.at_ex.refs_1_, s32[1]{0:T(128)} %bitcast.2.at_layer.refs_2_, bf16[1280,4096]{1,0:T(8,128)(2,1)S(1)} %bitcast.8, bf16[1024,128]{1,0:T(8,128)(2,1)S(1)} %get-tuple-element.36.refs_8_.refs_4_, ...), custom_call_target="tpu_custom_call" | custom-call | tf_op jit(solution)/shard_map/score0/pallas_call | solution.py:129
  33.1 1.0 %collective-permute-done.12.refs_6_ = bf16[1040,128]{1,0:T(8,128)(2,1)S(1)} collective-permute-done((bf16[1040,128]{1,0:T(8,128)(2,1)S(1)}, bf16[1040,128]{1,0:T(8,128)(2,1)S(1)}, u32[]{:S(2)}, u32[]{:S(2)}) %collective-permute-start.12) | collective-permute-done | bytes 266272 | tf_op jit(solution)/shard_map/s0_there_from_group/ppermute | solution.py:203
  34.1 0.5 collective-permute-start.14
  34.6 0.3 collective-permute-done.15.refs_10_
  34.9 1.5 %collective-permute-start.21 = (bf16[1024,128]{1,0:T(8,128)(2,1)S(1)}, bf16[1024,128]{1,0:T(8,128)(2,1)S(1)}, u32[]{:S(2)}, u32[]{:S(2)}) collective-permute-start(bf16[1024,128]{1,0:T(8,128)(2,1)S(1)} %collective-permute-done.15.refs_10_), channel_id=1, source_target_pairs={{0,16},{16,0},{1,17},{17,1},{2,18},{18,2},{3,19},{19,3},{4,20},{20... | collective-permute-start | bytes 786440 | tf_op jit(solution)/shard_map/s1_there_from_group/ppermute | solution.py:203
  36.4 3.3 %collective-permute-done.19.refs_4_ = bf16[1024,128]{1,0:T(8,128)(2,1)S(1)} collective-permute-done((bf16[1024,128]{1,0:T(8,128)(2,1)S(1)}, bf16[1024,128]{1,0:T(8,128)(2,1)S(1)}, u32[]{:S(2)}, u32[]{:S(2)}) %collective-permute-start.19) | collective-permute-done | bytes 262176 | tf_op jit(solution)/shard_map/s1_from_group/ppermute | solution.py:203
  39.7 1.8 %collective-permute-start.9 = (bf16[2,320,128]{2,1,0:T(8,128)(2,1)S(1)}, bf16[2,320,128]{2,1,0:T(8,128)(2,1)S(1)}, u32[]{:S(2)}, u32[]{:S(2)}) collective-permute-start(bf16[2,320,128]{2,1,0:T(8,128)(2,1)S(1)} %get-tuple-element.42), channel_id=1, source_target_pairs={{0,1},{1,0},{2,3},{3,2},{4,5},{5,4},{6,7},{7,6},{8,9},{9,8},{10,11... | collective-permute-start | bytes 491528 | tf_op jit(solution)/shard_map/sum0_from_layer_1/ppermute | solution.py:203
  41.5 3.3 %score1.1 = (bf16[2,320,128]{2,1,0:T(8,128)(2,1)S(1)}, f32[2,320,128]{2,1,0:T(8,128)S(1)}, bf16[2,320,128]{2,1,0:T(8,128)(2,1)S(1)}, f32[2,320,128]{2,1,0:T(8,128)S(1)}) custom-call(s32[1]{0:T(128)} %bitcast.at_group.after.refs_0_, s32[1]{0:T(128)} %bitcast.1.at_ex.refs_1_, s32[1]{0:T(128)} %bitcast.2.at_layer.refs_2_, bf16[1280,4096]{1,0:T(8,128)(2,1)S(1)} %bitcast.9, ...), custom_call_target="tpu_custom_call" | custom-call | tf_op jit(solution)/shard_map/score1/pallas_call | solution.py:129
  44.8 0.7 %collective-permute-done.9.got = bf16[2,320,128]{2,1,0:T(8,128)(2,1)S(1)} collective-permute-done((bf16[2,320,128]{2,1,0:T(8,128)(2,1)S(1)}, bf16[2,320,128]{2,1,0:T(8,128)(2,1)S(1)}, u32[]{:S(2)}, u32[]{:S(2)}) %collective-permute-start.9) | collective-permute-done | bytes 163872 | tf_op jit(solution)/shard_map/sum0_from_layer_1/ppermute | solution.py:203
  45.5 0.1 collective-permute-start.22
  45.6 0.5 collective-permute-start.20
  46.1 1.7 %collective-permute-start.24 = (bf16[2,320,128]{2,1,0:T(8,128)(2,1)S(1)}, bf16[2,320,128]{2,1,0:T(8,128)(2,1)S(1)}, u32[]{:S(2)}, u32[]{:S(2)}) collective-permute-start(bf16[2,320,128]{2,1,0:T(8,128)(2,1)S(1)} %get-tuple-element.59), channel_id=1, source_target_pairs={{0,1},{1,0},{2,3},{3,2},{4,5},{5,4},{6,7},{7,6},{8,9},{9,8},{10,11... | collective-permute-start | bytes 491528 | tf_op jit(solution)/shard_map/sum1_from_layer_1/ppermute | solution.py:203
  47.9 0.3 collective-permute-start.18
  48.2 2.9 %score2.1 = (bf16[2,320,128]{2,1,0:T(8,128)(2,1)S(1)}, f32[2,320,128]{2,1,0:T(8,128)S(1)}) custom-call(s32[1]{0:T(128)} %bitcast.at_group.after.refs_0_, s32[1]{0:T(128)} %bitcast.1.at_ex.refs_1_, s32[1]{0:T(128)} %bitcast.2.at_layer.refs_2_, bf16[1280,4096]{1,0:T(8,128)(2,1)S(1)} %bitcast.10, bf16[1024,128]{1,0:T(8,128)(2,1)S(1)} %collective-permute-done.19.refs_4_, ...), custom_call_target="tpu_custom_call" | custom-call | tf_op jit(solution)/shard_map/score2/pallas_call | solution.py:129
  51.1 1.8 %collective-permute-start.26 = (bf16[2,320,128]{2,1,0:T(8,128)(2,1)S(1)}, bf16[2,320,128]{2,1,0:T(8,128)(2,1)S(1)}, u32[]{:S(2)}, u32[]{:S(2)}) collective-permute-start(bf16[2,320,128]{2,1,0:T(8,128)(2,1)S(1)} %get-tuple-element.62), channel_id=1, source_target_pairs={{0,1},{1,0},{2,3},{3,2},{4,5},{5,4},{6,7},{7,6},{8,9},{9,8},{10,11... | collective-permute-start | bytes 491528 | tf_op jit(solution)/shard_map/sum3_from_layer_1/ppermute | solution.py:203
  52.9 2.6 %collective-permute-start.17 = (bf16[1,320,128]{2,1,0:T(8,128)(2,1)S(1)}, bf16[1,320,128]{2,1,0:T(8,128)(2,1)S(1)}, u32[]{:S(2)}, u32[]{:S(2)}) collective-permute-start(bf16[1,320,128]{2,1,0:T(8,128)(2,1)S(1)} %get-tuple-element.49), channel_id=1, source_target_pairs={{0,2},{1,3},{2,0},{3,1},{4,6},{5,7},{6,4},{7,5},{8,10},{9,11},{10,... | collective-permute-start | bytes 245768 | tf_op jit(solution)/shard_map/sum0_from_layer_2/ppermute | solution.py:203
  55.5 0.5 collective-permute-start.25
  56.0 3.3 %collective-permute-done.18.got = bf16[2,320,128]{2,1,0:T(8,128)(2,1)S(1)} collective-permute-done((bf16[2,320,128]{2,1,0:T(8,128)(2,1)S(1)}, bf16[2,320,128]{2,1,0:T(8,128)(2,1)S(1)}, u32[]{:S(2)}, u32[]{:S(2)}) %collective-permute-start.18) | collective-permute-done | bytes 163872 | tf_op jit(solution)/shard_map/sum2_from_layer_1/ppermute | solution.py:203
  59.4 2.8 %collective-permute-start.23 = (bf16[1,320,128]{2,1,0:T(8,128)(2,1)S(1)}, bf16[1,320,128]{2,1,0:T(8,128)(2,1)S(1)}, u32[]{:S(2)}, u32[]{:S(2)}) collective-permute-start(bf16[1,320,128]{2,1,0:T(8,128)(2,1)S(1)} %get-tuple-element.57), channel_id=1, source_target_pairs={{0,2},{1,3},{2,0},{3,1},{4,6},{5,7},{6,4},{7,5},{8,10},{9,11},{10,... | collective-permute-start | bytes 245768 | tf_op jit(solution)/shard_map/sum2_from_layer_2/ppermute | solution.py:203
  62.2 1.3 %collective-permute-done.26.got = bf16[2,320,128]{2,1,0:T(8,128)(2,1)S(1)} collective-permute-done((bf16[2,320,128]{2,1,0:T(8,128)(2,1)S(1)}, bf16[2,320,128]{2,1,0:T(8,128)(2,1)S(1)}, u32[]{:S(2)}, u32[]{:S(2)}) %collective-permute-start.26) | collective-permute-done | bytes 163872 | tf_op jit(solution)/shard_map/sum3_from_layer_1/ppermute | solution.py:203
  63.5 1.4 %collective-permute-start.27 = (bf16[1,320,128]{2,1,0:T(8,128)(2,1)S(1)}, bf16[1,320,128]{2,1,0:T(8,128)(2,1)S(1)}, u32[]{:S(2)}, u32[]{:S(2)}) collective-permute-start(bf16[1,320,128]{2,1,0:T(8,128)(2,1)S(1)} %get-tuple-element.64), channel_id=1, source_target_pairs={{0,2},{1,3},{2,0},{3,1},{4,6},{5,7},{6,4},{7,5},{8,10},{9,11},{10,... | collective-permute-start | bytes 245768 | tf_op jit(solution)/shard_map/sum3_from_layer_2/ppermute | solution.py:203
  64.9 5.6 %collective-permute-done.23.refs_6_ = bf16[1,320,128]{2,1,0:T(8,128)(2,1)S(1)} collective-permute-done((bf16[1,320,128]{2,1,0:T(8,128)(2,1)S(1)}, bf16[1,320,128]{2,1,0:T(8,128)(2,1)S(1)}, u32[]{:S(2)}, u32[]{:S(2)}) %collective-permute-start.23) | collective-permute-done | bytes 81952 | tf_op jit(solution)/shard_map/sum2_from_layer_2/ppermute | solution.py:203
  70.5 0.8 %finish.3.refs_3_ = f32[320,512]{1,0:T(8,128)} custom-call(s32[1]{0:T(128)} %bitcast.at_group.after.refs_0_, s32[1]{0:T(128)} %bitcast.1.at_ex.refs_1_, s32[1]{0:T(128)} %bitcast.2.at_layer.refs_2_, f32[1,320,128]{2,1,0:T(8,128)S(1)} %get-tuple-element.48.refs_8_.refs_3_, bf16[1,320,128]{2,1,0:T(8,128)(2,1)S(1)} %collective-permute-done.17.refs_4_, ...), custom_call_target="tpu_custom_call" | custom-call | tf_op jit(solution)/shard_map/finish/pallas_call | solution.py:180
  71.2 0.7 finish.4.refs_3_
  71.9 0.7 finish.5
  (30 shorter events, 0.2 us)
Async XLA Ops:
  1.0 9.3 %collective-permute-start.1 = (bf16[128,1024]{1,0:T(8,128)(2,1)S(1)}, bf16[128,1024]{1,0:T(8,128)(2,1)S(1)}, u32[]{:S(2)}, u32[]{:S(2)}) collective-permute-start(bf16[128,1024]{1,0:T(8,128)(2,1)S(1)} %take.2.after.refs_4_), channel_id=1, source_target_pairs={{0,8},{4,12},{8,0},{12,4},{1,9},{5,13},{9,1},{13,5},{2,10},{6,14},... | collective-permute-start | bytes 786440 | tf_op jit(solution)/shard_map/q0_from_chip/ppermute | solution.py:203
  4.0 8.1 %collective-permute-start = (bf16[128,1024]{1,0:T(8,128)(2,1)S(1)}, bf16[128,1024]{1,0:T(8,128)(2,1)S(1)}, u32[]{:S(2)}, u32[]{:S(2)}) collective-permute-start(bf16[128,1024]{1,0:T(8,128)(2,1)S(1)} %take.2.after.refs_4_), channel_id=1, source_target_pairs={{0,4},{4,0},{8,12},{12,8},{1,5},{5,1},{9,13},{13,9},{2,6},{6,2},{1... | collective-permute-start | bytes 786440 | tf_op jit(solution)/shard_map/q0_from_core/ppermute | solution.py:203
  8.4 21.7 %slice-start = ((s8[10485760]{0:T(1024)(128)(4,1)}), s8[4194304]{0:T(1024)(128)(4,1)S(1)}, s32[]{:S(2)}) async-start(s8[10485760]{0:T(1024)(128)(4,1)} %bitcast.6), calls=%async_computation | async-start | bytes 8388608
  8.4 21.7 %slice-start.1 = ((s8[10485760]{0:T(1024)(128)(4,1)}), s8[4194304]{0:T(1024)(128)(4,1)S(1)}, s32[]{:S(2)}) async-start(s8[10485760]{0:T(1024)(128)(4,1)} %bitcast.6), calls=%async_computation.1 | async-start | bytes 8388608
  10.3 1.8 %collective-permute-start.2 = (bf16[128,1024]{1,0:T(8,128)(2,1)S(1)}, bf16[128,1024]{1,0:T(8,128)(2,1)S(1)}, u32[]{:S(2)}, u32[]{:S(2)}) collective-permute-start(bf16[128,1024]{1,0:T(8,128)(2,1)S(1)} %collective-permute-done.1.refs_6_), channel_id=1, source_target_pairs={{0,4},{4,0},{8,12},{12,8},{1,5},{5,1},{9,13},{13,9},{2,6},{6,2},{1... | collective-permute-start | bytes 786440 | tf_op jit(solution)/shard_map/q0_there_from_core/ppermute | solution.py:203
  10.3 9.1 %collective-permute-start.6 = (bf16[128,1024]{1,0:T(8,128)(2,1)S(1)}, bf16[128,1024]{1,0:T(8,128)(2,1)S(1)}, u32[]{:S(2)}, u32[]{:S(2)}) collective-permute-start(bf16[128,1024]{1,0:T(8,128)(2,1)S(1)} %take.3.refs_8_.refs_4_), channel_id=1, source_target_pairs={{0,8},{4,12},{8,0},{12,4},{1,9},{5,13},{9,1},{13,5},{2,10},{6,14},... | collective-permute-start | bytes 786440 | tf_op jit(solution)/shard_map/q1_from_chip/ppermute | solution.py:203
  14.5 10.2 %collective-permute-start.4 = (bf16[1040,128]{1,0:T(8,128)(2,1)S(1)}, bf16[1040,128]{1,0:T(8,128)(2,1)S(1)}, u32[]{:S(2)}, u32[]{:S(2)}) collective-permute-start(bf16[1040,128]{1,0:T(8,128)(2,1)S(1)} %get-tuple-element.37), channel_id=1, source_target_pairs={{0,8},{4,12},{8,0},{12,4},{1,9},{5,13},{9,1},{13,5},{2,10},{6,14},... | collective-permute-start | bytes 798728 | tf_op jit(solution)/shard_map/s0_from_chip/ppermute | solution.py:203
  16.1 5.2 %collective-permute-start.5 = (bf16[128,1024]{1,0:T(8,128)(2,1)S(1)}, bf16[128,1024]{1,0:T(8,128)(2,1)S(1)}, u32[]{:S(2)}, u32[]{:S(2)}) collective-permute-start(bf16[128,1024]{1,0:T(8,128)(2,1)S(1)} %take.3.refs_8_.refs_4_), channel_id=1, source_target_pairs={{0,4},{4,0},{8,12},{12,8},{1,5},{5,1},{9,13},{13,9},{2,6},{6,2},{1... | collective-permute-start | bytes 786440 | tf_op jit(solution)/shard_map/q1_from_core/ppermute | solution.py:203
  19.4 2.0 %collective-permute-start.7 = (bf16[128,1024]{1,0:T(8,128)(2,1)S(1)}, bf16[128,1024]{1,0:T(8,128)(2,1)S(1)}, u32[]{:S(2)}, u32[]{:S(2)}) collective-permute-start(bf16[128,1024]{1,0:T(8,128)(2,1)S(1)} %collective-permute-done.6.refs_6_), channel_id=1, source_target_pairs={{0,4},{4,0},{8,12},{12,8},{1,5},{5,1},{9,13},{13,9},{2,6},{6,2},{1... | collective-permute-start | bytes 786440 | tf_op jit(solution)/shard_map/q1_there_from_core/ppermute | solution.py:203
  19.4 10.7 %slice-start.2 = ((s8[10485760]{0:T(1024)(128)(4,1)}), s8[2097152]{0:T(1024)(128)(4,1)S(1)}, s32[]{:S(2)}) async-start(s8[10485760]{0:T(1024)(128)(4,1)} %bitcast.6), calls=%async_computation.2 | async-start | bytes 4194304
  19.4 8.9 %collective-permute-start.10 = (bf16[1024,128]{1,0:T(8,128)(2,1)S(1)}, bf16[1024,128]{1,0:T(8,128)(2,1)S(1)}, u32[]{:S(2)}, u32[]{:S(2)}) collective-permute-start(bf16[1024,128]{1,0:T(8,128)(2,1)S(1)} %get-tuple-element.43), channel_id=1, source_target_pairs={{0,16},{16,0},{1,17},{17,1},{2,18},{18,2},{3,19},{19,3},{4,20},{20... | collective-permute-start | bytes 786440 | tf_op jit(solution)/shard_map/s0_from_group/ppermute | solution.py:203
  21.1 7.2 %collective-permute-start.3 = (bf16[1024,128]{1,0:T(8,128)(2,1)S(1)}, bf16[1024,128]{1,0:T(8,128)(2,1)S(1)}, u32[]{:S(2)}, u32[]{:S(2)}) collective-permute-start(bf16[1024,128]{1,0:T(8,128)(2,1)S(1)} %get-tuple-element.36.refs_8_.refs_4_), channel_id=1, source_target_pairs={{0,4},{4,0},{8,12},{12,8},{1,5},{5,1},{9,13},{13,9},{2,6},{6,2},{1... | collective-permute-start | bytes 786440 | tf_op jit(solution)/shard_map/s0_from_core/ppermute | solution.py:203
  24.7 5.4 %collective-permute-start.8 = (bf16[1040,128]{1,0:T(8,128)(2,1)S(1)}, bf16[1040,128]{1,0:T(8,128)(2,1)S(1)}, u32[]{:S(2)}, u32[]{:S(2)}) collective-permute-start(bf16[1040,128]{1,0:T(8,128)(2,1)S(1)} %collective-permute-done.4.refs_6_), channel_id=1, source_target_pairs={{0,4},{4,0},{8,12},{12,8},{1,5},{5,1},{9,13},{13,9},{2,6},{6,2},{1... | collective-permute-start | bytes 798728 | tf_op jit(solution)/shard_map/s0_there_from_core/ppermute | solution.py:203
  24.7 9.3 %collective-permute-start.12 = (bf16[1040,128]{1,0:T(8,128)(2,1)S(1)}, bf16[1040,128]{1,0:T(8,128)(2,1)S(1)}, u32[]{:S(2)}, u32[]{:S(2)}) collective-permute-start(bf16[1040,128]{1,0:T(8,128)(2,1)S(1)} %collective-permute-done.4.refs_6_), channel_id=1, source_target_pairs={{0,16},{16,0},{1,17},{17,1},{2,18},{18,2},{3,19},{19,3},{4,20},{20... | collective-permute-start | bytes 798728 | tf_op jit(solution)/shard_map/s0_there_from_group/ppermute | solution.py:203
  26.4 8.4 %collective-permute-start.15 = (bf16[1024,128]{1,0:T(8,128)(2,1)S(1)}, bf16[1024,128]{1,0:T(8,128)(2,1)S(1)}, u32[]{:S(2)}, u32[]{:S(2)}) collective-permute-start(bf16[1024,128]{1,0:T(8,128)(2,1)S(1)} %get-tuple-element.39.refs_8_), channel_id=1, source_target_pairs={{0,8},{4,12},{8,0},{12,4},{1,9},{5,13},{9,1},{13,5},{2,10},{6,14},... | collective-permute-start | bytes 786440 | tf_op jit(solution)/shard_map/s1_from_chip/ppermute | solution.py:203
  28.4 6.5 %collective-permute-start.11 = (bf16[1024,128]{1,0:T(8,128)(2,1)S(1)}, bf16[1024,128]{1,0:T(8,128)(2,1)S(1)}, u32[]{:S(2)}, u32[]{:S(2)}) collective-permute-start(bf16[1024,128]{1,0:T(8,128)(2,1)S(1)} %collective-permute-done.10.refs_4_), channel_id=1, source_target_pairs={{0,4},{4,0},{8,12},{12,8},{1,5},{5,1},{9,13},{13,9},{2,6},{6,2},{1... | collective-permute-start | bytes 786440 | tf_op jit(solution)/shard_map/s0_across_from_core/ppermute | solution.py:203
  28.4 11.3 %collective-permute-start.19 = (bf16[1024,128]{1,0:T(8,128)(2,1)S(1)}, bf16[1024,128]{1,0:T(8,128)(2,1)S(1)}, u32[]{:S(2)}, u32[]{:S(2)}) collective-permute-start(bf16[1024,128]{1,0:T(8,128)(2,1)S(1)} %get-tuple-element.51), channel_id=1, source_target_pairs={{0,16},{16,0},{1,17},{17,1},{2,18},{18,2},{3,19},{19,3},{4,20},{20... | collective-permute-start | bytes 786440 | tf_op jit(solution)/shard_map/s1_from_group/ppermute | solution.py:203
  34.1 7.4 %collective-permute-start.13 = (bf16[1040,128]{1,0:T(8,128)(2,1)S(1)}, bf16[1040,128]{1,0:T(8,128)(2,1)S(1)}, u32[]{:S(2)}, u32[]{:S(2)}) collective-permute-start(bf16[1040,128]{1,0:T(8,128)(2,1)S(1)} %collective-permute-done.12.refs_6_), channel_id=1, source_target_pairs={{0,4},{4,0},{8,12},{12,8},{1,5},{5,1},{9,13},{13,9},{2,6},{6,2},{1... | collective-permute-start | bytes 798728 | tf_op jit(solution)/shard_map/s0_diagonal_from_core/ppermute | solution.py:203
  34.1 7.4 %collective-permute-start.14 = (bf16[1024,128]{1,0:T(8,128)(2,1)S(1)}, bf16[1024,128]{1,0:T(8,128)(2,1)S(1)}, u32[]{:S(2)}, u32[]{:S(2)}) collective-permute-start(bf16[1024,128]{1,0:T(8,128)(2,1)S(1)} %get-tuple-element.39.refs_8_), channel_id=1, source_target_pairs={{0,4},{4,0},{8,12},{12,8},{1,5},{5,1},{9,13},{13,9},{2,6},{6,2},{1... | collective-permute-start | bytes 786440 | tf_op jit(solution)/shard_map/s1_from_core/ppermute | solution.py:203
  34.9 6.6 %collective-permute-start.16 = (bf16[1024,128]{1,0:T(8,128)(2,1)S(1)}, bf16[1024,128]{1,0:T(8,128)(2,1)S(1)}, u32[]{:S(2)}, u32[]{:S(2)}) collective-permute-start(bf16[1024,128]{1,0:T(8,128)(2,1)S(1)} %collective-permute-done.15.refs_10_), channel_id=1, source_target_pairs={{0,4},{4,0},{8,12},{12,8},{1,5},{5,1},{9,13},{13,9},{2,6},{6,2},{1... | collective-permute-start | bytes 786440 | tf_op jit(solution)/shard_map/s1_there_from_core/ppermute | solution.py:203
  34.9 10.6 %collective-permute-start.21 = (bf16[1024,128]{1,0:T(8,128)(2,1)S(1)}, bf16[1024,128]{1,0:T(8,128)(2,1)S(1)}, u32[]{:S(2)}, u32[]{:S(2)}) collective-permute-start(bf16[1024,128]{1,0:T(8,128)(2,1)S(1)} %collective-permute-done.15.refs_10_), channel_id=1, source_target_pairs={{0,16},{16,0},{1,17},{17,1},{2,18},{18,2},{3,19},{19,3},{4,20},{20... | collective-permute-start | bytes 786440 | tf_op jit(solution)/shard_map/s1_there_from_group/ppermute | solution.py:203
  39.7 5.8 %collective-permute-start.9 = (bf16[2,320,128]{2,1,0:T(8,128)(2,1)S(1)}, bf16[2,320,128]{2,1,0:T(8,128)(2,1)S(1)}, u32[]{:S(2)}, u32[]{:S(2)}) collective-permute-start(bf16[2,320,128]{2,1,0:T(8,128)(2,1)S(1)} %get-tuple-element.42), channel_id=1, source_target_pairs={{0,1},{1,0},{2,3},{3,2},{4,5},{5,4},{6,7},{7,6},{8,9},{9,8},{10,11... | collective-permute-start | bytes 491528 | tf_op jit(solution)/shard_map/sum0_from_layer_1/ppermute | solution.py:203
  45.5 2.6 %collective-permute-start.22 = (bf16[1024,128]{1,0:T(8,128)(2,1)S(1)}, bf16[1024,128]{1,0:T(8,128)(2,1)S(1)}, u32[]{:S(2)}, u32[]{:S(2)}) collective-permute-start(bf16[1024,128]{1,0:T(8,128)(2,1)S(1)} %collective-permute-done.21.refs_6_), channel_id=1, source_target_pairs={{0,4},{4,0},{8,12},{12,8},{1,5},{5,1},{9,13},{13,9},{2,6},{6,2},{1... | collective-permute-start | bytes 786440 | tf_op jit(solution)/shard_map/s1_diagonal_from_core/ppermute | solution.py:203
  45.6 2.5 %collective-permute-start.20 = (bf16[1024,128]{1,0:T(8,128)(2,1)S(1)}, bf16[1024,128]{1,0:T(8,128)(2,1)S(1)}, u32[]{:S(2)}, u32[]{:S(2)}) collective-permute-start(bf16[1024,128]{1,0:T(8,128)(2,1)S(1)} %collective-permute-done.19.refs_4_), channel_id=1, source_target_pairs={{0,4},{4,0},{8,12},{12,8},{1,5},{5,1},{9,13},{13,9},{2,6},{6,2},{1... | collective-permute-start | bytes 786440 | tf_op jit(solution)/shard_map/s1_across_from_core/ppermute | solution.py:203
  46.1 9.4 %collective-permute-start.24 = (bf16[2,320,128]{2,1,0:T(8,128)(2,1)S(1)}, bf16[2,320,128]{2,1,0:T(8,128)(2,1)S(1)}, u32[]{:S(2)}, u32[]{:S(2)}) collective-permute-start(bf16[2,320,128]{2,1,0:T(8,128)(2,1)S(1)} %get-tuple-element.59), channel_id=1, source_target_pairs={{0,1},{1,0},{2,3},{3,2},{4,5},{5,4},{6,7},{7,6},{8,9},{9,8},{10,11... | collective-permute-start | bytes 491528 | tf_op jit(solution)/shard_map/sum1_from_layer_1/ppermute | solution.py:203
  47.9 11.5 %collective-permute-start.18 = (bf16[2,320,128]{2,1,0:T(8,128)(2,1)S(1)}, bf16[2,320,128]{2,1,0:T(8,128)(2,1)S(1)}, u32[]{:S(2)}, u32[]{:S(2)}) collective-permute-start(bf16[2,320,128]{2,1,0:T(8,128)(2,1)S(1)} %get-tuple-element.50), channel_id=1, source_target_pairs={{0,1},{1,0},{2,3},{3,2},{4,5},{5,4},{6,7},{7,6},{8,9},{9,8},{10,11... | collective-permute-start | bytes 491528 | tf_op jit(solution)/shard_map/sum2_from_layer_1/ppermute | solution.py:203
  51.1 12.4 %collective-permute-start.26 = (bf16[2,320,128]{2,1,0:T(8,128)(2,1)S(1)}, bf16[2,320,128]{2,1,0:T(8,128)(2,1)S(1)}, u32[]{:S(2)}, u32[]{:S(2)}) collective-permute-start(bf16[2,320,128]{2,1,0:T(8,128)(2,1)S(1)} %get-tuple-element.62), channel_id=1, source_target_pairs={{0,1},{1,0},{2,3},{3,2},{4,5},{5,4},{6,7},{7,6},{8,9},{9,8},{10,11... | collective-permute-start | bytes 491528 | tf_op jit(solution)/shard_map/sum3_from_layer_1/ppermute | solution.py:203
  52.9 12.0 %collective-permute-start.17 = (bf16[1,320,128]{2,1,0:T(8,128)(2,1)S(1)}, bf16[1,320,128]{2,1,0:T(8,128)(2,1)S(1)}, u32[]{:S(2)}, u32[]{:S(2)}) collective-permute-start(bf16[1,320,128]{2,1,0:T(8,128)(2,1)S(1)} %get-tuple-element.49), channel_id=1, source_target_pairs={{0,2},{1,3},{2,0},{3,1},{4,6},{5,7},{6,4},{7,5},{8,10},{9,11},{10,... | collective-permute-start | bytes 245768 | tf_op jit(solution)/shard_map/sum0_from_layer_2/ppermute | solution.py:203
  55.5 15.7 %collective-permute-start.25 = (bf16[1,320,128]{2,1,0:T(8,128)(2,1)S(1)}, bf16[1,320,128]{2,1,0:T(8,128)(2,1)S(1)}, u32[]{:S(2)}, u32[]{:S(2)}) collective-permute-start(bf16[1,320,128]{2,1,0:T(8,128)(2,1)S(1)} %get-tuple-element.61), channel_id=1, source_target_pairs={{0,2},{1,3},{2,0},{3,1},{4,6},{5,7},{6,4},{7,5},{8,10},{9,11},{10,... | collective-permute-start | bytes 245768 | tf_op jit(solution)/shard_map/sum1_from_layer_2/ppermute | solution.py:203
  59.4 11.1 %collective-permute-start.23 = (bf16[1,320,128]{2,1,0:T(8,128)(2,1)S(1)}, bf16[1,320,128]{2,1,0:T(8,128)(2,1)S(1)}, u32[]{:S(2)}, u32[]{:S(2)}) collective-permute-start(bf16[1,320,128]{2,1,0:T(8,128)(2,1)S(1)} %get-tuple-element.57), channel_id=1, source_target_pairs={{0,2},{1,3},{2,0},{3,1},{4,6},{5,7},{6,4},{7,5},{8,10},{9,11},{10,... | collective-permute-start | bytes 245768 | tf_op jit(solution)/shard_map/sum2_from_layer_2/ppermute | solution.py:203
  63.5 8.4 %collective-permute-start.27 = (bf16[1,320,128]{2,1,0:T(8,128)(2,1)S(1)}, bf16[1,320,128]{2,1,0:T(8,128)(2,1)S(1)}, u32[]{:S(2)}, u32[]{:S(2)}) collective-permute-start(bf16[1,320,128]{2,1,0:T(8,128)(2,1)S(1)} %get-tuple-element.64), channel_id=1, source_target_pairs={{0,2},{1,3},{2,0},{3,1},{4,6},{5,7},{6,4},{7,5},{8,10},{9,11},{10,... | collective-permute-start | bytes 245768 | tf_op jit(solution)/shard_map/sum3_from_layer_2/ppermute | solution.py:203
